TPU v7x, 32 devices: a whole 2x2x4 slice. The times are simulated.
32 devices in a mesh: ctx: 8 (over z, x), exp: 4 (over y, core).
Axes of the slice: x: 2, y: 2, z: 4, core: 2. Of those that a mesh axis runs over, the one named last changes fastest.
Arguments:
- seq_input: bfloat16 [2048, 4096], P('ctx', 'exp'), may hold values from -6 to 6
- b_input: bfloat16 [2048, 128], P('ctx'), may hold values from -6 to 6
- c_input: bfloat16 [2048, 128], P('ctx'), may hold values from -6 to 6
- conv_x: float32 [4, 4096], P(None, 'exp'), may hold values from -3 to 3
- conv_bc: float32 [4, 256], replicated, may hold values from -3 to 3
- log_decay: float32 [64, 2048], P('exp', 'ctx'), may hold values from -1 to 0, as said below
- skip_gain: float32 [64], P('exp'), may hold values from 0.5 to 8
- norm_gain: float32 [4096], P('exp'), may hold values from 0.1 to 1.9
- moe_input: bfloat16 [512, 4096], P('ctx', 'exp'), may hold values from -6 to 6
- expert_ids: int32 [512, 2], P('ctx'), may hold values from 0 to 3, all different within a row; in each aligned block of 64 rows (0 to 63, 64 to 127, ...) at most 64 rows name the same one
- w_gate: bfloat16 [4, 4096, 8192], P('exp', None, 'ctx'), may hold values from -0.09375 to 0.09375
- w_up: bfloat16 [4, 4096, 8192], P('exp', None, 'ctx'), may hold values from -0.09375 to 0.09375
Outputs:
- mixed: bfloat16 [2048, 4096], P('ctx', 'exp')
- expert_hidden: bfloat16 [4, 512, 8192], P('exp', None, 'ctx')
Inputs may be any that keep to these rules, and one draw needn't show every extreme that they name: `log_decay`: every entry is negative. `expert_ids`: a row names two different experts; in each aligned block of 64 rows no expert is named by more than 64 rows.
All inputs are finite; a program needn't handle non-finite values.
Results may differ from a plain program's by a relative error of at most 0.001.
Values may be sent and summed in bfloat16 or wider, within the bound.
No kernel may reach another device: no remote copies, remote signals or barrier semaphores. Data moves between devices by JAX's collectives and lax.ppermute only.
A program may use at most 64 MiB of HBM per device.

v0:
```python
import jax
import jax.numpy as jnp
from jax import lax
from jax.sharding import PartitionSpec as P

HDIM = 64
STATE = 128
KCONV = 4
BLOCK = 256


HIGH = lax.Precision.HIGHEST


def passed_along(block, axis, distance):
    devices = range(lax.axis_size(axis))
    route = [(i - distance, i) for i in devices if i - distance in devices]
    return lax.ppermute(block, axis, route)


def causal_conv(padded, weights):
    length = padded.shape[0] - weights.shape[0] + 1
    total = jnp.zeros((length, padded.shape[1]), jnp.float32)
    for offset in range(weights.shape[0]):
        total = total + weights[offset][None, :] * padded[offset : offset + length].astype(
            jnp.float32
        )
    return jax.nn.silu(total)


def ssd_block(carry, pieces):
    drive, bmat, cmat, logs = pieces
    within = jnp.cumsum(logs, axis=1)
    length = logs.shape[1]
    lower = jnp.tril(jnp.ones((length, length), dtype=bool))[None]
    gaps = within[:, :, None] - within[:, None, :]
    decay = jnp.where(lower, jnp.exp(jnp.where(lower, gaps, 0.0)), 0.0)
    intersection = jnp.dot(cmat, bmat.T, precision=HIGH, preferred_element_type=jnp.float32)
    inner = jnp.einsum("hts,shp->thp", decay * intersection[None], drive, precision=HIGH)
    carried = jnp.einsum("tn,hpn->thp", cmat, carry, precision=HIGH) * jnp.exp(within).T[:, :, None]
    remain = jnp.exp(within[:, -1:] - within)
    fresh = jnp.einsum("thp,tn->hpn", drive * remain.T[:, :, None], bmat, precision=HIGH)
    updated = jnp.exp(within[:, -1])[:, None, None] * carry + fresh
    return (updated, inner + carried)


def expert_product(rows, gate_w, up_w):
    gate = jnp.dot(rows, gate_w, preferred_element_type=jnp.float32)
    upper = jnp.dot(rows, up_w, preferred_element_type=jnp.float32)
    return (jax.nn.silu(gate) * upper).astype(jnp.bfloat16)


def slot_matrix(pairs, experts, capacity, tokens):
    flat = pairs.reshape(-1)
    onehot = (flat[:, None] == jnp.arange(experts, dtype=jnp.int32)[None, :]).astype(jnp.int32)
    before = jnp.cumsum(onehot, axis=0) - onehot
    position = jnp.sum(before * onehot, axis=1)
    pos_hot = (position[:, None] == jnp.arange(capacity, dtype=jnp.int32)[None, :]).astype(
        jnp.float32
    )
    tok_hot = (
        (jnp.arange(flat.shape[0], dtype=jnp.int32) // 2)[:, None]
        == jnp.arange(tokens, dtype=jnp.int32)[None, :]
    ).astype(jnp.float32)
    return jnp.einsum("ae,aq,at->eqt", onehot.astype(jnp.float32), pos_hot, tok_hot)


def on_device(
    seq_input,
    b_input,
    c_input,
    conv_x,
    conv_bc,
    log_decay,
    skip_gain,
    norm_gain,
    moe_input,
    expert_ids,
    w_gate,
    w_up,
):
    rim = KCONV - 1
    tokens = seq_input.shape[0]
    heads = skip_gain.shape[0]
    tails = passed_along(
        (seq_input[tokens - rim :], b_input[tokens - rim :], c_input[tokens - rim :]), "ctx", 1
    )
    xconv = causal_conv(jnp.concatenate([tails[0], seq_input], 0), conv_x)
    both = jnp.concatenate(
        [jnp.concatenate([tails[1], tails[2]], 1), jnp.concatenate([b_input, c_input], 1)], 0
    )
    bc = causal_conv(both, conv_bc)
    bconv = bc[:, :STATE]
    cconv = bc[:, STATE:]
    xheads = xconv.reshape(tokens, heads, HDIM)
    inflow = jnp.sqrt(-jnp.expm1(2.0 * log_decay))
    drive = xheads * inflow.T[:, :, None]
    count = tokens // BLOCK
    logs = log_decay.reshape(heads, count, BLOCK).transpose(1, 0, 2)
    start = jnp.zeros((heads, HDIM, STATE), jnp.float32)
    final, outputs = lax.scan(
        ssd_block,
        start,
        (
            drive.reshape(count, BLOCK, heads, HDIM),
            bconv.reshape(count, BLOCK, STATE),
            cconv.reshape(count, BLOCK, STATE),
            logs,
        ),
    )
    through = jnp.exp(jnp.sum(log_decay, axis=1))

    def relay(index, arriving):
        return passed_along(through[:, None, None] * arriving + final, "ctx", 1)

    incoming = lax.fori_loop(0, lax.axis_size("ctx") - 1, relay, jnp.zeros_like(final))
    reach = jnp.exp(jnp.cumsum(log_decay, axis=1))
    carried = jnp.einsum("tn,hpn->thp", cconv, incoming, precision=HIGH) * reach.T[:, :, None]
    pre = outputs.reshape(tokens, heads, HDIM) + carried + skip_gain[None, :, None] * xheads
    scale = lax.rsqrt(jnp.mean(pre * pre, axis=2, keepdims=True) + 1e-05)
    mixed = (
        (pre * scale * norm_gain.reshape(heads, HDIM)[None])
        .reshape(tokens, heads * HDIM)
        .astype(jnp.bfloat16)
    )
    experts = lax.axis_size("exp") * w_gate.shape[0]
    rows_here = moe_input.shape[0]
    capacity = 4 * rows_here // experts
    dispatch = slot_matrix(expert_ids, experts, capacity, rows_here)
    slots = jnp.dot(
        dispatch.reshape(experts * capacity, rows_here).astype(jnp.bfloat16),
        moe_input,
        preferred_element_type=jnp.float32,
    ).astype(jnp.bfloat16)
    slots = slots.reshape(experts, capacity, moe_input.shape[1])
    gate_w = w_gate[0]
    up_w = w_up[0]
    routed = lax.all_to_all(slots, "exp", split_axis=0, concat_axis=2, tiled=True)
    hidden = expert_product(lax.all_gather(routed[0], "ctx", axis=0, tiled=True), gate_w, up_w)
    return (mixed, hidden[None])


def solution(mesh):
    in_specs = (
        P("ctx", "exp"),
        P("ctx", None),
        P("ctx", None),
        P(None, "exp"),
        P(),
        P("exp", "ctx"),
        P("exp"),
        P("exp"),
        P("ctx", "exp"),
        P("ctx", None),
        P("exp", None, "ctx"),
        P("exp", None, "ctx"),
    )
    out_specs = (P("ctx", "exp"), P("exp", None, "ctx"))
    return jax.shard_map(
        on_device, mesh=mesh, in_specs=in_specs, out_specs=out_specs, check_vma=False
    )
```

profile of v0, /device:TPU:24, one launch (start us, length us, event | category | flops | bytes accessed | tf_op | source)
XLA Modules:
  0.0 207.9 jit_solution(15309870306759046111)
XLA Ops:
  7.3 0.9 copy.40
  9.3 11.4 %all_to_all.15 = bf16[4,64,1024]{2,1,0:T(8,128)(2,1)S(1)} all-to-all(bf16[4,64,1024]{2,1,0:T(8,128)(2,1)S(1)} %bitcast.78), channel_id=1, replica_groups=mesh['ctx'=8,'exp'=4] {'exp'}, dimensions={0} | all-to-all | bytes 1048576 | tf_op jit(solution)/shard_map/all_to_all | solution.py:138
  21.2 1.0 copy.46
  22.2 3.4 %collective-permute-start.3 = (bf16[3,128]{1,0:T(4,128)(2,1)S(1)}, bf16[3,128]{1,0:T(4,128)(2,1)S(1)}, u32[]{:S(2)}, u32[]{:S(2)}) collective-permute-start(bf16[3,128]{1,0:T(4,128)(2,1)S(1)} %slice.82), channel_id=1, source_target_pairs={{0,4},{4,8},{8,12},{12,16},{16,20},{20,24},{24,28},{1,5},{5,9},{9,... | collective-permute-start | bytes 2312 | tf_op jit(solution)/shard_map/ppermute | solution.py:18
  25.6 1.9 collective-permute-start.2
  27.6 1.9 collective-permute-start.1
  29.5 0.6 reduce-window.12
  30.9 1.0 collective-permute-done.2
  32.6 1.5 collective-permute-done.1
  34.1 0.7 divide_multiply_fusion
  35.1 1.0 convolution_add_fusion
  36.1 4.8 %fusion.17 = f32[256,16,64]{0,2,1:T(8,128)S(1)} fusion(f32[256,256]{1,0:T(8,128)S(1)} %fusion.40, f32[16,256]{1,0:T(8,128)S(1)} %copy_bitcast_fusion, pred[256,256]{1,0:T(8,128)(4,1)S(1)} %iota_compare_fusion, f32[256,16,64]{0,2,1:T(8,128)S(1)} %bitcast.74, f32[256,16]{0,1:T(8,128)S(1)} %get-tuple-element.78), kind=kOutput, calls=%fused_computation.17 | convolution fusion | flops 809762816 | bytes 2457600 | tf_op jit(solution)/shard_map/while/body/eval_jaxpr/hts,shp->thp/dot_general | solution.py:39
  41.0 2.0 fusion.22
  43.0 136.1 %while.2 = (s32[]{:T(128)}, f32[16,64,128]{2,1,0:T(8,128)S(1)}, f32[16]{0:T(128)S(1)}, f32[16,64,128]{2,1,0:T(8,128)S(1)}, s32[]{:T(128)}) while((s32[]{:T(128)}, f32[16,64,128]{2,1,0:T(8,128)S(1)}, f32[16]{0:T(128)S(1)}, f32[16,64,128]{2,1,0:T(8,128)S(1)}, s32[]{:T(128)}) %tuple.40), condition=%wide.region_4.5_spmd, body=%wide.region_3.4_spmd.sunk | while | flops 262146 | bytes 3670181 | solution.py:116
  43.1 1.9 collective-permute-start
  45.1 20.3 %collective-permute-done = f32[16,64,128]{2,1,0:T(8,128)S(1)} collective-permute-done((f32[16,64,128]{2,1,0:T(8,128)S(1)}, f32[16,64,128]{2,1,0:T(8,128)S(1)}, u32[]{:S(2)}, u32[]{:S(2)}) %collective-permute-start) | collective-permute-done | bytes 524320 | tf_op jit(solution)/shard_map/while/body/eval_jaxpr/ppermute | solution.py:18
  65.5 1.9 collective-permute-start
  67.4 27.8 %collective-permute-done = f32[16,64,128]{2,1,0:T(8,128)S(1)} collective-permute-done((f32[16,64,128]{2,1,0:T(8,128)S(1)}, f32[16,64,128]{2,1,0:T(8,128)S(1)}, u32[]{:S(2)}, u32[]{:S(2)}) %collective-permute-start) | collective-permute-done | bytes 524320 | tf_op jit(solution)/shard_map/while/body/eval_jaxpr/ppermute | solution.py:18
  95.4 1.9 collective-permute-start
  97.3 20.4 %collective-permute-done = f32[16,64,128]{2,1,0:T(8,128)S(1)} collective-permute-done((f32[16,64,128]{2,1,0:T(8,128)S(1)}, f32[16,64,128]{2,1,0:T(8,128)S(1)}, u32[]{:S(2)}, u32[]{:S(2)}) %collective-permute-start) | collective-permute-done | bytes 524320 | tf_op jit(solution)/shard_map/while/body/eval_jaxpr/ppermute | solution.py:18
  117.9 1.9 collective-permute-start
  119.8 14.6 %collective-permute-done = f32[16,64,128]{2,1,0:T(8,128)S(1)} collective-permute-done((f32[16,64,128]{2,1,0:T(8,128)S(1)}, f32[16,64,128]{2,1,0:T(8,128)S(1)}, u32[]{:S(2)}, u32[]{:S(2)}) %collective-permute-start) | collective-permute-done | bytes 524320 | tf_op jit(solution)/shard_map/while/body/eval_jaxpr/ppermute | solution.py:18
  134.5 1.9 collective-permute-start
  136.5 13.7 %collective-permute-done = f32[16,64,128]{2,1,0:T(8,128)S(1)} collective-permute-done((f32[16,64,128]{2,1,0:T(8,128)S(1)}, f32[16,64,128]{2,1,0:T(8,128)S(1)}, u32[]{:S(2)}, u32[]{:S(2)}) %collective-permute-start) | collective-permute-done | bytes 524320 | tf_op jit(solution)/shard_map/while/body/eval_jaxpr/ppermute | solution.py:18
  150.3 1.9 collective-permute-start
  152.3 12.8 %collective-permute-done = f32[16,64,128]{2,1,0:T(8,128)S(1)} collective-permute-done((f32[16,64,128]{2,1,0:T(8,128)S(1)}, f32[16,64,128]{2,1,0:T(8,128)S(1)}, u32[]{:S(2)}, u32[]{:S(2)}) %collective-permute-start) | collective-permute-done | bytes 524320 | tf_op jit(solution)/shard_map/while/body/eval_jaxpr/ppermute | solution.py:18
  165.2 1.9 collective-permute-start
  167.2 11.9 %collective-permute-done = f32[16,64,128]{2,1,0:T(8,128)S(1)} collective-permute-done((f32[16,64,128]{2,1,0:T(8,128)S(1)}, f32[16,64,128]{2,1,0:T(8,128)S(1)}, u32[]{:S(2)}, u32[]{:S(2)}) %collective-permute-start) | collective-permute-done | bytes 524320 | tf_op jit(solution)/shard_map/while/body/eval_jaxpr/ppermute | solution.py:18
  179.1 2.3 %multiply_reduce_fusion = (f32[256,16]{0,1:T(8,128)S(1)}, f32[256,16,64]{0,2,1:T(8,128)S(1)}) fusion(f32[256,16,64]{0,2,1:T(8,128)S(1)} %bitcast.75, f32[16]{0:T(128)S(1)} %copy-done.8, f32[256,16,64]{0,2,1:T(8,128)} %fusion.22, f32[256,16]{0,1:T(8,128)S(1)} %get-tuple-element.63, f32[16,64,128]{2,1,0:T(8,128)S(1)} %get-tuple-element.45, ...), kind=kOutput, calls=%fused_computation.28 | convolution fusion | flops 404221952 | bytes 3834368 | tf_op jit(solution)/shard_map/tn,hpn->thp/dot_general | solution.py:118
  181.7 1.0 copy.43
  182.7 9.3 %fusion.2 = f32[512,1024]{1,0:T(8,128)S(1)} fusion(bf16[512,4096]{1,0:T(8,128)(2,1)} %all-gather.2.cloned.1.call-done, bf16[1,4096,1024]{2,1,0:T(8,128)(2,1)} %param.24), kind=kOutput, calls=%fused_computation.3 | convolution fusion | flops 4294967296 | bytes 14680064 | tf_op jit(solution)/shard_map/dot_general | solution.py:48
  192.0 9.1 %fusion.23 = bf16[1,512,1024]{2,1,0:T(8,128)(2,1)} fusion(bf16[512,4096]{1,0:T(8,128)(2,1)S(1)} %copy-done.9, bf16[1,4096,1024]{2,1,0:T(8,128)(2,1)} %param.25, f32[512,1024]{1,0:T(8,128)S(1)} %fusion.2), kind=kOutput, calls=%fused_computation.23 | convolution fusion | flops 4298113024 | bytes 15728640 | tf_op jit(solution)/shard_map/dot_general | solution.py:49
  (66 shorter events, 4.4 us)
Async XLA Ops:
  7.2 1.9 copy-start
  7.2 15.0 %copy-start.3 = (bf16[256,128]{1,0:T(8,128)(2,1)S(1)}, bf16[256,128]{1,0:T(8,128)(2,1)}, u32[]{:S(2)}) copy-start(bf16[256,128]{1,0:T(8,128)(2,1)} %param.16) | copy-start | bytes 196612
  7.2 18.4 %copy-start.2 = (bf16[256,128]{1,0:T(8,128)(2,1)S(1)}, bf16[256,128]{1,0:T(8,128)(2,1)}, u32[]{:S(2)}) copy-start(bf16[256,128]{1,0:T(8,128)(2,1)} %param.15) | copy-start | bytes 196612
  7.2 20.3 %copy-start.1 = (bf16[256,1024]{1,0:T(8,128)(2,1)S(1)}, bf16[256,1024]{1,0:T(8,128)(2,1)}, u32[]{:S(2)}) copy-start(bf16[256,1024]{1,0:T(8,128)(2,1)} %param.14) | copy-start | bytes 1572868
  7.2 22.3 %copy-start.4 = (f32[16,256]{1,0:T(8,128)S(1)}, f32[16,256]{1,0:T(8,128)}, u32[]{:S(2)}) copy-start(f32[16,256]{1,0:T(8,128)} %param.19) | copy-start | bytes 49156
  7.2 23.4 %copy-start.7 = (f32[4,256]{1,0:T(4,128)S(1)}, f32[4,256]{1,0:T(4,128)}, u32[]{:S(2)}) copy-start(f32[4,256]{1,0:T(4,128)} %param.18) | copy-start | bytes 12292
  7.2 23.4 %copy-start.5 = (f32[4,1024]{1,0:T(4,128)S(1)}, f32[4,1024]{1,0:T(4,128)}, u32[]{:S(2)}) copy-start(f32[4,1024]{1,0:T(4,128)} %param.17) | copy-start | bytes 49156
  7.2 23.6 %copy-start.6 = (f32[1024]{0:T(1024)S(1)}, f32[1024]{0:T(1024)}, u32[]{:S(2)}) copy-start(f32[1024]{0:T(1024)} %param.21) | copy-start | bytes 12292
  7.3 175.4 %all-gather.2.cloned.1.call-start = ((), (), s32[]{:S(2)}) async-start(), calls=%async_computation.1 | async-start | bytes 4718592 | tf_op jit(solution)/shard_map/all_gather | solution.py:139
  22.2 8.8 %collective-permute-start.3 = (bf16[3,128]{1,0:T(4,128)(2,1)S(1)}, bf16[3,128]{1,0:T(4,128)(2,1)S(1)}, u32[]{:S(2)}, u32[]{:S(2)}) collective-permute-start(bf16[3,128]{1,0:T(4,128)(2,1)S(1)} %slice.82), channel_id=1, source_target_pairs={{0,4},{4,8},{8,12},{12,16},{16,20},{20,24},{24,28},{1,5},{5,9},{9,... | collective-permute-start | bytes 2312 | tf_op jit(solution)/shard_map/ppermute | solution.py:18
  25.6 6.4 %collective-permute-start.2 = (bf16[3,128]{1,0:T(4,128)(2,1)S(1)}, bf16[3,128]{1,0:T(4,128)(2,1)S(1)}, u32[]{:S(2)}, u32[]{:S(2)}) collective-permute-start(bf16[3,128]{1,0:T(4,128)(2,1)S(1)} %slice.81), channel_id=1, source_target_pairs={{0,4},{4,8},{8,12},{12,16},{16,20},{20,24},{24,28},{1,5},{5,9},{9,... | collective-permute-start | bytes 2312 | tf_op jit(solution)/shard_map/ppermute | solution.py:18
  27.6 6.6 %collective-permute-start.1 = (bf16[3,1024]{1,0:T(4,128)(2,1)S(1)}, bf16[3,1024]{1,0:T(4,128)(2,1)S(1)}, u32[]{:S(2)}, u32[]{:S(2)}) collective-permute-start(bf16[3,1024]{1,0:T(4,128)(2,1)S(1)} %slice.71), channel_id=1, source_target_pairs={{0,4},{4,8},{8,12},{12,16},{16,20},{20,24},{24,28},{1,5},{5,9},{9,... | collective-permute-start | bytes 18440 | tf_op jit(solution)/shard_map/ppermute | solution.py:18
  42.9 136.2 %copy-start.8 = (f32[16]{0:T(128)S(1)}, f32[16]{0:T(128)}, u32[]{:S(2)}) copy-start(f32[16]{0:T(128)} %param.20) | copy-start | bytes 196
  43.1 22.2 %collective-permute-start = (f32[16,64,128]{2,1,0:T(8,128)S(1)}, f32[16,64,128]{2,1,0:T(8,128)S(1)}, u32[]{:S(2)}, u32[]{:S(2)}) collective-permute-start(f32[16,64,128]{2,1,0:T(8,128)S(1)} %multiply_add_fusion.2), channel_id=1, source_target_pairs={{0,4},{4,8},{8,12},{12,16},{16,20},{20,24},{24,28},{1,5},{5,9},{9,... | collective-permute-start | bytes 1572872 | tf_op jit(solution)/shard_map/while/body/eval_jaxpr/ppermute | solution.py:18
  65.5 29.8 %collective-permute-start = (f32[16,64,128]{2,1,0:T(8,128)S(1)}, f32[16,64,128]{2,1,0:T(8,128)S(1)}, u32[]{:S(2)}, u32[]{:S(2)}) collective-permute-start(f32[16,64,128]{2,1,0:T(8,128)S(1)} %multiply_add_fusion.2), channel_id=1, source_target_pairs={{0,4},{4,8},{8,12},{12,16},{16,20},{20,24},{24,28},{1,5},{5,9},{9,... | collective-permute-start | bytes 1572872 | tf_op jit(solution)/shard_map/while/body/eval_jaxpr/ppermute | solution.py:18
  95.4 22.3 %collective-permute-start = (f32[16,64,128]{2,1,0:T(8,128)S(1)}, f32[16,64,128]{2,1,0:T(8,128)S(1)}, u32[]{:S(2)}, u32[]{:S(2)}) collective-permute-start(f32[16,64,128]{2,1,0:T(8,128)S(1)} %multiply_add_fusion.2), channel_id=1, source_target_pairs={{0,4},{4,8},{8,12},{12,16},{16,20},{20,24},{24,28},{1,5},{5,9},{9,... | collective-permute-start | bytes 1572872 | tf_op jit(solution)/shard_map/while/body/eval_jaxpr/ppermute | solution.py:18
  117.9 16.5 %collective-permute-start = (f32[16,64,128]{2,1,0:T(8,128)S(1)}, f32[16,64,128]{2,1,0:T(8,128)S(1)}, u32[]{:S(2)}, u32[]{:S(2)}) collective-permute-start(f32[16,64,128]{2,1,0:T(8,128)S(1)} %multiply_add_fusion.2), channel_id=1, source_target_pairs={{0,4},{4,8},{8,12},{12,16},{16,20},{20,24},{24,28},{1,5},{5,9},{9,... | collective-permute-start | bytes 1572872 | tf_op jit(solution)/shard_map/while/body/eval_jaxpr/ppermute | solution.py:18
  134.5 15.7 %collective-permute-start = (f32[16,64,128]{2,1,0:T(8,128)S(1)}, f32[16,64,128]{2,1,0:T(8,128)S(1)}, u32[]{:S(2)}, u32[]{:S(2)}) collective-permute-start(f32[16,64,128]{2,1,0:T(8,128)S(1)} %multiply_add_fusion.2), channel_id=1, source_target_pairs={{0,4},{4,8},{8,12},{12,16},{16,20},{20,24},{24,28},{1,5},{5,9},{9,... | collective-permute-start | bytes 1572872 | tf_op jit(solution)/shard_map/while/body/eval_jaxpr/ppermute | solution.py:18
  150.3 14.8 %collective-permute-start = (f32[16,64,128]{2,1,0:T(8,128)S(1)}, f32[16,64,128]{2,1,0:T(8,128)S(1)}, u32[]{:S(2)}, u32[]{:S(2)}) collective-permute-start(f32[16,64,128]{2,1,0:T(8,128)S(1)} %multiply_add_fusion.2), channel_id=1, source_target_pairs={{0,4},{4,8},{8,12},{12,16},{16,20},{20,24},{24,28},{1,5},{5,9},{9,... | collective-permute-start | bytes 1572872 | tf_op jit(solution)/shard_map/while/body/eval_jaxpr/ppermute | solution.py:18
  165.2 13.8 %collective-permute-start = (f32[16,64,128]{2,1,0:T(8,128)S(1)}, f32[16,64,128]{2,1,0:T(8,128)S(1)}, u32[]{:S(2)}, u32[]{:S(2)}) collective-permute-start(f32[16,64,128]{2,1,0:T(8,128)S(1)} %multiply_add_fusion.2), channel_id=1, source_target_pairs={{0,4},{4,8},{8,12},{12,16},{16,20},{20,24},{24,28},{1,5},{5,9},{9,... | collective-permute-start | bytes 1572872 | tf_op jit(solution)/shard_map/while/body/eval_jaxpr/ppermute | solution.py:18
  182.7 9.3 %copy-start.9 = (bf16[512,4096]{1,0:T(8,128)(2,1)S(1)}, bf16[512,4096]{1,0:T(8,128)(2,1)}, u32[]{:S(2)}) copy-start(bf16[512,4096]{1,0:T(8,128)(2,1)} %all-gather.2.cloned.1.call-done) | copy-start | bytes 12582916
Sparse Core Ops, SparseCore 0:
  22.3 85.4 all-gather.1
where the time goes:
time: 208 us
  waiting for transfers between devices  124 us (60%)
  matrix products  29.3 us (14%)
  starting transfers between devices  20.7 us (10%)
  between operations  14.4 us (7%)
  blocking collectives  11.4 us (5%)
  local copies, waits for them, and re-layouts  4.37 us (2%)
  other arithmetic  3.29 us (2%)
    ppermute x10, waiting for transfers between devices, passed_along(): return lax.ppermute(block, axis, route)  124 us
    ppermute x10, starting transfers between devices, passed_along(): return lax.ppermute(block, axis, route)  20.7 us
    all_to_all x1, blocking collectives, on_device(): lax.all_to_all(slots, 'exp', split_axis=0, concat_axis=2, tiled=True)  11.4 us
    dot_general x1, matrix products, expert_product(): gate = jnp.dot(rows, gate_w, preferred_element_type=jnp.float32)  9.32 us
    dot_general x1, matrix products, expert_product(): upper = jnp.dot(rows, up_w, preferred_element_type=jnp.float32)  9.09 us
    dot_general x1, matrix products, ssd_block(): jnp.einsum('hts,shp->thp', decay * intersection[None], drive, precision=H...  4.83 us
  transfers between devices with their start and end apart: 11, of which 9 were waited for; matrix products, arithmetic and copies ran while one was open for 7% of the time, Pallas kernels for 0%

commit v1 on v0

v1 whole, which is shorter than its diff:
```python
import jax
import jax.numpy as jnp
from jax import lax
from jax.sharding import PartitionSpec as P

HDIM = 64
STATE = 128
KCONV = 4

HIGH = lax.Precision.HIGHEST


def passed_along(block, axis, distance):
    devices = range(lax.axis_size(axis))
    route = [(i - distance, i) for i in devices if i - distance in devices]
    return lax.ppermute(block, axis, route)


def swapped(block, bit):
    return lax.ppermute(block, "exp", [(i, i ^ bit) for i in range(lax.axis_size("exp"))])


def causal_conv(padded, weights):
    length = padded.shape[0] - weights.shape[0] + 1
    total = jnp.zeros((length, padded.shape[1]), jnp.float32)
    for offset in range(weights.shape[0]):
        total = total + weights[offset][None, :] * padded[offset : offset + length].astype(
            jnp.float32
        )
    return jax.nn.silu(total)


def slot_matrix(pairs, expert, capacity):
    tokens = pairs.shape[0]
    named = jnp.any(pairs == expert, axis=1).astype(jnp.int32)
    position = jnp.cumsum(named) - named
    hit = (position[None, :] == jnp.arange(capacity, dtype=jnp.int32)[:, None]) & (
        named[None, :] > 0
    )
    return hit.astype(jnp.bfloat16)


def three_parts(value):
    high = lax.reduce_precision(value, 8, 7)
    rest = value - high
    middle = lax.reduce_precision(rest, 8, 7)
    low = rest - middle
    return jnp.stack([high, middle, low]).astype(jnp.bfloat16)


def experts_by_tokens(tokens, pairs, w_gate, w_up):
    blocks, rows, columns = tokens.shape
    me = lax.axis_index("exp")
    own = tokens.reshape(blocks * rows, columns)
    across = swapped(own, 2)
    beside = swapped(own, 1)
    corner = swapped(across, 1)
    whole = jnp.zeros((4,) + own.shape, own.dtype)
    for bit, piece in enumerate((own, beside, across, corner)):
        whole = lax.dynamic_update_slice(whole, piece[None], (me ^ bit, 0, 0))
    whole = whole.transpose(1, 0, 2).reshape(blocks * rows, 4 * columns)
    gate = jnp.dot(whole, w_gate[0], preferred_element_type=jnp.float32)
    upper = jnp.dot(whole, w_up[0], preferred_element_type=jnp.float32)
    hidden = (jax.nn.silu(gate) * upper).astype(jnp.bfloat16)
    pick = jax.vmap(lambda p: slot_matrix(p, me, rows))(pairs)
    slots = jnp.einsum(
        "bqt,btf->bqf",
        pick,
        hidden.reshape(blocks, rows, -1),
        preferred_element_type=jnp.float32,
    )
    return slots.astype(jnp.bfloat16).reshape(1, blocks * rows, -1)


def experts_by_slots(moe_input, pairs, w_gate, w_up):
    experts = lax.axis_size("exp")
    tokens, columns = moe_input.shape
    capacity = 4 * tokens // experts
    pick = jax.vmap(lambda e: slot_matrix(pairs, e, capacity))(jnp.arange(experts))
    slots = jnp.einsum("eqt,td->eqd", pick, moe_input, preferred_element_type=jnp.float32)
    routed = lax.all_to_all(
        slots.astype(jnp.bfloat16), "exp", split_axis=0, concat_axis=2, tiled=True
    )
    rows = lax.all_gather(routed[0], "ctx", axis=0, tiled=True)
    gate = jnp.dot(rows, w_gate[0], preferred_element_type=jnp.float32)
    upper = jnp.dot(rows, w_up[0], preferred_element_type=jnp.float32)
    return (jax.nn.silu(gate) * upper).astype(jnp.bfloat16)[None]


def on_device(
    seq_input,
    b_input,
    c_input,
    conv_x,
    conv_bc,
    log_decay,
    skip_gain,
    norm_gain,
    moe_input,
    expert_ids,
    w_gate,
    w_up,
):
    rim = KCONV - 1
    tokens, channels = seq_input.shape
    heads = skip_gain.shape[0]
    ctx = lax.axis_size("ctx")
    me = lax.axis_index("ctx")
    rows = moe_input.shape[0]
    by_tokens = lax.axis_size("exp") == 4

    extra = jnp.zeros((8, moe_input.shape[1]), jnp.bfloat16)
    extra = extra.at[0, : 2 * rows].set(expert_ids.reshape(-1).astype(jnp.bfloat16))
    extra = extra.at[1:4, :heads].set(three_parts(jnp.sum(log_decay, axis=1)))
    sent = jnp.concatenate([moe_input, extra], 0) if by_tokens else extra
    gathered = lax.all_gather(sent, "ctx", axis=0)
    lines = gathered[:, -8:]
    sums = jnp.sum(lines[:, 1:4, :heads].astype(jnp.float32), axis=1)

    ends = jnp.concatenate([a[tokens - rim :] for a in (seq_input, b_input, c_input)], 1)
    before = passed_along(ends, "ctx", 1)
    xconv = causal_conv(jnp.concatenate([before[:, :channels], seq_input], 0), conv_x)
    both = jnp.concatenate([before[:, channels:], jnp.concatenate([b_input, c_input], 1)], 0)
    bc = causal_conv(both, conv_bc)
    bconv = bc[:, :STATE]
    cconv = bc[:, STATE:]
    xheads = xconv.reshape(tokens, heads, HDIM)
    drive = xheads * jnp.sqrt(-jnp.expm1(2.0 * log_decay)).T[:, :, None]
    within = jnp.cumsum(log_decay, axis=1)
    remain = jnp.exp(within[:, -1:] - within)
    final = jnp.einsum("thp,tn->hpn", drive * remain.T[:, :, None], bconv, precision=HIGH)

    share = heads * HDIM // ctx
    parts = lax.all_to_all(
        final.reshape(ctx, share, STATE), "ctx", split_axis=0, concat_axis=0, tiled=True
    )
    through = jnp.repeat(jnp.exp(sums), HDIM, axis=1)
    through = lax.dynamic_slice(through, (0, me * share), (ctx, share))
    state = jnp.zeros_like(parts[0])
    starts = [state]
    for i in range(ctx - 1):
        state = through[i][:, None] * state + parts[i]
        starts.append(state)
    incoming = lax.all_to_all(
        jnp.stack(starts), "ctx", split_axis=0, concat_axis=0, tiled=True
    ).reshape(heads, HDIM, STATE)

    lower = jnp.tril(jnp.ones((tokens, tokens), dtype=bool))[None]
    gaps = within[:, :, None] - within[:, None, :]
    decay = jnp.where(lower, jnp.exp(jnp.where(lower, gaps, 0.0)), 0.0)
    meet = jnp.dot(cconv, bconv.T, precision=HIGH, preferred_element_type=jnp.float32)
    inner = jnp.einsum("hts,shp->thp", decay * meet[None], drive, precision=HIGH)
    carried = jnp.einsum("tn,hpn->thp", cconv, incoming, precision=HIGH)
    carried = carried * jnp.exp(within).T[:, :, None]
    pre = inner + carried + skip_gain[None, :, None] * xheads
    scale = lax.rsqrt(jnp.mean(pre * pre, axis=2, keepdims=True) + 1e-05)
    mixed = (
        (pre * scale * norm_gain.reshape(heads, HDIM)[None])
        .reshape(tokens, channels)
        .astype(jnp.bfloat16)
    )

    if by_tokens:
        pairs = lines[:, 0, : 2 * rows].astype(jnp.int32).reshape(ctx, rows, 2)
        hidden = experts_by_tokens(gathered[:, :rows], pairs, w_gate, w_up)
    else:
        hidden = experts_by_slots(moe_input, expert_ids, w_gate, w_up)
    return (mixed, hidden)


def solution(mesh):
    in_specs = (
        P("ctx", "exp"),
        P("ctx", None),
        P("ctx", None),
        P(None, "exp"),
        P(),
        P("exp", "ctx"),
        P("exp"),
        P("exp"),
        P("ctx", "exp"),
        P("ctx", None),
        P("exp", None, "ctx"),
        P("exp", None, "ctx"),
    )
    out_specs = (P("ctx", "exp"), P("exp", None, "ctx"))
    return jax.shard_map(
        on_device, mesh=mesh, in_specs=in_specs, out_specs=out_specs, check_vma=False
    )
```

time: 208 us -> 120 us (0.58)
  the two profiles are of different devices: /device:TPU:24 before, /device:TPU:0 now
where the time goes in v1:
time: 120 us; the launch traced here: 119 us
  waiting for transfers between devices  27.9 us (23%)
  matrix products  25.9 us (22%)
  local copies, waits for them, and re-layouts  22.3 us (19%)
  starting transfers between devices  15.6 us (13%)
  between operations  14.3 us (12%)
  other arithmetic  13.3 us (11%)
    all_gather x1, waiting for transfers between devices, on_device(): gathered = lax.all_gather(sent, 'ctx', axis=0)  23.9 us
    dot_general x1, matrix products, experts_by_tokens(): gate = jnp.dot(whole, w_gate[0], preferred_element_type=jnp.float32)  9.23 us
    dot_general x1, matrix products, on_device(): jnp.einsum('hts,shp->thp', decay * meet[None], drive, precision=HIGH)  5.84 us
    all_to_all x1, starting transfers between devices, on_device(): lax.all_to_all(final.reshape(ctx, share, STATE), 'ctx', split_axis=0, con...  4.88 us
    ppermute x1, starting transfers between devices, passed_along(): return lax.ppermute(block, axis, route)  4.84 us
    dot_general x1, matrix products, experts_by_tokens(): upper = jnp.dot(whole, w_up[0], preferred_element_type=jnp.float32)  4.76 us
    all_to_all x1, starting transfers between devices, on_device(): lax.all_to_all(jnp.stack(starts), 'ctx', split_axis=0, concat_axis=0, til...  4.62 us
    broadcast_in_dim x3, local copies, waits for them, and re-layouts, experts_by_tokens(): whole = lax.dynamic_update_slice(whole, piece[None], (me ^ bit, 0, 0))  4.48 us
  transfers between devices with their start and end apart: 7, of which 3 were waited for; matrix products, arithmetic and copies ran while one was open for 30% of the time, Pallas kernels for 0%

profile of v1, /device:TPU:0, one launch (start us, length us, event | category | flops | bytes accessed | tf_op | source)
XLA Modules:
  0.0 119.2 jit_solution(8003316771513939249)
XLA Ops:
  9.0 0.9 exponential_bitcast_fusion
  11.2 1.6 %pad_maximum_fusion.1 = bf16[72,1024]{1,0:T(8,128)(2,1)} fusion(bf16[8,1024]{1,0:T(8,128)(2,1)S(1)} %scatter.9, bf16[64,1024]{1,0:T(8,128)(2,1)} %param.24), kind=kLoop, calls=%fused_computation.38 | loop fusion | flops 294912 | bytes 294912 | tf_op jit(solution)/shard_map/concatenate | solution.py:115
  14.9 4.8 %collective-permute-start = (bf16[3,1280]{1,0:T(4,128)(2,1)S(1)}, bf16[3,1280]{1,0:T(4,128)(2,1)S(1)}, u32[]{:S(2)}, u32[]{:S(2)}) collective-permute-start(bf16[3,1280]{1,0:T(4,128)(2,1)S(1)} %pad_maximum_fusion.3), channel_id=1, source_target_pairs={{0,4},{4,8},{8,12},{12,16},{16,20},{20,24},{24,28},{1,5},{5,9},{9,... | collective-permute-start | bytes 23048 | tf_op jit(solution)/shard_map/ppermute | solution.py:16
  19.7 0.8 fusion.46
  20.6 0.9 constant_dynamic-update-slice_fusion.1
  21.4 0.9 fusion.45
  22.3 0.9 constant_dynamic-update-slice_fusion
  23.2 2.7 %divide_multiply_fusion = f32[256,1024]{1,0:T(8,128)S(1)} fusion(bf16[256,1024]{1,0:T(8,128)(2,1)} %param.16, bf16[3,1024]{1,0:T(4,128)(2,1)S(1)} %slice.224, f32[1024]{0:T(1024)S(1)} %bitcast.109, f32[1024]{0:T(1024)S(1)} %bitcast.110, f32[1024]{0:T(1024)S(1)} %bitcast.108, f32[1024]{0:T(1024)S(1)} %bitcast.107), kind=kLoop, calls=%fused_computation.23 | loop fusion | flops 6291456 | bytes 1595392 | tf_op jit(solution)/shard_map/jit(silu)/mul | solution.py:30
  26.6 1.8 %fusion.30 = f32[8,128,128]{2,1,0:T(8,128)} fusion(f32[8,128,256]{2,1,0:T(8,128)S(1)} %bitcast.100, f32[256,256]{1,0:T(8,128)S(1)} %divide_multiply_fusion.1), kind=kOutput, calls=%fused_computation.42 | convolution fusion | flops 402653184 | bytes 1703936 | tf_op jit(solution)/shard_map/thp,tn->hpn/dot_general | solution.py:131
  28.4 4.9 %all-to-all-start = ((f32[8,128,128]{2,1,0:T(8,128)}), f32[8,128,128]{2,1,0:T(8,128)S(1)}, u32[]{:S(2)}, u32[]{:S(2)}) async-start(f32[8,128,128]{2,1,0:T(8,128)} %fusion.30), calls=%async_computation | async-start | bytes 1048576 | tf_op jit(solution)/shard_map/all_to_all | solution.py:134
  34.4 23.9 %all-gather.3.cloned.1.call-done = bf16[576,1024]{1,0:T(8,128)(2,1)} async-done(((bf16[72,1024]{1,0:T(8,128)(2,1)}), bf16[576,1024]{1,0:T(8,128)(2,1)}) %all-gather.3.cloned.1.call-update) | async-done | bytes 1179664 | tf_op jit(solution)/shard_map/all_gather | solution.py:116
  58.3 1.3 %slice.247 = bf16[8,64,1024]{2,1,0:T(8,128)(2,1)S(1)} slice(bf16[8,72,1024]{2,1,0:T(8,128)(2,1)} %bitcast.104), slice={[0:8], [0:64], [0:1024]} | slice | bytes 2097152 | tf_op jit(solution)/shard_map/slice | solution.py:165
  59.6 1.2 %collective-permute-start.2 = (bf16[512,1024]{1,0:T(8,128)(2,1)S(1)}, bf16[512,1024]{1,0:T(8,128)(2,1)}, u32[]{:S(2)}, u32[]{:S(2)}) collective-permute-start(bf16[512,1024]{1,0:T(8,128)(2,1)S(1)} %bitcast.97), channel_id=1, source_target_pairs={{0,2},{1,3},{2,0},{3,1},{4,6},{5,7},{6,4},{7,5},{8,10},{9,11},{10,... | collective-permute-start | bytes 3145736 | tf_op jit(solution)/shard_map/ppermute | solution.py:20
  60.8 0.7 convert_reduce_fusion
  62.4 0.7 constant_dynamic-update-slice_fusion.6
  63.9 0.7 constant_dynamic-update-slice_fusion.4
  65.3 0.7 constant_dynamic-update-slice_fusion.2
  66.8 4.6 %all-to-all-start.1 = ((f32[8,128,128]{2,1,0:T(8,128)}), f32[8,128,128]{2,1,0:T(8,128)}, u32[]{:S(2)}, u32[]{:S(2)}) async-start(f32[8,128,128]{2,1,0:T(8,128)} %fusion.40), calls=%async_computation.1 | async-start | bytes 1048576 | tf_op jit(solution)/shard_map/all_to_all | solution.py:144
  71.4 5.8 %fusion.17 = f32[256,16,64]{0,2,1:T(8,128)} fusion(f32[256,256]{1,0:T(8,128)S(1)} %fusion.36, f32[16,256]{1,0:T(8,128)S(1)} %copy_bitcast_fusion, pred[256,256]{1,0:T(8,128)(4,1)S(1)} %iota_compare_fusion.1, f32[256,16,64]{0,2,1:T(8,128)S(1)} %bitcast.93, f32[256,16]{0,1:T(8,128)S(1)} %get-tuple-element.70), kind=kOutput, calls=%fused_computation.17 | convolution fusion | flops 809762816 | bytes 2457600 | tf_op jit(solution)/shard_map/hts,shp->thp/dot_general | solution.py:152
  79.3 1.9 %copy-done = bf16[4,512,1024]{1,2,0:T(8,128)(2,1)} copy-done((bf16[4,512,1024]{1,2,0:T(8,128)(2,1)}, bf16[4,512,1024]{1,2,0:T(8,128)(2,1)S(1)}, u32[]{:S(2)}) %copy-start) | copy-done | bytes 4194328
  81.5 3.3 %collective-permute-done.2 = bf16[512,1024]{1,0:T(8,128)(2,1)} collective-permute-done((bf16[512,1024]{1,0:T(8,128)(2,1)S(1)}, bf16[512,1024]{1,0:T(8,128)(2,1)}, u32[]{:S(2)}, u32[]{:S(2)}) %collective-permute-start.2) | collective-permute-done | bytes 1048608 | tf_op jit(solution)/shard_map/ppermute | solution.py:20
  85.5 2.5 %multiply_reduce_fusion = (f32[256,16]{0,1:T(8,128)S(1)}, f32[256,16,64]{0,2,1:T(8,128)S(1)}) fusion(f32[256,16,64]{0,2,1:T(8,128)S(1)} %bitcast.94, f32[16]{0:T(128)S(1)} %copy-done.3, f32[256,16,64]{0,2,1:T(8,128)} %fusion.17, f32[256,16]{0,1:T(8,128)S(1)} %get-tuple-element.44, f32[16,64,128]{2,1,0:T(8,128)} %bitcast.25, ...), kind=kOutput, calls=%fused_computation.22 | convolution fusion | flops 404221952 | bytes 3834368 | tf_op jit(solution)/shard_map/tn,hpn->thp/dot_general | solution.py:153
  88.2 1.0 copy.74
  89.2 1.5 %copy.71 = bf16[1,512,1024]{1,2,0:T(8,128)(2,1)S(1)} copy(bf16[1,512,1024]{2,1,0:T(8,128)(2,1)} %bitcast.30) | data formatting | bytes 2097152 | tf_op jit(solution)/shard_map/broadcast_in_dim | solution.py:60
  90.7 1.5 %copy.72 = bf16[1,512,1024]{1,2,0:T(8,128)(2,1)S(1)} copy(bf16[1,512,1024]{2,1,0:T(8,128)(2,1)} %bitcast.31) | data formatting | bytes 2097152 | tf_op jit(solution)/shard_map/broadcast_in_dim | solution.py:60
  92.2 1.1 constant_dynamic-update-slice_fusion.9
  93.3 1.1 constant_dynamic-update-slice_fusion.8
  94.4 1.5 %copy.73 = bf16[1,512,1024]{1,2,0:T(8,128)(2,1)S(1)} copy(bf16[1,512,1024]{2,1,0:T(8,128)(2,1)} %bitcast.32) | data formatting | bytes 2097152 | tf_op jit(solution)/shard_map/broadcast_in_dim | solution.py:60
  95.9 1.0 constant_dynamic-update-slice_fusion.7
  96.9 9.2 %fusion.2 = f32[512,1024]{1,0:T(8,128)S(1)} fusion(bf16[512,4096]{0,1:T(8,128)(2,1)} %bitcast.95, bf16[1,4096,1024]{2,1,0:T(8,128)(2,1)} %param.26), kind=kOutput, calls=%fused_computation.2 | convolution fusion | flops 4294967296 | bytes 14680064 | tf_op jit(solution)/shard_map/dot_general | solution.py:62
  106.2 4.8 %multiply_convert_fusion = bf16[512,1024]{1,0:T(8,128)(2,1)S(1)} fusion(f32[512,1024]{1,0:T(8,128)S(1)} %fusion.2, bf16[512,4096]{0,1:T(8,128)(2,1)S(1)} %bitcast.96, bf16[1,4096,1024]{2,1,0:T(8,128)(2,1)S(1)} %bitcast.116), kind=kOutput, calls=%fused_computation.10 | convolution fusion | flops 4298113024 | bytes 15728640 | tf_op jit(solution)/shard_map/dot_general | solution.py:63
  111.0 1.4 %convolution_convert_fusion = bf16[8,64,1024]{2,1,0:T(8,128)(2,1)} fusion(bf16[8,64,1024]{2,1,0:T(8,128)(2,1)S(1)} %bitcast.103, s32[8,64]{1,0:T(8,128)S(1)} %convert_subtract_fusion, pred[8,64]{1,0:T(8,128)(4,1)S(1)} %get-tuple-element.63), kind=kOutput, calls=%fused_computation.16 | convolution fusion | flops 67698688 | bytes 2099712 | tf_op jit(solution)/shard_map/bqt,btf->bqf/dot_general | solution.py:66
  (71 shorter events, 13.2 us)
Async XLA Ops:
  7.2 51.1 %all-gather.3.cloned.1.call-start = ((), (), s32[]{:S(2)}) async-start(), calls=%async_computation.2 | async-start | bytes 1327104 | tf_op jit(solution)/shard_map/all_gather | solution.py:116
  14.9 8.3 %collective-permute-start = (bf16[3,1280]{1,0:T(4,128)(2,1)S(1)}, bf16[3,1280]{1,0:T(4,128)(2,1)S(1)}, u32[]{:S(2)}, u32[]{:S(2)}) collective-permute-start(bf16[3,1280]{1,0:T(4,128)(2,1)S(1)} %pad_maximum_fusion.3), channel_id=1, source_target_pairs={{0,4},{4,8},{8,12},{12,16},{16,20},{20,24},{24,28},{1,5},{5,9},{9,... | collective-permute-start | bytes 23048 | tf_op jit(solution)/shard_map/ppermute | solution.py:16
  23.2 10.0 %copy-start.2 = (f32[1024]{0:T(1024)S(1)}, f32[1024]{0:T(1024)}, u32[]{:S(2)}) copy-start(f32[1024]{0:T(1024)} %param.23) | copy-start | bytes 12292
  28.4 33.3 %all-to-all-start = ((f32[8,128,128]{2,1,0:T(8,128)}), f32[8,128,128]{2,1,0:T(8,128)S(1)}, u32[]{:S(2)}, u32[]{:S(2)}) async-start(f32[8,128,128]{2,1,0:T(8,128)} %fusion.30), calls=%async_computation | async-start | bytes 1048576 | tf_op jit(solution)/shard_map/all_to_all | solution.py:134
  59.6 25.3 %collective-permute-start.2 = (bf16[512,1024]{1,0:T(8,128)(2,1)S(1)}, bf16[512,1024]{1,0:T(8,128)(2,1)}, u32[]{:S(2)}, u32[]{:S(2)}) collective-permute-start(bf16[512,1024]{1,0:T(8,128)(2,1)S(1)} %bitcast.97), channel_id=1, source_target_pairs={{0,2},{1,3},{2,0},{3,1},{4,6},{5,7},{6,4},{7,5},{8,10},{9,11},{10,... | collective-permute-start | bytes 3145736 | tf_op jit(solution)/shard_map/ppermute | solution.py:20
  66.8 18.7 %all-to-all-start.1 = ((f32[8,128,128]{2,1,0:T(8,128)}), f32[8,128,128]{2,1,0:T(8,128)}, u32[]{:S(2)}, u32[]{:S(2)}) async-start(f32[8,128,128]{2,1,0:T(8,128)} %fusion.40), calls=%async_computation.1 | async-start | bytes 1048576 | tf_op jit(solution)/shard_map/all_to_all | solution.py:144
  77.2 12.0 %collective-permute-start.1 = (bf16[512,1024]{1,0:T(8,128)(2,1)S(1)}, bf16[512,1024]{1,0:T(8,128)(2,1)}, u32[]{:S(2)}, u32[]{:S(2)}) collective-permute-start(bf16[512,1024]{1,0:T(8,128)(2,1)S(1)} %bitcast.98), channel_id=1, source_target_pairs={{0,1},{1,0},{2,3},{3,2},{4,5},{5,4},{6,7},{7,6},{8,9},{9,8},{10,11... | collective-permute-start | bytes 3145736 | tf_op jit(solution)/shard_map/ppermute | solution.py:20
  78.0 7.5 %copy-start.3 = (f32[16]{0:T(128)S(1)}, f32[16]{0:T(128)}, u32[]{:S(2)}) copy-start(f32[16]{0:T(128)} %param.22) | copy-start | bytes 196
  79.3 1.9 %copy-start = (bf16[4,512,1024]{1,2,0:T(8,128)(2,1)}, bf16[4,512,1024]{1,2,0:T(8,128)(2,1)S(1)}, u32[]{:S(2)}) copy-start(bf16[4,512,1024]{1,2,0:T(8,128)(2,1)S(1)} %constant_dynamic-update-slice_fusion.10) | copy-start | bytes 12582916
  84.8 9.5 %collective-permute-start.3 = (bf16[512,1024]{1,0:T(8,128)(2,1)}, bf16[512,1024]{1,0:T(8,128)(2,1)}, u32[]{:S(2)}, u32[]{:S(2)}) collective-permute-start(bf16[512,1024]{1,0:T(8,128)(2,1)} %collective-permute-done.2), channel_id=1, source_target_pairs={{0,1},{1,0},{2,3},{3,2},{4,5},{5,4},{6,7},{7,6},{8,9},{9,8},{10,11... | collective-permute-start | bytes 3145736 | tf_op jit(solution)/shard_map/ppermute | solution.py:20
  95.9 10.3 %slice-start = ((s8[8388608]{0:T(1024)(128)(4,1)}), s8[4194304]{0:T(1024)(128)(4,1)S(1)}, s32[]{:S(2)}) async-start(s8[8388608]{0:T(1024)(128)(4,1)} %bitcast.115), calls=%async_computation.3 | async-start | bytes 8388608
  96.9 9.3 %copy-start.1 = (bf16[4,512,1024]{1,2,0:T(8,128)(2,1)S(1)}, bf16[4,512,1024]{1,2,0:T(8,128)(2,1)}, u32[]{:S(2)}) copy-start(bf16[4,512,1024]{1,2,0:T(8,128)(2,1)} %constant_dynamic-update-slice_fusion.7) | copy-start | bytes 12582916
  96.9 9.3 %slice-start.1 = ((s8[8388608]{0:T(1024)(128)(4,1)}), s8[4194304]{0:T(1024)(128)(4,1)S(1)}, s32[]{:S(2)}) async-start(s8[8388608]{0:T(1024)(128)(4,1)} %bitcast.115), calls=%async_computation.4 | async-start | bytes 8388608
Sparse Core Ops, SparseCore 0:
  12.9 45.3 all-gather.2

commit v2 on v1

v2 whole, which is shorter than its diff:
```python
import functools

import jax
import jax.numpy as jnp
from jax import lax
from jax.experimental import pallas as pl
from jax.experimental.pallas import tpu as pltpu
from jax.sharding import PartitionSpec as P

HDIM = 64
STATE = 128
KCONV = 4
EDGE = 16
NOTES = 8

HIGH = lax.Precision.HIGHEST
F32 = jnp.float32
BF16 = jnp.bfloat16


def dot(a, b, contract=((1,), (0,))):
    return lax.dot_general(a, b, (contract, ((), ())), precision=HIGH, preferred_element_type=F32)


def dot16(a, b, contract=((1,), (0,))):
    return lax.dot_general(a, b, (contract, ((), ())), preferred_element_type=F32)


def halves(value):
    high = value.astype(BF16)
    return high, (value - high.astype(F32)).astype(BF16)


def iota(shape, axis):
    return lax.broadcasted_iota(jnp.int32, shape, axis)


def head_spread(heads):
    shape = (heads, heads * HDIM)
    return (iota(shape, 1) // HDIM == iota(shape, 0)).astype(F32)


def upper_ones(length):
    return (iota((length, length), 0) <= iota((length, length), 1)).astype(F32)


def silu(value):
    return value / (1.0 + jnp.exp(-value))


def full(shape):
    return pl.BlockSpec(shape, lambda *_: (0,) * len(shape))


def call(body, outs, args, specs=None, scratch=(), flops=0, name=None):
    moved = sum(a.size * a.dtype.itemsize for a in (*args, *outs))
    return pl.pallas_call(
        body,
        out_shape=outs,
        grid=(1,),
        in_specs=specs or [full(a.shape) for a in args],
        out_specs=[full(o.shape) for o in outs],
        scratch_shapes=list(scratch),
        compiler_params=pltpu.CompilerParams(vmem_limit_bytes=32 * 2**20),
        cost_estimate=pl.CostEstimate(flops=flops, bytes_accessed=moved, transcendentals=0),
        name=name,
    )(*args)


def pack_body(x_ref, b_ref, c_ref, moe_ref, ends_ref, copies_ref):
    channels = x_ref.shape[1]
    ends_ref[:, :channels] = x_ref[...]
    ends_ref[:, channels : channels + STATE] = b_ref[...]
    ends_ref[:, channels + STATE :] = c_ref[...]
    for i in range(copies_ref.shape[0]):
        copies_ref[i] = moe_ref[...]


def pack(seq_input, b_input, c_input, moe_input, copies):
    tokens, channels = seq_input.shape
    last = tokens // EDGE - 1
    args = (seq_input, b_input, c_input, moe_input)
    specs = [pl.BlockSpec((EDGE, a.shape[1]), lambda *_: (last, 0)) for a in args[:3]]
    specs.append(full(moe_input.shape))
    outs = [
        jax.ShapeDtypeStruct((EDGE, channels + 2 * STATE), BF16),
        jax.ShapeDtypeStruct((copies,) + moe_input.shape, BF16),
    ]
    return call(pack_body, outs, args, specs, name="pack")


def front_body(
    by_tokens,
    x_ref,
    b_ref,
    c_ref,
    ends_ref,
    taps_ref,
    taps_bc_ref,
    logs_ref,
    inflow_ref,
    skip_ref,
    ids_ref,
    drive_ref,
    direct_ref,
    bc_ref,
    slab_ref,
    pad_ref,
):
    tokens, channels = x_ref.shape
    heads = logs_ref.shape[0]
    pad_ref[0:8, :] = ends_ref[...].astype(F32)[EDGE - 8 : EDGE]
    pad_ref[8 : 8 + tokens, :channels] = x_ref[...].astype(F32)
    pad_ref[8 : 8 + tokens, channels : channels + STATE] = b_ref[...].astype(F32)
    pad_ref[8 : 8 + tokens, channels + STATE :] = c_ref[...].astype(F32)

    def conv(taps, start, stop):
        total = jnp.zeros((tokens, stop - start), F32)
        for k in range(KCONV):
            first = 8 - (KCONV - 1) + k
            total = total + taps[k : k + 1] * pad_ref[first : first + tokens, start:stop]
        return silu(total)

    bc = conv(taps_bc_ref[...], channels, channels + 2 * STATE)
    bc_ref[...] = bc
    bmat = bc[:, :STATE]

    logs = logs_ref[...]
    inflow = inflow_ref[...]
    within = dot(logs, upper_ones(tokens))
    total = within[:, tokens - 1 :]
    remain = jnp.exp(total - within)
    spread = head_spread(heads)
    xconv = conv(taps_ref[...], 0, channels)
    first = ((0,), (0,))
    drive_ref[...] = xconv * dot(inflow, spread, first)
    direct_ref[...] = xconv * dot(skip_ref[...], spread)
    state = dot(bmat, xconv * dot(inflow * remain, spread, first), first)
    notes = dot(jnp.exp(jnp.broadcast_to(total, (heads, NOTES))), spread, first)
    if not by_tokens:
        slab_ref[:STATE] = state
        slab_ref[STATE:] = notes
        return
    parts, _, share = slab_ref.shape
    ids = ids_ref[...].astype(F32)
    rows = ids.shape[0]
    shape = (rows, 2 * rows)
    column = jnp.where(iota(shape, 1) < rows, ids[:, 0:1], ids[:, 1:2])
    column = jnp.where(iota(shape, 1) % rows == iota(shape, 0), column, 0.0)
    line = jnp.sum(column, axis=0, keepdims=True)
    for i in range(parts):
        cut = slice(i * share, (i + 1) * share)
        slab_ref[i, :STATE] = state[:, cut]
        slab_ref[i, STATE:] = jnp.where(iota((NOTES, share), 0) == 1, line, notes[:, cut])


def inner_body(drive_ref, direct_ref, bc_ref, logs_ref, pre_ref):
    tokens = drive_ref.shape[0]
    heads = logs_ref.shape[0]
    logs = logs_ref[...]
    ones = upper_ones(tokens)
    row = dot(logs, ones)
    column = dot(ones, logs, ((0,), (1,)))
    meet = dot(bc_ref[:, STATE:], bc_ref[:, :STATE], ((1,), (1,)))
    lower = iota((tokens, tokens), 0) >= iota((tokens, tokens), 1)
    left = iota((tokens, 2 * HDIM), 1) < HDIM
    for pair in range(heads // 2):
        cut = slice(pair * 2 * HDIM, (pair + 1) * 2 * HDIM)
        d_high, d_low = halves(drive_ref[:, cut])
        both = []
        for h in (2 * pair, 2 * pair + 1):
            gap = column[:, h : h + 1] - row[h : h + 1, :]
            mix = jnp.where(lower, jnp.exp(gap), 0.0) * meet
            m_high, m_low = halves(mix)
            both.append(dot16(m_high, d_high) + dot16(m_high, d_low) + dot16(m_low, d_high))
        pre_ref[:, cut] = direct_ref[:, cut] + jnp.where(left, both[0], both[1])


def prefix_body(parts_ref, starts_ref):
    ctx, rows, share = starts_ref.shape
    state = jnp.zeros((rows, share), F32)
    for i in range(ctx):
        starts_ref[i] = state
        if i < ctx - 1:
            state = parts_ref[i, STATE : STATE + 1] * state + parts_ref[i, :STATE]


def back_body(cuts, pre_ref, start_ref, bc_ref, logs_ref, gain_ref, out_ref):
    tokens, channels = pre_ref.shape
    heads = logs_ref.shape[0]
    within = dot(logs_ref[...], upper_ones(tokens))
    decay = dot(jnp.exp(within), head_spread(heads), ((0,), (0,)))
    width = min(channels, 2 * HDIM)
    group = (iota((width, width), 0) // HDIM == iota((width, width), 1) // HDIM).astype(BF16)
    c_high, c_low = halves(bc_ref[:, STATE:])
    for i in range(channels // width):
        cut = slice(i * width, (i + 1) * width)
        s_high, s_low = halves(start_ref[i] if cuts else start_ref[:, cut])
        carried = dot16(c_high, s_high) + dot16(c_high, s_low) + dot16(c_low, s_high)
        pre = pre_ref[:, cut] + carried * decay[:, cut]
        q_high, q_low = halves(pre * pre)
        mean = (dot16(q_high, group) + dot16(q_low, group)) * (1.0 / HDIM)
        out_ref[:, cut] = (pre * lax.rsqrt(mean + 1e-05) * gain_ref[:, cut]).astype(BF16)


def mixing(seq_input, b_input, c_input, before, conv_x, conv_bc, log_decay, skip, gain, ids, flag):
    tokens, channels = seq_input.shape
    heads = skip.shape[0]
    ctx = lax.axis_size("ctx")
    share = channels // ctx
    cuts = share == 2 * HDIM
    inflow = jnp.sqrt(-jnp.expm1(2.0 * log_decay))
    square = jax.ShapeDtypeStruct((tokens, channels), F32)
    slabs = (ctx, STATE + NOTES, share) if cuts else (STATE + NOTES, channels)
    outs = [
        square,
        square,
        jax.ShapeDtypeStruct((tokens, 2 * STATE), F32),
        jax.ShapeDtypeStruct(slabs, F32),
    ]
    drive, direct, bc, slab = call(
        functools.partial(front_body, cuts),
        outs,
        (
            seq_input,
            b_input,
            c_input,
            before,
            conv_x,
            conv_bc,
            log_decay,
            inflow,
            skip.reshape(1, heads),
            ids,
        ),
        scratch=[pltpu.VMEM((8 + tokens, channels + 2 * STATE), F32)],
        flops=10**9,
        name="front",
    )
    if not cuts:
        slab = slab.reshape(STATE + NOTES, ctx, share).transpose(1, 0, 2)
    parts = lax.all_to_all(slab, "ctx", split_axis=0, concat_axis=0, tiled=True)
    starts = call(
        prefix_body,
        [jax.ShapeDtypeStruct((ctx, STATE, share), F32)],
        (parts,),
        flops=10**6,
        name="prefix",
    )[0]
    start = lax.all_to_all(starts, "ctx", split_axis=0, concat_axis=0, tiled=True)
    if not cuts:
        start = start.transpose(1, 0, 2).reshape(STATE, channels)
    pre = call(
        inner_body, [square], (drive, direct, bc, log_decay), flops=4 * 10**9, name="inner"
    )[0]
    mixed = call(
        functools.partial(back_body, cuts),
        [jax.ShapeDtypeStruct((tokens, channels), BF16)],
        (pre, start, bc, log_decay, gain.reshape(1, channels)),
        flops=10**9,
        name="back",
    )[0]
    return mixed, parts


def swapped(block, axis, bit):
    return lax.ppermute(block, axis, [(i, i ^ bit) for i in range(lax.axis_size(axis))])


def first_body(place_ref, z, x, cz, cx, g0, g1, u0, u1, gate_ref, up_ref):
    half = z.shape[0]
    for w0, w1, out in ((g0, g1, gate_ref), (u0, u1, up_ref)):
        out[:half] = dot16(z[...], w0[0]) + dot16(cz[...], w1[0])
        out[half:] = dot16(x[...], w0[0]) + dot16(cx[...], w1[0])


def second_body(
    place_ref, y, d0, d1, cy, cd0, cd1, gate_ref, up_ref, g0, g1, u0, u1, notes_ref, out_ref, hid
):
    half = y.shape[0]
    part = d0.shape[0]
    rows = hid.shape[0] // notes_ref.shape[0]
    me = place_ref[0]
    side = place_ref[1]
    for a, b, start in ((y, cy, 0), (d0, cd0, half), (d1, cd1, half + part)):
        cut = slice(start, start + a.shape[0])
        gate = gate_ref[cut] + dot16(a[...], g0[0]) + dot16(b[...], g1[0])
        upper = up_ref[cut] + dot16(a[...], u0[0]) + dot16(b[...], u1[0])
        hid[cut] = (silu(gate) * upper).astype(BF16)
    shape = (rows, rows)
    earlier = (iota(shape, 1) < iota(shape, 0)).astype(F32)
    across = iota(shape, 1)
    diagonal = iota(shape, 0) == across
    for place in range(hid.shape[0] // rows):
        z = place % (half // rows)
        block = 2 * z + (side if place * rows < half else 1 - side)
        line = notes_ref[block][1:2, :]
        named = (line[:, :rows] == me.astype(F32)) | (line[:, rows : 2 * rows] == me.astype(F32))
        named = named.astype(F32)
        column = jnp.sum(jnp.where(diagonal, named, 0.0), axis=1, keepdims=True)
        position = jnp.sum(earlier * named, axis=1, keepdims=True).astype(jnp.int32)
        pick = jnp.where(position == across, column, 0.0).astype(BF16)
        picked = dot16(pick, hid[place * rows : (place + 1) * rows], ((0,), (0,)))
        out_ref[0, pl.ds(pl.multiple_of(block * rows, rows), rows), :] = picked.astype(BF16)


def experts_by_tokens(copies, notes, w_gate, w_up):
    zs, rows, columns = copies.shape
    ctx = lax.axis_size("ctx")
    groups = [list(range(s, ctx, 2)) for s in range(2)]
    z = lax.all_to_all(
        copies, "ctx", split_axis=0, concat_axis=0, tiled=True, axis_index_groups=groups
    )
    z = z.reshape(zs * rows, columns)
    half = z.shape[0]
    x = swapped(z, "ctx", 1)
    y = swapped(z, "exp", 2)
    cz = swapped(z, "exp", 1)
    d0 = swapped(y[: half // 2], "ctx", 1)
    d1 = swapped(x[half // 2 :], "exp", 2)
    cx = swapped(x, "exp", 1)
    cy = swapped(y, "exp", 1)
    cd0 = swapped(d0, "exp", 1)
    cd1 = swapped(d1, "exp", 1)

    hidden = w_gate.shape[2]
    tile = min(256, hidden)
    place = jnp.stack([lax.axis_index("exp"), lax.axis_index("ctx") % 2]).astype(jnp.int32)

    def weight(bit):
        return pl.BlockSpec((1, columns, tile), lambda n, s: (0, s[0] ^ bit, n))

    def whole(array):
        return pl.BlockSpec(array.shape, lambda n, s: (0,) * array.ndim)

    def partial_sum():
        return pl.BlockSpec((2 * half, tile), lambda n, s: (0, n))

    flops = 2 * 2 * half * 2 * columns * hidden * 2
    sums = jax.ShapeDtypeStruct((2 * half, hidden), F32)
    gate, upper = pl.pallas_call(
        first_body,
        out_shape=[sums, sums],
        grid_spec=pltpu.PrefetchScalarGridSpec(
            num_scalar_prefetch=1,
            grid=(hidden // tile,),
            in_specs=[whole(a) for a in (z, x, cz, cx)]
            + [weight(0), weight(1), weight(0), weight(1)],
            out_specs=[partial_sum(), partial_sum()],
        ),
        compiler_params=pltpu.CompilerParams(vmem_limit_bytes=40 * 2**20),
        cost_estimate=pl.CostEstimate(flops=flops, bytes_accessed=14 * 2**20, transcendentals=0),
        name="first",
    )(place, z, x, cz, cx, w_gate, w_gate, w_up, w_up)
    line = pl.BlockSpec((ctx, NOTES, notes.shape[2]), lambda n, s: (0, STATE // NOTES, 0))
    return pl.pallas_call(
        second_body,
        out_shape=jax.ShapeDtypeStruct((1, 2 * half, hidden), BF16),
        grid_spec=pltpu.PrefetchScalarGridSpec(
            num_scalar_prefetch=1,
            grid=(hidden // tile,),
            in_specs=[whole(a) for a in (y, d0, d1, cy, cd0, cd1)]
            + [partial_sum(), partial_sum()]
            + [weight(2), weight(3), weight(2), weight(3), line],
            out_specs=pl.BlockSpec((1, 2 * half, tile), lambda n, s: (0, 0, n)),
            scratch_shapes=[pltpu.VMEM((2 * half, tile), BF16)],
        ),
        compiler_params=pltpu.CompilerParams(vmem_limit_bytes=40 * 2**20),
        cost_estimate=pl.CostEstimate(flops=flops, bytes_accessed=15 * 2**20, transcendentals=0),
        name="second",
    )(place, y, d0, d1, cy, cd0, cd1, gate, upper, w_gate, w_gate, w_up, w_up, notes)


def slot_matrix(pairs, expert, capacity):
    named = jnp.any(pairs == expert, axis=1).astype(jnp.int32)
    position = jnp.cumsum(named) - named
    hit = position[None, :] == jnp.arange(capacity, dtype=jnp.int32)[:, None]
    return (hit & (named[None, :] > 0)).astype(BF16)


def experts_by_slots(moe_input, pairs, w_gate, w_up):
    experts = lax.axis_size("exp")
    capacity = 4 * moe_input.shape[0] // experts
    pick = jax.vmap(lambda e: slot_matrix(pairs, e, capacity))(jnp.arange(experts))
    slots = jnp.einsum("eqt,td->eqd", pick, moe_input, preferred_element_type=F32)
    routed = lax.all_to_all(slots.astype(BF16), "exp", split_axis=0, concat_axis=2, tiled=True)
    rows = lax.all_gather(routed[0], "ctx", axis=0, tiled=True)
    gate = jnp.dot(rows, w_gate[0], preferred_element_type=F32)
    upper = jnp.dot(rows, w_up[0], preferred_element_type=F32)
    return (jax.nn.silu(gate) * upper).astype(BF16)[None]


def on_device(
    seq_input,
    b_input,
    c_input,
    conv_x,
    conv_bc,
    log_decay,
    skip_gain,
    norm_gain,
    moe_input,
    expert_ids,
    w_gate,
    w_up,
):
    ctx = lax.axis_size("ctx")
    by_tokens = lax.axis_size("exp") == 4 and ctx == 8
    ends, copies = pack(seq_input, b_input, c_input, moe_input, ctx // 2 if by_tokens else 1)
    before = lax.ppermute(ends, "ctx", [(i, i + 1) for i in range(ctx - 1)])
    mixed, notes = mixing(
        seq_input,
        b_input,
        c_input,
        before,
        conv_x,
        conv_bc,
        log_decay,
        skip_gain,
        norm_gain,
        expert_ids,
        by_tokens,
    )
    if by_tokens:
        hidden = experts_by_tokens(copies, notes, w_gate, w_up)
    else:
        hidden = experts_by_slots(moe_input, expert_ids, w_gate, w_up)
    return (mixed, hidden)


def solution(mesh):
    in_specs = (
        P("ctx", "exp"),
        P("ctx", None),
        P("ctx", None),
        P(None, "exp"),
        P(),
        P("exp", "ctx"),
        P("exp"),
        P("exp"),
        P("ctx", "exp"),
        P("ctx", None),
        P("exp", None, "ctx"),
        P("exp", None, "ctx"),
    )
    out_specs = (P("ctx", "exp"), P("exp", None, "ctx"))
    return jax.shard_map(
        on_device, mesh=mesh, in_specs=in_specs, out_specs=out_specs, check_vma=False
    )
```

time: 120 us -> 102 us (0.85)
  Pallas kernels: 0 us -> 30.6 us
  matrix products: 25.9 us -> 0 us
  starting transfers between devices: 15.6 us -> 35.1 us
  between operations: 14.3 us -> 0.77 us
  other arithmetic: 13.3 us -> 0.82 us
  waiting for transfers between devices: 27.9 us -> 18.8 us
  local copies, waits for them, and re-layouts: 22.3 us -> 15.3 us
    pallas_call x0 -> x7, Pallas kernels: none -> 30.6 us  [the longest x5 13.8 us: call(): pl.pallas_call(body, out_shape=outs, grid=(1,), in_specs=specs or [full(a...]
    dot_general x7 -> x0, matrix products: 25.9 us -> none  [the longest x1 9.23 us: experts_by_tokens(): gate = jnp.dot(whole, w_gate[0], preferred_element_type=jnp.float32)]
    all_gather x1 -> x0, waiting for transfers between devices: 23.9 us -> none  [on_device(): gathered = lax.all_gather(sent, 'ctx', axis=0)]
    ppermute x4 -> x10, waiting for transfers between devices: 3.34 us -> 18.8 us  [the longest x9 18.7 us: swapped(): lax.ppermute(block, axis, [(i, i ^ bit) for i in range(lax.axis_size(axis...]
    all_to_all x2 -> x3, starting transfers between devices: 9.5 us -> 23.9 us  [the longest x1 13.1 us: mixing(): parts = lax.all_to_all(slab, 'ctx', split_axis=0, concat_axis=0, tiled=True)]
    unnamed x15 -> x39, local copies, waits for them, and re-layouts: 4.44 us -> 15.3 us
    slice x10 -> x2, local copies, waits for them, and re-layouts: 6.04 us -> 0.04 us  [the longest x1 0.02 us: experts_by_tokens(): d0 = swapped(y[:half // 2], 'ctx', 1)]
    ppermute x4 -> x10, starting transfers between devices: 6.05 us -> 11.1 us  [the longest x9 7.72 us: swapped(): lax.ppermute(block, axis, [(i, i ^ bit) for i in range(lax.axis_size(axis...]
  transfers between devices with their start and end apart: 7 -> 13, of which waited for: 3 -> 3; matrix products, arithmetic and copies ran while one was open for 30% -> 2% of each run, Pallas kernels for 0% -> 24%
where the time goes in v2:
time: 102 us; the launch traced here: 101 us
  starting transfers between devices  35.1 us (34%)
  Pallas kernels  30.6 us (30%)
  waiting for transfers between devices  18.8 us (18%)
  local copies, waits for them, and re-layouts  15.3 us (15%)
    ppermute x9, waiting for transfers between devices, swapped(): lax.ppermute(block, axis, [(i, i ^ bit) for i in range(lax.axis_size(axis...  18.7 us
    unnamed x39, local copies, waits for them, and re-layouts  15.3 us
    pallas_call x5, Pallas kernels, call(): pl.pallas_call(body, out_shape=outs, grid=(1,), in_specs=specs or [full(a...  13.8 us
    all_to_all x1, starting transfers between devices, mixing(): parts = lax.all_to_all(slab, 'ctx', split_axis=0, concat_axis=0, tiled=True)  13.1 us
    pallas_call x1, Pallas kernels, experts_by_tokens(): pl.pallas_call(second_body, out_shape=jax.ShapeDtypeStruct((1, 2 * half,...  9.11 us
    ppermute x9, starting transfers between devices, swapped(): lax.ppermute(block, axis, [(i, i ^ bit) for i in range(lax.axis_size(axis...  7.72 us
    pallas_call x1, Pallas kernels, experts_by_tokens(): pl.pallas_call(first_body, out_shape=[sums, sums], grid_spec=pltpu.Prefet...  7.72 us
    all_to_all x1, starting transfers between devices, experts_by_tokens(): lax.all_to_all(copies, 'ctx', split_axis=0, concat_axis=0, tiled=True, ax...  6.32 us
  transfers between devices with their start and end apart: 13, of which 3 were waited for; matrix products, arithmetic and copies ran while one was open for 2% of the time, Pallas kernels for 24%

profile of v2, /device:TPU:0, one launch (start us, length us, event | category | flops | bytes accessed | tf_op | source)
XLA Modules:
  0.0 101.3 jit_solution(7509478665507555592)
XLA Ops:
  0.6 1.0 %copy-done = bf16[256,1024]{1,0:T(8,128)(2,1)S(1)} copy-done((bf16[256,1024]{1,0:T(8,128)(2,1)S(1)}, bf16[256,1024]{1,0:T(8,128)(2,1)}, u32[]{:S(2)}) %copy-start) | copy-done | bytes 524312
  1.7 0.9 copy-done.2
  2.6 0.8 copy-done.3
  3.4 0.8 copy-done.5
  4.3 0.8 pack.1
  5.1 6.3 %all-to-all-start.2 = ((bf16[4,64,1024]{2,1,0:T(8,128)(2,1)}), bf16[4,64,1024]{2,1,0:T(8,128)(2,1)S(1)}, u32[]{:S(2)}, u32[]{:S(2)}) async-start(bf16[4,64,1024]{2,1,0:T(8,128)(2,1)} %get-tuple-element.15), calls=%async_computation.2 | async-start | bytes 1048576 | tf_op jit(solution)/shard_map/all_to_all | solution.py:311
  11.4 3.4 %collective-permute-start = (bf16[16,1280]{1,0:T(8,128)(2,1)S(1)}, bf16[16,1280]{1,0:T(8,128)(2,1)S(1)}, u32[]{:S(2)}, u32[]{:S(2)}) collective-permute-start(bf16[16,1280]{1,0:T(8,128)(2,1)S(1)} %get-tuple-element.10), channel_id=1, source_target_pairs={{0,4},{4,8},{8,12},{12,16},{16,20},{20,24},{24,28},{1,5},{5,9},{9,... | collective-permute-start | bytes 122888 | tf_op jit(solution)/shard_map/ppermute | solution.py:410
  14.8 0.7 negate_sqrt_fusion.inflow_ref
  15.5 0.8 copy.14.ids_ref
  16.5 1.0 %copy-done.1 = bf16[256,1024]{1,0:T(8,128)(2,1)S(1)} copy-done((bf16[256,1024]{1,0:T(8,128)(2,1)S(1)}, bf16[256,1024]{1,0:T(8,128)(2,1)}, u32[]{:S(2)}) %copy-start.1) | copy-done | bytes 524312
  17.5 0.8 copy-done.4
  18.3 0.8 copy-done.6
  19.2 0.7 copy-done.7
  22.0 4.0 %front.1 = (f32[256,1024]{1,0:T(8,128)S(1)}, f32[256,1024]{1,0:T(8,128)S(1)}, f32[256,256]{1,0:T(8,128)S(1)}, f32[8,136,128]{2,1,0:T(8,128)}) custom-call(bf16[256,1024]{1,0:T(8,128)(2,1)S(1)} %copy-done.1, bf16[256,128]{1,0:T(8,128)(2,1)S(1)} %copy-done.4, bf16[256,128]{1,0:T(8,128)(2,1)S(1)} %copy-done.6, ...), custom_call_target="tpu_custom_call" | custom-call | flops 1000000000 | bytes 3666496 | tf_op jit(solution)/shard_map/front/pallas_call | solution.py:57
  25.9 1.0 copy-done.15
  26.9 1.0 copy-done.17
  27.9 13.1 %all-to-all-start = ((f32[8,136,128]{2,1,0:T(8,128)}), f32[8,136,128]{2,1,0:T(8,128)S(1)}, u32[]{:S(2)}, u32[]{:S(2)}) async-start(f32[8,136,128]{2,1,0:T(8,128)} %get-tuple-element.14), calls=%async_computation | async-start | bytes 1114112 | tf_op jit(solution)/shard_map/all_to_all | solution.py:242
  41.0 2.0 %collective-permute-start.3 = (bf16[256,1024]{1,0:T(8,128)(2,1)S(1)}, bf16[256,1024]{1,0:T(8,128)(2,1)S(1)}, u32[]{:S(2)}, u32[]{:S(2)}) collective-permute-start(bf16[256,1024]{1,0:T(8,128)(2,1)S(1)} %bitcast.5), channel_id=1, source_target_pairs={{0,4},{4,0},{8,12},{12,8},{16,20},{20,16},{24,28},{28,24},{1,5},{5... | collective-permute-start | bytes 1572872 | tf_op jit(solution)/shard_map/ppermute | solution.py:267
  43.0 1.5 %collective-permute-start.1 = (bf16[256,1024]{1,0:T(8,128)(2,1)S(1)}, bf16[256,1024]{1,0:T(8,128)(2,1)S(1)}, u32[]{:S(2)}, u32[]{:S(2)}) collective-permute-start(bf16[256,1024]{1,0:T(8,128)(2,1)S(1)} %bitcast.6), channel_id=1, source_target_pairs={{0,2},{1,3},{2,0},{3,1},{4,6},{5,7},{6,4},{7,5},{8,10},{9,11},{10,... | collective-permute-start | bytes 1572872 | tf_op jit(solution)/shard_map/ppermute | solution.py:267
  44.5 14.5 %collective-permute-done.3.x = bf16[256,1024]{1,0:T(8,128)(2,1)S(1)} collective-permute-done((bf16[256,1024]{1,0:T(8,128)(2,1)S(1)}, bf16[256,1024]{1,0:T(8,128)(2,1)S(1)}, u32[]{:S(2)}, u32[]{:S(2)}) %collective-permute-start.3) | collective-permute-done | bytes 524320 | tf_op jit(solution)/shard_map/ppermute | solution.py:267
  59.1 0.8 prefix.1
  60.0 4.5 %all-to-all-start.1 = ((f32[8,128,128]{2,1,0:T(8,128)}), f32[8,128,128]{2,1,0:T(8,128)}, u32[]{:S(2)}, u32[]{:S(2)}) async-start(f32[8,128,128]{2,1,0:T(8,128)} %prefix.1), calls=%async_computation.1 | async-start | bytes 1048576 | tf_op jit(solution)/shard_map/all_to_all | solution.py:250
  64.5 2.1 %collective-permute-start.2 = (bf16[128,1024]{1,0:T(8,128)(2,1)S(1)}, bf16[128,1024]{1,0:T(8,128)(2,1)S(1)}, u32[]{:S(2)}, u32[]{:S(2)}) collective-permute-start(bf16[128,1024]{1,0:T(8,128)(2,1)S(1)} %slice.8), channel_id=1, source_target_pairs={{0,4},{4,0},{8,12},{12,8},{16,20},{20,16},{24,28},{28,24},{1,5},{5... | collective-permute-start | bytes 786440 | tf_op jit(solution)/shard_map/ppermute | solution.py:267
  66.6 1.6 %collective-permute-start.4 = (bf16[128,1024]{1,0:T(8,128)(2,1)S(1)}, bf16[128,1024]{1,0:T(8,128)(2,1)S(1)}, u32[]{:S(2)}, u32[]{:S(2)}) collective-permute-start(bf16[128,1024]{1,0:T(8,128)(2,1)S(1)} %slice.9), channel_id=1, source_target_pairs={{0,2},{1,3},{2,0},{3,1},{4,6},{5,7},{6,4},{7,5},{8,10},{9,11},{10,... | collective-permute-start | bytes 786440 | tf_op jit(solution)/shard_map/ppermute | solution.py:267
  68.2 1.2 %copy-done.16 = f32[256,1024]{1,0:T(8,128)S(1)} copy-done((f32[256,1024]{1,0:T(8,128)S(1)}, f32[256,1024]{1,0:T(8,128)}, u32[]{:S(2)}) %copy-start.16) | copy-done | bytes 1048600
  69.5 1.2 %copy-done.18 = f32[256,1024]{1,0:T(8,128)S(1)} copy-done((f32[256,1024]{1,0:T(8,128)S(1)}, f32[256,1024]{1,0:T(8,128)}, u32[]{:S(2)}) %copy-start.18) | copy-done | bytes 1048600
  70.7 3.0 %inner.1.pre_ref = f32[256,1024]{1,0:T(8,128)S(1)} custom-call(f32[256,1024]{1,0:T(8,128)S(1)} %copy-done.16, f32[256,1024]{1,0:T(8,128)S(1)} %copy-done.18, f32[256,256]{1,0:T(8,128)S(1)} %get-tuple-element.13.bc_ref, f32[16,256]{1,0:T(8,128)S(1)} %copy-done.8), custom_call_target="tpu_custom_call" | custom-call | flops 4000000000 | bytes 3424256 | tf_op jit(solution)/shard_map/inner/pallas_call | solution.py:57
  73.7 1.0 copy-done.13
  74.7 4.1 %collective-permute-done.2.d0 = bf16[128,1024]{1,0:T(8,128)(2,1)S(1)} collective-permute-done((bf16[128,1024]{1,0:T(8,128)(2,1)S(1)}, bf16[128,1024]{1,0:T(8,128)(2,1)S(1)}, u32[]{:S(2)}, u32[]{:S(2)}) %collective-permute-start.2) | collective-permute-done | bytes 262176 | tf_op jit(solution)/shard_map/ppermute | solution.py:267
  79.3 7.7 %first.1 = (f32[512,1024]{1,0:T(8,128)S(1)}, f32[512,1024]{1,0:T(8,128)S(1)}) custom-call(s32[2]{0:T(128)S(1)} %pad_add_fusion.place_ref, bf16[256,1024]{1,0:T(8,128)(2,1)S(1)} %bitcast.8, bf16[256,1024]{1,0:T(8,128)(2,1)S(1)} %collective-permute-done.3.x, bf16[256,1024]{1,0:T(8,128)(2,1)S(1)} %collective-permute-done.8.cz, ...), custom_call_target="tpu_custom_call" | custom-call | flops 4294967296 | bytes 14680064 | tf_op jit(solution)/shard_map/first/pallas_call | solution.py:341
  87.1 9.1 %second.1 = bf16[1,512,1024]{2,1,0:T(8,128)(2,1)} custom-call(s32[2]{0:T(128)S(1)} %pad_add_fusion.place_ref, bf16[256,1024]{1,0:T(8,128)(2,1)S(1)} %collective-permute-done.1.y, bf16[128,1024]{1,0:T(8,128)(2,1)S(1)} %collective-permute-done.2.d0, bf16[128,1024]{1,0:T(8,128)(2,1)S(1)} %collective-permute-done.4.d1, ...), custom_call_target="tpu_custom_call" | custom-call | flops 4294967296 | bytes 15728640 | tf_op jit(solution)/shard_map/second/pallas_call | solution.py:356
  96.2 5.1 %back.1 = bf16[256,1024]{1,0:T(8,128)(2,1)} custom-call(f32[256,1024]{1,0:T(8,128)S(1)} %copy-done.14, f32[8,128,128]{2,1,0:T(8,128)} %all-to-all-done.1.start_ref, f32[256,256]{1,0:T(8,128)S(1)} %get-tuple-element.13.bc_ref, f32[16,256]{1,0:T(8,128)S(1)} %copy-done.8, f32[1,1024]{1,0:T(1,128)S(1)} %bitcast.9), custom_call_target="tpu_custom_call" | custom-call | flops 1000000000 | bytes 2379776 | tf_op jit(solution)/shard_map/back/pallas_call | solution.py:57
  (44 shorter events, 2.9 us)
Async XLA Ops:
  0.6 1.0 %copy-start = (bf16[256,1024]{1,0:T(8,128)(2,1)S(1)}, bf16[256,1024]{1,0:T(8,128)(2,1)}, u32[]{:S(2)}) copy-start(bf16[256,1024]{1,0:T(8,128)(2,1)} %x_ref.3) | copy-start | bytes 1572868
  1.7 0.9 copy-start.2
  2.6 0.8 copy-start.3
  3.4 0.8 copy-start.5
  4.3 64.0 %copy-start.8 = (f32[16,256]{1,0:T(8,128)S(1)}, f32[16,256]{1,0:T(8,128)}, u32[]{:S(2)}) copy-start(f32[16,256]{1,0:T(8,128)} %logs_ref.5) | copy-start | bytes 49156
  5.1 22.8 %all-to-all-start.2 = ((bf16[4,64,1024]{2,1,0:T(8,128)(2,1)}), bf16[4,64,1024]{2,1,0:T(8,128)(2,1)S(1)}, u32[]{:S(2)}, u32[]{:S(2)}) async-start(bf16[4,64,1024]{2,1,0:T(8,128)(2,1)} %get-tuple-element.15), calls=%async_computation.2 | async-start | bytes 1048576 | tf_op jit(solution)/shard_map/all_to_all | solution.py:311
  11.4 5.0 %collective-permute-start = (bf16[16,1280]{1,0:T(8,128)(2,1)S(1)}, bf16[16,1280]{1,0:T(8,128)(2,1)S(1)}, u32[]{:S(2)}, u32[]{:S(2)}) collective-permute-start(bf16[16,1280]{1,0:T(8,128)(2,1)S(1)} %get-tuple-element.10), channel_id=1, source_target_pairs={{0,4},{4,8},{8,12},{12,16},{16,20},{20,24},{24,28},{1,5},{5,9},{9,... | collective-permute-start | bytes 122888 | tf_op jit(solution)/shard_map/ppermute | solution.py:410
  16.5 1.0 %copy-start.1 = (bf16[256,1024]{1,0:T(8,128)(2,1)S(1)}, bf16[256,1024]{1,0:T(8,128)(2,1)}, u32[]{:S(2)}) copy-start(bf16[256,1024]{1,0:T(8,128)(2,1)} %x_ref.3) | copy-start | bytes 1572868
  17.5 0.8 copy-start.4
  18.3 0.8 copy-start.6
  19.2 0.7 copy-start.7
  19.9 0.7 copy-start.9
  20.6 0.7 copy-start.10
  21.3 0.7 copy-start.12
  25.9 1.0 copy-start.15
  26.9 1.0 copy-start.17
  27.9 31.3 %all-to-all-start = ((f32[8,136,128]{2,1,0:T(8,128)}), f32[8,136,128]{2,1,0:T(8,128)S(1)}, u32[]{:S(2)}, u32[]{:S(2)}) async-start(f32[8,136,128]{2,1,0:T(8,128)} %get-tuple-element.14), calls=%async_computation | async-start | bytes 1114112 | tf_op jit(solution)/shard_map/all_to_all | solution.py:242
  41.0 18.1 %collective-permute-start.3 = (bf16[256,1024]{1,0:T(8,128)(2,1)S(1)}, bf16[256,1024]{1,0:T(8,128)(2,1)S(1)}, u32[]{:S(2)}, u32[]{:S(2)}) collective-permute-start(bf16[256,1024]{1,0:T(8,128)(2,1)S(1)} %bitcast.5), channel_id=1, source_target_pairs={{0,4},{4,0},{8,12},{12,8},{16,20},{20,16},{24,28},{28,24},{1,5},{5... | collective-permute-start | bytes 1572872 | tf_op jit(solution)/shard_map/ppermute | solution.py:267
  43.0 21.5 %collective-permute-start.1 = (bf16[256,1024]{1,0:T(8,128)(2,1)S(1)}, bf16[256,1024]{1,0:T(8,128)(2,1)S(1)}, u32[]{:S(2)}, u32[]{:S(2)}) collective-permute-start(bf16[256,1024]{1,0:T(8,128)(2,1)S(1)} %bitcast.6), channel_id=1, source_target_pairs={{0,2},{1,3},{2,0},{3,1},{4,6},{5,7},{6,4},{7,5},{8,10},{9,11},{10,... | collective-permute-start | bytes 1572872 | tf_op jit(solution)/shard_map/ppermute | solution.py:267
  44.5 34.8 %collective-permute-start.8 = (bf16[256,1024]{1,0:T(8,128)(2,1)S(1)}, bf16[256,1024]{1,0:T(8,128)(2,1)S(1)}, u32[]{:S(2)}, u32[]{:S(2)}) collective-permute-start(bf16[256,1024]{1,0:T(8,128)(2,1)S(1)} %bitcast.7), channel_id=1, source_target_pairs={{0,1},{1,0},{2,3},{3,2},{4,5},{5,4},{6,7},{7,6},{8,9},{9,8},{10,11... | collective-permute-start | bytes 1572872 | tf_op jit(solution)/shard_map/ppermute | solution.py:267
  59.0 20.2 %collective-permute-start.9 = (bf16[256,1024]{1,0:T(8,128)(2,1)S(1)}, bf16[256,1024]{1,0:T(8,128)(2,1)S(1)}, u32[]{:S(2)}, u32[]{:S(2)}) collective-permute-start(bf16[256,1024]{1,0:T(8,128)(2,1)S(1)} %collective-permute-done.3.x), channel_id=1, source_target_pairs={{0,1},{1,0},{2,3},{3,2},{4,5},{5,4},{6,7},{7,6},{8,9},{9,8},{10,11... | collective-permute-start | bytes 1572872 | tf_op jit(solution)/shard_map/ppermute | solution.py:267
  60.0 36.2 %all-to-all-start.1 = ((f32[8,128,128]{2,1,0:T(8,128)}), f32[8,128,128]{2,1,0:T(8,128)}, u32[]{:S(2)}, u32[]{:S(2)}) async-start(f32[8,128,128]{2,1,0:T(8,128)} %prefix.1), calls=%async_computation.1 | async-start | bytes 1048576 | tf_op jit(solution)/shard_map/all_to_all | solution.py:250
  64.5 14.2 %collective-permute-start.2 = (bf16[128,1024]{1,0:T(8,128)(2,1)S(1)}, bf16[128,1024]{1,0:T(8,128)(2,1)S(1)}, u32[]{:S(2)}, u32[]{:S(2)}) collective-permute-start(bf16[128,1024]{1,0:T(8,128)(2,1)S(1)} %slice.8), channel_id=1, source_target_pairs={{0,4},{4,0},{8,12},{12,8},{16,20},{20,16},{24,28},{28,24},{1,5},{5... | collective-permute-start | bytes 786440 | tf_op jit(solution)/shard_map/ppermute | solution.py:267
  66.6 12.1 %collective-permute-start.4 = (bf16[128,1024]{1,0:T(8,128)(2,1)S(1)}, bf16[128,1024]{1,0:T(8,128)(2,1)S(1)}, u32[]{:S(2)}, u32[]{:S(2)}) collective-permute-start(bf16[128,1024]{1,0:T(8,128)(2,1)S(1)} %slice.9), channel_id=1, source_target_pairs={{0,2},{1,3},{2,0},{3,1},{4,6},{5,7},{6,4},{7,5},{8,10},{9,11},{10,... | collective-permute-start | bytes 786440 | tf_op jit(solution)/shard_map/ppermute | solution.py:267
  68.2 18.8 %collective-permute-start.5 = (bf16[256,1024]{1,0:T(8,128)(2,1)S(1)}, bf16[256,1024]{1,0:T(8,128)(2,1)S(1)}, u32[]{:S(2)}, u32[]{:S(2)}) collective-permute-start(bf16[256,1024]{1,0:T(8,128)(2,1)S(1)} %collective-permute-done.1.y), channel_id=1, source_target_pairs={{0,1},{1,0},{2,3},{3,2},{4,5},{5,4},{6,7},{7,6},{8,9},{9,8},{10,11... | collective-permute-start | bytes 1572872 | tf_op jit(solution)/shard_map/ppermute | solution.py:267
  68.2 1.2 %copy-start.16 = (f32[256,1024]{1,0:T(8,128)S(1)}, f32[256,1024]{1,0:T(8,128)}, u32[]{:S(2)}) copy-start(f32[256,1024]{1,0:T(8,128)} %copy-done.15) | copy-start | bytes 3145732
  69.5 1.2 %copy-start.18 = (f32[256,1024]{1,0:T(8,128)S(1)}, f32[256,1024]{1,0:T(8,128)}, u32[]{:S(2)}) copy-start(f32[256,1024]{1,0:T(8,128)} %copy-done.17) | copy-start | bytes 3145732
  73.7 1.0 copy-start.13
  78.8 8.3 %collective-permute-start.6 = (bf16[128,1024]{1,0:T(8,128)(2,1)S(1)}, bf16[128,1024]{1,0:T(8,128)(2,1)S(1)}, u32[]{:S(2)}, u32[]{:S(2)}) collective-permute-start(bf16[128,1024]{1,0:T(8,128)(2,1)S(1)} %collective-permute-done.2.d0), channel_id=1, source_target_pairs={{0,1},{1,0},{2,3},{3,2},{4,5},{5,4},{6,7},{7,6},{8,9},{9,8},{10,11... | collective-permute-start | bytes 786440 | tf_op jit(solution)/shard_map/ppermute | solution.py:267
  78.8 8.3 %collective-permute-start.7 = (bf16[128,1024]{1,0:T(8,128)(2,1)S(1)}, bf16[128,1024]{1,0:T(8,128)(2,1)S(1)}, u32[]{:S(2)}, u32[]{:S(2)}) collective-permute-start(bf16[128,1024]{1,0:T(8,128)(2,1)S(1)} %collective-permute-done.4.d1), channel_id=1, source_target_pairs={{0,1},{1,0},{2,3},{3,2},{4,5},{5,4},{6,7},{7,6},{8,9},{9,8},{10,11... | collective-permute-start | bytes 786440 | tf_op jit(solution)/shard_map/ppermute | solution.py:267
  87.0 9.1 %copy-start.11 = (f32[1024]{0:T(1024)S(1)}, f32[1024]{0:T(1024)}, u32[]{:S(2)}) copy-start(f32[1024]{0:T(1024)} %param.19) | copy-start | bytes 12292
  87.0 9.1 %copy-start.14 = (f32[256,1024]{1,0:T(8,128)S(1)}, f32[256,1024]{1,0:T(8,128)}, u32[]{:S(2)}) copy-start(f32[256,1024]{1,0:T(8,128)} %copy-done.13) | copy-start | bytes 3145732

commit v3 on v2

v3 whole, which is shorter than its diff:
```python
import functools

import jax
import jax.numpy as jnp
from jax import lax
from jax.experimental import pallas as pl
from jax.experimental.pallas import tpu as pltpu
from jax.sharding import PartitionSpec as P

HDIM = 64
STATE = 128
KCONV = 4
EDGE = 16
NOTES = 8

F32 = jnp.float32
BF16 = jnp.bfloat16


def dot16(a, b, contract=((1,), (0,))):
    return lax.dot_general(a, b, (contract, ((), ())), preferred_element_type=F32)


def halves(value):
    high = value.astype(BF16)
    return high, (value - high.astype(F32)).astype(BF16)


def dot(a, b, contract=((1,), (0,))):
    a_high, a_low = halves(a)
    b_high, b_low = halves(b)
    cross = dot16(a_high, b_low, contract) + dot16(a_low, b_high, contract)
    return dot16(a_high, b_high, contract) + cross


def dot_exact(a, b, contract=((1,), (0,))):
    high, rest = halves(a)
    low = (a - high.astype(F32) - rest.astype(F32)).astype(BF16)
    return dot16(high, b, contract) + (dot16(rest, b, contract) + dot16(low, b, contract))


def dot_left(a, b, contract=((1,), (0,))):
    high, low = halves(a)
    return dot16(high, b, contract) + dot16(low, b, contract)


FIRST = ((0,), (0,))


def iota(shape, axis):
    return lax.broadcasted_iota(jnp.int32, shape, axis)


def head_spread(heads):
    shape = (heads, heads * HDIM)
    return (iota(shape, 1) // HDIM == iota(shape, 0)).astype(BF16)


def upper_ones(length):
    return (iota((length, length), 0) <= iota((length, length), 1)).astype(BF16)


def silu(value):
    return value / (1.0 + jnp.exp(-value))


def one_minus_exp(value):
    series = jnp.ones_like(value)
    for n in range(8, 1, -1):
        series = 1.0 + value * series * (1.0 / n)
    return jnp.where(value > -0.25, -value * series, 1.0 - jnp.exp(value))


def fetched(sources, targets, sems):
    copies = [
        pltpu.make_async_copy(a, b, sems.at[i]) for i, (a, b) in enumerate(zip(sources, targets))
    ]
    for copy in copies:
        copy.start()
    for copy in copies:
        copy.wait()


def call(body, outs, far, near, scratch=(), sems=0, flops=0, name=None):
    moved = sum(a.size * a.dtype.itemsize for a in (*far, *near, *outs))
    scratch = list(scratch) + ([pltpu.SemaphoreType.DMA((sems,))] if sems else [])
    return pl.pallas_call(
        body,
        out_shape=outs,
        in_specs=[pl.BlockSpec(memory_space=pltpu.HBM)] * len(far)
        + [pl.BlockSpec(memory_space=pltpu.VMEM)] * len(near),
        out_specs=[pl.BlockSpec(memory_space=pltpu.VMEM)] * len(outs),
        scratch_shapes=scratch,
        compiler_params=pltpu.CompilerParams(vmem_limit_bytes=24 * 2**20),
        cost_estimate=pl.CostEstimate(flops=flops, bytes_accessed=moved, transcendentals=0),
        name=name,
    )(*(pltpu.with_memory_space_constraint(a, pltpu.HBM) for a in far), *near)


def array(shape, dtype):
    return jax.ShapeDtypeStruct(shape, dtype)


def ends_body(x_ref, b_ref, c_ref, ends_ref, sems):
    tokens, channels = x_ref.shape
    cut = pl.ds(tokens - EDGE, EDGE)
    fetched(
        [x_ref.at[cut, :], b_ref.at[cut, :], c_ref.at[cut, :]],
        [
            ends_ref.at[:, pl.ds(0, channels)],
            ends_ref.at[:, pl.ds(channels, STATE)],
            ends_ref.at[:, pl.ds(channels + STATE, STATE)],
        ],
        sems,
    )


def front_body(
    by_tokens,
    x_hbm,
    b_hbm,
    c_hbm,
    taps_hbm,
    taps_bc_hbm,
    logs_hbm,
    skip_hbm,
    ids_hbm,
    ends_ref,
    drive_ref,
    direct_ref,
    bc_ref,
    row_ref,
    column_ref,
    slab_ref,
    pad_ref,
    x_ref,
    b_ref,
    c_ref,
    taps_ref,
    taps_bc_ref,
    logs_ref,
    skip_ref,
    ids_ref,
    sems,
):
    fetched(
        [x_hbm, b_hbm, c_hbm, taps_hbm, taps_bc_hbm, logs_hbm, skip_hbm, ids_hbm],
        [x_ref, b_ref, c_ref, taps_ref, taps_bc_ref, logs_ref, skip_ref, ids_ref],
        sems,
    )
    tokens, channels = x_ref.shape
    heads = logs_ref.shape[0]
    pad_ref[0:8, :] = ends_ref[...].astype(F32)[EDGE - 8 : EDGE]
    pad_ref[8 : 8 + tokens, :channels] = x_ref[...].astype(F32)
    pad_ref[8 : 8 + tokens, channels : channels + STATE] = b_ref[...].astype(F32)
    pad_ref[8 : 8 + tokens, channels + STATE :] = c_ref[...].astype(F32)

    def conv(taps, start, stop):
        total = jnp.zeros((tokens, stop - start), F32)
        for k in range(KCONV):
            first = 8 - (KCONV - 1) + k
            total = total + taps[k : k + 1] * pad_ref[first : first + tokens, start:stop]
        return silu(total)

    bc = conv(taps_bc_ref[...], channels, channels + 2 * STATE)
    bc_ref[...] = bc
    bmat = bc[:, :STATE]

    logs = logs_ref[...]
    inflow = jnp.sqrt(one_minus_exp(2.0 * logs))
    ones = upper_ones(tokens)
    within = dot_exact(logs, ones)
    row_ref[...] = within
    column_ref[...] = within.T
    total = within[:, tokens - 1 :]
    remain = jnp.exp(total - within)
    spread = head_spread(heads)
    xconv = conv(taps_ref[...], 0, channels)
    drive_ref[...] = xconv * dot_left(inflow, spread, FIRST)
    direct_ref[...] = xconv * dot_exact(skip_ref[...], spread)
    state = dot(bmat, xconv * dot_left(inflow * remain, spread, FIRST), FIRST)
    notes = dot_exact(jnp.exp(jnp.broadcast_to(total, (heads, NOTES))), spread, FIRST)
    if not by_tokens:
        slab_ref[:STATE] = state
        slab_ref[STATE:] = notes
        return
    parts, _, share = slab_ref.shape
    ids = ids_ref[...].astype(F32)
    line = jnp.concatenate([ids[0:1], ids[1:2]], axis=1)
    for i in range(parts):
        cut = slice(i * share, (i + 1) * share)
        slab_ref[i, :STATE] = state[:, cut]
        slab_ref[i, STATE:] = jnp.where(iota((NOTES, share), 0) == 1, line, notes[:, cut])


def weight_copies(w_gate, w_up, held, sems, bits):
    depth = held.shape[2]
    me = lax.axis_index("exp")
    copies = []
    for k, bit in enumerate(bits):
        cut = pl.ds(pl.multiple_of((me ^ bit) * depth, depth), depth)
        for i, w in enumerate((w_gate, w_up)):
            copies.append(
                pltpu.make_async_copy(w.at[0, cut, :], held.at[i, k], sems.at[2 * k + i])
            )
    return copies


def inner_body(
    bits,
    w_gate,
    w_up,
    gain_hbm,
    drive_ref,
    direct_ref,
    bc_ref,
    row_ref,
    column_ref,
    pre_ref,
    decay_ref,
    gain_ref,
    held_ref,
    sems,
):
    copies = [pltpu.make_async_copy(gain_hbm, gain_ref, sems.at[4])]
    copies += weight_copies(w_gate, w_up, held_ref, sems, bits)
    for copy in copies:
        copy.start()
    tokens = drive_ref.shape[0]
    heads = row_ref.shape[0]
    row = row_ref[...]
    column = column_ref[...]
    decay_ref[...] = dot_left(jnp.exp(row), head_spread(heads), FIRST)
    meet = dot(bc_ref[:, STATE:], bc_ref[:, :STATE], ((1,), (1,)))
    lower = iota((tokens, tokens), 0) >= iota((tokens, tokens), 1)
    left = iota((tokens, 2 * HDIM), 1) < HDIM
    for pair in range(heads // 2):
        cut = slice(pair * 2 * HDIM, (pair + 1) * 2 * HDIM)
        d_high, d_low = halves(drive_ref[:, cut])
        both = []
        for h in (2 * pair, 2 * pair + 1):
            gap = column[:, h : h + 1] - row[h : h + 1, :]
            mix = jnp.where(lower, jnp.exp(gap), 0.0) * meet
            m_high, m_low = halves(mix)
            both.append(dot16(m_high, d_high) + dot16(m_high, d_low) + dot16(m_low, d_high))
        pre_ref[:, cut] = direct_ref[:, cut] + jnp.where(left, both[0], both[1])
    for copy in copies:
        copy.wait()


def prefix_body(parts_ref, starts_ref):
    ctx, rows, share = starts_ref.shape
    state = jnp.zeros((rows, share), F32)
    for i in range(ctx):
        starts_ref[i] = state
        if i < ctx - 1:
            state = parts_ref[i, STATE : STATE + 1] * state + parts_ref[i, :STATE]


def back_body(cuts, pre_ref, decay_ref, start_ref, bc_ref, gain_ref, out_ref):
    channels = pre_ref.shape[1]
    width = min(channels, 4 * HDIM)
    group = (iota((width, width), 0) // HDIM == iota((width, width), 1) // HDIM).astype(BF16)
    c_high, c_low = halves(bc_ref[:, STATE:])
    for i in range(channels // width):
        cut = slice(i * width, (i + 1) * width)
        if cuts:
            start = jnp.concatenate([start_ref[2 * i], start_ref[2 * i + 1]], axis=1)
        else:
            start = start_ref[:, cut]
        s_high, s_low = halves(start)
        carried = dot16(c_high, s_high) + dot16(c_high, s_low) + dot16(c_low, s_high)
        pre = pre_ref[:, cut] + carried * decay_ref[:, cut]
        mean = dot_left(pre * pre, group) * (1.0 / HDIM)
        out_ref[:, cut] = (pre * lax.rsqrt(mean + 1e-05) * gain_ref[:, cut]).astype(BF16)


def mixing(
    seq_input, b_input, c_input, before, conv_x, conv_bc, log_decay, skip, gain, ids, w_gate, w_up
):
    tokens, channels = seq_input.shape
    heads = skip.shape[0]
    ctx = lax.axis_size("ctx")
    share = channels // ctx
    cuts = share == 2 * HDIM
    square = array((tokens, channels), F32)
    slabs = (ctx, STATE + NOTES, share) if cuts else (STATE + NOTES, channels)
    outs = [
        square,
        square,
        array((tokens, 2 * STATE), F32),
        array((heads, tokens), F32),
        array((tokens, heads), F32),
        array(slabs, F32),
    ]
    far = (seq_input, b_input, c_input, conv_x, conv_bc, log_decay, skip.reshape(1, heads), ids.T)
    drive, direct, bc, row, column, slab = call(
        functools.partial(front_body, cuts),
        outs,
        far,
        (before,),
        scratch=[pltpu.VMEM((8 + tokens, channels + 2 * STATE), F32)]
        + [pltpu.VMEM(a.shape, a.dtype) for a in far],
        sems=len(far),
        flops=10**9,
        name="front",
    )
    if not cuts:
        slab = slab.reshape(STATE + NOTES, ctx, share).transpose(1, 0, 2)
    parts = lax.all_to_all(slab, "ctx", split_axis=0, concat_axis=0, tiled=True)
    starts = call(
        prefix_body,
        [array((ctx, STATE, share), F32)],
        (),
        (parts,),
        flops=10**6,
        name="prefix",
    )[0]
    start = lax.all_to_all(starts, "ctx", split_axis=0, concat_axis=0, tiled=True)
    if not cuts:
        start = start.transpose(1, 0, 2).reshape(STATE, channels)
    depth = w_gate.shape[1] // lax.axis_size("exp")
    bits = (0, 1) if cuts else ()
    held_shape = (2, max(1, len(bits)), depth if cuts else 8, w_gate.shape[2] if cuts else 128)
    pre, decay, gain, held = call(
        functools.partial(inner_body, bits),
        [square, square, array((1, channels), F32), array(held_shape, BF16)],
        (w_gate, w_up, gain.reshape(1, channels)),
        (drive, direct, bc, row, column),
        sems=5,
        flops=4 * 10**9,
        name="inner",
    )
    mixed = call(
        functools.partial(back_body, cuts),
        [array((tokens, channels), BF16)],
        (),
        (pre, decay, start, bc, gain),
        flops=10**9,
        name="back",
    )[0]
    return mixed, parts, held


def copies_body(moe_ref, copies_ref, sems):
    zs = copies_ref.shape[0]
    fetched([moe_ref] * zs, [copies_ref.at[i] for i in range(zs)], sems)


def swapped(block, axis, bit):
    return lax.ppermute(block, axis, [(i, i ^ bit) for i in range(lax.axis_size(axis))])


TILE = 256


def first_body(w_gate, w_up, held_ref, z, x, cz, cx, gate_ref, up_ref, later_ref, sems):
    copies = weight_copies(w_gate, w_up, later_ref, sems, (2, 3))
    for copy in copies:
        copy.start()
    for start in range(0, gate_ref.shape[1], TILE):
        cut = slice(start, start + TILE)
        for i, out in enumerate((gate_ref, up_ref)):
            here = dot16(jnp.concatenate([z[...], x[...]], 0), held_ref[i, 0, :, cut])
            out[:, cut] = here + dot16(
                jnp.concatenate([cz[...], cx[...]], 0), held_ref[i, 1, :, cut]
            )
    for copy in copies:
        copy.wait()


def second_body(
    y, d0, d1, cy, cd0, cd1, gate_ref, up_ref, held_ref, notes_ref, out_ref, pick_ref, hid_ref
):
    blocks = notes_ref.shape[0]
    length = gate_ref.shape[0]
    rows = length // blocks
    me = lax.axis_index("exp").astype(F32)
    side = lax.axis_index("ctx") % 2
    shape = (rows, rows)
    earlier = (iota(shape, 1) < iota(shape, 0)).astype(F32)
    across = iota(shape, 1)
    diagonal = iota(shape, 0) == across

    def block_at(place):
        z = place % (blocks // 2)
        return 2 * z + (side if place < blocks // 2 else 1 - side)

    for place in range(blocks):
        line = notes_ref[block_at(place), STATE + 1 : STATE + 2, :]
        named = ((line[:, :rows] == me) | (line[:, rows : 2 * rows] == me)).astype(F32)
        column = jnp.sum(jnp.where(diagonal, named, 0.0), axis=1, keepdims=True)
        position = jnp.sum(earlier * named, axis=1, keepdims=True).astype(jnp.int32)
        pick_ref[place] = jnp.where(position == across, column, 0.0).astype(BF16)

    for start in range(0, gate_ref.shape[1], TILE):
        cut = slice(start, start + TILE)
        a = jnp.concatenate([y[...], d0[...], d1[...]], 0)
        b = jnp.concatenate([cy[...], cd0[...], cd1[...]], 0)
        gate = gate_ref[:, cut] + dot16(a, held_ref[0, 0, :, cut]) + dot16(b, held_ref[0, 1, :, cut])
        upper = up_ref[:, cut] + dot16(a, held_ref[1, 0, :, cut]) + dot16(b, held_ref[1, 1, :, cut])
        hid_ref[...] = (silu(gate) * upper).astype(BF16)
        for place in range(blocks):
            picked = dot16(pick_ref[place], hid_ref[place * rows : (place + 1) * rows], FIRST)
            at = pl.ds(pl.multiple_of(block_at(place) * rows, rows), rows)
            out_ref[0, at, cut] = picked.astype(BF16)


def experts_by_tokens(copies, notes, held, w_gate, w_up):
    zs, rows, columns = copies.shape
    ctx = lax.axis_size("ctx")
    groups = [list(range(s, ctx, 2)) for s in range(2)]
    z = lax.all_to_all(
        copies, "ctx", split_axis=0, concat_axis=0, tiled=True, axis_index_groups=groups
    )
    z = z.reshape(zs * rows, columns)
    half = z.shape[0]
    x = swapped(z, "ctx", 1)
    y = swapped(z, "exp", 2)
    cz = swapped(z, "exp", 1)
    d0 = swapped(y[: half // 2], "ctx", 1)
    d1 = swapped(x[half // 2 :], "exp", 2)
    cx = swapped(x, "exp", 1)
    cy = swapped(y, "exp", 1)
    cd0 = swapped(d0, "exp", 1)
    cd1 = swapped(d1, "exp", 1)

    hidden = w_gate.shape[2]
    flops = 2 * 2 * half * 2 * columns * hidden * 2
    sums = array((2 * half, hidden), F32)
    gate, upper, later = call(
        first_body,
        [sums, sums, array(held.shape, BF16)],
        (w_gate, w_up),
        (held, z, x, cz, cx),
        sems=4,
        flops=flops,
        name="first",
    )
    return call(
        second_body,
        [array((1, 2 * half, hidden), BF16)],
        (),
        (y, d0, d1, cy, cd0, cd1, gate, upper, later, notes),
        scratch=[pltpu.VMEM((ctx, rows, rows), BF16), pltpu.VMEM((2 * half, TILE), BF16)],
        flops=flops,
        name="second",
    )[0]


def slot_matrix(pairs, expert, capacity):
    named = jnp.any(pairs == expert, axis=1).astype(jnp.int32)
    position = jnp.cumsum(named) - named
    hit = position[None, :] == jnp.arange(capacity, dtype=jnp.int32)[:, None]
    return (hit & (named[None, :] > 0)).astype(BF16)


def experts_by_slots(moe_input, pairs, w_gate, w_up):
    experts = lax.axis_size("exp")
    capacity = 4 * moe_input.shape[0] // experts
    pick = jax.vmap(lambda e: slot_matrix(pairs, e, capacity))(jnp.arange(experts))
    slots = jnp.einsum("eqt,td->eqd", pick, moe_input, preferred_element_type=F32)
    routed = lax.all_to_all(slots.astype(BF16), "exp", split_axis=0, concat_axis=2, tiled=True)
    rows = lax.all_gather(routed[0], "ctx", axis=0, tiled=True)
    gate = jnp.dot(rows, w_gate[0], preferred_element_type=F32)
    upper = jnp.dot(rows, w_up[0], preferred_element_type=F32)
    return (jax.nn.silu(gate) * upper).astype(BF16)[None]


def on_device(
    seq_input,
    b_input,
    c_input,
    conv_x,
    conv_bc,
    log_decay,
    skip_gain,
    norm_gain,
    moe_input,
    expert_ids,
    w_gate,
    w_up,
):
    ctx = lax.axis_size("ctx")
    by_tokens = lax.axis_size("exp") == 4 and ctx == 8
    tokens, channels = seq_input.shape
    ends = call(
        ends_body,
        [array((EDGE, channels + 2 * STATE), BF16)],
        (seq_input, b_input, c_input),
        (),
        sems=3,
        name="ends",
    )[0]
    before = lax.ppermute(ends, "ctx", [(i, i + 1) for i in range(ctx - 1)])
    mixed, notes, held = mixing(
        seq_input,
        b_input,
        c_input,
        before,
        conv_x,
        conv_bc,
        log_decay,
        skip_gain,
        norm_gain,
        expert_ids,
        w_gate,
        w_up,
    )
    if by_tokens:
        zs = ctx // 2
        copies = call(
            copies_body,
            [array((zs,) + moe_input.shape, BF16)],
            (moe_input,),
            (),
            sems=zs,
            name="copies",
        )[0]
        hidden = experts_by_tokens(copies, notes, held, w_gate, w_up)
    else:
        hidden = experts_by_slots(moe_input, expert_ids, w_gate, w_up)
    return (mixed, hidden)


def solution(mesh):
    in_specs = (
        P("ctx", "exp"),
        P("ctx", None),
        P("ctx", None),
        P(None, "exp"),
        P(),
        P("exp", "ctx"),
        P("exp"),
        P("exp"),
        P("ctx", "exp"),
        P("ctx", None),
        P("exp", None, "ctx"),
        P("exp", None, "ctx"),
    )
    out_specs = (P("ctx", "exp"), P("exp", None, "ctx"))
    return jax.shard_map(
        on_device, mesh=mesh, in_specs=in_specs, out_specs=out_specs, check_vma=False
    )
```

time: 102 us -> 96.7 us (0.948)
  local copies, waits for them, and re-layouts: 15.3 us -> 11.7 us
  starting transfers between devices: 35.1 us -> 32.1 us
  Pallas kernels: 30.6 us -> 32.4 us
    ppermute x9, waiting for transfers between devices: 18.7 us -> 15 us  [swapped(): lax.ppermute(block, axis, [(i, i ^ bit) for i in range(lax.axis_size(axis...]
    unnamed x39 -> x24, local copies, waits for them, and re-layouts: 15.3 us -> 11.7 us
    all_to_all x1, starting transfers between devices: 13.1 us -> 10.1 us  [mixing(): parts = lax.all_to_all(slab, 'ctx', split_axis=0, concat_axis=0, tiled=True)]
    all_to_all x1, waiting for transfers between devices: 0.01 us -> 2.21 us  [experts_by_tokens(): lax.all_to_all(copies, 'ctx', split_axis=0, concat_axis=0, tiled=True, ax...]
    pallas_call x7 -> x8, Pallas kernels: 30.6 us -> 32.4 us  [call(): pl.pallas_call(body, out_shape=outs, in_specs=[pl.BlockSpec(memory_space=...]
    ppermute x1, waiting for transfers between devices: 0.14 us -> 1.65 us  [on_device(): before = lax.ppermute(ends, 'ctx', [(i, i + 1) for i in range(ctx - 1)])]
  transfers between devices with their start and end apart: 13 -> 13, of which waited for: 3 -> 4; matrix products, arithmetic and copies ran while one was open for 2% -> 0% of each run, Pallas kernels for 24% -> 28%
where the time goes in v3:
time: 96.7 us; the launch traced here: 95.8 us
  Pallas kernels  32.4 us (34%)
  starting transfers between devices  32.1 us (33%)
  waiting for transfers between devices  18.9 us (20%)
  local copies, waits for them, and re-layouts  11.7 us (12%)
    pallas_call x8, Pallas kernels, call(): pl.pallas_call(body, out_shape=outs, in_specs=[pl.BlockSpec(memory_space=...  32.4 us
    ppermute x9, waiting for transfers between devices, swapped(): lax.ppermute(block, axis, [(i, i ^ bit) for i in range(lax.axis_size(axis...  15 us
    unnamed x24, local copies, waits for them, and re-layouts  11.7 us
    all_to_all x1, starting transfers between devices, mixing(): parts = lax.all_to_all(slab, 'ctx', split_axis=0, concat_axis=0, tiled=True)  10.1 us
    ppermute x9, starting transfers between devices, swapped(): lax.ppermute(block, axis, [(i, i ^ bit) for i in range(lax.axis_size(axis...  7.73 us
    all_to_all x1, starting transfers between devices, experts_by_tokens(): lax.all_to_all(copies, 'ctx', split_axis=0, concat_axis=0, tiled=True, ax...  6.33 us
    all_to_all x1, starting transfers between devices, mixing(): lax.all_to_all(starts, 'ctx', split_axis=0, concat_axis=0, tiled=True)  4.54 us
    ppermute x1, starting transfers between devices, on_device(): before = lax.ppermute(ends, 'ctx', [(i, i + 1) for i in range(ctx - 1)])  3.4 us
  transfers between devices with their start and end apart: 13, of which 4 were waited for; matrix products, arithmetic and copies ran while one was open for 0% of the time, Pallas kernels for 28%

profile of v3, /device:TPU:0, one launch (start us, length us, event | category | flops | bytes accessed | tf_op | source)
XLA Modules:
  0.0 95.8 jit_solution(7028260494196110705)
XLA Ops:
  0.6 2.1 %copies.1 = bf16[4,64,1024]{2,1,0:T(8,128)(2,1)} custom-call(bf16[64,1024]{1,0:T(8,128)(2,1)} %moe_ref.1), custom_call_target="tpu_custom_call" | custom-call | bytes 655360 | tf_op jit(solution)/shard_map/copies/pallas_call | solution.py:87
  2.7 6.3 %all-to-all-start.2 = ((bf16[4,64,1024]{2,1,0:T(8,128)(2,1)}), bf16[4,64,1024]{2,1,0:T(8,128)(2,1)S(1)}, u32[]{:S(2)}, u32[]{:S(2)}) async-start(bf16[4,64,1024]{2,1,0:T(8,128)(2,1)} %copies.1), calls=%async_computation.2 | async-start | bytes 1048576 | tf_op jit(solution)/shard_map/all_to_all | solution.py:413
  9.0 0.8 ends.1
  9.8 3.4 %collective-permute-start = (bf16[16,1280]{1,0:T(8,128)(2,1)S(1)}, bf16[16,1280]{1,0:T(8,128)(2,1)S(1)}, u32[]{:S(2)}, u32[]{:S(2)}) collective-permute-start(bf16[16,1280]{1,0:T(8,128)(2,1)S(1)} %ends.1), channel_id=1, source_target_pairs={{0,4},{4,8},{8,12},{12,16},{16,20},{20,24},{24,28},{1,5},{5,9},{9,... | collective-permute-start | bytes 122888 | tf_op jit(solution)/shard_map/ppermute | solution.py:495
  13.2 1.7 %collective-permute-done.ends_ref = bf16[16,1280]{1,0:T(8,128)(2,1)S(1)} collective-permute-done((bf16[16,1280]{1,0:T(8,128)(2,1)S(1)}, bf16[16,1280]{1,0:T(8,128)(2,1)S(1)}, u32[]{:S(2)}, u32[]{:S(2)}) %collective-permute-start) | collective-permute-done | bytes 40992 | tf_op jit(solution)/shard_map/ppermute | solution.py:495
  14.9 4.5 %front.1 = (f32[256,1024]{1,0:T(8,128)S(1)}, f32[256,1024]{1,0:T(8,128)S(1)}, f32[256,256]{1,0:T(8,128)S(1)}, f32[16,256]{1,0:T(8,128)S(1)}, f32[256,16]{1,0:T(8,128)S(1)}, /*index=5*/f32[8,136,128]{2,1,0:T(8,128)}) custom-call(bf16[256,1024]{1,0:T(8,128)(2,1)} %x_hbm.1, bf16[256,128]{1,0:T(8,128)(2,1)} %b_hbm.1, bf16[256,128]{1,0:T(8,128)(2,1)} %c_hbm.1, ...), custom_call_target="tpu_custom_call" | custom-call | flops 1000000000 | bytes 3682880 | tf_op jit(solution)/shard_map/front/pallas_call | solution.py:87
  19.4 1.0 %copy-done.2 = f32[256,1024]{1,0:T(8,128)} copy-done((f32[256,1024]{1,0:T(8,128)}, f32[256,1024]{1,0:T(8,128)S(1)}, u32[]{:S(2)}) %copy-start.2) | copy-done | bytes 1048600
  20.3 1.0 %copy-done.4 = f32[256,1024]{1,0:T(8,128)} copy-done((f32[256,1024]{1,0:T(8,128)}, f32[256,1024]{1,0:T(8,128)S(1)}, u32[]{:S(2)}) %copy-start.4) | copy-done | bytes 1048600
  21.3 2.2 %all-to-all-done.2 = bf16[4,64,1024]{2,1,0:T(8,128)(2,1)S(1)} async-done(((bf16[4,64,1024]{2,1,0:T(8,128)(2,1)}), bf16[4,64,1024]{2,1,0:T(8,128)(2,1)S(1)}, u32[]{:S(2)}, u32[]{:S(2)}) %all-to-all-start.2) | async-done | bytes 524320 | tf_op jit(solution)/shard_map/all_to_all | solution.py:413
  23.5 10.1 %all-to-all-start = ((f32[8,136,128]{2,1,0:T(8,128)}), f32[8,136,128]{2,1,0:T(8,128)S(1)}, u32[]{:S(2)}, u32[]{:S(2)}) async-start(f32[8,136,128]{2,1,0:T(8,128)} %get-tuple-element.22), calls=%async_computation | async-start | bytes 1114112 | tf_op jit(solution)/shard_map/all_to_all | solution.py:310
  33.6 2.0 %collective-permute-start.3 = (bf16[256,1024]{1,0:T(8,128)(2,1)S(1)}, bf16[256,1024]{1,0:T(8,128)(2,1)S(1)}, u32[]{:S(2)}, u32[]{:S(2)}) collective-permute-start(bf16[256,1024]{1,0:T(8,128)(2,1)S(1)} %bitcast.4), channel_id=1, source_target_pairs={{0,4},{4,0},{8,12},{12,8},{16,20},{20,16},{24,28},{28,24},{1,5},{5... | collective-permute-start | bytes 1572872 | tf_op jit(solution)/shard_map/ppermute | solution.py:351
  35.6 1.5 %collective-permute-start.1 = (bf16[256,1024]{1,0:T(8,128)(2,1)S(1)}, bf16[256,1024]{1,0:T(8,128)(2,1)S(1)}, u32[]{:S(2)}, u32[]{:S(2)}) collective-permute-start(bf16[256,1024]{1,0:T(8,128)(2,1)S(1)} %bitcast.5), channel_id=1, source_target_pairs={{0,2},{1,3},{2,0},{3,1},{4,6},{5,7},{6,4},{7,5},{8,10},{9,11},{10,... | collective-permute-start | bytes 1572872 | tf_op jit(solution)/shard_map/ppermute | solution.py:351
  37.1 14.5 %collective-permute-done.3.x = bf16[256,1024]{1,0:T(8,128)(2,1)S(1)} collective-permute-done((bf16[256,1024]{1,0:T(8,128)(2,1)S(1)}, bf16[256,1024]{1,0:T(8,128)(2,1)S(1)}, u32[]{:S(2)}, u32[]{:S(2)}) %collective-permute-start.3) | collective-permute-done | bytes 524320 | tf_op jit(solution)/shard_map/ppermute | solution.py:351
  51.7 0.9 prefix.1
  52.6 4.5 %all-to-all-start.1 = ((f32[8,128,128]{2,1,0:T(8,128)}), f32[8,128,128]{2,1,0:T(8,128)}, u32[]{:S(2)}, u32[]{:S(2)}) async-start(f32[8,128,128]{2,1,0:T(8,128)} %prefix.1), calls=%async_computation.1 | async-start | bytes 1048576 | tf_op jit(solution)/shard_map/all_to_all | solution.py:319
  57.2 2.1 %collective-permute-start.2 = (bf16[128,1024]{1,0:T(8,128)(2,1)S(1)}, bf16[128,1024]{1,0:T(8,128)(2,1)S(1)}, u32[]{:S(2)}, u32[]{:S(2)}) collective-permute-start(bf16[128,1024]{1,0:T(8,128)(2,1)S(1)} %slice.8), channel_id=1, source_target_pairs={{0,4},{4,0},{8,12},{12,8},{16,20},{20,16},{24,28},{28,24},{1,5},{5... | collective-permute-start | bytes 786440 | tf_op jit(solution)/shard_map/ppermute | solution.py:351
  59.3 1.6 %collective-permute-start.4 = (bf16[128,1024]{1,0:T(8,128)(2,1)S(1)}, bf16[128,1024]{1,0:T(8,128)(2,1)S(1)}, u32[]{:S(2)}, u32[]{:S(2)}) collective-permute-start(bf16[128,1024]{1,0:T(8,128)(2,1)S(1)} %slice.9), channel_id=1, source_target_pairs={{0,2},{1,3},{2,0},{3,1},{4,6},{5,7},{6,4},{7,5},{8,10},{9,11},{10,... | collective-permute-start | bytes 786440 | tf_op jit(solution)/shard_map/ppermute | solution.py:351
  60.9 1.2 %copy-done.3 = f32[256,1024]{1,0:T(8,128)S(1)} copy-done((f32[256,1024]{1,0:T(8,128)S(1)}, f32[256,1024]{1,0:T(8,128)}, u32[]{:S(2)}) %copy-start.3) | copy-done | bytes 1048600
  62.1 1.2 %copy-done.5 = f32[256,1024]{1,0:T(8,128)S(1)} copy-done((f32[256,1024]{1,0:T(8,128)S(1)}, f32[256,1024]{1,0:T(8,128)}, u32[]{:S(2)}) %copy-start.5) | copy-done | bytes 1048600
  63.3 5.5 %inner.1 = (f32[256,1024]{1,0:T(8,128)S(1)}, f32[256,1024]{1,0:T(8,128)S(1)}, f32[1,1024]{1,0:T(1,128)S(1)}, bf16[2,2,1024,1024]{3,2,1,0:T(8,128)(2,1)S(1)}) custom-call(bf16[1,4096,1024]{2,1,0:T(8,128)(2,1)} %w_gate.3, bf16[1,4096,1024]{2,1,0:T(8,128)(2,1)} %w_up.3, f32[1,1024]{1,0:T(1,128)} %bitcast.8, f32[256,1024]{1,0:T(8,128)S(1)} %copy-done.3, ...), custom_call_target="tpu_custom_call" | custom-call | flops 4000000000 | bytes 29663232 | tf_op jit(solution)/shard_map/inner/pallas_call | solution.py:87
  68.9 1.0 %copy-done.8 = f32[256,1024]{1,0:T(8,128)} copy-done((f32[256,1024]{1,0:T(8,128)}, f32[256,1024]{1,0:T(8,128)S(1)}, u32[]{:S(2)}) %copy-start.8) | copy-done | bytes 1048600
  69.9 1.0 %copy-done.10 = f32[256,1024]{1,0:T(8,128)} copy-done((f32[256,1024]{1,0:T(8,128)}, f32[256,1024]{1,0:T(8,128)S(1)}, u32[]{:S(2)}) %copy-start.10) | copy-done | bytes 1048600
  70.8 0.5 collective-permute-done.2.d0
  71.4 0.5 collective-permute-start.7
  71.8 0.8 copy-done.6
  72.6 1.0 %copy-done.1 = bf16[256,1024]{1,0:T(8,128)(2,1)S(1)} copy-done((bf16[256,1024]{1,0:T(8,128)(2,1)S(1)}, bf16[256,1024]{1,0:T(8,128)(2,1)}, u32[]{:S(2)}) %copy-start.1) | copy-done | bytes 524312
  73.7 1.0 %copy-done.7 = bf16[256,1024]{1,0:T(8,128)(2,1)S(1)} copy-done((bf16[256,1024]{1,0:T(8,128)(2,1)S(1)}, bf16[256,1024]{1,0:T(8,128)(2,1)}, u32[]{:S(2)}) %copy-start.7) | copy-done | bytes 524312
  74.7 8.8 %first.1 = (f32[512,1024]{1,0:T(8,128)S(1)}, f32[512,1024]{1,0:T(8,128)S(1)}, bf16[2,2,1024,1024]{3,2,1,0:T(8,128)(2,1)S(1)}) custom-call(bf16[1,4096,1024]{2,1,0:T(8,128)(2,1)} %w_gate.3, bf16[1,4096,1024]{2,1,0:T(8,128)(2,1)} %w_up.3, bf16[2,2,1024,1024]{3,2,1,0:T(8,128)(2,1)S(1)} %get-tuple-element.24.held_ref, bf16[256,1024]{1,0:T(8,128)(2,1)S(1)} %bitcast.7, ...), custom_call_target="tpu_custom_call" | custom-call | flops 4294967296 | bytes 39845888 | tf_op jit(solution)/shard_map/first/pallas_call | solution.py:87
  83.6 6.2 %second.1 = bf16[1,512,1024]{2,1,0:T(8,128)(2,1)} custom-call(bf16[256,1024]{1,0:T(8,128)(2,1)S(1)} %collective-permute-done.1.y, bf16[128,1024]{1,0:T(8,128)(2,1)S(1)} %collective-permute-done.2.d0, bf16[128,1024]{1,0:T(8,128)(2,1)S(1)} %collective-permute-done.4.d1, bf16[256,1024]{1,0:T(8,128)(2,1)S(1)} %collective-permute-done.5.cy, ...), custom_call_target="tpu_custom_call" | custom-call | flops 4294967296 | bytes 16285696 | tf_op jit(solution)/shard_map/second/pallas_call | solution.py:87
  89.8 1.2 %copy-done.9 = f32[256,1024]{1,0:T(8,128)S(1)} copy-done((f32[256,1024]{1,0:T(8,128)S(1)}, f32[256,1024]{1,0:T(8,128)}, u32[]{:S(2)}) %copy-start.9) | copy-done | bytes 1048600
  91.0 1.2 %copy-done.11 = f32[256,1024]{1,0:T(8,128)S(1)} copy-done((f32[256,1024]{1,0:T(8,128)S(1)}, f32[256,1024]{1,0:T(8,128)}, u32[]{:S(2)}) %copy-start.11) | copy-done | bytes 1048600
  92.3 3.6 %back.1 = bf16[256,1024]{1,0:T(8,128)(2,1)} custom-call(f32[256,1024]{1,0:T(8,128)S(1)} %copy-done.9, f32[256,1024]{1,0:T(8,128)S(1)} %copy-done.11, f32[8,128,128]{2,1,0:T(8,128)} %all-to-all-done.1.start_ref, f32[256,256]{1,0:T(8,128)S(1)} %get-tuple-element.17.bc_ref, f32[1,1024]{1,0:T(1,128)S(1)} %get-tuple-element.23.gain_ref), custom_call_target="tpu_custom_call" | custom-call | flops 1000000000 | bytes 3411968 | tf_op jit(solution)/shard_map/back/pallas_call | solution.py:87
  (28 shorter events, 0.1 us)
Async XLA Ops:
  2.7 20.8 %all-to-all-start.2 = ((bf16[4,64,1024]{2,1,0:T(8,128)(2,1)}), bf16[4,64,1024]{2,1,0:T(8,128)(2,1)S(1)}, u32[]{:S(2)}, u32[]{:S(2)}) async-start(bf16[4,64,1024]{2,1,0:T(8,128)(2,1)} %copies.1), calls=%async_computation.2 | async-start | bytes 1048576 | tf_op jit(solution)/shard_map/all_to_all | solution.py:413
  9.8 5.1 %collective-permute-start = (bf16[16,1280]{1,0:T(8,128)(2,1)S(1)}, bf16[16,1280]{1,0:T(8,128)(2,1)S(1)}, u32[]{:S(2)}, u32[]{:S(2)}) collective-permute-start(bf16[16,1280]{1,0:T(8,128)(2,1)S(1)} %ends.1), channel_id=1, source_target_pairs={{0,4},{4,8},{8,12},{12,16},{16,20},{20,24},{24,28},{1,5},{5,9},{9,... | collective-permute-start | bytes 122888 | tf_op jit(solution)/shard_map/ppermute | solution.py:495
  19.3 1.0 %copy-start.2 = (f32[256,1024]{1,0:T(8,128)}, f32[256,1024]{1,0:T(8,128)S(1)}, u32[]{:S(2)}) copy-start(f32[256,1024]{1,0:T(8,128)S(1)} %get-tuple-element.15.drive_ref) | copy-start | bytes 3145732
  20.3 1.0 %copy-start.4 = (f32[256,1024]{1,0:T(8,128)}, f32[256,1024]{1,0:T(8,128)S(1)}, u32[]{:S(2)}) copy-start(f32[256,1024]{1,0:T(8,128)S(1)} %get-tuple-element.16.direct_ref) | copy-start | bytes 3145732
  23.5 28.2 %all-to-all-start = ((f32[8,136,128]{2,1,0:T(8,128)}), f32[8,136,128]{2,1,0:T(8,128)S(1)}, u32[]{:S(2)}, u32[]{:S(2)}) async-start(f32[8,136,128]{2,1,0:T(8,128)} %get-tuple-element.22), calls=%async_computation | async-start | bytes 1114112 | tf_op jit(solution)/shard_map/all_to_all | solution.py:310
  33.6 18.1 %collective-permute-start.3 = (bf16[256,1024]{1,0:T(8,128)(2,1)S(1)}, bf16[256,1024]{1,0:T(8,128)(2,1)S(1)}, u32[]{:S(2)}, u32[]{:S(2)}) collective-permute-start(bf16[256,1024]{1,0:T(8,128)(2,1)S(1)} %bitcast.4), channel_id=1, source_target_pairs={{0,4},{4,0},{8,12},{12,8},{16,20},{20,16},{24,28},{28,24},{1,5},{5... | collective-permute-start | bytes 1572872 | tf_op jit(solution)/shard_map/ppermute | solution.py:351
  35.6 21.5 %collective-permute-start.1 = (bf16[256,1024]{1,0:T(8,128)(2,1)S(1)}, bf16[256,1024]{1,0:T(8,128)(2,1)S(1)}, u32[]{:S(2)}, u32[]{:S(2)}) collective-permute-start(bf16[256,1024]{1,0:T(8,128)(2,1)S(1)} %bitcast.5), channel_id=1, source_target_pairs={{0,2},{1,3},{2,0},{3,1},{4,6},{5,7},{6,4},{7,5},{8,10},{9,11},{10,... | collective-permute-start | bytes 1572872 | tf_op jit(solution)/shard_map/ppermute | solution.py:351
  37.1 34.7 %collective-permute-start.8 = (bf16[256,1024]{1,0:T(8,128)(2,1)S(1)}, bf16[256,1024]{1,0:T(8,128)(2,1)S(1)}, u32[]{:S(2)}, u32[]{:S(2)}) collective-permute-start(bf16[256,1024]{1,0:T(8,128)(2,1)S(1)} %bitcast.6), channel_id=1, source_target_pairs={{0,1},{1,0},{2,3},{3,2},{4,5},{5,4},{6,7},{7,6},{8,9},{9,8},{10,11... | collective-permute-start | bytes 1572872 | tf_op jit(solution)/shard_map/ppermute | solution.py:351
  51.7 17.2 %copy-start = (bf16[256,1024]{1,0:T(8,128)(2,1)}, bf16[256,1024]{1,0:T(8,128)(2,1)S(1)}, u32[]{:S(2)}) copy-start(bf16[256,1024]{1,0:T(8,128)(2,1)S(1)} %collective-permute-done.3.x) | copy-start | bytes 1572868
  51.7 21.0 %collective-permute-start.9 = (bf16[256,1024]{1,0:T(8,128)(2,1)S(1)}, bf16[256,1024]{1,0:T(8,128)(2,1)}, u32[]{:S(2)}, u32[]{:S(2)}) collective-permute-start(bf16[256,1024]{1,0:T(8,128)(2,1)S(1)} %collective-permute-done.3.x), channel_id=1, source_target_pairs={{0,1},{1,0},{2,3},{3,2},{4,5},{5,4},{6,7},{7,6},{8,9},{9,8},{10,11... | collective-permute-start | bytes 1572872 | tf_op jit(solution)/shard_map/ppermute | solution.py:351
  52.6 37.2 %all-to-all-start.1 = ((f32[8,128,128]{2,1,0:T(8,128)}), f32[8,128,128]{2,1,0:T(8,128)}, u32[]{:S(2)}, u32[]{:S(2)}) async-start(f32[8,128,128]{2,1,0:T(8,128)} %prefix.1), calls=%async_computation.1 | async-start | bytes 1048576 | tf_op jit(solution)/shard_map/all_to_all | solution.py:319
  57.2 14.1 %collective-permute-start.2 = (bf16[128,1024]{1,0:T(8,128)(2,1)S(1)}, bf16[128,1024]{1,0:T(8,128)(2,1)S(1)}, u32[]{:S(2)}, u32[]{:S(2)}) collective-permute-start(bf16[128,1024]{1,0:T(8,128)(2,1)S(1)} %slice.8), channel_id=1, source_target_pairs={{0,4},{4,0},{8,12},{12,8},{16,20},{20,16},{24,28},{28,24},{1,5},{5... | collective-permute-start | bytes 786440 | tf_op jit(solution)/shard_map/ppermute | solution.py:351
  59.3 12.1 %collective-permute-start.4 = (bf16[128,1024]{1,0:T(8,128)(2,1)S(1)}, bf16[128,1024]{1,0:T(8,128)(2,1)S(1)}, u32[]{:S(2)}, u32[]{:S(2)}) collective-permute-start(bf16[128,1024]{1,0:T(8,128)(2,1)S(1)} %slice.9), channel_id=1, source_target_pairs={{0,2},{1,3},{2,0},{3,1},{4,6},{5,7},{6,4},{7,5},{8,10},{9,11},{10,... | collective-permute-start | bytes 786440 | tf_op jit(solution)/shard_map/ppermute | solution.py:351
  60.9 22.7 %collective-permute-start.5 = (bf16[256,1024]{1,0:T(8,128)(2,1)S(1)}, bf16[256,1024]{1,0:T(8,128)(2,1)S(1)}, u32[]{:S(2)}, u32[]{:S(2)}) collective-permute-start(bf16[256,1024]{1,0:T(8,128)(2,1)S(1)} %collective-permute-done.1.y), channel_id=1, source_target_pairs={{0,1},{1,0},{2,3},{3,2},{4,5},{5,4},{6,7},{7,6},{8,9},{9,8},{10,11... | collective-permute-start | bytes 1572872 | tf_op jit(solution)/shard_map/ppermute | solution.py:351
  60.9 1.2 %copy-start.3 = (f32[256,1024]{1,0:T(8,128)S(1)}, f32[256,1024]{1,0:T(8,128)}, u32[]{:S(2)}) copy-start(f32[256,1024]{1,0:T(8,128)} %copy-done.2) | copy-start | bytes 3145732
  62.1 1.2 %copy-start.5 = (f32[256,1024]{1,0:T(8,128)S(1)}, f32[256,1024]{1,0:T(8,128)}, u32[]{:S(2)}) copy-start(f32[256,1024]{1,0:T(8,128)} %copy-done.4) | copy-start | bytes 3145732
  68.9 1.0 %copy-start.8 = (f32[256,1024]{1,0:T(8,128)}, f32[256,1024]{1,0:T(8,128)S(1)}, u32[]{:S(2)}) copy-start(f32[256,1024]{1,0:T(8,128)S(1)} %get-tuple-element.20.pre_ref) | copy-start | bytes 3145732
  69.9 1.0 %copy-start.10 = (f32[256,1024]{1,0:T(8,128)}, f32[256,1024]{1,0:T(8,128)S(1)}, u32[]{:S(2)}) copy-start(f32[256,1024]{1,0:T(8,128)S(1)} %get-tuple-element.21.decay_ref) | copy-start | bytes 3145732
  71.3 12.2 %collective-permute-start.6 = (bf16[128,1024]{1,0:T(8,128)(2,1)S(1)}, bf16[128,1024]{1,0:T(8,128)(2,1)S(1)}, u32[]{:S(2)}, u32[]{:S(2)}) collective-permute-start(bf16[128,1024]{1,0:T(8,128)(2,1)S(1)} %collective-permute-done.2.d0), channel_id=1, source_target_pairs={{0,1},{1,0},{2,3},{3,2},{4,5},{5,4},{6,7},{7,6},{8,9},{9,8},{10,11... | collective-permute-start | bytes 786440 | tf_op jit(solution)/shard_map/ppermute | solution.py:351
  71.4 12.2 %collective-permute-start.7 = (bf16[128,1024]{1,0:T(8,128)(2,1)S(1)}, bf16[128,1024]{1,0:T(8,128)(2,1)S(1)}, u32[]{:S(2)}, u32[]{:S(2)}) collective-permute-start(bf16[128,1024]{1,0:T(8,128)(2,1)S(1)} %collective-permute-done.4.d1), channel_id=1, source_target_pairs={{0,1},{1,0},{2,3},{3,2},{4,5},{5,4},{6,7},{7,6},{8,9},{9,8},{10,11... | collective-permute-start | bytes 786440 | tf_op jit(solution)/shard_map/ppermute | solution.py:351
  71.8 0.8 copy-start.6
  72.6 1.0 %copy-start.1 = (bf16[256,1024]{1,0:T(8,128)(2,1)S(1)}, bf16[256,1024]{1,0:T(8,128)(2,1)}, u32[]{:S(2)}) copy-start(bf16[256,1024]{1,0:T(8,128)(2,1)} %copy-done) | copy-start | bytes 1572868
  73.7 1.0 %copy-start.7 = (bf16[256,1024]{1,0:T(8,128)(2,1)S(1)}, bf16[256,1024]{1,0:T(8,128)(2,1)}, u32[]{:S(2)}) copy-start(bf16[256,1024]{1,0:T(8,128)(2,1)} %copy-done.6) | copy-start | bytes 1572868
  89.8 1.2 %copy-start.9 = (f32[256,1024]{1,0:T(8,128)S(1)}, f32[256,1024]{1,0:T(8,128)}, u32[]{:S(2)}) copy-start(f32[256,1024]{1,0:T(8,128)} %copy-done.8) | copy-start | bytes 3145732
  91.0 1.2 %copy-start.11 = (f32[256,1024]{1,0:T(8,128)S(1)}, f32[256,1024]{1,0:T(8,128)}, u32[]{:S(2)}) copy-start(f32[256,1024]{1,0:T(8,128)} %copy-done.10) | copy-start | bytes 3145732

commit v4 on v3

v4 whole, which is shorter than its diff:
```python
import functools

import jax
import jax.numpy as jnp
from jax import lax
from jax.experimental import pallas as pl
from jax.experimental.pallas import tpu as pltpu
from jax.sharding import PartitionSpec as P

HDIM = 64
STATE = 128
KCONV = 4
EDGE = 16
NOTES = 8

F32 = jnp.float32
BF16 = jnp.bfloat16


def dot16(a, b, contract=((1,), (0,))):
    return lax.dot_general(a, b, (contract, ((), ())), preferred_element_type=F32)


def halves(value):
    high = value.astype(BF16)
    return high, (value - high.astype(F32)).astype(BF16)


def dot(a, b, contract=((1,), (0,))):
    a_high, a_low = halves(a)
    b_high, b_low = halves(b)
    cross = dot16(a_high, b_low, contract) + dot16(a_low, b_high, contract)
    return dot16(a_high, b_high, contract) + cross


def dot_exact(a, b, contract=((1,), (0,))):
    high, rest = halves(a)
    low = (a - high.astype(F32) - rest.astype(F32)).astype(BF16)
    return dot16(high, b, contract) + (dot16(rest, b, contract) + dot16(low, b, contract))


def dot_left(a, b, contract=((1,), (0,))):
    high, low = halves(a)
    return dot16(high, b, contract) + dot16(low, b, contract)


FIRST = ((0,), (0,))


def iota(shape, axis):
    return lax.broadcasted_iota(jnp.int32, shape, axis)


def head_spread(heads):
    shape = (heads, heads * HDIM)
    return (iota(shape, 1) // HDIM == iota(shape, 0)).astype(BF16)


def upper_ones(length):
    return (iota((length, length), 0) <= iota((length, length), 1)).astype(BF16)


def silu(value):
    return value / (1.0 + jnp.exp(-value))


def one_minus_exp(value):
    series = jnp.ones_like(value)
    for n in range(8, 1, -1):
        series = 1.0 + value * series * (1.0 / n)
    return jnp.where(value > -0.25, -value * series, 1.0 - jnp.exp(value))


def started(sources, targets, sems, first=0):
    copies = []
    for i, (source, target) in enumerate(zip(sources, targets)):
        copies.append(pltpu.make_async_copy(source, target, sems.at[first + i]))
        copies[-1].start()
    return copies


def finished(copies):
    for copy in copies:
        copy.wait()


def call(body, outs, args, fixed=0, scratch=(), sems=0, flops=0, grant=8, near=False, name=None):
    moved = sum(a.size * a.dtype.itemsize for a in (*args, *outs))
    scratch = list(scratch) + ([pltpu.SemaphoreType.DMA((sems,))] if sems else [])
    space = pltpu.VMEM if near else pl.ANY
    args = [
        pltpu.with_memory_space_constraint(a, pltpu.HBM) if i < fixed else a
        for i, a in enumerate(args)
    ]
    spaces = [pltpu.HBM if i < fixed else space for i in range(len(args))]
    return pl.pallas_call(
        body,
        out_shape=outs,
        in_specs=[pl.BlockSpec(memory_space=s) for s in spaces],
        out_specs=[pl.BlockSpec(memory_space=space)] * len(outs),
        scratch_shapes=scratch,
        compiler_params=pltpu.CompilerParams(vmem_limit_bytes=grant * 2**20),
        cost_estimate=pl.CostEstimate(flops=flops, bytes_accessed=moved, transcendentals=0),
        name=name,
    )(*args)


def room(arrays):
    return [pltpu.VMEM(a.shape, a.dtype) for a in arrays]


def array(shape, dtype):
    return jax.ShapeDtypeStruct(shape, dtype)


def ends_body(x_ref, b_ref, c_ref, ends_ref, sems):
    tokens, channels = x_ref.shape
    cut = pl.ds(tokens - EDGE, EDGE)
    finished(
        started(
            [x_ref.at[cut, :], b_ref.at[cut, :], c_ref.at[cut, :]],
            [
                ends_ref.at[:, pl.ds(0, channels)],
                ends_ref.at[:, pl.ds(channels, STATE)],
                ends_ref.at[:, pl.ds(channels + STATE, STATE)],
            ],
            sems,
        )
    )


def front_body(by_tokens, count, *refs):
    far, outs, rest = refs[:count], refs[count : count + 4], refs[count + 4 :]
    near, scratch, pad_ref, sems = rest[:count], rest[count : count + 4], rest[-2], rest[-1]
    copies = started(far, near, sems)
    x_ref, b_ref, c_ref, taps_ref, taps_bc_ref, logs_ref, skip_ref, ids_ref, ends_ref = near
    xconv_ref, bc_ref, lines_ref, slab_ref = scratch
    tokens, channels = x_ref.shape
    heads = logs_ref.shape[0]
    finished(copies)
    pad_ref[0:8, :] = ends_ref[...].astype(F32)[EDGE - 8 : EDGE]
    pad_ref[8 : 8 + tokens, :channels] = x_ref[...].astype(F32)
    pad_ref[8 : 8 + tokens, channels : channels + STATE] = b_ref[...].astype(F32)
    pad_ref[8 : 8 + tokens, channels + STATE :] = c_ref[...].astype(F32)

    def conv(taps, start, stop):
        total = jnp.zeros((tokens, stop - start), F32)
        for k in range(KCONV):
            first = 8 - (KCONV - 1) + k
            total = total + taps[k : k + 1] * pad_ref[first : first + tokens, start:stop]
        return silu(total)

    bc = conv(taps_bc_ref[...], channels, channels + 2 * STATE)
    bc_ref[...] = bc
    xconv = conv(taps_ref[...], 0, channels)
    xconv_ref[...] = xconv
    logs = logs_ref[...]
    inflow = jnp.sqrt(one_minus_exp(2.0 * logs))
    within = dot_exact(logs, upper_ones(tokens))
    lines_ref[0] = within
    lines_ref[1] = inflow
    out_copies = started(scratch[:3], outs[:3], sems)
    total = within[:, tokens - 1 :]
    remain = jnp.exp(total - within)
    spread = head_spread(heads)
    state = dot(bc[:, :STATE], xconv * dot_left(inflow * remain, spread, FIRST), FIRST)
    notes = dot_exact(jnp.exp(jnp.broadcast_to(total, (heads, NOTES))), spread, FIRST)
    if by_tokens:
        parts, _, share = slab_ref.shape
        ids = ids_ref[...].astype(F32)
        line = jnp.concatenate([ids[0:1], ids[1:2]], axis=1)
        for i in range(parts):
            cut = slice(i * share, (i + 1) * share)
            slab_ref[i, :STATE] = state[:, cut]
            slab_ref[i, STATE:] = jnp.where(iota((NOTES, share), 0) == 1, line, notes[:, cut])
    else:
        slab_ref[:STATE] = state
        slab_ref[STATE:] = notes
    finished(out_copies + started(scratch[3:], outs[3:], sems, 3))


def inner_body(skip_far, xconv_far, bc_far, lines_far, pre_far, decay_far, *rest):
    far = (skip_far, xconv_far, bc_far, lines_far)
    skip_ref, xconv_ref, bc_ref, lines_ref, pre_ref, decay_ref, sems = rest
    finished(started(far, rest[:4], sems))
    tokens, channels = xconv_ref.shape
    heads = channels // HDIM
    row = lines_ref[0]
    column = row.T
    spread = head_spread(heads)
    decay_ref[...] = dot_left(jnp.exp(row), spread, FIRST)
    copies = started([decay_ref], [decay_far], sems)
    inflow = dot_left(lines_ref[1], spread, FIRST)
    skip = dot_exact(skip_ref[...], spread)
    meet = dot(bc_ref[:, STATE:], bc_ref[:, :STATE], ((1,), (1,)))
    lower = iota((tokens, tokens), 0) >= iota((tokens, tokens), 1)
    left = iota((tokens, 2 * HDIM), 1) < HDIM
    for pair in range(heads // 2):
        cut = slice(pair * 2 * HDIM, (pair + 1) * 2 * HDIM)
        xconv = xconv_ref[:, cut]
        d_high, d_low = halves(xconv * inflow[:, cut])
        both = []
        for h in (2 * pair, 2 * pair + 1):
            gap = column[:, h : h + 1] - row[h : h + 1, :]
            mix = jnp.where(lower, jnp.exp(gap), 0.0) * meet
            m_high, m_low = halves(mix)
            both.append(dot16(m_high, d_high) + dot16(m_high, d_low) + dot16(m_low, d_high))
        pre_ref[:, cut] = skip[:, cut] * xconv + jnp.where(left, both[0], both[1])
    finished(copies + started([pre_ref], [pre_far], sems, 1))


def prefix_body(parts_ref, starts_ref):
    ctx, rows, share = starts_ref.shape
    state = jnp.zeros((rows, share), F32)
    for i in range(ctx):
        starts_ref[i] = state
        if i < ctx - 1:
            state = parts_ref[i, STATE : STATE + 1] * state + parts_ref[i, :STATE]


def back_body(cuts, gain_far, pre_far, decay_far, start_far, bc_far, out_far, *rest):
    far = (start_far, bc_far, pre_far, decay_far, gain_far)
    start_ref, bc_ref, pre_ref, decay_ref, gain_ref, out_ref, sems = rest
    copies = started(far, rest[:5], sems)
    channels = pre_ref.shape[1]
    width = min(channels, 4 * HDIM)
    group = (iota((width, width), 0) // HDIM == iota((width, width), 1) // HDIM).astype(BF16)
    finished(copies)
    c_high, c_low = halves(bc_ref[:, STATE:])
    copies = []
    for i in range(channels // width):
        cut = slice(i * width, (i + 1) * width)
        if cuts:
            start = jnp.concatenate([start_ref[2 * i], start_ref[2 * i + 1]], axis=1)
        else:
            start = start_ref[:, cut]
        s_high, s_low = halves(start)
        carried = dot16(c_high, s_high) + dot16(c_high, s_low) + dot16(c_low, s_high)
        pre = pre_ref[:, cut] + carried * decay_ref[:, cut]
        mean = dot_left(pre * pre, group) * (1.0 / HDIM)
        out_ref[:, cut] = (pre * lax.rsqrt(mean + 1e-05) * gain_ref[:, cut]).astype(BF16)
        copies += started([out_ref.at[:, cut]], [out_far.at[:, cut]], sems, i)
    finished(copies)


def mixing(seq_input, b_input, c_input, before, conv_x, conv_bc, log_decay, skip, gain, ids):
    tokens, channels = seq_input.shape
    heads = skip.shape[0]
    ctx = lax.axis_size("ctx")
    share = channels // ctx
    cuts = share == 2 * HDIM
    skip = skip.reshape(1, heads)
    square = array((tokens, channels), F32)
    slabs = (ctx, STATE + NOTES, share) if cuts else (STATE + NOTES, channels)
    outs = [
        square,
        array((tokens, 2 * STATE), F32),
        array((2, heads, tokens), F32),
        array(slabs, F32),
    ]
    args = (seq_input, b_input, c_input, conv_x, conv_bc, log_decay, skip, ids.T, before)
    xconv, bc, lines, slab = call(
        functools.partial(front_body, cuts, len(args)),
        outs,
        args,
        fixed=len(args) - 1,
        scratch=room(args)
        + room(outs)
        + [pltpu.VMEM((8 + tokens, channels + 2 * STATE), F32)],
        sems=len(args),
        flops=10**9,
        grant=16,
        name="front",
    )
    if not cuts:
        slab = slab.reshape(STATE + NOTES, ctx, share).transpose(1, 0, 2)
    parts = lax.all_to_all(slab, "ctx", split_axis=0, concat_axis=0, tiled=True)
    starts = call(
        prefix_body,
        [array((ctx, STATE, share), F32)],
        (parts,),
        flops=10**6,
        near=True,
        name="prefix",
    )[0]
    start = lax.all_to_all(starts, "ctx", split_axis=0, concat_axis=0, tiled=True)
    if not cuts:
        start = start.transpose(1, 0, 2).reshape(STATE, channels)
    args = (skip, xconv, bc, lines)
    outs = [square, square]
    pre, decay = call(
        inner_body,
        outs,
        args,
        fixed=1,
        scratch=room(args) + room(outs),
        sems=4,
        flops=4 * 10**9,
        grant=16,
        name="inner",
    )
    args = (gain.reshape(1, channels), pre, decay, start, bc)
    outs = [array((tokens, channels), BF16)]
    mixed = call(
        functools.partial(back_body, cuts),
        outs,
        args,
        fixed=1,
        scratch=room([start, bc, pre, decay, args[0]]) + room(outs),
        sems=5,
        flops=10**9,
        grant=16,
        name="back",
    )[0]
    return mixed, parts


TILE = 256


def join_body(a_ref, b_ref, out_ref, sems):
    rows = a_ref.shape[0]
    finished(
        started([a_ref, b_ref], [out_ref.at[pl.ds(0, rows), :], out_ref.at[pl.ds(rows, rows), :]], sems)
    )


def swapped(block, axis, bit):
    return lax.ppermute(block, axis, [(i, i ^ bit) for i in range(lax.axis_size(axis))])


def expert_body(pieces, *refs):
    (w_gate, w_up), far, (notes_far, out_far) = refs[:2], refs[2 : pieces + 2], refs[pieces + 2 : pieces + 4]
    rows_ref, held_ref, notes_ref, pick_ref, hid_ref, out_ref, sems, w_sems = refs[pieces + 4 :]
    length, width = rows_ref.shape
    depth = width // 4
    step = length // 4
    tiles = out_ref.shape[1] // TILE
    blocks = notes_ref.shape[0]
    rows = length // blocks
    me = lax.axis_index("exp")
    here = lax.axis_index("ctx")

    def piece_copies(k):
        cut = pl.ds(k * depth, depth)
        targets = [rows_ref.at[pl.ds(i * step, step), cut] for i in range(4)]
        return [
            pltpu.make_async_copy(far[4 * k + i], targets[i], sems.at[4 * k + i]) for i in range(4)
        ]

    def weight_copies(n, k):
        down = pl.ds(pl.multiple_of((me ^ k) * depth, depth), depth)
        across = pl.ds(n * TILE, TILE)
        return [
            pltpu.make_async_copy(
                w.at[0, down, across], held_ref.at[i, n, k], w_sems.at[i, n, k]
            )
            for i, w in enumerate((w_gate, w_up))
        ]

    for k in range(4):
        for copy in piece_copies(k) + weight_copies(0, k):
            copy.start()
    notes = pltpu.make_async_copy(
        notes_far.at[:, pl.ds(STATE, NOTES), :], notes_ref, sems.at[pieces]
    )
    notes.start()
    for n in range(1, tiles):
        for k in range(4):
            for copy in weight_copies(n, k):
                copy.start()

    shape = (rows, rows)
    earlier = (iota(shape, 1) < iota(shape, 0)).astype(F32)
    across = iota(shape, 1)
    diagonal = iota(shape, 0) == across
    out_copies = []
    for n in range(tiles):
        cut = slice(n * TILE, (n + 1) * TILE)
        gate = upper = None
        for k in range(4):
            if n == 0:
                finished(piece_copies(k))
            finished(weight_copies(n, k))
            block = rows_ref[:, k * depth : (k + 1) * depth]
            more = dot16(block, held_ref[0, n, k])
            gate = more if k == 0 else gate + more
            more = dot16(block, held_ref[1, n, k])
            upper = more if k == 0 else upper + more
        hid_ref[...] = (silu(gate) * upper).astype(BF16)
        if n == 0:
            notes.wait()
        for place in range(blocks):
            side, turn = place // 4, place % 4
            block = here ^ (2 * turn + side)
            if n == 0:
                line = notes_ref[block][1:2, :]
                mine = me.astype(F32)
                named = ((line[:, :rows] == mine) | (line[:, rows : 2 * rows] == mine)).astype(F32)
                column = jnp.sum(jnp.where(diagonal, named, 0.0), axis=1, keepdims=True)
                position = jnp.sum(earlier * named, axis=1, keepdims=True).astype(jnp.int32)
                pick_ref[place] = jnp.where(position == across, column, 0.0).astype(BF16)
            picked = dot16(pick_ref[place], hid_ref[place * rows : (place + 1) * rows], FIRST)
            at = pl.ds(pl.multiple_of(block * rows, rows), rows)
            out_ref[at, cut] = picked.astype(BF16)
        out_copies += started([out_ref.at[:, cut]], [out_far.at[0, :, cut]], sems, n)
    finished(out_copies)


def experts_by_tokens(moe_input, notes, w_gate, w_up):
    rows, columns = moe_input.shape
    ctx = lax.axis_size("ctx")
    joined = call(
        join_body,
        [array((2 * rows, columns), BF16)],
        (moe_input, swapped(moe_input, "ctx", 2)),
        fixed=1,
        sems=2,
        name="join",
    )[0]
    z = (joined, swapped(joined, "ctx", 4))
    x = [swapped(a, "ctx", 1) for a in z]
    y = [swapped(a, "exp", 2) for a in z]
    d = (swapped(y[0], "ctx", 1), swapped(x[1], "exp", 2))
    here = [*z, *x]
    there = [*y, *d]
    beside = [swapped(a, "exp", 1) for a in here]
    corner = [swapped(a, "exp", 1) for a in there]
    pieces = here + beside + there + corner
    hidden = w_gate.shape[2]
    length = ctx * rows
    return call(
        functools.partial(expert_body, len(pieces)),
        [array((1, length, hidden), BF16)],
        (w_gate, w_up, *pieces, notes),
        fixed=2,
        scratch=[
            pltpu.VMEM((length, 4 * columns), BF16),
            pltpu.VMEM((2, hidden // TILE, 4, columns, TILE), BF16),
            pltpu.VMEM((ctx, NOTES, notes.shape[2]), F32),
            pltpu.VMEM((ctx, rows, rows), BF16),
            pltpu.VMEM((length, TILE), BF16),
            pltpu.VMEM((length, hidden), BF16),
            pltpu.SemaphoreType.DMA((len(pieces) + 1,)),
            pltpu.SemaphoreType.DMA((2, hidden // TILE, 4)),
        ],
        flops=4 * length * 4 * columns * hidden,
        grant=36,
        name="experts",
    )[0]


def slot_matrix(pairs, expert, capacity):
    named = jnp.any(pairs == expert, axis=1).astype(jnp.int32)
    position = jnp.cumsum(named) - named
    hit = position[None, :] == jnp.arange(capacity, dtype=jnp.int32)[:, None]
    return (hit & (named[None, :] > 0)).astype(BF16)


def experts_by_slots(moe_input, pairs, w_gate, w_up):
    experts = lax.axis_size("exp")
    capacity = 4 * moe_input.shape[0] // experts
    pick = jax.vmap(lambda e: slot_matrix(pairs, e, capacity))(jnp.arange(experts))
    slots = jnp.einsum("eqt,td->eqd", pick, moe_input, preferred_element_type=F32)
    routed = lax.all_to_all(slots.astype(BF16), "exp", split_axis=0, concat_axis=2, tiled=True)
    rows = lax.all_gather(routed[0], "ctx", axis=0, tiled=True)
    gate = jnp.dot(rows, w_gate[0], preferred_element_type=F32)
    upper = jnp.dot(rows, w_up[0], preferred_element_type=F32)
    return (jax.nn.silu(gate) * upper).astype(BF16)[None]


def on_device(
    seq_input,
    b_input,
    c_input,
    conv_x,
    conv_bc,
    log_decay,
    skip_gain,
    norm_gain,
    moe_input,
    expert_ids,
    w_gate,
    w_up,
):
    ctx = lax.axis_size("ctx")
    by_tokens = lax.axis_size("exp") == 4 and ctx == 8
    tokens, channels = seq_input.shape
    ends = call(
        ends_body,
        [array((EDGE, channels + 2 * STATE), BF16)],
        (seq_input, b_input, c_input),
        fixed=3,
        sems=3,
        name="ends",
    )[0]
    before = lax.ppermute(ends, "ctx", [(i, i + 1) for i in range(ctx - 1)])
    mixed, notes = mixing(
        seq_input,
        b_input,
        c_input,
        before,
        conv_x,
        conv_bc,
        log_decay,
        skip_gain,
        norm_gain,
        expert_ids,
    )
    if by_tokens:
        hidden = experts_by_tokens(moe_input, notes, w_gate, w_up)
    else:
        hidden = experts_by_slots(moe_input, expert_ids, w_gate, w_up)
    return (mixed, hidden)


def solution(mesh):
    in_specs = (
        P("ctx", "exp"),
        P("ctx", None),
        P("ctx", None),
        P(None, "exp"),
        P(),
        P("exp", "ctx"),
        P("exp"),
        P("exp"),
        P("ctx", "exp"),
        P("ctx", None),
        P("exp", None, "ctx"),
        P("exp", None, "ctx"),
    )
    out_specs = (P("ctx", "exp"), P("exp", None, "ctx"))
    return jax.shard_map(
        on_device, mesh=mesh, in_specs=in_specs, out_specs=out_specs, check_vma=False
    )
```

time: 96.7 us -> 95.3 us (0.986)
  waiting for transfers between devices: 18.9 us -> 23.7 us
  Pallas kernels: 32.4 us -> 29.1 us
  local copies, waits for them, and re-layouts: 11.7 us -> 9.17 us
    ppermute x9 -> x16, starting transfers between devices: 7.73 us -> 14.9 us  [swapped(): lax.ppermute(block, axis, [(i, i ^ bit) for i in range(lax.axis_size(axis...]
    ppermute x9 -> x16, waiting for transfers between devices: 15 us -> 22 us  [swapped(): lax.ppermute(block, axis, [(i, i ^ bit) for i in range(lax.axis_size(axis...]
    all_to_all x1 -> x0, starting transfers between devices: 6.33 us -> none  [experts_by_tokens(): lax.all_to_all(copies, 'ctx', split_axis=0, concat_axis=0, tiled=True, ax...]
    all_to_all x1, starting transfers between devices: 10.1 us -> 6.64 us  [mixing(): parts = lax.all_to_all(slab, 'ctx', split_axis=0, concat_axis=0, tiled=True)]
    pallas_call x8 -> x7, Pallas kernels: 32.4 us -> 29.1 us  [call(): pl.pallas_call(body, out_shape=outs, in_specs=[pl.BlockSpec(memory_space=...]
    unnamed x24 -> x18, local copies, waits for them, and re-layouts: 11.7 us -> 9.17 us
    all_to_all x1 -> x0, waiting for transfers between devices: 2.21 us -> none  [experts_by_tokens(): lax.all_to_all(copies, 'ctx', split_axis=0, concat_axis=0, tiled=True, ax...]
    ppermute x1, starting transfers between devices: 3.4 us -> 4.84 us  [on_device(): before = lax.ppermute(ends, 'ctx', [(i, i + 1) for i in range(ctx - 1)])]
  transfers between devices with their start and end apart: 13 -> 19, of which waited for: 4 -> 4; matrix products, arithmetic and copies ran while one was open for 0% -> 0% of each run, Pallas kernels for 28% -> 21%
where the time goes in v4:
time: 95.3 us; the launch traced here: 94.7 us
  starting transfers between devices  31.8 us (33%)
  Pallas kernels  29.1 us (31%)
  waiting for transfers between devices  23.7 us (25%)
  local copies, waits for them, and re-layouts  9.17 us (10%)
    pallas_call x7, Pallas kernels, call(): pl.pallas_call(body, out_shape=outs, in_specs=[pl.BlockSpec(memory_space=...  29.1 us
    ppermute x16, waiting for transfers between devices, swapped(): lax.ppermute(block, axis, [(i, i ^ bit) for i in range(lax.axis_size(axis...  22 us
    ppermute x16, starting transfers between devices, swapped(): lax.ppermute(block, axis, [(i, i ^ bit) for i in range(lax.axis_size(axis...  14.9 us
    unnamed x18, local copies, waits for them, and re-layouts  9.17 us
    all_to_all x1, starting transfers between devices, mixing(): parts = lax.all_to_all(slab, 'ctx', split_axis=0, concat_axis=0, tiled=True)  6.64 us
    all_to_all x1, starting transfers between devices, mixing(): lax.all_to_all(starts, 'ctx', split_axis=0, concat_axis=0, tiled=True)  5.46 us
    ppermute x1, starting transfers between devices, on_device(): before = lax.ppermute(ends, 'ctx', [(i, i + 1) for i in range(ctx - 1)])  4.84 us
  transfers between devices with their start and end apart: 19, of which 4 were waited for; matrix products, arithmetic and copies ran while one was open for 0% of the time, Pallas kernels for 21%

profile of v4, /device:TPU:0, one launch (start us, length us, event | category | flops | bytes accessed | tf_op | source)
XLA Modules:
  0.0 94.7 jit_solution(4594822897293897019)
XLA Ops:
  0.6 0.8 ends.1
  1.4 4.8 %collective-permute-start = (bf16[16,1280]{1,0:T(8,128)(2,1)S(1)}, bf16[16,1280]{1,0:T(8,128)(2,1)S(1)}, u32[]{:S(2)}, u32[]{:S(2)}) collective-permute-start(bf16[16,1280]{1,0:T(8,128)(2,1)S(1)} %ends.1), channel_id=1, source_target_pairs={{0,4},{4,8},{8,12},{12,16},{16,20},{20,24},{24,28},{1,5},{5,9},{9,... | collective-permute-start | bytes 122888 | tf_op jit(solution)/shard_map/ppermute | solution.py:497
  6.3 1.7 %collective-permute-done.refs_8_ = bf16[16,1280]{1,0:T(8,128)(2,1)S(1)} collective-permute-done((bf16[16,1280]{1,0:T(8,128)(2,1)S(1)}, bf16[16,1280]{1,0:T(8,128)(2,1)S(1)}, u32[]{:S(2)}, u32[]{:S(2)}) %collective-permute-start) | collective-permute-done | bytes 40992 | tf_op jit(solution)/shard_map/ppermute | solution.py:497
  7.9 5.0 %front.1 = (f32[256,1024]{1,0:T(8,128)S(1)}, f32[256,256]{1,0:T(8,128)S(1)}, f32[2,16,256]{2,1,0:T(8,128)S(1)}, f32[8,136,128]{2,1,0:T(8,128)}) custom-call(bf16[256,1024]{1,0:T(8,128)(2,1)} %refs_0_.2, bf16[256,128]{1,0:T(8,128)(2,1)} %refs_1_.2, bf16[256,128]{1,0:T(8,128)(2,1)} %refs_2_.1, f32[4,1024]{1,0:T(4,128)} %refs_3_.1, f32[4,256]{1,0:T(4,128)} %refs_4_.1, ...), custom_call_target="tpu_custom_call" | custom-call | flops 1000000000 | bytes 2634304 | tf_op jit(solution)/shard_map/front/pallas_call | solution.py:96
  13.0 0.7 copy-done.4
  13.7 1.0 %copy-done.7 = f32[256,1024]{1,0:T(8,128)} copy-done((f32[256,1024]{1,0:T(8,128)}, f32[256,1024]{1,0:T(8,128)S(1)}, u32[]{:S(2)}) %copy-start.7) | copy-done | bytes 1048600
  14.7 6.6 %all-to-all-start = ((f32[8,136,128]{2,1,0:T(8,128)}), f32[8,136,128]{2,1,0:T(8,128)S(1)}, u32[]{:S(2)}, u32[]{:S(2)}) async-start(f32[8,136,128]{2,1,0:T(8,128)} %get-tuple-element.13), calls=%async_computation | async-start | bytes 1114112 | tf_op jit(solution)/shard_map/all_to_all | solution.py:277
  21.3 2.0 %collective-permute-start.1 = (bf16[64,1024]{1,0:T(8,128)(2,1)}, bf16[64,1024]{1,0:T(8,128)(2,1)S(1)}, u32[]{:S(2)}, u32[]{:S(2)}) collective-permute-start(bf16[64,1024]{1,0:T(8,128)(2,1)} %a_ref.1), channel_id=1, source_target_pairs={{0,8},{4,12},{8,0},{12,4},{16,24},{20,28},{24,16},{28,20},{1,9},{5... | collective-permute-start | bytes 393224 | tf_op jit(solution)/shard_map/ppermute | solution.py:329
  23.3 10.3 %collective-permute-done.1.b_ref = bf16[64,1024]{1,0:T(8,128)(2,1)S(1)} collective-permute-done((bf16[64,1024]{1,0:T(8,128)(2,1)}, bf16[64,1024]{1,0:T(8,128)(2,1)S(1)}, u32[]{:S(2)}, u32[]{:S(2)}) %collective-permute-start.1) | collective-permute-done | bytes 131104 | tf_op jit(solution)/shard_map/ppermute | solution.py:329
  33.6 0.9 join.1.refs_2_
  34.6 3.1 %collective-permute-start.2 = (bf16[128,1024]{1,0:T(8,128)(2,1)S(1)}, bf16[128,1024]{1,0:T(8,128)(2,1)S(1)}, u32[]{:S(2)}, u32[]{:S(2)}) collective-permute-start(bf16[128,1024]{1,0:T(8,128)(2,1)S(1)} %join.1.refs_2_), channel_id=1, source_target_pairs={{0,16},{4,20},{8,24},{12,28},{16,0},{20,4},{24,8},{28,12},{1,17},{... | collective-permute-start | bytes 786440 | tf_op jit(solution)/shard_map/ppermute | solution.py:329
  37.7 1.5 %collective-permute-start.3 = (bf16[128,1024]{1,0:T(8,128)(2,1)S(1)}, bf16[128,1024]{1,0:T(8,128)(2,1)S(1)}, u32[]{:S(2)}, u32[]{:S(2)}) collective-permute-start(bf16[128,1024]{1,0:T(8,128)(2,1)S(1)} %join.1.refs_2_), channel_id=1, source_target_pairs={{0,4},{4,0},{8,12},{12,8},{16,20},{20,16},{24,28},{28,24},{1,5},{5... | collective-permute-start | bytes 786440 | tf_op jit(solution)/shard_map/ppermute | solution.py:329
  39.1 1.5 %collective-permute-start.9 = (bf16[128,1024]{1,0:T(8,128)(2,1)S(1)}, bf16[128,1024]{1,0:T(8,128)(2,1)S(1)}, u32[]{:S(2)}, u32[]{:S(2)}) collective-permute-start(bf16[128,1024]{1,0:T(8,128)(2,1)S(1)} %join.1.refs_2_), channel_id=1, source_target_pairs={{0,2},{1,3},{2,0},{3,1},{4,6},{5,7},{6,4},{7,5},{8,10},{9,11},{10,... | collective-permute-start | bytes 786440 | tf_op jit(solution)/shard_map/ppermute | solution.py:329
  40.7 6.5 %collective-permute-done.2.refs_3_ = bf16[128,1024]{1,0:T(8,128)(2,1)S(1)} collective-permute-done((bf16[128,1024]{1,0:T(8,128)(2,1)S(1)}, bf16[128,1024]{1,0:T(8,128)(2,1)S(1)}, u32[]{:S(2)}, u32[]{:S(2)}) %collective-permute-start.2) | collective-permute-done | bytes 262176 | tf_op jit(solution)/shard_map/ppermute | solution.py:329
  47.2 1.5 %collective-permute-start.4 = (bf16[128,1024]{1,0:T(8,128)(2,1)S(1)}, bf16[128,1024]{1,0:T(8,128)(2,1)S(1)}, u32[]{:S(2)}, u32[]{:S(2)}) collective-permute-start(bf16[128,1024]{1,0:T(8,128)(2,1)S(1)} %collective-permute-done.2.refs_3_), channel_id=1, source_target_pairs={{0,4},{4,0},{8,12},{12,8},{16,20},{20,16},{24,28},{28,24},{1,5},{5... | collective-permute-start | bytes 786440 | tf_op jit(solution)/shard_map/ppermute | solution.py:329
  48.7 0.5 collective-permute-start.7
  49.2 1.5 %collective-permute-start.10 = (bf16[128,1024]{1,0:T(8,128)(2,1)S(1)}, bf16[128,1024]{1,0:T(8,128)(2,1)S(1)}, u32[]{:S(2)}, u32[]{:S(2)}) collective-permute-start(bf16[128,1024]{1,0:T(8,128)(2,1)S(1)} %collective-permute-done.2.refs_3_), channel_id=1, source_target_pairs={{0,2},{1,3},{2,0},{3,1},{4,6},{5,7},{6,4},{7,5},{8,10},{9,11},{10,... | collective-permute-start | bytes 786440 | tf_op jit(solution)/shard_map/ppermute | solution.py:329
  50.7 0.6 collective-permute-start.11
  51.3 5.2 %collective-permute-done.4.refs_5_ = bf16[128,1024]{1,0:T(8,128)(2,1)S(1)} collective-permute-done((bf16[128,1024]{1,0:T(8,128)(2,1)S(1)}, bf16[128,1024]{1,0:T(8,128)(2,1)S(1)}, u32[]{:S(2)}, u32[]{:S(2)}) %collective-permute-start.4) | collective-permute-done | bytes 262176 | tf_op jit(solution)/shard_map/ppermute | solution.py:329
  56.4 1.5 %collective-permute-start.12 = (bf16[128,1024]{1,0:T(8,128)(2,1)S(1)}, bf16[128,1024]{1,0:T(8,128)(2,1)}, u32[]{:S(2)}, u32[]{:S(2)}) collective-permute-start(bf16[128,1024]{1,0:T(8,128)(2,1)S(1)} %collective-permute-done.4.refs_5_), channel_id=1, source_target_pairs={{0,2},{1,3},{2,0},{3,1},{4,6},{5,7},{6,4},{7,5},{8,10},{9,11},{10,... | collective-permute-start | bytes 786440 | tf_op jit(solution)/shard_map/ppermute | solution.py:329
  57.9 0.8 prefix.1
  58.8 5.5 %all-to-all-start.1 = ((f32[8,128,128]{2,1,0:T(8,128)}), f32[8,128,128]{2,1,0:T(8,128)S(1)}, u32[]{:S(2)}, u32[]{:S(2)}) async-start(f32[8,128,128]{2,1,0:T(8,128)} %prefix.1), calls=%async_computation.1 | async-start | bytes 1048576 | tf_op jit(solution)/shard_map/all_to_all | solution.py:286
  65.4 0.9 %copy-done.5 = f32[256,256]{1,0:T(8,128)S(1)} copy-done((f32[256,256]{1,0:T(8,128)S(1)}, f32[256,256]{1,0:T(8,128)}, u32[]{:S(2)}) %copy-start.5) | copy-done | bytes 262168
  66.4 1.2 %copy-done.8 = f32[256,1024]{1,0:T(8,128)S(1)} copy-done((f32[256,1024]{1,0:T(8,128)S(1)}, f32[256,1024]{1,0:T(8,128)}, u32[]{:S(2)}) %copy-start.8) | copy-done | bytes 1048600
  67.6 4.1 %inner.1 = (f32[256,1024]{1,0:T(8,128)S(1)}, f32[256,1024]{1,0:T(8,128)S(1)}) custom-call(f32[1,16]{1,0:T(1,128)} %bitcast.6, f32[256,1024]{1,0:T(8,128)S(1)} %copy-done.8, f32[256,256]{1,0:T(8,128)S(1)} %copy-done.5, f32[2,16,256]{2,1,0:T(8,128)S(1)} %get-tuple-element.10.lines_far), custom_call_target="tpu_custom_call" | custom-call | flops 4000000000 | bytes 3440704 | tf_op jit(solution)/shard_map/inner/pallas_call | solution.py:96
  71.7 1.0 %copy-done = f32[256,1024]{1,0:T(8,128)} copy-done((f32[256,1024]{1,0:T(8,128)}, f32[256,1024]{1,0:T(8,128)S(1)}, u32[]{:S(2)}) %copy-start) | copy-done | bytes 1048600
  72.7 1.0 %copy-done.2 = f32[256,1024]{1,0:T(8,128)} copy-done((f32[256,1024]{1,0:T(8,128)}, f32[256,1024]{1,0:T(8,128)S(1)}, u32[]{:S(2)}) %copy-start.2) | copy-done | bytes 1048600
  73.7 14.1 %experts.1 = bf16[1,512,1024]{2,1,0:T(8,128)(2,1)} custom-call(bf16[1,4096,1024]{2,1,0:T(8,128)(2,1)} %refs_0_.3, bf16[1,4096,1024]{2,1,0:T(8,128)(2,1)} %refs_1_.3, bf16[128,1024]{1,0:T(8,128)(2,1)S(1)} %join.1.refs_2_, bf16[128,1024]{1,0:T(8,128)(2,1)S(1)} %collective-permute-done.2.refs_3_, bf16[128,1024]{1,0:T(8,128)(2,1)S(1)} %collective-permute-done.3.refs_4_, ...), custom_call_target="tpu_custom_call" | custom-call | flops 8589934592 | bytes 22577152 | tf_op jit(solution)/shard_map/experts/pallas_call | solution.py:96
  87.8 1.2 %copy-done.1 = f32[256,1024]{1,0:T(8,128)S(1)} copy-done((f32[256,1024]{1,0:T(8,128)S(1)}, f32[256,1024]{1,0:T(8,128)}, u32[]{:S(2)}) %copy-start.1) | copy-done | bytes 1048600
  89.0 1.2 %copy-done.3 = f32[256,1024]{1,0:T(8,128)S(1)} copy-done((f32[256,1024]{1,0:T(8,128)S(1)}, f32[256,1024]{1,0:T(8,128)}, u32[]{:S(2)}) %copy-start.3) | copy-done | bytes 1048600
  90.3 0.9 %copy-done.6 = f32[256,256]{1,0:T(8,128)S(1)} copy-done((f32[256,256]{1,0:T(8,128)S(1)}, f32[256,256]{1,0:T(8,128)}, u32[]{:S(2)}) %copy-start.6) | copy-done | bytes 262168
  91.2 3.3 %back.1 = bf16[256,1024]{1,0:T(8,128)(2,1)} custom-call(f32[1,1024]{1,0:T(1,128)} %bitcast.3, f32[256,1024]{1,0:T(8,128)S(1)} %copy-done.1, f32[256,1024]{1,0:T(8,128)S(1)} %copy-done.3, f32[8,128,128]{2,1,0:T(8,128)S(1)} %all-to-all-done.1.start_far, f32[256,256]{1,0:T(8,128)S(1)} %copy-done.6), custom_call_target="tpu_custom_call" | custom-call | flops 1000000000 | bytes 3411968 | tf_op jit(solution)/shard_map/back/pallas_call | solution.py:96
  (31 shorter events, 1.2 us)
Async XLA Ops:
  1.4 6.5 %collective-permute-start = (bf16[16,1280]{1,0:T(8,128)(2,1)S(1)}, bf16[16,1280]{1,0:T(8,128)(2,1)S(1)}, u32[]{:S(2)}, u32[]{:S(2)}) collective-permute-start(bf16[16,1280]{1,0:T(8,128)(2,1)S(1)} %ends.1), channel_id=1, source_target_pairs={{0,4},{4,8},{8,12},{12,16},{16,20},{20,24},{24,28},{1,5},{5,9},{9,... | collective-permute-start | bytes 122888 | tf_op jit(solution)/shard_map/ppermute | solution.py:497
  13.0 0.7 copy-start.4
  13.7 1.0 %copy-start.7 = (f32[256,1024]{1,0:T(8,128)}, f32[256,1024]{1,0:T(8,128)S(1)}, u32[]{:S(2)}) copy-start(f32[256,1024]{1,0:T(8,128)S(1)} %get-tuple-element.8.xconv_far) | copy-start | bytes 3145732
  14.7 43.3 %all-to-all-start = ((f32[8,136,128]{2,1,0:T(8,128)}), f32[8,136,128]{2,1,0:T(8,128)S(1)}, u32[]{:S(2)}, u32[]{:S(2)}) async-start(f32[8,136,128]{2,1,0:T(8,128)} %get-tuple-element.13), calls=%async_computation | async-start | bytes 1114112 | tf_op jit(solution)/shard_map/all_to_all | solution.py:277
  21.3 12.3 %collective-permute-start.1 = (bf16[64,1024]{1,0:T(8,128)(2,1)}, bf16[64,1024]{1,0:T(8,128)(2,1)S(1)}, u32[]{:S(2)}, u32[]{:S(2)}) collective-permute-start(bf16[64,1024]{1,0:T(8,128)(2,1)} %a_ref.1), channel_id=1, source_target_pairs={{0,8},{4,12},{8,0},{12,4},{16,24},{20,28},{24,16},{28,20},{1,9},{5... | collective-permute-start | bytes 393224 | tf_op jit(solution)/shard_map/ppermute | solution.py:329
  34.6 12.6 %collective-permute-start.2 = (bf16[128,1024]{1,0:T(8,128)(2,1)S(1)}, bf16[128,1024]{1,0:T(8,128)(2,1)S(1)}, u32[]{:S(2)}, u32[]{:S(2)}) collective-permute-start(bf16[128,1024]{1,0:T(8,128)(2,1)S(1)} %join.1.refs_2_), channel_id=1, source_target_pairs={{0,16},{4,20},{8,24},{12,28},{16,0},{20,4},{24,8},{28,12},{1,17},{... | collective-permute-start | bytes 786440 | tf_op jit(solution)/shard_map/ppermute | solution.py:329
  37.7 11.0 %collective-permute-start.3 = (bf16[128,1024]{1,0:T(8,128)(2,1)S(1)}, bf16[128,1024]{1,0:T(8,128)(2,1)S(1)}, u32[]{:S(2)}, u32[]{:S(2)}) collective-permute-start(bf16[128,1024]{1,0:T(8,128)(2,1)S(1)} %join.1.refs_2_), channel_id=1, source_target_pairs={{0,4},{4,0},{8,12},{12,8},{16,20},{20,16},{24,28},{28,24},{1,5},{5... | collective-permute-start | bytes 786440 | tf_op jit(solution)/shard_map/ppermute | solution.py:329
  39.1 10.0 %collective-permute-start.5 = (bf16[128,1024]{1,0:T(8,128)(2,1)S(1)}, bf16[128,1024]{1,0:T(8,128)(2,1)S(1)}, u32[]{:S(2)}, u32[]{:S(2)}) collective-permute-start(bf16[128,1024]{1,0:T(8,128)(2,1)S(1)} %join.1.refs_2_), channel_id=1, source_target_pairs={{0,1},{1,0},{2,3},{3,2},{4,5},{5,4},{6,7},{7,6},{8,9},{9,8},{10,11... | collective-permute-start | bytes 786440 | tf_op jit(solution)/shard_map/ppermute | solution.py:329
  39.1 11.6 %collective-permute-start.9 = (bf16[128,1024]{1,0:T(8,128)(2,1)S(1)}, bf16[128,1024]{1,0:T(8,128)(2,1)S(1)}, u32[]{:S(2)}, u32[]{:S(2)}) collective-permute-start(bf16[128,1024]{1,0:T(8,128)(2,1)S(1)} %join.1.refs_2_), channel_id=1, source_target_pairs={{0,2},{1,3},{2,0},{3,1},{4,6},{5,7},{6,4},{7,5},{8,10},{9,11},{10,... | collective-permute-start | bytes 786440 | tf_op jit(solution)/shard_map/ppermute | solution.py:329
  47.2 9.2 %collective-permute-start.4 = (bf16[128,1024]{1,0:T(8,128)(2,1)S(1)}, bf16[128,1024]{1,0:T(8,128)(2,1)S(1)}, u32[]{:S(2)}, u32[]{:S(2)}) collective-permute-start(bf16[128,1024]{1,0:T(8,128)(2,1)S(1)} %collective-permute-done.2.refs_3_), channel_id=1, source_target_pairs={{0,4},{4,0},{8,12},{12,8},{16,20},{20,16},{24,28},{28,24},{1,5},{5... | collective-permute-start | bytes 786440 | tf_op jit(solution)/shard_map/ppermute | solution.py:329
  48.6 15.6 %collective-permute-start.6 = (bf16[128,1024]{1,0:T(8,128)(2,1)S(1)}, bf16[128,1024]{1,0:T(8,128)(2,1)S(1)}, u32[]{:S(2)}, u32[]{:S(2)}) collective-permute-start(bf16[128,1024]{1,0:T(8,128)(2,1)S(1)} %collective-permute-done.2.refs_3_), channel_id=1, source_target_pairs={{0,1},{1,0},{2,3},{3,2},{4,5},{5,4},{6,7},{7,6},{8,9},{9,8},{10,11... | collective-permute-start | bytes 786440 | tf_op jit(solution)/shard_map/ppermute | solution.py:329
  48.7 15.7 %collective-permute-start.7 = (bf16[128,1024]{1,0:T(8,128)(2,1)S(1)}, bf16[128,1024]{1,0:T(8,128)(2,1)S(1)}, u32[]{:S(2)}, u32[]{:S(2)}) collective-permute-start(bf16[128,1024]{1,0:T(8,128)(2,1)S(1)} %collective-permute-done.3.refs_4_), channel_id=1, source_target_pairs={{0,1},{1,0},{2,3},{3,2},{4,5},{5,4},{6,7},{7,6},{8,9},{9,8},{10,11... | collective-permute-start | bytes 786440 | tf_op jit(solution)/shard_map/ppermute | solution.py:329
  49.2 15.7 %collective-permute-start.10 = (bf16[128,1024]{1,0:T(8,128)(2,1)S(1)}, bf16[128,1024]{1,0:T(8,128)(2,1)S(1)}, u32[]{:S(2)}, u32[]{:S(2)}) collective-permute-start(bf16[128,1024]{1,0:T(8,128)(2,1)S(1)} %collective-permute-done.2.refs_3_), channel_id=1, source_target_pairs={{0,2},{1,3},{2,0},{3,1},{4,6},{5,7},{6,4},{7,5},{8,10},{9,11},{10,... | collective-permute-start | bytes 786440 | tf_op jit(solution)/shard_map/ppermute | solution.py:329
  50.7 14.2 %collective-permute-start.11 = (bf16[128,1024]{1,0:T(8,128)(2,1)S(1)}, bf16[128,1024]{1,0:T(8,128)(2,1)}, u32[]{:S(2)}, u32[]{:S(2)}) collective-permute-start(bf16[128,1024]{1,0:T(8,128)(2,1)S(1)} %collective-permute-done.9.refs_10_), channel_id=1, source_target_pairs={{0,4},{4,0},{8,12},{12,8},{16,20},{20,16},{24,28},{28,24},{1,5},{5... | collective-permute-start | bytes 786440 | tf_op jit(solution)/shard_map/ppermute | solution.py:329
  56.4 8.9 %collective-permute-start.12 = (bf16[128,1024]{1,0:T(8,128)(2,1)S(1)}, bf16[128,1024]{1,0:T(8,128)(2,1)}, u32[]{:S(2)}, u32[]{:S(2)}) collective-permute-start(bf16[128,1024]{1,0:T(8,128)(2,1)S(1)} %collective-permute-done.4.refs_5_), channel_id=1, source_target_pairs={{0,2},{1,3},{2,0},{3,1},{4,6},{5,7},{6,4},{7,5},{8,10},{9,11},{10,... | collective-permute-start | bytes 786440 | tf_op jit(solution)/shard_map/ppermute | solution.py:329
  58.8 29.0 %all-to-all-start.1 = ((f32[8,128,128]{2,1,0:T(8,128)}), f32[8,128,128]{2,1,0:T(8,128)S(1)}, u32[]{:S(2)}, u32[]{:S(2)}) async-start(f32[8,128,128]{2,1,0:T(8,128)} %prefix.1), calls=%async_computation.1 | async-start | bytes 1048576 | tf_op jit(solution)/shard_map/all_to_all | solution.py:286
  64.2 9.4 %collective-permute-start.13 = (bf16[128,1024]{1,0:T(8,128)(2,1)S(1)}, bf16[128,1024]{1,0:T(8,128)(2,1)S(1)}, u32[]{:S(2)}, u32[]{:S(2)}) collective-permute-start(bf16[128,1024]{1,0:T(8,128)(2,1)S(1)} %collective-permute-done.9.refs_10_), channel_id=1, source_target_pairs={{0,1},{1,0},{2,3},{3,2},{4,5},{5,4},{6,7},{7,6},{8,9},{9,8},{10,11... | collective-permute-start | bytes 786440 | tf_op jit(solution)/shard_map/ppermute | solution.py:329
  64.3 9.3 %collective-permute-start.8 = (bf16[128,1024]{1,0:T(8,128)(2,1)S(1)}, bf16[128,1024]{1,0:T(8,128)(2,1)S(1)}, u32[]{:S(2)}, u32[]{:S(2)}) collective-permute-start(bf16[128,1024]{1,0:T(8,128)(2,1)S(1)} %collective-permute-done.4.refs_5_), channel_id=1, source_target_pairs={{0,1},{1,0},{2,3},{3,2},{4,5},{5,4},{6,7},{7,6},{8,9},{9,8},{10,11... | collective-permute-start | bytes 786440 | tf_op jit(solution)/shard_map/ppermute | solution.py:329
  64.8 8.8 %collective-permute-start.14 = (bf16[128,1024]{1,0:T(8,128)(2,1)S(1)}, bf16[128,1024]{1,0:T(8,128)(2,1)S(1)}, u32[]{:S(2)}, u32[]{:S(2)}) collective-permute-start(bf16[128,1024]{1,0:T(8,128)(2,1)S(1)} %collective-permute-done.10.refs_11_), channel_id=1, source_target_pairs={{0,1},{1,0},{2,3},{3,2},{4,5},{5,4},{6,7},{7,6},{8,9},{9,8},{10,11... | collective-permute-start | bytes 786440 | tf_op jit(solution)/shard_map/ppermute | solution.py:329
  64.9 8.7 %collective-permute-start.15 = (bf16[128,1024]{1,0:T(8,128)(2,1)}, bf16[128,1024]{1,0:T(8,128)(2,1)S(1)}, u32[]{:S(2)}, u32[]{:S(2)}) collective-permute-start(bf16[128,1024]{1,0:T(8,128)(2,1)} %collective-permute-done.11.refs_12_), channel_id=1, source_target_pairs={{0,1},{1,0},{2,3},{3,2},{4,5},{5,4},{6,7},{7,6},{8,9},{9,8},{10,11... | collective-permute-start | bytes 786440 | tf_op jit(solution)/shard_map/ppermute | solution.py:329
  65.3 8.3 %collective-permute-start.16 = (bf16[128,1024]{1,0:T(8,128)(2,1)}, bf16[128,1024]{1,0:T(8,128)(2,1)S(1)}, u32[]{:S(2)}, u32[]{:S(2)}) collective-permute-start(bf16[128,1024]{1,0:T(8,128)(2,1)} %collective-permute-done.12.refs_13_), channel_id=1, source_target_pairs={{0,1},{1,0},{2,3},{3,2},{4,5},{5,4},{6,7},{7,6},{8,9},{9,8},{10,11... | collective-permute-start | bytes 786440 | tf_op jit(solution)/shard_map/ppermute | solution.py:329
  65.4 0.9 %copy-start.5 = (f32[256,256]{1,0:T(8,128)S(1)}, f32[256,256]{1,0:T(8,128)}, u32[]{:S(2)}) copy-start(f32[256,256]{1,0:T(8,128)} %copy-done.4) | copy-start | bytes 786436
  66.4 1.2 %copy-start.8 = (f32[256,1024]{1,0:T(8,128)S(1)}, f32[256,1024]{1,0:T(8,128)}, u32[]{:S(2)}) copy-start(f32[256,1024]{1,0:T(8,128)} %copy-done.7) | copy-start | bytes 3145732
  71.7 1.0 %copy-start = (f32[256,1024]{1,0:T(8,128)}, f32[256,1024]{1,0:T(8,128)S(1)}, u32[]{:S(2)}) copy-start(f32[256,1024]{1,0:T(8,128)S(1)} %get-tuple-element.11.pre_far) | copy-start | bytes 3145732
  72.7 1.0 %copy-start.2 = (f32[256,1024]{1,0:T(8,128)}, f32[256,1024]{1,0:T(8,128)S(1)}, u32[]{:S(2)}) copy-start(f32[256,1024]{1,0:T(8,128)S(1)} %get-tuple-element.12.decay_far) | copy-start | bytes 3145732
  87.8 1.2 %copy-start.1 = (f32[256,1024]{1,0:T(8,128)S(1)}, f32[256,1024]{1,0:T(8,128)}, u32[]{:S(2)}) copy-start(f32[256,1024]{1,0:T(8,128)} %copy-done) | copy-start | bytes 3145732
  89.0 1.2 %copy-start.3 = (f32[256,1024]{1,0:T(8,128)S(1)}, f32[256,1024]{1,0:T(8,128)}, u32[]{:S(2)}) copy-start(f32[256,1024]{1,0:T(8,128)} %copy-done.2) | copy-start | bytes 3145732
  90.2 0.9 %copy-start.6 = (f32[256,256]{1,0:T(8,128)S(1)}, f32[256,256]{1,0:T(8,128)}, u32[]{:S(2)}) copy-start(f32[256,256]{1,0:T(8,128)} %copy-done.4) | copy-start | bytes 786436

commit v5 on v4

--- a/solution.py
+++ b/solution.py
@@ -1,4 +1,5 @@
 import functools
+import math
 
 import jax
 import jax.numpy as jnp
@@ -85,7 +86,7 @@
 
 
 def call(body, outs, args, fixed=0, scratch=(), sems=0, flops=0, grant=8, near=False, name=None):
-    moved = sum(a.size * a.dtype.itemsize for a in (*args, *outs))
+    moved = sum(math.prod(a.shape) * a.dtype.itemsize for a in (*args, *outs))
     scratch = list(scratch) + ([pltpu.SemaphoreType.DMA((sems,))] if sems else [])
     space = pltpu.VMEM if near else pl.ANY
     args = [
@@ -129,12 +130,12 @@
     )
 
 
-def front_body(by_tokens, count, *refs):
+def local_body(by_tokens, count, *refs):
     far, outs, rest = refs[:count], refs[count : count + 4], refs[count + 4 :]
     near, scratch, pad_ref, sems = rest[:count], rest[count : count + 4], rest[-2], rest[-1]
     copies = started(far, near, sems)
     x_ref, b_ref, c_ref, taps_ref, taps_bc_ref, logs_ref, skip_ref, ids_ref, ends_ref = near
-    xconv_ref, bc_ref, lines_ref, slab_ref = scratch
+    pre_ref, decay_ref, c_out_ref, state_ref = scratch
     tokens, channels = x_ref.shape
     heads = logs_ref.shape[0]
     finished(copies)
@@ -151,62 +152,53 @@
         return silu(total)
 
     bc = conv(taps_bc_ref[...], channels, channels + 2 * STATE)
-    bc_ref[...] = bc
-    xconv = conv(taps_ref[...], 0, channels)
-    xconv_ref[...] = xconv
+    bmat, cmat = bc[:, :STATE], bc[:, STATE:]
+    c_out_ref[...] = cmat
     logs = logs_ref[...]
     inflow = jnp.sqrt(one_minus_exp(2.0 * logs))
-    within = dot_exact(logs, upper_ones(tokens))
-    lines_ref[0] = within
-    lines_ref[1] = inflow
-    out_copies = started(scratch[:3], outs[:3], sems)
-    total = within[:, tokens - 1 :]
-    remain = jnp.exp(total - within)
+    row = dot_exact(logs, upper_ones(tokens))
+    column = row.T
+    total = row[:, tokens - 1 :]
     spread = head_spread(heads)
-    state = dot(bc[:, :STATE], xconv * dot_left(inflow * remain, spread, FIRST), FIRST)
+    decay_ref[...] = dot_left(jnp.exp(row), spread, FIRST)
+    copies = started(scratch[1:3], outs[1:3], sems)
+
+    xconv = conv(taps_ref[...], 0, channels)
+    pad_ref[:tokens, :channels] = xconv
+    drive = xconv * dot_left(inflow, spread, FIRST)
+    pre_ref[...] = drive
+    fresh = drive * dot_left(jnp.exp(total - row), spread, FIRST)
+    state_ref[:STATE] = dot(bmat, fresh, FIRST)
     notes = dot_exact(jnp.exp(jnp.broadcast_to(total, (heads, NOTES))), spread, FIRST)
     if by_tokens:
-        parts, _, share = slab_ref.shape
         ids = ids_ref[...].astype(F32)
-        line = jnp.concatenate([ids[0:1], ids[1:2]], axis=1)
-        for i in range(parts):
-            cut = slice(i * share, (i + 1) * share)
-            slab_ref[i, :STATE] = state[:, cut]
-            slab_ref[i, STATE:] = jnp.where(iota((NOTES, share), 0) == 1, line, notes[:, cut])
-    else:
-        slab_ref[:STATE] = state
-        slab_ref[STATE:] = notes
-    finished(out_copies + started(scratch[3:], outs[3:], sems, 3))
-
-
-def inner_body(skip_far, xconv_far, bc_far, lines_far, pre_far, decay_far, *rest):
-    far = (skip_far, xconv_far, bc_far, lines_far)
-    skip_ref, xconv_ref, bc_ref, lines_ref, pre_ref, decay_ref, sems = rest
-    finished(started(far, rest[:4], sems))
-    tokens, channels = xconv_ref.shape
-    heads = channels // HDIM
-    row = lines_ref[0]
-    column = row.T
-    spread = head_spread(heads)
-    decay_ref[...] = dot_left(jnp.exp(row), spread, FIRST)
-    copies = started([decay_ref], [decay_far], sems)
-    inflow = dot_left(lines_ref[1], spread, FIRST)
+        line = jnp.concatenate([ids[0:1], ids[1:2]] * (channels // (2 * ids.shape[1])), axis=1)
+        notes = jnp.where(iota(notes.shape, 0) == 1, line, notes)
+    state_ref[STATE:] = notes
+    copies += started(scratch[3:], outs[3:], sems, 2)
+
     skip = dot_exact(skip_ref[...], spread)
-    meet = dot(bc_ref[:, STATE:], bc_ref[:, :STATE], ((1,), (1,)))
+    meet = dot(cmat, bmat, ((1,), (1,)))
     lower = iota((tokens, tokens), 0) >= iota((tokens, tokens), 1)
     left = iota((tokens, 2 * HDIM), 1) < HDIM
     for pair in range(heads // 2):
         cut = slice(pair * 2 * HDIM, (pair + 1) * 2 * HDIM)
-        xconv = xconv_ref[:, cut]
-        d_high, d_low = halves(xconv * inflow[:, cut])
+        d_high, d_low = halves(pre_ref[:, cut])
         both = []
         for h in (2 * pair, 2 * pair + 1):
             gap = column[:, h : h + 1] - row[h : h + 1, :]
             mix = jnp.where(lower, jnp.exp(gap), 0.0) * meet
             m_high, m_low = halves(mix)
             both.append(dot16(m_high, d_high) + dot16(m_high, d_low) + dot16(m_low, d_high))
-        pre_ref[:, cut] = skip[:, cut] * xconv + jnp.where(left, both[0], both[1])
-    finished(copies + started([pre_ref], [pre_far], sems, 1))
+        direct = skip[:, cut] * pad_ref[:tokens, cut]
+        pre_ref[:, cut] = direct + jnp.where(left, both[0], both[1])
+    finished(copies + started(scratch[:1], outs[:1], sems, 3))
+
+
+def slabs_body(state_ref, after_ref, slabs_ref, sems):
+    parts, _, share = slabs_ref.shape
+    cuts = [state_ref.at[:, pl.ds(i * share, share)] for i in range(parts)]
+    finished(started(cuts, [slabs_ref.at[i] for i in range(parts)], sems))
 
 
 def prefix_body(parts_ref, starts_ref):
@@ -218,15 +210,15 @@
             state = parts_ref[i, STATE : STATE + 1] * state + parts_ref[i, :STATE]
 
 
-def back_body(cuts, gain_far, pre_far, decay_far, start_far, bc_far, out_far, *rest):
-    far = (start_far, bc_far, pre_far, decay_far, gain_far)
-    start_ref, bc_ref, pre_ref, decay_ref, gain_ref, out_ref, sems = rest
+def back_body(cuts, gain_far, pre_far, decay_far, c_far, start_far, out_far, *rest):
+    far = (start_far, c_far, pre_far, decay_far, gain_far)
+    start_ref, c_ref, pre_ref, decay_ref, gain_ref, out_ref, sems = rest
     copies = started(far, rest[:5], sems)
     channels = pre_ref.shape[1]
     width = min(channels, 4 * HDIM)
     group = (iota((width, width), 0) // HDIM == iota((width, width), 1) // HDIM).astype(BF16)
     finished(copies)
-    c_high, c_low = halves(bc_ref[:, STATE:])
+    c_high, c_low = halves(c_ref[...])
     copies = []
     for i in range(channels // width):
         cut = slice(i * width, (i + 1) * width)
@@ -243,70 +235,62 @@
     finished(copies)
 
 
-def mixing(seq_input, b_input, c_input, before, conv_x, conv_bc, log_decay, skip, gain, ids):
+def mixing(
+    seq_input, b_input, c_input, before, conv_x, conv_bc, log_decay, skip, gain, ids, after
+):
     tokens, channels = seq_input.shape
     heads = skip.shape[0]
     ctx = lax.axis_size("ctx")
     share = channels // ctx
-    cuts = share == 2 * HDIM
-    skip = skip.reshape(1, heads)
-    square = array((tokens, channels), F32)
-    slabs = (ctx, STATE + NOTES, share) if cuts else (STATE + NOTES, channels)
+    cuts = after is not None
     outs = [
-        square,
-        array((tokens, 2 * STATE), F32),
-        array((2, heads, tokens), F32),
-        array(slabs, F32),
+        pltpu.HBM((tokens, channels), F32),
+        pltpu.HBM((tokens, channels), F32),
+        pltpu.HBM((tokens, STATE), F32),
+        array((STATE + NOTES, channels), F32),
     ]
-    args = (seq_input, b_input, c_input, conv_x, conv_bc, log_decay, skip, ids.T, before)
-    xconv, bc, lines, slab = call(
-        functools.partial(front_body, cuts, len(args)),
+    args = (seq_input, b_input, c_input, conv_x, conv_bc, log_decay)
+    args = (*args, skip.reshape(1, heads), ids.T, before)
+    pre, decay, cmat, state = call(
+        functools.partial(local_body, cuts, len(args)),
         outs,
         args,
         fixed=len(args) - 1,
-        scratch=room(args)
-        + room(outs)
-        + [pltpu.VMEM((8 + tokens, channels + 2 * STATE), F32)],
+        scratch=room(args) + room(outs) + [pltpu.VMEM((8 + tokens, channels + 2 * STATE), F32)],
         sems=len(args),
-        flops=10**9,
-        grant=16,
-        name="front",
-    )
-    if not cuts:
-        slab = slab.reshape(STATE + NOTES, ctx, share).transpose(1, 0, 2)
-    parts = lax.all_to_all(slab, "ctx", split_axis=0, concat_axis=0, tiled=True)
+        flops=10**10,
+        grant=20,
+        name="local",
+    )
+    if cuts:
+        slabs = call(
+            slabs_body,
+            [array((ctx, STATE + NOTES, share), F32)],
+            (state, after),
+            sems=ctx,
+            name="slabs",
+        )[0]
+    else:
+        slabs = state.reshape(STATE + NOTES, ctx, share).transpose(1, 0, 2)
+    parts = lax.all_to_all(slabs, "ctx", split_axis=0, concat_axis=0, tiled=True)
     starts = call(
         prefix_body,
         [array((ctx, STATE, share), F32)],
         (parts,),
-        flops=10**6,
         near=True,
         name="prefix",
     )[0]
     start = lax.all_to_all(starts, "ctx", split_axis=0, concat_axis=0, tiled=True)
     if not cuts:
         start = start.transpose(1, 0, 2).reshape(STATE, channels)
-    args = (skip, xconv, bc, lines)
-    outs = [square, square]
-    pre, decay = call(
-        inner_body,
-        outs,
-        args,
-        fixed=1,
-        scratch=room(args) + room(outs),
-        sems=4,
-        flops=4 * 10**9,
-        grant=16,
-        name="inner",
-    )
-    args = (gain.reshape(1, channels), pre, decay, start, bc)
+    args = (gain.reshape(1, channels), pre, decay, cmat, start)
     outs = [array((tokens, channels), BF16)]
     mixed = call(
         functools.partial(back_body, cuts),
         outs,
         args,
-        fixed=1,
-        scratch=room([start, bc, pre, decay, args[0]]) + room(outs),
+        fixed=4,
+        scratch=room([start, cmat, pre, decay, args[0]]) + room(outs),
         sems=5,
         flops=10**9,
         grant=16,
@@ -342,32 +326,33 @@
     here = lax.axis_index("ctx")
 
     def piece_copies(k):
-        cut = pl.ds(k * depth, depth)
+        cut = pl.ds(pl.multiple_of((me ^ k) * depth, depth), depth)
         targets = [rows_ref.at[pl.ds(i * step, step), cut] for i in range(4)]
         return [
             pltpu.make_async_copy(far[4 * k + i], targets[i], sems.at[4 * k + i]) for i in range(4)
         ]
 
-    def weight_copies(n, k):
-        down = pl.ds(pl.multiple_of((me ^ k) * depth, depth), depth)
+    def weight_copies(n, i):
+        w = (w_gate, w_up)[i]
         across = pl.ds(n * TILE, TILE)
+        cuts = [pl.ds(k * depth, depth) for k in range(4)]
         return [
             pltpu.make_async_copy(
-                w.at[0, down, across], held_ref.at[i, n, k], w_sems.at[i, n, k]
+                w.at[0, cut, across], held_ref.at[i, n, cut, :], w_sems.at[i, n, k]
             )
-            for i, w in enumerate((w_gate, w_up))
+            for k, cut in enumerate(cuts)
         ]
 
     for k in range(4):
-        for copy in piece_copies(k) + weight_copies(0, k):
+        for copy in piece_copies(k):
             copy.start()
     notes = pltpu.make_async_copy(
         notes_far.at[:, pl.ds(STATE, NOTES), :], notes_ref, sems.at[pieces]
     )
     notes.start()
-    for n in range(1, tiles):
-        for k in range(4):
-            for copy in weight_copies(n, k):
+    for n in range(tiles):
+        for i in range(2):
+            for copy in weight_copies(n, i):
                 copy.start()
 
     shape = (rows, rows)
@@ -377,16 +362,13 @@
     out_copies = []
     for n in range(tiles):
         cut = slice(n * TILE, (n + 1) * TILE)
-        gate = upper = None
-        for k in range(4):
-            if n == 0:
+        if n == 0:
+            for k in range(4):
                 finished(piece_copies(k))
-            finished(weight_copies(n, k))
-            block = rows_ref[:, k * depth : (k + 1) * depth]
-            more = dot16(block, held_ref[0, n, k])
-            gate = more if k == 0 else gate + more
-            more = dot16(block, held_ref[1, n, k])
-            upper = more if k == 0 else upper + more
+        finished(weight_copies(n, 0))
+        gate = dot16(rows_ref[...], held_ref[0, n])
+        finished(weight_copies(n, 1))
+        upper = dot16(rows_ref[...], held_ref[1, n])
         hid_ref[...] = (silu(gate) * upper).astype(BF16)
         if n == 0:
             notes.wait()
@@ -407,9 +389,8 @@
     finished(out_copies)
 
 
-def experts_by_tokens(moe_input, notes, w_gate, w_up):
+def along_z(moe_input):
     rows, columns = moe_input.shape
-    ctx = lax.axis_size("ctx")
     joined = call(
         join_body,
         [array((2 * rows, columns), BF16)],
@@ -418,7 +399,12 @@
         sems=2,
         name="join",
     )[0]
-    z = (joined, swapped(joined, "ctx", 4))
+    return joined, swapped(joined, "ctx", 4)
+
+
+def experts_by_tokens(z, notes, w_gate, w_up):
+    ctx = lax.axis_size("ctx")
+    rows, columns = z[0].shape[0] // 2, z[0].shape[1]
     x = [swapped(a, "ctx", 1) for a in z]
     y = [swapped(a, "exp", 2) for a in z]
     d = (swapped(y[0], "ctx", 1), swapped(x[1], "exp", 2))
@@ -436,7 +422,7 @@
         fixed=2,
         scratch=[
             pltpu.VMEM((length, 4 * columns), BF16),
-            pltpu.VMEM((2, hidden // TILE, 4, columns, TILE), BF16),
+            pltpu.VMEM((2, hidden // TILE, 4 * columns, TILE), BF16),
             pltpu.VMEM((ctx, NOTES, notes.shape[2]), F32),
             pltpu.VMEM((ctx, rows, rows), BF16),
             pltpu.VMEM((length, TILE), BF16),
@@ -495,6 +481,7 @@
         name="ends",
     )[0]
     before = lax.ppermute(ends, "ctx", [(i, i + 1) for i in range(ctx - 1)])
+    z = along_z(moe_input) if by_tokens else (None, None)
     mixed, notes = mixing(
         seq_input,
         b_input,
@@ -506,9 +493,10 @@
         skip_gain,
         norm_gain,
         expert_ids,
+        z[1],
     )
     if by_tokens:
-        hidden = experts_by_tokens(moe_input, notes, w_gate, w_up)
+        hidden = experts_by_tokens(z, notes, w_gate, w_up)
     else:
         hidden = experts_by_slots(moe_input, expert_ids, w_gate, w_up)
     return (mixed, hidden)

time: 95.3 us -> 91.5 us (0.960)
  local copies, waits for them, and re-layouts: 9.17 us -> 0 us
  Pallas kernels: 29.1 us -> 37.9 us
  starting transfers between devices: 31.8 us -> 26.8 us
  waiting for transfers between devices: 23.7 us -> 25.4 us
    unnamed x18 -> x0, local copies, waits for them, and re-layouts: 9.17 us -> none
    pallas_call x7, Pallas kernels: 29.1 us -> 37.9 us  [call(): pl.pallas_call(body, out_shape=outs, in_specs=[pl.BlockSpec(memory_space=...]
    ppermute x16, waiting for transfers between devices: 22 us -> 25.4 us  [swapped(): lax.ppermute(block, axis, [(i, i ^ bit) for i in range(lax.axis_size(axis...]
    ppermute x1, waiting for transfers between devices: 1.65 us -> 0.01 us  [on_device(): before = lax.ppermute(ends, 'ctx', [(i, i + 1) for i in range(ctx - 1)])]
    all_to_all x1, starting transfers between devices: 6.64 us -> 5.05 us  [mixing(): lax.all_to_all(slabs, 'ctx', split_axis=0, concat_axis=0, tiled=True)]
    ppermute x1, starting transfers between devices: 4.84 us -> 3.4 us  [on_device(): before = lax.ppermute(ends, 'ctx', [(i, i + 1) for i in range(ctx - 1)])]
    all_to_all x1, starting transfers between devices: 5.46 us -> 4.34 us  [mixing(): lax.all_to_all(starts, 'ctx', split_axis=0, concat_axis=0, tiled=True)]
  transfers between devices with their start and end apart: 19 -> 19, of which waited for: 4 -> 6; matrix products, arithmetic and copies ran while one was open for 0% -> 0% of each run, Pallas kernels for 21% -> 36%
where the time goes in v5:
time: 91.5 us; the launch traced here: 91 us
  Pallas kernels  37.9 us (41%)
  starting transfers between devices  26.8 us (29%)
  waiting for transfers between devices  25.4 us (28%)
    pallas_call x7, Pallas kernels, call(): pl.pallas_call(body, out_shape=outs, in_specs=[pl.BlockSpec(memory_space=...  37.9 us
    ppermute x16, waiting for transfers between devices, swapped(): lax.ppermute(block, axis, [(i, i ^ bit) for i in range(lax.axis_size(axis...  25.4 us
    ppermute x16, starting transfers between devices, swapped(): lax.ppermute(block, axis, [(i, i ^ bit) for i in range(lax.axis_size(axis...  14 us
    all_to_all x1, starting transfers between devices, mixing(): lax.all_to_all(slabs, 'ctx', split_axis=0, concat_axis=0, tiled=True)  5.05 us
    all_to_all x1, starting transfers between devices, mixing(): lax.all_to_all(starts, 'ctx', split_axis=0, concat_axis=0, tiled=True)  4.34 us
    ppermute x1, starting transfers between devices, on_device(): before = lax.ppermute(ends, 'ctx', [(i, i + 1) for i in range(ctx - 1)])  3.4 us
  transfers between devices with their start and end apart: 19, of which 6 were waited for; matrix products, arithmetic and copies ran while one was open for 0% of the time, Pallas kernels for 36%

profile of v5, /device:TPU:0, one launch (start us, length us, event | category | flops | bytes accessed | tf_op | source)
XLA Modules:
  0.0 91.0 jit_solution(16470984348281652606)
XLA Ops:
  0.6 3.1 %collective-permute-start.1 = (bf16[64,1024]{1,0:T(8,128)(2,1)}, bf16[64,1024]{1,0:T(8,128)(2,1)S(1)}, u32[]{:S(2)}, u32[]{:S(2)}) collective-permute-start(bf16[64,1024]{1,0:T(8,128)(2,1)} %a_ref.1), channel_id=1, source_target_pairs={{0,8},{4,12},{8,0},{12,4},{16,24},{20,28},{24,16},{28,20},{1,9},{5... | collective-permute-start | bytes 393224 | tf_op jit(solution)/shard_map/ppermute | solution.py:313
  3.7 0.8 ends.1
  4.5 3.4 %collective-permute-start = (bf16[16,1280]{1,0:T(8,128)(2,1)S(1)}, bf16[16,1280]{1,0:T(8,128)(2,1)S(1)}, u32[]{:S(2)}, u32[]{:S(2)}) collective-permute-start(bf16[16,1280]{1,0:T(8,128)(2,1)S(1)} %ends.1), channel_id=1, source_target_pairs={{0,4},{4,8},{8,12},{12,16},{16,20},{20,24},{24,28},{1,5},{5,9},{9,... | collective-permute-start | bytes 122888 | tf_op jit(solution)/shard_map/ppermute | solution.py:483
  7.9 0.9 %join.1.refs_2_ = bf16[128,1024]{1,0:T(8,128)(2,1)S(1)} custom-call(bf16[64,1024]{1,0:T(8,128)(2,1)} %a_ref.1, bf16[64,1024]{1,0:T(8,128)(2,1)S(1)} %collective-permute-done.1.b_ref), custom_call_target="tpu_custom_call" | custom-call | bytes 524288 | tf_op jit(solution)/shard_map/join/pallas_call | solution.py:97
  8.9 2.7 %collective-permute-start.2 = (bf16[128,1024]{1,0:T(8,128)(2,1)S(1)}, bf16[128,1024]{1,0:T(8,128)(2,1)S(1)}, u32[]{:S(2)}, u32[]{:S(2)}) collective-permute-start(bf16[128,1024]{1,0:T(8,128)(2,1)S(1)} %join.1.refs_2_), channel_id=1, source_target_pairs={{0,16},{4,20},{8,24},{12,28},{16,0},{20,4},{24,8},{28,12},{1,17},{... | collective-permute-start | bytes 786440 | tf_op jit(solution)/shard_map/ppermute | solution.py:313
  11.5 7.5 %local.1 = (f32[256,1024]{1,0:T(8,128)}, f32[256,1024]{1,0:T(8,128)}, f32[256,128]{1,0:T(8,128)}, f32[136,1024]{1,0:T(8,128)S(1)}) custom-call(bf16[256,1024]{1,0:T(8,128)(2,1)} %refs_0_.2, bf16[256,128]{1,0:T(8,128)(2,1)} %refs_1_.2, bf16[256,128]{1,0:T(8,128)(2,1)} %refs_2_.1, f32[4,1024]{1,0:T(4,128)} %refs_3_.1, f32[4,256]{1,0:T(4,128)} %refs_4_.1, ...), custom_call_target="tpu_custom_call" | custom-call | flops 10000000000 | bytes 3519040 | tf_op jit(solution)/shard_map/local/pallas_call | solution.py:97
  19.1 3.9 %collective-permute-done.2.after_ref.refs_3_ = bf16[128,1024]{1,0:T(8,128)(2,1)S(1)} collective-permute-done((bf16[128,1024]{1,0:T(8,128)(2,1)S(1)}, bf16[128,1024]{1,0:T(8,128)(2,1)S(1)}, u32[]{:S(2)}, u32[]{:S(2)}) %collective-permute-start.2) | collective-permute-done | bytes 262176 | tf_op jit(solution)/shard_map/ppermute | solution.py:313
  22.9 0.9 slabs.1
  23.8 5.0 %all-to-all-start = ((f32[8,136,128]{2,1,0:T(8,128)}), f32[8,136,128]{2,1,0:T(8,128)S(1)}, u32[]{:S(2)}, u32[]{:S(2)}) async-start(f32[8,136,128]{2,1,0:T(8,128)} %slabs.1), calls=%async_computation | async-start | bytes 1114112 | tf_op jit(solution)/shard_map/all_to_all | solution.py:275
  28.8 2.0 %collective-permute-start.3 = (bf16[128,1024]{1,0:T(8,128)(2,1)S(1)}, bf16[128,1024]{1,0:T(8,128)(2,1)S(1)}, u32[]{:S(2)}, u32[]{:S(2)}) collective-permute-start(bf16[128,1024]{1,0:T(8,128)(2,1)S(1)} %join.1.refs_2_), channel_id=1, source_target_pairs={{0,4},{4,0},{8,12},{12,8},{16,20},{20,16},{24,28},{28,24},{1,5},{5... | collective-permute-start | bytes 786440 | tf_op jit(solution)/shard_map/ppermute | solution.py:313
  30.9 0.0 collective-permute-start.5
  30.9 1.5 %collective-permute-start.9 = (bf16[128,1024]{1,0:T(8,128)(2,1)S(1)}, bf16[128,1024]{1,0:T(8,128)(2,1)S(1)}, u32[]{:S(2)}, u32[]{:S(2)}) collective-permute-start(bf16[128,1024]{1,0:T(8,128)(2,1)S(1)} %join.1.refs_2_), channel_id=1, source_target_pairs={{0,2},{1,3},{2,0},{3,1},{4,6},{5,7},{6,4},{7,5},{8,10},{9,11},{10,... | collective-permute-start | bytes 786440 | tf_op jit(solution)/shard_map/ppermute | solution.py:313
  32.4 0.1 collective-permute-start.4
  32.5 0.2 collective-permute-start.6
  32.6 11.6 %collective-permute-done.3.refs_4_ = bf16[128,1024]{1,0:T(8,128)(2,1)S(1)} collective-permute-done((bf16[128,1024]{1,0:T(8,128)(2,1)S(1)}, bf16[128,1024]{1,0:T(8,128)(2,1)S(1)}, u32[]{:S(2)}, u32[]{:S(2)}) %collective-permute-start.3) | collective-permute-done | bytes 262176 | tf_op jit(solution)/shard_map/ppermute | solution.py:313
  44.2 0.0 collective-permute-done.5.refs_6_
  44.2 1.5 %collective-permute-start.10 = (bf16[128,1024]{1,0:T(8,128)(2,1)S(1)}, bf16[128,1024]{1,0:T(8,128)(2,1)S(1)}, u32[]{:S(2)}, u32[]{:S(2)}) collective-permute-start(bf16[128,1024]{1,0:T(8,128)(2,1)S(1)} %collective-permute-done.2.after_ref.refs_3_), channel_id=1, source_target_pairs={{0,2},{1,3},{2,0},{3,1},{4,6},{5,7},{6,4},{7,5},{8,10},{9,11},{10,... | collective-permute-start | bytes 786440 | tf_op jit(solution)/shard_map/ppermute | solution.py:313
  45.8 0.0 collective-permute-done.9.refs_10_
  45.8 0.0 collective-permute-start.11
  45.8 2.8 %collective-permute-done.4.refs_5_ = bf16[128,1024]{1,0:T(8,128)(2,1)S(1)} collective-permute-done((bf16[128,1024]{1,0:T(8,128)(2,1)S(1)}, bf16[128,1024]{1,0:T(8,128)(2,1)S(1)}, u32[]{:S(2)}, u32[]{:S(2)}) %collective-permute-start.4) | collective-permute-done | bytes 262176 | tf_op jit(solution)/shard_map/ppermute | solution.py:313
  48.6 2.5 %collective-permute-start.12 = (bf16[128,1024]{1,0:T(8,128)(2,1)S(1)}, bf16[128,1024]{1,0:T(8,128)(2,1)}, u32[]{:S(2)}, u32[]{:S(2)}) collective-permute-start(bf16[128,1024]{1,0:T(8,128)(2,1)S(1)} %collective-permute-done.4.refs_5_), channel_id=1, source_target_pairs={{0,2},{1,3},{2,0},{3,1},{4,6},{5,7},{6,4},{7,5},{8,10},{9,11},{10,... | collective-permute-start | bytes 786440 | tf_op jit(solution)/shard_map/ppermute | solution.py:313
  51.1 0.0 collective-permute-done.7.refs_8_
  51.1 0.5 collective-permute-start.8
  51.6 1.8 %collective-permute-done.10.refs_11_ = bf16[128,1024]{1,0:T(8,128)(2,1)S(1)} collective-permute-done((bf16[128,1024]{1,0:T(8,128)(2,1)S(1)}, bf16[128,1024]{1,0:T(8,128)(2,1)S(1)}, u32[]{:S(2)}, u32[]{:S(2)}) %collective-permute-start.10) | collective-permute-done | bytes 262176 | tf_op jit(solution)/shard_map/ppermute | solution.py:313
  53.3 1.0 %collective-permute-done.11.refs_12_ = bf16[128,1024]{1,0:T(8,128)(2,1)} collective-permute-done((bf16[128,1024]{1,0:T(8,128)(2,1)S(1)}, bf16[128,1024]{1,0:T(8,128)(2,1)}, u32[]{:S(2)}, u32[]{:S(2)}) %collective-permute-start.11) | collective-permute-done | bytes 262176 | tf_op jit(solution)/shard_map/ppermute | solution.py:313
  54.3 4.4 %collective-permute-done.12.refs_13_ = bf16[128,1024]{1,0:T(8,128)(2,1)} collective-permute-done((bf16[128,1024]{1,0:T(8,128)(2,1)S(1)}, bf16[128,1024]{1,0:T(8,128)(2,1)}, u32[]{:S(2)}, u32[]{:S(2)}) %collective-permute-start.12) | collective-permute-done | bytes 262176 | tf_op jit(solution)/shard_map/ppermute | solution.py:313
  58.7 0.8 prefix.1
  59.5 4.3 %all-to-all-start.1 = ((f32[8,128,128]{2,1,0:T(8,128)}), f32[8,128,128]{2,1,0:T(8,128)S(1)}, u32[]{:S(2)}, u32[]{:S(2)}) async-start(f32[8,128,128]{2,1,0:T(8,128)} %prefix.1), calls=%async_computation.1 | async-start | bytes 1048576 | tf_op jit(solution)/shard_map/all_to_all | solution.py:283
  63.9 0.0 collective-permute-done.13.refs_14_
  63.9 0.0 collective-permute-done.15.refs_16_
  63.9 22.9 %experts.1 = bf16[1,512,1024]{2,1,0:T(8,128)(2,1)} custom-call(bf16[1,4096,1024]{2,1,0:T(8,128)(2,1)} %refs_0_.3, bf16[1,4096,1024]{2,1,0:T(8,128)(2,1)} %refs_1_.3, bf16[128,1024]{1,0:T(8,128)(2,1)S(1)} %join.1.refs_2_, bf16[128,1024]{1,0:T(8,128)(2,1)S(1)} %collective-permute-done.2.after_ref.refs_3_, ...), custom_call_target="tpu_custom_call" | custom-call | flops 8589934592 | bytes 22577152 | tf_op jit(solution)/shard_map/experts/pallas_call | solution.py:97
  86.8 4.1 %back.1 = bf16[256,1024]{1,0:T(8,128)(2,1)} custom-call(f32[1,1024]{1,0:T(1,128)} %bitcast.3, f32[256,1024]{1,0:T(8,128)} %get-tuple-element.6.pre_far, f32[256,1024]{1,0:T(8,128)} %get-tuple-element.7.decay_far, f32[256,128]{1,0:T(8,128)} %get-tuple-element.8.c_far, f32[8,128,128]{2,1,0:T(8,128)S(1)} %all-to-all-done.1.start_far), custom_call_target="tpu_custom_call" | custom-call | flops 1000000000 | bytes 3280896 | tf_op jit(solution)/shard_map/back/pallas_call | solution.py:97
  (13 shorter events, 0.0 us)
Async XLA Ops:
  0.6 7.3 %collective-permute-start.1 = (bf16[64,1024]{1,0:T(8,128)(2,1)}, bf16[64,1024]{1,0:T(8,128)(2,1)S(1)}, u32[]{:S(2)}, u32[]{:S(2)}) collective-permute-start(bf16[64,1024]{1,0:T(8,128)(2,1)} %a_ref.1), channel_id=1, source_target_pairs={{0,8},{4,12},{8,0},{12,4},{16,24},{20,28},{24,16},{28,20},{1,9},{5... | collective-permute-start | bytes 393224 | tf_op jit(solution)/shard_map/ppermute | solution.py:313
  4.5 7.0 %collective-permute-start = (bf16[16,1280]{1,0:T(8,128)(2,1)S(1)}, bf16[16,1280]{1,0:T(8,128)(2,1)S(1)}, u32[]{:S(2)}, u32[]{:S(2)}) collective-permute-start(bf16[16,1280]{1,0:T(8,128)(2,1)S(1)} %ends.1), channel_id=1, source_target_pairs={{0,4},{4,8},{8,12},{12,16},{16,20},{20,24},{24,28},{1,5},{5,9},{9,... | collective-permute-start | bytes 122888 | tf_op jit(solution)/shard_map/ppermute | solution.py:483
  8.9 14.1 %collective-permute-start.2 = (bf16[128,1024]{1,0:T(8,128)(2,1)S(1)}, bf16[128,1024]{1,0:T(8,128)(2,1)S(1)}, u32[]{:S(2)}, u32[]{:S(2)}) collective-permute-start(bf16[128,1024]{1,0:T(8,128)(2,1)S(1)} %join.1.refs_2_), channel_id=1, source_target_pairs={{0,16},{4,20},{8,24},{12,28},{16,0},{20,4},{24,8},{28,12},{1,17},{... | collective-permute-start | bytes 786440 | tf_op jit(solution)/shard_map/ppermute | solution.py:313
  23.8 34.9 %all-to-all-start = ((f32[8,136,128]{2,1,0:T(8,128)}), f32[8,136,128]{2,1,0:T(8,128)S(1)}, u32[]{:S(2)}, u32[]{:S(2)}) async-start(f32[8,136,128]{2,1,0:T(8,128)} %slabs.1), calls=%async_computation | async-start | bytes 1114112 | tf_op jit(solution)/shard_map/all_to_all | solution.py:275
  28.8 15.4 %collective-permute-start.3 = (bf16[128,1024]{1,0:T(8,128)(2,1)S(1)}, bf16[128,1024]{1,0:T(8,128)(2,1)S(1)}, u32[]{:S(2)}, u32[]{:S(2)}) collective-permute-start(bf16[128,1024]{1,0:T(8,128)(2,1)S(1)} %join.1.refs_2_), channel_id=1, source_target_pairs={{0,4},{4,0},{8,12},{12,8},{16,20},{20,16},{24,28},{28,24},{1,5},{5... | collective-permute-start | bytes 786440 | tf_op jit(solution)/shard_map/ppermute | solution.py:313
  30.9 13.4 %collective-permute-start.5 = (bf16[128,1024]{1,0:T(8,128)(2,1)S(1)}, bf16[128,1024]{1,0:T(8,128)(2,1)S(1)}, u32[]{:S(2)}, u32[]{:S(2)}) collective-permute-start(bf16[128,1024]{1,0:T(8,128)(2,1)S(1)} %join.1.refs_2_), channel_id=1, source_target_pairs={{0,1},{1,0},{2,3},{3,2},{4,5},{5,4},{6,7},{7,6},{8,9},{9,8},{10,11... | collective-permute-start | bytes 786440 | tf_op jit(solution)/shard_map/ppermute | solution.py:313
  30.9 14.9 %collective-permute-start.9 = (bf16[128,1024]{1,0:T(8,128)(2,1)S(1)}, bf16[128,1024]{1,0:T(8,128)(2,1)S(1)}, u32[]{:S(2)}, u32[]{:S(2)}) collective-permute-start(bf16[128,1024]{1,0:T(8,128)(2,1)S(1)} %join.1.refs_2_), channel_id=1, source_target_pairs={{0,2},{1,3},{2,0},{3,1},{4,6},{5,7},{6,4},{7,5},{8,10},{9,11},{10,... | collective-permute-start | bytes 786440 | tf_op jit(solution)/shard_map/ppermute | solution.py:313
  32.4 16.2 %collective-permute-start.4 = (bf16[128,1024]{1,0:T(8,128)(2,1)S(1)}, bf16[128,1024]{1,0:T(8,128)(2,1)S(1)}, u32[]{:S(2)}, u32[]{:S(2)}) collective-permute-start(bf16[128,1024]{1,0:T(8,128)(2,1)S(1)} %collective-permute-done.2.after_ref.refs_3_), channel_id=1, source_target_pairs={{0,4},{4,0},{8,12},{12,8},{16,20},{20,16},{24,28},{28,24},{1,5},{5... | collective-permute-start | bytes 786440 | tf_op jit(solution)/shard_map/ppermute | solution.py:313
  32.5 18.6 %collective-permute-start.6 = (bf16[128,1024]{1,0:T(8,128)(2,1)S(1)}, bf16[128,1024]{1,0:T(8,128)(2,1)S(1)}, u32[]{:S(2)}, u32[]{:S(2)}) collective-permute-start(bf16[128,1024]{1,0:T(8,128)(2,1)S(1)} %collective-permute-done.2.after_ref.refs_3_), channel_id=1, source_target_pairs={{0,1},{1,0},{2,3},{3,2},{4,5},{5,4},{6,7},{7,6},{8,9},{9,8},{10,11... | collective-permute-start | bytes 786440 | tf_op jit(solution)/shard_map/ppermute | solution.py:313
  44.2 6.8 %collective-permute-start.7 = (bf16[128,1024]{1,0:T(8,128)(2,1)S(1)}, bf16[128,1024]{1,0:T(8,128)(2,1)S(1)}, u32[]{:S(2)}, u32[]{:S(2)}) collective-permute-start(bf16[128,1024]{1,0:T(8,128)(2,1)S(1)} %collective-permute-done.3.refs_4_), channel_id=1, source_target_pairs={{0,1},{1,0},{2,3},{3,2},{4,5},{5,4},{6,7},{7,6},{8,9},{9,8},{10,11... | collective-permute-start | bytes 786440 | tf_op jit(solution)/shard_map/ppermute | solution.py:313
  44.2 9.1 %collective-permute-start.10 = (bf16[128,1024]{1,0:T(8,128)(2,1)S(1)}, bf16[128,1024]{1,0:T(8,128)(2,1)S(1)}, u32[]{:S(2)}, u32[]{:S(2)}) collective-permute-start(bf16[128,1024]{1,0:T(8,128)(2,1)S(1)} %collective-permute-done.2.after_ref.refs_3_), channel_id=1, source_target_pairs={{0,2},{1,3},{2,0},{3,1},{4,6},{5,7},{6,4},{7,5},{8,10},{9,11},{10,... | collective-permute-start | bytes 786440 | tf_op jit(solution)/shard_map/ppermute | solution.py:313
  45.8 8.5 %collective-permute-start.11 = (bf16[128,1024]{1,0:T(8,128)(2,1)S(1)}, bf16[128,1024]{1,0:T(8,128)(2,1)}, u32[]{:S(2)}, u32[]{:S(2)}) collective-permute-start(bf16[128,1024]{1,0:T(8,128)(2,1)S(1)} %collective-permute-done.9.refs_10_), channel_id=1, source_target_pairs={{0,4},{4,0},{8,12},{12,8},{16,20},{20,16},{24,28},{28,24},{1,5},{5... | collective-permute-start | bytes 786440 | tf_op jit(solution)/shard_map/ppermute | solution.py:313
  48.6 10.1 %collective-permute-start.12 = (bf16[128,1024]{1,0:T(8,128)(2,1)S(1)}, bf16[128,1024]{1,0:T(8,128)(2,1)}, u32[]{:S(2)}, u32[]{:S(2)}) collective-permute-start(bf16[128,1024]{1,0:T(8,128)(2,1)S(1)} %collective-permute-done.4.refs_5_), channel_id=1, source_target_pairs={{0,2},{1,3},{2,0},{3,1},{4,6},{5,7},{6,4},{7,5},{8,10},{9,11},{10,... | collective-permute-start | bytes 786440 | tf_op jit(solution)/shard_map/ppermute | solution.py:313
  51.1 12.8 %collective-permute-start.13 = (bf16[128,1024]{1,0:T(8,128)(2,1)S(1)}, bf16[128,1024]{1,0:T(8,128)(2,1)}, u32[]{:S(2)}, u32[]{:S(2)}) collective-permute-start(bf16[128,1024]{1,0:T(8,128)(2,1)S(1)} %collective-permute-done.9.refs_10_), channel_id=1, source_target_pairs={{0,1},{1,0},{2,3},{3,2},{4,5},{5,4},{6,7},{7,6},{8,9},{9,8},{10,11... | collective-permute-start | bytes 786440 | tf_op jit(solution)/shard_map/ppermute | solution.py:313
  51.1 12.8 %collective-permute-start.8 = (bf16[128,1024]{1,0:T(8,128)(2,1)S(1)}, bf16[128,1024]{1,0:T(8,128)(2,1)}, u32[]{:S(2)}, u32[]{:S(2)}) collective-permute-start(bf16[128,1024]{1,0:T(8,128)(2,1)S(1)} %collective-permute-done.4.refs_5_), channel_id=1, source_target_pairs={{0,1},{1,0},{2,3},{3,2},{4,5},{5,4},{6,7},{7,6},{8,9},{9,8},{10,11... | collective-permute-start | bytes 786440 | tf_op jit(solution)/shard_map/ppermute | solution.py:313
  53.3 10.5 %collective-permute-start.14 = (bf16[128,1024]{1,0:T(8,128)(2,1)S(1)}, bf16[128,1024]{1,0:T(8,128)(2,1)}, u32[]{:S(2)}, u32[]{:S(2)}) collective-permute-start(bf16[128,1024]{1,0:T(8,128)(2,1)S(1)} %collective-permute-done.10.refs_11_), channel_id=1, source_target_pairs={{0,1},{1,0},{2,3},{3,2},{4,5},{5,4},{6,7},{7,6},{8,9},{9,8},{10,11... | collective-permute-start | bytes 786440 | tf_op jit(solution)/shard_map/ppermute | solution.py:313
  54.3 9.6 %collective-permute-start.15 = (bf16[128,1024]{1,0:T(8,128)(2,1)}, bf16[128,1024]{1,0:T(8,128)(2,1)}, u32[]{:S(2)}, u32[]{:S(2)}) collective-permute-start(bf16[128,1024]{1,0:T(8,128)(2,1)} %collective-permute-done.11.refs_12_), channel_id=1, source_target_pairs={{0,1},{1,0},{2,3},{3,2},{4,5},{5,4},{6,7},{7,6},{8,9},{9,8},{10,11... | collective-permute-start | bytes 786440 | tf_op jit(solution)/shard_map/ppermute | solution.py:313
  58.7 5.2 %collective-permute-start.16 = (bf16[128,1024]{1,0:T(8,128)(2,1)}, bf16[128,1024]{1,0:T(8,128)(2,1)}, u32[]{:S(2)}, u32[]{:S(2)}) collective-permute-start(bf16[128,1024]{1,0:T(8,128)(2,1)} %collective-permute-done.12.refs_13_), channel_id=1, source_target_pairs={{0,1},{1,0},{2,3},{3,2},{4,5},{5,4},{6,7},{7,6},{8,9},{9,8},{10,11... | collective-permute-start | bytes 786440 | tf_op jit(solution)/shard_map/ppermute | solution.py:313
  59.5 27.3 %all-to-all-start.1 = ((f32[8,128,128]{2,1,0:T(8,128)}), f32[8,128,128]{2,1,0:T(8,128)S(1)}, u32[]{:S(2)}, u32[]{:S(2)}) async-start(f32[8,128,128]{2,1,0:T(8,128)} %prefix.1), calls=%async_computation.1 | async-start | bytes 1048576 | tf_op jit(solution)/shard_map/all_to_all | solution.py:283

commit v6 on v4

v6 whole, which is shorter than its diff:
```python
import functools
import math

import jax
import jax.numpy as jnp
from jax import lax
from jax.experimental import pallas as pl
from jax.experimental.pallas import tpu as pltpu
from jax.sharding import PartitionSpec as P

HDIM = 64
STATE = 128
KCONV = 4
EDGE = 16
NOTES = 8

F32 = jnp.float32
BF16 = jnp.bfloat16


def dot16(a, b, contract=((1,), (0,))):
    return lax.dot_general(a, b, (contract, ((), ())), preferred_element_type=F32)


def halves(value):
    high = value.astype(BF16)
    return high, (value - high.astype(F32)).astype(BF16)


def dot(a, b, contract=((1,), (0,))):
    a_high, a_low = halves(a)
    b_high, b_low = halves(b)
    cross = dot16(a_high, b_low, contract) + dot16(a_low, b_high, contract)
    return dot16(a_high, b_high, contract) + cross


def dot_exact(a, b, contract=((1,), (0,))):
    high, rest = halves(a)
    low = (a - high.astype(F32) - rest.astype(F32)).astype(BF16)
    return dot16(high, b, contract) + (dot16(rest, b, contract) + dot16(low, b, contract))


def dot_left(a, b, contract=((1,), (0,))):
    high, low = halves(a)
    return dot16(high, b, contract) + dot16(low, b, contract)


FIRST = ((0,), (0,))


def iota(shape, axis):
    return lax.broadcasted_iota(jnp.int32, shape, axis)


def head_spread(heads):
    shape = (heads, heads * HDIM)
    return (iota(shape, 1) // HDIM == iota(shape, 0)).astype(BF16)


def upper_ones(length):
    return (iota((length, length), 0) <= iota((length, length), 1)).astype(BF16)


def silu(value):
    return value / (1.0 + jnp.exp(-value))


def one_minus_exp(value):
    series = jnp.ones_like(value)
    for n in range(8, 1, -1):
        series = 1.0 + value * series * (1.0 / n)
    return jnp.where(value > -0.25, -value * series, 1.0 - jnp.exp(value))


def started(sources, targets, sems, first=0):
    copies = []
    for i, (source, target) in enumerate(zip(sources, targets)):
        copies.append(pltpu.make_async_copy(source, target, sems.at[first + i]))
        copies[-1].start()
    return copies


def finished(copies):
    for copy in copies:
        copy.wait()


def call(
    body,
    outs,
    args,
    fixed=0,
    held=0,
    near_args=0,
    near_outs=0,
    scratch=(),
    sems=0,
    flops=0,
    grant=8,
    near=False,
    name=None,
):
    moved = sum(math.prod(a.shape) * a.dtype.itemsize for a in (*args, *outs))
    scratch = list(scratch) + ([pltpu.SemaphoreType.DMA((sems,))] if sems else [])
    space = pltpu.VMEM if near else pl.ANY
    spaces = [pltpu.HBM] * fixed + [pltpu.VMEM] * held
    args = [
        pltpu.with_memory_space_constraint(a, spaces[i]) if i < len(spaces) else a
        for i, a in enumerate(args)
    ]
    spaces += [space] * (len(args) - near_args - len(spaces)) + [pltpu.VMEM] * near_args
    out_spaces = [space] * (len(outs) - near_outs) + [pltpu.VMEM] * near_outs
    return pl.pallas_call(
        body,
        out_shape=outs,
        in_specs=[pl.BlockSpec(memory_space=s) for s in spaces],
        out_specs=[pl.BlockSpec(memory_space=s) for s in out_spaces],
        scratch_shapes=scratch,
        compiler_params=pltpu.CompilerParams(vmem_limit_bytes=grant * 2**20),
        cost_estimate=pl.CostEstimate(flops=flops, bytes_accessed=moved, transcendentals=0),
        name=name,
    )(*args)


def room(arrays):
    return [pltpu.VMEM(a.shape, a.dtype) for a in arrays]


def array(shape, dtype):
    return jax.ShapeDtypeStruct(shape, dtype)


def ends_body(x_ref, b_ref, c_ref, ends_ref, sems):
    tokens, channels = x_ref.shape
    cut = pl.ds(tokens - EDGE, EDGE)
    finished(
        started(
            [x_ref.at[cut, :], b_ref.at[cut, :], c_ref.at[cut, :]],
            [
                ends_ref.at[:, pl.ds(0, channels)],
                ends_ref.at[:, pl.ds(channels, STATE)],
                ends_ref.at[:, pl.ds(channels + STATE, STATE)],
            ],
            sems,
        )
    )


def front_body(paired, count, *refs):
    far, outs, rest = refs[:count], refs[count : count + 3], refs[count + 3 :]
    ends = rest[: 1 + paired]
    rest = rest[1 + paired :]
    near, scratch, pad_ref, sems = rest[:count], rest[count : count + 3], rest[-2], rest[-1]
    copies = started(far, near, sems)
    x_ref, b_ref, c_ref, taps_ref, taps_bc_ref, logs_ref, ids_ref, ends_ref = near
    xconv_ref, bc_ref, lines_ref = scratch
    tokens, channels = x_ref.shape
    heads = logs_ref.shape[0]
    finished(copies)
    pad_ref[0:8, :] = ends_ref[...].astype(F32)[EDGE - 8 : EDGE]
    pad_ref[8 : 8 + tokens, :channels] = x_ref[...].astype(F32)
    pad_ref[8 : 8 + tokens, channels : channels + STATE] = b_ref[...].astype(F32)
    pad_ref[8 : 8 + tokens, channels + STATE :] = c_ref[...].astype(F32)

    def conv(taps, start, stop):
        total = jnp.zeros((tokens, stop - start), F32)
        for k in range(KCONV):
            first = 8 - (KCONV - 1) + k
            total = total + taps[k : k + 1] * pad_ref[first : first + tokens, start:stop]
        return silu(total)

    bc = conv(taps_bc_ref[...], channels, channels + 2 * STATE)
    bc_ref[...] = bc
    xconv = conv(taps_ref[...], 0, channels)
    xconv_ref[...] = xconv
    logs = logs_ref[...]
    inflow = jnp.sqrt(one_minus_exp(2.0 * logs))
    row = dot_exact(logs, upper_ones(tokens))
    lines_ref[0] = row
    lines_ref[1] = inflow
    copies = started(scratch, outs, sems)
    total = row[:, tokens - 1 :]
    spread = head_spread(heads)
    fresh = xconv * dot_left(inflow * jnp.exp(total - row), spread, FIRST)
    state = dot(bc[:, :STATE], fresh, FIRST)
    total = jnp.broadcast_to(total, (heads, NOTES))
    if paired:
        total = dot_exact(total, spread, FIRST)
        half = channels // 2
        side = lax.axis_index("ctx") % 2
        ids = ids_ref[...].astype(F32)
        line = jnp.concatenate([ids[0:1], ids[1:2]], axis=1)
        line = jnp.concatenate([line] * (half // line.shape[1]), axis=1)
        for ref, first in ((ends[0], side == 0), (ends[1], side != 0)):
            mine = jnp.where(first, state[:, :half], state[:, half:])
            logsum = jnp.where(first, total[:1, :half], total[:1, half:])
            if ref is ends[0]:
                put(ref, mine, logsum, line)
            else:
                send(ref, mine, logsum, line)
    else:
        ends[0][:STATE] = state
        ends[0][STATE:] = dot_exact(jnp.exp(total), spread, FIRST)
    finished(copies)


def put(ref, state, logsum, line):
    ref[:STATE] = state
    at = iota((NOTES, state.shape[1]), 0)
    ref[STATE:] = jnp.where(at == 0, logsum, line)


def send(ref, state, logsum, line):
    largest = jnp.max(jnp.abs(state), axis=0, keepdims=True)
    power = jnp.ceil(jnp.log2(jnp.maximum(largest, 1e-30))) - 15.0
    whole = jnp.clip(jnp.round(state * jnp.exp2(-power)), -32767.0, 32767.0)
    ref[:STATE] = whole.astype(jnp.int32).astype(jnp.int16)
    logsum = jnp.round(jnp.maximum(logsum, -128.0) * 2.0**22).astype(jnp.int32)
    at = iota((16, state.shape[1]), 0)
    notes = jnp.where(at == 0, power.astype(jnp.int32), line.astype(jnp.int32))
    notes = jnp.where(at == 1, logsum >> 15, jnp.where(at == 2, logsum & 32767, notes))
    ref[STATE:] = notes.astype(jnp.int16)


def taken(ref):
    return ref[:STATE], ref[STATE : STATE + 1], ref[STATE + 1 : STATE + 2]


def received(ref):
    notes = ref[STATE:].astype(jnp.int32).astype(F32)
    state = ref[:STATE].astype(jnp.int32).astype(F32) * jnp.exp2(notes[0:1])
    return state, notes[1:2] * 2.0**-7 + notes[2:3] * 2.0**-22, notes[3:4]


def ordered(first, own, other):
    return [jnp.where(first, a, b) for a, b in zip(own, other)], [
        jnp.where(first, b, a) for a, b in zip(own, other)
    ]


def together(first, own, other, width):
    (a, a_log, a_line), (b, b_log, b_line) = ordered(first, own, other)
    line = jnp.concatenate([a_line[:, :width], b_line[:, :width]], axis=1)
    line = jnp.concatenate([line] * (a.shape[1] // line.shape[1]), axis=1)
    return jnp.exp(b_log) * a + b, a_log + b_log, line


def place():
    here = lax.axis_index("ctx")
    return here % 2, (here // 2) % 2, here // 4


def pair_body(width, own_ref, got_ref, pair_ref, sent_ref):
    x, _, _ = place()
    pair = together(x == 0, taken(own_ref), received(got_ref), width)
    put(pair_ref, *pair)
    send(sent_ref, *pair)


def four_body(width, pair_ref, got_ref, sent_ref):
    _, z, _ = place()
    send(sent_ref, *together(z == 0, taken(pair_ref), received(got_ref), 2 * width))


def turn_body(
    width, own_ref, got_ref, pair_ref, pair_got_ref, four_got_ref, mine_ref, sent_ref, ids_ref
):
    x, z, zz = place()
    pair, pair_got, four_got = taken(pair_ref), received(pair_got_ref), received(four_got_ref)
    line = together(z == 0, pair, pair_got, 2 * width)[2]
    lines = ordered(zz == 0, [line], [four_got[2]])
    at = iota(ids_ref.shape, 0)
    ids = jnp.zeros(ids_ref.shape, F32)
    for i in range(ids_ref.shape[0]):
        part = lines[i // 4][0][:, i % 4 * width : (i % 4 + 1) * width]
        ids = jnp.where(at == i, part, ids)
    ids_ref[...] = ids

    before = jnp.where(zz == 0, 0.0, four_got[0])
    before = jnp.where(z == 0, before, jnp.exp(pair_got[1]) * before + pair_got[0])
    (first, first_log), _ = ordered(x == 0, taken(own_ref)[:2], received(got_ref)[:2])
    after = jnp.exp(first_log) * before + first
    mine_ref[...] = jnp.where(x == 0, before, after)
    other = jnp.where(x == 0, after, before)
    send(sent_ref, other, jnp.zeros_like(first_log), jnp.zeros_like(first_log))


def inner_body(skip_far, xconv_far, bc_far, lines_far, pre_far, decay_far, *rest):
    far = (skip_far, xconv_far, bc_far, lines_far)
    skip_ref, xconv_ref, bc_ref, lines_ref, pre_ref, decay_ref, sems = rest
    finished(started(far, rest[:4], sems))
    tokens, channels = xconv_ref.shape
    heads = channels // HDIM
    row = lines_ref[0]
    column = row.T
    spread = head_spread(heads)
    decay_ref[...] = dot_left(jnp.exp(row), spread, FIRST)
    copies = started([decay_ref], [decay_far], sems)
    inflow = dot_left(lines_ref[1], spread, FIRST)
    skip = dot_exact(skip_ref[...], spread)
    meet = dot(bc_ref[:, STATE:], bc_ref[:, :STATE], ((1,), (1,)))
    lower = iota((tokens, tokens), 0) >= iota((tokens, tokens), 1)
    left = iota((tokens, 2 * HDIM), 1) < HDIM
    for pair in range(heads // 2):
        cut = slice(pair * 2 * HDIM, (pair + 1) * 2 * HDIM)
        xconv = xconv_ref[:, cut]
        d_high, d_low = halves(xconv * inflow[:, cut])
        both = []
        for h in (2 * pair, 2 * pair + 1):
            gap = column[:, h : h + 1] - row[h : h + 1, :]
            mix = jnp.where(lower, jnp.exp(gap), 0.0) * meet
            m_high, m_low = halves(mix)
            both.append(dot16(m_high, d_high) + dot16(m_high, d_low) + dot16(m_low, d_high))
        pre_ref[:, cut] = skip[:, cut] * xconv + jnp.where(left, both[0], both[1])
    finished(copies + started([pre_ref], [pre_far], sems, 1))


def prefix_body(parts_ref, starts_ref):
    ctx, rows, share = starts_ref.shape
    state = jnp.zeros((rows, share), F32)
    for i in range(ctx):
        starts_ref[i] = state
        if i < ctx - 1:
            state = parts_ref[i, STATE : STATE + 1] * state + parts_ref[i, :STATE]


def back_body(paired, gain_far, pre_far, decay_far, bc_far, *rest):
    starts, (out_far, *rest) = rest[: 1 + paired], rest[1 + paired :]
    far = (gain_far, pre_far, decay_far, bc_far)
    gain_ref, pre_ref, decay_ref, bc_ref, out_ref, sems = rest
    copies = started(far, rest[:4], sems)
    channels = pre_ref.shape[1]
    width = min(channels, 4 * HDIM)
    group = (iota((width, width), 0) // HDIM == iota((width, width), 1) // HDIM).astype(BF16)
    if paired:
        side = lax.axis_index("ctx") % 2
        mine, other = starts[0][...], received(starts[1])[0]
        start = [jnp.where(side == 0, mine, other), jnp.where(side == 0, other, mine)]
        start = jnp.concatenate(start, axis=1)
    else:
        start = starts[0][...]
    finished(copies)
    c_high, c_low = halves(bc_ref[:, STATE:])
    copies = []
    for i in range(channels // width):
        cut = slice(i * width, (i + 1) * width)
        s_high, s_low = halves(start[:, cut])
        carried = dot16(c_high, s_high) + dot16(c_high, s_low) + dot16(c_low, s_high)
        pre = pre_ref[:, cut] + carried * decay_ref[:, cut]
        mean = dot_left(pre * pre, group) * (1.0 / HDIM)
        out_ref[:, cut] = (pre * lax.rsqrt(mean + 1e-05) * gain_ref[:, cut]).astype(BF16)
        copies += started([out_ref.at[:, cut]], [out_far.at[:, cut]], sems, i)
    finished(copies)


def entering_by_pairs(keep, sent, width):
    pair_array, sent_array = array(keep.shape, F32), array(sent.shape, jnp.int16)
    got = swapped(sent, "ctx", 1)
    pair, sent = call(
        functools.partial(pair_body, width),
        [pair_array, sent_array],
        (keep, got),
        near=True,
        name="pair",
    )
    pair_got = swapped(sent, "ctx", 2)
    (sent,) = call(
        functools.partial(four_body, width), [sent_array], (pair, pair_got), near=True, name="four"
    )
    four_got = swapped(sent, "ctx", 4)
    mine, sent, ids = call(
        functools.partial(turn_body, width),
        [array((STATE, keep.shape[1]), F32), sent_array, array((8, width), F32)],
        (keep, got, pair, pair_got, four_got),
        near=True,
        name="turn",
    )
    return (mine, swapped(sent, "ctx", 1)), ids


def entering_by_rows(state):
    ctx = lax.axis_size("ctx")
    rows, channels = state.shape
    slabs = state.reshape(rows, ctx, channels // ctx).transpose(1, 0, 2)
    parts = lax.all_to_all(slabs, "ctx", split_axis=0, concat_axis=0, tiled=True)
    (starts,) = call(
        prefix_body,
        [array((ctx, STATE, channels // ctx), F32)],
        (parts,),
        near=True,
        name="prefix",
    )
    start = lax.all_to_all(starts, "ctx", split_axis=0, concat_axis=0, tiled=True)
    return start.transpose(1, 0, 2).reshape(STATE, channels)


def mixing(
    paired, seq_input, b_input, c_input, before, conv_x, conv_bc, log_decay, skip, gain, ids
):
    tokens, channels = seq_input.shape
    heads = skip.shape[0]
    width = 2 * ids.shape[0]
    outs = [
        array((tokens, channels), F32),
        array((tokens, 2 * STATE), F32),
        array((2, heads, tokens), F32),
    ]
    if paired:
        ends = [array((STATE + NOTES, channels // 2), F32)]
        ends.append(array((STATE + 16, channels // 2), jnp.int16))
    else:
        ends = [array((STATE + NOTES, channels), F32)]
    args = (seq_input, b_input, c_input, conv_x, conv_bc, log_decay, ids.T, before)
    xconv, bc, lines, *ends = call(
        functools.partial(front_body, paired, len(args)),
        outs + ends,
        args,
        fixed=len(args) - 1,
        near_outs=len(ends),
        scratch=room(args) + room(outs) + [pltpu.VMEM((8 + tokens, channels + 2 * STATE), F32)],
        sems=len(args),
        flops=10**9,
        grant=20,
        name="front",
    )
    if paired:
        starts, lines_of_ids = entering_by_pairs(*ends, width)
    else:
        starts, lines_of_ids = (entering_by_rows(ends[0]),), None
    args = (skip.reshape(1, heads), xconv, bc, lines)
    outs = [array((tokens, channels), F32)] * 2
    pre, decay = call(
        inner_body,
        outs,
        args,
        fixed=1,
        scratch=room(args) + room(outs),
        sems=4,
        flops=4 * 10**9,
        grant=16,
        name="inner",
    )
    args = (gain.reshape(1, channels), pre, decay, bc)
    outs = [array((tokens, channels), BF16)]
    (mixed,) = call(
        functools.partial(back_body, paired),
        outs,
        (*args, *starts),
        fixed=1,
        near_args=len(starts),
        scratch=room(args) + room(outs),
        sems=max(4, channels // (4 * HDIM)),
        flops=10**9,
        grant=16,
        name="back",
    )
    return mixed, lines_of_ids


TILE = 512


def join_body(a_ref, b_ref, out_ref, sems):
    rows = a_ref.shape[0]
    finished(
        started([a_ref, b_ref], [out_ref.at[pl.ds(0, rows), :], out_ref.at[pl.ds(rows, rows), :]], sems)
    )


def swapped(block, axis, bit):
    return lax.ppermute(block, axis, [(i, i ^ bit) for i in range(lax.axis_size(axis))])


def expert_body(pieces, w_gate, w_up, *refs):
    far, ids_ref, out_far = refs[:pieces], refs[pieces], refs[pieces + 1]
    pick_ref, hid_ref, out_ref, sems = refs[pieces + 2 :]
    length, hidden = out_ref.shape
    blocks = ids_ref.shape[0]
    rows = length // blocks
    depth = far[0].shape[1]
    me = lax.axis_index("exp")
    here = lax.axis_index("ctx")
    downs = [pl.ds(pl.multiple_of((me ^ k) * depth, depth), depth) for k in range(4)]

    shape = (rows, rows)
    earlier = (iota(shape, 1) < iota(shape, 0)).astype(F32)
    across = iota(shape, 1)
    diagonal = iota(shape, 0) == across
    turns = [here ^ (2 * (i % 4) + i // 4) for i in range(blocks)]
    for i, block in enumerate(turns):
        line = ids_ref[pl.ds(block, 1), :]
        mine = me.astype(F32)
        named = ((line[:, :rows] == mine) | (line[:, rows:] == mine)).astype(F32)
        column = jnp.sum(jnp.where(diagonal, named, 0.0), axis=1, keepdims=True)
        position = jnp.sum(earlier * named, axis=1, keepdims=True).astype(jnp.int32)
        pick_ref[i] = jnp.where(position == across, column, 0.0).astype(BF16)

    out_copies = []
    for n in range(hidden // TILE):
        cut = slice(n * TILE, (n + 1) * TILE)
        gate = upper = None
        for k in range(4):
            block = jnp.concatenate([piece[...] for piece in far[4 * k : 4 * k + 4]], axis=0)
            more = dot16(block, w_gate[0, downs[k], cut])
            gate = more if k == 0 else gate + more
            more = dot16(block, w_up[0, downs[k], cut])
            upper = more if k == 0 else upper + more
        hid_ref[...] = (silu(gate) * upper).astype(BF16)
        for i, block in enumerate(turns):
            picked = dot16(pick_ref[i], hid_ref[i * rows : (i + 1) * rows], FIRST)
            out_ref[pl.ds(pl.multiple_of(block * rows, rows), rows), cut] = picked.astype(BF16)
        out_copies += started([out_ref.at[:, cut]], [out_far.at[0, :, cut]], sems, n)
    finished(out_copies)


def along_z(moe_input):
    rows, columns = moe_input.shape
    joined = call(
        join_body,
        [array((2 * rows, columns), BF16)],
        (moe_input, swapped(moe_input, "ctx", 2)),
        fixed=1,
        sems=2,
        name="join",
    )[0]
    return joined, swapped(joined, "ctx", 4)


def experts_by_tokens(moe_input, ids, w_gate, w_up):
    z = along_z(moe_input)
    x = [swapped(a, "ctx", 1) for a in z]
    y = [swapped(a, "exp", 2) for a in z]
    d = (swapped(y[0], "ctx", 1), swapped(x[1], "exp", 2))
    here = [*z, *x]
    there = [*y, *d]
    beside = [swapped(a, "exp", 1) for a in here]
    corner = [swapped(a, "exp", 1) for a in there]
    pieces = here + beside + there + corner
    rows = moe_input.shape[0]
    length = rows * lax.axis_size("ctx")
    hidden = w_gate.shape[2]
    return call(
        functools.partial(expert_body, len(pieces)),
        [array((1, length, hidden), BF16)],
        (w_gate, w_up, *pieces, ids),
        held=2,
        near_args=len(pieces) + 1,
        scratch=[
            pltpu.VMEM((length // rows, rows, rows), BF16),
            pltpu.VMEM((length, TILE), BF16),
            pltpu.VMEM((length, hidden), BF16),
        ],
        sems=hidden // TILE,
        flops=4 * length * w_gate.shape[1] * hidden,
        grant=16,
        name="experts",
    )[0]


def slot_matrix(pairs, expert, capacity):
    named = jnp.any(pairs == expert, axis=1).astype(jnp.int32)
    position = jnp.cumsum(named) - named
    hit = position[None, :] == jnp.arange(capacity, dtype=jnp.int32)[:, None]
    return (hit & (named[None, :] > 0)).astype(BF16)


def experts_by_slots(moe_input, pairs, w_gate, w_up):
    experts = lax.axis_size("exp")
    capacity = 4 * moe_input.shape[0] // experts
    pick = jax.vmap(lambda e: slot_matrix(pairs, e, capacity))(jnp.arange(experts))
    slots = jnp.einsum("eqt,td->eqd", pick, moe_input, preferred_element_type=F32)
    routed = lax.all_to_all(slots.astype(BF16), "exp", split_axis=0, concat_axis=2, tiled=True)
    rows = lax.all_gather(routed[0], "ctx", axis=0, tiled=True)
    gate = jnp.dot(rows, w_gate[0], preferred_element_type=F32)
    upper = jnp.dot(rows, w_up[0], preferred_element_type=F32)
    return (jax.nn.silu(gate) * upper).astype(BF16)[None]


def on_device(
    seq_input,
    b_input,
    c_input,
    conv_x,
    conv_bc,
    log_decay,
    skip_gain,
    norm_gain,
    moe_input,
    expert_ids,
    w_gate,
    w_up,
):
    ctx = lax.axis_size("ctx")
    by_tokens = lax.axis_size("exp") == 4 and ctx == 8
    tokens, channels = seq_input.shape
    ends = call(
        ends_body,
        [array((EDGE, channels + 2 * STATE), BF16)],
        (seq_input, b_input, c_input),
        fixed=3,
        sems=3,
        name="ends",
    )[0]
    before = lax.ppermute(ends, "ctx", [(i, i + 1) for i in range(ctx - 1)])
    mixed, ids = mixing(
        by_tokens,
        seq_input,
        b_input,
        c_input,
        before,
        conv_x,
        conv_bc,
        log_decay,
        skip_gain,
        norm_gain,
        expert_ids,
    )
    if by_tokens:
        hidden = experts_by_tokens(moe_input, ids, w_gate, w_up)
    else:
        hidden = experts_by_slots(moe_input, expert_ids, w_gate, w_up)
    return (mixed, hidden)


def solution(mesh):
    in_specs = (
        P("ctx", "exp"),
        P("ctx", None),
        P("ctx", None),
        P(None, "exp"),
        P(),
        P("exp", "ctx"),
        P("exp"),
        P("exp"),
        P("ctx", "exp"),
        P("ctx", None),
        P("exp", None, "ctx"),
        P("exp", None, "ctx"),
    )
    out_specs = (P("ctx", "exp"), P("exp", None, "ctx"))
    return jax.shard_map(
        on_device, mesh=mesh, in_specs=in_specs, out_specs=out_specs, check_vma=False
    )
```

time: 95.3 us -> 70.7 us (0.74)
  local copies, waits for them, and re-layouts: 9.17 us -> 0.01 us
  waiting for transfers between devices: 23.7 us -> 17.7 us
  Pallas kernels: 29.1 us -> 24.2 us
  starting transfers between devices: 31.8 us -> 27.2 us
    all_to_all x2 -> x0, starting transfers between devices: 12.1 us -> none  [the longest x1 6.64 us: mixing(): parts = lax.all_to_all(slab, 'ctx', split_axis=0, concat_axis=0, tiled=True)]
    unnamed x18 -> x8, local copies, waits for them, and re-layouts: 9.17 us -> 0.01 us
    ppermute x16 -> x20, starting transfers between devices: 14.9 us -> 22.4 us  [swapped(): lax.ppermute(block, axis, [(i, i ^ bit) for i in range(lax.axis_size(axis...]
    pallas_call x7 -> x9, Pallas kernels: 29.1 us -> 24.2 us  [call(): pl.pallas_call(body, out_shape=outs, in_specs=[pl.BlockSpec(memory_space=...]
    ppermute x16 -> x20, waiting for transfers between devices: 22 us -> 17.7 us  [swapped(): lax.ppermute(block, axis, [(i, i ^ bit) for i in range(lax.axis_size(axis...]
    ppermute x1, waiting for transfers between devices: 1.65 us -> 0.01 us  [on_device(): before = lax.ppermute(ends, 'ctx', [(i, i + 1) for i in range(ctx - 1)])]
  transfers between devices with their start and end apart: 19 -> 21, of which waited for: 4 -> 7; matrix products, arithmetic and copies ran while one was open for 0% -> 0% of each run, Pallas kernels for 21% -> 19%
where the time goes in v6:
time: 70.7 us; the launch traced here: 70.1 us
  starting transfers between devices  27.2 us (38%)
  Pallas kernels  24.2 us (34%)
  waiting for transfers between devices  17.7 us (25%)
  between operations  0.97 us (1%)
    pallas_call x9, Pallas kernels, call(): pl.pallas_call(body, out_shape=outs, in_specs=[pl.BlockSpec(memory_space=...  24.2 us
    ppermute x20, starting transfers between devices, swapped(): lax.ppermute(block, axis, [(i, i ^ bit) for i in range(lax.axis_size(axis...  22.4 us
    ppermute x20, waiting for transfers between devices, swapped(): lax.ppermute(block, axis, [(i, i ^ bit) for i in range(lax.axis_size(axis...  17.7 us
    ppermute x1, starting transfers between devices, on_device(): before = lax.ppermute(ends, 'ctx', [(i, i + 1) for i in range(ctx - 1)])  4.84 us
  transfers between devices with their start and end apart: 21, of which 7 were waited for; matrix products, arithmetic and copies ran while one was open for 0% of the time, Pallas kernels for 19%

profile of v6, /device:TPU:0, one launch (start us, length us, event | category | flops | bytes accessed | tf_op | source)
XLA Modules:
  0.0 70.1 jit_solution(130067631175827675)
XLA Ops:
  0.6 0.8 %ends.1 = bf16[16,1280]{1,0:T(8,128)(2,1)S(1)} custom-call(bf16[256,1024]{1,0:T(8,128)(2,1)} %refs_0_.1, bf16[256,128]{1,0:T(8,128)(2,1)} %refs_1_.1, bf16[256,128]{1,0:T(8,128)(2,1)} %refs_2_.1), custom_call_target="tpu_custom_call" | custom-call | bytes 696320 | tf_op jit(solution)/shard_map/ends/pallas_call | solution.py:113
  1.4 4.8 %collective-permute-start = (bf16[16,1280]{1,0:T(8,128)(2,1)S(1)}, bf16[16,1280]{1,0:T(8,128)(2,1)S(1)}, u32[]{:S(2)}, u32[]{:S(2)}) collective-permute-start(bf16[16,1280]{1,0:T(8,128)(2,1)S(1)} %ends.1), channel_id=1, source_target_pairs={{0,4},{4,8},{8,12},{12,16},{16,20},{20,24},{24,28},{1,5},{5,9},{9,... | collective-permute-start | bytes 122888 | tf_op jit(solution)/shard_map/ppermute | solution.py:604
  6.3 1.6 %collective-permute-start.5 = (bf16[64,1024]{1,0:T(8,128)(2,1)}, bf16[64,1024]{1,0:T(8,128)(2,1)S(1)}, u32[]{:S(2)}, u32[]{:S(2)}) collective-permute-start(bf16[64,1024]{1,0:T(8,128)(2,1)} %a_ref.1), channel_id=1, source_target_pairs={{0,8},{4,12},{8,0},{12,4},{16,24},{20,28},{24,16},{28,20},{1,9},{5... | collective-permute-start | bytes 393224 | tf_op jit(solution)/shard_map/ppermute | solution.py:471
  7.9 4.4 %front.1 = (f32[256,1024]{1,0:T(8,128)S(1)}, f32[256,256]{1,0:T(8,128)S(1)}, f32[2,16,256]{2,1,0:T(8,128)S(1)}, f32[136,512]{1,0:T(8,128)S(1)}, s16[144,512]{1,0:T(8,128)(2,1)S(1)}) custom-call(bf16[256,1024]{1,0:T(8,128)(2,1)} %refs_0_.1, bf16[256,128]{1,0:T(8,128)(2,1)} %refs_1_.1, bf16[256,128]{1,0:T(8,128)(2,1)} %refs_2_.1, f32[4,1024]{1,0:T(4,128)} %refs_3_.1, ...), custom_call_target="tpu_custom_call" | custom-call | flops 1000000000 | bytes 2503168 | tf_op jit(solution)/shard_map/front/pallas_call | solution.py:113
  12.4 2.4 %collective-permute-start.1 = (s16[144,512]{1,0:T(8,128)(2,1)S(1)}, s16[144,512]{1,0:T(8,128)(2,1)S(1)}, u32[]{:S(2)}, u32[]{:S(2)}) collective-permute-start(s16[144,512]{1,0:T(8,128)(2,1)S(1)} %get-tuple-element.20), channel_id=1, source_target_pairs={{0,4},{4,0},{8,12},{12,8},{16,20},{20,16},{24,28},{28,24},{1,5},{5... | collective-permute-start | bytes 442376 | tf_op jit(solution)/shard_map/ppermute | solution.py:471
  14.8 0.9 %join.1.refs_0_ = bf16[128,1024]{1,0:T(8,128)(2,1)S(1)} custom-call(bf16[64,1024]{1,0:T(8,128)(2,1)} %a_ref.1, bf16[64,1024]{1,0:T(8,128)(2,1)S(1)} %collective-permute-done.5.b_ref), custom_call_target="tpu_custom_call" | custom-call | bytes 524288 | tf_op jit(solution)/shard_map/join/pallas_call | solution.py:113
  15.7 2.7 %collective-permute-start.6 = (bf16[128,1024]{1,0:T(8,128)(2,1)S(1)}, bf16[128,1024]{1,0:T(8,128)(2,1)S(1)}, u32[]{:S(2)}, u32[]{:S(2)}) collective-permute-start(bf16[128,1024]{1,0:T(8,128)(2,1)S(1)} %join.1.refs_0_), channel_id=1, source_target_pairs={{0,16},{4,20},{8,24},{12,28},{16,0},{20,4},{24,8},{28,12},{1,17},{... | collective-permute-start | bytes 786440 | tf_op jit(solution)/shard_map/ppermute | solution.py:471
  18.4 0.1 pair.1
  18.5 2.6 %collective-permute-start.2 = (s16[144,512]{1,0:T(8,128)(2,1)S(1)}, s16[144,512]{1,0:T(8,128)(2,1)S(1)}, u32[]{:S(2)}, u32[]{:S(2)}) collective-permute-start(s16[144,512]{1,0:T(8,128)(2,1)S(1)} %get-tuple-element.22), channel_id=1, source_target_pairs={{0,8},{4,12},{8,0},{12,4},{16,24},{20,28},{24,16},{28,20},{1,9},{5... | collective-permute-start | bytes 442376 | tf_op jit(solution)/shard_map/ppermute | solution.py:471
  21.1 4.6 %collective-permute-done.2.got_ref.pair_got_ref = s16[144,512]{1,0:T(8,128)(2,1)S(1)} collective-permute-done((s16[144,512]{1,0:T(8,128)(2,1)S(1)}, s16[144,512]{1,0:T(8,128)(2,1)S(1)}, u32[]{:S(2)}, u32[]{:S(2)}) %collective-permute-start.2) | collective-permute-done | bytes 147488 | tf_op jit(solution)/shard_map/ppermute | solution.py:471
  25.7 0.1 four.1
  25.8 3.2 %collective-permute-start.3 = (s16[144,512]{1,0:T(8,128)(2,1)S(1)}, s16[144,512]{1,0:T(8,128)(2,1)S(1)}, u32[]{:S(2)}, u32[]{:S(2)}) collective-permute-start(s16[144,512]{1,0:T(8,128)(2,1)S(1)} %four.1), channel_id=1, source_target_pairs={{0,16},{4,20},{8,24},{12,28},{16,0},{20,4},{24,8},{28,12},{1,17},{... | collective-permute-start | bytes 442376 | tf_op jit(solution)/shard_map/ppermute | solution.py:471
  29.0 0.7 collective-permute-start.7
  29.7 1.5 %collective-permute-start.13 = (bf16[128,1024]{1,0:T(8,128)(2,1)S(1)}, bf16[128,1024]{1,0:T(8,128)(2,1)S(1)}, u32[]{:S(2)}, u32[]{:S(2)}) collective-permute-start(bf16[128,1024]{1,0:T(8,128)(2,1)S(1)} %join.1.refs_0_), channel_id=1, source_target_pairs={{0,2},{1,3},{2,0},{3,1},{4,6},{5,7},{6,4},{7,5},{8,10},{9,11},{10,... | collective-permute-start | bytes 786440 | tf_op jit(solution)/shard_map/ppermute | solution.py:471
  31.2 0.4 collective-permute-done.6.refs_1_
  31.7 1.4 %collective-permute-start.8 = (bf16[128,1024]{1,0:T(8,128)(2,1)S(1)}, bf16[128,1024]{1,0:T(8,128)(2,1)S(1)}, u32[]{:S(2)}, u32[]{:S(2)}) collective-permute-start(bf16[128,1024]{1,0:T(8,128)(2,1)S(1)} %collective-permute-done.6.refs_1_), channel_id=1, source_target_pairs={{0,4},{4,0},{8,12},{12,8},{16,20},{20,16},{24,28},{28,24},{1,5},{5... | collective-permute-start | bytes 786440 | tf_op jit(solution)/shard_map/ppermute | solution.py:471
  33.1 2.1 %collective-permute-done.3.four_got_ref = s16[144,512]{1,0:T(8,128)(2,1)S(1)} collective-permute-done((s16[144,512]{1,0:T(8,128)(2,1)S(1)}, s16[144,512]{1,0:T(8,128)(2,1)S(1)}, u32[]{:S(2)}, u32[]{:S(2)}) %collective-permute-start.3) | collective-permute-done | bytes 147488 | tf_op jit(solution)/shard_map/ppermute | solution.py:471
  35.2 0.2 turn.1
  35.5 1.4 %collective-permute-start.4 = (s16[144,512]{1,0:T(8,128)(2,1)S(1)}, s16[144,512]{1,0:T(8,128)(2,1)S(1)}, u32[]{:S(2)}, u32[]{:S(2)}) collective-permute-start(s16[144,512]{1,0:T(8,128)(2,1)S(1)} %get-tuple-element.24), channel_id=1, source_target_pairs={{0,4},{4,0},{8,12},{12,8},{16,20},{20,16},{24,28},{28,24},{1,5},{5... | collective-permute-start | bytes 442376 | tf_op jit(solution)/shard_map/ppermute | solution.py:471
  36.9 0.5 collective-permute-start.11
  37.4 1.0 %collective-permute-done.13.refs_8_ = bf16[128,1024]{1,0:T(8,128)(2,1)S(1)} collective-permute-done((bf16[128,1024]{1,0:T(8,128)(2,1)S(1)}, bf16[128,1024]{1,0:T(8,128)(2,1)S(1)}, u32[]{:S(2)}, u32[]{:S(2)}) %collective-permute-start.13) | collective-permute-done | bytes 262176 | tf_op jit(solution)/shard_map/ppermute | solution.py:471
  38.4 1.5 %collective-permute-start.14 = (bf16[128,1024]{1,0:T(8,128)(2,1)S(1)}, bf16[128,1024]{1,0:T(8,128)(2,1)S(1)}, u32[]{:S(2)}, u32[]{:S(2)}) collective-permute-start(bf16[128,1024]{1,0:T(8,128)(2,1)S(1)} %collective-permute-done.6.refs_1_), channel_id=1, source_target_pairs={{0,2},{1,3},{2,0},{3,1},{4,6},{5,7},{6,4},{7,5},{8,10},{9,11},{10,... | collective-permute-start | bytes 786440 | tf_op jit(solution)/shard_map/ppermute | solution.py:471
  40.0 4.2 %collective-permute-done.4.rest_1_ = s16[144,512]{1,0:T(8,128)(2,1)S(1)} collective-permute-done((s16[144,512]{1,0:T(8,128)(2,1)S(1)}, s16[144,512]{1,0:T(8,128)(2,1)S(1)}, u32[]{:S(2)}, u32[]{:S(2)}) %collective-permute-start.4) | collective-permute-done | bytes 147488 | tf_op jit(solution)/shard_map/ppermute | solution.py:471
  44.2 0.7 collective-permute-start.15
  44.9 1.5 %collective-permute-start.16 = (bf16[128,1024]{1,0:T(8,128)(2,1)S(1)}, bf16[128,1024]{1,0:T(8,128)(2,1)S(1)}, u32[]{:S(2)}, u32[]{:S(2)}) collective-permute-start(bf16[128,1024]{1,0:T(8,128)(2,1)S(1)} %collective-permute-done.8.refs_3_), channel_id=1, source_target_pairs={{0,2},{1,3},{2,0},{3,1},{4,6},{5,7},{6,4},{7,5},{8,10},{9,11},{10,... | collective-permute-start | bytes 786440 | tf_op jit(solution)/shard_map/ppermute | solution.py:471
  46.4 0.5 collective-permute-start.12
  46.9 0.1 collective-permute-start.18
  47.0 4.2 %collective-permute-done.15.refs_10_ = bf16[128,1024]{1,0:T(8,128)(2,1)S(1)} collective-permute-done((bf16[128,1024]{1,0:T(8,128)(2,1)S(1)}, bf16[128,1024]{1,0:T(8,128)(2,1)S(1)}, u32[]{:S(2)}, u32[]{:S(2)}) %collective-permute-start.15) | collective-permute-done | bytes 262176 | tf_op jit(solution)/shard_map/ppermute | solution.py:471
  51.2 1.1 %collective-permute-done.16.refs_11_ = bf16[128,1024]{1,0:T(8,128)(2,1)S(1)} collective-permute-done((bf16[128,1024]{1,0:T(8,128)(2,1)S(1)}, bf16[128,1024]{1,0:T(8,128)(2,1)S(1)}, u32[]{:S(2)}, u32[]{:S(2)}) %collective-permute-start.16) | collective-permute-done | bytes 262176 | tf_op jit(solution)/shard_map/ppermute | solution.py:471
  52.3 4.2 %inner.1 = (f32[256,1024]{1,0:T(8,128)S(1)}, f32[256,1024]{1,0:T(8,128)S(1)}) custom-call(f32[1,16]{1,0:T(1,128)} %bitcast.9, f32[256,1024]{1,0:T(8,128)S(1)} %get-tuple-element.14.xconv_far, f32[256,256]{1,0:T(8,128)S(1)} %get-tuple-element.15.bc_far, f32[2,16,256]{2,1,0:T(8,128)S(1)} %get-tuple-element.16.lines_far), custom_call_target="tpu_custom_call" | custom-call | flops 4000000000 | bytes 3440704 | tf_op jit(solution)/shard_map/inner/pallas_call | solution.py:113
  56.5 3.1 %back.1 = bf16[256,1024]{1,0:T(8,128)(2,1)} custom-call(f32[1,1024]{1,0:T(1,128)} %bitcast.7, f32[256,1024]{1,0:T(8,128)S(1)} %get-tuple-element.17.pre_far, f32[256,1024]{1,0:T(8,128)S(1)} %get-tuple-element.18.decay_far, f32[256,256]{1,0:T(8,128)S(1)} %get-tuple-element.15.bc_far, f32[128,512]{1,0:T(8,128)S(1)} %get-tuple-element.23.rest_0_, ...), custom_call_target="tpu_custom_call" | custom-call | flops 1000000000 | bytes 3297280 | tf_op jit(solution)/shard_map/back/pallas_call | solution.py:113
  59.8 10.2 %experts.1 = bf16[1,512,1024]{2,1,0:T(8,128)(2,1)} custom-call(bf16[1,4096,1024]{2,1,0:T(8,128)(2,1)S(1)} %bitcast.4, bf16[1,4096,1024]{2,1,0:T(8,128)(2,1)S(1)} %bitcast.6, bf16[128,1024]{1,0:T(8,128)(2,1)S(1)} %join.1.refs_0_, bf16[128,1024]{1,0:T(8,128)(2,1)S(1)} %collective-permute-done.6.refs_1_, bf16[128,1024]{1,0:T(8,128)(2,1)S(1)} %collective-permute-done.7.refs_2_, ...), custom_call_target="tpu_custom_call" | custom-call | flops 8589934592 | bytes 22024192 | tf_op jit(solution)/shard_map/experts/pallas_call | solution.py:113
  (29 shorter events, 0.1 us)
Async XLA Ops:
  1.4 6.5 %collective-permute-start = (bf16[16,1280]{1,0:T(8,128)(2,1)S(1)}, bf16[16,1280]{1,0:T(8,128)(2,1)S(1)}, u32[]{:S(2)}, u32[]{:S(2)}) collective-permute-start(bf16[16,1280]{1,0:T(8,128)(2,1)S(1)} %ends.1), channel_id=1, source_target_pairs={{0,4},{4,8},{8,12},{12,16},{16,20},{20,24},{24,28},{1,5},{5,9},{9,... | collective-permute-start | bytes 122888 | tf_op jit(solution)/shard_map/ppermute | solution.py:604
  6.3 8.5 %collective-permute-start.5 = (bf16[64,1024]{1,0:T(8,128)(2,1)}, bf16[64,1024]{1,0:T(8,128)(2,1)S(1)}, u32[]{:S(2)}, u32[]{:S(2)}) collective-permute-start(bf16[64,1024]{1,0:T(8,128)(2,1)} %a_ref.1), channel_id=1, source_target_pairs={{0,8},{4,12},{8,0},{12,4},{16,24},{20,28},{24,16},{28,20},{1,9},{5... | collective-permute-start | bytes 393224 | tf_op jit(solution)/shard_map/ppermute | solution.py:471
  7.9 51.8 %slice-start.2 = ((s8[8388608]{0:T(1024)(128)(4,1)}), s8[4194304]{0:T(1024)(128)(4,1)S(1)}, s32[]{:S(2)}) async-start(s8[8388608]{0:T(1024)(128)(4,1)} %bitcast.5), calls=%async_computation.2 | async-start | bytes 8388608
  12.4 6.0 %collective-permute-start.1 = (s16[144,512]{1,0:T(8,128)(2,1)S(1)}, s16[144,512]{1,0:T(8,128)(2,1)S(1)}, u32[]{:S(2)}, u32[]{:S(2)}) collective-permute-start(s16[144,512]{1,0:T(8,128)(2,1)S(1)} %get-tuple-element.20), channel_id=1, source_target_pairs={{0,4},{4,0},{8,12},{12,8},{16,20},{20,16},{24,28},{28,24},{1,5},{5... | collective-permute-start | bytes 442376 | tf_op jit(solution)/shard_map/ppermute | solution.py:471
  15.7 16.0 %collective-permute-start.6 = (bf16[128,1024]{1,0:T(8,128)(2,1)S(1)}, bf16[128,1024]{1,0:T(8,128)(2,1)S(1)}, u32[]{:S(2)}, u32[]{:S(2)}) collective-permute-start(bf16[128,1024]{1,0:T(8,128)(2,1)S(1)} %join.1.refs_0_), channel_id=1, source_target_pairs={{0,16},{4,20},{8,24},{12,28},{16,0},{20,4},{24,8},{28,12},{1,17},{... | collective-permute-start | bytes 786440 | tf_op jit(solution)/shard_map/ppermute | solution.py:471
  18.5 7.2 %collective-permute-start.2 = (s16[144,512]{1,0:T(8,128)(2,1)S(1)}, s16[144,512]{1,0:T(8,128)(2,1)S(1)}, u32[]{:S(2)}, u32[]{:S(2)}) collective-permute-start(s16[144,512]{1,0:T(8,128)(2,1)S(1)} %get-tuple-element.22), channel_id=1, source_target_pairs={{0,8},{4,12},{8,0},{12,4},{16,24},{20,28},{24,16},{28,20},{1,9},{5... | collective-permute-start | bytes 442376 | tf_op jit(solution)/shard_map/ppermute | solution.py:471
  25.8 9.4 %collective-permute-start.3 = (s16[144,512]{1,0:T(8,128)(2,1)S(1)}, s16[144,512]{1,0:T(8,128)(2,1)S(1)}, u32[]{:S(2)}, u32[]{:S(2)}) collective-permute-start(s16[144,512]{1,0:T(8,128)(2,1)S(1)} %four.1), channel_id=1, source_target_pairs={{0,16},{4,20},{8,24},{12,28},{16,0},{20,4},{24,8},{28,12},{1,17},{... | collective-permute-start | bytes 442376 | tf_op jit(solution)/shard_map/ppermute | solution.py:471
  29.0 7.9 %collective-permute-start.7 = (bf16[128,1024]{1,0:T(8,128)(2,1)S(1)}, bf16[128,1024]{1,0:T(8,128)(2,1)S(1)}, u32[]{:S(2)}, u32[]{:S(2)}) collective-permute-start(bf16[128,1024]{1,0:T(8,128)(2,1)S(1)} %join.1.refs_0_), channel_id=1, source_target_pairs={{0,4},{4,0},{8,12},{12,8},{16,20},{20,16},{24,28},{28,24},{1,5},{5... | collective-permute-start | bytes 786440 | tf_op jit(solution)/shard_map/ppermute | solution.py:471
  29.7 7.2 %collective-permute-start.9 = (bf16[128,1024]{1,0:T(8,128)(2,1)S(1)}, bf16[128,1024]{1,0:T(8,128)(2,1)S(1)}, u32[]{:S(2)}, u32[]{:S(2)}) collective-permute-start(bf16[128,1024]{1,0:T(8,128)(2,1)S(1)} %join.1.refs_0_), channel_id=1, source_target_pairs={{0,1},{1,0},{2,3},{3,2},{4,5},{5,4},{6,7},{7,6},{8,9},{9,8},{10,11... | collective-permute-start | bytes 786440 | tf_op jit(solution)/shard_map/ppermute | solution.py:471
  29.7 8.7 %collective-permute-start.13 = (bf16[128,1024]{1,0:T(8,128)(2,1)S(1)}, bf16[128,1024]{1,0:T(8,128)(2,1)S(1)}, u32[]{:S(2)}, u32[]{:S(2)}) collective-permute-start(bf16[128,1024]{1,0:T(8,128)(2,1)S(1)} %join.1.refs_0_), channel_id=1, source_target_pairs={{0,2},{1,3},{2,0},{3,1},{4,6},{5,7},{6,4},{7,5},{8,10},{9,11},{10,... | collective-permute-start | bytes 786440 | tf_op jit(solution)/shard_map/ppermute | solution.py:471
  31.7 13.2 %collective-permute-start.8 = (bf16[128,1024]{1,0:T(8,128)(2,1)S(1)}, bf16[128,1024]{1,0:T(8,128)(2,1)S(1)}, u32[]{:S(2)}, u32[]{:S(2)}) collective-permute-start(bf16[128,1024]{1,0:T(8,128)(2,1)S(1)} %collective-permute-done.6.refs_1_), channel_id=1, source_target_pairs={{0,4},{4,0},{8,12},{12,8},{16,20},{20,16},{24,28},{28,24},{1,5},{5... | collective-permute-start | bytes 786440 | tf_op jit(solution)/shard_map/ppermute | solution.py:471
  35.2 24.5 %slice-start = ((s8[8388608]{0:T(1024)(128)(4,1)}), s8[4194304]{0:T(1024)(128)(4,1)S(1)}, s32[]{:S(2)}) async-start(s8[8388608]{0:T(1024)(128)(4,1)} %bitcast.3), calls=%async_computation | async-start | bytes 8388608
  35.5 8.7 %collective-permute-start.4 = (s16[144,512]{1,0:T(8,128)(2,1)S(1)}, s16[144,512]{1,0:T(8,128)(2,1)S(1)}, u32[]{:S(2)}, u32[]{:S(2)}) collective-permute-start(s16[144,512]{1,0:T(8,128)(2,1)S(1)} %get-tuple-element.24), channel_id=1, source_target_pairs={{0,4},{4,0},{8,12},{12,8},{16,20},{20,16},{24,28},{28,24},{1,5},{5... | collective-permute-start | bytes 442376 | tf_op jit(solution)/shard_map/ppermute | solution.py:471
  36.9 9.5 %collective-permute-start.10 = (bf16[128,1024]{1,0:T(8,128)(2,1)S(1)}, bf16[128,1024]{1,0:T(8,128)(2,1)S(1)}, u32[]{:S(2)}, u32[]{:S(2)}) collective-permute-start(bf16[128,1024]{1,0:T(8,128)(2,1)S(1)} %collective-permute-done.6.refs_1_), channel_id=1, source_target_pairs={{0,1},{1,0},{2,3},{3,2},{4,5},{5,4},{6,7},{7,6},{8,9},{9,8},{10,11... | collective-permute-start | bytes 786440 | tf_op jit(solution)/shard_map/ppermute | solution.py:471
  36.9 9.5 %collective-permute-start.11 = (bf16[128,1024]{1,0:T(8,128)(2,1)S(1)}, bf16[128,1024]{1,0:T(8,128)(2,1)S(1)}, u32[]{:S(2)}, u32[]{:S(2)}) collective-permute-start(bf16[128,1024]{1,0:T(8,128)(2,1)S(1)} %collective-permute-done.7.refs_2_), channel_id=1, source_target_pairs={{0,1},{1,0},{2,3},{3,2},{4,5},{5,4},{6,7},{7,6},{8,9},{9,8},{10,11... | collective-permute-start | bytes 786440 | tf_op jit(solution)/shard_map/ppermute | solution.py:471
  38.4 8.5 %collective-permute-start.14 = (bf16[128,1024]{1,0:T(8,128)(2,1)S(1)}, bf16[128,1024]{1,0:T(8,128)(2,1)S(1)}, u32[]{:S(2)}, u32[]{:S(2)}) collective-permute-start(bf16[128,1024]{1,0:T(8,128)(2,1)S(1)} %collective-permute-done.6.refs_1_), channel_id=1, source_target_pairs={{0,2},{1,3},{2,0},{3,1},{4,6},{5,7},{6,4},{7,5},{8,10},{9,11},{10,... | collective-permute-start | bytes 786440 | tf_op jit(solution)/shard_map/ppermute | solution.py:471
  44.2 7.0 %collective-permute-start.15 = (bf16[128,1024]{1,0:T(8,128)(2,1)S(1)}, bf16[128,1024]{1,0:T(8,128)(2,1)S(1)}, u32[]{:S(2)}, u32[]{:S(2)}) collective-permute-start(bf16[128,1024]{1,0:T(8,128)(2,1)S(1)} %collective-permute-done.13.refs_8_), channel_id=1, source_target_pairs={{0,4},{4,0},{8,12},{12,8},{16,20},{20,16},{24,28},{28,24},{1,5},{5... | collective-permute-start | bytes 786440 | tf_op jit(solution)/shard_map/ppermute | solution.py:471
  44.9 7.4 %collective-permute-start.16 = (bf16[128,1024]{1,0:T(8,128)(2,1)S(1)}, bf16[128,1024]{1,0:T(8,128)(2,1)S(1)}, u32[]{:S(2)}, u32[]{:S(2)}) collective-permute-start(bf16[128,1024]{1,0:T(8,128)(2,1)S(1)} %collective-permute-done.8.refs_3_), channel_id=1, source_target_pairs={{0,2},{1,3},{2,0},{3,1},{4,6},{5,7},{6,4},{7,5},{8,10},{9,11},{10,... | collective-permute-start | bytes 786440 | tf_op jit(solution)/shard_map/ppermute | solution.py:471
  46.4 13.3 %collective-permute-start.17 = (bf16[128,1024]{1,0:T(8,128)(2,1)S(1)}, bf16[128,1024]{1,0:T(8,128)(2,1)S(1)}, u32[]{:S(2)}, u32[]{:S(2)}) collective-permute-start(bf16[128,1024]{1,0:T(8,128)(2,1)S(1)} %collective-permute-done.13.refs_8_), channel_id=1, source_target_pairs={{0,1},{1,0},{2,3},{3,2},{4,5},{5,4},{6,7},{7,6},{8,9},{9,8},{10,11... | collective-permute-start | bytes 786440 | tf_op jit(solution)/shard_map/ppermute | solution.py:471
  46.4 13.3 %collective-permute-start.12 = (bf16[128,1024]{1,0:T(8,128)(2,1)S(1)}, bf16[128,1024]{1,0:T(8,128)(2,1)S(1)}, u32[]{:S(2)}, u32[]{:S(2)}) collective-permute-start(bf16[128,1024]{1,0:T(8,128)(2,1)S(1)} %collective-permute-done.8.refs_3_), channel_id=1, source_target_pairs={{0,1},{1,0},{2,3},{3,2},{4,5},{5,4},{6,7},{7,6},{8,9},{9,8},{10,11... | collective-permute-start | bytes 786440 | tf_op jit(solution)/shard_map/ppermute | solution.py:471
  46.9 12.8 %collective-permute-start.18 = (bf16[128,1024]{1,0:T(8,128)(2,1)S(1)}, bf16[128,1024]{1,0:T(8,128)(2,1)S(1)}, u32[]{:S(2)}, u32[]{:S(2)}) collective-permute-start(bf16[128,1024]{1,0:T(8,128)(2,1)S(1)} %collective-permute-done.14.refs_9_), channel_id=1, source_target_pairs={{0,1},{1,0},{2,3},{3,2},{4,5},{5,4},{6,7},{7,6},{8,9},{9,8},{10,11... | collective-permute-start | bytes 786440 | tf_op jit(solution)/shard_map/ppermute | solution.py:471
  51.2 8.5 %collective-permute-start.19 = (bf16[128,1024]{1,0:T(8,128)(2,1)S(1)}, bf16[128,1024]{1,0:T(8,128)(2,1)S(1)}, u32[]{:S(2)}, u32[]{:S(2)}) collective-permute-start(bf16[128,1024]{1,0:T(8,128)(2,1)S(1)} %collective-permute-done.15.refs_10_), channel_id=1, source_target_pairs={{0,1},{1,0},{2,3},{3,2},{4,5},{5,4},{6,7},{7,6},{8,9},{9,8},{10,11... | collective-permute-start | bytes 786440 | tf_op jit(solution)/shard_map/ppermute | solution.py:471
  52.3 7.4 %collective-permute-start.20 = (bf16[128,1024]{1,0:T(8,128)(2,1)S(1)}, bf16[128,1024]{1,0:T(8,128)(2,1)S(1)}, u32[]{:S(2)}, u32[]{:S(2)}) collective-permute-start(bf16[128,1024]{1,0:T(8,128)(2,1)S(1)} %collective-permute-done.16.refs_11_), channel_id=1, source_target_pairs={{0,1},{1,0},{2,3},{3,2},{4,5},{5,4},{6,7},{7,6},{8,9},{9,8},{10,11... | collective-permute-start | bytes 786440 | tf_op jit(solution)/shard_map/ppermute | solution.py:471
  52.3 7.4 %slice-start.1 = ((s8[8388608]{0:T(1024)(128)(4,1)}), s8[4194304]{0:T(1024)(128)(4,1)S(1)}, s32[]{:S(2)}) async-start(s8[8388608]{0:T(1024)(128)(4,1)} %bitcast.3), calls=%async_computation.1 | async-start | bytes 8388608
  52.3 7.5 %slice-start.3 = ((s8[8388608]{0:T(1024)(128)(4,1)}), s8[4194304]{0:T(1024)(128)(4,1)S(1)}, s32[]{:S(2)}) async-start(s8[8388608]{0:T(1024)(128)(4,1)} %bitcast.5), calls=%async_computation.3 | async-start | bytes 8388608

commit v7 on v6

--- a/solution.py
+++ b/solution.py
@@ -83,6 +83,10 @@
 def finished(copies):
     for copy in copies:
         copy.wait()
+
+
+def following(body, count, skipped):
+    return lambda *refs: body(*refs[:count], *refs[count + skipped :])
 
 
 def call(
@@ -93,13 +97,18 @@
     held=0,
     near_args=0,
     near_outs=0,
+    after=(),
+    after_far=(),
+    aliases=None,
     scratch=(),
     sems=0,
     flops=0,
     grant=8,
     near=False,
+    spaces_of=None,
     name=None,
 ):
+    body = following(body, len(args), len(after) + len(after_far))
     moved = sum(math.prod(a.shape) * a.dtype.itemsize for a in (*args, *outs))
     scratch = list(scratch) + ([pltpu.SemaphoreType.DMA((sems,))] if sems else [])
     space = pltpu.VMEM if near else pl.ANY
@@ -109,6 +118,10 @@
         for i, a in enumerate(args)
     ]
     spaces += [space] * (len(args) - near_args - len(spaces)) + [pltpu.VMEM] * near_args
+    spaces = spaces_of or spaces
+    args, spaces = [*args, *after], spaces + [pl.ANY] * len(after)
+    args += [pltpu.with_memory_space_constraint(a, pltpu.HBM) for a in after_far]
+    spaces += [pltpu.HBM] * len(after_far)
     out_spaces = [space] * (len(outs) - near_outs) + [pltpu.VMEM] * near_outs
     return pl.pallas_call(
         body,
@@ -116,6 +129,7 @@
         in_specs=[pl.BlockSpec(memory_space=s) for s in spaces],
         out_specs=[pl.BlockSpec(memory_space=s) for s in out_spaces],
         scratch_shapes=scratch,
+        input_output_aliases=aliases or {},
         compiler_params=pltpu.CompilerParams(vmem_limit_bytes=grant * 2**20),
         cost_estimate=pl.CostEstimate(flops=flops, bytes_accessed=moved, transcendentals=0),
         name=name,
@@ -353,7 +367,7 @@
     finished(copies)
 
 
-def entering_by_pairs(keep, sent, width):
+def entering_by_pairs(keep, sent, width, after):
     pair_array, sent_array = array(keep.shape, F32), array(sent.shape, jnp.int16)
     got = swapped(sent, "ctx", 1)
     pair, sent = call(
@@ -361,11 +375,17 @@
         [pair_array, sent_array],
         (keep, got),
         near=True,
+        after=after[0],
         name="pair",
     )
     pair_got = swapped(sent, "ctx", 2)
     (sent,) = call(
-        functools.partial(four_body, width), [sent_array], (pair, pair_got), near=True, name="four"
+        functools.partial(four_body, width),
+        [sent_array],
+        (pair, pair_got),
+        near=True,
+        after=after[1],
+        name="four",
     )
     four_got = swapped(sent, "ctx", 4)
     mine, sent, ids = call(
@@ -373,6 +393,7 @@
         [array((STATE, keep.shape[1]), F32), sent_array, array((8, width), F32)],
         (keep, got, pair, pair_got, four_got),
         near=True,
+        after=after[2],
         name="turn",
     )
     return (mine, swapped(sent, "ctx", 1)), ids
@@ -395,11 +416,12 @@
 
 
 def mixing(
-    paired, seq_input, b_input, c_input, before, conv_x, conv_bc, log_decay, skip, gain, ids
+    after, seq_input, b_input, c_input, before, conv_x, conv_bc, log_decay, skip, gain, ids
 ):
     tokens, channels = seq_input.shape
     heads = skip.shape[0]
     width = 2 * ids.shape[0]
+    paired = after is not None
     outs = [
         array((tokens, channels), F32),
         array((tokens, 2 * STATE), F32),
@@ -417,16 +439,13 @@
         args,
         fixed=len(args) - 1,
         near_outs=len(ends),
+        after=after[0] if paired else (),
         scratch=room(args) + room(outs) + [pltpu.VMEM((8 + tokens, channels + 2 * STATE), F32)],
         sems=len(args),
         flops=10**9,
         grant=20,
         name="front",
     )
-    if paired:
-        starts, lines_of_ids = entering_by_pairs(*ends, width)
-    else:
-        starts, lines_of_ids = (entering_by_rows(ends[0]),), None
     args = (skip.reshape(1, heads), xconv, bc, lines)
     outs = [array((tokens, channels), F32)] * 2
     pre, decay = call(
@@ -440,21 +459,30 @@
         grant=16,
         name="inner",
     )
-    args = (gain.reshape(1, channels), pre, decay, bc)
-    outs = [array((tokens, channels), BF16)]
-    (mixed,) = call(
-        functools.partial(back_body, paired),
-        outs,
-        (*args, *starts),
-        fixed=1,
-        near_args=len(starts),
-        scratch=room(args) + room(outs),
-        sems=max(4, channels // (4 * HDIM)),
-        flops=10**9,
-        grant=16,
-        name="back",
-    )
-    return mixed, lines_of_ids
+    if paired:
+        first, second, third = after[1:]
+        starts, lines_of_ids = entering_by_pairs(*ends, width, (first, (*second, pre), third))
+    else:
+        starts, lines_of_ids = (entering_by_rows(ends[0]),), None
+
+    def finish(after=()):
+        args = (gain.reshape(1, channels), pre, decay, bc)
+        outs = [array((tokens, channels), BF16)]
+        return call(
+            functools.partial(back_body, paired),
+            outs,
+            (*args, *starts),
+            fixed=1,
+            near_args=len(starts),
+            after_far=after,
+            scratch=room(args) + room(outs),
+            sems=max(4, channels // (4 * HDIM)),
+            flops=10**9,
+            grant=16,
+            name="back",
+        )[0]
+
+    return finish, lines_of_ids
 
 
 TILE = 512
@@ -471,24 +499,24 @@
     return lax.ppermute(block, axis, [(i, i ^ bit) for i in range(lax.axis_size(axis))])
 
 
-def expert_body(pieces, w_gate, w_up, *refs):
-    far, ids_ref, out_far = refs[:pieces], refs[pieces], refs[pieces + 1]
-    pick_ref, hid_ref, out_ref, sems = refs[pieces + 2 :]
+def expert_body(part, w_gate, w_up, *refs):
+    far, ids_ref, out_far = refs[:8], refs[8], refs[9 + part]
+    pick_ref, hid_ref, out_ref, sems = refs[10 + part :]
     length, hidden = out_ref.shape
-    blocks = ids_ref.shape[0]
-    rows = length // blocks
+    rows = far[0].shape[0] // 2
     depth = far[0].shape[1]
     me = lax.axis_index("exp")
     here = lax.axis_index("ctx")
     downs = [pl.ds(pl.multiple_of((me ^ k) * depth, depth), depth) for k in range(4)]
+    pair = (here // 4) ^ part
 
     shape = (rows, rows)
     earlier = (iota(shape, 1) < iota(shape, 0)).astype(F32)
     across = iota(shape, 1)
     diagonal = iota(shape, 0) == across
-    turns = [here ^ (2 * (i % 4) + i // 4) for i in range(blocks)]
+    turns = [(here % 4) ^ (2 * (i % 2) + i // 2) for i in range(length // rows)]
     for i, block in enumerate(turns):
-        line = ids_ref[pl.ds(block, 1), :]
+        line = ids_ref[pl.ds(4 * pair + block, 1), :]
         mine = me.astype(F32)
         named = ((line[:, :rows] == mine) | (line[:, rows:] == mine)).astype(F32)
         column = jnp.sum(jnp.where(diagonal, named, 0.0), axis=1, keepdims=True)
@@ -496,11 +524,12 @@
         pick_ref[i] = jnp.where(position == across, column, 0.0).astype(BF16)
 
     out_copies = []
+    out_rows = pl.ds(pl.multiple_of(pair * length, length), length)
     for n in range(hidden // TILE):
         cut = slice(n * TILE, (n + 1) * TILE)
         gate = upper = None
         for k in range(4):
-            block = jnp.concatenate([piece[...] for piece in far[4 * k : 4 * k + 4]], axis=0)
+            block = jnp.concatenate([piece[...] for piece in far[2 * k : 2 * k + 2]], axis=0)
             more = dot16(block, w_gate[0, downs[k], cut])
             gate = more if k == 0 else gate + more
             more = dot16(block, w_up[0, downs[k], cut])
@@ -509,7 +538,7 @@
         for i, block in enumerate(turns):
             picked = dot16(pick_ref[i], hid_ref[i * rows : (i + 1) * rows], FIRST)
             out_ref[pl.ds(pl.multiple_of(block * rows, rows), rows), cut] = picked.astype(BF16)
-        out_copies += started([out_ref.at[:, cut]], [out_far.at[0, :, cut]], sems, n)
+        out_copies += started([out_ref.at[:, cut]], [out_far.at[0, out_rows, cut]], sems, n)
     finished(out_copies)
 
 
@@ -526,25 +555,31 @@
     return joined, swapped(joined, "ctx", 4)
 
 
-def experts_by_tokens(moe_input, ids, w_gate, w_up):
+def gathered(moe_input):
     z = along_z(moe_input)
     x = [swapped(a, "ctx", 1) for a in z]
     y = [swapped(a, "exp", 2) for a in z]
     d = (swapped(y[0], "ctx", 1), swapped(x[1], "exp", 2))
-    here = [*z, *x]
-    there = [*y, *d]
-    beside = [swapped(a, "exp", 1) for a in here]
-    corner = [swapped(a, "exp", 1) for a in there]
-    pieces = here + beside + there + corner
-    rows = moe_input.shape[0]
-    length = rows * lax.axis_size("ctx")
+    halves_of_rows = []
+    for pieces in zip(z, x, y, d):
+        beside = [swapped(a, "exp", 1) for a in pieces]
+        halves_of_rows.append([*pieces[:2], *beside[:2], *pieces[2:], *beside[2:]])
+    return halves_of_rows
+
+
+def experts_by_tokens(part, pieces, ids, w_gate, w_up, so_far, after):
+    rows = pieces[0].shape[0] // 2
+    length = 4 * rows
     hidden = w_gate.shape[2]
+    args = (w_gate, w_up, *pieces, ids)
     return call(
-        functools.partial(expert_body, len(pieces)),
-        [array((1, length, hidden), BF16)],
-        (w_gate, w_up, *pieces, ids),
+        functools.partial(expert_body, part),
+        [pltpu.HBM((1, 2 * length, hidden), BF16)],
+        args + ((so_far,) if part else ()),
         held=2,
-        near_args=len(pieces) + 1,
+        near_args=0,
+        aliases={len(args): 0} if part else None,
+        after_far=after,
         scratch=[
             pltpu.VMEM((length // rows, rows, rows), BF16),
             pltpu.VMEM((length, TILE), BF16),
@@ -553,6 +588,7 @@
         sems=hidden // TILE,
         flops=4 * length * w_gate.shape[1] * hidden,
         grant=16,
+        spaces_of=[pltpu.VMEM] * len(args) + [pltpu.HBM] * part,
         name="experts",
     )[0]
 
@@ -602,8 +638,13 @@
         name="ends",
     )[0]
     before = lax.ppermute(ends, "ctx", [(i, i + 1) for i in range(ctx - 1)])
-    mixed, ids = mixing(
-        by_tokens,
+    follow = None
+    if by_tokens:
+        one, two = gathered(moe_input)
+        follow = (one[:1], (one[1], one[4], one[2]), two[:1])
+        follow += ((two[1], two[4], two[2], one[5], one[3], one[6]),)
+    finish, ids = mixing(
+        follow,
         seq_input,
         b_input,
         c_input,
@@ -616,8 +657,11 @@
         expert_ids,
     )
     if by_tokens:
-        hidden = experts_by_tokens(moe_input, ids, w_gate, w_up)
+        hidden = experts_by_tokens(0, one, ids, w_gate, w_up, None, ())
+        mixed = finish((hidden,))
+        hidden = experts_by_tokens(1, two, ids, w_gate, w_up, hidden, (mixed,))
     else:
+        mixed = finish()
         hidden = experts_by_slots(moe_input, expert_ids, w_gate, w_up)
     return (mixed, hidden)
 

time: 70.7 us -> 68 us (0.962)
  starting transfers between devices: 27.2 us -> 20 us
  waiting for transfers between devices: 17.7 us -> 21.3 us
  Pallas kernels: 24.2 us -> 25.4 us
    ppermute x20, starting transfers between devices: 22.4 us -> 16.7 us  [swapped(): lax.ppermute(block, axis, [(i, i ^ bit) for i in range(lax.axis_size(axis...]
    ppermute x20, waiting for transfers between devices: 17.7 us -> 21.3 us  [swapped(): lax.ppermute(block, axis, [(i, i ^ bit) for i in range(lax.axis_size(axis...]
    ppermute x1, starting transfers between devices: 4.84 us -> 3.4 us  [on_device(): before = lax.ppermute(ends, 'ctx', [(i, i + 1) for i in range(ctx - 1)])]
    pallas_call x9 -> x10, Pallas kernels: 24.2 us -> 25.4 us  [call(): pl.pallas_call(body, out_shape=outs, in_specs=[pl.BlockSpec(memory_space=...]
  transfers between devices with their start and end apart: 21 -> 21, of which waited for: 7 -> 5; matrix products, arithmetic and copies ran while one was open for 0% -> 0% of each run, Pallas kernels for 19% -> 29%
where the time goes in v7:
time: 68 us; the launch traced here: 67.8 us
  Pallas kernels  25.4 us (37%)
  waiting for transfers between devices  21.3 us (31%)
  starting transfers between devices  20 us (29%)
  between operations  1 us (1%)
    pallas_call x10, Pallas kernels, call(): pl.pallas_call(body, out_shape=outs, in_specs=[pl.BlockSpec(memory_space=...  25.4 us
    ppermute x20, waiting for transfers between devices, swapped(): lax.ppermute(block, axis, [(i, i ^ bit) for i in range(lax.axis_size(axis...  21.3 us
    ppermute x20, starting transfers between devices, swapped(): lax.ppermute(block, axis, [(i, i ^ bit) for i in range(lax.axis_size(axis...  16.7 us
    ppermute x1, starting transfers between devices, on_device(): before = lax.ppermute(ends, 'ctx', [(i, i + 1) for i in range(ctx - 1)])  3.4 us
  transfers between devices with their start and end apart: 21, of which 5 were waited for; matrix products, arithmetic and copies ran while one was open for 0% of the time, Pallas kernels for 29%

profile of v7, /device:TPU:0, one launch (start us, length us, event | category | flops | bytes accessed | tf_op | source)
XLA Modules:
  0.0 67.8 jit_solution(12134103858629171949)
XLA Ops:
  0.6 3.1 %collective-permute-start.1 = (bf16[64,1024]{1,0:T(8,128)(2,1)}, bf16[64,1024]{1,0:T(8,128)(2,1)S(1)}, u32[]{:S(2)}, u32[]{:S(2)}) collective-permute-start(bf16[64,1024]{1,0:T(8,128)(2,1)} %refs_0_.6), channel_id=1, source_target_pairs={{0,8},{4,12},{8,0},{12,4},{16,24},{20,28},{24,16},{28,20},{1,9},{5... | collective-permute-start | bytes 393224 | tf_op jit(solution)/shard_map/ppermute | solution.py:499
  3.7 0.8 %ends.1 = bf16[16,1280]{1,0:T(8,128)(2,1)S(1)} custom-call(bf16[256,1024]{1,0:T(8,128)(2,1)} %refs_0_.7, bf16[256,128]{1,0:T(8,128)(2,1)} %refs_1_.5, bf16[256,128]{1,0:T(8,128)(2,1)} %refs_2_.3), custom_call_target="tpu_custom_call" | custom-call | bytes 696320 | tf_op jit(solution)/shard_map/ends/pallas_call | solution.py:126
  4.5 3.4 %collective-permute-start = (bf16[16,1280]{1,0:T(8,128)(2,1)S(1)}, bf16[16,1280]{1,0:T(8,128)(2,1)S(1)}, u32[]{:S(2)}, u32[]{:S(2)}) collective-permute-start(bf16[16,1280]{1,0:T(8,128)(2,1)S(1)} %ends.1), channel_id=1, source_target_pairs={{0,4},{4,8},{8,12},{12,16},{16,20},{20,24},{24,28},{1,5},{5,9},{9,... | collective-permute-start | bytes 122888 | tf_op jit(solution)/shard_map/ppermute | solution.py:640
  7.9 0.0 collective-permute-done.1.refs_1_
  7.9 0.9 %join.1.refs_8_.refs_2_ = bf16[128,1024]{1,0:T(8,128)(2,1)S(1)} custom-call(bf16[64,1024]{1,0:T(8,128)(2,1)} %refs_0_.6, bf16[64,1024]{1,0:T(8,128)(2,1)S(1)} %collective-permute-done.1.refs_1_), custom_call_target="tpu_custom_call" | custom-call | bytes 524288 | tf_op jit(solution)/shard_map/join/pallas_call | solution.py:126
  8.9 2.7 %collective-permute-start.7 = (bf16[128,1024]{1,0:T(8,128)(2,1)S(1)}, bf16[128,1024]{1,0:T(8,128)(2,1)S(1)}, u32[]{:S(2)}, u32[]{:S(2)}) collective-permute-start(bf16[128,1024]{1,0:T(8,128)(2,1)S(1)} %join.1.refs_8_.refs_2_), channel_id=1, source_target_pairs={{0,16},{4,20},{8,24},{12,28},{16,0},{20,4},{24,8},{28,12},{1,17},{... | collective-permute-start | bytes 786440 | tf_op jit(solution)/shard_map/ppermute | solution.py:499
  11.5 1.5 %collective-permute-start.4 = (bf16[128,1024]{1,0:T(8,128)(2,1)S(1)}, bf16[128,1024]{1,0:T(8,128)(2,1)S(1)}, u32[]{:S(2)}, u32[]{:S(2)}) collective-permute-start(bf16[128,1024]{1,0:T(8,128)(2,1)S(1)} %join.1.refs_8_.refs_2_), channel_id=1, source_target_pairs={{0,2},{1,3},{2,0},{3,1},{4,6},{5,7},{6,4},{7,5},{8,10},{9,11},{10,... | collective-permute-start | bytes 786440 | tf_op jit(solution)/shard_map/ppermute | solution.py:499
  13.0 1.1 %collective-permute-start.3 = (bf16[128,1024]{1,0:T(8,128)(2,1)S(1)}, bf16[128,1024]{1,0:T(8,128)(2,1)S(1)}, u32[]{:S(2)}, u32[]{:S(2)}) collective-permute-start(bf16[128,1024]{1,0:T(8,128)(2,1)S(1)} %join.1.refs_8_.refs_2_), channel_id=1, source_target_pairs={{0,4},{4,0},{8,12},{12,8},{16,20},{20,16},{24,28},{28,24},{1,5},{5... | collective-permute-start | bytes 786440 | tf_op jit(solution)/shard_map/ppermute | solution.py:499
  14.2 4.4 %front.1 = (f32[256,1024]{1,0:T(8,128)S(1)}, f32[256,256]{1,0:T(8,128)S(1)}, f32[2,16,256]{2,1,0:T(8,128)S(1)}, f32[136,512]{1,0:T(8,128)S(1)}, s16[144,512]{1,0:T(8,128)(2,1)S(1)}) custom-call(bf16[256,1024]{1,0:T(8,128)(2,1)} %refs_0_.7, bf16[256,128]{1,0:T(8,128)(2,1)} %refs_1_.5, bf16[256,128]{1,0:T(8,128)(2,1)} %refs_2_.3, f32[4,1024]{1,0:T(4,128)} %refs_3_.1, ...), custom_call_target="tpu_custom_call" | custom-call | flops 1000000000 | bytes 2503168 | tf_op jit(solution)/shard_map/front/pallas_call | solution.py:126
  18.6 0.9 %collective-permute-start.2 = (s16[144,512]{1,0:T(8,128)(2,1)S(1)}, s16[144,512]{1,0:T(8,128)(2,1)S(1)}, u32[]{:S(2)}, u32[]{:S(2)}) collective-permute-start(s16[144,512]{1,0:T(8,128)(2,1)S(1)} %get-tuple-element.20), channel_id=1, source_target_pairs={{0,4},{4,0},{8,12},{12,8},{16,20},{20,16},{24,28},{28,24},{1,5},{5... | collective-permute-start | bytes 442376 | tf_op jit(solution)/shard_map/ppermute | solution.py:499
  19.6 3.3 %collective-permute-done.7.refs_2_ = bf16[128,1024]{1,0:T(8,128)(2,1)S(1)} collective-permute-done((bf16[128,1024]{1,0:T(8,128)(2,1)S(1)}, bf16[128,1024]{1,0:T(8,128)(2,1)S(1)}, u32[]{:S(2)}, u32[]{:S(2)}) %collective-permute-start.7) | collective-permute-done | bytes 262176 | tf_op jit(solution)/shard_map/ppermute | solution.py:499
  22.9 0.8 %collective-permute-start.9 = (bf16[128,1024]{1,0:T(8,128)(2,1)S(1)}, bf16[128,1024]{1,0:T(8,128)(2,1)S(1)}, u32[]{:S(2)}, u32[]{:S(2)}) collective-permute-start(bf16[128,1024]{1,0:T(8,128)(2,1)S(1)} %collective-permute-done.7.refs_2_), channel_id=1, source_target_pairs={{0,4},{4,0},{8,12},{12,8},{16,20},{20,16},{24,28},{28,24},{1,5},{5... | collective-permute-start | bytes 786440 | tf_op jit(solution)/shard_map/ppermute | solution.py:499
  23.8 1.2 %collective-permute-start.12 = (bf16[128,1024]{1,0:T(8,128)(2,1)S(1)}, bf16[128,1024]{1,0:T(8,128)(2,1)S(1)}, u32[]{:S(2)}, u32[]{:S(2)}) collective-permute-start(bf16[128,1024]{1,0:T(8,128)(2,1)S(1)} %collective-permute-done.4.refs_3_.refs_6_), channel_id=1, source_target_pairs={{0,4},{4,0},{8,12},{12,8},{16,20},{20,16},{24,28},{28,24},{1,5},{5... | collective-permute-start | bytes 786440 | tf_op jit(solution)/shard_map/ppermute | solution.py:499
  25.0 1.5 %collective-permute-start.10 = (bf16[128,1024]{1,0:T(8,128)(2,1)S(1)}, bf16[128,1024]{1,0:T(8,128)(2,1)S(1)}, u32[]{:S(2)}, u32[]{:S(2)}) collective-permute-start(bf16[128,1024]{1,0:T(8,128)(2,1)S(1)} %collective-permute-done.7.refs_2_), channel_id=1, source_target_pairs={{0,2},{1,3},{2,0},{3,1},{4,6},{5,7},{6,4},{7,5},{8,10},{9,11},{10,... | collective-permute-start | bytes 786440 | tf_op jit(solution)/shard_map/ppermute | solution.py:499
  26.5 0.1 pair.1
  26.6 1.0 %collective-permute-start.6 = (s16[144,512]{1,0:T(8,128)(2,1)S(1)}, s16[144,512]{1,0:T(8,128)(2,1)S(1)}, u32[]{:S(2)}, u32[]{:S(2)}) collective-permute-start(s16[144,512]{1,0:T(8,128)(2,1)S(1)} %get-tuple-element.22), channel_id=1, source_target_pairs={{0,8},{4,12},{8,0},{12,4},{16,24},{20,28},{24,16},{28,20},{1,9},{5... | collective-permute-start | bytes 442376 | tf_op jit(solution)/shard_map/ppermute | solution.py:499
  27.7 4.2 %collective-permute-done.6.refs_1_.refs_3_ = s16[144,512]{1,0:T(8,128)(2,1)S(1)} collective-permute-done((s16[144,512]{1,0:T(8,128)(2,1)S(1)}, s16[144,512]{1,0:T(8,128)(2,1)S(1)}, u32[]{:S(2)}, u32[]{:S(2)}) %collective-permute-start.6) | collective-permute-done | bytes 147488 | tf_op jit(solution)/shard_map/ppermute | solution.py:499
  31.9 0.3 collective-permute-done.9.refs_5_.refs_3_
  32.2 0.2 collective-permute-start.14
  32.4 4.0 %collective-permute-done.12.refs_8_.refs_7_ = bf16[128,1024]{1,0:T(8,128)(2,1)S(1)} collective-permute-done((bf16[128,1024]{1,0:T(8,128)(2,1)S(1)}, bf16[128,1024]{1,0:T(8,128)(2,1)S(1)}, u32[]{:S(2)}, u32[]{:S(2)}) %collective-permute-start.12) | collective-permute-done | bytes 262176 | tf_op jit(solution)/shard_map/ppermute | solution.py:499
  36.4 1.5 %collective-permute-start.18 = (bf16[128,1024]{1,0:T(8,128)(2,1)S(1)}, bf16[128,1024]{1,0:T(8,128)(2,1)S(1)}, u32[]{:S(2)}, u32[]{:S(2)}) collective-permute-start(bf16[128,1024]{1,0:T(8,128)(2,1)S(1)} %collective-permute-done.9.refs_5_.refs_3_), channel_id=1, source_target_pairs={{0,2},{1,3},{2,0},{3,1},{4,6},{5,7},{6,4},{7,5},{8,10},{9,11},{10,... | collective-permute-start | bytes 786440 | tf_op jit(solution)/shard_map/ppermute | solution.py:499
  37.9 4.2 %inner.1 = (f32[256,1024]{1,0:T(8,128)S(1)}, f32[256,1024]{1,0:T(8,128)S(1)}) custom-call(f32[1,16]{1,0:T(1,128)} %bitcast.9, f32[256,1024]{1,0:T(8,128)S(1)} %get-tuple-element.14.refs_1_, f32[256,256]{1,0:T(8,128)S(1)} %get-tuple-element.15.refs_2_.refs_3_, f32[2,16,256]{2,1,0:T(8,128)S(1)} %get-tuple-element.16.refs_3_), custom_call_target="tpu_custom_call" | custom-call | flops 4000000000 | bytes 3440704 | tf_op jit(solution)/shard_map/inner/pallas_call | solution.py:126
  42.1 0.1 four.1
  42.3 0.1 collective-permute-start.8
  42.4 0.3 collective-permute-start.17
  42.7 0.3 collective-permute-start.19
  42.9 9.4 %collective-permute-done.8.refs_4_ = s16[144,512]{1,0:T(8,128)(2,1)S(1)} collective-permute-done((s16[144,512]{1,0:T(8,128)(2,1)S(1)}, s16[144,512]{1,0:T(8,128)(2,1)S(1)}, u32[]{:S(2)}, u32[]{:S(2)}) %collective-permute-start.8) | collective-permute-done | bytes 147488 | tf_op jit(solution)/shard_map/ppermute | solution.py:499
  52.4 0.2 turn.1
  52.6 0.4 collective-permute-start.15
  53.0 5.7 %experts.2.refs_6_.refs_11_ = bf16[1,512,1024]{2,1,0:T(8,128)(2,1)} custom-call(bf16[1,4096,1024]{2,1,0:T(8,128)(2,1)S(1)} %bitcast.4, bf16[1,4096,1024]{2,1,0:T(8,128)(2,1)S(1)} %bitcast.6, bf16[128,1024]{1,0:T(8,128)(2,1)S(1)} %join.1.refs_8_.refs_2_, bf16[128,1024]{1,0:T(8,128)(2,1)S(1)} %collective-permute-done.3.refs_2_.refs_3_, ...), custom_call_target="tpu_custom_call" | custom-call | flops 4294967296 | bytes 19927040 | tf_op jit(solution)/shard_map/experts/pallas_call | solution.py:126
  58.7 3.1 %back.1.refs_12_ = bf16[256,1024]{1,0:T(8,128)(2,1)} custom-call(f32[1,1024]{1,0:T(1,128)} %bitcast.7, f32[256,1024]{1,0:T(8,128)S(1)} %get-tuple-element.17.refs_3_.refs_1_, f32[256,1024]{1,0:T(8,128)S(1)} %get-tuple-element.18.refs_2_, f32[256,256]{1,0:T(8,128)S(1)} %get-tuple-element.15.refs_2_.refs_3_, f32[128,512]{1,0:T(8,128)S(1)} %get-tuple-element.23.refs_4_, ...), custom_call_target="tpu_custom_call" | custom-call | flops 1000000000 | bytes 3297280 | tf_op jit(solution)/shard_map/back/pallas_call | solution.py:126
  61.9 5.7 %experts.3 = bf16[1,512,1024]{2,1,0:T(8,128)(2,1)} custom-call(bf16[1,4096,1024]{2,1,0:T(8,128)(2,1)S(1)} %bitcast.4, bf16[1,4096,1024]{2,1,0:T(8,128)(2,1)S(1)} %bitcast.6, bf16[128,1024]{1,0:T(8,128)(2,1)S(1)} %collective-permute-done.7.refs_2_, bf16[128,1024]{1,0:T(8,128)(2,1)S(1)} %collective-permute-done.9.refs_5_.refs_3_, ...), custom_call_target="tpu_custom_call", output_to_operand_aliasing={{}: (11, {})} | custom-call | flops 4294967296 | bytes 20975616 | tf_op jit(solution)/shard_map/experts/pallas_call | solution.py:126
  (30 shorter events, 0.1 us)
Async XLA Ops:
  0.6 7.3 %collective-permute-start.1 = (bf16[64,1024]{1,0:T(8,128)(2,1)}, bf16[64,1024]{1,0:T(8,128)(2,1)S(1)}, u32[]{:S(2)}, u32[]{:S(2)}) collective-permute-start(bf16[64,1024]{1,0:T(8,128)(2,1)} %refs_0_.6), channel_id=1, source_target_pairs={{0,8},{4,12},{8,0},{12,4},{16,24},{20,28},{24,16},{28,20},{1,9},{5... | collective-permute-start | bytes 393224 | tf_op jit(solution)/shard_map/ppermute | solution.py:499
  4.5 9.7 %collective-permute-start = (bf16[16,1280]{1,0:T(8,128)(2,1)S(1)}, bf16[16,1280]{1,0:T(8,128)(2,1)S(1)}, u32[]{:S(2)}, u32[]{:S(2)}) collective-permute-start(bf16[16,1280]{1,0:T(8,128)(2,1)S(1)} %ends.1), channel_id=1, source_target_pairs={{0,4},{4,8},{8,12},{12,16},{16,20},{20,24},{24,28},{1,5},{5,9},{9,... | collective-permute-start | bytes 122888 | tf_op jit(solution)/shard_map/ppermute | solution.py:640
  8.9 14.1 %collective-permute-start.7 = (bf16[128,1024]{1,0:T(8,128)(2,1)S(1)}, bf16[128,1024]{1,0:T(8,128)(2,1)S(1)}, u32[]{:S(2)}, u32[]{:S(2)}) collective-permute-start(bf16[128,1024]{1,0:T(8,128)(2,1)S(1)} %join.1.refs_8_.refs_2_), channel_id=1, source_target_pairs={{0,16},{4,20},{8,24},{12,28},{16,0},{20,4},{24,8},{28,12},{1,17},{... | collective-permute-start | bytes 786440 | tf_op jit(solution)/shard_map/ppermute | solution.py:499
  11.5 12.3 %collective-permute-start.4 = (bf16[128,1024]{1,0:T(8,128)(2,1)S(1)}, bf16[128,1024]{1,0:T(8,128)(2,1)S(1)}, u32[]{:S(2)}, u32[]{:S(2)}) collective-permute-start(bf16[128,1024]{1,0:T(8,128)(2,1)S(1)} %join.1.refs_8_.refs_2_), channel_id=1, source_target_pairs={{0,2},{1,3},{2,0},{3,1},{4,6},{5,7},{6,4},{7,5},{8,10},{9,11},{10,... | collective-permute-start | bytes 786440 | tf_op jit(solution)/shard_map/ppermute | solution.py:499
  13.0 13.4 %collective-permute-start.3 = (bf16[128,1024]{1,0:T(8,128)(2,1)S(1)}, bf16[128,1024]{1,0:T(8,128)(2,1)S(1)}, u32[]{:S(2)}, u32[]{:S(2)}) collective-permute-start(bf16[128,1024]{1,0:T(8,128)(2,1)S(1)} %join.1.refs_8_.refs_2_), channel_id=1, source_target_pairs={{0,4},{4,0},{8,12},{12,8},{16,20},{20,16},{24,28},{28,24},{1,5},{5... | collective-permute-start | bytes 786440 | tf_op jit(solution)/shard_map/ppermute | solution.py:499
  14.2 12.3 %collective-permute-start.5 = (bf16[128,1024]{1,0:T(8,128)(2,1)S(1)}, bf16[128,1024]{1,0:T(8,128)(2,1)S(1)}, u32[]{:S(2)}, u32[]{:S(2)}) collective-permute-start(bf16[128,1024]{1,0:T(8,128)(2,1)S(1)} %join.1.refs_8_.refs_2_), channel_id=1, source_target_pairs={{0,1},{1,0},{2,3},{3,2},{4,5},{5,4},{6,7},{7,6},{8,9},{9,8},{10,11... | collective-permute-start | bytes 786440 | tf_op jit(solution)/shard_map/ppermute | solution.py:499
  14.2 38.8 %slice-start.2 = ((s8[8388608]{0:T(1024)(128)(4,1)}), s8[4194304]{0:T(1024)(128)(4,1)S(1)}, s32[]{:S(2)}) async-start(s8[8388608]{0:T(1024)(128)(4,1)} %bitcast.5), calls=%async_computation.2 | async-start | bytes 8388608
  18.6 6.3 %collective-permute-start.2 = (s16[144,512]{1,0:T(8,128)(2,1)S(1)}, s16[144,512]{1,0:T(8,128)(2,1)S(1)}, u32[]{:S(2)}, u32[]{:S(2)}) collective-permute-start(s16[144,512]{1,0:T(8,128)(2,1)S(1)} %get-tuple-element.20), channel_id=1, source_target_pairs={{0,4},{4,0},{8,12},{12,8},{16,20},{20,16},{24,28},{28,24},{1,5},{5... | collective-permute-start | bytes 442376 | tf_op jit(solution)/shard_map/ppermute | solution.py:499
  22.9 9.2 %collective-permute-start.9 = (bf16[128,1024]{1,0:T(8,128)(2,1)S(1)}, bf16[128,1024]{1,0:T(8,128)(2,1)S(1)}, u32[]{:S(2)}, u32[]{:S(2)}) collective-permute-start(bf16[128,1024]{1,0:T(8,128)(2,1)S(1)} %collective-permute-done.7.refs_2_), channel_id=1, source_target_pairs={{0,4},{4,0},{8,12},{12,8},{16,20},{20,16},{24,28},{28,24},{1,5},{5... | collective-permute-start | bytes 786440 | tf_op jit(solution)/shard_map/ppermute | solution.py:499
  23.8 12.6 %collective-permute-start.12 = (bf16[128,1024]{1,0:T(8,128)(2,1)S(1)}, bf16[128,1024]{1,0:T(8,128)(2,1)S(1)}, u32[]{:S(2)}, u32[]{:S(2)}) collective-permute-start(bf16[128,1024]{1,0:T(8,128)(2,1)S(1)} %collective-permute-done.4.refs_3_.refs_6_), channel_id=1, source_target_pairs={{0,4},{4,0},{8,12},{12,8},{16,20},{20,16},{24,28},{28,24},{1,5},{5... | collective-permute-start | bytes 786440 | tf_op jit(solution)/shard_map/ppermute | solution.py:499
  25.0 11.4 %collective-permute-start.10 = (bf16[128,1024]{1,0:T(8,128)(2,1)S(1)}, bf16[128,1024]{1,0:T(8,128)(2,1)S(1)}, u32[]{:S(2)}, u32[]{:S(2)}) collective-permute-start(bf16[128,1024]{1,0:T(8,128)(2,1)S(1)} %collective-permute-done.7.refs_2_), channel_id=1, source_target_pairs={{0,2},{1,3},{2,0},{3,1},{4,6},{5,7},{6,4},{7,5},{8,10},{9,11},{10,... | collective-permute-start | bytes 786440 | tf_op jit(solution)/shard_map/ppermute | solution.py:499
  26.6 5.2 %collective-permute-start.6 = (s16[144,512]{1,0:T(8,128)(2,1)S(1)}, s16[144,512]{1,0:T(8,128)(2,1)S(1)}, u32[]{:S(2)}, u32[]{:S(2)}) collective-permute-start(s16[144,512]{1,0:T(8,128)(2,1)S(1)} %get-tuple-element.22), channel_id=1, source_target_pairs={{0,8},{4,12},{8,0},{12,4},{16,24},{20,28},{24,16},{28,20},{1,9},{5... | collective-permute-start | bytes 442376 | tf_op jit(solution)/shard_map/ppermute | solution.py:499
  27.7 14.6 %collective-permute-start.11 = (bf16[128,1024]{1,0:T(8,128)(2,1)S(1)}, bf16[128,1024]{1,0:T(8,128)(2,1)S(1)}, u32[]{:S(2)}, u32[]{:S(2)}) collective-permute-start(bf16[128,1024]{1,0:T(8,128)(2,1)S(1)} %collective-permute-done.7.refs_2_), channel_id=1, source_target_pairs={{0,1},{1,0},{2,3},{3,2},{4,5},{5,4},{6,7},{7,6},{8,9},{9,8},{10,11... | collective-permute-start | bytes 786440 | tf_op jit(solution)/shard_map/ppermute | solution.py:499
  31.8 10.5 %collective-permute-start.13 = (bf16[128,1024]{1,0:T(8,128)(2,1)S(1)}, bf16[128,1024]{1,0:T(8,128)(2,1)S(1)}, u32[]{:S(2)}, u32[]{:S(2)}) collective-permute-start(bf16[128,1024]{1,0:T(8,128)(2,1)S(1)} %collective-permute-done.3.refs_2_.refs_3_), channel_id=1, source_target_pairs={{0,1},{1,0},{2,3},{3,2},{4,5},{5,4},{6,7},{7,6},{8,9},{9,8},{10,11... | collective-permute-start | bytes 786440 | tf_op jit(solution)/shard_map/ppermute | solution.py:499
  32.2 10.5 %collective-permute-start.14 = (bf16[128,1024]{1,0:T(8,128)(2,1)S(1)}, bf16[128,1024]{1,0:T(8,128)(2,1)S(1)}, u32[]{:S(2)}, u32[]{:S(2)}) collective-permute-start(bf16[128,1024]{1,0:T(8,128)(2,1)S(1)} %collective-permute-done.4.refs_3_.refs_6_), channel_id=1, source_target_pairs={{0,1},{1,0},{2,3},{3,2},{4,5},{5,4},{6,7},{7,6},{8,9},{9,8},{10,11... | collective-permute-start | bytes 786440 | tf_op jit(solution)/shard_map/ppermute | solution.py:499
  36.3 16.6 %collective-permute-start.16 = (bf16[128,1024]{1,0:T(8,128)(2,1)S(1)}, bf16[128,1024]{1,0:T(8,128)(2,1)S(1)}, u32[]{:S(2)}, u32[]{:S(2)}) collective-permute-start(bf16[128,1024]{1,0:T(8,128)(2,1)S(1)} %collective-permute-done.12.refs_8_.refs_7_), channel_id=1, source_target_pairs={{0,1},{1,0},{2,3},{3,2},{4,5},{5,4},{6,7},{7,6},{8,9},{9,8},{10,11... | collective-permute-start | bytes 786440 | tf_op jit(solution)/shard_map/ppermute | solution.py:499
  36.4 16.6 %collective-permute-start.18 = (bf16[128,1024]{1,0:T(8,128)(2,1)S(1)}, bf16[128,1024]{1,0:T(8,128)(2,1)S(1)}, u32[]{:S(2)}, u32[]{:S(2)}) collective-permute-start(bf16[128,1024]{1,0:T(8,128)(2,1)S(1)} %collective-permute-done.9.refs_5_.refs_3_), channel_id=1, source_target_pairs={{0,2},{1,3},{2,0},{3,1},{4,6},{5,7},{6,4},{7,5},{8,10},{9,11},{10,... | collective-permute-start | bytes 786440 | tf_op jit(solution)/shard_map/ppermute | solution.py:499
  37.9 15.1 %slice-start = ((s8[8388608]{0:T(1024)(128)(4,1)}), s8[4194304]{0:T(1024)(128)(4,1)S(1)}, s32[]{:S(2)}) async-start(s8[8388608]{0:T(1024)(128)(4,1)} %bitcast.3), calls=%async_computation | async-start | bytes 8388608
  37.9 15.1 %slice-start.1 = ((s8[8388608]{0:T(1024)(128)(4,1)}), s8[4194304]{0:T(1024)(128)(4,1)S(1)}, s32[]{:S(2)}) async-start(s8[8388608]{0:T(1024)(128)(4,1)} %bitcast.3), calls=%async_computation.1 | async-start | bytes 8388608
  37.9 15.1 %slice-start.3 = ((s8[8388608]{0:T(1024)(128)(4,1)}), s8[4194304]{0:T(1024)(128)(4,1)S(1)}, s32[]{:S(2)}) async-start(s8[8388608]{0:T(1024)(128)(4,1)} %bitcast.5), calls=%async_computation.3 | async-start | bytes 8388608
  42.3 10.1 %collective-permute-start.8 = (s16[144,512]{1,0:T(8,128)(2,1)S(1)}, s16[144,512]{1,0:T(8,128)(2,1)S(1)}, u32[]{:S(2)}, u32[]{:S(2)}) collective-permute-start(s16[144,512]{1,0:T(8,128)(2,1)S(1)} %four.1), channel_id=1, source_target_pairs={{0,16},{4,20},{8,24},{12,28},{16,0},{20,4},{24,8},{28,12},{1,17},{... | collective-permute-start | bytes 442376 | tf_op jit(solution)/shard_map/ppermute | solution.py:499
  42.4 19.5 %collective-permute-start.17 = (bf16[128,1024]{1,0:T(8,128)(2,1)S(1)}, bf16[128,1024]{1,0:T(8,128)(2,1)S(1)}, u32[]{:S(2)}, u32[]{:S(2)}) collective-permute-start(bf16[128,1024]{1,0:T(8,128)(2,1)S(1)} %collective-permute-done.9.refs_5_.refs_3_), channel_id=1, source_target_pairs={{0,1},{1,0},{2,3},{3,2},{4,5},{5,4},{6,7},{7,6},{8,9},{9,8},{10,11... | collective-permute-start | bytes 786440 | tf_op jit(solution)/shard_map/ppermute | solution.py:499
  42.7 19.2 %collective-permute-start.19 = (bf16[128,1024]{1,0:T(8,128)(2,1)S(1)}, bf16[128,1024]{1,0:T(8,128)(2,1)S(1)}, u32[]{:S(2)}, u32[]{:S(2)}) collective-permute-start(bf16[128,1024]{1,0:T(8,128)(2,1)S(1)} %collective-permute-done.10.refs_6_), channel_id=1, source_target_pairs={{0,1},{1,0},{2,3},{3,2},{4,5},{5,4},{6,7},{7,6},{8,9},{9,8},{10,11... | collective-permute-start | bytes 786440 | tf_op jit(solution)/shard_map/ppermute | solution.py:499
  52.6 6.1 %collective-permute-start.15 = (s16[144,512]{1,0:T(8,128)(2,1)S(1)}, s16[144,512]{1,0:T(8,128)(2,1)S(1)}, u32[]{:S(2)}, u32[]{:S(2)}) collective-permute-start(s16[144,512]{1,0:T(8,128)(2,1)S(1)} %get-tuple-element.24), channel_id=1, source_target_pairs={{0,4},{4,0},{8,12},{12,8},{16,20},{20,16},{24,28},{28,24},{1,5},{5... | collective-permute-start | bytes 442376 | tf_op jit(solution)/shard_map/ppermute | solution.py:499
  53.0 8.9 %collective-permute-start.20 = (bf16[128,1024]{1,0:T(8,128)(2,1)S(1)}, bf16[128,1024]{1,0:T(8,128)(2,1)S(1)}, u32[]{:S(2)}, u32[]{:S(2)}) collective-permute-start(bf16[128,1024]{1,0:T(8,128)(2,1)S(1)} %collective-permute-done.18.refs_7_), channel_id=1, source_target_pairs={{0,1},{1,0},{2,3},{3,2},{4,5},{5,4},{6,7},{7,6},{8,9},{9,8},{10,11... | collective-permute-start | bytes 786440 | tf_op jit(solution)/shard_map/ppermute | solution.py:499

commit v8 on v7

--- a/solution.py
+++ b/solution.py
@@ -160,14 +160,14 @@
     )
 
 
-def front_body(paired, count, *refs):
+def local_body(paired, count, *refs):
     far, outs, rest = refs[:count], refs[count : count + 3], refs[count + 3 :]
     ends = rest[: 1 + paired]
     rest = rest[1 + paired :]
     near, scratch, pad_ref, sems = rest[:count], rest[count : count + 3], rest[-2], rest[-1]
     copies = started(far, near, sems)
-    x_ref, b_ref, c_ref, taps_ref, taps_bc_ref, logs_ref, ids_ref, ends_ref = near
-    xconv_ref, bc_ref, lines_ref = scratch
+    x_ref, b_ref, c_ref, taps_ref, taps_bc_ref, logs_ref, skip_ref, ids_ref, ends_ref = near
+    pre_ref, decay_ref, c_out_ref = scratch
     tokens, channels = x_ref.shape
     heads = logs_ref.shape[0]
     finished(copies)
@@ -184,19 +184,23 @@
         return silu(total)
 
     bc = conv(taps_bc_ref[...], channels, channels + 2 * STATE)
-    bc_ref[...] = bc
-    xconv = conv(taps_ref[...], 0, channels)
-    xconv_ref[...] = xconv
+    bmat, cmat = bc[:, :STATE], bc[:, STATE:]
+    c_out_ref[...] = cmat
     logs = logs_ref[...]
     inflow = jnp.sqrt(one_minus_exp(2.0 * logs))
     row = dot_exact(logs, upper_ones(tokens))
-    lines_ref[0] = row
-    lines_ref[1] = inflow
-    copies = started(scratch, outs, sems)
+    column = row.T
     total = row[:, tokens - 1 :]
     spread = head_spread(heads)
-    fresh = xconv * dot_left(inflow * jnp.exp(total - row), spread, FIRST)
-    state = dot(bc[:, :STATE], fresh, FIRST)
+    decay_ref[...] = dot_left(jnp.exp(row), spread, FIRST)
+    copies = started(scratch[1:], outs[1:], sems)
+
+    xconv = conv(taps_ref[...], 0, channels)
+    pad_ref[:tokens, :channels] = xconv
+    drive = xconv * dot_left(inflow, spread, FIRST)
+    pre_ref[...] = drive
+    fresh = drive * dot_left(jnp.exp(total - row), spread, FIRST)
+    state = dot(bmat, fresh, FIRST)
     total = jnp.broadcast_to(total, (heads, NOTES))
     if paired:
         total = dot_exact(total, spread, FIRST)
@@ -215,7 +219,23 @@
     else:
         ends[0][:STATE] = state
         ends[0][STATE:] = dot_exact(jnp.exp(total), spread, FIRST)
-    finished(copies)
+
+    skip = dot_exact(skip_ref[...], spread)
+    meet = dot(cmat, bmat, ((1,), (1,)))
+    lower = iota((tokens, tokens), 0) >= iota((tokens, tokens), 1)
+    left = iota((tokens, 2 * HDIM), 1) < HDIM
+    for pair in range(heads // 2):
+        cut = slice(pair * 2 * HDIM, (pair + 1) * 2 * HDIM)
+        d_high, d_low = halves(pre_ref[:, cut])
+        both = []
+        for h in (2 * pair, 2 * pair + 1):
+            gap = column[:, h : h + 1] - row[h : h + 1, :]
+            mix = jnp.where(lower, jnp.exp(gap), 0.0) * meet
+            m_high, m_low = halves(mix)
+            both.append(dot16(m_high, d_high) + dot16(m_high, d_low) + dot16(m_low, d_high))
+        direct = skip[:, cut] * pad_ref[:tokens, cut]
+        pre_ref[:, cut] = direct + jnp.where(left, both[0], both[1])
+    finished(copies + started(scratch[:1], outs[:1], sems, 2))
 
 
 def put(ref, state, logsum, line):
@@ -271,24 +291,41 @@
     send(sent_ref, *pair)
 
 
-def four_body(width, pair_ref, got_ref, sent_ref):
+def list_ids(ids_ref, early, late, width):
+    at = iota(ids_ref.shape, 0)
+    ids = jnp.zeros(ids_ref.shape, F32)
+    for i in range(ids_ref.shape[0]):
+        line = (early, late)[i // 4]
+        ids = jnp.where(at == i, line[:, i % 4 * width : (i % 4 + 1) * width], ids)
+    ids_ref[...] = ids
+
+
+def four_body(width, pair_ref, got_ref, sent_ref, ids_ref):
     _, z, _ = place()
-    send(sent_ref, *together(z == 0, taken(pair_ref), received(got_ref), 2 * width))
+    four = together(z == 0, taken(pair_ref), received(got_ref), 2 * width)
+    send(sent_ref, *four)
+    list_ids(ids_ref, four[2], four[2], width)
 
 
 def turn_body(
-    width, own_ref, got_ref, pair_ref, pair_got_ref, four_got_ref, mine_ref, sent_ref, ids_ref
+    width,
+    own_ref,
+    got_ref,
+    pair_ref,
+    pair_got_ref,
+    four_got_ref,
+    rows_ref,
+    mine_ref,
+    sent_ref,
+    ids_ref,
+    same_rows_ref,
 ):
+    same_rows_ref[...] = rows_ref[...]
     x, z, zz = place()
     pair, pair_got, four_got = taken(pair_ref), received(pair_got_ref), received(four_got_ref)
     line = together(z == 0, pair, pair_got, 2 * width)[2]
-    lines = ordered(zz == 0, [line], [four_got[2]])
-    at = iota(ids_ref.shape, 0)
-    ids = jnp.zeros(ids_ref.shape, F32)
-    for i in range(ids_ref.shape[0]):
-        part = lines[i // 4][0][:, i % 4 * width : (i % 4 + 1) * width]
-        ids = jnp.where(at == i, part, ids)
-    ids_ref[...] = ids
+    (early,), (late,) = ordered(zz == 0, [line], [four_got[2]])
+    list_ids(ids_ref, early, late, width)
 
     before = jnp.where(zz == 0, 0.0, four_got[0])
     before = jnp.where(z == 0, before, jnp.exp(pair_got[1]) * before + pair_got[0])
@@ -299,36 +336,6 @@
     send(sent_ref, other, jnp.zeros_like(first_log), jnp.zeros_like(first_log))
 
 
-def inner_body(skip_far, xconv_far, bc_far, lines_far, pre_far, decay_far, *rest):
-    far = (skip_far, xconv_far, bc_far, lines_far)
-    skip_ref, xconv_ref, bc_ref, lines_ref, pre_ref, decay_ref, sems = rest
-    finished(started(far, rest[:4], sems))
-    tokens, channels = xconv_ref.shape
-    heads = channels // HDIM
-    row = lines_ref[0]
-    column = row.T
-    spread = head_spread(heads)
-    decay_ref[...] = dot_left(jnp.exp(row), spread, FIRST)
-    copies = started([decay_ref], [decay_far], sems)
-    inflow = dot_left(lines_ref[1], spread, FIRST)
-    skip = dot_exact(skip_ref[...], spread)
-    meet = dot(bc_ref[:, STATE:], bc_ref[:, :STATE], ((1,), (1,)))
-    lower = iota((tokens, tokens), 0) >= iota((tokens, tokens), 1)
-    left = iota((tokens, 2 * HDIM), 1) < HDIM
-    for pair in range(heads // 2):
-        cut = slice(pair * 2 * HDIM, (pair + 1) * 2 * HDIM)
-        xconv = xconv_ref[:, cut]
-        d_high, d_low = halves(xconv * inflow[:, cut])
-        both = []
-        for h in (2 * pair, 2 * pair + 1):
-            gap = column[:, h : h + 1] - row[h : h + 1, :]
-            mix = jnp.where(lower, jnp.exp(gap), 0.0) * meet
-            m_high, m_low = halves(mix)
-            both.append(dot16(m_high, d_high) + dot16(m_high, d_low) + dot16(m_low, d_high))
-        pre_ref[:, cut] = skip[:, cut] * xconv + jnp.where(left, both[0], both[1])
-    finished(copies + started([pre_ref], [pre_far], sems, 1))
-
-
 def prefix_body(parts_ref, starts_ref):
     ctx, rows, share = starts_ref.shape
     state = jnp.zeros((rows, share), F32)
@@ -338,10 +345,10 @@
             state = parts_ref[i, STATE : STATE + 1] * state + parts_ref[i, :STATE]
 
 
-def back_body(paired, gain_far, pre_far, decay_far, bc_far, *rest):
+def back_body(paired, gain_far, pre_far, decay_far, c_far, *rest):
     starts, (out_far, *rest) = rest[: 1 + paired], rest[1 + paired :]
-    far = (gain_far, pre_far, decay_far, bc_far)
-    gain_ref, pre_ref, decay_ref, bc_ref, out_ref, sems = rest
+    far = (gain_far, pre_far, decay_far, c_far)
+    gain_ref, pre_ref, decay_ref, c_ref, out_ref, sems = rest
     copies = started(far, rest[:4], sems)
     channels = pre_ref.shape[1]
     width = min(channels, 4 * HDIM)
@@ -354,7 +361,7 @@
     else:
         start = starts[0][...]
     finished(copies)
-    c_high, c_low = halves(bc_ref[:, STATE:])
+    c_high, c_low = halves(c_ref[...])
     copies = []
     for i in range(channels // width):
         cut = slice(i * width, (i + 1) * width)
@@ -367,8 +374,9 @@
     finished(copies)
 
 
-def entering_by_pairs(keep, sent, width, after):
+def entering_by_pairs(keep, sent, width, after, meanwhile, late_rows):
     pair_array, sent_array = array(keep.shape, F32), array(sent.shape, jnp.int16)
+    ids_array = array((8, width), F32)
     got = swapped(sent, "ctx", 1)
     pair, sent = call(
         functools.partial(pair_body, width),
@@ -379,24 +387,26 @@
         name="pair",
     )
     pair_got = swapped(sent, "ctx", 2)
-    (sent,) = call(
+    sent, ids = call(
         functools.partial(four_body, width),
-        [sent_array],
+        [sent_array, ids_array],
         (pair, pair_got),
         near=True,
         after=after[1],
         name="four",
     )
     four_got = swapped(sent, "ctx", 4)
-    mine, sent, ids = call(
+    done = meanwhile(ids)
+    mine, sent, ids, late_rows = call(
         functools.partial(turn_body, width),
-        [array((STATE, keep.shape[1]), F32), sent_array, array((8, width), F32)],
-        (keep, got, pair, pair_got, four_got),
+        [array((STATE, keep.shape[1]), F32), sent_array, ids_array, late_rows],
+        (keep, got, pair, pair_got, four_got, late_rows),
         near=True,
         after=after[2],
+        after_far=(done,),
         name="turn",
     )
-    return (mine, swapped(sent, "ctx", 1)), ids
+    return (mine, swapped(sent, "ctx", 1)), ids, (done, late_rows)
 
 
 def entering_by_rows(state):
@@ -416,7 +426,7 @@
 
 
 def mixing(
-    after, seq_input, b_input, c_input, before, conv_x, conv_bc, log_decay, skip, gain, ids
+    after, meanwhile, late_rows, seq_input, b_input, c_input, before, conv_x, conv_bc, log_decay, skip, gain, ids
 ):
     tokens, channels = seq_input.shape
     heads = skip.shape[0]
@@ -424,17 +434,18 @@
     paired = after is not None
     outs = [
         array((tokens, channels), F32),
-        array((tokens, 2 * STATE), F32),
-        array((2, heads, tokens), F32),
+        array((tokens, channels), F32),
+        array((tokens, STATE), F32),
     ]
     if paired:
         ends = [array((STATE + NOTES, channels // 2), F32)]
         ends.append(array((STATE + 16, channels // 2), jnp.int16))
     else:
         ends = [array((STATE + NOTES, channels), F32)]
-    args = (seq_input, b_input, c_input, conv_x, conv_bc, log_decay, ids.T, before)
-    xconv, bc, lines, *ends = call(
-        functools.partial(front_body, paired, len(args)),
+    args = (seq_input, b_input, c_input, conv_x, conv_bc, log_decay)
+    args = (*args, skip.reshape(1, heads), ids.T, before)
+    pre, decay, cmat, *ends = call(
+        functools.partial(local_body, paired, len(args)),
         outs + ends,
         args,
         fixed=len(args) - 1,
@@ -442,31 +453,22 @@
         after=after[0] if paired else (),
         scratch=room(args) + room(outs) + [pltpu.VMEM((8 + tokens, channels + 2 * STATE), F32)],
         sems=len(args),
-        flops=10**9,
+        flops=5 * 10**9,
         grant=20,
-        name="front",
-    )
-    args = (skip.reshape(1, heads), xconv, bc, lines)
-    outs = [array((tokens, channels), F32)] * 2
-    pre, decay = call(
-        inner_body,
-        outs,
-        args,
-        fixed=1,
-        scratch=room(args) + room(outs),
-        sems=4,
-        flops=4 * 10**9,
-        grant=16,
-        name="inner",
-    )
+        name="local",
+    )
+    done = None
     if paired:
         first, second, third = after[1:]
-        starts, lines_of_ids = entering_by_pairs(*ends, width, (first, (*second, pre), third))
+        after = (first, second, third)
+        starts, lines_of_ids, done = entering_by_pairs(
+            *ends, width, after, meanwhile, late_rows
+        )
     else:
         starts, lines_of_ids = (entering_by_rows(ends[0]),), None
 
     def finish(after=()):
-        args = (gain.reshape(1, channels), pre, decay, bc)
+        args = (gain.reshape(1, channels), pre, decay, cmat)
         outs = [array((tokens, channels), BF16)]
         return call(
             functools.partial(back_body, paired),
@@ -482,7 +484,7 @@
             name="back",
         )[0]
 
-    return finish, lines_of_ids
+    return finish, lines_of_ids, done
 
 
 TILE = 512
@@ -542,7 +544,7 @@
     finished(out_copies)
 
 
-def along_z(moe_input):
+def along_z(moe_input, before):
     rows, columns = moe_input.shape
     joined = call(
         join_body,
@@ -550,24 +552,25 @@
         (moe_input, swapped(moe_input, "ctx", 2)),
         fixed=1,
         sems=2,
+        after=(before,),
         name="join",
     )[0]
     return joined, swapped(joined, "ctx", 4)
 
 
-def gathered(moe_input):
-    z = along_z(moe_input)
+def gathered(moe_input, before):
+    z = along_z(moe_input, before)
     x = [swapped(a, "ctx", 1) for a in z]
     y = [swapped(a, "exp", 2) for a in z]
     d = (swapped(y[0], "ctx", 1), swapped(x[1], "exp", 2))
     halves_of_rows = []
-    for pieces in zip(z, x, y, d):
-        beside = [swapped(a, "exp", 1) for a in pieces]
+    for i, pieces in enumerate(zip(z, x, y, d)):
+        beside = [swapped(a, "exp", 1) for a in pieces[: 4 - i]]
         halves_of_rows.append([*pieces[:2], *beside[:2], *pieces[2:], *beside[2:]])
     return halves_of_rows
 
 
-def experts_by_tokens(part, pieces, ids, w_gate, w_up, so_far, after):
+def experts_by_tokens(part, pieces, ids, w_gate, w_up, so_far):
     rows = pieces[0].shape[0] // 2
     length = 4 * rows
     hidden = w_gate.shape[2]
@@ -579,7 +582,6 @@
         held=2,
         near_args=0,
         aliases={len(args): 0} if part else None,
-        after_far=after,
         scratch=[
             pltpu.VMEM((length // rows, rows, rows), BF16),
             pltpu.VMEM((length, TILE), BF16),
@@ -638,13 +640,20 @@
         name="ends",
     )[0]
     before = lax.ppermute(ends, "ctx", [(i, i + 1) for i in range(ctx - 1)])
-    follow = None
+    follow = meanwhile = late_rows = None
     if by_tokens:
-        one, two = gathered(moe_input)
-        follow = (one[:1], (one[1], one[4], one[2]), two[:1])
-        follow += ((two[1], two[4], two[2], one[5], one[3], one[6]),)
-    finish, ids = mixing(
+        one, two = gathered(moe_input, before)
+        follow = (one[:1], (), (two[0], one[1], one[4], one[2]))
+        follow += ((two[1], two[4], two[2]),)
+        late_rows = two[5]
+
+        def meanwhile(ids):
+            return experts_by_tokens(0, one, ids, w_gate, w_up, None)
+
+    finish, ids, done = mixing(
         follow,
+        meanwhile,
+        late_rows,
         seq_input,
         b_input,
         c_input,
@@ -657,9 +666,10 @@
         expert_ids,
     )
     if by_tokens:
-        hidden = experts_by_tokens(0, one, ids, w_gate, w_up, None, ())
+        hidden, late_rows = done
+        two.append(swapped(late_rows, "exp", 1))
+        hidden = experts_by_tokens(1, two, ids, w_gate, w_up, hidden)
         mixed = finish((hidden,))
-        hidden = experts_by_tokens(1, two, ids, w_gate, w_up, hidden, (mixed,))
     else:
         mixed = finish()
         hidden = experts_by_slots(moe_input, expert_ids, w_gate, w_up)

time: 68 us -> 63.9 us (0.940)
  waiting for transfers between devices: 21.3 us -> 15.1 us
  starting transfers between devices: 20 us -> 23.4 us
  Pallas kernels: 25.4 us -> 24.2 us
    ppermute x20, waiting for transfers between devices: 21.3 us -> 13.4 us  [swapped(): lax.ppermute(block, axis, [(i, i ^ bit) for i in range(lax.axis_size(axis...]
    ppermute x20, starting transfers between devices: 16.7 us -> 20 us  [swapped(): lax.ppermute(block, axis, [(i, i ^ bit) for i in range(lax.axis_size(axis...]
    ppermute x1, waiting for transfers between devices: 0.01 us -> 1.65 us  [on_device(): before = lax.ppermute(ends, 'ctx', [(i, i + 1) for i in range(ctx - 1)])]
    pallas_call x10 -> x9, Pallas kernels: 25.4 us -> 24.2 us  [call(): pl.pallas_call(body, out_shape=outs, in_specs=[pl.BlockSpec(memory_space=...]
  transfers between devices with their start and end apart: 21 -> 21, of which waited for: 5 -> 6; matrix products, arithmetic and copies ran while one was open for 0% -> 0% of each run, Pallas kernels for 29% -> 31%
where the time goes in v8:
time: 63.9 us; the launch traced here: 63.7 us
  Pallas kernels  24.2 us (38%)
  starting transfers between devices  23.4 us (37%)
  waiting for transfers between devices  15.1 us (24%)
  between operations  0.92 us (1%)
    pallas_call x9, Pallas kernels, call(): pl.pallas_call(body, out_shape=outs, in_specs=[pl.BlockSpec(memory_space=...  24.2 us
    ppermute x20, starting transfers between devices, swapped(): lax.ppermute(block, axis, [(i, i ^ bit) for i in range(lax.axis_size(axis...  20 us
    ppermute x20, waiting for transfers between devices, swapped(): lax.ppermute(block, axis, [(i, i ^ bit) for i in range(lax.axis_size(axis...  13.4 us
    ppermute x1, starting transfers between devices, on_device(): before = lax.ppermute(ends, 'ctx', [(i, i + 1) for i in range(ctx - 1)])  3.4 us
    ppermute x1, waiting for transfers between devices, on_device(): before = lax.ppermute(ends, 'ctx', [(i, i + 1) for i in range(ctx - 1)])  1.65 us
  transfers between devices with their start and end apart: 21, of which 6 were waited for; matrix products, arithmetic and copies ran while one was open for 0% of the time, Pallas kernels for 31%

profile of v8, /device:TPU:0, one launch (start us, length us, event | category | flops | bytes accessed | tf_op | source)
XLA Modules:
  0.0 63.7 jit_solution(1208955937851438101)
XLA Ops:
  0.6 3.1 %collective-permute-start.1 = (bf16[64,1024]{1,0:T(8,128)(2,1)}, bf16[64,1024]{1,0:T(8,128)(2,1)S(1)}, u32[]{:S(2)}, u32[]{:S(2)}) collective-permute-start(bf16[64,1024]{1,0:T(8,128)(2,1)} %refs_0_.6), channel_id=1, source_target_pairs={{0,8},{4,12},{8,0},{12,4},{16,24},{20,28},{24,16},{28,20},{1,9},{5... | collective-permute-start | bytes 393224 | tf_op jit(solution)/shard_map/ppermute | solution.py:501
  3.7 0.8 %ends.1 = bf16[16,1280]{1,0:T(8,128)(2,1)S(1)} custom-call(bf16[256,1024]{1,0:T(8,128)(2,1)} %refs_0_.7, bf16[256,128]{1,0:T(8,128)(2,1)} %refs_1_.5, bf16[256,128]{1,0:T(8,128)(2,1)} %refs_2_.3), custom_call_target="tpu_custom_call" | custom-call | bytes 696320 | tf_op jit(solution)/shard_map/ends/pallas_call | solution.py:126
  4.5 3.4 %collective-permute-start = (bf16[16,1280]{1,0:T(8,128)(2,1)S(1)}, bf16[16,1280]{1,0:T(8,128)(2,1)S(1)}, u32[]{:S(2)}, u32[]{:S(2)}) collective-permute-start(bf16[16,1280]{1,0:T(8,128)(2,1)S(1)} %ends.1), channel_id=1, source_target_pairs={{0,4},{4,8},{8,12},{12,16},{16,20},{20,24},{24,28},{1,5},{5,9},{9,... | collective-permute-start | bytes 122888 | tf_op jit(solution)/shard_map/ppermute | solution.py:642
  7.9 1.7 %collective-permute-done.refs_2_.refs_8_ = bf16[16,1280]{1,0:T(8,128)(2,1)S(1)} collective-permute-done((bf16[16,1280]{1,0:T(8,128)(2,1)S(1)}, bf16[16,1280]{1,0:T(8,128)(2,1)S(1)}, u32[]{:S(2)}, u32[]{:S(2)}) %collective-permute-start) | collective-permute-done | bytes 40992 | tf_op jit(solution)/shard_map/ppermute | solution.py:642
  9.6 1.1 %join.1.refs_9_.refs_2_ = bf16[128,1024]{1,0:T(8,128)(2,1)S(1)} custom-call(bf16[64,1024]{1,0:T(8,128)(2,1)} %refs_0_.6, bf16[64,1024]{1,0:T(8,128)(2,1)S(1)} %collective-permute-done.1.refs_1_, bf16[16,1280]{1,0:T(8,128)(2,1)S(1)} %collective-permute-done.refs_2_.refs_8_), custom_call_target="tpu_custom_call" | custom-call | bytes 524288 | tf_op jit(solution)/shard_map/join/pallas_call | solution.py:126
  10.7 1.6 %collective-permute-start.6 = (bf16[128,1024]{1,0:T(8,128)(2,1)S(1)}, bf16[128,1024]{1,0:T(8,128)(2,1)S(1)}, u32[]{:S(2)}, u32[]{:S(2)}) collective-permute-start(bf16[128,1024]{1,0:T(8,128)(2,1)S(1)} %join.1.refs_9_.refs_2_), channel_id=1, source_target_pairs={{0,2},{1,3},{2,0},{3,1},{4,6},{5,7},{6,4},{7,5},{8,10},{9,11},{10,... | collective-permute-start | bytes 786440 | tf_op jit(solution)/shard_map/ppermute | solution.py:501
  12.2 7.2 %local.1 = (f32[256,1024]{1,0:T(8,128)S(1)}, f32[256,1024]{1,0:T(8,128)S(1)}, f32[256,128]{1,0:T(8,128)S(1)}, f32[136,512]{1,0:T(8,128)S(1)}, s16[144,512]{1,0:T(8,128)(2,1)S(1)}) custom-call(bf16[256,1024]{1,0:T(8,128)(2,1)} %refs_0_.7, bf16[256,128]{1,0:T(8,128)(2,1)} %refs_1_.5, bf16[256,128]{1,0:T(8,128)(2,1)} %refs_2_.3, f32[4,1024]{1,0:T(4,128)} %refs_3_.1, ...), custom_call_target="tpu_custom_call" | custom-call | flops 5000000000 | bytes 3387968 | tf_op jit(solution)/shard_map/local/pallas_call | solution.py:126
  19.5 2.4 %collective-permute-start.2 = (s16[144,512]{1,0:T(8,128)(2,1)S(1)}, s16[144,512]{1,0:T(8,128)(2,1)S(1)}, u32[]{:S(2)}, u32[]{:S(2)}) collective-permute-start(s16[144,512]{1,0:T(8,128)(2,1)S(1)} %get-tuple-element.19), channel_id=1, source_target_pairs={{0,4},{4,0},{8,12},{12,8},{16,20},{20,16},{24,28},{28,24},{1,5},{5... | collective-permute-start | bytes 442376 | tf_op jit(solution)/shard_map/ppermute | solution.py:501
  21.9 2.6 %collective-permute-start.4 = (bf16[128,1024]{1,0:T(8,128)(2,1)S(1)}, bf16[128,1024]{1,0:T(8,128)(2,1)S(1)}, u32[]{:S(2)}, u32[]{:S(2)}) collective-permute-start(bf16[128,1024]{1,0:T(8,128)(2,1)S(1)} %join.1.refs_9_.refs_2_), channel_id=1, source_target_pairs={{0,16},{4,20},{8,24},{12,28},{16,0},{20,4},{24,8},{28,12},{1,17},{... | collective-permute-start | bytes 786440 | tf_op jit(solution)/shard_map/ppermute | solution.py:501
  24.5 1.4 %collective-permute-start.5 = (bf16[128,1024]{1,0:T(8,128)(2,1)S(1)}, bf16[128,1024]{1,0:T(8,128)(2,1)S(1)}, u32[]{:S(2)}, u32[]{:S(2)}) collective-permute-start(bf16[128,1024]{1,0:T(8,128)(2,1)S(1)} %join.1.refs_9_.refs_2_), channel_id=1, source_target_pairs={{0,4},{4,0},{8,12},{12,8},{16,20},{20,16},{24,28},{28,24},{1,5},{5... | collective-permute-start | bytes 786440 | tf_op jit(solution)/shard_map/ppermute | solution.py:501
  25.9 0.6 collective-permute-start.14
  26.5 0.1 pair.1
  26.7 2.0 %collective-permute-start.3 = (s16[144,512]{1,0:T(8,128)(2,1)S(1)}, s16[144,512]{1,0:T(8,128)(2,1)S(1)}, u32[]{:S(2)}, u32[]{:S(2)}) collective-permute-start(s16[144,512]{1,0:T(8,128)(2,1)S(1)} %get-tuple-element.21), channel_id=1, source_target_pairs={{0,8},{4,12},{8,0},{12,4},{16,24},{20,28},{24,16},{28,20},{1,9},{5... | collective-permute-start | bytes 442376 | tf_op jit(solution)/shard_map/ppermute | solution.py:501
  28.7 5.9 %collective-permute-done.4.refs_2_ = bf16[128,1024]{1,0:T(8,128)(2,1)S(1)} collective-permute-done((bf16[128,1024]{1,0:T(8,128)(2,1)S(1)}, bf16[128,1024]{1,0:T(8,128)(2,1)S(1)}, u32[]{:S(2)}, u32[]{:S(2)}) %collective-permute-start.4) | collective-permute-done | bytes 262176 | tf_op jit(solution)/shard_map/ppermute | solution.py:501
  34.6 0.5 collective-permute-start.13
  35.1 1.4 %collective-permute-start.9 = (bf16[128,1024]{1,0:T(8,128)(2,1)S(1)}, bf16[128,1024]{1,0:T(8,128)(2,1)S(1)}, u32[]{:S(2)}, u32[]{:S(2)}) collective-permute-start(bf16[128,1024]{1,0:T(8,128)(2,1)S(1)} %collective-permute-done.4.refs_2_), channel_id=1, source_target_pairs={{0,4},{4,0},{8,12},{12,8},{16,20},{20,16},{24,28},{28,24},{1,5},{5... | collective-permute-start | bytes 786440 | tf_op jit(solution)/shard_map/ppermute | solution.py:501
  36.5 1.2 %collective-permute-done.3.refs_1_.refs_3_ = s16[144,512]{1,0:T(8,128)(2,1)S(1)} collective-permute-done((s16[144,512]{1,0:T(8,128)(2,1)S(1)}, s16[144,512]{1,0:T(8,128)(2,1)S(1)}, u32[]{:S(2)}, u32[]{:S(2)}) %collective-permute-start.3) | collective-permute-done | bytes 147488 | tf_op jit(solution)/shard_map/ppermute | solution.py:501
  37.6 0.5 collective-permute-start.11
  38.1 0.1 four.1
  38.3 0.6 collective-permute-start.12
  38.9 0.9 %collective-permute-start.8 = (s16[144,512]{1,0:T(8,128)(2,1)S(1)}, s16[144,512]{1,0:T(8,128)(2,1)S(1)}, u32[]{:S(2)}, u32[]{:S(2)}) collective-permute-start(s16[144,512]{1,0:T(8,128)(2,1)S(1)} %get-tuple-element.22), channel_id=1, source_target_pairs={{0,16},{4,20},{8,24},{12,28},{16,0},{20,4},{24,8},{28,12},{1,17},{... | collective-permute-start | bytes 442376 | tf_op jit(solution)/shard_map/ppermute | solution.py:501
  39.7 3.6 %collective-permute-done.9.refs_6_.refs_3_ = bf16[128,1024]{1,0:T(8,128)(2,1)S(1)} collective-permute-done((bf16[128,1024]{1,0:T(8,128)(2,1)S(1)}, bf16[128,1024]{1,0:T(8,128)(2,1)S(1)}, u32[]{:S(2)}, u32[]{:S(2)}) %collective-permute-start.9) | collective-permute-done | bytes 262176 | tf_op jit(solution)/shard_map/ppermute | solution.py:501
  43.4 0.5 collective-permute-start.10
  43.9 2.6 %collective-permute-done.11.refs_7_.refs_6_ = bf16[128,1024]{1,0:T(8,128)(2,1)S(1)} collective-permute-done((bf16[128,1024]{1,0:T(8,128)(2,1)S(1)}, bf16[128,1024]{1,0:T(8,128)(2,1)S(1)}, u32[]{:S(2)}, u32[]{:S(2)}) %collective-permute-start.11) | collective-permute-done | bytes 262176 | tf_op jit(solution)/shard_map/ppermute | solution.py:501
  46.5 0.5 collective-permute-start.19
  47.0 5.7 %experts.2.refs_9_.refs_11_ = bf16[1,512,1024]{2,1,0:T(8,128)(2,1)} custom-call(bf16[1,4096,1024]{2,1,0:T(8,128)(2,1)S(1)} %bitcast.4, bf16[1,4096,1024]{2,1,0:T(8,128)(2,1)S(1)} %copy-done, bf16[128,1024]{1,0:T(8,128)(2,1)S(1)} %join.1.refs_9_.refs_2_, bf16[128,1024]{1,0:T(8,128)(2,1)S(1)} %collective-permute-done.5.refs_3_, ...), custom_call_target="tpu_custom_call" | custom-call | flops 4294967296 | bytes 19927040 | tf_op jit(solution)/shard_map/experts/pallas_call | solution.py:126
  52.7 0.3 turn.1
  53.1 0.1 collective-permute-start.20
  53.2 1.4 %collective-permute-start.17 = (s16[144,512]{1,0:T(8,128)(2,1)S(1)}, s16[144,512]{1,0:T(8,128)(2,1)S(1)}, u32[]{:S(2)}, u32[]{:S(2)}) collective-permute-start(s16[144,512]{1,0:T(8,128)(2,1)S(1)} %get-tuple-element.25), channel_id=1, source_target_pairs={{0,4},{4,0},{8,12},{12,8},{16,20},{20,16},{24,28},{28,24},{1,5},{5... | collective-permute-start | bytes 442376 | tf_op jit(solution)/shard_map/ppermute | solution.py:501
  54.6 0.1 collective-permute-done.20.refs_9_
  54.7 5.7 %experts.3.refs_6_ = bf16[1,512,1024]{2,1,0:T(8,128)(2,1)} custom-call(bf16[1,4096,1024]{2,1,0:T(8,128)(2,1)S(1)} %bitcast.4, bf16[1,4096,1024]{2,1,0:T(8,128)(2,1)S(1)} %copy-done, bf16[128,1024]{1,0:T(8,128)(2,1)S(1)} %collective-permute-done.4.refs_2_, ...), custom_call_target="tpu_custom_call", output_to_operand_aliasing={{}: (11, {})} | custom-call | flops 4294967296 | bytes 20975616 | tf_op jit(solution)/shard_map/experts/pallas_call | solution.py:126
  60.4 3.1 %back.1 = bf16[256,1024]{1,0:T(8,128)(2,1)} custom-call(f32[1,1024]{1,0:T(1,128)} %bitcast.5, f32[256,1024]{1,0:T(8,128)S(1)} %get-tuple-element.15.refs_1_, f32[256,1024]{1,0:T(8,128)S(1)} %get-tuple-element.16.refs_2_, f32[256,128]{1,0:T(8,128)S(1)} %get-tuple-element.17.refs_3_, f32[128,512]{1,0:T(8,128)S(1)} %get-tuple-element.24.refs_4_, ...), custom_call_target="tpu_custom_call" | custom-call | flops 1000000000 | bytes 3166208 | tf_op jit(solution)/shard_map/back/pallas_call | solution.py:126
  (26 shorter events, 0.1 us)
Async XLA Ops:
  0.6 8.9 %collective-permute-start.1 = (bf16[64,1024]{1,0:T(8,128)(2,1)}, bf16[64,1024]{1,0:T(8,128)(2,1)S(1)}, u32[]{:S(2)}, u32[]{:S(2)}) collective-permute-start(bf16[64,1024]{1,0:T(8,128)(2,1)} %refs_0_.6), channel_id=1, source_target_pairs={{0,8},{4,12},{8,0},{12,4},{16,24},{20,28},{24,16},{28,20},{1,9},{5... | collective-permute-start | bytes 393224 | tf_op jit(solution)/shard_map/ppermute | solution.py:501
  4.5 5.1 %collective-permute-start = (bf16[16,1280]{1,0:T(8,128)(2,1)S(1)}, bf16[16,1280]{1,0:T(8,128)(2,1)S(1)}, u32[]{:S(2)}, u32[]{:S(2)}) collective-permute-start(bf16[16,1280]{1,0:T(8,128)(2,1)S(1)} %ends.1), channel_id=1, source_target_pairs={{0,4},{4,8},{8,12},{12,16},{16,20},{20,24},{24,28},{1,5},{5,9},{9,... | collective-permute-start | bytes 122888 | tf_op jit(solution)/shard_map/ppermute | solution.py:642
  9.6 37.4 %slice-start = ((s8[8388608]{0:T(1024)(128)(4,1)}), s8[4194304]{0:T(1024)(128)(4,1)S(1)}, s32[]{:S(2)}) async-start(s8[8388608]{0:T(1024)(128)(4,1)} %bitcast.3), calls=%async_computation | async-start | bytes 8388608
  10.7 15.2 %collective-permute-start.6 = (bf16[128,1024]{1,0:T(8,128)(2,1)S(1)}, bf16[128,1024]{1,0:T(8,128)(2,1)S(1)}, u32[]{:S(2)}, u32[]{:S(2)}) collective-permute-start(bf16[128,1024]{1,0:T(8,128)(2,1)S(1)} %join.1.refs_9_.refs_2_), channel_id=1, source_target_pairs={{0,2},{1,3},{2,0},{3,1},{4,6},{5,7},{6,4},{7,5},{8,10},{9,11},{10,... | collective-permute-start | bytes 786440 | tf_op jit(solution)/shard_map/ppermute | solution.py:501
  12.2 34.8 %slice-start.1 = ((s8[8388608]{0:T(1024)(128)(4,1)}), s8[4194304]{0:T(1024)(128)(4,1)S(1)}, s32[]{:S(2)}) async-start(s8[8388608]{0:T(1024)(128)(4,1)} %bitcast.3), calls=%async_computation.1 | async-start | bytes 8388608
  12.2 34.8 %copy-start = (bf16[1,4096,1024]{2,1,0:T(8,128)(2,1)S(1)}, bf16[1,4096,1024]{2,1,0:T(8,128)(2,1)}, u32[]{:S(2)}) copy-start(bf16[1,4096,1024]{2,1,0:T(8,128)(2,1)} %refs_1_.7) | copy-start | bytes 25165828
  19.5 7.0 %collective-permute-start.2 = (s16[144,512]{1,0:T(8,128)(2,1)S(1)}, s16[144,512]{1,0:T(8,128)(2,1)S(1)}, u32[]{:S(2)}, u32[]{:S(2)}) collective-permute-start(s16[144,512]{1,0:T(8,128)(2,1)S(1)} %get-tuple-element.19), channel_id=1, source_target_pairs={{0,4},{4,0},{8,12},{12,8},{16,20},{20,16},{24,28},{28,24},{1,5},{5... | collective-permute-start | bytes 442376 | tf_op jit(solution)/shard_map/ppermute | solution.py:501
  21.9 12.7 %collective-permute-start.4 = (bf16[128,1024]{1,0:T(8,128)(2,1)S(1)}, bf16[128,1024]{1,0:T(8,128)(2,1)S(1)}, u32[]{:S(2)}, u32[]{:S(2)}) collective-permute-start(bf16[128,1024]{1,0:T(8,128)(2,1)S(1)} %join.1.refs_9_.refs_2_), channel_id=1, source_target_pairs={{0,16},{4,20},{8,24},{12,28},{16,0},{20,4},{24,8},{28,12},{1,17},{... | collective-permute-start | bytes 786440 | tf_op jit(solution)/shard_map/ppermute | solution.py:501
  24.5 10.1 %collective-permute-start.5 = (bf16[128,1024]{1,0:T(8,128)(2,1)S(1)}, bf16[128,1024]{1,0:T(8,128)(2,1)S(1)}, u32[]{:S(2)}, u32[]{:S(2)}) collective-permute-start(bf16[128,1024]{1,0:T(8,128)(2,1)S(1)} %join.1.refs_9_.refs_2_), channel_id=1, source_target_pairs={{0,4},{4,0},{8,12},{12,8},{16,20},{20,16},{24,28},{28,24},{1,5},{5... | collective-permute-start | bytes 786440 | tf_op jit(solution)/shard_map/ppermute | solution.py:501
  25.9 9.2 %collective-permute-start.7 = (bf16[128,1024]{1,0:T(8,128)(2,1)S(1)}, bf16[128,1024]{1,0:T(8,128)(2,1)S(1)}, u32[]{:S(2)}, u32[]{:S(2)}) collective-permute-start(bf16[128,1024]{1,0:T(8,128)(2,1)S(1)} %join.1.refs_9_.refs_2_), channel_id=1, source_target_pairs={{0,1},{1,0},{2,3},{3,2},{4,5},{5,4},{6,7},{7,6},{8,9},{9,8},{10,11... | collective-permute-start | bytes 786440 | tf_op jit(solution)/shard_map/ppermute | solution.py:501
  25.9 12.2 %collective-permute-start.14 = (bf16[128,1024]{1,0:T(8,128)(2,1)S(1)}, bf16[128,1024]{1,0:T(8,128)(2,1)S(1)}, u32[]{:S(2)}, u32[]{:S(2)}) collective-permute-start(bf16[128,1024]{1,0:T(8,128)(2,1)S(1)} %collective-permute-done.6.refs_4_.refs_6_), channel_id=1, source_target_pairs={{0,4},{4,0},{8,12},{12,8},{16,20},{20,16},{24,28},{28,24},{1,5},{5... | collective-permute-start | bytes 786440 | tf_op jit(solution)/shard_map/ppermute | solution.py:501
  26.7 11.0 %collective-permute-start.3 = (s16[144,512]{1,0:T(8,128)(2,1)S(1)}, s16[144,512]{1,0:T(8,128)(2,1)S(1)}, u32[]{:S(2)}, u32[]{:S(2)}) collective-permute-start(s16[144,512]{1,0:T(8,128)(2,1)S(1)} %get-tuple-element.21), channel_id=1, source_target_pairs={{0,8},{4,12},{8,0},{12,4},{16,24},{20,28},{24,16},{28,20},{1,9},{5... | collective-permute-start | bytes 442376 | tf_op jit(solution)/shard_map/ppermute | solution.py:501
  34.6 3.7 %collective-permute-start.15 = (bf16[128,1024]{1,0:T(8,128)(2,1)S(1)}, bf16[128,1024]{1,0:T(8,128)(2,1)S(1)}, u32[]{:S(2)}, u32[]{:S(2)}) collective-permute-start(bf16[128,1024]{1,0:T(8,128)(2,1)S(1)} %collective-permute-done.6.refs_4_.refs_6_), channel_id=1, source_target_pairs={{0,1},{1,0},{2,3},{3,2},{4,5},{5,4},{6,7},{7,6},{8,9},{9,8},{10,11... | collective-permute-start | bytes 786440 | tf_op jit(solution)/shard_map/ppermute | solution.py:501
  34.6 4.3 %collective-permute-start.13 = (bf16[128,1024]{1,0:T(8,128)(2,1)S(1)}, bf16[128,1024]{1,0:T(8,128)(2,1)S(1)}, u32[]{:S(2)}, u32[]{:S(2)}) collective-permute-start(bf16[128,1024]{1,0:T(8,128)(2,1)S(1)} %collective-permute-done.5.refs_3_), channel_id=1, source_target_pairs={{0,1},{1,0},{2,3},{3,2},{4,5},{5,4},{6,7},{7,6},{8,9},{9,8},{10,11... | collective-permute-start | bytes 786440 | tf_op jit(solution)/shard_map/ppermute | solution.py:501
  35.1 8.3 %collective-permute-start.9 = (bf16[128,1024]{1,0:T(8,128)(2,1)S(1)}, bf16[128,1024]{1,0:T(8,128)(2,1)S(1)}, u32[]{:S(2)}, u32[]{:S(2)}) collective-permute-start(bf16[128,1024]{1,0:T(8,128)(2,1)S(1)} %collective-permute-done.4.refs_2_), channel_id=1, source_target_pairs={{0,4},{4,0},{8,12},{12,8},{16,20},{20,16},{24,28},{28,24},{1,5},{5... | collective-permute-start | bytes 786440 | tf_op jit(solution)/shard_map/ppermute | solution.py:501
  37.6 8.9 %collective-permute-start.11 = (bf16[128,1024]{1,0:T(8,128)(2,1)S(1)}, bf16[128,1024]{1,0:T(8,128)(2,1)S(1)}, u32[]{:S(2)}, u32[]{:S(2)}) collective-permute-start(bf16[128,1024]{1,0:T(8,128)(2,1)S(1)} %collective-permute-done.4.refs_2_), channel_id=1, source_target_pairs={{0,2},{1,3},{2,0},{3,1},{4,6},{5,7},{6,4},{7,5},{8,10},{9,11},{10,... | collective-permute-start | bytes 786440 | tf_op jit(solution)/shard_map/ppermute | solution.py:501
  38.1 8.4 %collective-permute-start.16 = (bf16[128,1024]{1,0:T(8,128)(2,1)S(1)}, bf16[128,1024]{1,0:T(8,128)(2,1)S(1)}, u32[]{:S(2)}, u32[]{:S(2)}) collective-permute-start(bf16[128,1024]{1,0:T(8,128)(2,1)S(1)} %collective-permute-done.14.refs_7_), channel_id=1, source_target_pairs={{0,1},{1,0},{2,3},{3,2},{4,5},{5,4},{6,7},{7,6},{8,9},{9,8},{10,11... | collective-permute-start | bytes 786440 | tf_op jit(solution)/shard_map/ppermute | solution.py:501
  38.3 14.4 %collective-permute-start.12 = (bf16[128,1024]{1,0:T(8,128)(2,1)S(1)}, bf16[128,1024]{1,0:T(8,128)(2,1)S(1)}, u32[]{:S(2)}, u32[]{:S(2)}) collective-permute-start(bf16[128,1024]{1,0:T(8,128)(2,1)S(1)} %collective-permute-done.4.refs_2_), channel_id=1, source_target_pairs={{0,1},{1,0},{2,3},{3,2},{4,5},{5,4},{6,7},{7,6},{8,9},{9,8},{10,11... | collective-permute-start | bytes 786440 | tf_op jit(solution)/shard_map/ppermute | solution.py:501
  38.9 13.9 %collective-permute-start.8 = (s16[144,512]{1,0:T(8,128)(2,1)S(1)}, s16[144,512]{1,0:T(8,128)(2,1)S(1)}, u32[]{:S(2)}, u32[]{:S(2)}) collective-permute-start(s16[144,512]{1,0:T(8,128)(2,1)S(1)} %get-tuple-element.22), channel_id=1, source_target_pairs={{0,16},{4,20},{8,24},{12,28},{16,0},{20,4},{24,8},{28,12},{1,17},{... | collective-permute-start | bytes 442376 | tf_op jit(solution)/shard_map/ppermute | solution.py:501
  43.4 9.4 %collective-permute-start.10 = (bf16[128,1024]{1,0:T(8,128)(2,1)S(1)}, bf16[128,1024]{1,0:T(8,128)(2,1)S(1)}, u32[]{:S(2)}, u32[]{:S(2)}) collective-permute-start(bf16[128,1024]{1,0:T(8,128)(2,1)S(1)} %collective-permute-done.9.refs_6_.refs_3_), channel_id=1, source_target_pairs={{0,2},{1,3},{2,0},{3,1},{4,6},{5,7},{6,4},{7,5},{8,10},{9,11},{10,... | collective-permute-start | bytes 786440 | tf_op jit(solution)/shard_map/ppermute | solution.py:501
  46.5 8.1 %collective-permute-start.18 = (bf16[128,1024]{1,0:T(8,128)(2,1)S(1)}, bf16[128,1024]{1,0:T(8,128)(2,1)S(1)}, u32[]{:S(2)}, u32[]{:S(2)}) collective-permute-start(bf16[128,1024]{1,0:T(8,128)(2,1)S(1)} %collective-permute-done.9.refs_6_.refs_3_), channel_id=1, source_target_pairs={{0,1},{1,0},{2,3},{3,2},{4,5},{5,4},{6,7},{7,6},{8,9},{9,8},{10,11... | collective-permute-start | bytes 786440 | tf_op jit(solution)/shard_map/ppermute | solution.py:501
  46.5 8.1 %collective-permute-start.19 = (bf16[128,1024]{1,0:T(8,128)(2,1)S(1)}, bf16[128,1024]{1,0:T(8,128)(2,1)S(1)}, u32[]{:S(2)}, u32[]{:S(2)}) collective-permute-start(bf16[128,1024]{1,0:T(8,128)(2,1)S(1)} %collective-permute-done.11.refs_7_.refs_6_), channel_id=1, source_target_pairs={{0,1},{1,0},{2,3},{3,2},{4,5},{5,4},{6,7},{7,6},{8,9},{9,8},{10,11... | collective-permute-start | bytes 786440 | tf_op jit(solution)/shard_map/ppermute | solution.py:501
  53.1 1.6 %collective-permute-start.20 = (bf16[128,1024]{1,0:T(8,128)(2,1)S(1)}, bf16[128,1024]{1,0:T(8,128)(2,1)S(1)}, u32[]{:S(2)}, u32[]{:S(2)}) collective-permute-start(bf16[128,1024]{1,0:T(8,128)(2,1)S(1)} %get-tuple-element.26), channel_id=1, source_target_pairs={{0,1},{1,0},{2,3},{3,2},{4,5},{5,4},{6,7},{7,6},{8,9},{9,8},{10,11... | collective-permute-start | bytes 786440 | tf_op jit(solution)/shard_map/ppermute | solution.py:501
  53.2 7.2 %collective-permute-start.17 = (s16[144,512]{1,0:T(8,128)(2,1)S(1)}, s16[144,512]{1,0:T(8,128)(2,1)S(1)}, u32[]{:S(2)}, u32[]{:S(2)}) collective-permute-start(s16[144,512]{1,0:T(8,128)(2,1)S(1)} %get-tuple-element.25), channel_id=1, source_target_pairs={{0,4},{4,0},{8,12},{12,8},{16,20},{20,16},{24,28},{28,24},{1,5},{5... | collective-permute-start | bytes 442376 | tf_op jit(solution)/shard_map/ppermute | solution.py:501

commit v9 on v8

--- a/solution.py
+++ b/solution.py
@@ -544,7 +544,7 @@
     finished(out_copies)
 
 
-def along_z(moe_input, before):
+def along_z(moe_input):
     rows, columns = moe_input.shape
     joined = call(
         join_body,
@@ -552,17 +552,16 @@
         (moe_input, swapped(moe_input, "ctx", 2)),
         fixed=1,
         sems=2,
-        after=(before,),
         name="join",
     )[0]
     return joined, swapped(joined, "ctx", 4)
 
 
-def gathered(moe_input, before):
-    z = along_z(moe_input, before)
+def gathered(moe_input):
+    z = along_z(moe_input)
     x = [swapped(a, "ctx", 1) for a in z]
     y = [swapped(a, "exp", 2) for a in z]
-    d = (swapped(y[0], "ctx", 1), swapped(x[1], "exp", 2))
+    d = (swapped(x[0], "exp", 2), swapped(y[1], "ctx", 1))
     halves_of_rows = []
     for i, pieces in enumerate(zip(z, x, y, d)):
         beside = [swapped(a, "exp", 1) for a in pieces[: 4 - i]]
@@ -642,8 +641,8 @@
     before = lax.ppermute(ends, "ctx", [(i, i + 1) for i in range(ctx - 1)])
     follow = meanwhile = late_rows = None
     if by_tokens:
-        one, two = gathered(moe_input, before)
-        follow = (one[:1], (), (two[0], one[1], one[4], one[2]))
+        one, two = gathered(moe_input)
+        follow = (one[:1], (one[1], one[4], one[2], two[0]), ())
         follow += ((two[1], two[4], two[2]),)
         late_rows = two[5]
 

time: 63.9 us -> 58.7 us (0.919)
  starting transfers between devices: 23.4 us -> 20.3 us
  waiting for transfers between devices: 15.1 us -> 12.6 us
    ppermute x20, starting transfers between devices: 20 us -> 16.9 us  [swapped(): lax.ppermute(block, axis, [(i, i ^ bit) for i in range(lax.axis_size(axis...]
    ppermute x1, waiting for transfers between devices: 1.65 us -> 0.01 us  [on_device(): before = lax.ppermute(ends, 'ctx', [(i, i + 1) for i in range(ctx - 1)])]
    ppermute x20, waiting for transfers between devices: 13.4 us -> 12.6 us  [swapped(): lax.ppermute(block, axis, [(i, i ^ bit) for i in range(lax.axis_size(axis...]
  transfers between devices with their start and end apart: 21 -> 21, of which waited for: 6 -> 5; matrix products, arithmetic and copies ran while one was open for 0% -> 0% of each run, Pallas kernels for 31% -> 36%
where the time goes in v9:
time: 58.7 us; the launch traced here: 58.1 us
  Pallas kernels  24.2 us (41%)
  starting transfers between devices  20.3 us (35%)
  waiting for transfers between devices  12.6 us (21%)
  between operations  0.95 us (2%)
    pallas_call x9, Pallas kernels, call(): pl.pallas_call(body, out_shape=outs, in_specs=[pl.BlockSpec(memory_space=...  24.2 us
    ppermute x20, starting transfers between devices, swapped(): lax.ppermute(block, axis, [(i, i ^ bit) for i in range(lax.axis_size(axis...  16.9 us
    ppermute x20, waiting for transfers between devices, swapped(): lax.ppermute(block, axis, [(i, i ^ bit) for i in range(lax.axis_size(axis...  12.6 us
    ppermute x1, starting transfers between devices, on_device(): before = lax.ppermute(ends, 'ctx', [(i, i + 1) for i in range(ctx - 1)])  3.4 us
  transfers between devices with their start and end apart: 21, of which 5 were waited for; matrix products, arithmetic and copies ran while one was open for 0% of the time, Pallas kernels for 36%

profile of v9, /device:TPU:0, one launch (start us, length us, event | category | flops | bytes accessed | tf_op | source)
XLA Modules:
  0.0 58.1 jit_solution(3187501735066426279)
XLA Ops:
  0.6 3.1 %collective-permute-start.1 = (bf16[64,1024]{1,0:T(8,128)(2,1)}, bf16[64,1024]{1,0:T(8,128)(2,1)S(1)}, u32[]{:S(2)}, u32[]{:S(2)}) collective-permute-start(bf16[64,1024]{1,0:T(8,128)(2,1)} %refs_0_.6), channel_id=1, source_target_pairs={{0,8},{4,12},{8,0},{12,4},{16,24},{20,28},{24,16},{28,20},{1,9},{5... | collective-permute-start | bytes 393224 | tf_op jit(solution)/shard_map/ppermute | solution.py:501
  3.7 0.8 %ends.1 = bf16[16,1280]{1,0:T(8,128)(2,1)S(1)} custom-call(bf16[256,1024]{1,0:T(8,128)(2,1)} %refs_0_.7, bf16[256,128]{1,0:T(8,128)(2,1)} %refs_1_.5, bf16[256,128]{1,0:T(8,128)(2,1)} %refs_2_.3), custom_call_target="tpu_custom_call" | custom-call | bytes 696320 | tf_op jit(solution)/shard_map/ends/pallas_call | solution.py:126
  4.5 3.4 %collective-permute-start = (bf16[16,1280]{1,0:T(8,128)(2,1)S(1)}, bf16[16,1280]{1,0:T(8,128)(2,1)S(1)}, u32[]{:S(2)}, u32[]{:S(2)}) collective-permute-start(bf16[16,1280]{1,0:T(8,128)(2,1)S(1)} %ends.1), channel_id=1, source_target_pairs={{0,4},{4,8},{8,12},{12,16},{16,20},{20,24},{24,28},{1,5},{5,9},{9,... | collective-permute-start | bytes 122888 | tf_op jit(solution)/shard_map/ppermute | solution.py:641
  7.9 0.0 slice-start
  7.9 1.1 %join.1.refs_9_.refs_2_ = bf16[128,1024]{1,0:T(8,128)(2,1)S(1)} custom-call(bf16[64,1024]{1,0:T(8,128)(2,1)} %refs_0_.6, bf16[64,1024]{1,0:T(8,128)(2,1)S(1)} %collective-permute-done.1.refs_1_), custom_call_target="tpu_custom_call" | custom-call | bytes 524288 | tf_op jit(solution)/shard_map/join/pallas_call | solution.py:126
  9.0 2.7 %collective-permute-start.6 = (bf16[128,1024]{1,0:T(8,128)(2,1)S(1)}, bf16[128,1024]{1,0:T(8,128)(2,1)S(1)}, u32[]{:S(2)}, u32[]{:S(2)}) collective-permute-start(bf16[128,1024]{1,0:T(8,128)(2,1)S(1)} %join.1.refs_9_.refs_2_), channel_id=1, source_target_pairs={{0,16},{4,20},{8,24},{12,28},{16,0},{20,4},{24,8},{28,12},{1,17},{... | collective-permute-start | bytes 786440 | tf_op jit(solution)/shard_map/ppermute | solution.py:501
  11.7 1.1 %collective-permute-start.3 = (bf16[128,1024]{1,0:T(8,128)(2,1)S(1)}, bf16[128,1024]{1,0:T(8,128)(2,1)S(1)}, u32[]{:S(2)}, u32[]{:S(2)}) collective-permute-start(bf16[128,1024]{1,0:T(8,128)(2,1)S(1)} %join.1.refs_9_.refs_2_), channel_id=1, source_target_pairs={{0,4},{4,0},{8,12},{12,8},{16,20},{20,16},{24,28},{28,24},{1,5},{5... | collective-permute-start | bytes 786440 | tf_op jit(solution)/shard_map/ppermute | solution.py:501
  12.8 1.5 %collective-permute-start.4 = (bf16[128,1024]{1,0:T(8,128)(2,1)S(1)}, bf16[128,1024]{1,0:T(8,128)(2,1)S(1)}, u32[]{:S(2)}, u32[]{:S(2)}) collective-permute-start(bf16[128,1024]{1,0:T(8,128)(2,1)S(1)} %join.1.refs_9_.refs_2_), channel_id=1, source_target_pairs={{0,2},{1,3},{2,0},{3,1},{4,6},{5,7},{6,4},{7,5},{8,10},{9,11},{10,... | collective-permute-start | bytes 786440 | tf_op jit(solution)/shard_map/ppermute | solution.py:501
  14.4 7.2 %local.1 = (f32[256,1024]{1,0:T(8,128)S(1)}, f32[256,1024]{1,0:T(8,128)S(1)}, f32[256,128]{1,0:T(8,128)S(1)}, f32[136,512]{1,0:T(8,128)S(1)}, s16[144,512]{1,0:T(8,128)(2,1)S(1)}) custom-call(bf16[256,1024]{1,0:T(8,128)(2,1)} %refs_0_.7, bf16[256,128]{1,0:T(8,128)(2,1)} %refs_1_.5, bf16[256,128]{1,0:T(8,128)(2,1)} %refs_2_.3, f32[4,1024]{1,0:T(4,128)} %refs_3_.1, ...), custom_call_target="tpu_custom_call" | custom-call | flops 5000000000 | bytes 3387968 | tf_op jit(solution)/shard_map/local/pallas_call | solution.py:126
  21.6 1.0 %collective-permute-start.2 = (s16[144,512]{1,0:T(8,128)(2,1)S(1)}, s16[144,512]{1,0:T(8,128)(2,1)S(1)}, u32[]{:S(2)}, u32[]{:S(2)}) collective-permute-start(s16[144,512]{1,0:T(8,128)(2,1)S(1)} %get-tuple-element.19), channel_id=1, source_target_pairs={{0,4},{4,0},{8,12},{12,8},{16,20},{20,16},{24,28},{28,24},{1,5},{5... | collective-permute-start | bytes 442376 | tf_op jit(solution)/shard_map/ppermute | solution.py:501
  22.6 0.5 collective-permute-start.14
  23.1 4.8 %collective-permute-done.2.refs_1_ = s16[144,512]{1,0:T(8,128)(2,1)S(1)} collective-permute-done((s16[144,512]{1,0:T(8,128)(2,1)S(1)}, s16[144,512]{1,0:T(8,128)(2,1)S(1)}, u32[]{:S(2)}, u32[]{:S(2)}) %collective-permute-start.2) | collective-permute-done | bytes 147488 | tf_op jit(solution)/shard_map/ppermute | solution.py:501
  27.9 0.1 pair.1
  28.1 1.8 %collective-permute-start.7 = (s16[144,512]{1,0:T(8,128)(2,1)S(1)}, s16[144,512]{1,0:T(8,128)(2,1)S(1)}, u32[]{:S(2)}, u32[]{:S(2)}) collective-permute-start(s16[144,512]{1,0:T(8,128)(2,1)S(1)} %get-tuple-element.21), channel_id=1, source_target_pairs={{0,8},{4,12},{8,0},{12,4},{16,24},{20,28},{24,16},{28,20},{1,9},{5... | collective-permute-start | bytes 442376 | tf_op jit(solution)/shard_map/ppermute | solution.py:501
  29.8 0.5 collective-permute-start.15
  30.4 0.5 collective-permute-start.9
  30.9 2.7 %collective-permute-done.7.refs_1_.refs_3_ = s16[144,512]{1,0:T(8,128)(2,1)S(1)} collective-permute-done((s16[144,512]{1,0:T(8,128)(2,1)S(1)}, s16[144,512]{1,0:T(8,128)(2,1)S(1)}, u32[]{:S(2)}, u32[]{:S(2)}) %collective-permute-start.7) | collective-permute-done | bytes 147488 | tf_op jit(solution)/shard_map/ppermute | solution.py:501
  33.6 0.9 %collective-permute-start.11 = (bf16[128,1024]{1,0:T(8,128)(2,1)S(1)}, bf16[128,1024]{1,0:T(8,128)(2,1)S(1)}, u32[]{:S(2)}, u32[]{:S(2)}) collective-permute-start(bf16[128,1024]{1,0:T(8,128)(2,1)S(1)} %collective-permute-done.6.refs_5_.refs_2_), channel_id=1, source_target_pairs={{0,4},{4,0},{8,12},{12,8},{16,20},{20,16},{24,28},{28,24},{1,5},{5... | collective-permute-start | bytes 786440 | tf_op jit(solution)/shard_map/ppermute | solution.py:501
  34.5 0.1 four.1
  34.7 0.6 collective-permute-start.12
  35.2 0.3 collective-permute-start.8
  35.6 3.0 %collective-permute-done.9.refs_7_.refs_6_ = bf16[128,1024]{1,0:T(8,128)(2,1)S(1)} collective-permute-done((bf16[128,1024]{1,0:T(8,128)(2,1)S(1)}, bf16[128,1024]{1,0:T(8,128)(2,1)S(1)}, u32[]{:S(2)}, u32[]{:S(2)}) %collective-permute-start.9) | collective-permute-done | bytes 262176 | tf_op jit(solution)/shard_map/ppermute | solution.py:501
  38.6 0.4 collective-permute-start.10
  39.0 1.9 %collective-permute-done.11.refs_6_.refs_3_ = bf16[128,1024]{1,0:T(8,128)(2,1)S(1)} collective-permute-done((bf16[128,1024]{1,0:T(8,128)(2,1)S(1)}, bf16[128,1024]{1,0:T(8,128)(2,1)S(1)}, u32[]{:S(2)}, u32[]{:S(2)}) %collective-permute-start.11) | collective-permute-done | bytes 262176 | tf_op jit(solution)/shard_map/ppermute | solution.py:501
  40.9 0.5 collective-permute-start.18
  41.4 5.7 %experts.2.refs_9_.refs_11_ = bf16[1,512,1024]{2,1,0:T(8,128)(2,1)} custom-call(bf16[1,4096,1024]{2,1,0:T(8,128)(2,1)S(1)} %bitcast.4, bf16[1,4096,1024]{2,1,0:T(8,128)(2,1)S(1)} %copy-done, bf16[128,1024]{1,0:T(8,128)(2,1)S(1)} %join.1.refs_9_.refs_2_, bf16[128,1024]{1,0:T(8,128)(2,1)S(1)} %collective-permute-done.3.refs_2_.refs_3_, ...), custom_call_target="tpu_custom_call" | custom-call | flops 4294967296 | bytes 19927040 | tf_op jit(solution)/shard_map/experts/pallas_call | solution.py:126
  47.2 0.3 turn.1
  47.5 0.1 collective-permute-start.20
  47.6 1.4 %collective-permute-start.17 = (s16[144,512]{1,0:T(8,128)(2,1)S(1)}, s16[144,512]{1,0:T(8,128)(2,1)S(1)}, u32[]{:S(2)}, u32[]{:S(2)}) collective-permute-start(s16[144,512]{1,0:T(8,128)(2,1)S(1)} %get-tuple-element.25), channel_id=1, source_target_pairs={{0,4},{4,0},{8,12},{12,8},{16,20},{20,16},{24,28},{28,24},{1,5},{5... | collective-permute-start | bytes 442376 | tf_op jit(solution)/shard_map/ppermute | solution.py:501
  49.0 0.1 collective-permute-done.20.refs_9_
  49.1 5.7 %experts.3.refs_6_ = bf16[1,512,1024]{2,1,0:T(8,128)(2,1)} custom-call(bf16[1,4096,1024]{2,1,0:T(8,128)(2,1)S(1)} %bitcast.4, bf16[1,4096,1024]{2,1,0:T(8,128)(2,1)S(1)} %copy-done, bf16[128,1024]{1,0:T(8,128)(2,1)S(1)} %collective-permute-done.6.refs_5_.refs_2_, ...), custom_call_target="tpu_custom_call", output_to_operand_aliasing={{}: (11, {})} | custom-call | flops 4294967296 | bytes 20975616 | tf_op jit(solution)/shard_map/experts/pallas_call | solution.py:126
  54.8 3.1 %back.1 = bf16[256,1024]{1,0:T(8,128)(2,1)} custom-call(f32[1,1024]{1,0:T(1,128)} %bitcast.5, f32[256,1024]{1,0:T(8,128)S(1)} %get-tuple-element.15.refs_1_, f32[256,1024]{1,0:T(8,128)S(1)} %get-tuple-element.16.refs_2_, f32[256,128]{1,0:T(8,128)S(1)} %get-tuple-element.17.refs_3_, f32[128,512]{1,0:T(8,128)S(1)} %get-tuple-element.24.refs_4_, ...), custom_call_target="tpu_custom_call" | custom-call | flops 1000000000 | bytes 3166208 | tf_op jit(solution)/shard_map/back/pallas_call | solution.py:126
  (26 shorter events, 0.1 us)
Async XLA Ops:
  0.6 7.3 %collective-permute-start.1 = (bf16[64,1024]{1,0:T(8,128)(2,1)}, bf16[64,1024]{1,0:T(8,128)(2,1)S(1)}, u32[]{:S(2)}, u32[]{:S(2)}) collective-permute-start(bf16[64,1024]{1,0:T(8,128)(2,1)} %refs_0_.6), channel_id=1, source_target_pairs={{0,8},{4,12},{8,0},{12,4},{16,24},{20,28},{24,16},{28,20},{1,9},{5... | collective-permute-start | bytes 393224 | tf_op jit(solution)/shard_map/ppermute | solution.py:501
  4.5 9.8 %collective-permute-start = (bf16[16,1280]{1,0:T(8,128)(2,1)S(1)}, bf16[16,1280]{1,0:T(8,128)(2,1)S(1)}, u32[]{:S(2)}, u32[]{:S(2)}) collective-permute-start(bf16[16,1280]{1,0:T(8,128)(2,1)S(1)} %ends.1), channel_id=1, source_target_pairs={{0,4},{4,8},{8,12},{12,16},{16,20},{20,24},{24,28},{1,5},{5,9},{9,... | collective-permute-start | bytes 122888 | tf_op jit(solution)/shard_map/ppermute | solution.py:641
  7.9 33.5 %slice-start = ((s8[8388608]{0:T(1024)(128)(4,1)}), s8[4194304]{0:T(1024)(128)(4,1)S(1)}, s32[]{:S(2)}) async-start(s8[8388608]{0:T(1024)(128)(4,1)} %bitcast.3), calls=%async_computation | async-start | bytes 8388608
  9.0 18.9 %collective-permute-start.6 = (bf16[128,1024]{1,0:T(8,128)(2,1)S(1)}, bf16[128,1024]{1,0:T(8,128)(2,1)S(1)}, u32[]{:S(2)}, u32[]{:S(2)}) collective-permute-start(bf16[128,1024]{1,0:T(8,128)(2,1)S(1)} %join.1.refs_9_.refs_2_), channel_id=1, source_target_pairs={{0,16},{4,20},{8,24},{12,28},{16,0},{20,4},{24,8},{28,12},{1,17},{... | collective-permute-start | bytes 786440 | tf_op jit(solution)/shard_map/ppermute | solution.py:501
  11.7 10.9 %collective-permute-start.3 = (bf16[128,1024]{1,0:T(8,128)(2,1)S(1)}, bf16[128,1024]{1,0:T(8,128)(2,1)S(1)}, u32[]{:S(2)}, u32[]{:S(2)}) collective-permute-start(bf16[128,1024]{1,0:T(8,128)(2,1)S(1)} %join.1.refs_9_.refs_2_), channel_id=1, source_target_pairs={{0,4},{4,0},{8,12},{12,8},{16,20},{20,16},{24,28},{28,24},{1,5},{5... | collective-permute-start | bytes 786440 | tf_op jit(solution)/shard_map/ppermute | solution.py:501
  12.8 15.1 %collective-permute-start.4 = (bf16[128,1024]{1,0:T(8,128)(2,1)S(1)}, bf16[128,1024]{1,0:T(8,128)(2,1)S(1)}, u32[]{:S(2)}, u32[]{:S(2)}) collective-permute-start(bf16[128,1024]{1,0:T(8,128)(2,1)S(1)} %join.1.refs_9_.refs_2_), channel_id=1, source_target_pairs={{0,2},{1,3},{2,0},{3,1},{4,6},{5,7},{6,4},{7,5},{8,10},{9,11},{10,... | collective-permute-start | bytes 786440 | tf_op jit(solution)/shard_map/ppermute | solution.py:501
  14.3 13.6 %collective-permute-start.5 = (bf16[128,1024]{1,0:T(8,128)(2,1)S(1)}, bf16[128,1024]{1,0:T(8,128)(2,1)S(1)}, u32[]{:S(2)}, u32[]{:S(2)}) collective-permute-start(bf16[128,1024]{1,0:T(8,128)(2,1)S(1)} %join.1.refs_9_.refs_2_), channel_id=1, source_target_pairs={{0,1},{1,0},{2,3},{3,2},{4,5},{5,4},{6,7},{7,6},{8,9},{9,8},{10,11... | collective-permute-start | bytes 786440 | tf_op jit(solution)/shard_map/ppermute | solution.py:501
  14.3 27.1 %slice-start.1 = ((s8[8388608]{0:T(1024)(128)(4,1)}), s8[4194304]{0:T(1024)(128)(4,1)S(1)}, s32[]{:S(2)}) async-start(s8[8388608]{0:T(1024)(128)(4,1)} %bitcast.3), calls=%async_computation.1 | async-start | bytes 8388608
  14.3 27.1 %copy-start = (bf16[1,4096,1024]{2,1,0:T(8,128)(2,1)S(1)}, bf16[1,4096,1024]{2,1,0:T(8,128)(2,1)}, u32[]{:S(2)}) copy-start(bf16[1,4096,1024]{2,1,0:T(8,128)(2,1)} %refs_1_.7) | copy-start | bytes 25165828
  21.6 6.3 %collective-permute-start.2 = (s16[144,512]{1,0:T(8,128)(2,1)S(1)}, s16[144,512]{1,0:T(8,128)(2,1)S(1)}, u32[]{:S(2)}, u32[]{:S(2)}) collective-permute-start(s16[144,512]{1,0:T(8,128)(2,1)S(1)} %get-tuple-element.19), channel_id=1, source_target_pairs={{0,4},{4,0},{8,12},{12,8},{16,20},{20,16},{24,28},{28,24},{1,5},{5... | collective-permute-start | bytes 442376 | tf_op jit(solution)/shard_map/ppermute | solution.py:501
  22.6 11.9 %collective-permute-start.14 = (bf16[128,1024]{1,0:T(8,128)(2,1)S(1)}, bf16[128,1024]{1,0:T(8,128)(2,1)S(1)}, u32[]{:S(2)}, u32[]{:S(2)}) collective-permute-start(bf16[128,1024]{1,0:T(8,128)(2,1)S(1)} %collective-permute-done.3.refs_2_.refs_3_), channel_id=1, source_target_pairs={{0,2},{1,3},{2,0},{3,1},{4,6},{5,7},{6,4},{7,5},{8,10},{9,11},{10,... | collective-permute-start | bytes 786440 | tf_op jit(solution)/shard_map/ppermute | solution.py:501
  28.1 5.5 %collective-permute-start.7 = (s16[144,512]{1,0:T(8,128)(2,1)S(1)}, s16[144,512]{1,0:T(8,128)(2,1)S(1)}, u32[]{:S(2)}, u32[]{:S(2)}) collective-permute-start(s16[144,512]{1,0:T(8,128)(2,1)S(1)} %get-tuple-element.21), channel_id=1, source_target_pairs={{0,8},{4,12},{8,0},{12,4},{16,24},{20,28},{24,16},{28,20},{1,9},{5... | collective-permute-start | bytes 442376 | tf_op jit(solution)/shard_map/ppermute | solution.py:501
  29.8 4.8 %collective-permute-start.13 = (bf16[128,1024]{1,0:T(8,128)(2,1)S(1)}, bf16[128,1024]{1,0:T(8,128)(2,1)S(1)}, u32[]{:S(2)}, u32[]{:S(2)}) collective-permute-start(bf16[128,1024]{1,0:T(8,128)(2,1)S(1)} %collective-permute-done.3.refs_2_.refs_3_), channel_id=1, source_target_pairs={{0,1},{1,0},{2,3},{3,2},{4,5},{5,4},{6,7},{7,6},{8,9},{9,8},{10,11... | collective-permute-start | bytes 786440 | tf_op jit(solution)/shard_map/ppermute | solution.py:501
  29.8 5.4 %collective-permute-start.15 = (bf16[128,1024]{1,0:T(8,128)(2,1)S(1)}, bf16[128,1024]{1,0:T(8,128)(2,1)S(1)}, u32[]{:S(2)}, u32[]{:S(2)}) collective-permute-start(bf16[128,1024]{1,0:T(8,128)(2,1)S(1)} %collective-permute-done.4.refs_3_.refs_6_), channel_id=1, source_target_pairs={{0,1},{1,0},{2,3},{3,2},{4,5},{5,4},{6,7},{7,6},{8,9},{9,8},{10,11... | collective-permute-start | bytes 786440 | tf_op jit(solution)/shard_map/ppermute | solution.py:501
  30.4 8.2 %collective-permute-start.9 = (bf16[128,1024]{1,0:T(8,128)(2,1)S(1)}, bf16[128,1024]{1,0:T(8,128)(2,1)S(1)}, u32[]{:S(2)}, u32[]{:S(2)}) collective-permute-start(bf16[128,1024]{1,0:T(8,128)(2,1)S(1)} %collective-permute-done.6.refs_5_.refs_2_), channel_id=1, source_target_pairs={{0,2},{1,3},{2,0},{3,1},{4,6},{5,7},{6,4},{7,5},{8,10},{9,11},{10,... | collective-permute-start | bytes 786440 | tf_op jit(solution)/shard_map/ppermute | solution.py:501
  33.6 7.3 %collective-permute-start.11 = (bf16[128,1024]{1,0:T(8,128)(2,1)S(1)}, bf16[128,1024]{1,0:T(8,128)(2,1)S(1)}, u32[]{:S(2)}, u32[]{:S(2)}) collective-permute-start(bf16[128,1024]{1,0:T(8,128)(2,1)S(1)} %collective-permute-done.6.refs_5_.refs_2_), channel_id=1, source_target_pairs={{0,4},{4,0},{8,12},{12,8},{16,20},{20,16},{24,28},{28,24},{1,5},{5... | collective-permute-start | bytes 786440 | tf_op jit(solution)/shard_map/ppermute | solution.py:501
  34.5 6.4 %collective-permute-start.16 = (bf16[128,1024]{1,0:T(8,128)(2,1)S(1)}, bf16[128,1024]{1,0:T(8,128)(2,1)S(1)}, u32[]{:S(2)}, u32[]{:S(2)}) collective-permute-start(bf16[128,1024]{1,0:T(8,128)(2,1)S(1)} %collective-permute-done.14.refs_7_), channel_id=1, source_target_pairs={{0,1},{1,0},{2,3},{3,2},{4,5},{5,4},{6,7},{7,6},{8,9},{9,8},{10,11... | collective-permute-start | bytes 786440 | tf_op jit(solution)/shard_map/ppermute | solution.py:501
  34.7 12.5 %collective-permute-start.12 = (bf16[128,1024]{1,0:T(8,128)(2,1)S(1)}, bf16[128,1024]{1,0:T(8,128)(2,1)S(1)}, u32[]{:S(2)}, u32[]{:S(2)}) collective-permute-start(bf16[128,1024]{1,0:T(8,128)(2,1)S(1)} %collective-permute-done.6.refs_5_.refs_2_), channel_id=1, source_target_pairs={{0,1},{1,0},{2,3},{3,2},{4,5},{5,4},{6,7},{7,6},{8,9},{9,8},{10,11... | collective-permute-start | bytes 786440 | tf_op jit(solution)/shard_map/ppermute | solution.py:501
  35.2 11.9 %collective-permute-start.8 = (s16[144,512]{1,0:T(8,128)(2,1)S(1)}, s16[144,512]{1,0:T(8,128)(2,1)S(1)}, u32[]{:S(2)}, u32[]{:S(2)}) collective-permute-start(s16[144,512]{1,0:T(8,128)(2,1)S(1)} %get-tuple-element.22), channel_id=1, source_target_pairs={{0,16},{4,20},{8,24},{12,28},{16,0},{20,4},{24,8},{28,12},{1,17},{... | collective-permute-start | bytes 442376 | tf_op jit(solution)/shard_map/ppermute | solution.py:501
  38.6 8.6 %collective-permute-start.10 = (bf16[128,1024]{1,0:T(8,128)(2,1)S(1)}, bf16[128,1024]{1,0:T(8,128)(2,1)S(1)}, u32[]{:S(2)}, u32[]{:S(2)}) collective-permute-start(bf16[128,1024]{1,0:T(8,128)(2,1)S(1)} %collective-permute-done.9.refs_7_.refs_6_), channel_id=1, source_target_pairs={{0,4},{4,0},{8,12},{12,8},{16,20},{20,16},{24,28},{28,24},{1,5},{5... | collective-permute-start | bytes 786440 | tf_op jit(solution)/shard_map/ppermute | solution.py:501
  40.9 8.1 %collective-permute-start.19 = (bf16[128,1024]{1,0:T(8,128)(2,1)S(1)}, bf16[128,1024]{1,0:T(8,128)(2,1)S(1)}, u32[]{:S(2)}, u32[]{:S(2)}) collective-permute-start(bf16[128,1024]{1,0:T(8,128)(2,1)S(1)} %collective-permute-done.9.refs_7_.refs_6_), channel_id=1, source_target_pairs={{0,1},{1,0},{2,3},{3,2},{4,5},{5,4},{6,7},{7,6},{8,9},{9,8},{10,11... | collective-permute-start | bytes 786440 | tf_op jit(solution)/shard_map/ppermute | solution.py:501
  40.9 8.1 %collective-permute-start.18 = (bf16[128,1024]{1,0:T(8,128)(2,1)S(1)}, bf16[128,1024]{1,0:T(8,128)(2,1)S(1)}, u32[]{:S(2)}, u32[]{:S(2)}) collective-permute-start(bf16[128,1024]{1,0:T(8,128)(2,1)S(1)} %collective-permute-done.11.refs_6_.refs_3_), channel_id=1, source_target_pairs={{0,1},{1,0},{2,3},{3,2},{4,5},{5,4},{6,7},{7,6},{8,9},{9,8},{10,11... | collective-permute-start | bytes 786440 | tf_op jit(solution)/shard_map/ppermute | solution.py:501
  47.5 1.6 %collective-permute-start.20 = (bf16[128,1024]{1,0:T(8,128)(2,1)S(1)}, bf16[128,1024]{1,0:T(8,128)(2,1)S(1)}, u32[]{:S(2)}, u32[]{:S(2)}) collective-permute-start(bf16[128,1024]{1,0:T(8,128)(2,1)S(1)} %get-tuple-element.26), channel_id=1, source_target_pairs={{0,1},{1,0},{2,3},{3,2},{4,5},{5,4},{6,7},{7,6},{8,9},{9,8},{10,11... | collective-permute-start | bytes 786440 | tf_op jit(solution)/shard_map/ppermute | solution.py:501
  47.6 7.2 %collective-permute-start.17 = (s16[144,512]{1,0:T(8,128)(2,1)S(1)}, s16[144,512]{1,0:T(8,128)(2,1)S(1)}, u32[]{:S(2)}, u32[]{:S(2)}) collective-permute-start(s16[144,512]{1,0:T(8,128)(2,1)S(1)} %get-tuple-element.25), channel_id=1, source_target_pairs={{0,4},{4,0},{8,12},{12,8},{16,20},{20,16},{24,28},{28,24},{1,5},{5... | collective-permute-start | bytes 442376 | tf_op jit(solution)/shard_map/ppermute | solution.py:501

commit v10 on v9

--- a/solution.py
+++ b/solution.py
@@ -300,7 +300,14 @@
     ids_ref[...] = ids
 
 
-def four_body(width, pair_ref, got_ref, sent_ref, ids_ref):
+def join_rows(pieces, joined_ref):
+    rows = pieces[0].shape[0]
+    for i, piece in enumerate(pieces):
+        joined_ref[i * rows : (i + 1) * rows] = piece[...]
+
+
+def four_body(width, pair_ref, got_ref, a, b, c, d, sent_ref, ids_ref, joined_ref):
+    join_rows((a, b, c, d), joined_ref)
     _, z, _ = place()
     four = together(z == 0, taken(pair_ref), received(got_ref), 2 * width)
     send(sent_ref, *four)
@@ -314,13 +321,16 @@
     pair_ref,
     pair_got_ref,
     four_got_ref,
-    rows_ref,
+    a,
+    b,
+    c,
+    d,
     mine_ref,
     sent_ref,
     ids_ref,
-    same_rows_ref,
+    joined_ref,
 ):
-    same_rows_ref[...] = rows_ref[...]
+    join_rows((a, b, c, d), joined_ref)
     x, z, zz = place()
     pair, pair_got, four_got = taken(pair_ref), received(pair_got_ref), received(four_got_ref)
     line = together(z == 0, pair, pair_got, 2 * width)[2]
@@ -374,39 +384,39 @@
     finished(copies)
 
 
-def entering_by_pairs(keep, sent, width, after, meanwhile, late_rows):
+def entering_by_pairs(keep, sent, width, follow, pieces, meanwhile):
     pair_array, sent_array = array(keep.shape, F32), array(sent.shape, jnp.int16)
     ids_array = array((8, width), F32)
+    joined_array = [array((4 * p[0].shape[0], p[0].shape[1]), BF16) for p in pieces]
     got = swapped(sent, "ctx", 1)
     pair, sent = call(
         functools.partial(pair_body, width),
         [pair_array, sent_array],
         (keep, got),
         near=True,
-        after=after[0],
+        after=follow,
         name="pair",
     )
     pair_got = swapped(sent, "ctx", 2)
-    sent, ids = call(
+    sent, ids, joined = call(
         functools.partial(four_body, width),
-        [sent_array, ids_array],
-        (pair, pair_got),
+        [sent_array, ids_array, joined_array[0]],
+        (pair, pair_got, *pieces[0]),
         near=True,
-        after=after[1],
+        after=pieces[1][1:3],
         name="four",
     )
     four_got = swapped(sent, "ctx", 4)
-    done = meanwhile(ids)
-    mine, sent, ids, late_rows = call(
+    done = meanwhile(ids, joined)
+    mine, sent, ids, joined = call(
         functools.partial(turn_body, width),
-        [array((STATE, keep.shape[1]), F32), sent_array, ids_array, late_rows],
-        (keep, got, pair, pair_got, four_got, late_rows),
+        [array((STATE, keep.shape[1]), F32), sent_array, ids_array, joined_array[1]],
+        (keep, got, pair, pair_got, four_got, *pieces[1]),
         near=True,
-        after=after[2],
         after_far=(done,),
         name="turn",
     )
-    return (mine, swapped(sent, "ctx", 1)), ids, (done, late_rows)
+    return (mine, swapped(sent, "ctx", 1)), ids, joined, done
 
 
 def entering_by_rows(state):
@@ -426,12 +436,12 @@
 
 
 def mixing(
-    after, meanwhile, late_rows, seq_input, b_input, c_input, before, conv_x, conv_bc, log_decay, skip, gain, ids
+    pieces, meanwhile, seq_input, b_input, c_input, before, conv_x, conv_bc, log_decay, skip, gain, ids
 ):
     tokens, channels = seq_input.shape
     heads = skip.shape[0]
     width = 2 * ids.shape[0]
-    paired = after is not None
+    paired = pieces is not None
     outs = [
         array((tokens, channels), F32),
         array((tokens, channels), F32),
@@ -450,22 +460,19 @@
         args,
         fixed=len(args) - 1,
         near_outs=len(ends),
-        after=after[0] if paired else (),
+        after=pieces[0][:1] if paired else (),
         scratch=room(args) + room(outs) + [pltpu.VMEM((8 + tokens, channels + 2 * STATE), F32)],
         sems=len(args),
         flops=5 * 10**9,
         grant=20,
         name="local",
     )
-    done = None
+    late = None
     if paired:
-        first, second, third = after[1:]
-        after = (first, second, third)
-        starts, lines_of_ids, done = entering_by_pairs(
-            *ends, width, after, meanwhile, late_rows
-        )
+        follow = (*pieces[0][1:3], pieces[1][0])
+        starts, *late = entering_by_pairs(*ends, width, follow, pieces, meanwhile)
     else:
-        starts, lines_of_ids = (entering_by_rows(ends[0]),), None
+        starts = (entering_by_rows(ends[0]),)
 
     def finish(after=()):
         args = (gain.reshape(1, channels), pre, decay, cmat)
@@ -484,7 +491,7 @@
             name="back",
         )[0]
 
-    return finish, lines_of_ids, done
+    return finish, late
 
 
 TILE = 512
@@ -502,11 +509,11 @@
 
 
 def expert_body(part, w_gate, w_up, *refs):
-    far, ids_ref, out_far = refs[:8], refs[8], refs[9 + part]
-    pick_ref, hid_ref, out_ref, sems = refs[10 + part :]
+    pieces, joined_ref, ids_ref, out_far = refs[:4], refs[4], refs[5], refs[6 + part]
+    pick_ref, hid_ref, out_ref, sems = refs[7 + part :]
     length, hidden = out_ref.shape
-    rows = far[0].shape[0] // 2
-    depth = far[0].shape[1]
+    rows = pieces[0].shape[0] // 2
+    depth = pieces[0].shape[1]
     me = lax.axis_index("exp")
     here = lax.axis_index("ctx")
     downs = [pl.ds(pl.multiple_of((me ^ k) * depth, depth), depth) for k in range(4)]
@@ -531,7 +538,10 @@
         cut = slice(n * TILE, (n + 1) * TILE)
         gate = upper = None
         for k in range(4):
-            block = jnp.concatenate([piece[...] for piece in far[2 * k : 2 * k + 2]], axis=0)
+            if k % 2 == 0:
+                block = jnp.concatenate([piece[...] for piece in pieces[k : k + 2]], axis=0)
+            else:
+                block = joined_ref[k // 2 * length : (k // 2 + 1) * length]
             more = dot16(block, w_gate[0, downs[k], cut])
             gate = more if k == 0 else gate + more
             more = dot16(block, w_up[0, downs[k], cut])
@@ -562,18 +572,14 @@
     x = [swapped(a, "ctx", 1) for a in z]
     y = [swapped(a, "exp", 2) for a in z]
     d = (swapped(x[0], "exp", 2), swapped(y[1], "ctx", 1))
-    halves_of_rows = []
-    for i, pieces in enumerate(zip(z, x, y, d)):
-        beside = [swapped(a, "exp", 1) for a in pieces[: 4 - i]]
-        halves_of_rows.append([*pieces[:2], *beside[:2], *pieces[2:], *beside[2:]])
-    return halves_of_rows
-
-
-def experts_by_tokens(part, pieces, ids, w_gate, w_up, so_far):
+    return list(zip(z, x, y, d))
+
+
+def experts_by_tokens(part, pieces, joined, ids, w_gate, w_up, so_far):
     rows = pieces[0].shape[0] // 2
     length = 4 * rows
     hidden = w_gate.shape[2]
-    args = (w_gate, w_up, *pieces, ids)
+    args = (w_gate, w_up, *pieces, swapped(joined, "exp", 1), ids)
     return call(
         functools.partial(expert_body, part),
         [pltpu.HBM((1, 2 * length, hidden), BF16)],
@@ -639,20 +645,16 @@
         name="ends",
     )[0]
     before = lax.ppermute(ends, "ctx", [(i, i + 1) for i in range(ctx - 1)])
-    follow = meanwhile = late_rows = None
+    pieces = meanwhile = None
     if by_tokens:
-        one, two = gathered(moe_input)
-        follow = (one[:1], (one[1], one[4], one[2], two[0]), ())
-        follow += ((two[1], two[4], two[2]),)
-        late_rows = two[5]
-
-        def meanwhile(ids):
-            return experts_by_tokens(0, one, ids, w_gate, w_up, None)
-
-    finish, ids, done = mixing(
-        follow,
+        pieces = gathered(moe_input)
+
+        def meanwhile(ids, joined):
+            return experts_by_tokens(0, pieces[0], joined, ids, w_gate, w_up, None)
+
+    finish, late = mixing(
+        pieces,
         meanwhile,
-        late_rows,
         seq_input,
         b_input,
         c_input,
@@ -665,9 +667,8 @@
         expert_ids,
     )
     if by_tokens:
-        hidden, late_rows = done
-        two.append(swapped(late_rows, "exp", 1))
-        hidden = experts_by_tokens(1, two, ids, w_gate, w_up, hidden)
+        ids, joined, hidden = late
+        hidden = experts_by_tokens(1, pieces[1], joined, ids, w_gate, w_up, hidden)
         mixed = finish((hidden,))
     else:
         mixed = finish()

time: 58.7 us -> 59.4 us (1.012)
  waiting for transfers between devices: 12.6 us -> 14.9 us
  starting transfers between devices: 20.3 us -> 19.1 us
    ppermute x20 -> x14, waiting for transfers between devices: 12.6 us -> 14.9 us  [swapped(): lax.ppermute(block, axis, [(i, i ^ bit) for i in range(lax.axis_size(axis...]
    ppermute x20 -> x14, starting transfers between devices: 16.9 us -> 15.7 us  [swapped(): lax.ppermute(block, axis, [(i, i ^ bit) for i in range(lax.axis_size(axis...]
  transfers between devices with their start and end apart: 21 -> 15, of which waited for: 5 -> 7; matrix products, arithmetic and copies ran while one was open for 0% -> 0% of each run, Pallas kernels for 36% -> 35%
where the time goes in v10:
time: 59.4 us; the launch traced here: 59.2 us
  Pallas kernels  24.3 us (41%)
  starting transfers between devices  19.1 us (32%)
  waiting for transfers between devices  14.9 us (25%)
  between operations  0.95 us (2%)
    pallas_call x9, Pallas kernels, call(): pl.pallas_call(body, out_shape=outs, in_specs=[pl.BlockSpec(memory_space=...  24.3 us
    ppermute x14, starting transfers between devices, swapped(): lax.ppermute(block, axis, [(i, i ^ bit) for i in range(lax.axis_size(axis...  15.7 us
    ppermute x14, waiting for transfers between devices, swapped(): lax.ppermute(block, axis, [(i, i ^ bit) for i in range(lax.axis_size(axis...  14.9 us
    ppermute x1, starting transfers between devices, on_device(): before = lax.ppermute(ends, 'ctx', [(i, i + 1) for i in range(ctx - 1)])  3.4 us
  transfers between devices with their start and end apart: 15, of which 7 were waited for; matrix products, arithmetic and copies ran while one was open for 0% of the time, Pallas kernels for 35%

profile of v10, /device:TPU:0, one launch (start us, length us, event | category | flops | bytes accessed | tf_op | source)
XLA Modules:
  0.0 59.2 jit_solution(11394898207005065159)
XLA Ops:
  0.6 3.1 %collective-permute-start.1 = (bf16[64,1024]{1,0:T(8,128)(2,1)}, bf16[64,1024]{1,0:T(8,128)(2,1)S(1)}, u32[]{:S(2)}, u32[]{:S(2)}) collective-permute-start(bf16[64,1024]{1,0:T(8,128)(2,1)} %refs_0_.6), channel_id=1, source_target_pairs={{0,8},{4,12},{8,0},{12,4},{16,24},{20,28},{24,16},{28,20},{1,9},{5... | collective-permute-start | bytes 393224 | tf_op jit(solution)/shard_map/ppermute | solution.py:508
  3.7 0.8 %ends.1 = bf16[16,1280]{1,0:T(8,128)(2,1)S(1)} custom-call(bf16[256,1024]{1,0:T(8,128)(2,1)} %refs_0_.7, bf16[256,128]{1,0:T(8,128)(2,1)} %refs_1_.5, bf16[256,128]{1,0:T(8,128)(2,1)} %refs_2_.3), custom_call_target="tpu_custom_call" | custom-call | bytes 696320 | tf_op jit(solution)/shard_map/ends/pallas_call | solution.py:126
  4.5 3.4 %collective-permute-start = (bf16[16,1280]{1,0:T(8,128)(2,1)S(1)}, bf16[16,1280]{1,0:T(8,128)(2,1)S(1)}, u32[]{:S(2)}, u32[]{:S(2)}) collective-permute-start(bf16[16,1280]{1,0:T(8,128)(2,1)S(1)} %ends.1), channel_id=1, source_target_pairs={{0,4},{4,8},{8,12},{12,16},{16,20},{20,24},{24,28},{1,5},{5,9},{9,... | collective-permute-start | bytes 122888 | tf_op jit(solution)/shard_map/ppermute | solution.py:647
  7.9 0.0 slice-start
  7.9 1.1 %join.1.refs_9_.refs_2_ = bf16[128,1024]{1,0:T(8,128)(2,1)S(1)} custom-call(bf16[64,1024]{1,0:T(8,128)(2,1)} %refs_0_.6, bf16[64,1024]{1,0:T(8,128)(2,1)S(1)} %collective-permute-done.1.refs_1_), custom_call_target="tpu_custom_call" | custom-call | bytes 524288 | tf_op jit(solution)/shard_map/join/pallas_call | solution.py:126
  9.0 2.7 %collective-permute-start.5 = (bf16[128,1024]{1,0:T(8,128)(2,1)S(1)}, bf16[128,1024]{1,0:T(8,128)(2,1)S(1)}, u32[]{:S(2)}, u32[]{:S(2)}) collective-permute-start(bf16[128,1024]{1,0:T(8,128)(2,1)S(1)} %join.1.refs_9_.refs_2_), channel_id=1, source_target_pairs={{0,16},{4,20},{8,24},{12,28},{16,0},{20,4},{24,8},{28,12},{1,17},{... | collective-permute-start | bytes 786440 | tf_op jit(solution)/shard_map/ppermute | solution.py:508
  11.7 1.1 %collective-permute-start.3 = (bf16[128,1024]{1,0:T(8,128)(2,1)S(1)}, bf16[128,1024]{1,0:T(8,128)(2,1)S(1)}, u32[]{:S(2)}, u32[]{:S(2)}) collective-permute-start(bf16[128,1024]{1,0:T(8,128)(2,1)S(1)} %join.1.refs_9_.refs_2_), channel_id=1, source_target_pairs={{0,4},{4,0},{8,12},{12,8},{16,20},{20,16},{24,28},{28,24},{1,5},{5... | collective-permute-start | bytes 786440 | tf_op jit(solution)/shard_map/ppermute | solution.py:508
  12.8 1.5 %collective-permute-start.4 = (bf16[128,1024]{1,0:T(8,128)(2,1)S(1)}, bf16[128,1024]{1,0:T(8,128)(2,1)S(1)}, u32[]{:S(2)}, u32[]{:S(2)}) collective-permute-start(bf16[128,1024]{1,0:T(8,128)(2,1)S(1)} %join.1.refs_9_.refs_2_), channel_id=1, source_target_pairs={{0,2},{1,3},{2,0},{3,1},{4,6},{5,7},{6,4},{7,5},{8,10},{9,11},{10,... | collective-permute-start | bytes 786440 | tf_op jit(solution)/shard_map/ppermute | solution.py:508
  14.3 7.2 %local.1 = (f32[256,1024]{1,0:T(8,128)S(1)}, f32[256,1024]{1,0:T(8,128)S(1)}, f32[256,128]{1,0:T(8,128)S(1)}, f32[136,512]{1,0:T(8,128)S(1)}, s16[144,512]{1,0:T(8,128)(2,1)S(1)}) custom-call(bf16[256,1024]{1,0:T(8,128)(2,1)} %refs_0_.7, bf16[256,128]{1,0:T(8,128)(2,1)} %refs_1_.5, bf16[256,128]{1,0:T(8,128)(2,1)} %refs_2_.3, f32[4,1024]{1,0:T(4,128)} %refs_3_.1, ...), custom_call_target="tpu_custom_call" | custom-call | flops 5000000000 | bytes 3387968 | tf_op jit(solution)/shard_map/local/pallas_call | solution.py:126
  21.6 1.0 %collective-permute-start.2 = (s16[144,512]{1,0:T(8,128)(2,1)S(1)}, s16[144,512]{1,0:T(8,128)(2,1)S(1)}, u32[]{:S(2)}, u32[]{:S(2)}) collective-permute-start(s16[144,512]{1,0:T(8,128)(2,1)S(1)} %get-tuple-element.20), channel_id=1, source_target_pairs={{0,4},{4,0},{8,12},{12,8},{16,20},{20,16},{24,28},{28,24},{1,5},{5... | collective-permute-start | bytes 442376 | tf_op jit(solution)/shard_map/ppermute | solution.py:508
  22.5 0.6 collective-permute-done.5.refs_4_.refs_5_.refs_2_
  23.1 1.5 %collective-permute-start.9 = (bf16[128,1024]{1,0:T(8,128)(2,1)S(1)}, bf16[128,1024]{1,0:T(8,128)(2,1)S(1)}, u32[]{:S(2)}, u32[]{:S(2)}) collective-permute-start(bf16[128,1024]{1,0:T(8,128)(2,1)S(1)} %collective-permute-done.5.refs_4_.refs_5_.refs_2_), channel_id=1, source_target_pairs={{0,2},{1,3},{2,0},{3,1},{4,6},{5,7},{6,4},{7,5},{8,10},{9,11},{10,... | collective-permute-start | bytes 786440 | tf_op jit(solution)/shard_map/ppermute | solution.py:508
  24.6 0.8 %collective-permute-start.8 = (bf16[128,1024]{1,0:T(8,128)(2,1)S(1)}, bf16[128,1024]{1,0:T(8,128)(2,1)S(1)}, u32[]{:S(2)}, u32[]{:S(2)}) collective-permute-start(bf16[128,1024]{1,0:T(8,128)(2,1)S(1)} %collective-permute-done.5.refs_4_.refs_5_.refs_2_), channel_id=1, source_target_pairs={{0,4},{4,0},{8,12},{12,8},{16,20},{20,16},{24,28},{28,24},{1,5},{5... | collective-permute-start | bytes 786440 | tf_op jit(solution)/shard_map/ppermute | solution.py:508
  25.4 0.5 collective-permute-start.7
  26.0 1.1 %collective-permute-done.2.refs_1_ = s16[144,512]{1,0:T(8,128)(2,1)S(1)} collective-permute-done((s16[144,512]{1,0:T(8,128)(2,1)S(1)}, s16[144,512]{1,0:T(8,128)(2,1)S(1)}, u32[]{:S(2)}, u32[]{:S(2)}) %collective-permute-start.2) | collective-permute-done | bytes 147488 | tf_op jit(solution)/shard_map/ppermute | solution.py:508
  27.0 0.1 pair.1
  27.2 3.1 %collective-permute-start.6 = (s16[144,512]{1,0:T(8,128)(2,1)S(1)}, s16[144,512]{1,0:T(8,128)(2,1)S(1)}, u32[]{:S(2)}, u32[]{:S(2)}) collective-permute-start(s16[144,512]{1,0:T(8,128)(2,1)S(1)} %get-tuple-element.22), channel_id=1, source_target_pairs={{0,8},{4,12},{8,0},{12,4},{16,24},{20,28},{24,16},{28,20},{1,9},{5... | collective-permute-start | bytes 442376 | tf_op jit(solution)/shard_map/ppermute | solution.py:508
  30.3 3.1 %collective-permute-done.6.refs_1_.refs_3_ = s16[144,512]{1,0:T(8,128)(2,1)S(1)} collective-permute-done((s16[144,512]{1,0:T(8,128)(2,1)S(1)}, s16[144,512]{1,0:T(8,128)(2,1)S(1)}, u32[]{:S(2)}, u32[]{:S(2)}) %collective-permute-start.6) | collective-permute-done | bytes 147488 | tf_op jit(solution)/shard_map/ppermute | solution.py:508
  33.4 3.1 %collective-permute-done.7.refs_5_ = bf16[128,1024]{1,0:T(8,128)(2,1)S(1)} collective-permute-done((bf16[128,1024]{1,0:T(8,128)(2,1)S(1)}, bf16[128,1024]{1,0:T(8,128)(2,1)S(1)}, u32[]{:S(2)}, u32[]{:S(2)}) %collective-permute-start.7) | collective-permute-done | bytes 262176 | tf_op jit(solution)/shard_map/ppermute | solution.py:508
  36.5 0.2 four.1
  36.7 0.1 collective-permute-start.12
  36.8 0.1 collective-permute-start.10
  36.9 0.1 collective-permute-start.11
  37.0 2.5 %collective-permute-done.12.refs_6_ = bf16[512,1024]{1,0:T(8,128)(2,1)S(1)} collective-permute-done((bf16[512,1024]{1,0:T(8,128)(2,1)S(1)}, bf16[512,1024]{1,0:T(8,128)(2,1)S(1)}, u32[]{:S(2)}, u32[]{:S(2)}) %collective-permute-start.12) | collective-permute-done | bytes 1048608 | tf_op jit(solution)/shard_map/ppermute | solution.py:508
  39.5 5.7 %experts.2.refs_9_.refs_8_ = bf16[1,512,1024]{2,1,0:T(8,128)(2,1)} custom-call(bf16[1,4096,1024]{2,1,0:T(8,128)(2,1)S(1)} %bitcast.4, bf16[1,4096,1024]{2,1,0:T(8,128)(2,1)S(1)} %copy-done, bf16[128,1024]{1,0:T(8,128)(2,1)S(1)} %join.1.refs_9_.refs_2_, bf16[128,1024]{1,0:T(8,128)(2,1)S(1)} %collective-permute-done.3.refs_2_.refs_3_, ...), custom_call_target="tpu_custom_call" | custom-call | flops 4294967296 | bytes 19927040 | tf_op jit(solution)/shard_map/experts/pallas_call | solution.py:126
  45.2 2.0 %collective-permute-done.10.refs_4_ = s16[144,512]{1,0:T(8,128)(2,1)S(1)} collective-permute-done((s16[144,512]{1,0:T(8,128)(2,1)S(1)}, s16[144,512]{1,0:T(8,128)(2,1)S(1)}, u32[]{:S(2)}, u32[]{:S(2)}) %collective-permute-start.10) | collective-permute-done | bytes 147488 | tf_op jit(solution)/shard_map/ppermute | solution.py:508
  47.1 0.4 turn.1
  47.5 0.1 collective-permute-start.14
  47.6 0.1 collective-permute-start.13
  47.7 2.6 %collective-permute-done.14.refs_6_ = bf16[512,1024]{1,0:T(8,128)(2,1)S(1)} collective-permute-done((bf16[512,1024]{1,0:T(8,128)(2,1)S(1)}, bf16[512,1024]{1,0:T(8,128)(2,1)S(1)}, u32[]{:S(2)}, u32[]{:S(2)}) %collective-permute-start.14) | collective-permute-done | bytes 1048608 | tf_op jit(solution)/shard_map/ppermute | solution.py:508
  50.3 5.7 %experts.3.refs_6_ = bf16[1,512,1024]{2,1,0:T(8,128)(2,1)} custom-call(bf16[1,4096,1024]{2,1,0:T(8,128)(2,1)S(1)} %bitcast.4, bf16[1,4096,1024]{2,1,0:T(8,128)(2,1)S(1)} %copy-done, bf16[128,1024]{1,0:T(8,128)(2,1)S(1)} %collective-permute-done.5.refs_4_.refs_5_.refs_2_, ...), custom_call_target="tpu_custom_call", output_to_operand_aliasing={{}: (8, {})} | custom-call | flops 4294967296 | bytes 20975616 | tf_op jit(solution)/shard_map/experts/pallas_call | solution.py:126
  55.9 3.1 %back.1 = bf16[256,1024]{1,0:T(8,128)(2,1)} custom-call(f32[1,1024]{1,0:T(1,128)} %bitcast.5, f32[256,1024]{1,0:T(8,128)S(1)} %get-tuple-element.16.refs_1_, f32[256,1024]{1,0:T(8,128)S(1)} %get-tuple-element.17.refs_2_, f32[256,128]{1,0:T(8,128)S(1)} %get-tuple-element.18.refs_3_, f32[128,512]{1,0:T(8,128)S(1)} %get-tuple-element.26.refs_4_, ...), custom_call_target="tpu_custom_call" | custom-call | flops 1000000000 | bytes 3166208 | tf_op jit(solution)/shard_map/back/pallas_call | solution.py:126
  (14 shorter events, 0.0 us)
Async XLA Ops:
  0.6 7.3 %collective-permute-start.1 = (bf16[64,1024]{1,0:T(8,128)(2,1)}, bf16[64,1024]{1,0:T(8,128)(2,1)S(1)}, u32[]{:S(2)}, u32[]{:S(2)}) collective-permute-start(bf16[64,1024]{1,0:T(8,128)(2,1)} %refs_0_.6), channel_id=1, source_target_pairs={{0,8},{4,12},{8,0},{12,4},{16,24},{20,28},{24,16},{28,20},{1,9},{5... | collective-permute-start | bytes 393224 | tf_op jit(solution)/shard_map/ppermute | solution.py:508
  4.5 9.8 %collective-permute-start = (bf16[16,1280]{1,0:T(8,128)(2,1)S(1)}, bf16[16,1280]{1,0:T(8,128)(2,1)S(1)}, u32[]{:S(2)}, u32[]{:S(2)}) collective-permute-start(bf16[16,1280]{1,0:T(8,128)(2,1)S(1)} %ends.1), channel_id=1, source_target_pairs={{0,4},{4,8},{8,12},{12,16},{16,20},{20,24},{24,28},{1,5},{5,9},{9,... | collective-permute-start | bytes 122888 | tf_op jit(solution)/shard_map/ppermute | solution.py:647
  7.9 31.5 %slice-start = ((s8[8388608]{0:T(1024)(128)(4,1)}), s8[4194304]{0:T(1024)(128)(4,1)S(1)}, s32[]{:S(2)}) async-start(s8[8388608]{0:T(1024)(128)(4,1)} %bitcast.3), calls=%async_computation | async-start | bytes 8388608
  9.0 14.1 %collective-permute-start.5 = (bf16[128,1024]{1,0:T(8,128)(2,1)S(1)}, bf16[128,1024]{1,0:T(8,128)(2,1)S(1)}, u32[]{:S(2)}, u32[]{:S(2)}) collective-permute-start(bf16[128,1024]{1,0:T(8,128)(2,1)S(1)} %join.1.refs_9_.refs_2_), channel_id=1, source_target_pairs={{0,16},{4,20},{8,24},{12,28},{16,0},{20,4},{24,8},{28,12},{1,17},{... | collective-permute-start | bytes 786440 | tf_op jit(solution)/shard_map/ppermute | solution.py:508
  11.7 13.8 %collective-permute-start.3 = (bf16[128,1024]{1,0:T(8,128)(2,1)S(1)}, bf16[128,1024]{1,0:T(8,128)(2,1)S(1)}, u32[]{:S(2)}, u32[]{:S(2)}) collective-permute-start(bf16[128,1024]{1,0:T(8,128)(2,1)S(1)} %join.1.refs_9_.refs_2_), channel_id=1, source_target_pairs={{0,4},{4,0},{8,12},{12,8},{16,20},{20,16},{24,28},{28,24},{1,5},{5... | collective-permute-start | bytes 786440 | tf_op jit(solution)/shard_map/ppermute | solution.py:508
  12.8 14.2 %collective-permute-start.4 = (bf16[128,1024]{1,0:T(8,128)(2,1)S(1)}, bf16[128,1024]{1,0:T(8,128)(2,1)S(1)}, u32[]{:S(2)}, u32[]{:S(2)}) collective-permute-start(bf16[128,1024]{1,0:T(8,128)(2,1)S(1)} %join.1.refs_9_.refs_2_), channel_id=1, source_target_pairs={{0,2},{1,3},{2,0},{3,1},{4,6},{5,7},{6,4},{7,5},{8,10},{9,11},{10,... | collective-permute-start | bytes 786440 | tf_op jit(solution)/shard_map/ppermute | solution.py:508
  14.3 25.1 %slice-start.1 = ((s8[8388608]{0:T(1024)(128)(4,1)}), s8[4194304]{0:T(1024)(128)(4,1)S(1)}, s32[]{:S(2)}) async-start(s8[8388608]{0:T(1024)(128)(4,1)} %bitcast.3), calls=%async_computation.1 | async-start | bytes 8388608
  14.3 25.1 %copy-start = (bf16[1,4096,1024]{2,1,0:T(8,128)(2,1)S(1)}, bf16[1,4096,1024]{2,1,0:T(8,128)(2,1)}, u32[]{:S(2)}) copy-start(bf16[1,4096,1024]{2,1,0:T(8,128)(2,1)} %refs_1_.7) | copy-start | bytes 25165828
  21.6 5.4 %collective-permute-start.2 = (s16[144,512]{1,0:T(8,128)(2,1)S(1)}, s16[144,512]{1,0:T(8,128)(2,1)S(1)}, u32[]{:S(2)}, u32[]{:S(2)}) collective-permute-start(s16[144,512]{1,0:T(8,128)(2,1)S(1)} %get-tuple-element.20), channel_id=1, source_target_pairs={{0,4},{4,0},{8,12},{12,8},{16,20},{20,16},{24,28},{28,24},{1,5},{5... | collective-permute-start | bytes 442376 | tf_op jit(solution)/shard_map/ppermute | solution.py:508
  23.1 10.3 %collective-permute-start.9 = (bf16[128,1024]{1,0:T(8,128)(2,1)S(1)}, bf16[128,1024]{1,0:T(8,128)(2,1)S(1)}, u32[]{:S(2)}, u32[]{:S(2)}) collective-permute-start(bf16[128,1024]{1,0:T(8,128)(2,1)S(1)} %collective-permute-done.5.refs_4_.refs_5_.refs_2_), channel_id=1, source_target_pairs={{0,2},{1,3},{2,0},{3,1},{4,6},{5,7},{6,4},{7,5},{8,10},{9,11},{10,... | collective-permute-start | bytes 786440 | tf_op jit(solution)/shard_map/ppermute | solution.py:508
  24.6 8.8 %collective-permute-start.8 = (bf16[128,1024]{1,0:T(8,128)(2,1)S(1)}, bf16[128,1024]{1,0:T(8,128)(2,1)S(1)}, u32[]{:S(2)}, u32[]{:S(2)}) collective-permute-start(bf16[128,1024]{1,0:T(8,128)(2,1)S(1)} %collective-permute-done.5.refs_4_.refs_5_.refs_2_), channel_id=1, source_target_pairs={{0,4},{4,0},{8,12},{12,8},{16,20},{20,16},{24,28},{28,24},{1,5},{5... | collective-permute-start | bytes 786440 | tf_op jit(solution)/shard_map/ppermute | solution.py:508
  25.4 11.1 %collective-permute-start.7 = (bf16[128,1024]{1,0:T(8,128)(2,1)S(1)}, bf16[128,1024]{1,0:T(8,128)(2,1)S(1)}, u32[]{:S(2)}, u32[]{:S(2)}) collective-permute-start(bf16[128,1024]{1,0:T(8,128)(2,1)S(1)} %collective-permute-done.3.refs_2_.refs_3_), channel_id=1, source_target_pairs={{0,2},{1,3},{2,0},{3,1},{4,6},{5,7},{6,4},{7,5},{8,10},{9,11},{10,... | collective-permute-start | bytes 786440 | tf_op jit(solution)/shard_map/ppermute | solution.py:508
  27.2 6.3 %collective-permute-start.6 = (s16[144,512]{1,0:T(8,128)(2,1)S(1)}, s16[144,512]{1,0:T(8,128)(2,1)S(1)}, u32[]{:S(2)}, u32[]{:S(2)}) collective-permute-start(s16[144,512]{1,0:T(8,128)(2,1)S(1)} %get-tuple-element.22), channel_id=1, source_target_pairs={{0,8},{4,12},{8,0},{12,4},{16,24},{20,28},{24,16},{28,20},{1,9},{5... | collective-permute-start | bytes 442376 | tf_op jit(solution)/shard_map/ppermute | solution.py:508
  36.7 2.7 %collective-permute-start.12 = (bf16[512,1024]{1,0:T(8,128)(2,1)S(1)}, bf16[512,1024]{1,0:T(8,128)(2,1)S(1)}, u32[]{:S(2)}, u32[]{:S(2)}) collective-permute-start(bf16[512,1024]{1,0:T(8,128)(2,1)S(1)} %get-tuple-element.24), channel_id=1, source_target_pairs={{0,1},{1,0},{2,3},{3,2},{4,5},{5,4},{6,7},{7,6},{8,9},{9,8},{10,11... | collective-permute-start | bytes 3145736 | tf_op jit(solution)/shard_map/ppermute | solution.py:508
  36.8 10.3 %collective-permute-start.10 = (s16[144,512]{1,0:T(8,128)(2,1)S(1)}, s16[144,512]{1,0:T(8,128)(2,1)S(1)}, u32[]{:S(2)}, u32[]{:S(2)}) collective-permute-start(s16[144,512]{1,0:T(8,128)(2,1)S(1)} %get-tuple-element.23), channel_id=1, source_target_pairs={{0,16},{4,20},{8,24},{12,28},{16,0},{20,4},{24,8},{28,12},{1,17},{... | collective-permute-start | bytes 442376 | tf_op jit(solution)/shard_map/ppermute | solution.py:508
  36.9 10.2 %collective-permute-start.11 = (bf16[128,1024]{1,0:T(8,128)(2,1)S(1)}, bf16[128,1024]{1,0:T(8,128)(2,1)S(1)}, u32[]{:S(2)}, u32[]{:S(2)}) collective-permute-start(bf16[128,1024]{1,0:T(8,128)(2,1)S(1)} %collective-permute-done.9.refs_7_.refs_4_), channel_id=1, source_target_pairs={{0,4},{4,0},{8,12},{12,8},{16,20},{20,16},{24,28},{28,24},{1,5},{5... | collective-permute-start | bytes 786440 | tf_op jit(solution)/shard_map/ppermute | solution.py:508
  47.5 2.7 %collective-permute-start.14 = (bf16[512,1024]{1,0:T(8,128)(2,1)S(1)}, bf16[512,1024]{1,0:T(8,128)(2,1)S(1)}, u32[]{:S(2)}, u32[]{:S(2)}) collective-permute-start(bf16[512,1024]{1,0:T(8,128)(2,1)S(1)} %get-tuple-element.28), channel_id=1, source_target_pairs={{0,1},{1,0},{2,3},{3,2},{4,5},{5,4},{6,7},{7,6},{8,9},{9,8},{10,11... | collective-permute-start | bytes 3145736 | tf_op jit(solution)/shard_map/ppermute | solution.py:508
  47.6 8.3 %collective-permute-start.13 = (s16[144,512]{1,0:T(8,128)(2,1)S(1)}, s16[144,512]{1,0:T(8,128)(2,1)S(1)}, u32[]{:S(2)}, u32[]{:S(2)}) collective-permute-start(s16[144,512]{1,0:T(8,128)(2,1)S(1)} %get-tuple-element.27), channel_id=1, source_target_pairs={{0,4},{4,0},{8,12},{12,8},{16,20},{20,16},{24,28},{28,24},{1,5},{5... | collective-permute-start | bytes 442376 | tf_op jit(solution)/shard_map/ppermute | solution.py:508

commit v11 on v10

--- a/solution.py
+++ b/solution.py
@@ -469,7 +469,7 @@
     )
     late = None
     if paired:
-        follow = (*pieces[0][1:3], pieces[1][0])
+        follow = (*pieces[0][1:], pieces[1][0])
         starts, *late = entering_by_pairs(*ends, width, follow, pieces, meanwhile)
     else:
         starts = (entering_by_rows(ends[0]),)
@@ -571,7 +571,8 @@
     z = along_z(moe_input)
     x = [swapped(a, "ctx", 1) for a in z]
     y = [swapped(a, "exp", 2) for a in z]
-    d = (swapped(x[0], "exp", 2), swapped(y[1], "ctx", 1))
+    corner = lax.axis_size("exp") | 2
+    d = [swapped(a, ("ctx", "exp"), corner) for a in z]
     return list(zip(z, x, y, d))
 
 

time: 59.4 us -> 60.4 us (1.017)
  starting transfers between devices: 19.1 us -> 20.6 us
    ppermute x14, starting transfers between devices: 15.7 us -> 17.2 us  [swapped(): lax.ppermute(block, axis, [(i, i ^ bit) for i in range(lax.axis_size(axis...]
  transfers between devices with their start and end apart: 15 -> 15, of which waited for: 7 -> 6; matrix products, arithmetic and copies ran while one was open for 0% -> 0% of each run, Pallas kernels for 35% -> 34%
where the time goes in v11:
time: 60.4 us; the launch traced here: 60.1 us
  Pallas kernels  24.3 us (40%)
  starting transfers between devices  20.6 us (34%)
  waiting for transfers between devices  14.3 us (24%)
  between operations  0.93 us (2%)
    pallas_call x9, Pallas kernels, call(): pl.pallas_call(body, out_shape=outs, in_specs=[pl.BlockSpec(memory_space=...  24.3 us
    ppermute x14, starting transfers between devices, swapped(): lax.ppermute(block, axis, [(i, i ^ bit) for i in range(lax.axis_size(axis...  17.2 us
    ppermute x14, waiting for transfers between devices, swapped(): lax.ppermute(block, axis, [(i, i ^ bit) for i in range(lax.axis_size(axis...  14.3 us
    ppermute x1, starting transfers between devices, on_device(): before = lax.ppermute(ends, 'ctx', [(i, i + 1) for i in range(ctx - 1)])  3.4 us
  transfers between devices with their start and end apart: 15, of which 6 were waited for; matrix products, arithmetic and copies ran while one was open for 0% of the time, Pallas kernels for 34%

profile of v11, /device:TPU:0, one launch (start us, length us, event | category | flops | bytes accessed | tf_op | source)
XLA Modules:
  0.0 60.1 jit_solution(953911513599490432)
XLA Ops:
  0.6 3.1 %collective-permute-start.1 = (bf16[64,1024]{1,0:T(8,128)(2,1)}, bf16[64,1024]{1,0:T(8,128)(2,1)S(1)}, u32[]{:S(2)}, u32[]{:S(2)}) collective-permute-start(bf16[64,1024]{1,0:T(8,128)(2,1)} %refs_0_.6), channel_id=1, source_target_pairs={{0,8},{4,12},{8,0},{12,4},{16,24},{20,28},{24,16},{28,20},{1,9},{5... | collective-permute-start | bytes 393224 | tf_op jit(solution)/shard_map/ppermute | solution.py:508
  3.7 0.8 %ends.1 = bf16[16,1280]{1,0:T(8,128)(2,1)S(1)} custom-call(bf16[256,1024]{1,0:T(8,128)(2,1)} %refs_0_.7, bf16[256,128]{1,0:T(8,128)(2,1)} %refs_1_.5, bf16[256,128]{1,0:T(8,128)(2,1)} %refs_2_.3), custom_call_target="tpu_custom_call" | custom-call | bytes 696320 | tf_op jit(solution)/shard_map/ends/pallas_call | solution.py:126
  4.5 3.4 %collective-permute-start = (bf16[16,1280]{1,0:T(8,128)(2,1)S(1)}, bf16[16,1280]{1,0:T(8,128)(2,1)S(1)}, u32[]{:S(2)}, u32[]{:S(2)}) collective-permute-start(bf16[16,1280]{1,0:T(8,128)(2,1)S(1)} %ends.1), channel_id=1, source_target_pairs={{0,4},{4,8},{8,12},{12,16},{16,20},{20,24},{24,28},{1,5},{5,9},{9,... | collective-permute-start | bytes 122888 | tf_op jit(solution)/shard_map/ppermute | solution.py:648
  7.9 0.0 collective-permute-done.1.refs_1_
  7.9 0.0 slice-start
  7.9 1.1 %join.1.refs_9_.refs_2_ = bf16[128,1024]{1,0:T(8,128)(2,1)S(1)} custom-call(bf16[64,1024]{1,0:T(8,128)(2,1)} %refs_0_.6, bf16[64,1024]{1,0:T(8,128)(2,1)S(1)} %collective-permute-done.1.refs_1_), custom_call_target="tpu_custom_call" | custom-call | bytes 524288 | tf_op jit(solution)/shard_map/join/pallas_call | solution.py:126
  9.0 2.7 %collective-permute-start.6 = (bf16[128,1024]{1,0:T(8,128)(2,1)S(1)}, bf16[128,1024]{1,0:T(8,128)(2,1)S(1)}, u32[]{:S(2)}, u32[]{:S(2)}) collective-permute-start(bf16[128,1024]{1,0:T(8,128)(2,1)S(1)} %join.1.refs_9_.refs_2_), channel_id=1, source_target_pairs={{0,16},{4,20},{8,24},{12,28},{16,0},{20,4},{24,8},{28,12},{1,17},{... | collective-permute-start | bytes 786440 | tf_op jit(solution)/shard_map/ppermute | solution.py:508
  11.7 1.1 %collective-permute-start.3 = (bf16[128,1024]{1,0:T(8,128)(2,1)S(1)}, bf16[128,1024]{1,0:T(8,128)(2,1)S(1)}, u32[]{:S(2)}, u32[]{:S(2)}) collective-permute-start(bf16[128,1024]{1,0:T(8,128)(2,1)S(1)} %join.1.refs_9_.refs_2_), channel_id=1, source_target_pairs={{0,4},{4,0},{8,12},{12,8},{16,20},{20,16},{24,28},{28,24},{1,5},{5... | collective-permute-start | bytes 786440 | tf_op jit(solution)/shard_map/ppermute | solution.py:508
  12.8 1.5 %collective-permute-start.4 = (bf16[128,1024]{1,0:T(8,128)(2,1)S(1)}, bf16[128,1024]{1,0:T(8,128)(2,1)S(1)}, u32[]{:S(2)}, u32[]{:S(2)}) collective-permute-start(bf16[128,1024]{1,0:T(8,128)(2,1)S(1)} %join.1.refs_9_.refs_2_), channel_id=1, source_target_pairs={{0,2},{1,3},{2,0},{3,1},{4,6},{5,7},{6,4},{7,5},{8,10},{9,11},{10,... | collective-permute-start | bytes 786440 | tf_op jit(solution)/shard_map/ppermute | solution.py:508
  14.3 0.8 %collective-permute-start.5 = (bf16[128,1024]{1,0:T(8,128)(2,1)S(1)}, bf16[128,1024]{1,0:T(8,128)(2,1)S(1)}, u32[]{:S(2)}, u32[]{:S(2)}) collective-permute-start(bf16[128,1024]{1,0:T(8,128)(2,1)S(1)} %join.1.refs_9_.refs_2_), channel_id=1, source_target_pairs={{0,6},{1,7},{2,4},{3,5},{4,2},{5,3},{6,0},{7,1},{8,14},{9,15},{10,... | collective-permute-start | bytes 786440 | tf_op jit(solution)/shard_map/ppermute | solution.py:508
  15.2 7.2 %local.1 = (f32[256,1024]{1,0:T(8,128)S(1)}, f32[256,1024]{1,0:T(8,128)S(1)}, f32[256,128]{1,0:T(8,128)S(1)}, f32[136,512]{1,0:T(8,128)S(1)}, s16[144,512]{1,0:T(8,128)(2,1)S(1)}) custom-call(bf16[256,1024]{1,0:T(8,128)(2,1)} %refs_0_.7, bf16[256,128]{1,0:T(8,128)(2,1)} %refs_1_.5, bf16[256,128]{1,0:T(8,128)(2,1)} %refs_2_.3, f32[4,1024]{1,0:T(4,128)} %refs_3_.1, ...), custom_call_target="tpu_custom_call" | custom-call | flops 5000000000 | bytes 3387968 | tf_op jit(solution)/shard_map/local/pallas_call | solution.py:126
  22.4 1.2 %collective-permute-start.2 = (s16[144,512]{1,0:T(8,128)(2,1)S(1)}, s16[144,512]{1,0:T(8,128)(2,1)S(1)}, u32[]{:S(2)}, u32[]{:S(2)}) collective-permute-start(s16[144,512]{1,0:T(8,128)(2,1)S(1)} %get-tuple-element.20), channel_id=1, source_target_pairs={{0,4},{4,0},{8,12},{12,8},{16,20},{20,16},{24,28},{28,24},{1,5},{5... | collective-permute-start | bytes 442376 | tf_op jit(solution)/shard_map/ppermute | solution.py:508
  23.6 0.9 %collective-permute-start.8 = (bf16[128,1024]{1,0:T(8,128)(2,1)S(1)}, bf16[128,1024]{1,0:T(8,128)(2,1)S(1)}, u32[]{:S(2)}, u32[]{:S(2)}) collective-permute-start(bf16[128,1024]{1,0:T(8,128)(2,1)S(1)} %collective-permute-done.6.refs_5_.refs_2_), channel_id=1, source_target_pairs={{0,4},{4,0},{8,12},{12,8},{16,20},{20,16},{24,28},{28,24},{1,5},{5... | collective-permute-start | bytes 786440 | tf_op jit(solution)/shard_map/ppermute | solution.py:508
  24.5 4.8 %collective-permute-done.2.refs_1_ = s16[144,512]{1,0:T(8,128)(2,1)S(1)} collective-permute-done((s16[144,512]{1,0:T(8,128)(2,1)S(1)}, s16[144,512]{1,0:T(8,128)(2,1)S(1)}, u32[]{:S(2)}, u32[]{:S(2)}) %collective-permute-start.2) | collective-permute-done | bytes 147488 | tf_op jit(solution)/shard_map/ppermute | solution.py:508
  29.3 1.5 %collective-permute-start.9 = (bf16[128,1024]{1,0:T(8,128)(2,1)S(1)}, bf16[128,1024]{1,0:T(8,128)(2,1)S(1)}, u32[]{:S(2)}, u32[]{:S(2)}) collective-permute-start(bf16[128,1024]{1,0:T(8,128)(2,1)S(1)} %collective-permute-done.6.refs_5_.refs_2_), channel_id=1, source_target_pairs={{0,2},{1,3},{2,0},{3,1},{4,6},{5,7},{6,4},{7,5},{8,10},{9,11},{10,... | collective-permute-start | bytes 786440 | tf_op jit(solution)/shard_map/ppermute | solution.py:508
  30.8 0.1 pair.1
  31.0 1.3 %collective-permute-start.7 = (s16[144,512]{1,0:T(8,128)(2,1)S(1)}, s16[144,512]{1,0:T(8,128)(2,1)S(1)}, u32[]{:S(2)}, u32[]{:S(2)}) collective-permute-start(s16[144,512]{1,0:T(8,128)(2,1)S(1)} %get-tuple-element.22), channel_id=1, source_target_pairs={{0,8},{4,12},{8,0},{12,4},{16,24},{20,28},{24,16},{28,20},{1,9},{5... | collective-permute-start | bytes 442376 | tf_op jit(solution)/shard_map/ppermute | solution.py:508
  32.2 3.9 %collective-permute-done.7.refs_1_.refs_3_ = s16[144,512]{1,0:T(8,128)(2,1)S(1)} collective-permute-done((s16[144,512]{1,0:T(8,128)(2,1)S(1)}, s16[144,512]{1,0:T(8,128)(2,1)S(1)}, u32[]{:S(2)}, u32[]{:S(2)}) %collective-permute-start.7) | collective-permute-done | bytes 147488 | tf_op jit(solution)/shard_map/ppermute | solution.py:508
  36.2 0.2 four.1
  36.4 0.1 collective-permute-start.12
  36.5 1.6 %collective-permute-start.11 = (bf16[128,1024]{1,0:T(8,128)(2,1)S(1)}, bf16[128,1024]{1,0:T(8,128)(2,1)S(1)}, u32[]{:S(2)}, u32[]{:S(2)}) collective-permute-start(bf16[128,1024]{1,0:T(8,128)(2,1)S(1)} %collective-permute-done.6.refs_5_.refs_2_), channel_id=1, source_target_pairs={{0,6},{1,7},{2,4},{3,5},{4,2},{5,3},{6,0},{7,1},{8,14},{9,15},{10,... | collective-permute-start | bytes 786440 | tf_op jit(solution)/shard_map/ppermute | solution.py:508
  38.1 0.3 collective-permute-start.10
  38.4 0.7 %collective-permute-done.12.refs_6_ = bf16[512,1024]{1,0:T(8,128)(2,1)S(1)} collective-permute-done((bf16[512,1024]{1,0:T(8,128)(2,1)S(1)}, bf16[512,1024]{1,0:T(8,128)(2,1)S(1)}, u32[]{:S(2)}, u32[]{:S(2)}) %collective-permute-start.12) | collective-permute-done | bytes 1048608 | tf_op jit(solution)/shard_map/ppermute | solution.py:508
  39.1 5.7 %experts.2.refs_9_.refs_8_ = bf16[1,512,1024]{2,1,0:T(8,128)(2,1)} custom-call(bf16[1,4096,1024]{2,1,0:T(8,128)(2,1)S(1)} %bitcast.4, bf16[1,4096,1024]{2,1,0:T(8,128)(2,1)S(1)} %copy-done, bf16[128,1024]{1,0:T(8,128)(2,1)S(1)} %join.1.refs_9_.refs_2_, bf16[128,1024]{1,0:T(8,128)(2,1)S(1)} %collective-permute-done.3.refs_2_.refs_3_, ...), custom_call_target="tpu_custom_call" | custom-call | flops 4294967296 | bytes 19927040 | tf_op jit(solution)/shard_map/experts/pallas_call | solution.py:126
  44.8 1.3 %collective-permute-done.11.refs_8_.refs_5_ = bf16[128,1024]{1,0:T(8,128)(2,1)S(1)} collective-permute-done((bf16[128,1024]{1,0:T(8,128)(2,1)S(1)}, bf16[128,1024]{1,0:T(8,128)(2,1)S(1)}, u32[]{:S(2)}, u32[]{:S(2)}) %collective-permute-start.11) | collective-permute-done | bytes 262176 | tf_op jit(solution)/shard_map/ppermute | solution.py:508
  46.1 2.0 %collective-permute-done.10.refs_4_ = s16[144,512]{1,0:T(8,128)(2,1)S(1)} collective-permute-done((s16[144,512]{1,0:T(8,128)(2,1)S(1)}, s16[144,512]{1,0:T(8,128)(2,1)S(1)}, u32[]{:S(2)}, u32[]{:S(2)}) %collective-permute-start.10) | collective-permute-done | bytes 147488 | tf_op jit(solution)/shard_map/ppermute | solution.py:508
  48.1 0.4 turn.1
  48.5 0.1 collective-permute-start.14
  48.5 1.0 %collective-permute-start.13 = (s16[144,512]{1,0:T(8,128)(2,1)S(1)}, s16[144,512]{1,0:T(8,128)(2,1)S(1)}, u32[]{:S(2)}, u32[]{:S(2)}) collective-permute-start(s16[144,512]{1,0:T(8,128)(2,1)S(1)} %get-tuple-element.27), channel_id=1, source_target_pairs={{0,4},{4,0},{8,12},{12,8},{16,20},{20,16},{24,28},{28,24},{1,5},{5... | collective-permute-start | bytes 442376 | tf_op jit(solution)/shard_map/ppermute | solution.py:508
  49.5 1.7 %collective-permute-done.14.refs_6_ = bf16[512,1024]{1,0:T(8,128)(2,1)S(1)} collective-permute-done((bf16[512,1024]{1,0:T(8,128)(2,1)S(1)}, bf16[512,1024]{1,0:T(8,128)(2,1)S(1)}, u32[]{:S(2)}, u32[]{:S(2)}) %collective-permute-start.14) | collective-permute-done | bytes 1048608 | tf_op jit(solution)/shard_map/ppermute | solution.py:508
  51.2 5.7 %experts.3.refs_6_ = bf16[1,512,1024]{2,1,0:T(8,128)(2,1)} custom-call(bf16[1,4096,1024]{2,1,0:T(8,128)(2,1)S(1)} %bitcast.4, bf16[1,4096,1024]{2,1,0:T(8,128)(2,1)S(1)} %copy-done, bf16[128,1024]{1,0:T(8,128)(2,1)S(1)} %collective-permute-done.6.refs_5_.refs_2_, ...), custom_call_target="tpu_custom_call", output_to_operand_aliasing={{}: (8, {})} | custom-call | flops 4294967296 | bytes 20975616 | tf_op jit(solution)/shard_map/experts/pallas_call | solution.py:126
  56.9 3.1 %back.1 = bf16[256,1024]{1,0:T(8,128)(2,1)} custom-call(f32[1,1024]{1,0:T(1,128)} %bitcast.5, f32[256,1024]{1,0:T(8,128)S(1)} %get-tuple-element.16.refs_1_, f32[256,1024]{1,0:T(8,128)S(1)} %get-tuple-element.17.refs_2_, f32[256,128]{1,0:T(8,128)S(1)} %get-tuple-element.18.refs_3_, f32[128,512]{1,0:T(8,128)S(1)} %get-tuple-element.26.refs_4_, ...), custom_call_target="tpu_custom_call" | custom-call | flops 1000000000 | bytes 3166208 | tf_op jit(solution)/shard_map/back/pallas_call | solution.py:126
  (14 shorter events, 0.0 us)
Async XLA Ops:
  0.6 7.3 %collective-permute-start.1 = (bf16[64,1024]{1,0:T(8,128)(2,1)}, bf16[64,1024]{1,0:T(8,128)(2,1)S(1)}, u32[]{:S(2)}, u32[]{:S(2)}) collective-permute-start(bf16[64,1024]{1,0:T(8,128)(2,1)} %refs_0_.6), channel_id=1, source_target_pairs={{0,8},{4,12},{8,0},{12,4},{16,24},{20,28},{24,16},{28,20},{1,9},{5... | collective-permute-start | bytes 393224 | tf_op jit(solution)/shard_map/ppermute | solution.py:508
  4.5 10.7 %collective-permute-start = (bf16[16,1280]{1,0:T(8,128)(2,1)S(1)}, bf16[16,1280]{1,0:T(8,128)(2,1)S(1)}, u32[]{:S(2)}, u32[]{:S(2)}) collective-permute-start(bf16[16,1280]{1,0:T(8,128)(2,1)S(1)} %ends.1), channel_id=1, source_target_pairs={{0,4},{4,8},{8,12},{12,16},{16,20},{20,24},{24,28},{1,5},{5,9},{9,... | collective-permute-start | bytes 122888 | tf_op jit(solution)/shard_map/ppermute | solution.py:648
  7.9 31.2 %slice-start = ((s8[8388608]{0:T(1024)(128)(4,1)}), s8[4194304]{0:T(1024)(128)(4,1)S(1)}, s32[]{:S(2)}) async-start(s8[8388608]{0:T(1024)(128)(4,1)} %bitcast.3), calls=%async_computation | async-start | bytes 8388608
  9.0 14.6 %collective-permute-start.6 = (bf16[128,1024]{1,0:T(8,128)(2,1)S(1)}, bf16[128,1024]{1,0:T(8,128)(2,1)S(1)}, u32[]{:S(2)}, u32[]{:S(2)}) collective-permute-start(bf16[128,1024]{1,0:T(8,128)(2,1)S(1)} %join.1.refs_9_.refs_2_), channel_id=1, source_target_pairs={{0,16},{4,20},{8,24},{12,28},{16,0},{20,4},{24,8},{28,12},{1,17},{... | collective-permute-start | bytes 786440 | tf_op jit(solution)/shard_map/ppermute | solution.py:508
  11.7 19.1 %collective-permute-start.3 = (bf16[128,1024]{1,0:T(8,128)(2,1)S(1)}, bf16[128,1024]{1,0:T(8,128)(2,1)S(1)}, u32[]{:S(2)}, u32[]{:S(2)}) collective-permute-start(bf16[128,1024]{1,0:T(8,128)(2,1)S(1)} %join.1.refs_9_.refs_2_), channel_id=1, source_target_pairs={{0,4},{4,0},{8,12},{12,8},{16,20},{20,16},{24,28},{28,24},{1,5},{5... | collective-permute-start | bytes 786440 | tf_op jit(solution)/shard_map/ppermute | solution.py:508
  12.8 18.0 %collective-permute-start.4 = (bf16[128,1024]{1,0:T(8,128)(2,1)S(1)}, bf16[128,1024]{1,0:T(8,128)(2,1)S(1)}, u32[]{:S(2)}, u32[]{:S(2)}) collective-permute-start(bf16[128,1024]{1,0:T(8,128)(2,1)S(1)} %join.1.refs_9_.refs_2_), channel_id=1, source_target_pairs={{0,2},{1,3},{2,0},{3,1},{4,6},{5,7},{6,4},{7,5},{8,10},{9,11},{10,... | collective-permute-start | bytes 786440 | tf_op jit(solution)/shard_map/ppermute | solution.py:508
  14.3 16.5 %collective-permute-start.5 = (bf16[128,1024]{1,0:T(8,128)(2,1)S(1)}, bf16[128,1024]{1,0:T(8,128)(2,1)S(1)}, u32[]{:S(2)}, u32[]{:S(2)}) collective-permute-start(bf16[128,1024]{1,0:T(8,128)(2,1)S(1)} %join.1.refs_9_.refs_2_), channel_id=1, source_target_pairs={{0,6},{1,7},{2,4},{3,5},{4,2},{5,3},{6,0},{7,1},{8,14},{9,15},{10,... | collective-permute-start | bytes 786440 | tf_op jit(solution)/shard_map/ppermute | solution.py:508
  15.2 23.9 %slice-start.1 = ((s8[8388608]{0:T(1024)(128)(4,1)}), s8[4194304]{0:T(1024)(128)(4,1)S(1)}, s32[]{:S(2)}) async-start(s8[8388608]{0:T(1024)(128)(4,1)} %bitcast.3), calls=%async_computation.1 | async-start | bytes 8388608
  15.2 23.9 %copy-start = (bf16[1,4096,1024]{2,1,0:T(8,128)(2,1)S(1)}, bf16[1,4096,1024]{2,1,0:T(8,128)(2,1)}, u32[]{:S(2)}) copy-start(bf16[1,4096,1024]{2,1,0:T(8,128)(2,1)} %refs_1_.7) | copy-start | bytes 25165828
  22.4 6.9 %collective-permute-start.2 = (s16[144,512]{1,0:T(8,128)(2,1)S(1)}, s16[144,512]{1,0:T(8,128)(2,1)S(1)}, u32[]{:S(2)}, u32[]{:S(2)}) collective-permute-start(s16[144,512]{1,0:T(8,128)(2,1)S(1)} %get-tuple-element.20), channel_id=1, source_target_pairs={{0,4},{4,0},{8,12},{12,8},{16,20},{20,16},{24,28},{28,24},{1,5},{5... | collective-permute-start | bytes 442376 | tf_op jit(solution)/shard_map/ppermute | solution.py:508
  23.6 12.5 %collective-permute-start.8 = (bf16[128,1024]{1,0:T(8,128)(2,1)S(1)}, bf16[128,1024]{1,0:T(8,128)(2,1)S(1)}, u32[]{:S(2)}, u32[]{:S(2)}) collective-permute-start(bf16[128,1024]{1,0:T(8,128)(2,1)S(1)} %collective-permute-done.6.refs_5_.refs_2_), channel_id=1, source_target_pairs={{0,4},{4,0},{8,12},{12,8},{16,20},{20,16},{24,28},{28,24},{1,5},{5... | collective-permute-start | bytes 786440 | tf_op jit(solution)/shard_map/ppermute | solution.py:508
  29.3 6.9 %collective-permute-start.9 = (bf16[128,1024]{1,0:T(8,128)(2,1)S(1)}, bf16[128,1024]{1,0:T(8,128)(2,1)S(1)}, u32[]{:S(2)}, u32[]{:S(2)}) collective-permute-start(bf16[128,1024]{1,0:T(8,128)(2,1)S(1)} %collective-permute-done.6.refs_5_.refs_2_), channel_id=1, source_target_pairs={{0,2},{1,3},{2,0},{3,1},{4,6},{5,7},{6,4},{7,5},{8,10},{9,11},{10,... | collective-permute-start | bytes 786440 | tf_op jit(solution)/shard_map/ppermute | solution.py:508
  31.0 5.2 %collective-permute-start.7 = (s16[144,512]{1,0:T(8,128)(2,1)S(1)}, s16[144,512]{1,0:T(8,128)(2,1)S(1)}, u32[]{:S(2)}, u32[]{:S(2)}) collective-permute-start(s16[144,512]{1,0:T(8,128)(2,1)S(1)} %get-tuple-element.22), channel_id=1, source_target_pairs={{0,8},{4,12},{8,0},{12,4},{16,24},{20,28},{24,16},{28,20},{1,9},{5... | collective-permute-start | bytes 442376 | tf_op jit(solution)/shard_map/ppermute | solution.py:508
  36.4 2.7 %collective-permute-start.12 = (bf16[512,1024]{1,0:T(8,128)(2,1)S(1)}, bf16[512,1024]{1,0:T(8,128)(2,1)S(1)}, u32[]{:S(2)}, u32[]{:S(2)}) collective-permute-start(bf16[512,1024]{1,0:T(8,128)(2,1)S(1)} %get-tuple-element.24), channel_id=1, source_target_pairs={{0,1},{1,0},{2,3},{3,2},{4,5},{5,4},{6,7},{7,6},{8,9},{9,8},{10,11... | collective-permute-start | bytes 3145736 | tf_op jit(solution)/shard_map/ppermute | solution.py:508
  36.5 9.6 %collective-permute-start.11 = (bf16[128,1024]{1,0:T(8,128)(2,1)S(1)}, bf16[128,1024]{1,0:T(8,128)(2,1)S(1)}, u32[]{:S(2)}, u32[]{:S(2)}) collective-permute-start(bf16[128,1024]{1,0:T(8,128)(2,1)S(1)} %collective-permute-done.6.refs_5_.refs_2_), channel_id=1, source_target_pairs={{0,6},{1,7},{2,4},{3,5},{4,2},{5,3},{6,0},{7,1},{8,14},{9,15},{10,... | collective-permute-start | bytes 786440 | tf_op jit(solution)/shard_map/ppermute | solution.py:508
  38.1 10.0 %collective-permute-start.10 = (s16[144,512]{1,0:T(8,128)(2,1)S(1)}, s16[144,512]{1,0:T(8,128)(2,1)S(1)}, u32[]{:S(2)}, u32[]{:S(2)}) collective-permute-start(s16[144,512]{1,0:T(8,128)(2,1)S(1)} %get-tuple-element.23), channel_id=1, source_target_pairs={{0,16},{4,20},{8,24},{12,28},{16,0},{20,4},{24,8},{28,12},{1,17},{... | collective-permute-start | bytes 442376 | tf_op jit(solution)/shard_map/ppermute | solution.py:508
  48.5 2.7 %collective-permute-start.14 = (bf16[512,1024]{1,0:T(8,128)(2,1)S(1)}, bf16[512,1024]{1,0:T(8,128)(2,1)S(1)}, u32[]{:S(2)}, u32[]{:S(2)}) collective-permute-start(bf16[512,1024]{1,0:T(8,128)(2,1)S(1)} %get-tuple-element.28), channel_id=1, source_target_pairs={{0,1},{1,0},{2,3},{3,2},{4,5},{5,4},{6,7},{7,6},{8,9},{9,8},{10,11... | collective-permute-start | bytes 3145736 | tf_op jit(solution)/shard_map/ppermute | solution.py:508
  48.5 8.3 %collective-permute-start.13 = (s16[144,512]{1,0:T(8,128)(2,1)S(1)}, s16[144,512]{1,0:T(8,128)(2,1)S(1)}, u32[]{:S(2)}, u32[]{:S(2)}) collective-permute-start(s16[144,512]{1,0:T(8,128)(2,1)S(1)} %get-tuple-element.27), channel_id=1, source_target_pairs={{0,4},{4,0},{8,12},{12,8},{16,20},{20,16},{24,28},{28,24},{1,5},{5... | collective-permute-start | bytes 442376 | tf_op jit(solution)/shard_map/ppermute | solution.py:508

commit v12 on v10

--- a/solution.py
+++ b/solution.py
@@ -306,8 +306,7 @@
         joined_ref[i * rows : (i + 1) * rows] = piece[...]
 
 
-def four_body(width, pair_ref, got_ref, a, b, c, d, sent_ref, ids_ref, joined_ref):
-    join_rows((a, b, c, d), joined_ref)
+def four_body(width, pair_ref, got_ref, sent_ref, ids_ref):
     _, z, _ = place()
     four = together(z == 0, taken(pair_ref), received(got_ref), 2 * width)
     send(sent_ref, *four)
@@ -387,7 +386,7 @@
 def entering_by_pairs(keep, sent, width, follow, pieces, meanwhile):
     pair_array, sent_array = array(keep.shape, F32), array(sent.shape, jnp.int16)
     ids_array = array((8, width), F32)
-    joined_array = [array((4 * p[0].shape[0], p[0].shape[1]), BF16) for p in pieces]
+    joined_array = array((4 * pieces[0].shape[0], pieces[0].shape[1]), BF16)
     got = swapped(sent, "ctx", 1)
     pair, sent = call(
         functools.partial(pair_body, width),
@@ -398,20 +397,19 @@
         name="pair",
     )
     pair_got = swapped(sent, "ctx", 2)
-    sent, ids, joined = call(
+    sent, ids = call(
         functools.partial(four_body, width),
-        [sent_array, ids_array, joined_array[0]],
-        (pair, pair_got, *pieces[0]),
+        [sent_array, ids_array],
+        (pair, pair_got),
         near=True,
-        after=pieces[1][1:3],
         name="four",
     )
     four_got = swapped(sent, "ctx", 4)
-    done = meanwhile(ids, joined)
+    done = meanwhile(ids)
     mine, sent, ids, joined = call(
         functools.partial(turn_body, width),
-        [array((STATE, keep.shape[1]), F32), sent_array, ids_array, joined_array[1]],
-        (keep, got, pair, pair_got, four_got, *pieces[1]),
+        [array((STATE, keep.shape[1]), F32), sent_array, ids_array, joined_array],
+        (keep, got, pair, pair_got, four_got, *pieces),
         near=True,
         after_far=(done,),
         name="turn",
@@ -470,7 +468,7 @@
     late = None
     if paired:
         follow = (*pieces[0][1:3], pieces[1][0])
-        starts, *late = entering_by_pairs(*ends, width, follow, pieces, meanwhile)
+        starts, *late = entering_by_pairs(*ends, width, follow, pieces[1], meanwhile)
     else:
         starts = (entering_by_rows(ends[0]),)
 
@@ -509,8 +507,10 @@
 
 
 def expert_body(part, w_gate, w_up, *refs):
-    pieces, joined_ref, ids_ref, out_far = refs[:4], refs[4], refs[5], refs[6 + part]
-    pick_ref, hid_ref, out_ref, sems = refs[7 + part :]
+    count = 1 if part else 4
+    pieces, beside, refs = refs[:4], refs[4 : 4 + count], refs[4 + count :]
+    ids_ref, out_far = refs[0], refs[1 + part]
+    pick_ref, hid_ref, out_ref, sems = refs[2 + part :]
     length, hidden = out_ref.shape
     rows = pieces[0].shape[0] // 2
     depth = pieces[0].shape[1]
@@ -538,10 +538,12 @@
         cut = slice(n * TILE, (n + 1) * TILE)
         gate = upper = None
         for k in range(4):
-            if k % 2 == 0:
-                block = jnp.concatenate([piece[...] for piece in pieces[k : k + 2]], axis=0)
+            first = k // 2 * 2
+            if k % 2 == 1 and part:
+                block = beside[0][k // 2 * length : (k // 2 + 1) * length]
             else:
-                block = joined_ref[k // 2 * length : (k // 2 + 1) * length]
+                block = (beside if k % 2 else pieces)[first : first + 2]
+                block = jnp.concatenate([piece[...] for piece in block], axis=0)
             more = dot16(block, w_gate[0, downs[k], cut])
             gate = more if k == 0 else gate + more
             more = dot16(block, w_up[0, downs[k], cut])
@@ -575,11 +577,11 @@
     return list(zip(z, x, y, d))
 
 
-def experts_by_tokens(part, pieces, joined, ids, w_gate, w_up, so_far):
+def experts_by_tokens(part, pieces, sent, ids, w_gate, w_up, so_far):
     rows = pieces[0].shape[0] // 2
     length = 4 * rows
     hidden = w_gate.shape[2]
-    args = (w_gate, w_up, *pieces, swapped(joined, "exp", 1), ids)
+    args = (w_gate, w_up, *pieces, *(swapped(a, "exp", 1) for a in sent), ids)
     return call(
         functools.partial(expert_body, part),
         [pltpu.HBM((1, 2 * length, hidden), BF16)],
@@ -649,8 +651,8 @@
     if by_tokens:
         pieces = gathered(moe_input)
 
-        def meanwhile(ids, joined):
-            return experts_by_tokens(0, pieces[0], joined, ids, w_gate, w_up, None)
+        def meanwhile(ids):
+            return experts_by_tokens(0, pieces[0], pieces[0], ids, w_gate, w_up, None)
 
     finish, late = mixing(
         pieces,
@@ -668,7 +670,7 @@
     )
     if by_tokens:
         ids, joined, hidden = late
-        hidden = experts_by_tokens(1, pieces[1], joined, ids, w_gate, w_up, hidden)
+        hidden = experts_by_tokens(1, pieces[1], [joined], ids, w_gate, w_up, hidden)
         mixed = finish((hidden,))
     else:
         mixed = finish()

time: 59.4 us -> 59 us (level)
    ppermute x14 -> x17, waiting for transfers between devices: 14.9 us -> 14.4 us  [swapped(): lax.ppermute(block, axis, [(i, i ^ bit) for i in range(lax.axis_size(axis...]
    ppermute x14 -> x17, starting transfers between devices: 15.7 us -> 15.9 us  [swapped(): lax.ppermute(block, axis, [(i, i ^ bit) for i in range(lax.axis_size(axis...]
  transfers between devices with their start and end apart: 15 -> 18, of which waited for: 7 -> 5; matrix products, arithmetic and copies ran while one was open for 0% -> 0% of each run, Pallas kernels for 35% -> 35%
where the time goes in v12:
time: 59 us; the launch traced here: 58.8 us
  Pallas kernels  24.2 us (41%)
  starting transfers between devices  19.3 us (33%)
  waiting for transfers between devices  14.4 us (24%)
  between operations  0.95 us (2%)
    pallas_call x9, Pallas kernels, call(): pl.pallas_call(body, out_shape=outs, in_specs=[pl.BlockSpec(memory_space=...  24.2 us
    ppermute x17, starting transfers between devices, swapped(): lax.ppermute(block, axis, [(i, i ^ bit) for i in range(lax.axis_size(axis...  15.9 us
    ppermute x17, waiting for transfers between devices, swapped(): lax.ppermute(block, axis, [(i, i ^ bit) for i in range(lax.axis_size(axis...  14.4 us
    ppermute x1, starting transfers between devices, on_device(): before = lax.ppermute(ends, 'ctx', [(i, i + 1) for i in range(ctx - 1)])  3.4 us
  transfers between devices with their start and end apart: 18, of which 5 were waited for; matrix products, arithmetic and copies ran while one was open for 0% of the time, Pallas kernels for 35%

profile of v12, /device:TPU:0, one launch (start us, length us, event | category | flops | bytes accessed | tf_op | source)
XLA Modules:
  0.0 58.8 jit_solution(11257036062096052674)
XLA Ops:
  0.6 3.1 %collective-permute-start.1 = (bf16[64,1024]{1,0:T(8,128)(2,1)}, bf16[64,1024]{1,0:T(8,128)(2,1)S(1)}, u32[]{:S(2)}, u32[]{:S(2)}) collective-permute-start(bf16[64,1024]{1,0:T(8,128)(2,1)} %refs_0_.6), channel_id=1, source_target_pairs={{0,8},{4,12},{8,0},{12,4},{16,24},{20,28},{24,16},{28,20},{1,9},{5... | collective-permute-start | bytes 393224 | tf_op jit(solution)/shard_map/ppermute | solution.py:506
  3.7 0.8 %ends.1 = bf16[16,1280]{1,0:T(8,128)(2,1)S(1)} custom-call(bf16[256,1024]{1,0:T(8,128)(2,1)} %refs_0_.7, bf16[256,128]{1,0:T(8,128)(2,1)} %refs_1_.5, bf16[256,128]{1,0:T(8,128)(2,1)} %refs_2_.3), custom_call_target="tpu_custom_call" | custom-call | bytes 696320 | tf_op jit(solution)/shard_map/ends/pallas_call | solution.py:126
  4.5 3.4 %collective-permute-start = (bf16[16,1280]{1,0:T(8,128)(2,1)S(1)}, bf16[16,1280]{1,0:T(8,128)(2,1)S(1)}, u32[]{:S(2)}, u32[]{:S(2)}) collective-permute-start(bf16[16,1280]{1,0:T(8,128)(2,1)S(1)} %ends.1), channel_id=1, source_target_pairs={{0,4},{4,8},{8,12},{12,16},{16,20},{20,24},{24,28},{1,5},{5,9},{9,... | collective-permute-start | bytes 122888 | tf_op jit(solution)/shard_map/ppermute | solution.py:649
  7.9 0.0 slice-start
  7.9 1.1 %join.1.refs_9_.refs_2_ = bf16[128,1024]{1,0:T(8,128)(2,1)S(1)} custom-call(bf16[64,1024]{1,0:T(8,128)(2,1)} %refs_0_.6, bf16[64,1024]{1,0:T(8,128)(2,1)S(1)} %collective-permute-done.1.refs_1_), custom_call_target="tpu_custom_call" | custom-call | bytes 524288 | tf_op jit(solution)/shard_map/join/pallas_call | solution.py:126
  9.0 2.7 %collective-permute-start.5 = (bf16[128,1024]{1,0:T(8,128)(2,1)S(1)}, bf16[128,1024]{1,0:T(8,128)(2,1)S(1)}, u32[]{:S(2)}, u32[]{:S(2)}) collective-permute-start(bf16[128,1024]{1,0:T(8,128)(2,1)S(1)} %join.1.refs_9_.refs_2_), channel_id=1, source_target_pairs={{0,16},{4,20},{8,24},{12,28},{16,0},{20,4},{24,8},{28,12},{1,17},{... | collective-permute-start | bytes 786440 | tf_op jit(solution)/shard_map/ppermute | solution.py:506
  11.7 1.1 %collective-permute-start.3 = (bf16[128,1024]{1,0:T(8,128)(2,1)S(1)}, bf16[128,1024]{1,0:T(8,128)(2,1)S(1)}, u32[]{:S(2)}, u32[]{:S(2)}) collective-permute-start(bf16[128,1024]{1,0:T(8,128)(2,1)S(1)} %join.1.refs_9_.refs_2_), channel_id=1, source_target_pairs={{0,4},{4,0},{8,12},{12,8},{16,20},{20,16},{24,28},{28,24},{1,5},{5... | collective-permute-start | bytes 786440 | tf_op jit(solution)/shard_map/ppermute | solution.py:506
  12.8 1.5 %collective-permute-start.4 = (bf16[128,1024]{1,0:T(8,128)(2,1)S(1)}, bf16[128,1024]{1,0:T(8,128)(2,1)S(1)}, u32[]{:S(2)}, u32[]{:S(2)}) collective-permute-start(bf16[128,1024]{1,0:T(8,128)(2,1)S(1)} %join.1.refs_9_.refs_2_), channel_id=1, source_target_pairs={{0,2},{1,3},{2,0},{3,1},{4,6},{5,7},{6,4},{7,5},{8,10},{9,11},{10,... | collective-permute-start | bytes 786440 | tf_op jit(solution)/shard_map/ppermute | solution.py:506
  14.3 0.0 collective-permute-done.refs_8_
  14.3 7.2 %local.1 = (f32[256,1024]{1,0:T(8,128)S(1)}, f32[256,1024]{1,0:T(8,128)S(1)}, f32[256,128]{1,0:T(8,128)S(1)}, f32[136,512]{1,0:T(8,128)S(1)}, s16[144,512]{1,0:T(8,128)(2,1)S(1)}) custom-call(bf16[256,1024]{1,0:T(8,128)(2,1)} %refs_0_.7, bf16[256,128]{1,0:T(8,128)(2,1)} %refs_1_.5, bf16[256,128]{1,0:T(8,128)(2,1)} %refs_2_.3, f32[4,1024]{1,0:T(4,128)} %refs_3_.1, ...), custom_call_target="tpu_custom_call" | custom-call | flops 5000000000 | bytes 3387968 | tf_op jit(solution)/shard_map/local/pallas_call | solution.py:126
  21.6 1.0 %collective-permute-start.2 = (s16[144,512]{1,0:T(8,128)(2,1)S(1)}, s16[144,512]{1,0:T(8,128)(2,1)S(1)}, u32[]{:S(2)}, u32[]{:S(2)}) collective-permute-start(s16[144,512]{1,0:T(8,128)(2,1)S(1)} %get-tuple-element.19), channel_id=1, source_target_pairs={{0,4},{4,0},{8,12},{12,8},{16,20},{20,16},{24,28},{28,24},{1,5},{5... | collective-permute-start | bytes 442376 | tf_op jit(solution)/shard_map/ppermute | solution.py:506
  22.5 0.5 collective-permute-start.11
  23.0 3.7 %collective-permute-done.2.refs_1_ = s16[144,512]{1,0:T(8,128)(2,1)S(1)} collective-permute-done((s16[144,512]{1,0:T(8,128)(2,1)S(1)}, s16[144,512]{1,0:T(8,128)(2,1)S(1)}, u32[]{:S(2)}, u32[]{:S(2)}) %collective-permute-start.2) | collective-permute-done | bytes 147488 | tf_op jit(solution)/shard_map/ppermute | solution.py:506
  26.8 0.1 pair.1
  26.9 1.8 %collective-permute-start.6 = (s16[144,512]{1,0:T(8,128)(2,1)S(1)}, s16[144,512]{1,0:T(8,128)(2,1)S(1)}, u32[]{:S(2)}, u32[]{:S(2)}) collective-permute-start(s16[144,512]{1,0:T(8,128)(2,1)S(1)} %get-tuple-element.21), channel_id=1, source_target_pairs={{0,8},{4,12},{8,0},{12,4},{16,24},{20,28},{24,16},{28,20},{1,9},{5... | collective-permute-start | bytes 442376 | tf_op jit(solution)/shard_map/ppermute | solution.py:506
  28.7 0.5 collective-permute-start.13
  29.2 0.5 collective-permute-start.9
  29.7 2.4 %collective-permute-done.6.refs_1_.refs_3_ = s16[144,512]{1,0:T(8,128)(2,1)S(1)} collective-permute-done((s16[144,512]{1,0:T(8,128)(2,1)S(1)}, s16[144,512]{1,0:T(8,128)(2,1)S(1)}, u32[]{:S(2)}, u32[]{:S(2)}) %collective-permute-start.6) | collective-permute-done | bytes 147488 | tf_op jit(solution)/shard_map/ppermute | solution.py:506
  32.2 0.5 collective-permute-start.15
  32.7 0.1 four.1
  32.8 1.0 %collective-permute-start.8 = (bf16[128,1024]{1,0:T(8,128)(2,1)S(1)}, bf16[128,1024]{1,0:T(8,128)(2,1)S(1)}, u32[]{:S(2)}, u32[]{:S(2)}) collective-permute-start(bf16[128,1024]{1,0:T(8,128)(2,1)S(1)} %collective-permute-done.5.refs_4_.refs_5_.refs_2_), channel_id=1, source_target_pairs={{0,4},{4,0},{8,12},{12,8},{16,20},{20,16},{24,28},{28,24},{1,5},{5... | collective-permute-start | bytes 786440 | tf_op jit(solution)/shard_map/ppermute | solution.py:506
  33.8 0.3 collective-permute-start.7
  34.1 3.3 %collective-permute-done.9.refs_7_.refs_4_ = bf16[128,1024]{1,0:T(8,128)(2,1)S(1)} collective-permute-done((bf16[128,1024]{1,0:T(8,128)(2,1)S(1)}, bf16[128,1024]{1,0:T(8,128)(2,1)S(1)}, u32[]{:S(2)}, u32[]{:S(2)}) %collective-permute-start.9) | collective-permute-done | bytes 262176 | tf_op jit(solution)/shard_map/ppermute | solution.py:506
  37.4 0.4 collective-permute-start.10
  37.9 5.7 %experts.2.refs_9_.refs_8_ = bf16[1,512,1024]{2,1,0:T(8,128)(2,1)} custom-call(bf16[1,4096,1024]{2,1,0:T(8,128)(2,1)S(1)} %bitcast.4, bf16[1,4096,1024]{2,1,0:T(8,128)(2,1)S(1)} %copy-done, bf16[128,1024]{1,0:T(8,128)(2,1)S(1)} %join.1.refs_9_.refs_2_, bf16[128,1024]{1,0:T(8,128)(2,1)S(1)} %collective-permute-done.3.refs_2_.refs_3_, ...), custom_call_target="tpu_custom_call" | custom-call | flops 4294967296 | bytes 19927040 | tf_op jit(solution)/shard_map/experts/pallas_call | solution.py:126
  43.6 3.1 %collective-permute-done.10.refs_8_.refs_5_ = bf16[128,1024]{1,0:T(8,128)(2,1)S(1)} collective-permute-done((bf16[128,1024]{1,0:T(8,128)(2,1)S(1)}, bf16[128,1024]{1,0:T(8,128)(2,1)S(1)}, u32[]{:S(2)}, u32[]{:S(2)}) %collective-permute-start.10) | collective-permute-done | bytes 262176 | tf_op jit(solution)/shard_map/ppermute | solution.py:506
  46.7 0.4 turn.1
  47.1 0.1 collective-permute-start.17
  47.2 1.0 %collective-permute-start.16 = (s16[144,512]{1,0:T(8,128)(2,1)S(1)}, s16[144,512]{1,0:T(8,128)(2,1)S(1)}, u32[]{:S(2)}, u32[]{:S(2)}) collective-permute-start(s16[144,512]{1,0:T(8,128)(2,1)S(1)} %get-tuple-element.25), channel_id=1, source_target_pairs={{0,4},{4,0},{8,12},{12,8},{16,20},{20,16},{24,28},{28,24},{1,5},{5... | collective-permute-start | bytes 442376 | tf_op jit(solution)/shard_map/ppermute | solution.py:506
  48.2 1.7 %collective-permute-done.17.refs_6_ = bf16[512,1024]{1,0:T(8,128)(2,1)S(1)} collective-permute-done((bf16[512,1024]{1,0:T(8,128)(2,1)S(1)}, bf16[512,1024]{1,0:T(8,128)(2,1)S(1)}, u32[]{:S(2)}, u32[]{:S(2)}) %collective-permute-start.17) | collective-permute-done | bytes 1048608 | tf_op jit(solution)/shard_map/ppermute | solution.py:506
  49.8 5.7 %experts.3.refs_6_ = bf16[1,512,1024]{2,1,0:T(8,128)(2,1)} custom-call(bf16[1,4096,1024]{2,1,0:T(8,128)(2,1)S(1)} %bitcast.4, bf16[1,4096,1024]{2,1,0:T(8,128)(2,1)S(1)} %copy-done, bf16[128,1024]{1,0:T(8,128)(2,1)S(1)} %collective-permute-done.5.refs_4_.refs_5_.refs_2_, ...), custom_call_target="tpu_custom_call", output_to_operand_aliasing={{}: (8, {})} | custom-call | flops 4294967296 | bytes 20975616 | tf_op jit(solution)/shard_map/experts/pallas_call | solution.py:126
  55.5 3.1 %back.1 = bf16[256,1024]{1,0:T(8,128)(2,1)} custom-call(f32[1,1024]{1,0:T(1,128)} %bitcast.5, f32[256,1024]{1,0:T(8,128)S(1)} %get-tuple-element.15.refs_1_, f32[256,1024]{1,0:T(8,128)S(1)} %get-tuple-element.16.refs_2_, f32[256,128]{1,0:T(8,128)S(1)} %get-tuple-element.17.refs_3_, f32[128,512]{1,0:T(8,128)S(1)} %get-tuple-element.24.refs_4_, ...), custom_call_target="tpu_custom_call" | custom-call | flops 1000000000 | bytes 3166208 | tf_op jit(solution)/shard_map/back/pallas_call | solution.py:126
  (20 shorter events, 0.0 us)
Async XLA Ops:
  0.6 7.3 %collective-permute-start.1 = (bf16[64,1024]{1,0:T(8,128)(2,1)}, bf16[64,1024]{1,0:T(8,128)(2,1)S(1)}, u32[]{:S(2)}, u32[]{:S(2)}) collective-permute-start(bf16[64,1024]{1,0:T(8,128)(2,1)} %refs_0_.6), channel_id=1, source_target_pairs={{0,8},{4,12},{8,0},{12,4},{16,24},{20,28},{24,16},{28,20},{1,9},{5... | collective-permute-start | bytes 393224 | tf_op jit(solution)/shard_map/ppermute | solution.py:506
  4.5 9.8 %collective-permute-start = (bf16[16,1280]{1,0:T(8,128)(2,1)S(1)}, bf16[16,1280]{1,0:T(8,128)(2,1)S(1)}, u32[]{:S(2)}, u32[]{:S(2)}) collective-permute-start(bf16[16,1280]{1,0:T(8,128)(2,1)S(1)} %ends.1), channel_id=1, source_target_pairs={{0,4},{4,8},{8,12},{12,16},{16,20},{20,24},{24,28},{1,5},{5,9},{9,... | collective-permute-start | bytes 122888 | tf_op jit(solution)/shard_map/ppermute | solution.py:649
  7.9 29.9 %slice-start = ((s8[8388608]{0:T(1024)(128)(4,1)}), s8[4194304]{0:T(1024)(128)(4,1)S(1)}, s32[]{:S(2)}) async-start(s8[8388608]{0:T(1024)(128)(4,1)} %bitcast.3), calls=%async_computation | async-start | bytes 8388608
  9.0 17.8 %collective-permute-start.5 = (bf16[128,1024]{1,0:T(8,128)(2,1)S(1)}, bf16[128,1024]{1,0:T(8,128)(2,1)S(1)}, u32[]{:S(2)}, u32[]{:S(2)}) collective-permute-start(bf16[128,1024]{1,0:T(8,128)(2,1)S(1)} %join.1.refs_9_.refs_2_), channel_id=1, source_target_pairs={{0,16},{4,20},{8,24},{12,28},{16,0},{20,4},{24,8},{28,12},{1,17},{... | collective-permute-start | bytes 786440 | tf_op jit(solution)/shard_map/ppermute | solution.py:506
  11.7 10.9 %collective-permute-start.3 = (bf16[128,1024]{1,0:T(8,128)(2,1)S(1)}, bf16[128,1024]{1,0:T(8,128)(2,1)S(1)}, u32[]{:S(2)}, u32[]{:S(2)}) collective-permute-start(bf16[128,1024]{1,0:T(8,128)(2,1)S(1)} %join.1.refs_9_.refs_2_), channel_id=1, source_target_pairs={{0,4},{4,0},{8,12},{12,8},{16,20},{20,16},{24,28},{28,24},{1,5},{5... | collective-permute-start | bytes 786440 | tf_op jit(solution)/shard_map/ppermute | solution.py:506
  12.8 14.0 %collective-permute-start.4 = (bf16[128,1024]{1,0:T(8,128)(2,1)S(1)}, bf16[128,1024]{1,0:T(8,128)(2,1)S(1)}, u32[]{:S(2)}, u32[]{:S(2)}) collective-permute-start(bf16[128,1024]{1,0:T(8,128)(2,1)S(1)} %join.1.refs_9_.refs_2_), channel_id=1, source_target_pairs={{0,2},{1,3},{2,0},{3,1},{4,6},{5,7},{6,4},{7,5},{8,10},{9,11},{10,... | collective-permute-start | bytes 786440 | tf_op jit(solution)/shard_map/ppermute | solution.py:506
  14.3 23.5 %slice-start.1 = ((s8[8388608]{0:T(1024)(128)(4,1)}), s8[4194304]{0:T(1024)(128)(4,1)S(1)}, s32[]{:S(2)}) async-start(s8[8388608]{0:T(1024)(128)(4,1)} %bitcast.3), calls=%async_computation.1 | async-start | bytes 8388608
  14.3 23.5 %copy-start = (bf16[1,4096,1024]{2,1,0:T(8,128)(2,1)S(1)}, bf16[1,4096,1024]{2,1,0:T(8,128)(2,1)}, u32[]{:S(2)}) copy-start(bf16[1,4096,1024]{2,1,0:T(8,128)(2,1)} %refs_1_.7) | copy-start | bytes 25165828
  21.6 5.2 %collective-permute-start.2 = (s16[144,512]{1,0:T(8,128)(2,1)S(1)}, s16[144,512]{1,0:T(8,128)(2,1)S(1)}, u32[]{:S(2)}, u32[]{:S(2)}) collective-permute-start(s16[144,512]{1,0:T(8,128)(2,1)S(1)} %get-tuple-element.19), channel_id=1, source_target_pairs={{0,4},{4,0},{8,12},{12,8},{16,20},{20,16},{24,28},{28,24},{1,5},{5... | collective-permute-start | bytes 442376 | tf_op jit(solution)/shard_map/ppermute | solution.py:506
  22.5 9.6 %collective-permute-start.11 = (bf16[128,1024]{1,0:T(8,128)(2,1)S(1)}, bf16[128,1024]{1,0:T(8,128)(2,1)S(1)}, u32[]{:S(2)}, u32[]{:S(2)}) collective-permute-start(bf16[128,1024]{1,0:T(8,128)(2,1)S(1)} %collective-permute-done.3.refs_2_.refs_3_), channel_id=1, source_target_pairs={{0,2},{1,3},{2,0},{3,1},{4,6},{5,7},{6,4},{7,5},{8,10},{9,11},{10,... | collective-permute-start | bytes 786440 | tf_op jit(solution)/shard_map/ppermute | solution.py:506
  26.9 5.2 %collective-permute-start.6 = (s16[144,512]{1,0:T(8,128)(2,1)S(1)}, s16[144,512]{1,0:T(8,128)(2,1)S(1)}, u32[]{:S(2)}, u32[]{:S(2)}) collective-permute-start(s16[144,512]{1,0:T(8,128)(2,1)S(1)} %get-tuple-element.21), channel_id=1, source_target_pairs={{0,8},{4,12},{8,0},{12,4},{16,24},{20,28},{24,16},{28,20},{1,9},{5... | collective-permute-start | bytes 442376 | tf_op jit(solution)/shard_map/ppermute | solution.py:506
  28.7 4.1 %collective-permute-start.12 = (bf16[128,1024]{1,0:T(8,128)(2,1)S(1)}, bf16[128,1024]{1,0:T(8,128)(2,1)S(1)}, u32[]{:S(2)}, u32[]{:S(2)}) collective-permute-start(bf16[128,1024]{1,0:T(8,128)(2,1)S(1)} %join.1.refs_9_.refs_2_), channel_id=1, source_target_pairs={{0,1},{1,0},{2,3},{3,2},{4,5},{5,4},{6,7},{7,6},{8,9},{9,8},{10,11... | collective-permute-start | bytes 786440 | tf_op jit(solution)/shard_map/ppermute | solution.py:506
  28.7 5.1 %collective-permute-start.13 = (bf16[128,1024]{1,0:T(8,128)(2,1)S(1)}, bf16[128,1024]{1,0:T(8,128)(2,1)S(1)}, u32[]{:S(2)}, u32[]{:S(2)}) collective-permute-start(bf16[128,1024]{1,0:T(8,128)(2,1)S(1)} %collective-permute-done.3.refs_2_.refs_3_), channel_id=1, source_target_pairs={{0,1},{1,0},{2,3},{3,2},{4,5},{5,4},{6,7},{7,6},{8,9},{9,8},{10,11... | collective-permute-start | bytes 786440 | tf_op jit(solution)/shard_map/ppermute | solution.py:506
  29.2 8.2 %collective-permute-start.9 = (bf16[128,1024]{1,0:T(8,128)(2,1)S(1)}, bf16[128,1024]{1,0:T(8,128)(2,1)S(1)}, u32[]{:S(2)}, u32[]{:S(2)}) collective-permute-start(bf16[128,1024]{1,0:T(8,128)(2,1)S(1)} %collective-permute-done.5.refs_4_.refs_5_.refs_2_), channel_id=1, source_target_pairs={{0,2},{1,3},{2,0},{3,1},{4,6},{5,7},{6,4},{7,5},{8,10},{9,11},{10,... | collective-permute-start | bytes 786440 | tf_op jit(solution)/shard_map/ppermute | solution.py:506
  32.2 5.7 %collective-permute-start.14 = (bf16[128,1024]{1,0:T(8,128)(2,1)S(1)}, bf16[128,1024]{1,0:T(8,128)(2,1)S(1)}, u32[]{:S(2)}, u32[]{:S(2)}) collective-permute-start(bf16[128,1024]{1,0:T(8,128)(2,1)S(1)} %collective-permute-done.4.refs_3_.refs_4_), channel_id=1, source_target_pairs={{0,1},{1,0},{2,3},{3,2},{4,5},{5,4},{6,7},{7,6},{8,9},{9,8},{10,11... | collective-permute-start | bytes 786440 | tf_op jit(solution)/shard_map/ppermute | solution.py:506
  32.2 5.7 %collective-permute-start.15 = (bf16[128,1024]{1,0:T(8,128)(2,1)S(1)}, bf16[128,1024]{1,0:T(8,128)(2,1)S(1)}, u32[]{:S(2)}, u32[]{:S(2)}) collective-permute-start(bf16[128,1024]{1,0:T(8,128)(2,1)S(1)} %collective-permute-done.11.refs_5_), channel_id=1, source_target_pairs={{0,1},{1,0},{2,3},{3,2},{4,5},{5,4},{6,7},{7,6},{8,9},{9,8},{10,11... | collective-permute-start | bytes 786440 | tf_op jit(solution)/shard_map/ppermute | solution.py:506
  32.8 10.7 %collective-permute-start.8 = (bf16[128,1024]{1,0:T(8,128)(2,1)S(1)}, bf16[128,1024]{1,0:T(8,128)(2,1)S(1)}, u32[]{:S(2)}, u32[]{:S(2)}) collective-permute-start(bf16[128,1024]{1,0:T(8,128)(2,1)S(1)} %collective-permute-done.5.refs_4_.refs_5_.refs_2_), channel_id=1, source_target_pairs={{0,4},{4,0},{8,12},{12,8},{16,20},{20,16},{24,28},{28,24},{1,5},{5... | collective-permute-start | bytes 786440 | tf_op jit(solution)/shard_map/ppermute | solution.py:506
  33.8 9.8 %collective-permute-start.7 = (s16[144,512]{1,0:T(8,128)(2,1)S(1)}, s16[144,512]{1,0:T(8,128)(2,1)S(1)}, u32[]{:S(2)}, u32[]{:S(2)}) collective-permute-start(s16[144,512]{1,0:T(8,128)(2,1)S(1)} %get-tuple-element.22), channel_id=1, source_target_pairs={{0,16},{4,20},{8,24},{12,28},{16,0},{20,4},{24,8},{28,12},{1,17},{... | collective-permute-start | bytes 442376 | tf_op jit(solution)/shard_map/ppermute | solution.py:506
  37.4 9.3 %collective-permute-start.10 = (bf16[128,1024]{1,0:T(8,128)(2,1)S(1)}, bf16[128,1024]{1,0:T(8,128)(2,1)S(1)}, u32[]{:S(2)}, u32[]{:S(2)}) collective-permute-start(bf16[128,1024]{1,0:T(8,128)(2,1)S(1)} %collective-permute-done.9.refs_7_.refs_4_), channel_id=1, source_target_pairs={{0,4},{4,0},{8,12},{12,8},{16,20},{20,16},{24,28},{28,24},{1,5},{5... | collective-permute-start | bytes 786440 | tf_op jit(solution)/shard_map/ppermute | solution.py:506
  47.1 2.7 %collective-permute-start.17 = (bf16[512,1024]{1,0:T(8,128)(2,1)S(1)}, bf16[512,1024]{1,0:T(8,128)(2,1)S(1)}, u32[]{:S(2)}, u32[]{:S(2)}) collective-permute-start(bf16[512,1024]{1,0:T(8,128)(2,1)S(1)} %get-tuple-element.26), channel_id=1, source_target_pairs={{0,1},{1,0},{2,3},{3,2},{4,5},{5,4},{6,7},{7,6},{8,9},{9,8},{10,11... | collective-permute-start | bytes 3145736 | tf_op jit(solution)/shard_map/ppermute | solution.py:506
  47.2 8.3 %collective-permute-start.16 = (s16[144,512]{1,0:T(8,128)(2,1)S(1)}, s16[144,512]{1,0:T(8,128)(2,1)S(1)}, u32[]{:S(2)}, u32[]{:S(2)}) collective-permute-start(s16[144,512]{1,0:T(8,128)(2,1)S(1)} %get-tuple-element.25), channel_id=1, source_target_pairs={{0,4},{4,0},{8,12},{12,8},{16,20},{20,16},{24,28},{28,24},{1,5},{5... | collective-permute-start | bytes 442376 | tf_op jit(solution)/shard_map/ppermute | solution.py:506

commit v13 on v10

--- a/solution.py
+++ b/solution.py
@@ -160,14 +160,14 @@
     )
 
 
-def local_body(paired, count, *refs):
+def front_body(paired, count, *refs):
     far, outs, rest = refs[:count], refs[count : count + 3], refs[count + 3 :]
     ends = rest[: 1 + paired]
     rest = rest[1 + paired :]
     near, scratch, pad_ref, sems = rest[:count], rest[count : count + 3], rest[-2], rest[-1]
     copies = started(far, near, sems)
-    x_ref, b_ref, c_ref, taps_ref, taps_bc_ref, logs_ref, skip_ref, ids_ref, ends_ref = near
-    pre_ref, decay_ref, c_out_ref = scratch
+    x_ref, b_ref, c_ref, taps_ref, taps_bc_ref, logs_ref, ids_ref, ends_ref = near
+    xconv_ref, bc_ref, lines_ref = scratch
     tokens, channels = x_ref.shape
     heads = logs_ref.shape[0]
     finished(copies)
@@ -184,23 +184,19 @@
         return silu(total)
 
     bc = conv(taps_bc_ref[...], channels, channels + 2 * STATE)
-    bmat, cmat = bc[:, :STATE], bc[:, STATE:]
-    c_out_ref[...] = cmat
+    bc_ref[...] = bc
+    xconv = conv(taps_ref[...], 0, channels)
+    xconv_ref[...] = xconv
     logs = logs_ref[...]
     inflow = jnp.sqrt(one_minus_exp(2.0 * logs))
     row = dot_exact(logs, upper_ones(tokens))
-    column = row.T
+    lines_ref[0] = row
+    lines_ref[1] = inflow
+    copies = started(scratch, outs, sems)
     total = row[:, tokens - 1 :]
     spread = head_spread(heads)
-    decay_ref[...] = dot_left(jnp.exp(row), spread, FIRST)
-    copies = started(scratch[1:], outs[1:], sems)
-
-    xconv = conv(taps_ref[...], 0, channels)
-    pad_ref[:tokens, :channels] = xconv
-    drive = xconv * dot_left(inflow, spread, FIRST)
-    pre_ref[...] = drive
-    fresh = drive * dot_left(jnp.exp(total - row), spread, FIRST)
-    state = dot(bmat, fresh, FIRST)
+    fresh = xconv * dot_left(inflow * jnp.exp(total - row), spread, FIRST)
+    state = dot(bc[:, :STATE], fresh, FIRST)
     total = jnp.broadcast_to(total, (heads, NOTES))
     if paired:
         total = dot_exact(total, spread, FIRST)
@@ -219,23 +215,37 @@
     else:
         ends[0][:STATE] = state
         ends[0][STATE:] = dot_exact(jnp.exp(total), spread, FIRST)
-
+    finished(copies)
+
+
+def inner_body(skip_far, xconv_far, bc_far, lines_far, pre_far, decay_far, *rest):
+    far = (skip_far, xconv_far, bc_far, lines_far)
+    skip_ref, xconv_ref, bc_ref, lines_ref, pre_ref, decay_ref, sems = rest
+    finished(started(far, rest[:4], sems))
+    tokens, channels = xconv_ref.shape
+    heads = channels // HDIM
+    row = lines_ref[0]
+    column = row.T
+    spread = head_spread(heads)
+    decay_ref[...] = dot_left(jnp.exp(row), spread, FIRST)
+    copies = started([decay_ref], [decay_far], sems)
+    inflow = dot_left(lines_ref[1], spread, FIRST)
     skip = dot_exact(skip_ref[...], spread)
-    meet = dot(cmat, bmat, ((1,), (1,)))
+    meet = dot(bc_ref[:, STATE:], bc_ref[:, :STATE], ((1,), (1,)))
     lower = iota((tokens, tokens), 0) >= iota((tokens, tokens), 1)
     left = iota((tokens, 2 * HDIM), 1) < HDIM
     for pair in range(heads // 2):
         cut = slice(pair * 2 * HDIM, (pair + 1) * 2 * HDIM)
-        d_high, d_low = halves(pre_ref[:, cut])
+        xconv = xconv_ref[:, cut]
+        d_high, d_low = halves(xconv * inflow[:, cut])
         both = []
         for h in (2 * pair, 2 * pair + 1):
             gap = column[:, h : h + 1] - row[h : h + 1, :]
             mix = jnp.where(lower, jnp.exp(gap), 0.0) * meet
             m_high, m_low = halves(mix)
             both.append(dot16(m_high, d_high) + dot16(m_high, d_low) + dot16(m_low, d_high))
-        direct = skip[:, cut] * pad_ref[:tokens, cut]
-        pre_ref[:, cut] = direct + jnp.where(left, both[0], both[1])
-    finished(copies + started(scratch[:1], outs[:1], sems, 2))
+        pre_ref[:, cut] = skip[:, cut] * xconv + jnp.where(left, both[0], both[1])
+    finished(copies + started([pre_ref], [pre_far], sems, 1))
 
 
 def put(ref, state, logsum, line):
@@ -284,7 +294,8 @@
     return here % 2, (here // 2) % 2, here // 4
 
 
-def pair_body(width, own_ref, got_ref, pair_ref, sent_ref):
+def pair_body(width, own_ref, got_ref, rows_ref, pair_ref, sent_ref, same_rows_ref):
+    same_rows_ref[...] = rows_ref[...]
     x, _, _ = place()
     pair = together(x == 0, taken(own_ref), received(got_ref), width)
     put(pair_ref, *pair)
@@ -355,10 +366,10 @@
             state = parts_ref[i, STATE : STATE + 1] * state + parts_ref[i, :STATE]
 
 
-def back_body(paired, gain_far, pre_far, decay_far, c_far, *rest):
+def back_body(paired, gain_far, pre_far, decay_far, bc_far, *rest):
     starts, (out_far, *rest) = rest[: 1 + paired], rest[1 + paired :]
-    far = (gain_far, pre_far, decay_far, c_far)
-    gain_ref, pre_ref, decay_ref, c_ref, out_ref, sems = rest
+    far = (gain_far, pre_far, decay_far, bc_far)
+    gain_ref, pre_ref, decay_ref, bc_ref, out_ref, sems = rest
     copies = started(far, rest[:4], sems)
     channels = pre_ref.shape[1]
     width = min(channels, 4 * HDIM)
@@ -371,7 +382,7 @@
     else:
         start = starts[0][...]
     finished(copies)
-    c_high, c_low = halves(c_ref[...])
+    c_high, c_low = halves(bc_ref[:, STATE:])
     copies = []
     for i in range(channels // width):
         cut = slice(i * width, (i + 1) * width)
@@ -384,39 +395,40 @@
     finished(copies)
 
 
-def entering_by_pairs(keep, sent, width, follow, pieces, meanwhile):
+def entering_by_pairs(keep, sent, width, pre, near_pieces, far_rows, meanwhile):
     pair_array, sent_array = array(keep.shape, F32), array(sent.shape, jnp.int16)
     ids_array = array((8, width), F32)
-    joined_array = [array((4 * p[0].shape[0], p[0].shape[1]), BF16) for p in pieces]
+    joined_array = array((4 * far_rows.shape[0], far_rows.shape[1]), BF16)
     got = swapped(sent, "ctx", 1)
-    pair, sent = call(
+    pair, sent, rows = call(
         functools.partial(pair_body, width),
-        [pair_array, sent_array],
-        (keep, got),
+        [pair_array, sent_array, array(far_rows.shape, BF16)],
+        (keep, got, far_rows),
         near=True,
-        after=follow,
+        after=(*near_pieces[2:], pre),
         name="pair",
     )
+    far_pieces = spread_rows(rows, 1)
     pair_got = swapped(sent, "ctx", 2)
     sent, ids, joined = call(
         functools.partial(four_body, width),
-        [sent_array, ids_array, joined_array[0]],
-        (pair, pair_got, *pieces[0]),
+        [sent_array, ids_array, joined_array],
+        (pair, pair_got, *near_pieces),
         near=True,
-        after=pieces[1][1:3],
+        after=far_pieces[1:3],
         name="four",
     )
     four_got = swapped(sent, "ctx", 4)
     done = meanwhile(ids, joined)
     mine, sent, ids, joined = call(
         functools.partial(turn_body, width),
-        [array((STATE, keep.shape[1]), F32), sent_array, ids_array, joined_array[1]],
-        (keep, got, pair, pair_got, four_got, *pieces[1]),
+        [array((STATE, keep.shape[1]), F32), sent_array, ids_array, joined_array],
+        (keep, got, pair, pair_got, four_got, *far_pieces),
         near=True,
         after_far=(done,),
         name="turn",
     )
-    return (mine, swapped(sent, "ctx", 1)), ids, joined, done
+    return (mine, swapped(sent, "ctx", 1)), far_pieces, ids, joined, done
 
 
 def entering_by_rows(state):
@@ -436,46 +448,57 @@
 
 
 def mixing(
-    pieces, meanwhile, seq_input, b_input, c_input, before, conv_x, conv_bc, log_decay, skip, gain, ids
+    rows, meanwhile, seq_input, b_input, c_input, before, conv_x, conv_bc, log_decay, skip, gain, ids
 ):
     tokens, channels = seq_input.shape
     heads = skip.shape[0]
     width = 2 * ids.shape[0]
-    paired = pieces is not None
+    paired = rows is not None
     outs = [
         array((tokens, channels), F32),
-        array((tokens, channels), F32),
-        array((tokens, STATE), F32),
+        array((tokens, 2 * STATE), F32),
+        array((2, heads, tokens), F32),
     ]
     if paired:
         ends = [array((STATE + NOTES, channels // 2), F32)]
         ends.append(array((STATE + 16, channels // 2), jnp.int16))
     else:
         ends = [array((STATE + NOTES, channels), F32)]
-    args = (seq_input, b_input, c_input, conv_x, conv_bc, log_decay)
-    args = (*args, skip.reshape(1, heads), ids.T, before)
-    pre, decay, cmat, *ends = call(
-        functools.partial(local_body, paired, len(args)),
+    args = (seq_input, b_input, c_input, conv_x, conv_bc, log_decay, ids.T, before)
+    xconv, bc, lines, *ends = call(
+        functools.partial(front_body, paired, len(args)),
         outs + ends,
         args,
         fixed=len(args) - 1,
         near_outs=len(ends),
-        after=pieces[0][:1] if paired else (),
+        after=rows[0][:1] if paired else (),
         scratch=room(args) + room(outs) + [pltpu.VMEM((8 + tokens, channels + 2 * STATE), F32)],
         sems=len(args),
         flops=5 * 10**9,
         grant=20,
-        name="local",
+        name="front",
+    )
+    args = (skip.reshape(1, heads), xconv, bc, lines)
+    outs = [array((tokens, channels), F32)] * 2
+    pre, decay = call(
+        inner_body,
+        outs,
+        args,
+        fixed=1,
+        scratch=room(args) + room(outs),
+        sems=4,
+        flops=4 * 10**9,
+        grant=16,
+        name="inner",
     )
     late = None
     if paired:
-        follow = (*pieces[0][1:3], pieces[1][0])
-        starts, *late = entering_by_pairs(*ends, width, follow, pieces, meanwhile)
+        starts, *late = entering_by_pairs(*ends, width, pre, *rows, meanwhile)
     else:
         starts = (entering_by_rows(ends[0]),)
 
     def finish(after=()):
-        args = (gain.reshape(1, channels), pre, decay, cmat)
+        args = (gain.reshape(1, channels), pre, decay, bc)
         outs = [array((tokens, channels), BF16)]
         return call(
             functools.partial(back_body, paired),
@@ -567,12 +590,10 @@
     return joined, swapped(joined, "ctx", 4)
 
 
-def gathered(moe_input):
-    z = along_z(moe_input)
-    x = [swapped(a, "ctx", 1) for a in z]
-    y = [swapped(a, "exp", 2) for a in z]
-    d = (swapped(x[0], "exp", 2), swapped(y[1], "ctx", 1))
-    return list(zip(z, x, y, d))
+def spread_rows(z, through):
+    x, y = swapped(z, "ctx", 1), swapped(z, "exp", 2)
+    d = swapped(y, "ctx", 1) if through else swapped(x, "exp", 2)
+    return (z, x, y, d)
 
 
 def experts_by_tokens(part, pieces, joined, ids, w_gate, w_up, so_far):
@@ -647,7 +668,8 @@
     before = lax.ppermute(ends, "ctx", [(i, i + 1) for i in range(ctx - 1)])
     pieces = meanwhile = None
     if by_tokens:
-        pieces = gathered(moe_input)
+        near_rows, far_rows = along_z(moe_input)
+        pieces = spread_rows(near_rows, 0), far_rows
 
         def meanwhile(ids, joined):
             return experts_by_tokens(0, pieces[0], joined, ids, w_gate, w_up, None)
@@ -667,8 +689,8 @@
         expert_ids,
     )
     if by_tokens:
-        ids, joined, hidden = late
-        hidden = experts_by_tokens(1, pieces[1], joined, ids, w_gate, w_up, hidden)
+        far_pieces, ids, joined, hidden = late
+        hidden = experts_by_tokens(1, far_pieces, joined, ids, w_gate, w_up, hidden)
         mixed = finish((hidden,))
     else:
         mixed = finish()

time: 59.4 us -> 56.7 us (0.955)
  waiting for transfers between devices: 14.9 us -> 10.2 us
  Pallas kernels: 24.3 us -> 25.8 us
    ppermute x14, waiting for transfers between devices: 14.9 us -> 10.2 us  [swapped(): lax.ppermute(block, axis, [(i, i ^ bit) for i in range(lax.axis_size(axis...]
    pallas_call x9 -> x10, Pallas kernels: 24.3 us -> 25.8 us  [call(): pl.pallas_call(body, out_shape=outs, in_specs=[pl.BlockSpec(memory_space=...]
  transfers between devices with their start and end apart: 15 -> 15, of which waited for: 7 -> 7; matrix products, arithmetic and copies ran while one was open for 0% -> 0% of each run, Pallas kernels for 35% -> 39%
where the time goes in v13:
time: 56.7 us; the launch traced here: 56.4 us
  Pallas kernels  25.8 us (46%)
  starting transfers between devices  19.5 us (34%)
  waiting for transfers between devices  10.2 us (18%)
  between operations  0.95 us (2%)
    pallas_call x10, Pallas kernels, call(): pl.pallas_call(body, out_shape=outs, in_specs=[pl.BlockSpec(memory_space=...  25.8 us
    ppermute x14, starting transfers between devices, swapped(): lax.ppermute(block, axis, [(i, i ^ bit) for i in range(lax.axis_size(axis...  16.1 us
    ppermute x14, waiting for transfers between devices, swapped(): lax.ppermute(block, axis, [(i, i ^ bit) for i in range(lax.axis_size(axis...  10.2 us
    ppermute x1, starting transfers between devices, on_device(): before = lax.ppermute(ends, 'ctx', [(i, i + 1) for i in range(ctx - 1)])  3.4 us
  transfers between devices with their start and end apart: 15, of which 7 were waited for; matrix products, arithmetic and copies ran while one was open for 0% of the time, Pallas kernels for 39%

profile of v13, /device:TPU:0, one launch (start us, length us, event | category | flops | bytes accessed | tf_op | source)
XLA Modules:
  0.0 56.4 jit_solution(14217990374346797458)
XLA Ops:
  0.6 3.1 %collective-permute-start.1 = (bf16[64,1024]{1,0:T(8,128)(2,1)}, bf16[64,1024]{1,0:T(8,128)(2,1)S(1)}, u32[]{:S(2)}, u32[]{:S(2)}) collective-permute-start(bf16[64,1024]{1,0:T(8,128)(2,1)} %refs_0_.6), channel_id=1, source_target_pairs={{0,8},{4,12},{8,0},{12,4},{16,24},{20,28},{24,16},{28,20},{1,9},{5... | collective-permute-start | bytes 393224 | tf_op jit(solution)/shard_map/ppermute | solution.py:531
  3.7 0.8 %ends.1 = bf16[16,1280]{1,0:T(8,128)(2,1)S(1)} custom-call(bf16[256,1024]{1,0:T(8,128)(2,1)} %refs_0_.7, bf16[256,128]{1,0:T(8,128)(2,1)} %refs_1_.5, bf16[256,128]{1,0:T(8,128)(2,1)} %refs_2_.3), custom_call_target="tpu_custom_call" | custom-call | bytes 696320 | tf_op jit(solution)/shard_map/ends/pallas_call | solution.py:126
  4.5 3.4 %collective-permute-start = (bf16[16,1280]{1,0:T(8,128)(2,1)S(1)}, bf16[16,1280]{1,0:T(8,128)(2,1)S(1)}, u32[]{:S(2)}, u32[]{:S(2)}) collective-permute-start(bf16[16,1280]{1,0:T(8,128)(2,1)S(1)} %ends.1), channel_id=1, source_target_pairs={{0,4},{4,8},{8,12},{12,16},{16,20},{20,24},{24,28},{1,5},{5,9},{9,... | collective-permute-start | bytes 122888 | tf_op jit(solution)/shard_map/ppermute | solution.py:668
  7.9 0.9 %join.1.refs_8_.refs_2_ = bf16[128,1024]{1,0:T(8,128)(2,1)S(1)} custom-call(bf16[64,1024]{1,0:T(8,128)(2,1)} %refs_0_.6, bf16[64,1024]{1,0:T(8,128)(2,1)S(1)} %collective-permute-done.1.refs_1_), custom_call_target="tpu_custom_call" | custom-call | bytes 524288 | tf_op jit(solution)/shard_map/join/pallas_call | solution.py:126
  8.9 1.2 %collective-permute-start.5 = (bf16[128,1024]{1,0:T(8,128)(2,1)S(1)}, bf16[128,1024]{1,0:T(8,128)(2,1)S(1)}, u32[]{:S(2)}, u32[]{:S(2)}) collective-permute-start(bf16[128,1024]{1,0:T(8,128)(2,1)S(1)} %join.1.refs_8_.refs_2_), channel_id=1, source_target_pairs={{0,4},{4,0},{8,12},{12,8},{16,20},{20,16},{24,28},{28,24},{1,5},{5... | collective-permute-start | bytes 786440 | tf_op jit(solution)/shard_map/ppermute | solution.py:531
  10.1 1.5 %collective-permute-start.4 = (bf16[128,1024]{1,0:T(8,128)(2,1)S(1)}, bf16[128,1024]{1,0:T(8,128)(2,1)S(1)}, u32[]{:S(2)}, u32[]{:S(2)}) collective-permute-start(bf16[128,1024]{1,0:T(8,128)(2,1)S(1)} %join.1.refs_8_.refs_2_), channel_id=1, source_target_pairs={{0,2},{1,3},{2,0},{3,1},{4,6},{5,7},{6,4},{7,5},{8,10},{9,11},{10,... | collective-permute-start | bytes 786440 | tf_op jit(solution)/shard_map/ppermute | solution.py:531
  11.6 2.6 %collective-permute-start.3 = (bf16[128,1024]{1,0:T(8,128)(2,1)S(1)}, bf16[128,1024]{1,0:T(8,128)(2,1)S(1)}, u32[]{:S(2)}, u32[]{:S(2)}) collective-permute-start(bf16[128,1024]{1,0:T(8,128)(2,1)S(1)} %join.1.refs_8_.refs_2_), channel_id=1, source_target_pairs={{0,16},{4,20},{8,24},{12,28},{16,0},{20,4},{24,8},{28,12},{1,17},{... | collective-permute-start | bytes 786440 | tf_op jit(solution)/shard_map/ppermute | solution.py:531
  14.2 4.4 %front.1 = (f32[256,1024]{1,0:T(8,128)S(1)}, f32[256,256]{1,0:T(8,128)S(1)}, f32[2,16,256]{2,1,0:T(8,128)S(1)}, f32[136,512]{1,0:T(8,128)S(1)}, s16[144,512]{1,0:T(8,128)(2,1)S(1)}) custom-call(bf16[256,1024]{1,0:T(8,128)(2,1)} %refs_0_.7, bf16[256,128]{1,0:T(8,128)(2,1)} %refs_1_.5, bf16[256,128]{1,0:T(8,128)(2,1)} %refs_2_.3, f32[4,1024]{1,0:T(4,128)} %refs_3_.1, ...), custom_call_target="tpu_custom_call" | custom-call | flops 5000000000 | bytes 2503168 | tf_op jit(solution)/shard_map/front/pallas_call | solution.py:126
  18.6 0.9 %collective-permute-start.2 = (s16[144,512]{1,0:T(8,128)(2,1)S(1)}, s16[144,512]{1,0:T(8,128)(2,1)S(1)}, u32[]{:S(2)}, u32[]{:S(2)}) collective-permute-start(s16[144,512]{1,0:T(8,128)(2,1)S(1)} %get-tuple-element.25), channel_id=1, source_target_pairs={{0,4},{4,0},{8,12},{12,8},{16,20},{20,16},{24,28},{28,24},{1,5},{5... | collective-permute-start | bytes 442376 | tf_op jit(solution)/shard_map/ppermute | solution.py:531
  19.6 0.5 collective-permute-start.6
  20.1 4.4 %inner.1 = (f32[256,1024]{1,0:T(8,128)S(1)}, f32[256,1024]{1,0:T(8,128)S(1)}) custom-call(f32[1,16]{1,0:T(1,128)} %bitcast.9, f32[256,1024]{1,0:T(8,128)S(1)} %get-tuple-element.19.refs_1_, f32[256,256]{1,0:T(8,128)S(1)} %get-tuple-element.20.refs_2_.refs_3_, f32[2,16,256]{2,1,0:T(8,128)S(1)} %get-tuple-element.21.refs_3_), custom_call_target="tpu_custom_call" | custom-call | flops 4000000000 | bytes 3440704 | tf_op jit(solution)/shard_map/inner/pallas_call | solution.py:126
  24.5 0.2 collective-permute-done.3.refs_2_
  24.7 1.2 %collective-permute-done.6.refs_4_.refs_5_ = bf16[128,1024]{1,0:T(8,128)(2,1)S(1)} collective-permute-done((bf16[128,1024]{1,0:T(8,128)(2,1)S(1)}, bf16[128,1024]{1,0:T(8,128)(2,1)S(1)}, u32[]{:S(2)}, u32[]{:S(2)}) %collective-permute-start.6) | collective-permute-done | bytes 262176 | tf_op jit(solution)/shard_map/ppermute | solution.py:531
  25.9 0.2 pair.1
  26.1 1.2 %collective-permute-start.8 = (bf16[128,1024]{1,0:T(8,128)(2,1)S(1)}, bf16[128,1024]{1,0:T(8,128)(2,1)S(1)}, u32[]{:S(2)}, u32[]{:S(2)}) collective-permute-start(bf16[128,1024]{1,0:T(8,128)(2,1)S(1)} %get-tuple-element.28.refs_5_.refs_2_), channel_id=1, source_target_pairs={{0,4},{4,0},{8,12},{12,8},{16,20},{20,16},{24,28},{28,24},{1,5},{5... | collective-permute-start | bytes 786440 | tf_op jit(solution)/shard_map/ppermute | solution.py:531
  27.3 0.5 collective-permute-start.9
  27.8 1.7 %collective-permute-start.7 = (s16[144,512]{1,0:T(8,128)(2,1)S(1)}, s16[144,512]{1,0:T(8,128)(2,1)S(1)}, u32[]{:S(2)}, u32[]{:S(2)}) collective-permute-start(s16[144,512]{1,0:T(8,128)(2,1)S(1)} %get-tuple-element.27), channel_id=1, source_target_pairs={{0,8},{4,12},{8,0},{12,4},{16,24},{20,28},{24,16},{28,20},{1,9},{5... | collective-permute-start | bytes 442376 | tf_op jit(solution)/shard_map/ppermute | solution.py:531
  29.5 3.4 %collective-permute-done.7.refs_1_.refs_3_ = s16[144,512]{1,0:T(8,128)(2,1)S(1)} collective-permute-done((s16[144,512]{1,0:T(8,128)(2,1)S(1)}, s16[144,512]{1,0:T(8,128)(2,1)S(1)}, u32[]{:S(2)}, u32[]{:S(2)}) %collective-permute-start.7) | collective-permute-done | bytes 147488 | tf_op jit(solution)/shard_map/ppermute | solution.py:531
  33.0 0.7 %collective-permute-done.9.refs_7_.refs_4_ = bf16[128,1024]{1,0:T(8,128)(2,1)S(1)} collective-permute-done((bf16[128,1024]{1,0:T(8,128)(2,1)S(1)}, bf16[128,1024]{1,0:T(8,128)(2,1)S(1)}, u32[]{:S(2)}, u32[]{:S(2)}) %collective-permute-start.9) | collective-permute-done | bytes 262176 | tf_op jit(solution)/shard_map/ppermute | solution.py:531
  33.7 0.2 four.1
  33.9 0.1 collective-permute-start.12
  34.0 0.4 collective-permute-start.10
  34.4 1.3 %collective-permute-start.11 = (bf16[128,1024]{1,0:T(8,128)(2,1)S(1)}, bf16[128,1024]{1,0:T(8,128)(2,1)S(1)}, u32[]{:S(2)}, u32[]{:S(2)}) collective-permute-start(bf16[128,1024]{1,0:T(8,128)(2,1)S(1)} %collective-permute-done.9.refs_7_.refs_4_), channel_id=1, source_target_pairs={{0,4},{4,0},{8,12},{12,8},{16,20},{20,16},{24,28},{28,24},{1,5},{5... | collective-permute-start | bytes 786440 | tf_op jit(solution)/shard_map/ppermute | solution.py:531
  35.7 0.9 %collective-permute-done.12.refs_6_ = bf16[512,1024]{1,0:T(8,128)(2,1)S(1)} collective-permute-done((bf16[512,1024]{1,0:T(8,128)(2,1)S(1)}, bf16[512,1024]{1,0:T(8,128)(2,1)S(1)}, u32[]{:S(2)}, u32[]{:S(2)}) %collective-permute-start.12) | collective-permute-done | bytes 1048608 | tf_op jit(solution)/shard_map/ppermute | solution.py:531
  36.7 5.7 %experts.2.refs_9_.refs_8_ = bf16[1,512,1024]{2,1,0:T(8,128)(2,1)} custom-call(bf16[1,4096,1024]{2,1,0:T(8,128)(2,1)S(1)} %bitcast.4, bf16[1,4096,1024]{2,1,0:T(8,128)(2,1)S(1)} %bitcast.6, bf16[128,1024]{1,0:T(8,128)(2,1)S(1)} %join.1.refs_8_.refs_2_, bf16[128,1024]{1,0:T(8,128)(2,1)S(1)} %collective-permute-done.5.refs_3_, ...), custom_call_target="tpu_custom_call" | custom-call | flops 4294967296 | bytes 19927040 | tf_op jit(solution)/shard_map/experts/pallas_call | solution.py:126
  42.4 1.9 %collective-permute-done.10.refs_4_ = s16[144,512]{1,0:T(8,128)(2,1)S(1)} collective-permute-done((s16[144,512]{1,0:T(8,128)(2,1)S(1)}, s16[144,512]{1,0:T(8,128)(2,1)S(1)}, u32[]{:S(2)}, u32[]{:S(2)}) %collective-permute-start.10) | collective-permute-done | bytes 147488 | tf_op jit(solution)/shard_map/ppermute | solution.py:531
  44.3 0.4 turn.1
  44.7 0.1 collective-permute-start.14
  44.8 0.9 %collective-permute-start.13 = (s16[144,512]{1,0:T(8,128)(2,1)S(1)}, s16[144,512]{1,0:T(8,128)(2,1)S(1)}, u32[]{:S(2)}, u32[]{:S(2)}) collective-permute-start(s16[144,512]{1,0:T(8,128)(2,1)S(1)} %get-tuple-element.33), channel_id=1, source_target_pairs={{0,4},{4,0},{8,12},{12,8},{16,20},{20,16},{24,28},{28,24},{1,5},{5... | collective-permute-start | bytes 442376 | tf_op jit(solution)/shard_map/ppermute | solution.py:531
  45.7 1.7 %collective-permute-done.14.refs_6_ = bf16[512,1024]{1,0:T(8,128)(2,1)S(1)} collective-permute-done((bf16[512,1024]{1,0:T(8,128)(2,1)S(1)}, bf16[512,1024]{1,0:T(8,128)(2,1)S(1)}, u32[]{:S(2)}, u32[]{:S(2)}) %collective-permute-start.14) | collective-permute-done | bytes 1048608 | tf_op jit(solution)/shard_map/ppermute | solution.py:531
  47.4 5.7 %experts.3.refs_6_ = bf16[1,512,1024]{2,1,0:T(8,128)(2,1)} custom-call(bf16[1,4096,1024]{2,1,0:T(8,128)(2,1)S(1)} %bitcast.4, bf16[1,4096,1024]{2,1,0:T(8,128)(2,1)S(1)} %bitcast.6, bf16[128,1024]{1,0:T(8,128)(2,1)S(1)} %get-tuple-element.28.refs_5_.refs_2_, ...), custom_call_target="tpu_custom_call", output_to_operand_aliasing={{}: (8, {})} | custom-call | flops 4294967296 | bytes 20975616 | tf_op jit(solution)/shard_map/experts/pallas_call | solution.py:126
  53.1 3.1 %back.1 = bf16[256,1024]{1,0:T(8,128)(2,1)} custom-call(f32[1,1024]{1,0:T(1,128)} %bitcast.7, f32[256,1024]{1,0:T(8,128)S(1)} %get-tuple-element.22.refs_5_.refs_1_, f32[256,1024]{1,0:T(8,128)S(1)} %get-tuple-element.23.refs_2_, f32[256,256]{1,0:T(8,128)S(1)} %get-tuple-element.20.refs_2_.refs_3_, f32[128,512]{1,0:T(8,128)S(1)} %get-tuple-element.32.refs_4_, ...), custom_call_target="tpu_custom_call" | custom-call | flops 1000000000 | bytes 3297280 | tf_op jit(solution)/shard_map/back/pallas_call | solution.py:126
  (18 shorter events, 0.0 us)
Async XLA Ops:
  0.6 7.3 %collective-permute-start.1 = (bf16[64,1024]{1,0:T(8,128)(2,1)}, bf16[64,1024]{1,0:T(8,128)(2,1)S(1)}, u32[]{:S(2)}, u32[]{:S(2)}) collective-permute-start(bf16[64,1024]{1,0:T(8,128)(2,1)} %refs_0_.6), channel_id=1, source_target_pairs={{0,8},{4,12},{8,0},{12,4},{16,24},{20,28},{24,16},{28,20},{1,9},{5... | collective-permute-start | bytes 393224 | tf_op jit(solution)/shard_map/ppermute | solution.py:531
  4.5 9.7 %collective-permute-start = (bf16[16,1280]{1,0:T(8,128)(2,1)S(1)}, bf16[16,1280]{1,0:T(8,128)(2,1)S(1)}, u32[]{:S(2)}, u32[]{:S(2)}) collective-permute-start(bf16[16,1280]{1,0:T(8,128)(2,1)S(1)} %ends.1), channel_id=1, source_target_pairs={{0,4},{4,8},{8,12},{12,16},{16,20},{20,24},{24,28},{1,5},{5,9},{9,... | collective-permute-start | bytes 122888 | tf_op jit(solution)/shard_map/ppermute | solution.py:668
  8.9 10.7 %collective-permute-start.5 = (bf16[128,1024]{1,0:T(8,128)(2,1)S(1)}, bf16[128,1024]{1,0:T(8,128)(2,1)S(1)}, u32[]{:S(2)}, u32[]{:S(2)}) collective-permute-start(bf16[128,1024]{1,0:T(8,128)(2,1)S(1)} %join.1.refs_8_.refs_2_), channel_id=1, source_target_pairs={{0,4},{4,0},{8,12},{12,8},{16,20},{20,16},{24,28},{28,24},{1,5},{5... | collective-permute-start | bytes 786440 | tf_op jit(solution)/shard_map/ppermute | solution.py:531
  10.1 14.4 %collective-permute-start.4 = (bf16[128,1024]{1,0:T(8,128)(2,1)S(1)}, bf16[128,1024]{1,0:T(8,128)(2,1)S(1)}, u32[]{:S(2)}, u32[]{:S(2)}) collective-permute-start(bf16[128,1024]{1,0:T(8,128)(2,1)S(1)} %join.1.refs_8_.refs_2_), channel_id=1, source_target_pairs={{0,2},{1,3},{2,0},{3,1},{4,6},{5,7},{6,4},{7,5},{8,10},{9,11},{10,... | collective-permute-start | bytes 786440 | tf_op jit(solution)/shard_map/ppermute | solution.py:531
  11.6 13.1 %collective-permute-start.3 = (bf16[128,1024]{1,0:T(8,128)(2,1)S(1)}, bf16[128,1024]{1,0:T(8,128)(2,1)S(1)}, u32[]{:S(2)}, u32[]{:S(2)}) collective-permute-start(bf16[128,1024]{1,0:T(8,128)(2,1)S(1)} %join.1.refs_8_.refs_2_), channel_id=1, source_target_pairs={{0,16},{4,20},{8,24},{12,28},{16,0},{20,4},{24,8},{28,12},{1,17},{... | collective-permute-start | bytes 786440 | tf_op jit(solution)/shard_map/ppermute | solution.py:531
  14.2 22.4 %slice-start = ((s8[8388608]{0:T(1024)(128)(4,1)}), s8[4194304]{0:T(1024)(128)(4,1)S(1)}, s32[]{:S(2)}) async-start(s8[8388608]{0:T(1024)(128)(4,1)} %bitcast.3), calls=%async_computation | async-start | bytes 8388608
  14.2 22.4 %slice-start.2 = ((s8[8388608]{0:T(1024)(128)(4,1)}), s8[4194304]{0:T(1024)(128)(4,1)S(1)}, s32[]{:S(2)}) async-start(s8[8388608]{0:T(1024)(128)(4,1)} %bitcast.5), calls=%async_computation.2 | async-start | bytes 8388608
  18.6 5.9 %collective-permute-start.2 = (s16[144,512]{1,0:T(8,128)(2,1)S(1)}, s16[144,512]{1,0:T(8,128)(2,1)S(1)}, u32[]{:S(2)}, u32[]{:S(2)}) collective-permute-start(s16[144,512]{1,0:T(8,128)(2,1)S(1)} %get-tuple-element.25), channel_id=1, source_target_pairs={{0,4},{4,0},{8,12},{12,8},{16,20},{20,16},{24,28},{28,24},{1,5},{5... | collective-permute-start | bytes 442376 | tf_op jit(solution)/shard_map/ppermute | solution.py:531
  19.6 6.4 %collective-permute-start.6 = (bf16[128,1024]{1,0:T(8,128)(2,1)S(1)}, bf16[128,1024]{1,0:T(8,128)(2,1)S(1)}, u32[]{:S(2)}, u32[]{:S(2)}) collective-permute-start(bf16[128,1024]{1,0:T(8,128)(2,1)S(1)} %collective-permute-done.5.refs_3_), channel_id=1, source_target_pairs={{0,2},{1,3},{2,0},{3,1},{4,6},{5,7},{6,4},{7,5},{8,10},{9,11},{10,... | collective-permute-start | bytes 786440 | tf_op jit(solution)/shard_map/ppermute | solution.py:531
  20.1 16.6 %slice-start.1 = ((s8[8388608]{0:T(1024)(128)(4,1)}), s8[4194304]{0:T(1024)(128)(4,1)S(1)}, s32[]{:S(2)}) async-start(s8[8388608]{0:T(1024)(128)(4,1)} %bitcast.3), calls=%async_computation.1 | async-start | bytes 8388608
  20.1 16.6 %slice-start.3 = ((s8[8388608]{0:T(1024)(128)(4,1)}), s8[4194304]{0:T(1024)(128)(4,1)S(1)}, s32[]{:S(2)}) async-start(s8[8388608]{0:T(1024)(128)(4,1)} %bitcast.5), calls=%async_computation.3 | async-start | bytes 8388608
  26.1 6.9 %collective-permute-start.8 = (bf16[128,1024]{1,0:T(8,128)(2,1)S(1)}, bf16[128,1024]{1,0:T(8,128)(2,1)S(1)}, u32[]{:S(2)}, u32[]{:S(2)}) collective-permute-start(bf16[128,1024]{1,0:T(8,128)(2,1)S(1)} %get-tuple-element.28.refs_5_.refs_2_), channel_id=1, source_target_pairs={{0,4},{4,0},{8,12},{12,8},{16,20},{20,16},{24,28},{28,24},{1,5},{5... | collective-permute-start | bytes 786440 | tf_op jit(solution)/shard_map/ppermute | solution.py:531
  27.3 6.4 %collective-permute-start.9 = (bf16[128,1024]{1,0:T(8,128)(2,1)S(1)}, bf16[128,1024]{1,0:T(8,128)(2,1)S(1)}, u32[]{:S(2)}, u32[]{:S(2)}) collective-permute-start(bf16[128,1024]{1,0:T(8,128)(2,1)S(1)} %get-tuple-element.28.refs_5_.refs_2_), channel_id=1, source_target_pairs={{0,2},{1,3},{2,0},{3,1},{4,6},{5,7},{6,4},{7,5},{8,10},{9,11},{10,... | collective-permute-start | bytes 786440 | tf_op jit(solution)/shard_map/ppermute | solution.py:531
  27.8 5.1 %collective-permute-start.7 = (s16[144,512]{1,0:T(8,128)(2,1)S(1)}, s16[144,512]{1,0:T(8,128)(2,1)S(1)}, u32[]{:S(2)}, u32[]{:S(2)}) collective-permute-start(s16[144,512]{1,0:T(8,128)(2,1)S(1)} %get-tuple-element.27), channel_id=1, source_target_pairs={{0,8},{4,12},{8,0},{12,4},{16,24},{20,28},{24,16},{28,20},{1,9},{5... | collective-permute-start | bytes 442376 | tf_op jit(solution)/shard_map/ppermute | solution.py:531
  33.9 2.7 %collective-permute-start.12 = (bf16[512,1024]{1,0:T(8,128)(2,1)S(1)}, bf16[512,1024]{1,0:T(8,128)(2,1)S(1)}, u32[]{:S(2)}, u32[]{:S(2)}) collective-permute-start(bf16[512,1024]{1,0:T(8,128)(2,1)S(1)} %get-tuple-element.30), channel_id=1, source_target_pairs={{0,1},{1,0},{2,3},{3,2},{4,5},{5,4},{6,7},{7,6},{8,9},{9,8},{10,11... | collective-permute-start | bytes 3145736 | tf_op jit(solution)/shard_map/ppermute | solution.py:531
  34.0 10.3 %collective-permute-start.10 = (s16[144,512]{1,0:T(8,128)(2,1)S(1)}, s16[144,512]{1,0:T(8,128)(2,1)S(1)}, u32[]{:S(2)}, u32[]{:S(2)}) collective-permute-start(s16[144,512]{1,0:T(8,128)(2,1)S(1)} %get-tuple-element.29), channel_id=1, source_target_pairs={{0,16},{4,20},{8,24},{12,28},{16,0},{20,4},{24,8},{28,12},{1,17},{... | collective-permute-start | bytes 442376 | tf_op jit(solution)/shard_map/ppermute | solution.py:531
  34.4 9.9 %collective-permute-start.11 = (bf16[128,1024]{1,0:T(8,128)(2,1)S(1)}, bf16[128,1024]{1,0:T(8,128)(2,1)S(1)}, u32[]{:S(2)}, u32[]{:S(2)}) collective-permute-start(bf16[128,1024]{1,0:T(8,128)(2,1)S(1)} %collective-permute-done.9.refs_7_.refs_4_), channel_id=1, source_target_pairs={{0,4},{4,0},{8,12},{12,8},{16,20},{20,16},{24,28},{28,24},{1,5},{5... | collective-permute-start | bytes 786440 | tf_op jit(solution)/shard_map/ppermute | solution.py:531
  44.7 2.7 %collective-permute-start.14 = (bf16[512,1024]{1,0:T(8,128)(2,1)S(1)}, bf16[512,1024]{1,0:T(8,128)(2,1)S(1)}, u32[]{:S(2)}, u32[]{:S(2)}) collective-permute-start(bf16[512,1024]{1,0:T(8,128)(2,1)S(1)} %get-tuple-element.34), channel_id=1, source_target_pairs={{0,1},{1,0},{2,3},{3,2},{4,5},{5,4},{6,7},{7,6},{8,9},{9,8},{10,11... | collective-permute-start | bytes 3145736 | tf_op jit(solution)/shard_map/ppermute | solution.py:531
  44.8 8.3 %collective-permute-start.13 = (s16[144,512]{1,0:T(8,128)(2,1)S(1)}, s16[144,512]{1,0:T(8,128)(2,1)S(1)}, u32[]{:S(2)}, u32[]{:S(2)}) collective-permute-start(s16[144,512]{1,0:T(8,128)(2,1)S(1)} %get-tuple-element.33), channel_id=1, source_target_pairs={{0,4},{4,0},{8,12},{12,8},{16,20},{20,16},{24,28},{28,24},{1,5},{5... | collective-permute-start | bytes 442376 | tf_op jit(solution)/shard_map/ppermute | solution.py:531

commit v14 on v13

--- a/solution.py
+++ b/solution.py
@@ -294,8 +294,11 @@
     return here % 2, (here // 2) % 2, here // 4
 
 
-def pair_body(width, own_ref, got_ref, rows_ref, pair_ref, sent_ref, same_rows_ref):
+def pair_body(
+    width, own_ref, got_ref, rows_ref, a, b, c, d, pair_ref, sent_ref, same_rows_ref, joined_ref
+):
     same_rows_ref[...] = rows_ref[...]
+    join_rows((a, b, c, d), joined_ref)
     x, _, _ = place()
     pair = together(x == 0, taken(own_ref), received(got_ref), width)
     put(pair_ref, *pair)
@@ -317,8 +320,7 @@
         joined_ref[i * rows : (i + 1) * rows] = piece[...]
 
 
-def four_body(width, pair_ref, got_ref, a, b, c, d, sent_ref, ids_ref, joined_ref):
-    join_rows((a, b, c, d), joined_ref)
+def four_body(width, pair_ref, got_ref, sent_ref, ids_ref):
     _, z, _ = place()
     four = together(z == 0, taken(pair_ref), received(got_ref), 2 * width)
     send(sent_ref, *four)
@@ -366,24 +368,21 @@
             state = parts_ref[i, STATE : STATE + 1] * state + parts_ref[i, :STATE]
 
 
-def back_body(paired, gain_far, pre_far, decay_far, bc_far, *rest):
-    starts, (out_far, *rest) = rest[: 1 + paired], rest[1 + paired :]
-    far = (gain_far, pre_far, decay_far, bc_far)
-    gain_ref, pre_ref, decay_ref, bc_ref, out_ref, sems = rest
-    copies = started(far, rest[:4], sems)
+def back_body(turn, gain_far, pre_far, decay_far, bc_far, start_ref, *rest):
+    rest = rest[1:] if turn == 1 else rest
+    out_far, gain_ref, pre_ref, decay_ref, bc_ref, out_ref, sems = rest
     channels = pre_ref.shape[1]
+    half = pl.ds(0, channels)
+    if turn is not None:
+        side = (lax.axis_index("ctx") + turn) % 2
+        half = pl.ds(pl.multiple_of(side * channels, channels), channels)
+    far = (gain_far.at[:, half], pre_far.at[:, half], decay_far.at[:, half], bc_far)
+    copies = started(far, (gain_ref, pre_ref, decay_ref, bc_ref), sems)
     width = min(channels, 4 * HDIM)
     group = (iota((width, width), 0) // HDIM == iota((width, width), 1) // HDIM).astype(BF16)
-    if paired:
-        side = lax.axis_index("ctx") % 2
-        mine, other = starts[0][...], received(starts[1])[0]
-        start = [jnp.where(side == 0, mine, other), jnp.where(side == 0, other, mine)]
-        start = jnp.concatenate(start, axis=1)
-    else:
-        start = starts[0][...]
+    start = received(start_ref)[0] if turn == 1 else start_ref[...]
     finished(copies)
     c_high, c_low = halves(bc_ref[:, STATE:])
-    copies = []
     for i in range(channels // width):
         cut = slice(i * width, (i + 1) * width)
         s_high, s_low = halves(start[:, cut])
@@ -391,8 +390,7 @@
         pre = pre_ref[:, cut] + carried * decay_ref[:, cut]
         mean = dot_left(pre * pre, group) * (1.0 / HDIM)
         out_ref[:, cut] = (pre * lax.rsqrt(mean + 1e-05) * gain_ref[:, cut]).astype(BF16)
-        copies += started([out_ref.at[:, cut]], [out_far.at[:, cut]], sems, i)
-    finished(copies)
+    finished(started([out_ref], [out_far.at[:, half]], sems))
 
 
 def entering_by_pairs(keep, sent, width, pre, near_pieces, far_rows, meanwhile):
@@ -400,26 +398,27 @@
     ids_array = array((8, width), F32)
     joined_array = array((4 * far_rows.shape[0], far_rows.shape[1]), BF16)
     got = swapped(sent, "ctx", 1)
-    pair, sent, rows = call(
+    pair, sent, rows, joined = call(
         functools.partial(pair_body, width),
-        [pair_array, sent_array, array(far_rows.shape, BF16)],
-        (keep, got, far_rows),
+        [pair_array, sent_array, array(far_rows.shape, BF16), joined_array],
+        (keep, got, far_rows, *near_pieces),
         near=True,
-        after=(*near_pieces[2:], pre),
+        after=(pre,),
         name="pair",
     )
     far_pieces = spread_rows(rows, 1)
+    beside = swapped(joined, "exp", 1)
     pair_got = swapped(sent, "ctx", 2)
-    sent, ids, joined = call(
+    sent, ids = call(
         functools.partial(four_body, width),
-        [sent_array, ids_array, joined_array],
-        (pair, pair_got, *near_pieces),
+        [sent_array, ids_array],
+        (pair, pair_got),
         near=True,
-        after=far_pieces[1:3],
+        after=(*far_pieces[1:3], beside),
         name="four",
     )
     four_got = swapped(sent, "ctx", 4)
-    done = meanwhile(ids, joined)
+    done = meanwhile(ids, beside)
     mine, sent, ids, joined = call(
         functools.partial(turn_body, width),
         [array((STATE, keep.shape[1]), F32), sent_array, ids_array, joined_array],
@@ -428,6 +427,7 @@
         after_far=(done,),
         name="turn",
     )
+    joined = swapped(joined, "exp", 1)
     return (mine, swapped(sent, "ctx", 1)), far_pieces, ids, joined, done
 
 
@@ -497,18 +497,23 @@
     else:
         starts = (entering_by_rows(ends[0]),)
 
-    def finish(after=()):
+    def finish(turn=None, so_far=None, after=()):
         args = (gain.reshape(1, channels), pre, decay, bc)
-        outs = [array((tokens, channels), BF16)]
+        parts = 1 if turn is None else 2
+        shapes = [a.shape[:-1] + (a.shape[-1] // parts,) for a in args[:3]]
+        inside = [array(shape, F32) for shape in shapes] + [bc, array(shapes[1], BF16)]
+        start = starts[turn or 0]
+        last = (so_far,) if turn == 1 else ()
         return call(
-            functools.partial(back_body, paired),
-            outs,
-            (*args, *starts),
+            functools.partial(back_body, turn),
+            [pltpu.HBM((tokens, channels), BF16)],
+            (*args, start, *last),
             fixed=1,
-            near_args=len(starts),
+            spaces_of=[pltpu.HBM] + [pl.ANY] * 3 + [pltpu.VMEM] + [pltpu.HBM] * len(last),
+            aliases={len(args) + 1: 0} if last else None,
             after_far=after,
-            scratch=room(args) + room(outs),
-            sems=max(4, channels // (4 * HDIM)),
+            scratch=room(inside),
+            sems=len(args),
             flops=10**9,
             grant=16,
             name="back",
@@ -596,11 +601,11 @@
     return (z, x, y, d)
 
 
-def experts_by_tokens(part, pieces, joined, ids, w_gate, w_up, so_far):
+def experts_by_tokens(part, pieces, joined, ids, w_gate, w_up, so_far, after=()):
     rows = pieces[0].shape[0] // 2
     length = 4 * rows
     hidden = w_gate.shape[2]
-    args = (w_gate, w_up, *pieces, swapped(joined, "exp", 1), ids)
+    args = (w_gate, w_up, *pieces, joined, ids)
     return call(
         functools.partial(expert_body, part),
         [pltpu.HBM((1, 2 * length, hidden), BF16)],
@@ -608,6 +613,7 @@
         held=2,
         near_args=0,
         aliases={len(args): 0} if part else None,
+        after_far=after,
         scratch=[
             pltpu.VMEM((length // rows, rows, rows), BF16),
             pltpu.VMEM((length, TILE), BF16),
@@ -690,8 +696,9 @@
     )
     if by_tokens:
         far_pieces, ids, joined, hidden = late
-        hidden = experts_by_tokens(1, far_pieces, joined, ids, w_gate, w_up, hidden)
-        mixed = finish((hidden,))
+        mixed = finish(0)
+        hidden = experts_by_tokens(1, far_pieces, joined, ids, w_gate, w_up, hidden, (mixed,))
+        mixed = finish(1, mixed, (hidden,))
     else:
         mixed = finish()
         hidden = experts_by_slots(moe_input, expert_ids, w_gate, w_up)

time: 56.7 us -> 57.9 us (1.021)
  Pallas kernels: 25.8 us -> 27.2 us
    pallas_call x10 -> x11, Pallas kernels: 25.8 us -> 27.2 us  [call(): pl.pallas_call(body, out_shape=outs, in_specs=[pl.BlockSpec(memory_space=...]
  transfers between devices with their start and end apart: 15 -> 15, of which waited for: 7 -> 5; matrix products, arithmetic and copies ran while one was open for 0% -> 0% of each run, Pallas kernels for 39% -> 42%
where the time goes in v14:
time: 57.9 us; the launch traced here: 57.6 us
  Pallas kernels  27.2 us (47%)
  starting transfers between devices  19.6 us (34%)
  waiting for transfers between devices  9.84 us (17%)
  between operations  0.96 us (2%)
    pallas_call x11, Pallas kernels, call(): pl.pallas_call(body, out_shape=outs, in_specs=[pl.BlockSpec(memory_space=...  27.2 us
    ppermute x14, starting transfers between devices, swapped(): lax.ppermute(block, axis, [(i, i ^ bit) for i in range(lax.axis_size(axis...  16.2 us
    ppermute x14, waiting for transfers between devices, swapped(): lax.ppermute(block, axis, [(i, i ^ bit) for i in range(lax.axis_size(axis...  9.84 us
    ppermute x1, starting transfers between devices, on_device(): before = lax.ppermute(ends, 'ctx', [(i, i + 1) for i in range(ctx - 1)])  3.4 us
  transfers between devices with their start and end apart: 15, of which 5 were waited for; matrix products, arithmetic and copies ran while one was open for 0% of the time, Pallas kernels for 42%

profile of v14, /device:TPU:0, one launch (start us, length us, event | category | flops | bytes accessed | tf_op | source)
XLA Modules:
  0.0 57.6 jit_solution(6477553529815671385)
XLA Ops:
  0.6 3.1 %collective-permute-start.1 = (bf16[64,1024]{1,0:T(8,128)(2,1)}, bf16[64,1024]{1,0:T(8,128)(2,1)S(1)}, u32[]{:S(2)}, u32[]{:S(2)}) collective-permute-start(bf16[64,1024]{1,0:T(8,128)(2,1)} %refs_0_.6), channel_id=1, source_target_pairs={{0,8},{4,12},{8,0},{12,4},{16,24},{20,28},{24,16},{28,20},{1,9},{5... | collective-permute-start | bytes 393224 | tf_op jit(solution)/shard_map/ppermute | solution.py:536
  3.7 0.8 %ends.1 = bf16[16,1280]{1,0:T(8,128)(2,1)S(1)} custom-call(bf16[256,1024]{1,0:T(8,128)(2,1)} %refs_0_.7, bf16[256,128]{1,0:T(8,128)(2,1)} %refs_1_.5, bf16[256,128]{1,0:T(8,128)(2,1)} %refs_2_.3), custom_call_target="tpu_custom_call" | custom-call | bytes 696320 | tf_op jit(solution)/shard_map/ends/pallas_call | solution.py:126
  4.5 3.4 %collective-permute-start = (bf16[16,1280]{1,0:T(8,128)(2,1)S(1)}, bf16[16,1280]{1,0:T(8,128)(2,1)S(1)}, u32[]{:S(2)}, u32[]{:S(2)}) collective-permute-start(bf16[16,1280]{1,0:T(8,128)(2,1)S(1)} %ends.1), channel_id=1, source_target_pairs={{0,4},{4,8},{8,12},{12,16},{16,20},{20,24},{24,28},{1,5},{5,9},{9,... | collective-permute-start | bytes 122888 | tf_op jit(solution)/shard_map/ppermute | solution.py:674
  7.9 0.0 collective-permute-done.1.refs_1_
  7.9 0.9 %join.1.refs_8_.refs_3_.refs_2_ = bf16[128,1024]{1,0:T(8,128)(2,1)S(1)} custom-call(bf16[64,1024]{1,0:T(8,128)(2,1)} %refs_0_.6, bf16[64,1024]{1,0:T(8,128)(2,1)S(1)} %collective-permute-done.1.refs_1_), custom_call_target="tpu_custom_call" | custom-call | bytes 524288 | tf_op jit(solution)/shard_map/join/pallas_call | solution.py:126
  8.9 1.2 %collective-permute-start.4 = (bf16[128,1024]{1,0:T(8,128)(2,1)S(1)}, bf16[128,1024]{1,0:T(8,128)(2,1)S(1)}, u32[]{:S(2)}, u32[]{:S(2)}) collective-permute-start(bf16[128,1024]{1,0:T(8,128)(2,1)S(1)} %join.1.refs_8_.refs_3_.refs_2_), channel_id=1, source_target_pairs={{0,4},{4,0},{8,12},{12,8},{16,20},{20,16},{24,28},{28,24},{1,5},{5... | collective-permute-start | bytes 786440 | tf_op jit(solution)/shard_map/ppermute | solution.py:536
  10.1 1.5 %collective-permute-start.5 = (bf16[128,1024]{1,0:T(8,128)(2,1)S(1)}, bf16[128,1024]{1,0:T(8,128)(2,1)S(1)}, u32[]{:S(2)}, u32[]{:S(2)}) collective-permute-start(bf16[128,1024]{1,0:T(8,128)(2,1)S(1)} %join.1.refs_8_.refs_3_.refs_2_), channel_id=1, source_target_pairs={{0,2},{1,3},{2,0},{3,1},{4,6},{5,7},{6,4},{7,5},{8,10},{9,11},{10,... | collective-permute-start | bytes 786440 | tf_op jit(solution)/shard_map/ppermute | solution.py:536
  11.6 2.6 %collective-permute-start.3 = (bf16[128,1024]{1,0:T(8,128)(2,1)S(1)}, bf16[128,1024]{1,0:T(8,128)(2,1)S(1)}, u32[]{:S(2)}, u32[]{:S(2)}) collective-permute-start(bf16[128,1024]{1,0:T(8,128)(2,1)S(1)} %join.1.refs_8_.refs_3_.refs_2_), channel_id=1, source_target_pairs={{0,16},{4,20},{8,24},{12,28},{16,0},{20,4},{24,8},{28,12},{1,17},{... | collective-permute-start | bytes 786440 | tf_op jit(solution)/shard_map/ppermute | solution.py:536
  14.2 4.4 %front.1 = (f32[256,1024]{1,0:T(8,128)S(1)}, f32[256,256]{1,0:T(8,128)S(1)}, f32[2,16,256]{2,1,0:T(8,128)S(1)}, f32[136,512]{1,0:T(8,128)S(1)}, s16[144,512]{1,0:T(8,128)(2,1)S(1)}) custom-call(bf16[256,1024]{1,0:T(8,128)(2,1)} %refs_0_.7, bf16[256,128]{1,0:T(8,128)(2,1)} %refs_1_.5, bf16[256,128]{1,0:T(8,128)(2,1)} %refs_2_.3, f32[4,1024]{1,0:T(4,128)} %refs_3_.1, ...), custom_call_target="tpu_custom_call" | custom-call | flops 5000000000 | bytes 2503168 | tf_op jit(solution)/shard_map/front/pallas_call | solution.py:126
  18.6 0.9 %collective-permute-start.2 = (s16[144,512]{1,0:T(8,128)(2,1)S(1)}, s16[144,512]{1,0:T(8,128)(2,1)S(1)}, u32[]{:S(2)}, u32[]{:S(2)}) collective-permute-start(s16[144,512]{1,0:T(8,128)(2,1)S(1)} %get-tuple-element.25), channel_id=1, source_target_pairs={{0,4},{4,0},{8,12},{12,8},{16,20},{20,16},{24,28},{28,24},{1,5},{5... | collective-permute-start | bytes 442376 | tf_op jit(solution)/shard_map/ppermute | solution.py:536
  19.6 0.5 collective-permute-start.6
  20.1 4.2 %inner.1 = (f32[256,1024]{1,0:T(8,128)S(1)}, f32[256,1024]{1,0:T(8,128)S(1)}) custom-call(f32[1,16]{1,0:T(1,128)} %bitcast.10, f32[256,1024]{1,0:T(8,128)S(1)} %get-tuple-element.19.refs_1_, f32[256,256]{1,0:T(8,128)S(1)} %get-tuple-element.20.refs_2_.refs_3_, f32[2,16,256]{2,1,0:T(8,128)S(1)} %get-tuple-element.21.refs_3_), custom_call_target="tpu_custom_call" | custom-call | flops 4000000000 | bytes 3440704 | tf_op jit(solution)/shard_map/inner/pallas_call | solution.py:126
  24.3 0.4 collective-permute-done.3.refs_2_
  24.7 1.2 %collective-permute-done.6.refs_6_.refs_5_ = bf16[128,1024]{1,0:T(8,128)(2,1)S(1)} collective-permute-done((bf16[128,1024]{1,0:T(8,128)(2,1)S(1)}, bf16[128,1024]{1,0:T(8,128)(2,1)S(1)}, u32[]{:S(2)}, u32[]{:S(2)}) %collective-permute-start.6) | collective-permute-done | bytes 262176 | tf_op jit(solution)/shard_map/ppermute | solution.py:536
  26.0 0.2 pair.1
  26.2 0.1 collective-permute-start.10
  26.3 0.6 collective-permute-start.9
  26.8 1.1 %collective-permute-start.8 = (bf16[128,1024]{1,0:T(8,128)(2,1)S(1)}, bf16[128,1024]{1,0:T(8,128)(2,1)S(1)}, u32[]{:S(2)}, u32[]{:S(2)}) collective-permute-start(bf16[128,1024]{1,0:T(8,128)(2,1)S(1)} %get-tuple-element.28.refs_5_.refs_2_), channel_id=1, source_target_pairs={{0,4},{4,0},{8,12},{12,8},{16,20},{20,16},{24,28},{28,24},{1,5},{5... | collective-permute-start | bytes 786440 | tf_op jit(solution)/shard_map/ppermute | solution.py:536
  28.0 1.7 %collective-permute-start.7 = (s16[144,512]{1,0:T(8,128)(2,1)S(1)}, s16[144,512]{1,0:T(8,128)(2,1)S(1)}, u32[]{:S(2)}, u32[]{:S(2)}) collective-permute-start(s16[144,512]{1,0:T(8,128)(2,1)S(1)} %get-tuple-element.27), channel_id=1, source_target_pairs={{0,8},{4,12},{8,0},{12,4},{16,24},{20,28},{24,16},{28,20},{1,9},{5... | collective-permute-start | bytes 442376 | tf_op jit(solution)/shard_map/ppermute | solution.py:536
  29.7 5.3 %collective-permute-done.9.refs_3_.refs_7_.refs_4_ = bf16[128,1024]{1,0:T(8,128)(2,1)S(1)} collective-permute-done((bf16[128,1024]{1,0:T(8,128)(2,1)S(1)}, bf16[128,1024]{1,0:T(8,128)(2,1)S(1)}, u32[]{:S(2)}, u32[]{:S(2)}) %collective-permute-start.9) | collective-permute-done | bytes 262176 | tf_op jit(solution)/shard_map/ppermute | solution.py:536
  35.0 1.1 %collective-permute-start.12 = (bf16[128,1024]{1,0:T(8,128)(2,1)S(1)}, bf16[128,1024]{1,0:T(8,128)(2,1)S(1)}, u32[]{:S(2)}, u32[]{:S(2)}) collective-permute-start(bf16[128,1024]{1,0:T(8,128)(2,1)S(1)} %collective-permute-done.9.refs_3_.refs_7_.refs_4_), channel_id=1, source_target_pairs={{0,4},{4,0},{8,12},{12,8},{16,20},{20,16},{24,28},{28,24},{1,5},{5... | collective-permute-start | bytes 786440 | tf_op jit(solution)/shard_map/ppermute | solution.py:536
  36.1 0.1 four.1
  36.3 0.6 %collective-permute-start.11 = (s16[144,512]{1,0:T(8,128)(2,1)S(1)}, s16[144,512]{1,0:T(8,128)(2,1)S(1)}, u32[]{:S(2)}, u32[]{:S(2)}) collective-permute-start(s16[144,512]{1,0:T(8,128)(2,1)S(1)} %get-tuple-element.30), channel_id=1, source_target_pairs={{0,16},{4,20},{8,24},{12,28},{16,0},{20,4},{24,8},{28,12},{1,17},{... | collective-permute-start | bytes 442376 | tf_op jit(solution)/shard_map/ppermute | solution.py:536
  37.0 5.7 %experts.2.refs_9_.refs_8_ = bf16[1,512,1024]{2,1,0:T(8,128)(2,1)} custom-call(bf16[1,4096,1024]{2,1,0:T(8,128)(2,1)S(1)} %bitcast.4, bf16[1,4096,1024]{2,1,0:T(8,128)(2,1)S(1)} %bitcast.6, bf16[128,1024]{1,0:T(8,128)(2,1)S(1)} %join.1.refs_8_.refs_3_.refs_2_, bf16[128,1024]{1,0:T(8,128)(2,1)S(1)} %collective-permute-done.4.refs_4_.refs_3_, ...), custom_call_target="tpu_custom_call" | custom-call | flops 4294967296 | bytes 19927040 | tf_op jit(solution)/shard_map/experts/pallas_call | solution.py:126
  42.6 0.2 collective-permute-done.12.refs_8_.refs_5_
  42.8 2.7 %collective-permute-done.11.refs_4_ = s16[144,512]{1,0:T(8,128)(2,1)S(1)} collective-permute-done((s16[144,512]{1,0:T(8,128)(2,1)S(1)}, s16[144,512]{1,0:T(8,128)(2,1)S(1)}, u32[]{:S(2)}, u32[]{:S(2)}) %collective-permute-start.11) | collective-permute-done | bytes 147488 | tf_op jit(solution)/shard_map/ppermute | solution.py:536
  45.5 0.4 turn.1
  45.9 0.1 collective-permute-start.14
  46.0 0.9 %collective-permute-start.13 = (s16[144,512]{1,0:T(8,128)(2,1)S(1)}, s16[144,512]{1,0:T(8,128)(2,1)S(1)}, u32[]{:S(2)}, u32[]{:S(2)}) collective-permute-start(s16[144,512]{1,0:T(8,128)(2,1)S(1)} %get-tuple-element.32), channel_id=1, source_target_pairs={{0,4},{4,0},{8,12},{12,8},{16,20},{20,16},{24,28},{28,24},{1,5},{5... | collective-permute-start | bytes 442376 | tf_op jit(solution)/shard_map/ppermute | solution.py:536
  47.0 2.4 %back.2.refs_9_.refs_5_ = bf16[256,1024]{1,0:T(8,128)(2,1)} custom-call(f32[1,1024]{1,0:T(1,128)} %bitcast.7, f32[256,1024]{1,0:T(8,128)S(1)} %get-tuple-element.22.refs_7_.refs_1_, f32[256,1024]{1,0:T(8,128)S(1)} %get-tuple-element.23.refs_2_, f32[256,256]{1,0:T(8,128)S(1)} %get-tuple-element.20.refs_2_.refs_3_, f32[128,512]{1,0:T(8,128)S(1)} %get-tuple-element.33.refs_4_), custom_call_target="tpu_custom_call" | custom-call | flops 1000000000 | bytes 3149824 | tf_op jit(solution)/shard_map/back/pallas_call | solution.py:126
  49.3 5.7 %experts.3.refs_6_ = bf16[1,512,1024]{2,1,0:T(8,128)(2,1)} custom-call(bf16[1,4096,1024]{2,1,0:T(8,128)(2,1)S(1)} %bitcast.4, bf16[1,4096,1024]{2,1,0:T(8,128)(2,1)S(1)} %bitcast.6, bf16[128,1024]{1,0:T(8,128)(2,1)S(1)} %get-tuple-element.28.refs_5_.refs_2_, ...), custom_call_target="tpu_custom_call", output_to_operand_aliasing={{}: (8, {})} | custom-call | flops 4294967296 | bytes 20975616 | tf_op jit(solution)/shard_map/experts/pallas_call | solution.py:126
  55.0 2.4 %back.3 = bf16[256,1024]{1,0:T(8,128)(2,1)} custom-call(f32[1,1024]{1,0:T(1,128)} %bitcast.8, f32[256,1024]{1,0:T(8,128)S(1)} %get-tuple-element.22.refs_7_.refs_1_, f32[256,1024]{1,0:T(8,128)S(1)} %get-tuple-element.23.refs_2_, f32[256,256]{1,0:T(8,128)S(1)} %get-tuple-element.20.refs_2_.refs_3_, ...), custom_call_target="tpu_custom_call", output_to_operand_aliasing={{}: (5, {})} | custom-call | flops 1000000000 | bytes 3559424 | tf_op jit(solution)/shard_map/back/pallas_call | solution.py:126
  (19 shorter events, 0.0 us)
Async XLA Ops:
  0.6 7.3 %collective-permute-start.1 = (bf16[64,1024]{1,0:T(8,128)(2,1)}, bf16[64,1024]{1,0:T(8,128)(2,1)S(1)}, u32[]{:S(2)}, u32[]{:S(2)}) collective-permute-start(bf16[64,1024]{1,0:T(8,128)(2,1)} %refs_0_.6), channel_id=1, source_target_pairs={{0,8},{4,12},{8,0},{12,4},{16,24},{20,28},{24,16},{28,20},{1,9},{5... | collective-permute-start | bytes 393224 | tf_op jit(solution)/shard_map/ppermute | solution.py:536
  4.5 9.7 %collective-permute-start = (bf16[16,1280]{1,0:T(8,128)(2,1)S(1)}, bf16[16,1280]{1,0:T(8,128)(2,1)S(1)}, u32[]{:S(2)}, u32[]{:S(2)}) collective-permute-start(bf16[16,1280]{1,0:T(8,128)(2,1)S(1)} %ends.1), channel_id=1, source_target_pairs={{0,4},{4,8},{8,12},{12,16},{16,20},{20,24},{24,28},{1,5},{5,9},{9,... | collective-permute-start | bytes 122888 | tf_op jit(solution)/shard_map/ppermute | solution.py:674
  8.9 10.7 %collective-permute-start.4 = (bf16[128,1024]{1,0:T(8,128)(2,1)S(1)}, bf16[128,1024]{1,0:T(8,128)(2,1)S(1)}, u32[]{:S(2)}, u32[]{:S(2)}) collective-permute-start(bf16[128,1024]{1,0:T(8,128)(2,1)S(1)} %join.1.refs_8_.refs_3_.refs_2_), channel_id=1, source_target_pairs={{0,4},{4,0},{8,12},{12,8},{16,20},{20,16},{24,28},{28,24},{1,5},{5... | collective-permute-start | bytes 786440 | tf_op jit(solution)/shard_map/ppermute | solution.py:536
  10.1 14.3 %collective-permute-start.5 = (bf16[128,1024]{1,0:T(8,128)(2,1)S(1)}, bf16[128,1024]{1,0:T(8,128)(2,1)S(1)}, u32[]{:S(2)}, u32[]{:S(2)}) collective-permute-start(bf16[128,1024]{1,0:T(8,128)(2,1)S(1)} %join.1.refs_8_.refs_3_.refs_2_), channel_id=1, source_target_pairs={{0,2},{1,3},{2,0},{3,1},{4,6},{5,7},{6,4},{7,5},{8,10},{9,11},{10,... | collective-permute-start | bytes 786440 | tf_op jit(solution)/shard_map/ppermute | solution.py:536
  11.6 13.1 %collective-permute-start.3 = (bf16[128,1024]{1,0:T(8,128)(2,1)S(1)}, bf16[128,1024]{1,0:T(8,128)(2,1)S(1)}, u32[]{:S(2)}, u32[]{:S(2)}) collective-permute-start(bf16[128,1024]{1,0:T(8,128)(2,1)S(1)} %join.1.refs_8_.refs_3_.refs_2_), channel_id=1, source_target_pairs={{0,16},{4,20},{8,24},{12,28},{16,0},{20,4},{24,8},{28,12},{1,17},{... | collective-permute-start | bytes 786440 | tf_op jit(solution)/shard_map/ppermute | solution.py:536
  14.2 22.7 %slice-start.2 = ((s8[8388608]{0:T(1024)(128)(4,1)}), s8[4194304]{0:T(1024)(128)(4,1)S(1)}, s32[]{:S(2)}) async-start(s8[8388608]{0:T(1024)(128)(4,1)} %bitcast.5), calls=%async_computation.2 | async-start | bytes 8388608
  18.6 5.7 %collective-permute-start.2 = (s16[144,512]{1,0:T(8,128)(2,1)S(1)}, s16[144,512]{1,0:T(8,128)(2,1)S(1)}, u32[]{:S(2)}, u32[]{:S(2)}) collective-permute-start(s16[144,512]{1,0:T(8,128)(2,1)S(1)} %get-tuple-element.25), channel_id=1, source_target_pairs={{0,4},{4,0},{8,12},{12,8},{16,20},{20,16},{24,28},{28,24},{1,5},{5... | collective-permute-start | bytes 442376 | tf_op jit(solution)/shard_map/ppermute | solution.py:536
  19.6 6.4 %collective-permute-start.6 = (bf16[128,1024]{1,0:T(8,128)(2,1)S(1)}, bf16[128,1024]{1,0:T(8,128)(2,1)S(1)}, u32[]{:S(2)}, u32[]{:S(2)}) collective-permute-start(bf16[128,1024]{1,0:T(8,128)(2,1)S(1)} %collective-permute-done.4.refs_4_.refs_3_), channel_id=1, source_target_pairs={{0,2},{1,3},{2,0},{3,1},{4,6},{5,7},{6,4},{7,5},{8,10},{9,11},{10,... | collective-permute-start | bytes 786440 | tf_op jit(solution)/shard_map/ppermute | solution.py:536
  20.1 16.8 %slice-start = ((s8[8388608]{0:T(1024)(128)(4,1)}), s8[4194304]{0:T(1024)(128)(4,1)S(1)}, s32[]{:S(2)}) async-start(s8[8388608]{0:T(1024)(128)(4,1)} %bitcast.3), calls=%async_computation | async-start | bytes 8388608
  20.1 16.8 %slice-start.1 = ((s8[8388608]{0:T(1024)(128)(4,1)}), s8[4194304]{0:T(1024)(128)(4,1)S(1)}, s32[]{:S(2)}) async-start(s8[8388608]{0:T(1024)(128)(4,1)} %bitcast.3), calls=%async_computation.1 | async-start | bytes 8388608
  20.1 16.8 %slice-start.3 = ((s8[8388608]{0:T(1024)(128)(4,1)}), s8[4194304]{0:T(1024)(128)(4,1)S(1)}, s32[]{:S(2)}) async-start(s8[8388608]{0:T(1024)(128)(4,1)} %bitcast.5), calls=%async_computation.3 | async-start | bytes 8388608
  26.2 10.0 %collective-permute-start.10 = (bf16[512,1024]{1,0:T(8,128)(2,1)S(1)}, bf16[512,1024]{1,0:T(8,128)(2,1)S(1)}, u32[]{:S(2)}, u32[]{:S(2)}) collective-permute-start(bf16[512,1024]{1,0:T(8,128)(2,1)S(1)} %get-tuple-element.29), channel_id=1, source_target_pairs={{0,1},{1,0},{2,3},{3,2},{4,5},{5,4},{6,7},{7,6},{8,9},{9,8},{10,11... | collective-permute-start | bytes 3145736 | tf_op jit(solution)/shard_map/ppermute | solution.py:536
  26.3 8.7 %collective-permute-start.9 = (bf16[128,1024]{1,0:T(8,128)(2,1)S(1)}, bf16[128,1024]{1,0:T(8,128)(2,1)S(1)}, u32[]{:S(2)}, u32[]{:S(2)}) collective-permute-start(bf16[128,1024]{1,0:T(8,128)(2,1)S(1)} %get-tuple-element.28.refs_5_.refs_2_), channel_id=1, source_target_pairs={{0,2},{1,3},{2,0},{3,1},{4,6},{5,7},{6,4},{7,5},{8,10},{9,11},{10,... | collective-permute-start | bytes 786440 | tf_op jit(solution)/shard_map/ppermute | solution.py:536
  26.8 9.3 %collective-permute-start.8 = (bf16[128,1024]{1,0:T(8,128)(2,1)S(1)}, bf16[128,1024]{1,0:T(8,128)(2,1)S(1)}, u32[]{:S(2)}, u32[]{:S(2)}) collective-permute-start(bf16[128,1024]{1,0:T(8,128)(2,1)S(1)} %get-tuple-element.28.refs_5_.refs_2_), channel_id=1, source_target_pairs={{0,4},{4,0},{8,12},{12,8},{16,20},{20,16},{24,28},{28,24},{1,5},{5... | collective-permute-start | bytes 786440 | tf_op jit(solution)/shard_map/ppermute | solution.py:536
  28.0 8.2 %collective-permute-start.7 = (s16[144,512]{1,0:T(8,128)(2,1)S(1)}, s16[144,512]{1,0:T(8,128)(2,1)S(1)}, u32[]{:S(2)}, u32[]{:S(2)}) collective-permute-start(s16[144,512]{1,0:T(8,128)(2,1)S(1)} %get-tuple-element.27), channel_id=1, source_target_pairs={{0,8},{4,12},{8,0},{12,4},{16,24},{20,28},{24,16},{28,20},{1,9},{5... | collective-permute-start | bytes 442376 | tf_op jit(solution)/shard_map/ppermute | solution.py:536
  35.0 7.9 %collective-permute-start.12 = (bf16[128,1024]{1,0:T(8,128)(2,1)S(1)}, bf16[128,1024]{1,0:T(8,128)(2,1)S(1)}, u32[]{:S(2)}, u32[]{:S(2)}) collective-permute-start(bf16[128,1024]{1,0:T(8,128)(2,1)S(1)} %collective-permute-done.9.refs_3_.refs_7_.refs_4_), channel_id=1, source_target_pairs={{0,4},{4,0},{8,12},{12,8},{16,20},{20,16},{24,28},{28,24},{1,5},{5... | collective-permute-start | bytes 786440 | tf_op jit(solution)/shard_map/ppermute | solution.py:536
  36.3 9.3 %collective-permute-start.11 = (s16[144,512]{1,0:T(8,128)(2,1)S(1)}, s16[144,512]{1,0:T(8,128)(2,1)S(1)}, u32[]{:S(2)}, u32[]{:S(2)}) collective-permute-start(s16[144,512]{1,0:T(8,128)(2,1)S(1)} %get-tuple-element.30), channel_id=1, source_target_pairs={{0,16},{4,20},{8,24},{12,28},{16,0},{20,4},{24,8},{28,12},{1,17},{... | collective-permute-start | bytes 442376 | tf_op jit(solution)/shard_map/ppermute | solution.py:536
  45.9 3.4 %collective-permute-start.14 = (bf16[512,1024]{1,0:T(8,128)(2,1)S(1)}, bf16[512,1024]{1,0:T(8,128)(2,1)S(1)}, u32[]{:S(2)}, u32[]{:S(2)}) collective-permute-start(bf16[512,1024]{1,0:T(8,128)(2,1)S(1)} %get-tuple-element.34), channel_id=1, source_target_pairs={{0,1},{1,0},{2,3},{3,2},{4,5},{5,4},{6,7},{7,6},{8,9},{9,8},{10,11... | collective-permute-start | bytes 3145736 | tf_op jit(solution)/shard_map/ppermute | solution.py:536
  46.0 9.0 %collective-permute-start.13 = (s16[144,512]{1,0:T(8,128)(2,1)S(1)}, s16[144,512]{1,0:T(8,128)(2,1)S(1)}, u32[]{:S(2)}, u32[]{:S(2)}) collective-permute-start(s16[144,512]{1,0:T(8,128)(2,1)S(1)} %get-tuple-element.32), channel_id=1, source_target_pairs={{0,4},{4,0},{8,12},{12,8},{16,20},{20,16},{24,28},{28,24},{1,5},{5... | collective-permute-start | bytes 442376 | tf_op jit(solution)/shard_map/ppermute | solution.py:536

commit v15 on v13

--- a/solution.py
+++ b/solution.py
@@ -161,13 +161,11 @@
 
 
 def front_body(paired, count, *refs):
-    far, outs, rest = refs[:count], refs[count : count + 3], refs[count + 3 :]
-    ends = rest[: 1 + paired]
-    rest = rest[1 + paired :]
-    near, scratch, pad_ref, sems = rest[:count], rest[count : count + 3], rest[-2], rest[-1]
+    far, (xconv_ref, bc_ref, lines_ref), rest = refs[:count], refs[count : count + 3], refs[count + 3 :]
+    ends, rest = rest[: 1 + paired], rest[1 + paired :]
+    near, pad_ref, sems = rest[:count], rest[-2], rest[-1]
     copies = started(far, near, sems)
     x_ref, b_ref, c_ref, taps_ref, taps_bc_ref, logs_ref, ids_ref, ends_ref = near
-    xconv_ref, bc_ref, lines_ref = scratch
     tokens, channels = x_ref.shape
     heads = logs_ref.shape[0]
     finished(copies)
@@ -192,7 +190,6 @@
     row = dot_exact(logs, upper_ones(tokens))
     lines_ref[0] = row
     lines_ref[1] = inflow
-    copies = started(scratch, outs, sems)
     total = row[:, tokens - 1 :]
     spread = head_spread(heads)
     fresh = xconv * dot_left(inflow * jnp.exp(total - row), spread, FIRST)
@@ -215,25 +212,33 @@
     else:
         ends[0][:STATE] = state
         ends[0][STATE:] = dot_exact(jnp.exp(total), spread, FIRST)
-    finished(copies)
-
-
-def inner_body(skip_far, xconv_far, bc_far, lines_far, pre_far, decay_far, *rest):
-    far = (skip_far, xconv_far, bc_far, lines_far)
-    skip_ref, xconv_ref, bc_ref, lines_ref, pre_ref, decay_ref, sems = rest
-    finished(started(far, rest[:4], sems))
+
+
+def inner_body(
+    skip_far,
+    gain_far,
+    xconv_ref,
+    bc_ref,
+    lines_ref,
+    pre_ref,
+    decay_ref,
+    gain_ref,
+    skip_ref,
+    sems,
+):
+    copies = started([skip_far, gain_far], [skip_ref, gain_ref], sems)
     tokens, channels = xconv_ref.shape
     heads = channels // HDIM
     row = lines_ref[0]
     column = row.T
     spread = head_spread(heads)
     decay_ref[...] = dot_left(jnp.exp(row), spread, FIRST)
-    copies = started([decay_ref], [decay_far], sems)
     inflow = dot_left(lines_ref[1], spread, FIRST)
-    skip = dot_exact(skip_ref[...], spread)
     meet = dot(bc_ref[:, STATE:], bc_ref[:, :STATE], ((1,), (1,)))
     lower = iota((tokens, tokens), 0) >= iota((tokens, tokens), 1)
     left = iota((tokens, 2 * HDIM), 1) < HDIM
+    finished(copies)
+    skip = dot_exact(skip_ref[...], spread)
     for pair in range(heads // 2):
         cut = slice(pair * 2 * HDIM, (pair + 1) * 2 * HDIM)
         xconv = xconv_ref[:, cut]
@@ -245,7 +250,6 @@
             m_high, m_low = halves(mix)
             both.append(dot16(m_high, d_high) + dot16(m_high, d_low) + dot16(m_low, d_high))
         pre_ref[:, cut] = skip[:, cut] * xconv + jnp.where(left, both[0], both[1])
-    finished(copies + started([pre_ref], [pre_far], sems, 1))
 
 
 def put(ref, state, logsum, line):
@@ -366,11 +370,8 @@
             state = parts_ref[i, STATE : STATE + 1] * state + parts_ref[i, :STATE]
 
 
-def back_body(paired, gain_far, pre_far, decay_far, bc_far, *rest):
-    starts, (out_far, *rest) = rest[: 1 + paired], rest[1 + paired :]
-    far = (gain_far, pre_far, decay_far, bc_far)
-    gain_ref, pre_ref, decay_ref, bc_ref, out_ref, sems = rest
-    copies = started(far, rest[:4], sems)
+def back_body(paired, gain_ref, pre_ref, decay_ref, bc_ref, *rest):
+    starts, (out_far, out_ref, sems) = rest[: 1 + paired], rest[1 + paired :]
     channels = pre_ref.shape[1]
     width = min(channels, 4 * HDIM)
     group = (iota((width, width), 0) // HDIM == iota((width, width), 1) // HDIM).astype(BF16)
@@ -381,7 +382,6 @@
         start = jnp.concatenate(start, axis=1)
     else:
         start = starts[0][...]
-    finished(copies)
     c_high, c_low = halves(bc_ref[:, STATE:])
     copies = []
     for i in range(channels // width):
@@ -470,23 +470,24 @@
         outs + ends,
         args,
         fixed=len(args) - 1,
-        near_outs=len(ends),
+        near_outs=len(outs + ends),
         after=rows[0][:1] if paired else (),
-        scratch=room(args) + room(outs) + [pltpu.VMEM((8 + tokens, channels + 2 * STATE), F32)],
+        scratch=room(args) + [pltpu.VMEM((8 + tokens, channels + 2 * STATE), F32)],
         sems=len(args),
         flops=5 * 10**9,
         grant=20,
         name="front",
     )
-    args = (skip.reshape(1, heads), xconv, bc, lines)
-    outs = [array((tokens, channels), F32)] * 2
-    pre, decay = call(
+    args = (skip.reshape(1, heads), gain.reshape(1, channels), xconv, bc, lines)
+    pre, decay, gain = call(
         inner_body,
-        outs,
+        [array((tokens, channels), F32)] * 2 + [array((1, channels), F32)],
         args,
-        fixed=1,
-        scratch=room(args) + room(outs),
-        sems=4,
+        fixed=2,
+        near_args=3,
+        near_outs=3,
+        scratch=room(args[:1]),
+        sems=2,
         flops=4 * 10**9,
         grant=16,
         name="inner",
@@ -498,17 +499,16 @@
         starts = (entering_by_rows(ends[0]),)
 
     def finish(after=()):
-        args = (gain.reshape(1, channels), pre, decay, bc)
         outs = [array((tokens, channels), BF16)]
+        args = (gain, pre, decay, bc, *starts)
         return call(
             functools.partial(back_body, paired),
             outs,
-            (*args, *starts),
-            fixed=1,
-            near_args=len(starts),
+            args,
+            near_args=len(args),
             after_far=after,
-            scratch=room(args) + room(outs),
-            sems=max(4, channels // (4 * HDIM)),
+            scratch=room(outs),
+            sems=max(1, channels // (4 * HDIM)),
             flops=10**9,
             grant=16,
             name="back",

time: 56.7 us -> 55.6 us (0.981)
  Pallas kernels: 25.8 us -> 24.2 us
  starting transfers between devices: 19.5 us -> 20.1 us
    pallas_call x10, Pallas kernels: 25.8 us -> 24.2 us  [call(): pl.pallas_call(body, out_shape=outs, in_specs=[pl.BlockSpec(memory_space=...]
    ppermute x14, starting transfers between devices: 16.1 us -> 16.7 us  [swapped(): lax.ppermute(block, axis, [(i, i ^ bit) for i in range(lax.axis_size(axis...]
  transfers between devices with their start and end apart: 15 -> 15, of which waited for: 7 -> 7; matrix products, arithmetic and copies ran while one was open for 0% -> 0% of each run, Pallas kernels for 39% -> 38%
where the time goes in v15:
time: 55.6 us; the launch traced here: 55.4 us
  Pallas kernels  24.2 us (44%)
  starting transfers between devices  20.1 us (36%)
  waiting for transfers between devices  10.2 us (18%)
  between operations  0.95 us (2%)
    pallas_call x10, Pallas kernels, call(): pl.pallas_call(body, out_shape=outs, in_specs=[pl.BlockSpec(memory_space=...  24.2 us
    ppermute x14, starting transfers between devices, swapped(): lax.ppermute(block, axis, [(i, i ^ bit) for i in range(lax.axis_size(axis...  16.7 us
    ppermute x14, waiting for transfers between devices, swapped(): lax.ppermute(block, axis, [(i, i ^ bit) for i in range(lax.axis_size(axis...  10.1 us
    ppermute x1, starting transfers between devices, on_device(): before = lax.ppermute(ends, 'ctx', [(i, i + 1) for i in range(ctx - 1)])  3.4 us
  transfers between devices with their start and end apart: 15, of which 7 were waited for; matrix products, arithmetic and copies ran while one was open for 0% of the time, Pallas kernels for 38%

profile of v15, /device:TPU:0, one launch (start us, length us, event | category | flops | bytes accessed | tf_op | source)
XLA Modules:
  0.0 55.4 jit_solution(7890816440256571177)
XLA Ops:
  0.6 3.1 %collective-permute-start.1 = (bf16[64,1024]{1,0:T(8,128)(2,1)}, bf16[64,1024]{1,0:T(8,128)(2,1)S(1)}, u32[]{:S(2)}, u32[]{:S(2)}) collective-permute-start(bf16[64,1024]{1,0:T(8,128)(2,1)} %refs_0_.6), channel_id=1, source_target_pairs={{0,8},{4,12},{8,0},{12,4},{16,24},{20,28},{24,16},{28,20},{1,9},{5... | collective-permute-start | bytes 393224 | tf_op jit(solution)/shard_map/ppermute | solution.py:531
  3.7 0.8 %ends.1 = bf16[16,1280]{1,0:T(8,128)(2,1)S(1)} custom-call(bf16[256,1024]{1,0:T(8,128)(2,1)} %refs_0_.7, bf16[256,128]{1,0:T(8,128)(2,1)} %refs_1_.5, bf16[256,128]{1,0:T(8,128)(2,1)} %refs_2_.3), custom_call_target="tpu_custom_call" | custom-call | bytes 696320 | tf_op jit(solution)/shard_map/ends/pallas_call | solution.py:126
  4.5 3.4 %collective-permute-start = (bf16[16,1280]{1,0:T(8,128)(2,1)S(1)}, bf16[16,1280]{1,0:T(8,128)(2,1)S(1)}, u32[]{:S(2)}, u32[]{:S(2)}) collective-permute-start(bf16[16,1280]{1,0:T(8,128)(2,1)S(1)} %ends.1), channel_id=1, source_target_pairs={{0,4},{4,8},{8,12},{12,16},{16,20},{20,24},{24,28},{1,5},{5,9},{9,... | collective-permute-start | bytes 122888 | tf_op jit(solution)/shard_map/ppermute | solution.py:668
  7.9 0.9 %join.1.refs_8_.refs_2_ = bf16[128,1024]{1,0:T(8,128)(2,1)S(1)} custom-call(bf16[64,1024]{1,0:T(8,128)(2,1)} %refs_0_.6, bf16[64,1024]{1,0:T(8,128)(2,1)S(1)} %collective-permute-done.1.refs_1_), custom_call_target="tpu_custom_call" | custom-call | bytes 524288 | tf_op jit(solution)/shard_map/join/pallas_call | solution.py:126
  8.9 1.2 %collective-permute-start.5 = (bf16[128,1024]{1,0:T(8,128)(2,1)S(1)}, bf16[128,1024]{1,0:T(8,128)(2,1)S(1)}, u32[]{:S(2)}, u32[]{:S(2)}) collective-permute-start(bf16[128,1024]{1,0:T(8,128)(2,1)S(1)} %join.1.refs_8_.refs_2_), channel_id=1, source_target_pairs={{0,4},{4,0},{8,12},{12,8},{16,20},{20,16},{24,28},{28,24},{1,5},{5... | collective-permute-start | bytes 786440 | tf_op jit(solution)/shard_map/ppermute | solution.py:531
  10.1 1.5 %collective-permute-start.4 = (bf16[128,1024]{1,0:T(8,128)(2,1)S(1)}, bf16[128,1024]{1,0:T(8,128)(2,1)S(1)}, u32[]{:S(2)}, u32[]{:S(2)}) collective-permute-start(bf16[128,1024]{1,0:T(8,128)(2,1)S(1)} %join.1.refs_8_.refs_2_), channel_id=1, source_target_pairs={{0,2},{1,3},{2,0},{3,1},{4,6},{5,7},{6,4},{7,5},{8,10},{9,11},{10,... | collective-permute-start | bytes 786440 | tf_op jit(solution)/shard_map/ppermute | solution.py:531
  11.6 2.6 %collective-permute-start.3 = (bf16[128,1024]{1,0:T(8,128)(2,1)S(1)}, bf16[128,1024]{1,0:T(8,128)(2,1)S(1)}, u32[]{:S(2)}, u32[]{:S(2)}) collective-permute-start(bf16[128,1024]{1,0:T(8,128)(2,1)S(1)} %join.1.refs_8_.refs_2_), channel_id=1, source_target_pairs={{0,16},{4,20},{8,24},{12,28},{16,0},{20,4},{24,8},{28,12},{1,17},{... | collective-permute-start | bytes 786440 | tf_op jit(solution)/shard_map/ppermute | solution.py:531
  14.2 3.7 %front.1 = (f32[256,1024]{1,0:T(8,128)S(1)}, f32[256,256]{1,0:T(8,128)S(1)}, f32[2,16,256]{2,1,0:T(8,128)S(1)}, f32[136,512]{1,0:T(8,128)S(1)}, s16[144,512]{1,0:T(8,128)(2,1)S(1)}) custom-call(bf16[256,1024]{1,0:T(8,128)(2,1)} %refs_0_.7, bf16[256,128]{1,0:T(8,128)(2,1)} %refs_1_.5, bf16[256,128]{1,0:T(8,128)(2,1)} %refs_2_.3, f32[4,1024]{1,0:T(4,128)} %refs_3_.1, ...), custom_call_target="tpu_custom_call" | custom-call | flops 5000000000 | bytes 2503168 | tf_op jit(solution)/shard_map/front/pallas_call | solution.py:126
  17.9 0.9 %collective-permute-start.2 = (s16[144,512]{1,0:T(8,128)(2,1)S(1)}, s16[144,512]{1,0:T(8,128)(2,1)S(1)}, u32[]{:S(2)}, u32[]{:S(2)}) collective-permute-start(s16[144,512]{1,0:T(8,128)(2,1)S(1)} %get-tuple-element.27), channel_id=1, source_target_pairs={{0,4},{4,0},{8,12},{12,8},{16,20},{20,16},{24,28},{28,24},{1,5},{5... | collective-permute-start | bytes 442376 | tf_op jit(solution)/shard_map/ppermute | solution.py:531
  18.9 0.5 collective-permute-start.6
  19.4 4.0 %inner.1 = (f32[256,1024]{1,0:T(8,128)S(1)}, f32[256,1024]{1,0:T(8,128)S(1)}, f32[1,1024]{1,0:T(1,128)S(1)}) custom-call(f32[1,16]{1,0:T(1,128)} %bitcast.9, f32[1,1024]{1,0:T(1,128)} %bitcast.7, f32[256,1024]{1,0:T(8,128)S(1)} %get-tuple-element.20.refs_2_, f32[256,256]{1,0:T(8,128)S(1)} %get-tuple-element.21.refs_3_, ...), custom_call_target="tpu_custom_call" | custom-call | flops 4000000000 | bytes 3448896 | tf_op jit(solution)/shard_map/inner/pallas_call | solution.py:126
  23.4 1.3 %collective-permute-done.3.refs_2_ = bf16[128,1024]{1,0:T(8,128)(2,1)S(1)} collective-permute-done((bf16[128,1024]{1,0:T(8,128)(2,1)S(1)}, bf16[128,1024]{1,0:T(8,128)(2,1)S(1)}, u32[]{:S(2)}, u32[]{:S(2)}) %collective-permute-start.3) | collective-permute-done | bytes 262176 | tf_op jit(solution)/shard_map/ppermute | solution.py:531
  24.7 0.5 collective-permute-done.6.refs_4_.refs_5_
  25.2 0.2 pair.1
  25.4 1.2 %collective-permute-start.8 = (bf16[128,1024]{1,0:T(8,128)(2,1)S(1)}, bf16[128,1024]{1,0:T(8,128)(2,1)S(1)}, u32[]{:S(2)}, u32[]{:S(2)}) collective-permute-start(bf16[128,1024]{1,0:T(8,128)(2,1)S(1)} %get-tuple-element.30.refs_5_.refs_2_), channel_id=1, source_target_pairs={{0,4},{4,0},{8,12},{12,8},{16,20},{20,16},{24,28},{28,24},{1,5},{5... | collective-permute-start | bytes 786440 | tf_op jit(solution)/shard_map/ppermute | solution.py:531
  26.6 0.5 collective-permute-start.9
  27.1 1.7 %collective-permute-start.7 = (s16[144,512]{1,0:T(8,128)(2,1)S(1)}, s16[144,512]{1,0:T(8,128)(2,1)S(1)}, u32[]{:S(2)}, u32[]{:S(2)}) collective-permute-start(s16[144,512]{1,0:T(8,128)(2,1)S(1)} %get-tuple-element.29), channel_id=1, source_target_pairs={{0,8},{4,12},{8,0},{12,4},{16,24},{20,28},{24,16},{28,20},{1,9},{5... | collective-permute-start | bytes 442376 | tf_op jit(solution)/shard_map/ppermute | solution.py:531
  28.8 3.4 %collective-permute-done.7.refs_1_.refs_3_ = s16[144,512]{1,0:T(8,128)(2,1)S(1)} collective-permute-done((s16[144,512]{1,0:T(8,128)(2,1)S(1)}, s16[144,512]{1,0:T(8,128)(2,1)S(1)}, u32[]{:S(2)}, u32[]{:S(2)}) %collective-permute-start.7) | collective-permute-done | bytes 147488 | tf_op jit(solution)/shard_map/ppermute | solution.py:531
  32.3 0.9 %collective-permute-done.9.refs_7_.refs_4_ = bf16[128,1024]{1,0:T(8,128)(2,1)S(1)} collective-permute-done((bf16[128,1024]{1,0:T(8,128)(2,1)S(1)}, bf16[128,1024]{1,0:T(8,128)(2,1)S(1)}, u32[]{:S(2)}, u32[]{:S(2)}) %collective-permute-start.9) | collective-permute-done | bytes 262176 | tf_op jit(solution)/shard_map/ppermute | solution.py:531
  33.1 0.2 four.1
  33.3 0.1 collective-permute-start.12
  33.4 1.1 %collective-permute-start.10 = (s16[144,512]{1,0:T(8,128)(2,1)S(1)}, s16[144,512]{1,0:T(8,128)(2,1)S(1)}, u32[]{:S(2)}, u32[]{:S(2)}) collective-permute-start(s16[144,512]{1,0:T(8,128)(2,1)S(1)} %get-tuple-element.31), channel_id=1, source_target_pairs={{0,16},{4,20},{8,24},{12,28},{16,0},{20,4},{24,8},{28,12},{1,17},{... | collective-permute-start | bytes 442376 | tf_op jit(solution)/shard_map/ppermute | solution.py:531
  34.5 1.4 %collective-permute-start.11 = (bf16[128,1024]{1,0:T(8,128)(2,1)S(1)}, bf16[128,1024]{1,0:T(8,128)(2,1)S(1)}, u32[]{:S(2)}, u32[]{:S(2)}) collective-permute-start(bf16[128,1024]{1,0:T(8,128)(2,1)S(1)} %collective-permute-done.9.refs_7_.refs_4_), channel_id=1, source_target_pairs={{0,4},{4,0},{8,12},{12,8},{16,20},{20,16},{24,28},{28,24},{1,5},{5... | collective-permute-start | bytes 786440 | tf_op jit(solution)/shard_map/ppermute | solution.py:531
  35.9 0.2 collective-permute-done.12.refs_6_
  36.1 5.7 %experts.2.refs_9_.refs_8_ = bf16[1,512,1024]{2,1,0:T(8,128)(2,1)} custom-call(bf16[1,4096,1024]{2,1,0:T(8,128)(2,1)S(1)} %bitcast.4, bf16[1,4096,1024]{2,1,0:T(8,128)(2,1)S(1)} %bitcast.6, bf16[128,1024]{1,0:T(8,128)(2,1)S(1)} %join.1.refs_8_.refs_2_, bf16[128,1024]{1,0:T(8,128)(2,1)S(1)} %collective-permute-done.5.refs_3_, ...), custom_call_target="tpu_custom_call" | custom-call | flops 4294967296 | bytes 19927040 | tf_op jit(solution)/shard_map/experts/pallas_call | solution.py:126
  41.8 1.9 %collective-permute-done.10.refs_4_ = s16[144,512]{1,0:T(8,128)(2,1)S(1)} collective-permute-done((s16[144,512]{1,0:T(8,128)(2,1)S(1)}, s16[144,512]{1,0:T(8,128)(2,1)S(1)}, u32[]{:S(2)}, u32[]{:S(2)}) %collective-permute-start.10) | collective-permute-done | bytes 147488 | tf_op jit(solution)/shard_map/ppermute | solution.py:531
  43.7 0.4 turn.1
  44.1 0.1 collective-permute-start.14
  44.2 0.8 %collective-permute-start.13 = (s16[144,512]{1,0:T(8,128)(2,1)S(1)}, s16[144,512]{1,0:T(8,128)(2,1)S(1)}, u32[]{:S(2)}, u32[]{:S(2)}) collective-permute-start(s16[144,512]{1,0:T(8,128)(2,1)S(1)} %get-tuple-element.35), channel_id=1, source_target_pairs={{0,4},{4,0},{8,12},{12,8},{16,20},{20,16},{24,28},{28,24},{1,5},{5... | collective-permute-start | bytes 442376 | tf_op jit(solution)/shard_map/ppermute | solution.py:531
  45.0 1.9 %collective-permute-done.14.refs_6_ = bf16[512,1024]{1,0:T(8,128)(2,1)S(1)} collective-permute-done((bf16[512,1024]{1,0:T(8,128)(2,1)S(1)}, bf16[512,1024]{1,0:T(8,128)(2,1)S(1)}, u32[]{:S(2)}, u32[]{:S(2)}) %collective-permute-start.14) | collective-permute-done | bytes 1048608 | tf_op jit(solution)/shard_map/ppermute | solution.py:531
  46.9 5.9 %experts.3.refs_6_ = bf16[1,512,1024]{2,1,0:T(8,128)(2,1)} custom-call(bf16[1,4096,1024]{2,1,0:T(8,128)(2,1)S(1)} %bitcast.4, bf16[1,4096,1024]{2,1,0:T(8,128)(2,1)S(1)} %bitcast.6, bf16[128,1024]{1,0:T(8,128)(2,1)S(1)} %get-tuple-element.30.refs_5_.refs_2_, ...), custom_call_target="tpu_custom_call", output_to_operand_aliasing={{}: (8, {})} | custom-call | flops 4294967296 | bytes 20975616 | tf_op jit(solution)/shard_map/experts/pallas_call | solution.py:126
  52.8 2.5 %back.1 = bf16[256,1024]{1,0:T(8,128)(2,1)} custom-call(f32[1,1024]{1,0:T(1,128)S(1)} %get-tuple-element.23.refs_0_, f32[256,1024]{1,0:T(8,128)S(1)} %get-tuple-element.24.refs_5_.refs_1_, f32[256,1024]{1,0:T(8,128)S(1)} %get-tuple-element.25.refs_2_, f32[256,256]{1,0:T(8,128)S(1)} %get-tuple-element.21.refs_3_, f32[128,512]{1,0:T(8,128)S(1)} %get-tuple-element.34.refs_4_, ...), custom_call_target="tpu_custom_call" | custom-call | flops 1000000000 | bytes 3297280 | tf_op jit(solution)/shard_map/back/pallas_call | solution.py:126
  (18 shorter events, 0.0 us)
Async XLA Ops:
  0.6 7.3 %collective-permute-start.1 = (bf16[64,1024]{1,0:T(8,128)(2,1)}, bf16[64,1024]{1,0:T(8,128)(2,1)S(1)}, u32[]{:S(2)}, u32[]{:S(2)}) collective-permute-start(bf16[64,1024]{1,0:T(8,128)(2,1)} %refs_0_.6), channel_id=1, source_target_pairs={{0,8},{4,12},{8,0},{12,4},{16,24},{20,28},{24,16},{28,20},{1,9},{5... | collective-permute-start | bytes 393224 | tf_op jit(solution)/shard_map/ppermute | solution.py:531
  4.5 9.7 %collective-permute-start = (bf16[16,1280]{1,0:T(8,128)(2,1)S(1)}, bf16[16,1280]{1,0:T(8,128)(2,1)S(1)}, u32[]{:S(2)}, u32[]{:S(2)}) collective-permute-start(bf16[16,1280]{1,0:T(8,128)(2,1)S(1)} %ends.1), channel_id=1, source_target_pairs={{0,4},{4,8},{8,12},{12,16},{16,20},{20,24},{24,28},{1,5},{5,9},{9,... | collective-permute-start | bytes 122888 | tf_op jit(solution)/shard_map/ppermute | solution.py:668
  8.9 10.0 %collective-permute-start.5 = (bf16[128,1024]{1,0:T(8,128)(2,1)S(1)}, bf16[128,1024]{1,0:T(8,128)(2,1)S(1)}, u32[]{:S(2)}, u32[]{:S(2)}) collective-permute-start(bf16[128,1024]{1,0:T(8,128)(2,1)S(1)} %join.1.refs_8_.refs_2_), channel_id=1, source_target_pairs={{0,4},{4,0},{8,12},{12,8},{16,20},{20,16},{24,28},{28,24},{1,5},{5... | collective-permute-start | bytes 786440 | tf_op jit(solution)/shard_map/ppermute | solution.py:531
  10.1 13.3 %collective-permute-start.4 = (bf16[128,1024]{1,0:T(8,128)(2,1)S(1)}, bf16[128,1024]{1,0:T(8,128)(2,1)S(1)}, u32[]{:S(2)}, u32[]{:S(2)}) collective-permute-start(bf16[128,1024]{1,0:T(8,128)(2,1)S(1)} %join.1.refs_8_.refs_2_), channel_id=1, source_target_pairs={{0,2},{1,3},{2,0},{3,1},{4,6},{5,7},{6,4},{7,5},{8,10},{9,11},{10,... | collective-permute-start | bytes 786440 | tf_op jit(solution)/shard_map/ppermute | solution.py:531
  11.6 13.1 %collective-permute-start.3 = (bf16[128,1024]{1,0:T(8,128)(2,1)S(1)}, bf16[128,1024]{1,0:T(8,128)(2,1)S(1)}, u32[]{:S(2)}, u32[]{:S(2)}) collective-permute-start(bf16[128,1024]{1,0:T(8,128)(2,1)S(1)} %join.1.refs_8_.refs_2_), channel_id=1, source_target_pairs={{0,16},{4,20},{8,24},{12,28},{16,0},{20,4},{24,8},{28,12},{1,17},{... | collective-permute-start | bytes 786440 | tf_op jit(solution)/shard_map/ppermute | solution.py:531
  14.2 21.9 %slice-start = ((s8[8388608]{0:T(1024)(128)(4,1)}), s8[4194304]{0:T(1024)(128)(4,1)S(1)}, s32[]{:S(2)}) async-start(s8[8388608]{0:T(1024)(128)(4,1)} %bitcast.3), calls=%async_computation | async-start | bytes 8388608
  14.2 21.9 %slice-start.2 = ((s8[8388608]{0:T(1024)(128)(4,1)}), s8[4194304]{0:T(1024)(128)(4,1)S(1)}, s32[]{:S(2)}) async-start(s8[8388608]{0:T(1024)(128)(4,1)} %bitcast.5), calls=%async_computation.2 | async-start | bytes 8388608
  17.9 5.5 %collective-permute-start.2 = (s16[144,512]{1,0:T(8,128)(2,1)S(1)}, s16[144,512]{1,0:T(8,128)(2,1)S(1)}, u32[]{:S(2)}, u32[]{:S(2)}) collective-permute-start(s16[144,512]{1,0:T(8,128)(2,1)S(1)} %get-tuple-element.27), channel_id=1, source_target_pairs={{0,4},{4,0},{8,12},{12,8},{16,20},{20,16},{24,28},{28,24},{1,5},{5... | collective-permute-start | bytes 442376 | tf_op jit(solution)/shard_map/ppermute | solution.py:531
  18.9 6.4 %collective-permute-start.6 = (bf16[128,1024]{1,0:T(8,128)(2,1)S(1)}, bf16[128,1024]{1,0:T(8,128)(2,1)S(1)}, u32[]{:S(2)}, u32[]{:S(2)}) collective-permute-start(bf16[128,1024]{1,0:T(8,128)(2,1)S(1)} %collective-permute-done.5.refs_3_), channel_id=1, source_target_pairs={{0,2},{1,3},{2,0},{3,1},{4,6},{5,7},{6,4},{7,5},{8,10},{9,11},{10,... | collective-permute-start | bytes 786440 | tf_op jit(solution)/shard_map/ppermute | solution.py:531
  19.4 16.7 %slice-start.1 = ((s8[8388608]{0:T(1024)(128)(4,1)}), s8[4194304]{0:T(1024)(128)(4,1)S(1)}, s32[]{:S(2)}) async-start(s8[8388608]{0:T(1024)(128)(4,1)} %bitcast.3), calls=%async_computation.1 | async-start | bytes 8388608
  19.4 16.7 %slice-start.3 = ((s8[8388608]{0:T(1024)(128)(4,1)}), s8[4194304]{0:T(1024)(128)(4,1)S(1)}, s32[]{:S(2)}) async-start(s8[8388608]{0:T(1024)(128)(4,1)} %bitcast.5), calls=%async_computation.3 | async-start | bytes 8388608
  25.4 6.9 %collective-permute-start.8 = (bf16[128,1024]{1,0:T(8,128)(2,1)S(1)}, bf16[128,1024]{1,0:T(8,128)(2,1)S(1)}, u32[]{:S(2)}, u32[]{:S(2)}) collective-permute-start(bf16[128,1024]{1,0:T(8,128)(2,1)S(1)} %get-tuple-element.30.refs_5_.refs_2_), channel_id=1, source_target_pairs={{0,4},{4,0},{8,12},{12,8},{16,20},{20,16},{24,28},{28,24},{1,5},{5... | collective-permute-start | bytes 786440 | tf_op jit(solution)/shard_map/ppermute | solution.py:531
  26.6 6.5 %collective-permute-start.9 = (bf16[128,1024]{1,0:T(8,128)(2,1)S(1)}, bf16[128,1024]{1,0:T(8,128)(2,1)S(1)}, u32[]{:S(2)}, u32[]{:S(2)}) collective-permute-start(bf16[128,1024]{1,0:T(8,128)(2,1)S(1)} %get-tuple-element.30.refs_5_.refs_2_), channel_id=1, source_target_pairs={{0,2},{1,3},{2,0},{3,1},{4,6},{5,7},{6,4},{7,5},{8,10},{9,11},{10,... | collective-permute-start | bytes 786440 | tf_op jit(solution)/shard_map/ppermute | solution.py:531
  27.1 5.1 %collective-permute-start.7 = (s16[144,512]{1,0:T(8,128)(2,1)S(1)}, s16[144,512]{1,0:T(8,128)(2,1)S(1)}, u32[]{:S(2)}, u32[]{:S(2)}) collective-permute-start(s16[144,512]{1,0:T(8,128)(2,1)S(1)} %get-tuple-element.29), channel_id=1, source_target_pairs={{0,8},{4,12},{8,0},{12,4},{16,24},{20,28},{24,16},{28,20},{1,9},{5... | collective-permute-start | bytes 442376 | tf_op jit(solution)/shard_map/ppermute | solution.py:531
  33.3 2.7 %collective-permute-start.12 = (bf16[512,1024]{1,0:T(8,128)(2,1)S(1)}, bf16[512,1024]{1,0:T(8,128)(2,1)S(1)}, u32[]{:S(2)}, u32[]{:S(2)}) collective-permute-start(bf16[512,1024]{1,0:T(8,128)(2,1)S(1)} %get-tuple-element.32), channel_id=1, source_target_pairs={{0,1},{1,0},{2,3},{3,2},{4,5},{5,4},{6,7},{7,6},{8,9},{9,8},{10,11... | collective-permute-start | bytes 3145736 | tf_op jit(solution)/shard_map/ppermute | solution.py:531
  33.4 10.3 %collective-permute-start.10 = (s16[144,512]{1,0:T(8,128)(2,1)S(1)}, s16[144,512]{1,0:T(8,128)(2,1)S(1)}, u32[]{:S(2)}, u32[]{:S(2)}) collective-permute-start(s16[144,512]{1,0:T(8,128)(2,1)S(1)} %get-tuple-element.31), channel_id=1, source_target_pairs={{0,16},{4,20},{8,24},{12,28},{16,0},{20,4},{24,8},{28,12},{1,17},{... | collective-permute-start | bytes 442376 | tf_op jit(solution)/shard_map/ppermute | solution.py:531
  34.5 9.3 %collective-permute-start.11 = (bf16[128,1024]{1,0:T(8,128)(2,1)S(1)}, bf16[128,1024]{1,0:T(8,128)(2,1)S(1)}, u32[]{:S(2)}, u32[]{:S(2)}) collective-permute-start(bf16[128,1024]{1,0:T(8,128)(2,1)S(1)} %collective-permute-done.9.refs_7_.refs_4_), channel_id=1, source_target_pairs={{0,4},{4,0},{8,12},{12,8},{16,20},{20,16},{24,28},{28,24},{1,5},{5... | collective-permute-start | bytes 786440 | tf_op jit(solution)/shard_map/ppermute | solution.py:531
  44.1 2.7 %collective-permute-start.14 = (bf16[512,1024]{1,0:T(8,128)(2,1)S(1)}, bf16[512,1024]{1,0:T(8,128)(2,1)S(1)}, u32[]{:S(2)}, u32[]{:S(2)}) collective-permute-start(bf16[512,1024]{1,0:T(8,128)(2,1)S(1)} %get-tuple-element.36), channel_id=1, source_target_pairs={{0,1},{1,0},{2,3},{3,2},{4,5},{5,4},{6,7},{7,6},{8,9},{9,8},{10,11... | collective-permute-start | bytes 3145736 | tf_op jit(solution)/shard_map/ppermute | solution.py:531
  44.2 8.5 %collective-permute-start.13 = (s16[144,512]{1,0:T(8,128)(2,1)S(1)}, s16[144,512]{1,0:T(8,128)(2,1)S(1)}, u32[]{:S(2)}, u32[]{:S(2)}) collective-permute-start(s16[144,512]{1,0:T(8,128)(2,1)S(1)} %get-tuple-element.35), channel_id=1, source_target_pairs={{0,4},{4,0},{8,12},{12,8},{16,20},{20,16},{24,28},{28,24},{1,5},{5... | collective-permute-start | bytes 442376 | tf_op jit(solution)/shard_map/ppermute | solution.py:531

commit v16 on v15

--- a/solution.py
+++ b/solution.py
@@ -298,8 +298,11 @@
     return here % 2, (here // 2) % 2, here // 4
 
 
-def pair_body(width, own_ref, got_ref, rows_ref, pair_ref, sent_ref, same_rows_ref):
+def pair_body(
+    width, own_ref, got_ref, rows_ref, a, b, c, d, pair_ref, sent_ref, same_rows_ref, joined_ref
+):
     same_rows_ref[...] = rows_ref[...]
+    join_rows((a, b, c, d), joined_ref)
     x, _, _ = place()
     pair = together(x == 0, taken(own_ref), received(got_ref), width)
     put(pair_ref, *pair)
@@ -321,8 +324,7 @@
         joined_ref[i * rows : (i + 1) * rows] = piece[...]
 
 
-def four_body(width, pair_ref, got_ref, a, b, c, d, sent_ref, ids_ref, joined_ref):
-    join_rows((a, b, c, d), joined_ref)
+def four_body(width, pair_ref, got_ref, sent_ref, ids_ref):
     _, z, _ = place()
     four = together(z == 0, taken(pair_ref), received(got_ref), 2 * width)
     send(sent_ref, *four)
@@ -400,20 +402,20 @@
     ids_array = array((8, width), F32)
     joined_array = array((4 * far_rows.shape[0], far_rows.shape[1]), BF16)
     got = swapped(sent, "ctx", 1)
-    pair, sent, rows = call(
+    pair, sent, rows, joined = call(
         functools.partial(pair_body, width),
-        [pair_array, sent_array, array(far_rows.shape, BF16)],
-        (keep, got, far_rows),
+        [pair_array, sent_array, array(far_rows.shape, BF16), joined_array],
+        (keep, got, far_rows, *near_pieces),
         near=True,
-        after=(*near_pieces[2:], pre),
+        after=(pre,),
         name="pair",
     )
     far_pieces = spread_rows(rows, 1)
     pair_got = swapped(sent, "ctx", 2)
-    sent, ids, joined = call(
+    sent, ids = call(
         functools.partial(four_body, width),
-        [sent_array, ids_array, joined_array],
-        (pair, pair_got, *near_pieces),
+        [sent_array, ids_array],
+        (pair, pair_got),
         near=True,
         after=far_pieces[1:3],
         name="four",

time: 55.6 us -> 56.3 us (1.013)
  waiting for transfers between devices: 10.2 us -> 11.1 us
    ppermute x14, waiting for transfers between devices: 10.1 us -> 11.1 us  [swapped(): lax.ppermute(block, axis, [(i, i ^ bit) for i in range(lax.axis_size(axis...]
where the time goes in v16:
time: 56.3 us; the launch traced here: 56.1 us
  Pallas kernels  24.1 us (43%)
  starting transfers between devices  19.9 us (35%)
  waiting for transfers between devices  11.1 us (20%)
  between operations  0.96 us (2%)
    pallas_call x10, Pallas kernels, call(): pl.pallas_call(body, out_shape=outs, in_specs=[pl.BlockSpec(memory_space=...  24.1 us
    ppermute x14, starting transfers between devices, swapped(): lax.ppermute(block, axis, [(i, i ^ bit) for i in range(lax.axis_size(axis...  16.5 us
    ppermute x14, waiting for transfers between devices, swapped(): lax.ppermute(block, axis, [(i, i ^ bit) for i in range(lax.axis_size(axis...  11.1 us
    ppermute x1, starting transfers between devices, on_device(): before = lax.ppermute(ends, 'ctx', [(i, i + 1) for i in range(ctx - 1)])  3.4 us
  transfers between devices with their start and end apart: 15, of which 7 were waited for; matrix products, arithmetic and copies ran while one was open for 0% of the time, Pallas kernels for 38%

profile of v16, /device:TPU:0, one launch (start us, length us, event | category | flops | bytes accessed | tf_op | source)
XLA Modules:
  0.0 56.1 jit_solution(7264383781275563244)
XLA Ops:
  0.6 3.1 %collective-permute-start.1 = (bf16[64,1024]{1,0:T(8,128)(2,1)}, bf16[64,1024]{1,0:T(8,128)(2,1)S(1)}, u32[]{:S(2)}, u32[]{:S(2)}) collective-permute-start(bf16[64,1024]{1,0:T(8,128)(2,1)} %refs_0_.6), channel_id=1, source_target_pairs={{0,8},{4,12},{8,0},{12,4},{16,24},{20,28},{24,16},{28,20},{1,9},{5... | collective-permute-start | bytes 393224 | tf_op jit(solution)/shard_map/ppermute | solution.py:533
  3.7 0.8 %ends.1 = bf16[16,1280]{1,0:T(8,128)(2,1)S(1)} custom-call(bf16[256,1024]{1,0:T(8,128)(2,1)} %refs_0_.7, bf16[256,128]{1,0:T(8,128)(2,1)} %refs_1_.5, bf16[256,128]{1,0:T(8,128)(2,1)} %refs_2_.3), custom_call_target="tpu_custom_call" | custom-call | bytes 696320 | tf_op jit(solution)/shard_map/ends/pallas_call | solution.py:126
  4.5 3.4 %collective-permute-start = (bf16[16,1280]{1,0:T(8,128)(2,1)S(1)}, bf16[16,1280]{1,0:T(8,128)(2,1)S(1)}, u32[]{:S(2)}, u32[]{:S(2)}) collective-permute-start(bf16[16,1280]{1,0:T(8,128)(2,1)S(1)} %ends.1), channel_id=1, source_target_pairs={{0,4},{4,8},{8,12},{12,16},{16,20},{20,24},{24,28},{1,5},{5,9},{9,... | collective-permute-start | bytes 122888 | tf_op jit(solution)/shard_map/ppermute | solution.py:670
  7.9 0.9 %join.1.refs_8_.refs_3_.refs_2_ = bf16[128,1024]{1,0:T(8,128)(2,1)S(1)} custom-call(bf16[64,1024]{1,0:T(8,128)(2,1)} %refs_0_.6, bf16[64,1024]{1,0:T(8,128)(2,1)S(1)} %collective-permute-done.1.refs_1_), custom_call_target="tpu_custom_call" | custom-call | bytes 524288 | tf_op jit(solution)/shard_map/join/pallas_call | solution.py:126
  8.9 1.2 %collective-permute-start.4 = (bf16[128,1024]{1,0:T(8,128)(2,1)S(1)}, bf16[128,1024]{1,0:T(8,128)(2,1)S(1)}, u32[]{:S(2)}, u32[]{:S(2)}) collective-permute-start(bf16[128,1024]{1,0:T(8,128)(2,1)S(1)} %join.1.refs_8_.refs_3_.refs_2_), channel_id=1, source_target_pairs={{0,4},{4,0},{8,12},{12,8},{16,20},{20,16},{24,28},{28,24},{1,5},{5... | collective-permute-start | bytes 786440 | tf_op jit(solution)/shard_map/ppermute | solution.py:533
  10.1 1.5 %collective-permute-start.5 = (bf16[128,1024]{1,0:T(8,128)(2,1)S(1)}, bf16[128,1024]{1,0:T(8,128)(2,1)S(1)}, u32[]{:S(2)}, u32[]{:S(2)}) collective-permute-start(bf16[128,1024]{1,0:T(8,128)(2,1)S(1)} %join.1.refs_8_.refs_3_.refs_2_), channel_id=1, source_target_pairs={{0,2},{1,3},{2,0},{3,1},{4,6},{5,7},{6,4},{7,5},{8,10},{9,11},{10,... | collective-permute-start | bytes 786440 | tf_op jit(solution)/shard_map/ppermute | solution.py:533
  11.6 2.6 %collective-permute-start.3 = (bf16[128,1024]{1,0:T(8,128)(2,1)S(1)}, bf16[128,1024]{1,0:T(8,128)(2,1)S(1)}, u32[]{:S(2)}, u32[]{:S(2)}) collective-permute-start(bf16[128,1024]{1,0:T(8,128)(2,1)S(1)} %join.1.refs_8_.refs_3_.refs_2_), channel_id=1, source_target_pairs={{0,16},{4,20},{8,24},{12,28},{16,0},{20,4},{24,8},{28,12},{1,17},{... | collective-permute-start | bytes 786440 | tf_op jit(solution)/shard_map/ppermute | solution.py:533
  14.2 3.7 %front.1 = (f32[256,1024]{1,0:T(8,128)S(1)}, f32[256,256]{1,0:T(8,128)S(1)}, f32[2,16,256]{2,1,0:T(8,128)S(1)}, f32[136,512]{1,0:T(8,128)S(1)}, s16[144,512]{1,0:T(8,128)(2,1)S(1)}) custom-call(bf16[256,1024]{1,0:T(8,128)(2,1)} %refs_0_.7, bf16[256,128]{1,0:T(8,128)(2,1)} %refs_1_.5, bf16[256,128]{1,0:T(8,128)(2,1)} %refs_2_.3, f32[4,1024]{1,0:T(4,128)} %refs_3_.1, ...), custom_call_target="tpu_custom_call" | custom-call | flops 5000000000 | bytes 2503168 | tf_op jit(solution)/shard_map/front/pallas_call | solution.py:126
  17.9 0.9 %collective-permute-start.2 = (s16[144,512]{1,0:T(8,128)(2,1)S(1)}, s16[144,512]{1,0:T(8,128)(2,1)S(1)}, u32[]{:S(2)}, u32[]{:S(2)}) collective-permute-start(s16[144,512]{1,0:T(8,128)(2,1)S(1)} %get-tuple-element.27), channel_id=1, source_target_pairs={{0,4},{4,0},{8,12},{12,8},{16,20},{20,16},{24,28},{28,24},{1,5},{5... | collective-permute-start | bytes 442376 | tf_op jit(solution)/shard_map/ppermute | solution.py:533
  18.9 0.5 collective-permute-start.6
  19.4 4.0 %inner.1 = (f32[256,1024]{1,0:T(8,128)S(1)}, f32[256,1024]{1,0:T(8,128)S(1)}, f32[1,1024]{1,0:T(1,128)S(1)}) custom-call(f32[1,16]{1,0:T(1,128)} %bitcast.9, f32[1,1024]{1,0:T(1,128)} %bitcast.7, f32[256,1024]{1,0:T(8,128)S(1)} %get-tuple-element.20.refs_2_, f32[256,256]{1,0:T(8,128)S(1)} %get-tuple-element.21.refs_3_, ...), custom_call_target="tpu_custom_call" | custom-call | flops 4000000000 | bytes 3448896 | tf_op jit(solution)/shard_map/inner/pallas_call | solution.py:126
  23.4 1.3 %collective-permute-done.3.refs_2_ = bf16[128,1024]{1,0:T(8,128)(2,1)S(1)} collective-permute-done((bf16[128,1024]{1,0:T(8,128)(2,1)S(1)}, bf16[128,1024]{1,0:T(8,128)(2,1)S(1)}, u32[]{:S(2)}, u32[]{:S(2)}) %collective-permute-start.3) | collective-permute-done | bytes 262176 | tf_op jit(solution)/shard_map/ppermute | solution.py:533
  24.7 0.5 collective-permute-done.6.refs_6_.refs_5_
  25.2 0.2 pair.1
  25.5 0.1 collective-permute-start.12
  25.5 1.2 %collective-permute-start.8 = (bf16[128,1024]{1,0:T(8,128)(2,1)S(1)}, bf16[128,1024]{1,0:T(8,128)(2,1)S(1)}, u32[]{:S(2)}, u32[]{:S(2)}) collective-permute-start(bf16[128,1024]{1,0:T(8,128)(2,1)S(1)} %get-tuple-element.30.refs_5_.refs_2_), channel_id=1, source_target_pairs={{0,4},{4,0},{8,12},{12,8},{16,20},{20,16},{24,28},{28,24},{1,5},{5... | collective-permute-start | bytes 786440 | tf_op jit(solution)/shard_map/ppermute | solution.py:533
  26.8 0.5 collective-permute-start.9
  27.3 1.7 %collective-permute-start.7 = (s16[144,512]{1,0:T(8,128)(2,1)S(1)}, s16[144,512]{1,0:T(8,128)(2,1)S(1)}, u32[]{:S(2)}, u32[]{:S(2)}) collective-permute-start(s16[144,512]{1,0:T(8,128)(2,1)S(1)} %get-tuple-element.29), channel_id=1, source_target_pairs={{0,8},{4,12},{8,0},{12,4},{16,24},{20,28},{24,16},{28,20},{1,9},{5... | collective-permute-start | bytes 442376 | tf_op jit(solution)/shard_map/ppermute | solution.py:533
  29.0 3.9 %collective-permute-done.7.refs_1_.refs_3_ = s16[144,512]{1,0:T(8,128)(2,1)S(1)} collective-permute-done((s16[144,512]{1,0:T(8,128)(2,1)S(1)}, s16[144,512]{1,0:T(8,128)(2,1)S(1)}, u32[]{:S(2)}, u32[]{:S(2)}) %collective-permute-start.7) | collective-permute-done | bytes 147488 | tf_op jit(solution)/shard_map/ppermute | solution.py:533
  32.9 1.4 %collective-permute-done.8.refs_2_.refs_6_.refs_3_ = bf16[128,1024]{1,0:T(8,128)(2,1)S(1)} collective-permute-done((bf16[128,1024]{1,0:T(8,128)(2,1)S(1)}, bf16[128,1024]{1,0:T(8,128)(2,1)S(1)}, u32[]{:S(2)}, u32[]{:S(2)}) %collective-permute-start.8) | collective-permute-done | bytes 262176 | tf_op jit(solution)/shard_map/ppermute | solution.py:533
  34.3 0.9 %collective-permute-done.9.refs_3_.refs_7_.refs_4_ = bf16[128,1024]{1,0:T(8,128)(2,1)S(1)} collective-permute-done((bf16[128,1024]{1,0:T(8,128)(2,1)S(1)}, bf16[128,1024]{1,0:T(8,128)(2,1)S(1)}, u32[]{:S(2)}, u32[]{:S(2)}) %collective-permute-start.9) | collective-permute-done | bytes 262176 | tf_op jit(solution)/shard_map/ppermute | solution.py:533
  35.1 0.1 four.1
  35.3 0.7 %collective-permute-start.10 = (s16[144,512]{1,0:T(8,128)(2,1)S(1)}, s16[144,512]{1,0:T(8,128)(2,1)S(1)}, u32[]{:S(2)}, u32[]{:S(2)}) collective-permute-start(s16[144,512]{1,0:T(8,128)(2,1)S(1)} %get-tuple-element.31), channel_id=1, source_target_pairs={{0,16},{4,20},{8,24},{12,28},{16,0},{20,4},{24,8},{28,12},{1,17},{... | collective-permute-start | bytes 442376 | tf_op jit(solution)/shard_map/ppermute | solution.py:533
  36.0 1.5 %collective-permute-start.11 = (bf16[128,1024]{1,0:T(8,128)(2,1)S(1)}, bf16[128,1024]{1,0:T(8,128)(2,1)S(1)}, u32[]{:S(2)}, u32[]{:S(2)}) collective-permute-start(bf16[128,1024]{1,0:T(8,128)(2,1)S(1)} %collective-permute-done.9.refs_3_.refs_7_.refs_4_), channel_id=1, source_target_pairs={{0,4},{4,0},{8,12},{12,8},{16,20},{20,16},{24,28},{28,24},{1,5},{5... | collective-permute-start | bytes 786440 | tf_op jit(solution)/shard_map/ppermute | solution.py:533
  37.5 5.7 %experts.2.refs_9_.refs_8_ = bf16[1,512,1024]{2,1,0:T(8,128)(2,1)} custom-call(bf16[1,4096,1024]{2,1,0:T(8,128)(2,1)S(1)} %bitcast.4, bf16[1,4096,1024]{2,1,0:T(8,128)(2,1)S(1)} %bitcast.6, bf16[128,1024]{1,0:T(8,128)(2,1)S(1)} %join.1.refs_8_.refs_3_.refs_2_, bf16[128,1024]{1,0:T(8,128)(2,1)S(1)} %collective-permute-done.4.refs_4_.refs_3_, ...), custom_call_target="tpu_custom_call" | custom-call | flops 4294967296 | bytes 19927040 | tf_op jit(solution)/shard_map/experts/pallas_call | solution.py:126
  43.2 1.3 %collective-permute-done.10.refs_4_ = s16[144,512]{1,0:T(8,128)(2,1)S(1)} collective-permute-done((s16[144,512]{1,0:T(8,128)(2,1)S(1)}, s16[144,512]{1,0:T(8,128)(2,1)S(1)}, u32[]{:S(2)}, u32[]{:S(2)}) %collective-permute-start.10) | collective-permute-done | bytes 147488 | tf_op jit(solution)/shard_map/ppermute | solution.py:533
  44.5 0.4 turn.1
  44.9 0.1 collective-permute-start.14
  45.0 0.9 %collective-permute-start.13 = (s16[144,512]{1,0:T(8,128)(2,1)S(1)}, s16[144,512]{1,0:T(8,128)(2,1)S(1)}, u32[]{:S(2)}, u32[]{:S(2)}) collective-permute-start(s16[144,512]{1,0:T(8,128)(2,1)S(1)} %get-tuple-element.35), channel_id=1, source_target_pairs={{0,4},{4,0},{8,12},{12,8},{16,20},{20,16},{24,28},{28,24},{1,5},{5... | collective-permute-start | bytes 442376 | tf_op jit(solution)/shard_map/ppermute | solution.py:533
  45.9 1.7 %collective-permute-done.14.refs_6_ = bf16[512,1024]{1,0:T(8,128)(2,1)S(1)} collective-permute-done((bf16[512,1024]{1,0:T(8,128)(2,1)S(1)}, bf16[512,1024]{1,0:T(8,128)(2,1)S(1)}, u32[]{:S(2)}, u32[]{:S(2)}) %collective-permute-start.14) | collective-permute-done | bytes 1048608 | tf_op jit(solution)/shard_map/ppermute | solution.py:533
  47.6 5.8 %experts.3.refs_6_ = bf16[1,512,1024]{2,1,0:T(8,128)(2,1)} custom-call(bf16[1,4096,1024]{2,1,0:T(8,128)(2,1)S(1)} %bitcast.4, bf16[1,4096,1024]{2,1,0:T(8,128)(2,1)S(1)} %bitcast.6, bf16[128,1024]{1,0:T(8,128)(2,1)S(1)} %get-tuple-element.30.refs_5_.refs_2_, ...), custom_call_target="tpu_custom_call", output_to_operand_aliasing={{}: (8, {})} | custom-call | flops 4294967296 | bytes 20975616 | tf_op jit(solution)/shard_map/experts/pallas_call | solution.py:126
  53.5 2.5 %back.1 = bf16[256,1024]{1,0:T(8,128)(2,1)} custom-call(f32[1,1024]{1,0:T(1,128)S(1)} %get-tuple-element.23.refs_0_, f32[256,1024]{1,0:T(8,128)S(1)} %get-tuple-element.24.refs_7_.refs_1_, f32[256,1024]{1,0:T(8,128)S(1)} %get-tuple-element.25.refs_2_, f32[256,256]{1,0:T(8,128)S(1)} %get-tuple-element.21.refs_3_, f32[128,512]{1,0:T(8,128)S(1)} %get-tuple-element.34.refs_4_, ...), custom_call_target="tpu_custom_call" | custom-call | flops 1000000000 | bytes 3297280 | tf_op jit(solution)/shard_map/back/pallas_call | solution.py:126
  (18 shorter events, 0.0 us)
Async XLA Ops:
  0.6 7.3 %collective-permute-start.1 = (bf16[64,1024]{1,0:T(8,128)(2,1)}, bf16[64,1024]{1,0:T(8,128)(2,1)S(1)}, u32[]{:S(2)}, u32[]{:S(2)}) collective-permute-start(bf16[64,1024]{1,0:T(8,128)(2,1)} %refs_0_.6), channel_id=1, source_target_pairs={{0,8},{4,12},{8,0},{12,4},{16,24},{20,28},{24,16},{28,20},{1,9},{5... | collective-permute-start | bytes 393224 | tf_op jit(solution)/shard_map/ppermute | solution.py:533
  4.5 9.7 %collective-permute-start = (bf16[16,1280]{1,0:T(8,128)(2,1)S(1)}, bf16[16,1280]{1,0:T(8,128)(2,1)S(1)}, u32[]{:S(2)}, u32[]{:S(2)}) collective-permute-start(bf16[16,1280]{1,0:T(8,128)(2,1)S(1)} %ends.1), channel_id=1, source_target_pairs={{0,4},{4,8},{8,12},{12,16},{16,20},{20,24},{24,28},{1,5},{5,9},{9,... | collective-permute-start | bytes 122888 | tf_op jit(solution)/shard_map/ppermute | solution.py:670
  8.9 10.0 %collective-permute-start.4 = (bf16[128,1024]{1,0:T(8,128)(2,1)S(1)}, bf16[128,1024]{1,0:T(8,128)(2,1)S(1)}, u32[]{:S(2)}, u32[]{:S(2)}) collective-permute-start(bf16[128,1024]{1,0:T(8,128)(2,1)S(1)} %join.1.refs_8_.refs_3_.refs_2_), channel_id=1, source_target_pairs={{0,4},{4,0},{8,12},{12,8},{16,20},{20,16},{24,28},{28,24},{1,5},{5... | collective-permute-start | bytes 786440 | tf_op jit(solution)/shard_map/ppermute | solution.py:533
  10.1 13.3 %collective-permute-start.5 = (bf16[128,1024]{1,0:T(8,128)(2,1)S(1)}, bf16[128,1024]{1,0:T(8,128)(2,1)S(1)}, u32[]{:S(2)}, u32[]{:S(2)}) collective-permute-start(bf16[128,1024]{1,0:T(8,128)(2,1)S(1)} %join.1.refs_8_.refs_3_.refs_2_), channel_id=1, source_target_pairs={{0,2},{1,3},{2,0},{3,1},{4,6},{5,7},{6,4},{7,5},{8,10},{9,11},{10,... | collective-permute-start | bytes 786440 | tf_op jit(solution)/shard_map/ppermute | solution.py:533
  11.6 13.1 %collective-permute-start.3 = (bf16[128,1024]{1,0:T(8,128)(2,1)S(1)}, bf16[128,1024]{1,0:T(8,128)(2,1)S(1)}, u32[]{:S(2)}, u32[]{:S(2)}) collective-permute-start(bf16[128,1024]{1,0:T(8,128)(2,1)S(1)} %join.1.refs_8_.refs_3_.refs_2_), channel_id=1, source_target_pairs={{0,16},{4,20},{8,24},{12,28},{16,0},{20,4},{24,8},{28,12},{1,17},{... | collective-permute-start | bytes 786440 | tf_op jit(solution)/shard_map/ppermute | solution.py:533
  14.2 23.2 %slice-start = ((s8[8388608]{0:T(1024)(128)(4,1)}), s8[4194304]{0:T(1024)(128)(4,1)S(1)}, s32[]{:S(2)}) async-start(s8[8388608]{0:T(1024)(128)(4,1)} %bitcast.3), calls=%async_computation | async-start | bytes 8388608
  14.2 23.2 %slice-start.2 = ((s8[8388608]{0:T(1024)(128)(4,1)}), s8[4194304]{0:T(1024)(128)(4,1)S(1)}, s32[]{:S(2)}) async-start(s8[8388608]{0:T(1024)(128)(4,1)} %bitcast.5), calls=%async_computation.2 | async-start | bytes 8388608
  17.9 5.5 %collective-permute-start.2 = (s16[144,512]{1,0:T(8,128)(2,1)S(1)}, s16[144,512]{1,0:T(8,128)(2,1)S(1)}, u32[]{:S(2)}, u32[]{:S(2)}) collective-permute-start(s16[144,512]{1,0:T(8,128)(2,1)S(1)} %get-tuple-element.27), channel_id=1, source_target_pairs={{0,4},{4,0},{8,12},{12,8},{16,20},{20,16},{24,28},{28,24},{1,5},{5... | collective-permute-start | bytes 442376 | tf_op jit(solution)/shard_map/ppermute | solution.py:533
  18.9 6.4 %collective-permute-start.6 = (bf16[128,1024]{1,0:T(8,128)(2,1)S(1)}, bf16[128,1024]{1,0:T(8,128)(2,1)S(1)}, u32[]{:S(2)}, u32[]{:S(2)}) collective-permute-start(bf16[128,1024]{1,0:T(8,128)(2,1)S(1)} %collective-permute-done.4.refs_4_.refs_3_), channel_id=1, source_target_pairs={{0,2},{1,3},{2,0},{3,1},{4,6},{5,7},{6,4},{7,5},{8,10},{9,11},{10,... | collective-permute-start | bytes 786440 | tf_op jit(solution)/shard_map/ppermute | solution.py:533
  19.4 18.1 %slice-start.1 = ((s8[8388608]{0:T(1024)(128)(4,1)}), s8[4194304]{0:T(1024)(128)(4,1)S(1)}, s32[]{:S(2)}) async-start(s8[8388608]{0:T(1024)(128)(4,1)} %bitcast.3), calls=%async_computation.1 | async-start | bytes 8388608
  19.4 18.1 %slice-start.3 = ((s8[8388608]{0:T(1024)(128)(4,1)}), s8[4194304]{0:T(1024)(128)(4,1)S(1)}, s32[]{:S(2)}) async-start(s8[8388608]{0:T(1024)(128)(4,1)} %bitcast.5), calls=%async_computation.3 | async-start | bytes 8388608
  25.5 12.0 %collective-permute-start.12 = (bf16[512,1024]{1,0:T(8,128)(2,1)S(1)}, bf16[512,1024]{1,0:T(8,128)(2,1)S(1)}, u32[]{:S(2)}, u32[]{:S(2)}) collective-permute-start(bf16[512,1024]{1,0:T(8,128)(2,1)S(1)} %get-tuple-element.32), channel_id=1, source_target_pairs={{0,1},{1,0},{2,3},{3,2},{4,5},{5,4},{6,7},{7,6},{8,9},{9,8},{10,11... | collective-permute-start | bytes 3145736 | tf_op jit(solution)/shard_map/ppermute | solution.py:533
  25.5 8.7 %collective-permute-start.8 = (bf16[128,1024]{1,0:T(8,128)(2,1)S(1)}, bf16[128,1024]{1,0:T(8,128)(2,1)S(1)}, u32[]{:S(2)}, u32[]{:S(2)}) collective-permute-start(bf16[128,1024]{1,0:T(8,128)(2,1)S(1)} %get-tuple-element.30.refs_5_.refs_2_), channel_id=1, source_target_pairs={{0,4},{4,0},{8,12},{12,8},{16,20},{20,16},{24,28},{28,24},{1,5},{5... | collective-permute-start | bytes 786440 | tf_op jit(solution)/shard_map/ppermute | solution.py:533
  26.8 8.4 %collective-permute-start.9 = (bf16[128,1024]{1,0:T(8,128)(2,1)S(1)}, bf16[128,1024]{1,0:T(8,128)(2,1)S(1)}, u32[]{:S(2)}, u32[]{:S(2)}) collective-permute-start(bf16[128,1024]{1,0:T(8,128)(2,1)S(1)} %get-tuple-element.30.refs_5_.refs_2_), channel_id=1, source_target_pairs={{0,2},{1,3},{2,0},{3,1},{4,6},{5,7},{6,4},{7,5},{8,10},{9,11},{10,... | collective-permute-start | bytes 786440 | tf_op jit(solution)/shard_map/ppermute | solution.py:533
  27.3 5.6 %collective-permute-start.7 = (s16[144,512]{1,0:T(8,128)(2,1)S(1)}, s16[144,512]{1,0:T(8,128)(2,1)S(1)}, u32[]{:S(2)}, u32[]{:S(2)}) collective-permute-start(s16[144,512]{1,0:T(8,128)(2,1)S(1)} %get-tuple-element.29), channel_id=1, source_target_pairs={{0,8},{4,12},{8,0},{12,4},{16,24},{20,28},{24,16},{28,20},{1,9},{5... | collective-permute-start | bytes 442376 | tf_op jit(solution)/shard_map/ppermute | solution.py:533
  35.3 9.2 %collective-permute-start.10 = (s16[144,512]{1,0:T(8,128)(2,1)S(1)}, s16[144,512]{1,0:T(8,128)(2,1)S(1)}, u32[]{:S(2)}, u32[]{:S(2)}) collective-permute-start(s16[144,512]{1,0:T(8,128)(2,1)S(1)} %get-tuple-element.31), channel_id=1, source_target_pairs={{0,16},{4,20},{8,24},{12,28},{16,0},{20,4},{24,8},{28,12},{1,17},{... | collective-permute-start | bytes 442376 | tf_op jit(solution)/shard_map/ppermute | solution.py:533
  36.0 8.5 %collective-permute-start.11 = (bf16[128,1024]{1,0:T(8,128)(2,1)S(1)}, bf16[128,1024]{1,0:T(8,128)(2,1)S(1)}, u32[]{:S(2)}, u32[]{:S(2)}) collective-permute-start(bf16[128,1024]{1,0:T(8,128)(2,1)S(1)} %collective-permute-done.9.refs_3_.refs_7_.refs_4_), channel_id=1, source_target_pairs={{0,4},{4,0},{8,12},{12,8},{16,20},{20,16},{24,28},{28,24},{1,5},{5... | collective-permute-start | bytes 786440 | tf_op jit(solution)/shard_map/ppermute | solution.py:533
  44.9 2.7 %collective-permute-start.14 = (bf16[512,1024]{1,0:T(8,128)(2,1)S(1)}, bf16[512,1024]{1,0:T(8,128)(2,1)S(1)}, u32[]{:S(2)}, u32[]{:S(2)}) collective-permute-start(bf16[512,1024]{1,0:T(8,128)(2,1)S(1)} %get-tuple-element.36), channel_id=1, source_target_pairs={{0,1},{1,0},{2,3},{3,2},{4,5},{5,4},{6,7},{7,6},{8,9},{9,8},{10,11... | collective-permute-start | bytes 3145736 | tf_op jit(solution)/shard_map/ppermute | solution.py:533
  45.0 8.5 %collective-permute-start.13 = (s16[144,512]{1,0:T(8,128)(2,1)S(1)}, s16[144,512]{1,0:T(8,128)(2,1)S(1)}, u32[]{:S(2)}, u32[]{:S(2)}) collective-permute-start(s16[144,512]{1,0:T(8,128)(2,1)S(1)} %get-tuple-element.35), channel_id=1, source_target_pairs={{0,4},{4,0},{8,12},{12,8},{16,20},{20,16},{24,28},{28,24},{1,5},{5... | collective-permute-start | bytes 442376 | tf_op jit(solution)/shard_map/ppermute | solution.py:533

commit v17 on v15

--- a/solution.py
+++ b/solution.py
@@ -321,8 +321,11 @@
         joined_ref[i * rows : (i + 1) * rows] = piece[...]
 
 
-def four_body(width, pair_ref, got_ref, a, b, c, d, sent_ref, ids_ref, joined_ref):
+def four_body(
+    width, pair_ref, got_ref, a, b, c, d, e, f, g, sent_ref, ids_ref, joined_ref, later_ref
+):
     join_rows((a, b, c, d), joined_ref)
+    join_rows((e, f, g), later_ref)
     _, z, _ = place()
     four = together(z == 0, taken(pair_ref), received(got_ref), 2 * width)
     send(sent_ref, *four)
@@ -336,16 +339,13 @@
     pair_ref,
     pair_got_ref,
     four_got_ref,
-    a,
-    b,
-    c,
-    d,
+    rows_ref,
     mine_ref,
     sent_ref,
     ids_ref,
-    joined_ref,
+    same_rows_ref,
 ):
-    join_rows((a, b, c, d), joined_ref)
+    same_rows_ref[...] = rows_ref[...]
     x, z, zz = place()
     pair, pair_got, four_got = taken(pair_ref), received(pair_got_ref), received(four_got_ref)
     line = together(z == 0, pair, pair_got, 2 * width)[2]
@@ -410,25 +410,25 @@
     )
     far_pieces = spread_rows(rows, 1)
     pair_got = swapped(sent, "ctx", 2)
-    sent, ids, joined = call(
+    later_array = array((3 * far_rows.shape[0], far_rows.shape[1]), BF16)
+    sent, ids, joined, later = call(
         functools.partial(four_body, width),
-        [sent_array, ids_array, joined_array],
-        (pair, pair_got, *near_pieces),
+        [sent_array, ids_array, joined_array, later_array],
+        (pair, pair_got, *near_pieces, *far_pieces[:3]),
         near=True,
-        after=far_pieces[1:3],
         name="four",
     )
     four_got = swapped(sent, "ctx", 4)
     done = meanwhile(ids, joined)
-    mine, sent, ids, joined = call(
+    mine, sent, ids, rows = call(
         functools.partial(turn_body, width),
-        [array((STATE, keep.shape[1]), F32), sent_array, ids_array, joined_array],
-        (keep, got, pair, pair_got, four_got, *far_pieces),
+        [array((STATE, keep.shape[1]), F32), sent_array, ids_array, array(rows.shape, BF16)],
+        (keep, got, pair, pair_got, four_got, far_pieces[3]),
         near=True,
         after_far=(done,),
         name="turn",
     )
-    return (mine, swapped(sent, "ctx", 1)), far_pieces, ids, joined, done
+    return (mine, swapped(sent, "ctx", 1)), far_pieces, ids, (later, rows), done
 
 
 def entering_by_rows(state):
@@ -532,8 +532,10 @@
 
 
 def expert_body(part, w_gate, w_up, *refs):
-    pieces, joined_ref, ids_ref, out_far = refs[:4], refs[4], refs[5], refs[6 + part]
-    pick_ref, hid_ref, out_ref, sems = refs[7 + part :]
+    count = 1 + part
+    pieces, beside, refs = refs[:4], refs[4 : 4 + count], refs[4 + count :]
+    ids_ref, out_far = refs[0], refs[1 + part]
+    pick_ref, hid_ref, out_ref, sems = refs[2 + part :]
     length, hidden = out_ref.shape
     rows = pieces[0].shape[0] // 2
     depth = pieces[0].shape[1]
@@ -564,7 +566,9 @@
             if k % 2 == 0:
                 block = jnp.concatenate([piece[...] for piece in pieces[k : k + 2]], axis=0)
             else:
-                block = joined_ref[k // 2 * length : (k // 2 + 1) * length]
+                block = beside[0][k // 2 * length : min((k // 2 + 1) * length, beside[0].shape[0])]
+                if block.shape[0] < length:
+                    block = jnp.concatenate([block, beside[1][...]], axis=0)
             more = dot16(block, w_gate[0, downs[k], cut])
             gate = more if k == 0 else gate + more
             more = dot16(block, w_up[0, downs[k], cut])
@@ -596,11 +600,11 @@
     return (z, x, y, d)
 
 
-def experts_by_tokens(part, pieces, joined, ids, w_gate, w_up, so_far):
+def experts_by_tokens(part, pieces, sent, ids, w_gate, w_up, so_far):
     rows = pieces[0].shape[0] // 2
     length = 4 * rows
     hidden = w_gate.shape[2]
-    args = (w_gate, w_up, *pieces, swapped(joined, "exp", 1), ids)
+    args = (w_gate, w_up, *pieces, *(swapped(a, "exp", 1) for a in sent), ids)
     return call(
         functools.partial(expert_body, part),
         [pltpu.HBM((1, 2 * length, hidden), BF16)],
@@ -672,7 +676,7 @@
         pieces = spread_rows(near_rows, 0), far_rows
 
         def meanwhile(ids, joined):
-            return experts_by_tokens(0, pieces[0], joined, ids, w_gate, w_up, None)
+            return experts_by_tokens(0, pieces[0], (joined,), ids, w_gate, w_up, None)
 
     finish, late = mixing(
         pieces,

time: 55.6 us -> 54.5 us (0.980)
  waiting for transfers between devices: 10.2 us -> 8.65 us
    ppermute x14 -> x15, waiting for transfers between devices: 10.1 us -> 8.64 us  [swapped(): lax.ppermute(block, axis, [(i, i ^ bit) for i in range(lax.axis_size(axis...]
    ppermute x14 -> x15, starting transfers between devices: 16.7 us -> 17.1 us  [swapped(): lax.ppermute(block, axis, [(i, i ^ bit) for i in range(lax.axis_size(axis...]
  transfers between devices with their start and end apart: 15 -> 16, of which waited for: 7 -> 6; matrix products, arithmetic and copies ran while one was open for 0% -> 0% of each run, Pallas kernels for 38% -> 39%
where the time goes in v17:
time: 54.5 us; the launch traced here: 54.3 us
  Pallas kernels  24.2 us (44%)
  starting transfers between devices  20.5 us (38%)
  waiting for transfers between devices  8.65 us (16%)
  between operations  0.96 us (2%)
    pallas_call x10, Pallas kernels, call(): pl.pallas_call(body, out_shape=outs, in_specs=[pl.BlockSpec(memory_space=...  24.2 us
    ppermute x15, starting transfers between devices, swapped(): lax.ppermute(block, axis, [(i, i ^ bit) for i in range(lax.axis_size(axis...  17.1 us
    ppermute x15, waiting for transfers between devices, swapped(): lax.ppermute(block, axis, [(i, i ^ bit) for i in range(lax.axis_size(axis...  8.64 us
    ppermute x1, starting transfers between devices, on_device(): before = lax.ppermute(ends, 'ctx', [(i, i + 1) for i in range(ctx - 1)])  3.4 us
  transfers between devices with their start and end apart: 16, of which 6 were waited for; matrix products, arithmetic and copies ran while one was open for 0% of the time, Pallas kernels for 39%

profile of v17, /device:TPU:0, one launch (start us, length us, event | category | flops | bytes accessed | tf_op | source)
XLA Modules:
  0.0 54.3 jit_solution(10621221199196787758)
XLA Ops:
  0.6 3.1 %collective-permute-start.1 = (bf16[64,1024]{1,0:T(8,128)(2,1)}, bf16[64,1024]{1,0:T(8,128)(2,1)S(1)}, u32[]{:S(2)}, u32[]{:S(2)}) collective-permute-start(bf16[64,1024]{1,0:T(8,128)(2,1)} %refs_0_.6), channel_id=1, source_target_pairs={{0,8},{4,12},{8,0},{12,4},{16,24},{20,28},{24,16},{28,20},{1,9},{5... | collective-permute-start | bytes 393224 | tf_op jit(solution)/shard_map/ppermute | solution.py:531
  3.7 0.8 %ends.1 = bf16[16,1280]{1,0:T(8,128)(2,1)S(1)} custom-call(bf16[256,1024]{1,0:T(8,128)(2,1)} %refs_0_.7, bf16[256,128]{1,0:T(8,128)(2,1)} %refs_1_.5, bf16[256,128]{1,0:T(8,128)(2,1)} %refs_2_.3), custom_call_target="tpu_custom_call" | custom-call | bytes 696320 | tf_op jit(solution)/shard_map/ends/pallas_call | solution.py:126
  4.5 3.4 %collective-permute-start = (bf16[16,1280]{1,0:T(8,128)(2,1)S(1)}, bf16[16,1280]{1,0:T(8,128)(2,1)S(1)}, u32[]{:S(2)}, u32[]{:S(2)}) collective-permute-start(bf16[16,1280]{1,0:T(8,128)(2,1)S(1)} %ends.1), channel_id=1, source_target_pairs={{0,4},{4,8},{8,12},{12,16},{16,20},{20,24},{24,28},{1,5},{5,9},{9,... | collective-permute-start | bytes 122888 | tf_op jit(solution)/shard_map/ppermute | solution.py:672
  7.9 0.9 %join.1.refs_8_.refs_2_ = bf16[128,1024]{1,0:T(8,128)(2,1)S(1)} custom-call(bf16[64,1024]{1,0:T(8,128)(2,1)} %refs_0_.6, bf16[64,1024]{1,0:T(8,128)(2,1)S(1)} %collective-permute-done.1.refs_1_), custom_call_target="tpu_custom_call" | custom-call | bytes 524288 | tf_op jit(solution)/shard_map/join/pallas_call | solution.py:126
  8.9 1.2 %collective-permute-start.5 = (bf16[128,1024]{1,0:T(8,128)(2,1)S(1)}, bf16[128,1024]{1,0:T(8,128)(2,1)S(1)}, u32[]{:S(2)}, u32[]{:S(2)}) collective-permute-start(bf16[128,1024]{1,0:T(8,128)(2,1)S(1)} %join.1.refs_8_.refs_2_), channel_id=1, source_target_pairs={{0,4},{4,0},{8,12},{12,8},{16,20},{20,16},{24,28},{28,24},{1,5},{5... | collective-permute-start | bytes 786440 | tf_op jit(solution)/shard_map/ppermute | solution.py:531
  10.1 1.5 %collective-permute-start.4 = (bf16[128,1024]{1,0:T(8,128)(2,1)S(1)}, bf16[128,1024]{1,0:T(8,128)(2,1)S(1)}, u32[]{:S(2)}, u32[]{:S(2)}) collective-permute-start(bf16[128,1024]{1,0:T(8,128)(2,1)S(1)} %join.1.refs_8_.refs_2_), channel_id=1, source_target_pairs={{0,2},{1,3},{2,0},{3,1},{4,6},{5,7},{6,4},{7,5},{8,10},{9,11},{10,... | collective-permute-start | bytes 786440 | tf_op jit(solution)/shard_map/ppermute | solution.py:531
  11.6 2.6 %collective-permute-start.3 = (bf16[128,1024]{1,0:T(8,128)(2,1)S(1)}, bf16[128,1024]{1,0:T(8,128)(2,1)S(1)}, u32[]{:S(2)}, u32[]{:S(2)}) collective-permute-start(bf16[128,1024]{1,0:T(8,128)(2,1)S(1)} %join.1.refs_8_.refs_2_), channel_id=1, source_target_pairs={{0,16},{4,20},{8,24},{12,28},{16,0},{20,4},{24,8},{28,12},{1,17},{... | collective-permute-start | bytes 786440 | tf_op jit(solution)/shard_map/ppermute | solution.py:531
  14.2 3.7 %front.1 = (f32[256,1024]{1,0:T(8,128)S(1)}, f32[256,256]{1,0:T(8,128)S(1)}, f32[2,16,256]{2,1,0:T(8,128)S(1)}, f32[136,512]{1,0:T(8,128)S(1)}, s16[144,512]{1,0:T(8,128)(2,1)S(1)}) custom-call(bf16[256,1024]{1,0:T(8,128)(2,1)} %refs_0_.7, bf16[256,128]{1,0:T(8,128)(2,1)} %refs_1_.5, bf16[256,128]{1,0:T(8,128)(2,1)} %refs_2_.3, f32[4,1024]{1,0:T(4,128)} %refs_3_.1, ...), custom_call_target="tpu_custom_call" | custom-call | flops 5000000000 | bytes 2503168 | tf_op jit(solution)/shard_map/front/pallas_call | solution.py:126
  17.9 0.9 %collective-permute-start.2 = (s16[144,512]{1,0:T(8,128)(2,1)S(1)}, s16[144,512]{1,0:T(8,128)(2,1)S(1)}, u32[]{:S(2)}, u32[]{:S(2)}) collective-permute-start(s16[144,512]{1,0:T(8,128)(2,1)S(1)} %get-tuple-element.28), channel_id=1, source_target_pairs={{0,4},{4,0},{8,12},{12,8},{16,20},{20,16},{24,28},{28,24},{1,5},{5... | collective-permute-start | bytes 442376 | tf_op jit(solution)/shard_map/ppermute | solution.py:531
  18.9 0.5 collective-permute-start.6
  19.4 4.0 %inner.1 = (f32[256,1024]{1,0:T(8,128)S(1)}, f32[256,1024]{1,0:T(8,128)S(1)}, f32[1,1024]{1,0:T(1,128)S(1)}) custom-call(f32[1,16]{1,0:T(1,128)} %bitcast.9, f32[1,1024]{1,0:T(1,128)} %bitcast.7, f32[256,1024]{1,0:T(8,128)S(1)} %get-tuple-element.21.refs_2_, f32[256,256]{1,0:T(8,128)S(1)} %get-tuple-element.22.refs_3_, ...), custom_call_target="tpu_custom_call" | custom-call | flops 4000000000 | bytes 3448896 | tf_op jit(solution)/shard_map/inner/pallas_call | solution.py:126
  23.4 1.3 %collective-permute-done.3.refs_2_ = bf16[128,1024]{1,0:T(8,128)(2,1)S(1)} collective-permute-done((bf16[128,1024]{1,0:T(8,128)(2,1)S(1)}, bf16[128,1024]{1,0:T(8,128)(2,1)S(1)}, u32[]{:S(2)}, u32[]{:S(2)}) %collective-permute-start.3) | collective-permute-done | bytes 262176 | tf_op jit(solution)/shard_map/ppermute | solution.py:531
  24.7 0.5 collective-permute-done.6.refs_4_.refs_5_
  25.2 0.2 pair.1
  25.4 1.2 %collective-permute-start.8 = (bf16[128,1024]{1,0:T(8,128)(2,1)S(1)}, bf16[128,1024]{1,0:T(8,128)(2,1)S(1)}, u32[]{:S(2)}, u32[]{:S(2)}) collective-permute-start(bf16[128,1024]{1,0:T(8,128)(2,1)S(1)} %get-tuple-element.31.refs_6_.refs_2_), channel_id=1, source_target_pairs={{0,4},{4,0},{8,12},{12,8},{16,20},{20,16},{24,28},{28,24},{1,5},{5... | collective-permute-start | bytes 786440 | tf_op jit(solution)/shard_map/ppermute | solution.py:531
  26.6 0.5 collective-permute-start.9
  27.1 1.7 %collective-permute-start.7 = (s16[144,512]{1,0:T(8,128)(2,1)S(1)}, s16[144,512]{1,0:T(8,128)(2,1)S(1)}, u32[]{:S(2)}, u32[]{:S(2)}) collective-permute-start(s16[144,512]{1,0:T(8,128)(2,1)S(1)} %get-tuple-element.30), channel_id=1, source_target_pairs={{0,8},{4,12},{8,0},{12,4},{16,24},{20,28},{24,16},{28,20},{1,9},{5... | collective-permute-start | bytes 442376 | tf_op jit(solution)/shard_map/ppermute | solution.py:531
  28.8 3.4 %collective-permute-done.7.refs_1_.refs_3_ = s16[144,512]{1,0:T(8,128)(2,1)S(1)} collective-permute-done((s16[144,512]{1,0:T(8,128)(2,1)S(1)}, s16[144,512]{1,0:T(8,128)(2,1)S(1)}, u32[]{:S(2)}, u32[]{:S(2)}) %collective-permute-start.7) | collective-permute-done | bytes 147488 | tf_op jit(solution)/shard_map/ppermute | solution.py:531
  32.3 0.9 %collective-permute-done.9.refs_8_.refs_4_ = bf16[128,1024]{1,0:T(8,128)(2,1)S(1)} collective-permute-done((bf16[128,1024]{1,0:T(8,128)(2,1)S(1)}, bf16[128,1024]{1,0:T(8,128)(2,1)S(1)}, u32[]{:S(2)}, u32[]{:S(2)}) %collective-permute-start.9) | collective-permute-done | bytes 262176 | tf_op jit(solution)/shard_map/ppermute | solution.py:531
  33.1 0.3 four.1
  33.4 0.1 collective-permute-start.12
  33.5 0.5 collective-permute-start.14
  34.0 1.0 %collective-permute-start.10 = (s16[144,512]{1,0:T(8,128)(2,1)S(1)}, s16[144,512]{1,0:T(8,128)(2,1)S(1)}, u32[]{:S(2)}, u32[]{:S(2)}) collective-permute-start(s16[144,512]{1,0:T(8,128)(2,1)S(1)} %get-tuple-element.32), channel_id=1, source_target_pairs={{0,16},{4,20},{8,24},{12,28},{16,0},{20,4},{24,8},{28,12},{1,17},{... | collective-permute-start | bytes 442376 | tf_op jit(solution)/shard_map/ppermute | solution.py:531
  35.0 1.4 %collective-permute-start.11 = (bf16[128,1024]{1,0:T(8,128)(2,1)S(1)}, bf16[128,1024]{1,0:T(8,128)(2,1)S(1)}, u32[]{:S(2)}, u32[]{:S(2)}) collective-permute-start(bf16[128,1024]{1,0:T(8,128)(2,1)S(1)} %collective-permute-done.9.refs_8_.refs_4_), channel_id=1, source_target_pairs={{0,4},{4,0},{8,12},{12,8},{16,20},{20,16},{24,28},{28,24},{1,5},{5... | collective-permute-start | bytes 786440 | tf_op jit(solution)/shard_map/ppermute | solution.py:531
  36.4 5.7 %experts.2.refs_6_.refs_9_ = bf16[1,512,1024]{2,1,0:T(8,128)(2,1)} custom-call(bf16[1,4096,1024]{2,1,0:T(8,128)(2,1)S(1)} %bitcast.4, bf16[1,4096,1024]{2,1,0:T(8,128)(2,1)S(1)} %bitcast.6, bf16[128,1024]{1,0:T(8,128)(2,1)S(1)} %join.1.refs_8_.refs_2_, bf16[128,1024]{1,0:T(8,128)(2,1)S(1)} %collective-permute-done.5.refs_3_, ...), custom_call_target="tpu_custom_call" | custom-call | flops 4294967296 | bytes 19927040 | tf_op jit(solution)/shard_map/experts/pallas_call | solution.py:126
  42.1 1.7 %collective-permute-done.10.refs_4_ = s16[144,512]{1,0:T(8,128)(2,1)S(1)} collective-permute-done((s16[144,512]{1,0:T(8,128)(2,1)S(1)}, s16[144,512]{1,0:T(8,128)(2,1)S(1)}, u32[]{:S(2)}, u32[]{:S(2)}) %collective-permute-start.10) | collective-permute-done | bytes 147488 | tf_op jit(solution)/shard_map/ppermute | solution.py:531
  43.9 0.3 turn.1
  44.2 0.1 collective-permute-start.15
  44.3 0.8 %collective-permute-start.13 = (s16[144,512]{1,0:T(8,128)(2,1)S(1)}, s16[144,512]{1,0:T(8,128)(2,1)S(1)}, u32[]{:S(2)}, u32[]{:S(2)}) collective-permute-start(s16[144,512]{1,0:T(8,128)(2,1)S(1)} %get-tuple-element.36), channel_id=1, source_target_pairs={{0,4},{4,0},{8,12},{12,8},{16,20},{20,16},{24,28},{28,24},{1,5},{5... | collective-permute-start | bytes 442376 | tf_op jit(solution)/shard_map/ppermute | solution.py:531
  45.1 0.7 %collective-permute-done.15.refs_7_ = bf16[128,1024]{1,0:T(8,128)(2,1)S(1)} collective-permute-done((bf16[128,1024]{1,0:T(8,128)(2,1)S(1)}, bf16[128,1024]{1,0:T(8,128)(2,1)S(1)}, u32[]{:S(2)}, u32[]{:S(2)}) %collective-permute-start.15) | collective-permute-done | bytes 262176 | tf_op jit(solution)/shard_map/ppermute | solution.py:531
  45.8 5.9 %experts.3.refs_6_ = bf16[1,512,1024]{2,1,0:T(8,128)(2,1)} custom-call(bf16[1,4096,1024]{2,1,0:T(8,128)(2,1)S(1)} %bitcast.4, bf16[1,4096,1024]{2,1,0:T(8,128)(2,1)S(1)} %bitcast.6, bf16[128,1024]{1,0:T(8,128)(2,1)S(1)} %get-tuple-element.31.refs_6_.refs_2_, ...), custom_call_target="tpu_custom_call", output_to_operand_aliasing={{}: (9, {})} | custom-call | flops 4294967296 | bytes 20975616 | tf_op jit(solution)/shard_map/experts/pallas_call | solution.py:126
  51.7 2.5 %back.1 = bf16[256,1024]{1,0:T(8,128)(2,1)} custom-call(f32[1,1024]{1,0:T(1,128)S(1)} %get-tuple-element.24.refs_0_, f32[256,1024]{1,0:T(8,128)S(1)} %get-tuple-element.25.refs_5_.refs_1_, f32[256,1024]{1,0:T(8,128)S(1)} %get-tuple-element.26.refs_2_, f32[256,256]{1,0:T(8,128)S(1)} %get-tuple-element.22.refs_3_, f32[128,512]{1,0:T(8,128)S(1)} %get-tuple-element.35.refs_4_, ...), custom_call_target="tpu_custom_call" | custom-call | flops 1000000000 | bytes 3297280 | tf_op jit(solution)/shard_map/back/pallas_call | solution.py:126
  (20 shorter events, 0.0 us)
Async XLA Ops:
  0.6 7.3 %collective-permute-start.1 = (bf16[64,1024]{1,0:T(8,128)(2,1)}, bf16[64,1024]{1,0:T(8,128)(2,1)S(1)}, u32[]{:S(2)}, u32[]{:S(2)}) collective-permute-start(bf16[64,1024]{1,0:T(8,128)(2,1)} %refs_0_.6), channel_id=1, source_target_pairs={{0,8},{4,12},{8,0},{12,4},{16,24},{20,28},{24,16},{28,20},{1,9},{5... | collective-permute-start | bytes 393224 | tf_op jit(solution)/shard_map/ppermute | solution.py:531
  4.5 9.7 %collective-permute-start = (bf16[16,1280]{1,0:T(8,128)(2,1)S(1)}, bf16[16,1280]{1,0:T(8,128)(2,1)S(1)}, u32[]{:S(2)}, u32[]{:S(2)}) collective-permute-start(bf16[16,1280]{1,0:T(8,128)(2,1)S(1)} %ends.1), channel_id=1, source_target_pairs={{0,4},{4,8},{8,12},{12,16},{16,20},{20,24},{24,28},{1,5},{5,9},{9,... | collective-permute-start | bytes 122888 | tf_op jit(solution)/shard_map/ppermute | solution.py:672
  8.9 10.0 %collective-permute-start.5 = (bf16[128,1024]{1,0:T(8,128)(2,1)S(1)}, bf16[128,1024]{1,0:T(8,128)(2,1)S(1)}, u32[]{:S(2)}, u32[]{:S(2)}) collective-permute-start(bf16[128,1024]{1,0:T(8,128)(2,1)S(1)} %join.1.refs_8_.refs_2_), channel_id=1, source_target_pairs={{0,4},{4,0},{8,12},{12,8},{16,20},{20,16},{24,28},{28,24},{1,5},{5... | collective-permute-start | bytes 786440 | tf_op jit(solution)/shard_map/ppermute | solution.py:531
  10.1 13.3 %collective-permute-start.4 = (bf16[128,1024]{1,0:T(8,128)(2,1)S(1)}, bf16[128,1024]{1,0:T(8,128)(2,1)S(1)}, u32[]{:S(2)}, u32[]{:S(2)}) collective-permute-start(bf16[128,1024]{1,0:T(8,128)(2,1)S(1)} %join.1.refs_8_.refs_2_), channel_id=1, source_target_pairs={{0,2},{1,3},{2,0},{3,1},{4,6},{5,7},{6,4},{7,5},{8,10},{9,11},{10,... | collective-permute-start | bytes 786440 | tf_op jit(solution)/shard_map/ppermute | solution.py:531
  11.6 13.1 %collective-permute-start.3 = (bf16[128,1024]{1,0:T(8,128)(2,1)S(1)}, bf16[128,1024]{1,0:T(8,128)(2,1)S(1)}, u32[]{:S(2)}, u32[]{:S(2)}) collective-permute-start(bf16[128,1024]{1,0:T(8,128)(2,1)S(1)} %join.1.refs_8_.refs_2_), channel_id=1, source_target_pairs={{0,16},{4,20},{8,24},{12,28},{16,0},{20,4},{24,8},{28,12},{1,17},{... | collective-permute-start | bytes 786440 | tf_op jit(solution)/shard_map/ppermute | solution.py:531
  14.2 22.2 %slice-start.2 = ((s8[8388608]{0:T(1024)(128)(4,1)}), s8[4194304]{0:T(1024)(128)(4,1)S(1)}, s32[]{:S(2)}) async-start(s8[8388608]{0:T(1024)(128)(4,1)} %bitcast.5), calls=%async_computation.2 | async-start | bytes 8388608
  17.9 5.5 %collective-permute-start.2 = (s16[144,512]{1,0:T(8,128)(2,1)S(1)}, s16[144,512]{1,0:T(8,128)(2,1)S(1)}, u32[]{:S(2)}, u32[]{:S(2)}) collective-permute-start(s16[144,512]{1,0:T(8,128)(2,1)S(1)} %get-tuple-element.28), channel_id=1, source_target_pairs={{0,4},{4,0},{8,12},{12,8},{16,20},{20,16},{24,28},{28,24},{1,5},{5... | collective-permute-start | bytes 442376 | tf_op jit(solution)/shard_map/ppermute | solution.py:531
  18.9 6.4 %collective-permute-start.6 = (bf16[128,1024]{1,0:T(8,128)(2,1)S(1)}, bf16[128,1024]{1,0:T(8,128)(2,1)S(1)}, u32[]{:S(2)}, u32[]{:S(2)}) collective-permute-start(bf16[128,1024]{1,0:T(8,128)(2,1)S(1)} %collective-permute-done.5.refs_3_), channel_id=1, source_target_pairs={{0,2},{1,3},{2,0},{3,1},{4,6},{5,7},{6,4},{7,5},{8,10},{9,11},{10,... | collective-permute-start | bytes 786440 | tf_op jit(solution)/shard_map/ppermute | solution.py:531
  19.4 17.0 %slice-start = ((s8[8388608]{0:T(1024)(128)(4,1)}), s8[4194304]{0:T(1024)(128)(4,1)S(1)}, s32[]{:S(2)}) async-start(s8[8388608]{0:T(1024)(128)(4,1)} %bitcast.3), calls=%async_computation | async-start | bytes 8388608
  19.4 17.0 %slice-start.1 = ((s8[8388608]{0:T(1024)(128)(4,1)}), s8[4194304]{0:T(1024)(128)(4,1)S(1)}, s32[]{:S(2)}) async-start(s8[8388608]{0:T(1024)(128)(4,1)} %bitcast.3), calls=%async_computation.1 | async-start | bytes 8388608
  19.4 17.0 %slice-start.3 = ((s8[8388608]{0:T(1024)(128)(4,1)}), s8[4194304]{0:T(1024)(128)(4,1)S(1)}, s32[]{:S(2)}) async-start(s8[8388608]{0:T(1024)(128)(4,1)} %bitcast.5), calls=%async_computation.3 | async-start | bytes 8388608
  25.4 6.9 %collective-permute-start.8 = (bf16[128,1024]{1,0:T(8,128)(2,1)S(1)}, bf16[128,1024]{1,0:T(8,128)(2,1)S(1)}, u32[]{:S(2)}, u32[]{:S(2)}) collective-permute-start(bf16[128,1024]{1,0:T(8,128)(2,1)S(1)} %get-tuple-element.31.refs_6_.refs_2_), channel_id=1, source_target_pairs={{0,4},{4,0},{8,12},{12,8},{16,20},{20,16},{24,28},{28,24},{1,5},{5... | collective-permute-start | bytes 786440 | tf_op jit(solution)/shard_map/ppermute | solution.py:531
  26.6 6.5 %collective-permute-start.9 = (bf16[128,1024]{1,0:T(8,128)(2,1)S(1)}, bf16[128,1024]{1,0:T(8,128)(2,1)S(1)}, u32[]{:S(2)}, u32[]{:S(2)}) collective-permute-start(bf16[128,1024]{1,0:T(8,128)(2,1)S(1)} %get-tuple-element.31.refs_6_.refs_2_), channel_id=1, source_target_pairs={{0,2},{1,3},{2,0},{3,1},{4,6},{5,7},{6,4},{7,5},{8,10},{9,11},{10,... | collective-permute-start | bytes 786440 | tf_op jit(solution)/shard_map/ppermute | solution.py:531
  27.1 5.1 %collective-permute-start.7 = (s16[144,512]{1,0:T(8,128)(2,1)S(1)}, s16[144,512]{1,0:T(8,128)(2,1)S(1)}, u32[]{:S(2)}, u32[]{:S(2)}) collective-permute-start(s16[144,512]{1,0:T(8,128)(2,1)S(1)} %get-tuple-element.30), channel_id=1, source_target_pairs={{0,8},{4,12},{8,0},{12,4},{16,24},{20,28},{24,16},{28,20},{1,9},{5... | collective-permute-start | bytes 442376 | tf_op jit(solution)/shard_map/ppermute | solution.py:531
  33.4 3.0 %collective-permute-start.12 = (bf16[512,1024]{1,0:T(8,128)(2,1)S(1)}, bf16[512,1024]{1,0:T(8,128)(2,1)S(1)}, u32[]{:S(2)}, u32[]{:S(2)}) collective-permute-start(bf16[512,1024]{1,0:T(8,128)(2,1)S(1)} %get-tuple-element.33), channel_id=1, source_target_pairs={{0,1},{1,0},{2,3},{3,2},{4,5},{5,4},{6,7},{7,6},{8,9},{9,8},{10,11... | collective-permute-start | bytes 3145736 | tf_op jit(solution)/shard_map/ppermute | solution.py:531
  33.5 11.6 %collective-permute-start.14 = (bf16[384,1024]{1,0:T(8,128)(2,1)S(1)}, bf16[384,1024]{1,0:T(8,128)(2,1)S(1)}, u32[]{:S(2)}, u32[]{:S(2)}) collective-permute-start(bf16[384,1024]{1,0:T(8,128)(2,1)S(1)} %get-tuple-element.37), channel_id=1, source_target_pairs={{0,1},{1,0},{2,3},{3,2},{4,5},{5,4},{6,7},{7,6},{8,9},{9,8},{10,11... | collective-permute-start | bytes 2359304 | tf_op jit(solution)/shard_map/ppermute | solution.py:531
  34.0 9.9 %collective-permute-start.10 = (s16[144,512]{1,0:T(8,128)(2,1)S(1)}, s16[144,512]{1,0:T(8,128)(2,1)S(1)}, u32[]{:S(2)}, u32[]{:S(2)}) collective-permute-start(s16[144,512]{1,0:T(8,128)(2,1)S(1)} %get-tuple-element.32), channel_id=1, source_target_pairs={{0,16},{4,20},{8,24},{12,28},{16,0},{20,4},{24,8},{28,12},{1,17},{... | collective-permute-start | bytes 442376 | tf_op jit(solution)/shard_map/ppermute | solution.py:531
  35.0 8.9 %collective-permute-start.11 = (bf16[128,1024]{1,0:T(8,128)(2,1)S(1)}, bf16[128,1024]{1,0:T(8,128)(2,1)S(1)}, u32[]{:S(2)}, u32[]{:S(2)}) collective-permute-start(bf16[128,1024]{1,0:T(8,128)(2,1)S(1)} %collective-permute-done.9.refs_8_.refs_4_), channel_id=1, source_target_pairs={{0,4},{4,0},{8,12},{12,8},{16,20},{20,16},{24,28},{28,24},{1,5},{5... | collective-permute-start | bytes 786440 | tf_op jit(solution)/shard_map/ppermute | solution.py:531
  44.2 1.6 %collective-permute-start.15 = (bf16[128,1024]{1,0:T(8,128)(2,1)S(1)}, bf16[128,1024]{1,0:T(8,128)(2,1)S(1)}, u32[]{:S(2)}, u32[]{:S(2)}) collective-permute-start(bf16[128,1024]{1,0:T(8,128)(2,1)S(1)} %get-tuple-element.38), channel_id=1, source_target_pairs={{0,1},{1,0},{2,3},{3,2},{4,5},{5,4},{6,7},{7,6},{8,9},{9,8},{10,11... | collective-permute-start | bytes 786440 | tf_op jit(solution)/shard_map/ppermute | solution.py:531
  44.3 7.4 %collective-permute-start.13 = (s16[144,512]{1,0:T(8,128)(2,1)S(1)}, s16[144,512]{1,0:T(8,128)(2,1)S(1)}, u32[]{:S(2)}, u32[]{:S(2)}) collective-permute-start(s16[144,512]{1,0:T(8,128)(2,1)S(1)} %get-tuple-element.36), channel_id=1, source_target_pairs={{0,4},{4,0},{8,12},{12,8},{16,20},{20,16},{24,28},{28,24},{1,5},{5... | collective-permute-start | bytes 442376 | tf_op jit(solution)/shard_map/ppermute | solution.py:531

commit v18 on v17

--- a/solution.py
+++ b/solution.py
@@ -144,16 +144,17 @@
     return jax.ShapeDtypeStruct(shape, dtype)
 
 
-def ends_body(x_ref, b_ref, c_ref, ends_ref, sems):
+def ends_body(x_ref, b_ref, c_ref, rows_ref, ends_ref, held_ref, sems):
     tokens, channels = x_ref.shape
     cut = pl.ds(tokens - EDGE, EDGE)
     finished(
         started(
-            [x_ref.at[cut, :], b_ref.at[cut, :], c_ref.at[cut, :]],
+            [x_ref.at[cut, :], b_ref.at[cut, :], c_ref.at[cut, :], rows_ref],
             [
                 ends_ref.at[:, pl.ds(0, channels)],
                 ends_ref.at[:, pl.ds(channels, STATE)],
                 ends_ref.at[:, pl.ds(channels + STATE, STATE)],
+                held_ref,
             ],
             sems,
         )
@@ -520,11 +521,8 @@
 TILE = 512
 
 
-def join_body(a_ref, b_ref, out_ref, sems):
-    rows = a_ref.shape[0]
-    finished(
-        started([a_ref, b_ref], [out_ref.at[pl.ds(0, rows), :], out_ref.at[pl.ds(rows, rows), :]], sems)
-    )
+def join_body(a, b, joined_ref):
+    join_rows((a, b), joined_ref)
 
 
 def swapped(block, axis, bit):
@@ -581,16 +579,15 @@
     finished(out_copies)
 
 
-def along_z(moe_input):
+def along_z(moe_input, held):
     rows, columns = moe_input.shape
-    joined = call(
+    (joined,) = call(
         join_body,
         [array((2 * rows, columns), BF16)],
-        (moe_input, swapped(moe_input, "ctx", 2)),
-        fixed=1,
-        sems=2,
+        (held, swapped(moe_input, "ctx", 2)),
+        near=True,
         name="join",
-    )[0]
+    )
     return joined, swapped(joined, "ctx", 4)
 
 
@@ -661,18 +658,19 @@
     ctx = lax.axis_size("ctx")
     by_tokens = lax.axis_size("exp") == 4 and ctx == 8
     tokens, channels = seq_input.shape
-    ends = call(
+    ends, held = call(
         ends_body,
-        [array((EDGE, channels + 2 * STATE), BF16)],
-        (seq_input, b_input, c_input),
-        fixed=3,
-        sems=3,
+        [array((EDGE, channels + 2 * STATE), BF16), array(moe_input.shape, BF16)],
+        (seq_input, b_input, c_input, moe_input),
+        fixed=4,
+        near_outs=1,
+        sems=4,
         name="ends",
-    )[0]
+    )
     before = lax.ppermute(ends, "ctx", [(i, i + 1) for i in range(ctx - 1)])
     pieces = meanwhile = None
     if by_tokens:
-        near_rows, far_rows = along_z(moe_input)
+        near_rows, far_rows = along_z(moe_input, held)
         pieces = spread_rows(near_rows, 0), far_rows
 
         def meanwhile(ids, joined):

time: 54.5 us -> 53.8 us (0.987)
  Pallas kernels: 24.2 us -> 23.5 us
    pallas_call x10, Pallas kernels: 24.2 us -> 23.5 us  [call(): pl.pallas_call(body, out_shape=outs, in_specs=[pl.BlockSpec(memory_space=...]
where the time goes in v18:
time: 53.8 us; the launch traced here: 53.6 us
  Pallas kernels  23.5 us (44%)
  starting transfers between devices  20 us (37%)
  waiting for transfers between devices  9.14 us (17%)
  between operations  0.96 us (2%)
    pallas_call x10, Pallas kernels, call(): pl.pallas_call(body, out_shape=outs, in_specs=[pl.BlockSpec(memory_space=...  23.5 us
    ppermute x15, starting transfers between devices, swapped(): lax.ppermute(block, axis, [(i, i ^ bit) for i in range(lax.axis_size(axis...  16.6 us
    ppermute x15, waiting for transfers between devices, swapped(): lax.ppermute(block, axis, [(i, i ^ bit) for i in range(lax.axis_size(axis...  9.13 us
    ppermute x1, starting transfers between devices, on_device(): before = lax.ppermute(ends, 'ctx', [(i, i + 1) for i in range(ctx - 1)])  3.4 us
  transfers between devices with their start and end apart: 16, of which 6 were waited for; matrix products, arithmetic and copies ran while one was open for 0% of the time, Pallas kernels for 39%

profile of v18, /device:TPU:0, one launch (start us, length us, event | category | flops | bytes accessed | tf_op | source)
XLA Modules:
  0.0 53.6 jit_solution(11245558307235769628)
XLA Ops:
  0.6 3.1 %collective-permute-start.1 = (bf16[64,1024]{1,0:T(8,128)(2,1)}, bf16[64,1024]{1,0:T(8,128)(2,1)S(1)}, u32[]{:S(2)}, u32[]{:S(2)}) collective-permute-start(bf16[64,1024]{1,0:T(8,128)(2,1)} %refs_3_.2), channel_id=1, source_target_pairs={{0,8},{4,12},{8,0},{12,4},{16,24},{20,28},{24,16},{28,20},{1,9},{5... | collective-permute-start | bytes 393224 | tf_op jit(solution)/shard_map/ppermute | solution.py:529
  3.7 1.0 %ends.1 = (bf16[16,1280]{1,0:T(8,128)(2,1)S(1)}, bf16[64,1024]{1,0:T(8,128)(2,1)S(1)}) custom-call(bf16[256,1024]{1,0:T(8,128)(2,1)} %refs_0_.5, bf16[256,128]{1,0:T(8,128)(2,1)} %refs_1_.5, bf16[256,128]{1,0:T(8,128)(2,1)} %refs_2_.3, bf16[64,1024]{1,0:T(8,128)(2,1)} %refs_3_.2), custom_call_target="tpu_custom_call" | custom-call | bytes 958464 | tf_op jit(solution)/shard_map/ends/pallas_call | solution.py:126
  4.7 3.4 %collective-permute-start = (bf16[16,1280]{1,0:T(8,128)(2,1)S(1)}, bf16[16,1280]{1,0:T(8,128)(2,1)S(1)}, u32[]{:S(2)}, u32[]{:S(2)}) collective-permute-start(bf16[16,1280]{1,0:T(8,128)(2,1)S(1)} %get-tuple-element.23), channel_id=1, source_target_pairs={{0,4},{4,8},{8,12},{12,16},{16,20},{20,24},{24,28},{1,5},{5,9},{9,... | collective-permute-start | bytes 122888 | tf_op jit(solution)/shard_map/ppermute | solution.py:670
  8.2 1.0 %collective-permute-start.5 = (bf16[128,1024]{1,0:T(8,128)(2,1)S(1)}, bf16[128,1024]{1,0:T(8,128)(2,1)S(1)}, u32[]{:S(2)}, u32[]{:S(2)}) collective-permute-start(bf16[128,1024]{1,0:T(8,128)(2,1)S(1)} %join.1.refs_8_.refs_2_), channel_id=1, source_target_pairs={{0,4},{4,0},{8,12},{12,8},{16,20},{20,16},{24,28},{28,24},{1,5},{5... | collective-permute-start | bytes 786440 | tf_op jit(solution)/shard_map/ppermute | solution.py:529
  9.2 1.5 %collective-permute-start.4 = (bf16[128,1024]{1,0:T(8,128)(2,1)S(1)}, bf16[128,1024]{1,0:T(8,128)(2,1)S(1)}, u32[]{:S(2)}, u32[]{:S(2)}) collective-permute-start(bf16[128,1024]{1,0:T(8,128)(2,1)S(1)} %join.1.refs_8_.refs_2_), channel_id=1, source_target_pairs={{0,2},{1,3},{2,0},{3,1},{4,6},{5,7},{6,4},{7,5},{8,10},{9,11},{10,... | collective-permute-start | bytes 786440 | tf_op jit(solution)/shard_map/ppermute | solution.py:529
  10.7 2.6 %collective-permute-start.3 = (bf16[128,1024]{1,0:T(8,128)(2,1)S(1)}, bf16[128,1024]{1,0:T(8,128)(2,1)S(1)}, u32[]{:S(2)}, u32[]{:S(2)}) collective-permute-start(bf16[128,1024]{1,0:T(8,128)(2,1)S(1)} %join.1.refs_8_.refs_2_), channel_id=1, source_target_pairs={{0,16},{4,20},{8,24},{12,28},{16,0},{20,4},{24,8},{28,12},{1,17},{... | collective-permute-start | bytes 786440 | tf_op jit(solution)/shard_map/ppermute | solution.py:529
  13.3 0.0 collective-permute-done.refs_7_
  13.3 3.7 %front.1 = (f32[256,1024]{1,0:T(8,128)S(1)}, f32[256,256]{1,0:T(8,128)S(1)}, f32[2,16,256]{2,1,0:T(8,128)S(1)}, f32[136,512]{1,0:T(8,128)S(1)}, s16[144,512]{1,0:T(8,128)(2,1)S(1)}) custom-call(bf16[256,1024]{1,0:T(8,128)(2,1)} %refs_0_.5, bf16[256,128]{1,0:T(8,128)(2,1)} %refs_1_.5, bf16[256,128]{1,0:T(8,128)(2,1)} %refs_2_.3, f32[4,1024]{1,0:T(4,128)} %refs_3_.3, ...), custom_call_target="tpu_custom_call" | custom-call | flops 5000000000 | bytes 2503168 | tf_op jit(solution)/shard_map/front/pallas_call | solution.py:126
  17.0 1.2 %collective-permute-start.2 = (s16[144,512]{1,0:T(8,128)(2,1)S(1)}, s16[144,512]{1,0:T(8,128)(2,1)S(1)}, u32[]{:S(2)}, u32[]{:S(2)}) collective-permute-start(s16[144,512]{1,0:T(8,128)(2,1)S(1)} %get-tuple-element.32), channel_id=1, source_target_pairs={{0,4},{4,0},{8,12},{12,8},{16,20},{20,16},{24,28},{28,24},{1,5},{5... | collective-permute-start | bytes 442376 | tf_op jit(solution)/shard_map/ppermute | solution.py:529
  18.2 0.5 collective-permute-start.6
  18.7 4.0 %inner.1 = (f32[256,1024]{1,0:T(8,128)S(1)}, f32[256,1024]{1,0:T(8,128)S(1)}, f32[1,1024]{1,0:T(1,128)S(1)}) custom-call(f32[1,16]{1,0:T(1,128)} %bitcast.9, f32[1,1024]{1,0:T(1,128)} %bitcast.7, f32[256,1024]{1,0:T(8,128)S(1)} %get-tuple-element.25.refs_2_, f32[256,256]{1,0:T(8,128)S(1)} %get-tuple-element.26.refs_3_, ...), custom_call_target="tpu_custom_call" | custom-call | flops 4000000000 | bytes 3448896 | tf_op jit(solution)/shard_map/inner/pallas_call | solution.py:126
  22.7 1.1 %collective-permute-done.3.refs_2_ = bf16[128,1024]{1,0:T(8,128)(2,1)S(1)} collective-permute-done((bf16[128,1024]{1,0:T(8,128)(2,1)S(1)}, bf16[128,1024]{1,0:T(8,128)(2,1)S(1)}, u32[]{:S(2)}, u32[]{:S(2)}) %collective-permute-start.3) | collective-permute-done | bytes 262176 | tf_op jit(solution)/shard_map/ppermute | solution.py:529
  23.8 0.7 %collective-permute-done.6.refs_4_.refs_5_ = bf16[128,1024]{1,0:T(8,128)(2,1)S(1)} collective-permute-done((bf16[128,1024]{1,0:T(8,128)(2,1)S(1)}, bf16[128,1024]{1,0:T(8,128)(2,1)S(1)}, u32[]{:S(2)}, u32[]{:S(2)}) %collective-permute-start.6) | collective-permute-done | bytes 262176 | tf_op jit(solution)/shard_map/ppermute | solution.py:529
  24.6 0.2 pair.1
  24.7 1.0 %collective-permute-start.8 = (bf16[128,1024]{1,0:T(8,128)(2,1)S(1)}, bf16[128,1024]{1,0:T(8,128)(2,1)S(1)}, u32[]{:S(2)}, u32[]{:S(2)}) collective-permute-start(bf16[128,1024]{1,0:T(8,128)(2,1)S(1)} %get-tuple-element.35.refs_6_.refs_2_), channel_id=1, source_target_pairs={{0,4},{4,0},{8,12},{12,8},{16,20},{20,16},{24,28},{28,24},{1,5},{5... | collective-permute-start | bytes 786440 | tf_op jit(solution)/shard_map/ppermute | solution.py:529
  25.7 0.5 collective-permute-start.9
  26.2 1.6 %collective-permute-start.7 = (s16[144,512]{1,0:T(8,128)(2,1)S(1)}, s16[144,512]{1,0:T(8,128)(2,1)S(1)}, u32[]{:S(2)}, u32[]{:S(2)}) collective-permute-start(s16[144,512]{1,0:T(8,128)(2,1)S(1)} %get-tuple-element.34), channel_id=1, source_target_pairs={{0,8},{4,12},{8,0},{12,4},{16,24},{20,28},{24,16},{28,20},{1,9},{5... | collective-permute-start | bytes 442376 | tf_op jit(solution)/shard_map/ppermute | solution.py:529
  27.8 3.6 %collective-permute-done.7.refs_1_.refs_3_ = s16[144,512]{1,0:T(8,128)(2,1)S(1)} collective-permute-done((s16[144,512]{1,0:T(8,128)(2,1)S(1)}, s16[144,512]{1,0:T(8,128)(2,1)S(1)}, u32[]{:S(2)}, u32[]{:S(2)}) %collective-permute-start.7) | collective-permute-done | bytes 147488 | tf_op jit(solution)/shard_map/ppermute | solution.py:529
  31.3 1.1 %collective-permute-done.9.refs_8_.refs_4_ = bf16[128,1024]{1,0:T(8,128)(2,1)S(1)} collective-permute-done((bf16[128,1024]{1,0:T(8,128)(2,1)S(1)}, bf16[128,1024]{1,0:T(8,128)(2,1)S(1)}, u32[]{:S(2)}, u32[]{:S(2)}) %collective-permute-start.9) | collective-permute-done | bytes 262176 | tf_op jit(solution)/shard_map/ppermute | solution.py:529
  32.5 0.3 four.1
  32.7 0.1 collective-permute-start.12
  32.8 0.5 collective-permute-start.14
  33.3 0.9 %collective-permute-start.10 = (s16[144,512]{1,0:T(8,128)(2,1)S(1)}, s16[144,512]{1,0:T(8,128)(2,1)S(1)}, u32[]{:S(2)}, u32[]{:S(2)}) collective-permute-start(s16[144,512]{1,0:T(8,128)(2,1)S(1)} %get-tuple-element.36), channel_id=1, source_target_pairs={{0,16},{4,20},{8,24},{12,28},{16,0},{20,4},{24,8},{28,12},{1,17},{... | collective-permute-start | bytes 442376 | tf_op jit(solution)/shard_map/ppermute | solution.py:529
  34.2 1.4 %collective-permute-start.11 = (bf16[128,1024]{1,0:T(8,128)(2,1)S(1)}, bf16[128,1024]{1,0:T(8,128)(2,1)S(1)}, u32[]{:S(2)}, u32[]{:S(2)}) collective-permute-start(bf16[128,1024]{1,0:T(8,128)(2,1)S(1)} %collective-permute-done.9.refs_8_.refs_4_), channel_id=1, source_target_pairs={{0,4},{4,0},{8,12},{12,8},{16,20},{20,16},{24,28},{28,24},{1,5},{5... | collective-permute-start | bytes 786440 | tf_op jit(solution)/shard_map/ppermute | solution.py:529
  35.6 5.7 %experts.2.refs_6_.refs_9_ = bf16[1,512,1024]{2,1,0:T(8,128)(2,1)} custom-call(bf16[1,4096,1024]{2,1,0:T(8,128)(2,1)S(1)} %bitcast.4, bf16[1,4096,1024]{2,1,0:T(8,128)(2,1)S(1)} %bitcast.6, bf16[128,1024]{1,0:T(8,128)(2,1)S(1)} %join.1.refs_8_.refs_2_, bf16[128,1024]{1,0:T(8,128)(2,1)S(1)} %collective-permute-done.5.refs_3_, ...), custom_call_target="tpu_custom_call" | custom-call | flops 4294967296 | bytes 19927040 | tf_op jit(solution)/shard_map/experts/pallas_call | solution.py:126
  41.3 1.9 %collective-permute-done.10.refs_4_ = s16[144,512]{1,0:T(8,128)(2,1)S(1)} collective-permute-done((s16[144,512]{1,0:T(8,128)(2,1)S(1)}, s16[144,512]{1,0:T(8,128)(2,1)S(1)}, u32[]{:S(2)}, u32[]{:S(2)}) %collective-permute-start.10) | collective-permute-done | bytes 147488 | tf_op jit(solution)/shard_map/ppermute | solution.py:529
  43.2 0.3 turn.1
  43.5 0.1 collective-permute-start.15
  43.6 0.8 %collective-permute-start.13 = (s16[144,512]{1,0:T(8,128)(2,1)S(1)}, s16[144,512]{1,0:T(8,128)(2,1)S(1)}, u32[]{:S(2)}, u32[]{:S(2)}) collective-permute-start(s16[144,512]{1,0:T(8,128)(2,1)S(1)} %get-tuple-element.40), channel_id=1, source_target_pairs={{0,4},{4,0},{8,12},{12,8},{16,20},{20,16},{24,28},{28,24},{1,5},{5... | collective-permute-start | bytes 442376 | tf_op jit(solution)/shard_map/ppermute | solution.py:529
  44.4 0.7 %collective-permute-done.15.refs_7_ = bf16[128,1024]{1,0:T(8,128)(2,1)S(1)} collective-permute-done((bf16[128,1024]{1,0:T(8,128)(2,1)S(1)}, bf16[128,1024]{1,0:T(8,128)(2,1)S(1)}, u32[]{:S(2)}, u32[]{:S(2)}) %collective-permute-start.15) | collective-permute-done | bytes 262176 | tf_op jit(solution)/shard_map/ppermute | solution.py:529
  45.1 5.9 %experts.3.refs_6_ = bf16[1,512,1024]{2,1,0:T(8,128)(2,1)} custom-call(bf16[1,4096,1024]{2,1,0:T(8,128)(2,1)S(1)} %bitcast.4, bf16[1,4096,1024]{2,1,0:T(8,128)(2,1)S(1)} %bitcast.6, bf16[128,1024]{1,0:T(8,128)(2,1)S(1)} %get-tuple-element.35.refs_6_.refs_2_, ...), custom_call_target="tpu_custom_call", output_to_operand_aliasing={{}: (9, {})} | custom-call | flops 4294967296 | bytes 20975616 | tf_op jit(solution)/shard_map/experts/pallas_call | solution.py:126
  51.0 2.5 %back.1 = bf16[256,1024]{1,0:T(8,128)(2,1)} custom-call(f32[1,1024]{1,0:T(1,128)S(1)} %get-tuple-element.28.refs_0_, f32[256,1024]{1,0:T(8,128)S(1)} %get-tuple-element.29.refs_5_.refs_1_, f32[256,1024]{1,0:T(8,128)S(1)} %get-tuple-element.30.refs_2_, f32[256,256]{1,0:T(8,128)S(1)} %get-tuple-element.26.refs_3_, f32[128,512]{1,0:T(8,128)S(1)} %get-tuple-element.39.refs_4_, ...), custom_call_target="tpu_custom_call" | custom-call | flops 1000000000 | bytes 3297280 | tf_op jit(solution)/shard_map/back/pallas_call | solution.py:126
  (20 shorter events, 0.1 us)
Async XLA Ops:
  0.6 7.5 %collective-permute-start.1 = (bf16[64,1024]{1,0:T(8,128)(2,1)}, bf16[64,1024]{1,0:T(8,128)(2,1)S(1)}, u32[]{:S(2)}, u32[]{:S(2)}) collective-permute-start(bf16[64,1024]{1,0:T(8,128)(2,1)} %refs_3_.2), channel_id=1, source_target_pairs={{0,8},{4,12},{8,0},{12,4},{16,24},{20,28},{24,16},{28,20},{1,9},{5... | collective-permute-start | bytes 393224 | tf_op jit(solution)/shard_map/ppermute | solution.py:529
  4.7 8.5 %collective-permute-start = (bf16[16,1280]{1,0:T(8,128)(2,1)S(1)}, bf16[16,1280]{1,0:T(8,128)(2,1)S(1)}, u32[]{:S(2)}, u32[]{:S(2)}) collective-permute-start(bf16[16,1280]{1,0:T(8,128)(2,1)S(1)} %get-tuple-element.23), channel_id=1, source_target_pairs={{0,4},{4,8},{8,12},{12,16},{16,20},{20,24},{24,28},{1,5},{5,9},{9,... | collective-permute-start | bytes 122888 | tf_op jit(solution)/shard_map/ppermute | solution.py:670
  8.2 10.0 %collective-permute-start.5 = (bf16[128,1024]{1,0:T(8,128)(2,1)S(1)}, bf16[128,1024]{1,0:T(8,128)(2,1)S(1)}, u32[]{:S(2)}, u32[]{:S(2)}) collective-permute-start(bf16[128,1024]{1,0:T(8,128)(2,1)S(1)} %join.1.refs_8_.refs_2_), channel_id=1, source_target_pairs={{0,4},{4,0},{8,12},{12,8},{16,20},{20,16},{24,28},{28,24},{1,5},{5... | collective-permute-start | bytes 786440 | tf_op jit(solution)/shard_map/ppermute | solution.py:529
  9.2 13.5 %collective-permute-start.4 = (bf16[128,1024]{1,0:T(8,128)(2,1)S(1)}, bf16[128,1024]{1,0:T(8,128)(2,1)S(1)}, u32[]{:S(2)}, u32[]{:S(2)}) collective-permute-start(bf16[128,1024]{1,0:T(8,128)(2,1)S(1)} %join.1.refs_8_.refs_2_), channel_id=1, source_target_pairs={{0,2},{1,3},{2,0},{3,1},{4,6},{5,7},{6,4},{7,5},{8,10},{9,11},{10,... | collective-permute-start | bytes 786440 | tf_op jit(solution)/shard_map/ppermute | solution.py:529
  10.7 13.1 %collective-permute-start.3 = (bf16[128,1024]{1,0:T(8,128)(2,1)S(1)}, bf16[128,1024]{1,0:T(8,128)(2,1)S(1)}, u32[]{:S(2)}, u32[]{:S(2)}) collective-permute-start(bf16[128,1024]{1,0:T(8,128)(2,1)S(1)} %join.1.refs_8_.refs_2_), channel_id=1, source_target_pairs={{0,16},{4,20},{8,24},{12,28},{16,0},{20,4},{24,8},{28,12},{1,17},{... | collective-permute-start | bytes 786440 | tf_op jit(solution)/shard_map/ppermute | solution.py:529
  13.3 22.3 %slice-start.2 = ((s8[8388608]{0:T(1024)(128)(4,1)}), s8[4194304]{0:T(1024)(128)(4,1)S(1)}, s32[]{:S(2)}) async-start(s8[8388608]{0:T(1024)(128)(4,1)} %bitcast.5), calls=%async_computation.2 | async-start | bytes 8388608
  17.0 5.7 %collective-permute-start.2 = (s16[144,512]{1,0:T(8,128)(2,1)S(1)}, s16[144,512]{1,0:T(8,128)(2,1)S(1)}, u32[]{:S(2)}, u32[]{:S(2)}) collective-permute-start(s16[144,512]{1,0:T(8,128)(2,1)S(1)} %get-tuple-element.32), channel_id=1, source_target_pairs={{0,4},{4,0},{8,12},{12,8},{16,20},{20,16},{24,28},{28,24},{1,5},{5... | collective-permute-start | bytes 442376 | tf_op jit(solution)/shard_map/ppermute | solution.py:529
  18.2 6.4 %collective-permute-start.6 = (bf16[128,1024]{1,0:T(8,128)(2,1)S(1)}, bf16[128,1024]{1,0:T(8,128)(2,1)S(1)}, u32[]{:S(2)}, u32[]{:S(2)}) collective-permute-start(bf16[128,1024]{1,0:T(8,128)(2,1)S(1)} %collective-permute-done.5.refs_3_), channel_id=1, source_target_pairs={{0,2},{1,3},{2,0},{3,1},{4,6},{5,7},{6,4},{7,5},{8,10},{9,11},{10,... | collective-permute-start | bytes 786440 | tf_op jit(solution)/shard_map/ppermute | solution.py:529
  18.7 16.8 %slice-start = ((s8[8388608]{0:T(1024)(128)(4,1)}), s8[4194304]{0:T(1024)(128)(4,1)S(1)}, s32[]{:S(2)}) async-start(s8[8388608]{0:T(1024)(128)(4,1)} %bitcast.3), calls=%async_computation | async-start | bytes 8388608
  18.7 16.9 %slice-start.1 = ((s8[8388608]{0:T(1024)(128)(4,1)}), s8[4194304]{0:T(1024)(128)(4,1)S(1)}, s32[]{:S(2)}) async-start(s8[8388608]{0:T(1024)(128)(4,1)} %bitcast.3), calls=%async_computation.1 | async-start | bytes 8388608
  18.7 16.9 %slice-start.3 = ((s8[8388608]{0:T(1024)(128)(4,1)}), s8[4194304]{0:T(1024)(128)(4,1)S(1)}, s32[]{:S(2)}) async-start(s8[8388608]{0:T(1024)(128)(4,1)} %bitcast.5), calls=%async_computation.3 | async-start | bytes 8388608
  24.7 6.6 %collective-permute-start.8 = (bf16[128,1024]{1,0:T(8,128)(2,1)S(1)}, bf16[128,1024]{1,0:T(8,128)(2,1)S(1)}, u32[]{:S(2)}, u32[]{:S(2)}) collective-permute-start(bf16[128,1024]{1,0:T(8,128)(2,1)S(1)} %get-tuple-element.35.refs_6_.refs_2_), channel_id=1, source_target_pairs={{0,4},{4,0},{8,12},{12,8},{16,20},{20,16},{24,28},{28,24},{1,5},{5... | collective-permute-start | bytes 786440 | tf_op jit(solution)/shard_map/ppermute | solution.py:529
  25.7 6.8 %collective-permute-start.9 = (bf16[128,1024]{1,0:T(8,128)(2,1)S(1)}, bf16[128,1024]{1,0:T(8,128)(2,1)S(1)}, u32[]{:S(2)}, u32[]{:S(2)}) collective-permute-start(bf16[128,1024]{1,0:T(8,128)(2,1)S(1)} %get-tuple-element.35.refs_6_.refs_2_), channel_id=1, source_target_pairs={{0,2},{1,3},{2,0},{3,1},{4,6},{5,7},{6,4},{7,5},{8,10},{9,11},{10,... | collective-permute-start | bytes 786440 | tf_op jit(solution)/shard_map/ppermute | solution.py:529
  26.2 5.1 %collective-permute-start.7 = (s16[144,512]{1,0:T(8,128)(2,1)S(1)}, s16[144,512]{1,0:T(8,128)(2,1)S(1)}, u32[]{:S(2)}, u32[]{:S(2)}) collective-permute-start(s16[144,512]{1,0:T(8,128)(2,1)S(1)} %get-tuple-element.34), channel_id=1, source_target_pairs={{0,8},{4,12},{8,0},{12,4},{16,24},{20,28},{24,16},{28,20},{1,9},{5... | collective-permute-start | bytes 442376 | tf_op jit(solution)/shard_map/ppermute | solution.py:529
  32.7 2.8 %collective-permute-start.12 = (bf16[512,1024]{1,0:T(8,128)(2,1)S(1)}, bf16[512,1024]{1,0:T(8,128)(2,1)S(1)}, u32[]{:S(2)}, u32[]{:S(2)}) collective-permute-start(bf16[512,1024]{1,0:T(8,128)(2,1)S(1)} %get-tuple-element.37), channel_id=1, source_target_pairs={{0,1},{1,0},{2,3},{3,2},{4,5},{5,4},{6,7},{7,6},{8,9},{9,8},{10,11... | collective-permute-start | bytes 3145736 | tf_op jit(solution)/shard_map/ppermute | solution.py:529
  32.8 11.6 %collective-permute-start.14 = (bf16[384,1024]{1,0:T(8,128)(2,1)S(1)}, bf16[384,1024]{1,0:T(8,128)(2,1)S(1)}, u32[]{:S(2)}, u32[]{:S(2)}) collective-permute-start(bf16[384,1024]{1,0:T(8,128)(2,1)S(1)} %get-tuple-element.41), channel_id=1, source_target_pairs={{0,1},{1,0},{2,3},{3,2},{4,5},{5,4},{6,7},{7,6},{8,9},{9,8},{10,11... | collective-permute-start | bytes 2359304 | tf_op jit(solution)/shard_map/ppermute | solution.py:529
  33.3 9.9 %collective-permute-start.10 = (s16[144,512]{1,0:T(8,128)(2,1)S(1)}, s16[144,512]{1,0:T(8,128)(2,1)S(1)}, u32[]{:S(2)}, u32[]{:S(2)}) collective-permute-start(s16[144,512]{1,0:T(8,128)(2,1)S(1)} %get-tuple-element.36), channel_id=1, source_target_pairs={{0,16},{4,20},{8,24},{12,28},{16,0},{20,4},{24,8},{28,12},{1,17},{... | collective-permute-start | bytes 442376 | tf_op jit(solution)/shard_map/ppermute | solution.py:529
  34.2 9.0 %collective-permute-start.11 = (bf16[128,1024]{1,0:T(8,128)(2,1)S(1)}, bf16[128,1024]{1,0:T(8,128)(2,1)S(1)}, u32[]{:S(2)}, u32[]{:S(2)}) collective-permute-start(bf16[128,1024]{1,0:T(8,128)(2,1)S(1)} %collective-permute-done.9.refs_8_.refs_4_), channel_id=1, source_target_pairs={{0,4},{4,0},{8,12},{12,8},{16,20},{20,16},{24,28},{28,24},{1,5},{5... | collective-permute-start | bytes 786440 | tf_op jit(solution)/shard_map/ppermute | solution.py:529
  43.5 1.6 %collective-permute-start.15 = (bf16[128,1024]{1,0:T(8,128)(2,1)S(1)}, bf16[128,1024]{1,0:T(8,128)(2,1)S(1)}, u32[]{:S(2)}, u32[]{:S(2)}) collective-permute-start(bf16[128,1024]{1,0:T(8,128)(2,1)S(1)} %get-tuple-element.42), channel_id=1, source_target_pairs={{0,1},{1,0},{2,3},{3,2},{4,5},{5,4},{6,7},{7,6},{8,9},{9,8},{10,11... | collective-permute-start | bytes 786440 | tf_op jit(solution)/shard_map/ppermute | solution.py:529
  43.6 7.4 %collective-permute-start.13 = (s16[144,512]{1,0:T(8,128)(2,1)S(1)}, s16[144,512]{1,0:T(8,128)(2,1)S(1)}, u32[]{:S(2)}, u32[]{:S(2)}) collective-permute-start(s16[144,512]{1,0:T(8,128)(2,1)S(1)} %get-tuple-element.40), channel_id=1, source_target_pairs={{0,4},{4,0},{8,12},{12,8},{16,20},{20,16},{24,28},{28,24},{1,5},{5... | collective-permute-start | bytes 442376 | tf_op jit(solution)/shard_map/ppermute | solution.py:529

commit v19 on v18

--- a/solution.py
+++ b/solution.py
@@ -518,7 +518,7 @@
     return finish, late
 
 
-TILE = 512
+TILE = 1024
 
 
 def join_body(a, b, joined_ref):

time: 53.8 us -> 53.4 us (level)
  transfers between devices with their start and end apart: 16 -> 16, of which waited for: 6 -> 6; matrix products, arithmetic and copies ran while one was open for 0% -> 0% of each run, Pallas kernels for 39% -> 38%
where the time goes in v19:
time: 53.4 us; the launch traced here: 53.2 us
  Pallas kernels  23.2 us (43%)
  starting transfers between devices  20 us (37%)
  waiting for transfers between devices  9.22 us (17%)
  between operations  0.8 us (1%)
    pallas_call x10, Pallas kernels, call(): pl.pallas_call(body, out_shape=outs, in_specs=[pl.BlockSpec(memory_space=...  23.2 us
    ppermute x15, starting transfers between devices, swapped(): lax.ppermute(block, axis, [(i, i ^ bit) for i in range(lax.axis_size(axis...  16.6 us
    ppermute x15, waiting for transfers between devices, swapped(): lax.ppermute(block, axis, [(i, i ^ bit) for i in range(lax.axis_size(axis...  9.22 us
    ppermute x1, starting transfers between devices, on_device(): before = lax.ppermute(ends, 'ctx', [(i, i + 1) for i in range(ctx - 1)])  3.4 us
  transfers between devices with their start and end apart: 16, of which 6 were waited for; matrix products, arithmetic and copies ran while one was open for 0% of the time, Pallas kernels for 38%

profile of v19, /device:TPU:0, one launch (start us, length us, event | category | flops | bytes accessed | tf_op | source)
XLA Modules:
  0.0 53.2 jit_solution(992316830805811841)
XLA Ops:
  0.6 3.1 %collective-permute-start.1 = (bf16[64,1024]{1,0:T(8,128)(2,1)}, bf16[64,1024]{1,0:T(8,128)(2,1)S(1)}, u32[]{:S(2)}, u32[]{:S(2)}) collective-permute-start(bf16[64,1024]{1,0:T(8,128)(2,1)} %refs_3_.2), channel_id=1, source_target_pairs={{0,8},{4,12},{8,0},{12,4},{16,24},{20,28},{24,16},{28,20},{1,9},{5... | collective-permute-start | bytes 393224 | tf_op jit(solution)/shard_map/ppermute | solution.py:529
  3.7 1.0 %ends.1 = (bf16[16,1280]{1,0:T(8,128)(2,1)S(1)}, bf16[64,1024]{1,0:T(8,128)(2,1)S(1)}) custom-call(bf16[256,1024]{1,0:T(8,128)(2,1)} %refs_0_.5, bf16[256,128]{1,0:T(8,128)(2,1)} %refs_1_.5, bf16[256,128]{1,0:T(8,128)(2,1)} %refs_2_.3, bf16[64,1024]{1,0:T(8,128)(2,1)} %refs_3_.2), custom_call_target="tpu_custom_call" | custom-call | bytes 958464 | tf_op jit(solution)/shard_map/ends/pallas_call | solution.py:126
  4.7 3.4 %collective-permute-start = (bf16[16,1280]{1,0:T(8,128)(2,1)S(1)}, bf16[16,1280]{1,0:T(8,128)(2,1)S(1)}, u32[]{:S(2)}, u32[]{:S(2)}) collective-permute-start(bf16[16,1280]{1,0:T(8,128)(2,1)S(1)} %get-tuple-element.23), channel_id=1, source_target_pairs={{0,4},{4,8},{8,12},{12,16},{16,20},{20,24},{24,28},{1,5},{5,9},{9,... | collective-permute-start | bytes 122888 | tf_op jit(solution)/shard_map/ppermute | solution.py:670
  8.1 0.0 collective-permute-done.1.refs_1_
  8.2 1.0 %collective-permute-start.5 = (bf16[128,1024]{1,0:T(8,128)(2,1)S(1)}, bf16[128,1024]{1,0:T(8,128)(2,1)S(1)}, u32[]{:S(2)}, u32[]{:S(2)}) collective-permute-start(bf16[128,1024]{1,0:T(8,128)(2,1)S(1)} %join.1.refs_8_.refs_2_), channel_id=1, source_target_pairs={{0,4},{4,0},{8,12},{12,8},{16,20},{20,16},{24,28},{28,24},{1,5},{5... | collective-permute-start | bytes 786440 | tf_op jit(solution)/shard_map/ppermute | solution.py:529
  9.2 1.5 %collective-permute-start.4 = (bf16[128,1024]{1,0:T(8,128)(2,1)S(1)}, bf16[128,1024]{1,0:T(8,128)(2,1)S(1)}, u32[]{:S(2)}, u32[]{:S(2)}) collective-permute-start(bf16[128,1024]{1,0:T(8,128)(2,1)S(1)} %join.1.refs_8_.refs_2_), channel_id=1, source_target_pairs={{0,2},{1,3},{2,0},{3,1},{4,6},{5,7},{6,4},{7,5},{8,10},{9,11},{10,... | collective-permute-start | bytes 786440 | tf_op jit(solution)/shard_map/ppermute | solution.py:529
  10.7 2.6 %collective-permute-start.3 = (bf16[128,1024]{1,0:T(8,128)(2,1)S(1)}, bf16[128,1024]{1,0:T(8,128)(2,1)S(1)}, u32[]{:S(2)}, u32[]{:S(2)}) collective-permute-start(bf16[128,1024]{1,0:T(8,128)(2,1)S(1)} %join.1.refs_8_.refs_2_), channel_id=1, source_target_pairs={{0,16},{4,20},{8,24},{12,28},{16,0},{20,4},{24,8},{28,12},{1,17},{... | collective-permute-start | bytes 786440 | tf_op jit(solution)/shard_map/ppermute | solution.py:529
  13.3 3.7 %front.1 = (f32[256,1024]{1,0:T(8,128)S(1)}, f32[256,256]{1,0:T(8,128)S(1)}, f32[2,16,256]{2,1,0:T(8,128)S(1)}, f32[136,512]{1,0:T(8,128)S(1)}, s16[144,512]{1,0:T(8,128)(2,1)S(1)}) custom-call(bf16[256,1024]{1,0:T(8,128)(2,1)} %refs_0_.5, bf16[256,128]{1,0:T(8,128)(2,1)} %refs_1_.5, bf16[256,128]{1,0:T(8,128)(2,1)} %refs_2_.3, f32[4,1024]{1,0:T(4,128)} %refs_3_.3, ...), custom_call_target="tpu_custom_call" | custom-call | flops 5000000000 | bytes 2503168 | tf_op jit(solution)/shard_map/front/pallas_call | solution.py:126
  17.0 1.2 %collective-permute-start.2 = (s16[144,512]{1,0:T(8,128)(2,1)S(1)}, s16[144,512]{1,0:T(8,128)(2,1)S(1)}, u32[]{:S(2)}, u32[]{:S(2)}) collective-permute-start(s16[144,512]{1,0:T(8,128)(2,1)S(1)} %get-tuple-element.32), channel_id=1, source_target_pairs={{0,4},{4,0},{8,12},{12,8},{16,20},{20,16},{24,28},{28,24},{1,5},{5... | collective-permute-start | bytes 442376 | tf_op jit(solution)/shard_map/ppermute | solution.py:529
  18.2 0.5 collective-permute-start.6
  18.7 4.0 %inner.1 = (f32[256,1024]{1,0:T(8,128)S(1)}, f32[256,1024]{1,0:T(8,128)S(1)}, f32[1,1024]{1,0:T(1,128)S(1)}) custom-call(f32[1,16]{1,0:T(1,128)} %bitcast.9, f32[1,1024]{1,0:T(1,128)} %bitcast.7, f32[256,1024]{1,0:T(8,128)S(1)} %get-tuple-element.25.refs_2_, f32[256,256]{1,0:T(8,128)S(1)} %get-tuple-element.26.refs_3_, ...), custom_call_target="tpu_custom_call" | custom-call | flops 4000000000 | bytes 3448896 | tf_op jit(solution)/shard_map/inner/pallas_call | solution.py:126
  22.7 1.1 %collective-permute-done.3.refs_2_ = bf16[128,1024]{1,0:T(8,128)(2,1)S(1)} collective-permute-done((bf16[128,1024]{1,0:T(8,128)(2,1)S(1)}, bf16[128,1024]{1,0:T(8,128)(2,1)S(1)}, u32[]{:S(2)}, u32[]{:S(2)}) %collective-permute-start.3) | collective-permute-done | bytes 262176 | tf_op jit(solution)/shard_map/ppermute | solution.py:529
  23.8 0.7 %collective-permute-done.6.refs_4_.refs_5_ = bf16[128,1024]{1,0:T(8,128)(2,1)S(1)} collective-permute-done((bf16[128,1024]{1,0:T(8,128)(2,1)S(1)}, bf16[128,1024]{1,0:T(8,128)(2,1)S(1)}, u32[]{:S(2)}, u32[]{:S(2)}) %collective-permute-start.6) | collective-permute-done | bytes 262176 | tf_op jit(solution)/shard_map/ppermute | solution.py:529
  24.6 0.2 pair.1
  24.7 1.0 %collective-permute-start.8 = (bf16[128,1024]{1,0:T(8,128)(2,1)S(1)}, bf16[128,1024]{1,0:T(8,128)(2,1)S(1)}, u32[]{:S(2)}, u32[]{:S(2)}) collective-permute-start(bf16[128,1024]{1,0:T(8,128)(2,1)S(1)} %get-tuple-element.35.refs_6_.refs_2_), channel_id=1, source_target_pairs={{0,4},{4,0},{8,12},{12,8},{16,20},{20,16},{24,28},{28,24},{1,5},{5... | collective-permute-start | bytes 786440 | tf_op jit(solution)/shard_map/ppermute | solution.py:529
  25.7 0.5 collective-permute-start.9
  26.2 1.6 %collective-permute-start.7 = (s16[144,512]{1,0:T(8,128)(2,1)S(1)}, s16[144,512]{1,0:T(8,128)(2,1)S(1)}, u32[]{:S(2)}, u32[]{:S(2)}) collective-permute-start(s16[144,512]{1,0:T(8,128)(2,1)S(1)} %get-tuple-element.34), channel_id=1, source_target_pairs={{0,8},{4,12},{8,0},{12,4},{16,24},{20,28},{24,16},{28,20},{1,9},{5... | collective-permute-start | bytes 442376 | tf_op jit(solution)/shard_map/ppermute | solution.py:529
  27.8 3.6 %collective-permute-done.7.refs_1_.refs_3_ = s16[144,512]{1,0:T(8,128)(2,1)S(1)} collective-permute-done((s16[144,512]{1,0:T(8,128)(2,1)S(1)}, s16[144,512]{1,0:T(8,128)(2,1)S(1)}, u32[]{:S(2)}, u32[]{:S(2)}) %collective-permute-start.7) | collective-permute-done | bytes 147488 | tf_op jit(solution)/shard_map/ppermute | solution.py:529
  31.3 1.1 %collective-permute-done.9.refs_8_.refs_4_ = bf16[128,1024]{1,0:T(8,128)(2,1)S(1)} collective-permute-done((bf16[128,1024]{1,0:T(8,128)(2,1)S(1)}, bf16[128,1024]{1,0:T(8,128)(2,1)S(1)}, u32[]{:S(2)}, u32[]{:S(2)}) %collective-permute-start.9) | collective-permute-done | bytes 262176 | tf_op jit(solution)/shard_map/ppermute | solution.py:529
  32.5 0.3 four.1
  32.7 0.1 collective-permute-start.12
  32.8 0.5 collective-permute-start.14
  33.3 0.9 %collective-permute-start.10 = (s16[144,512]{1,0:T(8,128)(2,1)S(1)}, s16[144,512]{1,0:T(8,128)(2,1)S(1)}, u32[]{:S(2)}, u32[]{:S(2)}) collective-permute-start(s16[144,512]{1,0:T(8,128)(2,1)S(1)} %get-tuple-element.36), channel_id=1, source_target_pairs={{0,16},{4,20},{8,24},{12,28},{16,0},{20,4},{24,8},{28,12},{1,17},{... | collective-permute-start | bytes 442376 | tf_op jit(solution)/shard_map/ppermute | solution.py:529
  34.1 1.4 %collective-permute-start.11 = (bf16[128,1024]{1,0:T(8,128)(2,1)S(1)}, bf16[128,1024]{1,0:T(8,128)(2,1)S(1)}, u32[]{:S(2)}, u32[]{:S(2)}) collective-permute-start(bf16[128,1024]{1,0:T(8,128)(2,1)S(1)} %collective-permute-done.9.refs_8_.refs_4_), channel_id=1, source_target_pairs={{0,4},{4,0},{8,12},{12,8},{16,20},{20,16},{24,28},{28,24},{1,5},{5... | collective-permute-start | bytes 786440 | tf_op jit(solution)/shard_map/ppermute | solution.py:529
  35.6 5.6 %experts.2.refs_6_.refs_9_ = bf16[1,512,1024]{2,1,0:T(8,128)(2,1)} custom-call(bf16[1,4096,1024]{2,1,0:T(8,128)(2,1)S(1)} %bitcast.4, bf16[1,4096,1024]{2,1,0:T(8,128)(2,1)S(1)} %bitcast.6, bf16[128,1024]{1,0:T(8,128)(2,1)S(1)} %join.1.refs_8_.refs_2_, bf16[128,1024]{1,0:T(8,128)(2,1)S(1)} %collective-permute-done.5.refs_3_, ...), custom_call_target="tpu_custom_call" | custom-call | flops 4294967296 | bytes 19927040 | tf_op jit(solution)/shard_map/experts/pallas_call | solution.py:126
  41.2 1.9 %collective-permute-done.10.refs_4_ = s16[144,512]{1,0:T(8,128)(2,1)S(1)} collective-permute-done((s16[144,512]{1,0:T(8,128)(2,1)S(1)}, s16[144,512]{1,0:T(8,128)(2,1)S(1)}, u32[]{:S(2)}, u32[]{:S(2)}) %collective-permute-start.10) | collective-permute-done | bytes 147488 | tf_op jit(solution)/shard_map/ppermute | solution.py:529
  43.2 0.3 turn.1
  43.5 0.1 collective-permute-start.15
  43.6 0.8 %collective-permute-start.13 = (s16[144,512]{1,0:T(8,128)(2,1)S(1)}, s16[144,512]{1,0:T(8,128)(2,1)S(1)}, u32[]{:S(2)}, u32[]{:S(2)}) collective-permute-start(s16[144,512]{1,0:T(8,128)(2,1)S(1)} %get-tuple-element.40), channel_id=1, source_target_pairs={{0,4},{4,0},{8,12},{12,8},{16,20},{20,16},{24,28},{28,24},{1,5},{5... | collective-permute-start | bytes 442376 | tf_op jit(solution)/shard_map/ppermute | solution.py:529
  44.4 0.7 %collective-permute-done.15.refs_7_ = bf16[128,1024]{1,0:T(8,128)(2,1)S(1)} collective-permute-done((bf16[128,1024]{1,0:T(8,128)(2,1)S(1)}, bf16[128,1024]{1,0:T(8,128)(2,1)S(1)}, u32[]{:S(2)}, u32[]{:S(2)}) %collective-permute-start.15) | collective-permute-done | bytes 262176 | tf_op jit(solution)/shard_map/ppermute | solution.py:529
  45.1 5.6 %experts.3.refs_6_ = bf16[1,512,1024]{2,1,0:T(8,128)(2,1)} custom-call(bf16[1,4096,1024]{2,1,0:T(8,128)(2,1)S(1)} %bitcast.4, bf16[1,4096,1024]{2,1,0:T(8,128)(2,1)S(1)} %bitcast.6, bf16[128,1024]{1,0:T(8,128)(2,1)S(1)} %get-tuple-element.35.refs_6_.refs_2_, ...), custom_call_target="tpu_custom_call", output_to_operand_aliasing={{}: (9, {})} | custom-call | flops 4294967296 | bytes 20975616 | tf_op jit(solution)/shard_map/experts/pallas_call | solution.py:126
  50.8 2.5 %back.1 = bf16[256,1024]{1,0:T(8,128)(2,1)} custom-call(f32[1,1024]{1,0:T(1,128)S(1)} %get-tuple-element.28.refs_0_, f32[256,1024]{1,0:T(8,128)S(1)} %get-tuple-element.29.refs_5_.refs_1_, f32[256,1024]{1,0:T(8,128)S(1)} %get-tuple-element.30.refs_2_, f32[256,256]{1,0:T(8,128)S(1)} %get-tuple-element.26.refs_3_, f32[128,512]{1,0:T(8,128)S(1)} %get-tuple-element.39.refs_4_, ...), custom_call_target="tpu_custom_call" | custom-call | flops 1000000000 | bytes 3297280 | tf_op jit(solution)/shard_map/back/pallas_call | solution.py:126
  (20 shorter events, 0.1 us)
Async XLA Ops:
  0.6 7.5 %collective-permute-start.1 = (bf16[64,1024]{1,0:T(8,128)(2,1)}, bf16[64,1024]{1,0:T(8,128)(2,1)S(1)}, u32[]{:S(2)}, u32[]{:S(2)}) collective-permute-start(bf16[64,1024]{1,0:T(8,128)(2,1)} %refs_3_.2), channel_id=1, source_target_pairs={{0,8},{4,12},{8,0},{12,4},{16,24},{20,28},{24,16},{28,20},{1,9},{5... | collective-permute-start | bytes 393224 | tf_op jit(solution)/shard_map/ppermute | solution.py:529
  4.7 8.5 %collective-permute-start = (bf16[16,1280]{1,0:T(8,128)(2,1)S(1)}, bf16[16,1280]{1,0:T(8,128)(2,1)S(1)}, u32[]{:S(2)}, u32[]{:S(2)}) collective-permute-start(bf16[16,1280]{1,0:T(8,128)(2,1)S(1)} %get-tuple-element.23), channel_id=1, source_target_pairs={{0,4},{4,8},{8,12},{12,16},{16,20},{20,24},{24,28},{1,5},{5,9},{9,... | collective-permute-start | bytes 122888 | tf_op jit(solution)/shard_map/ppermute | solution.py:670
  8.2 10.0 %collective-permute-start.5 = (bf16[128,1024]{1,0:T(8,128)(2,1)S(1)}, bf16[128,1024]{1,0:T(8,128)(2,1)S(1)}, u32[]{:S(2)}, u32[]{:S(2)}) collective-permute-start(bf16[128,1024]{1,0:T(8,128)(2,1)S(1)} %join.1.refs_8_.refs_2_), channel_id=1, source_target_pairs={{0,4},{4,0},{8,12},{12,8},{16,20},{20,16},{24,28},{28,24},{1,5},{5... | collective-permute-start | bytes 786440 | tf_op jit(solution)/shard_map/ppermute | solution.py:529
  9.2 13.5 %collective-permute-start.4 = (bf16[128,1024]{1,0:T(8,128)(2,1)S(1)}, bf16[128,1024]{1,0:T(8,128)(2,1)S(1)}, u32[]{:S(2)}, u32[]{:S(2)}) collective-permute-start(bf16[128,1024]{1,0:T(8,128)(2,1)S(1)} %join.1.refs_8_.refs_2_), channel_id=1, source_target_pairs={{0,2},{1,3},{2,0},{3,1},{4,6},{5,7},{6,4},{7,5},{8,10},{9,11},{10,... | collective-permute-start | bytes 786440 | tf_op jit(solution)/shard_map/ppermute | solution.py:529
  10.7 13.1 %collective-permute-start.3 = (bf16[128,1024]{1,0:T(8,128)(2,1)S(1)}, bf16[128,1024]{1,0:T(8,128)(2,1)S(1)}, u32[]{:S(2)}, u32[]{:S(2)}) collective-permute-start(bf16[128,1024]{1,0:T(8,128)(2,1)S(1)} %join.1.refs_8_.refs_2_), channel_id=1, source_target_pairs={{0,16},{4,20},{8,24},{12,28},{16,0},{20,4},{24,8},{28,12},{1,17},{... | collective-permute-start | bytes 786440 | tf_op jit(solution)/shard_map/ppermute | solution.py:529
  13.3 22.3 %slice-start.2 = ((s8[8388608]{0:T(1024)(128)(4,1)}), s8[4194304]{0:T(1024)(128)(4,1)S(1)}, s32[]{:S(2)}) async-start(s8[8388608]{0:T(1024)(128)(4,1)} %bitcast.5), calls=%async_computation.2 | async-start | bytes 8388608
  17.0 5.7 %collective-permute-start.2 = (s16[144,512]{1,0:T(8,128)(2,1)S(1)}, s16[144,512]{1,0:T(8,128)(2,1)S(1)}, u32[]{:S(2)}, u32[]{:S(2)}) collective-permute-start(s16[144,512]{1,0:T(8,128)(2,1)S(1)} %get-tuple-element.32), channel_id=1, source_target_pairs={{0,4},{4,0},{8,12},{12,8},{16,20},{20,16},{24,28},{28,24},{1,5},{5... | collective-permute-start | bytes 442376 | tf_op jit(solution)/shard_map/ppermute | solution.py:529
  18.2 6.4 %collective-permute-start.6 = (bf16[128,1024]{1,0:T(8,128)(2,1)S(1)}, bf16[128,1024]{1,0:T(8,128)(2,1)S(1)}, u32[]{:S(2)}, u32[]{:S(2)}) collective-permute-start(bf16[128,1024]{1,0:T(8,128)(2,1)S(1)} %collective-permute-done.5.refs_3_), channel_id=1, source_target_pairs={{0,2},{1,3},{2,0},{3,1},{4,6},{5,7},{6,4},{7,5},{8,10},{9,11},{10,... | collective-permute-start | bytes 786440 | tf_op jit(solution)/shard_map/ppermute | solution.py:529
  18.7 16.8 %slice-start = ((s8[8388608]{0:T(1024)(128)(4,1)}), s8[4194304]{0:T(1024)(128)(4,1)S(1)}, s32[]{:S(2)}) async-start(s8[8388608]{0:T(1024)(128)(4,1)} %bitcast.3), calls=%async_computation | async-start | bytes 8388608
  18.7 16.9 %slice-start.1 = ((s8[8388608]{0:T(1024)(128)(4,1)}), s8[4194304]{0:T(1024)(128)(4,1)S(1)}, s32[]{:S(2)}) async-start(s8[8388608]{0:T(1024)(128)(4,1)} %bitcast.3), calls=%async_computation.1 | async-start | bytes 8388608
  18.7 16.9 %slice-start.3 = ((s8[8388608]{0:T(1024)(128)(4,1)}), s8[4194304]{0:T(1024)(128)(4,1)S(1)}, s32[]{:S(2)}) async-start(s8[8388608]{0:T(1024)(128)(4,1)} %bitcast.5), calls=%async_computation.3 | async-start | bytes 8388608
  24.7 6.6 %collective-permute-start.8 = (bf16[128,1024]{1,0:T(8,128)(2,1)S(1)}, bf16[128,1024]{1,0:T(8,128)(2,1)S(1)}, u32[]{:S(2)}, u32[]{:S(2)}) collective-permute-start(bf16[128,1024]{1,0:T(8,128)(2,1)S(1)} %get-tuple-element.35.refs_6_.refs_2_), channel_id=1, source_target_pairs={{0,4},{4,0},{8,12},{12,8},{16,20},{20,16},{24,28},{28,24},{1,5},{5... | collective-permute-start | bytes 786440 | tf_op jit(solution)/shard_map/ppermute | solution.py:529
  25.7 6.8 %collective-permute-start.9 = (bf16[128,1024]{1,0:T(8,128)(2,1)S(1)}, bf16[128,1024]{1,0:T(8,128)(2,1)S(1)}, u32[]{:S(2)}, u32[]{:S(2)}) collective-permute-start(bf16[128,1024]{1,0:T(8,128)(2,1)S(1)} %get-tuple-element.35.refs_6_.refs_2_), channel_id=1, source_target_pairs={{0,2},{1,3},{2,0},{3,1},{4,6},{5,7},{6,4},{7,5},{8,10},{9,11},{10,... | collective-permute-start | bytes 786440 | tf_op jit(solution)/shard_map/ppermute | solution.py:529
  26.2 5.1 %collective-permute-start.7 = (s16[144,512]{1,0:T(8,128)(2,1)S(1)}, s16[144,512]{1,0:T(8,128)(2,1)S(1)}, u32[]{:S(2)}, u32[]{:S(2)}) collective-permute-start(s16[144,512]{1,0:T(8,128)(2,1)S(1)} %get-tuple-element.34), channel_id=1, source_target_pairs={{0,8},{4,12},{8,0},{12,4},{16,24},{20,28},{24,16},{28,20},{1,9},{5... | collective-permute-start | bytes 442376 | tf_op jit(solution)/shard_map/ppermute | solution.py:529
  32.7 2.8 %collective-permute-start.12 = (bf16[512,1024]{1,0:T(8,128)(2,1)S(1)}, bf16[512,1024]{1,0:T(8,128)(2,1)S(1)}, u32[]{:S(2)}, u32[]{:S(2)}) collective-permute-start(bf16[512,1024]{1,0:T(8,128)(2,1)S(1)} %get-tuple-element.37), channel_id=1, source_target_pairs={{0,1},{1,0},{2,3},{3,2},{4,5},{5,4},{6,7},{7,6},{8,9},{9,8},{10,11... | collective-permute-start | bytes 3145736 | tf_op jit(solution)/shard_map/ppermute | solution.py:529
  32.8 11.6 %collective-permute-start.14 = (bf16[384,1024]{1,0:T(8,128)(2,1)S(1)}, bf16[384,1024]{1,0:T(8,128)(2,1)S(1)}, u32[]{:S(2)}, u32[]{:S(2)}) collective-permute-start(bf16[384,1024]{1,0:T(8,128)(2,1)S(1)} %get-tuple-element.41), channel_id=1, source_target_pairs={{0,1},{1,0},{2,3},{3,2},{4,5},{5,4},{6,7},{7,6},{8,9},{9,8},{10,11... | collective-permute-start | bytes 2359304 | tf_op jit(solution)/shard_map/ppermute | solution.py:529
  33.3 9.9 %collective-permute-start.10 = (s16[144,512]{1,0:T(8,128)(2,1)S(1)}, s16[144,512]{1,0:T(8,128)(2,1)S(1)}, u32[]{:S(2)}, u32[]{:S(2)}) collective-permute-start(s16[144,512]{1,0:T(8,128)(2,1)S(1)} %get-tuple-element.36), channel_id=1, source_target_pairs={{0,16},{4,20},{8,24},{12,28},{16,0},{20,4},{24,8},{28,12},{1,17},{... | collective-permute-start | bytes 442376 | tf_op jit(solution)/shard_map/ppermute | solution.py:529
  34.1 9.0 %collective-permute-start.11 = (bf16[128,1024]{1,0:T(8,128)(2,1)S(1)}, bf16[128,1024]{1,0:T(8,128)(2,1)S(1)}, u32[]{:S(2)}, u32[]{:S(2)}) collective-permute-start(bf16[128,1024]{1,0:T(8,128)(2,1)S(1)} %collective-permute-done.9.refs_8_.refs_4_), channel_id=1, source_target_pairs={{0,4},{4,0},{8,12},{12,8},{16,20},{20,16},{24,28},{28,24},{1,5},{5... | collective-permute-start | bytes 786440 | tf_op jit(solution)/shard_map/ppermute | solution.py:529
  43.5 1.6 %collective-permute-start.15 = (bf16[128,1024]{1,0:T(8,128)(2,1)S(1)}, bf16[128,1024]{1,0:T(8,128)(2,1)S(1)}, u32[]{:S(2)}, u32[]{:S(2)}) collective-permute-start(bf16[128,1024]{1,0:T(8,128)(2,1)S(1)} %get-tuple-element.42), channel_id=1, source_target_pairs={{0,1},{1,0},{2,3},{3,2},{4,5},{5,4},{6,7},{7,6},{8,9},{9,8},{10,11... | collective-permute-start | bytes 786440 | tf_op jit(solution)/shard_map/ppermute | solution.py:529
  43.6 7.2 %collective-permute-start.13 = (s16[144,512]{1,0:T(8,128)(2,1)S(1)}, s16[144,512]{1,0:T(8,128)(2,1)S(1)}, u32[]{:S(2)}, u32[]{:S(2)}) collective-permute-start(s16[144,512]{1,0:T(8,128)(2,1)S(1)} %get-tuple-element.40), channel_id=1, source_target_pairs={{0,4},{4,0},{8,12},{12,8},{16,20},{20,16},{24,28},{28,24},{1,5},{5... | collective-permute-start | bytes 442376 | tf_op jit(solution)/shard_map/ppermute | solution.py:529

commit v20 on v19

--- a/solution.py
+++ b/solution.py
@@ -144,32 +144,30 @@
     return jax.ShapeDtypeStruct(shape, dtype)
 
 
-def ends_body(x_ref, b_ref, c_ref, rows_ref, ends_ref, held_ref, sems):
-    tokens, channels = x_ref.shape
+def ends_body(count, *refs):
+    far, ends_ref, near, sems = refs[:count], refs[count], refs[count + 1 : -1], refs[-1]
+    tokens, channels = far[0].shape
     cut = pl.ds(tokens - EDGE, EDGE)
     finished(
         started(
-            [x_ref.at[cut, :], b_ref.at[cut, :], c_ref.at[cut, :], rows_ref],
+            [*(a.at[cut, :] for a in far[:3]), *far],
             [
                 ends_ref.at[:, pl.ds(0, channels)],
                 ends_ref.at[:, pl.ds(channels, STATE)],
                 ends_ref.at[:, pl.ds(channels + STATE, STATE)],
-                held_ref,
+                *near,
             ],
             sems,
         )
     )
 
 
-def front_body(paired, count, *refs):
-    far, (xconv_ref, bc_ref, lines_ref), rest = refs[:count], refs[count : count + 3], refs[count + 3 :]
-    ends, rest = rest[: 1 + paired], rest[1 + paired :]
-    near, pad_ref, sems = rest[:count], rest[-2], rest[-1]
-    copies = started(far, near, sems)
-    x_ref, b_ref, c_ref, taps_ref, taps_bc_ref, logs_ref, ids_ref, ends_ref = near
+def front_body(paired, *refs):
+    x_ref, b_ref, c_ref, taps_ref, taps_bc_ref, logs_ref, ids_ref, ends_ref = refs[:8]
+    xconv_ref, bc_ref, lines_ref = refs[8:11]
+    ends, pad_ref = refs[11:-1], refs[-1]
     tokens, channels = x_ref.shape
     heads = logs_ref.shape[0]
-    finished(copies)
     pad_ref[0:8, :] = ends_ref[...].astype(F32)[EDGE - 8 : EDGE]
     pad_ref[8 : 8 + tokens, :channels] = x_ref[...].astype(F32)
     pad_ref[8 : 8 + tokens, channels : channels + STATE] = b_ref[...].astype(F32)
@@ -453,7 +451,7 @@
 ):
     tokens, channels = seq_input.shape
     heads = skip.shape[0]
-    width = 2 * ids.shape[0]
+    width = 2 * ids.shape[1]
     paired = rows is not None
     outs = [
         array((tokens, channels), F32),
@@ -465,16 +463,13 @@
         ends.append(array((STATE + 16, channels // 2), jnp.int16))
     else:
         ends = [array((STATE + NOTES, channels), F32)]
-    args = (seq_input, b_input, c_input, conv_x, conv_bc, log_decay, ids.T, before)
     xconv, bc, lines, *ends = call(
-        functools.partial(front_body, paired, len(args)),
+        functools.partial(front_body, paired),
         outs + ends,
-        args,
-        fixed=len(args) - 1,
-        near_outs=len(outs + ends),
+        (seq_input, b_input, c_input, conv_x, conv_bc, log_decay, ids, before),
+        near=True,
         after=rows[0][:1] if paired else (),
-        scratch=room(args) + [pltpu.VMEM((8 + tokens, channels + 2 * STATE), F32)],
-        sems=len(args),
+        scratch=[pltpu.VMEM((8 + tokens, channels + 2 * STATE), F32)],
         flops=5 * 10**9,
         grant=20,
         name="front",
@@ -658,15 +653,17 @@
     ctx = lax.axis_size("ctx")
     by_tokens = lax.axis_size("exp") == 4 and ctx == 8
     tokens, channels = seq_input.shape
-    ends, held = call(
-        ends_body,
-        [array((EDGE, channels + 2 * STATE), BF16), array(moe_input.shape, BF16)],
-        (seq_input, b_input, c_input, moe_input),
-        fixed=4,
-        near_outs=1,
-        sems=4,
+    far = (seq_input, b_input, c_input, moe_input, conv_x, conv_bc, log_decay, expert_ids.T)
+    ends, *near = call(
+        functools.partial(ends_body, len(far)),
+        [array((EDGE, channels + 2 * STATE), BF16)] + [array(a.shape, a.dtype) for a in far],
+        far,
+        fixed=len(far),
+        near_outs=len(far),
+        sems=3 + len(far),
         name="ends",
     )
+    seq_input, b_input, c_input, held, conv_x, conv_bc, log_decay, ids = near
     before = lax.ppermute(ends, "ctx", [(i, i + 1) for i in range(ctx - 1)])
     pieces = meanwhile = None
     if by_tokens:
@@ -688,7 +685,7 @@
         log_decay,
         skip_gain,
         norm_gain,
-        expert_ids,
+        ids,
     )
     if by_tokens:
         far_pieces, ids, joined, hidden = late

time: 53.4 us -> 54 us (1.011)
  starting transfers between devices: 20 us -> 23 us
  waiting for transfers between devices: 9.22 us -> 7.63 us
  Pallas kernels: 23.2 us -> 22.3 us
    ppermute x15, starting transfers between devices: 16.6 us -> 19.5 us  [swapped(): lax.ppermute(block, axis, [(i, i ^ bit) for i in range(lax.axis_size(axis...]
    ppermute x15, waiting for transfers between devices: 9.22 us -> 7.63 us  [swapped(): lax.ppermute(block, axis, [(i, i ^ bit) for i in range(lax.axis_size(axis...]
    pallas_call x10, Pallas kernels: 23.2 us -> 22.3 us  [call(): pl.pallas_call(body, out_shape=outs, in_specs=[pl.BlockSpec(memory_space=...]
  transfers between devices with their start and end apart: 16 -> 16, of which waited for: 6 -> 5; matrix products, arithmetic and copies ran while one was open for 0% -> 0% of each run, Pallas kernels for 38% -> 36%
where the time goes in v20:
time: 54 us; the launch traced here: 53.8 us
  starting transfers between devices  23 us (43%)
  Pallas kernels  22.3 us (41%)
  waiting for transfers between devices  7.63 us (14%)
  between operations  0.97 us (2%)
    pallas_call x10, Pallas kernels, call(): pl.pallas_call(body, out_shape=outs, in_specs=[pl.BlockSpec(memory_space=...  22.3 us
    ppermute x15, starting transfers between devices, swapped(): lax.ppermute(block, axis, [(i, i ^ bit) for i in range(lax.axis_size(axis...  19.5 us
    ppermute x15, waiting for transfers between devices, swapped(): lax.ppermute(block, axis, [(i, i ^ bit) for i in range(lax.axis_size(axis...  7.63 us
    ppermute x1, starting transfers between devices, on_device(): before = lax.ppermute(ends, 'ctx', [(i, i + 1) for i in range(ctx - 1)])  3.42 us
  transfers between devices with their start and end apart: 16, of which 5 were waited for; matrix products, arithmetic and copies ran while one was open for 0% of the time, Pallas kernels for 36%

profile of v20, /device:TPU:0, one launch (start us, length us, event | category | flops | bytes accessed | tf_op | source)
XLA Modules:
  0.0 53.8 jit_solution(5328259761698559666)
XLA Ops:
  0.6 3.1 %collective-permute-start.1 = (bf16[64,1024]{1,0:T(8,128)(2,1)}, bf16[64,1024]{1,0:T(8,128)(2,1)S(1)}, u32[]{:S(2)}, u32[]{:S(2)}) collective-permute-start(bf16[64,1024]{1,0:T(8,128)(2,1)} %refs_3_.1), channel_id=1, source_target_pairs={{0,8},{4,12},{8,0},{12,4},{16,24},{20,28},{24,16},{28,20},{1,9},{5... | collective-permute-start | bytes 393224 | tf_op jit(solution)/shard_map/ppermute | solution.py:524
  3.7 1.3 %ends.1 = (bf16[16,1280]{1,0:T(8,128)(2,1)S(1)}, bf16[256,1024]{1,0:T(8,128)(2,1)S(1)}, bf16[256,128]{1,0:T(8,128)(2,1)S(1)}, bf16[256,128]{1,0:T(8,128)(2,1)S(1...) custom-call(bf16[256,1024]{1,0:T(8,128)(2,1)} %refs_0_.3, ...), custom_call_target="tpu_custom_call" | custom-call | bytes 1688576 | tf_op jit(solution)/shard_map/ends/pallas_call | solution.py:126
  5.0 3.4 %collective-permute-start = (bf16[16,1280]{1,0:T(8,128)(2,1)S(1)}, bf16[16,1280]{1,0:T(8,128)(2,1)S(1)}, u32[]{:S(2)}, u32[]{:S(2)}) collective-permute-start(bf16[16,1280]{1,0:T(8,128)(2,1)S(1)} %get-tuple-element.37), channel_id=1, source_target_pairs={{0,4},{4,8},{8,12},{12,16},{16,20},{20,24},{24,28},{1,5},{5,9},{9,... | collective-permute-start | bytes 122888 | tf_op jit(solution)/shard_map/ppermute | solution.py:667
  8.4 0.0 collective-permute-done.1.refs_1_
  8.5 0.7 %collective-permute-start.5 = (bf16[128,1024]{1,0:T(8,128)(2,1)S(1)}, bf16[128,1024]{1,0:T(8,128)(2,1)S(1)}, u32[]{:S(2)}, u32[]{:S(2)}) collective-permute-start(bf16[128,1024]{1,0:T(8,128)(2,1)S(1)} %join.1.refs_8_.refs_2_), channel_id=1, source_target_pairs={{0,4},{4,0},{8,12},{12,8},{16,20},{20,16},{24,28},{28,24},{1,5},{5... | collective-permute-start | bytes 786440 | tf_op jit(solution)/shard_map/ppermute | solution.py:524
  9.2 1.5 %collective-permute-start.4 = (bf16[128,1024]{1,0:T(8,128)(2,1)S(1)}, bf16[128,1024]{1,0:T(8,128)(2,1)S(1)}, u32[]{:S(2)}, u32[]{:S(2)}) collective-permute-start(bf16[128,1024]{1,0:T(8,128)(2,1)S(1)} %join.1.refs_8_.refs_2_), channel_id=1, source_target_pairs={{0,2},{1,3},{2,0},{3,1},{4,6},{5,7},{6,4},{7,5},{8,10},{9,11},{10,... | collective-permute-start | bytes 786440 | tf_op jit(solution)/shard_map/ppermute | solution.py:524
  10.7 2.6 %collective-permute-start.3 = (bf16[128,1024]{1,0:T(8,128)(2,1)S(1)}, bf16[128,1024]{1,0:T(8,128)(2,1)S(1)}, u32[]{:S(2)}, u32[]{:S(2)}) collective-permute-start(bf16[128,1024]{1,0:T(8,128)(2,1)S(1)} %join.1.refs_8_.refs_2_), channel_id=1, source_target_pairs={{0,16},{4,20},{8,24},{12,28},{16,0},{20,4},{24,8},{28,12},{1,17},{... | collective-permute-start | bytes 786440 | tf_op jit(solution)/shard_map/ppermute | solution.py:524
  13.3 0.0 collective-permute-done.refs_7_
  13.3 2.4 %front.1 = (f32[256,1024]{1,0:T(8,128)S(1)}, f32[256,256]{1,0:T(8,128)S(1)}, f32[2,16,256]{2,1,0:T(8,128)S(1)}, f32[136,512]{1,0:T(8,128)S(1)}, s16[144,512]{1,0:T(8,128)(2,1)S(1)}) custom-call(bf16[256,1024]{1,0:T(8,128)(2,1)S(1)} %get-tuple-element.30.refs_0_, bf16[256,128]{1,0:T(8,128)(2,1)S(1)} %get-tuple-element.31.refs_1_, ...), custom_call_target="tpu_custom_call" | custom-call | flops 5000000000 | bytes 2503168 | tf_op jit(solution)/shard_map/front/pallas_call | solution.py:126
  15.7 1.4 %collective-permute-start.2 = (s16[144,512]{1,0:T(8,128)(2,1)S(1)}, s16[144,512]{1,0:T(8,128)(2,1)S(1)}, u32[]{:S(2)}, u32[]{:S(2)}) collective-permute-start(s16[144,512]{1,0:T(8,128)(2,1)S(1)} %get-tuple-element.46), channel_id=1, source_target_pairs={{0,4},{4,0},{8,12},{12,8},{16,20},{20,16},{24,28},{28,24},{1,5},{5... | collective-permute-start | bytes 442376 | tf_op jit(solution)/shard_map/ppermute | solution.py:524
  17.2 0.7 %collective-permute-start.6 = (bf16[128,1024]{1,0:T(8,128)(2,1)S(1)}, bf16[128,1024]{1,0:T(8,128)(2,1)S(1)}, u32[]{:S(2)}, u32[]{:S(2)}) collective-permute-start(bf16[128,1024]{1,0:T(8,128)(2,1)S(1)} %collective-permute-done.5.refs_3_), channel_id=1, source_target_pairs={{0,2},{1,3},{2,0},{3,1},{4,6},{5,7},{6,4},{7,5},{8,10},{9,11},{10,... | collective-permute-start | bytes 786440 | tf_op jit(solution)/shard_map/ppermute | solution.py:524
  17.9 3.9 %inner.1 = (f32[256,1024]{1,0:T(8,128)S(1)}, f32[256,1024]{1,0:T(8,128)S(1)}, f32[1,1024]{1,0:T(1,128)S(1)}) custom-call(f32[1,16]{1,0:T(1,128)} %bitcast.9, f32[1,1024]{1,0:T(1,128)} %bitcast.8, f32[256,1024]{1,0:T(8,128)S(1)} %get-tuple-element.39.refs_2_, f32[256,256]{1,0:T(8,128)S(1)} %get-tuple-element.40.refs_3_, ...), custom_call_target="tpu_custom_call" | custom-call | flops 4000000000 | bytes 3448896 | tf_op jit(solution)/shard_map/inner/pallas_call | solution.py:126
  21.8 2.1 %collective-permute-done.3.refs_2_ = bf16[128,1024]{1,0:T(8,128)(2,1)S(1)} collective-permute-done((bf16[128,1024]{1,0:T(8,128)(2,1)S(1)}, bf16[128,1024]{1,0:T(8,128)(2,1)S(1)}, u32[]{:S(2)}, u32[]{:S(2)}) %collective-permute-start.3) | collective-permute-done | bytes 262176 | tf_op jit(solution)/shard_map/ppermute | solution.py:524
  23.9 0.2 pair.1
  24.0 1.7 %collective-permute-start.8 = (bf16[128,1024]{1,0:T(8,128)(2,1)S(1)}, bf16[128,1024]{1,0:T(8,128)(2,1)S(1)}, u32[]{:S(2)}, u32[]{:S(2)}) collective-permute-start(bf16[128,1024]{1,0:T(8,128)(2,1)S(1)} %get-tuple-element.49.refs_6_.refs_2_), channel_id=1, source_target_pairs={{0,4},{4,0},{8,12},{12,8},{16,20},{20,16},{24,28},{28,24},{1,5},{5... | collective-permute-start | bytes 786440 | tf_op jit(solution)/shard_map/ppermute | solution.py:524
  25.7 0.5 collective-permute-start.9
  26.2 2.4 %collective-permute-start.7 = (s16[144,512]{1,0:T(8,128)(2,1)S(1)}, s16[144,512]{1,0:T(8,128)(2,1)S(1)}, u32[]{:S(2)}, u32[]{:S(2)}) collective-permute-start(s16[144,512]{1,0:T(8,128)(2,1)S(1)} %get-tuple-element.48), channel_id=1, source_target_pairs={{0,8},{4,12},{8,0},{12,4},{16,24},{20,28},{24,16},{28,20},{1,9},{5... | collective-permute-start | bytes 442376 | tf_op jit(solution)/shard_map/ppermute | solution.py:524
  28.6 3.1 %collective-permute-done.7.refs_1_.refs_3_ = s16[144,512]{1,0:T(8,128)(2,1)S(1)} collective-permute-done((s16[144,512]{1,0:T(8,128)(2,1)S(1)}, s16[144,512]{1,0:T(8,128)(2,1)S(1)}, u32[]{:S(2)}, u32[]{:S(2)}) %collective-permute-start.7) | collective-permute-done | bytes 147488 | tf_op jit(solution)/shard_map/ppermute | solution.py:524
  31.8 0.9 %collective-permute-done.9.refs_8_.refs_4_ = bf16[128,1024]{1,0:T(8,128)(2,1)S(1)} collective-permute-done((bf16[128,1024]{1,0:T(8,128)(2,1)S(1)}, bf16[128,1024]{1,0:T(8,128)(2,1)S(1)}, u32[]{:S(2)}, u32[]{:S(2)}) %collective-permute-start.9) | collective-permute-done | bytes 262176 | tf_op jit(solution)/shard_map/ppermute | solution.py:524
  32.7 0.3 four.1
  33.0 0.1 collective-permute-start.12
  33.0 0.5 collective-permute-start.14
  33.5 1.2 %collective-permute-start.10 = (s16[144,512]{1,0:T(8,128)(2,1)S(1)}, s16[144,512]{1,0:T(8,128)(2,1)S(1)}, u32[]{:S(2)}, u32[]{:S(2)}) collective-permute-start(s16[144,512]{1,0:T(8,128)(2,1)S(1)} %get-tuple-element.50), channel_id=1, source_target_pairs={{0,16},{4,20},{8,24},{12,28},{16,0},{20,4},{24,8},{28,12},{1,17},{... | collective-permute-start | bytes 442376 | tf_op jit(solution)/shard_map/ppermute | solution.py:524
  34.8 1.8 %collective-permute-start.11 = (bf16[128,1024]{1,0:T(8,128)(2,1)S(1)}, bf16[128,1024]{1,0:T(8,128)(2,1)S(1)}, u32[]{:S(2)}, u32[]{:S(2)}) collective-permute-start(bf16[128,1024]{1,0:T(8,128)(2,1)S(1)} %collective-permute-done.9.refs_8_.refs_4_), channel_id=1, source_target_pairs={{0,4},{4,0},{8,12},{12,8},{16,20},{20,16},{24,28},{28,24},{1,5},{5... | collective-permute-start | bytes 786440 | tf_op jit(solution)/shard_map/ppermute | solution.py:524
  36.6 5.6 %experts.2.refs_6_.refs_9_ = bf16[1,512,1024]{2,1,0:T(8,128)(2,1)} custom-call(bf16[1,4096,1024]{2,1,0:T(8,128)(2,1)S(1)} %bitcast.4, bf16[1,4096,1024]{2,1,0:T(8,128)(2,1)S(1)} %bitcast.6, bf16[128,1024]{1,0:T(8,128)(2,1)S(1)} %join.1.refs_8_.refs_2_, bf16[128,1024]{1,0:T(8,128)(2,1)S(1)} %collective-permute-done.5.refs_3_, ...), custom_call_target="tpu_custom_call" | custom-call | flops 4294967296 | bytes 19927040 | tf_op jit(solution)/shard_map/experts/pallas_call | solution.py:126
  42.3 1.2 %collective-permute-done.10.refs_4_ = s16[144,512]{1,0:T(8,128)(2,1)S(1)} collective-permute-done((s16[144,512]{1,0:T(8,128)(2,1)S(1)}, s16[144,512]{1,0:T(8,128)(2,1)S(1)}, u32[]{:S(2)}, u32[]{:S(2)}) %collective-permute-start.10) | collective-permute-done | bytes 147488 | tf_op jit(solution)/shard_map/ppermute | solution.py:524
  43.4 0.3 turn.1
  43.8 0.1 collective-permute-start.15
  43.8 1.2 %collective-permute-start.13 = (s16[144,512]{1,0:T(8,128)(2,1)S(1)}, s16[144,512]{1,0:T(8,128)(2,1)S(1)}, u32[]{:S(2)}, u32[]{:S(2)}) collective-permute-start(s16[144,512]{1,0:T(8,128)(2,1)S(1)} %get-tuple-element.54), channel_id=1, source_target_pairs={{0,4},{4,0},{8,12},{12,8},{16,20},{20,16},{24,28},{28,24},{1,5},{5... | collective-permute-start | bytes 442376 | tf_op jit(solution)/shard_map/ppermute | solution.py:524
  45.1 0.3 collective-permute-done.15.refs_7_
  45.4 5.8 %experts.3.refs_6_ = bf16[1,512,1024]{2,1,0:T(8,128)(2,1)} custom-call(bf16[1,4096,1024]{2,1,0:T(8,128)(2,1)S(1)} %bitcast.4, bf16[1,4096,1024]{2,1,0:T(8,128)(2,1)S(1)} %bitcast.6, bf16[128,1024]{1,0:T(8,128)(2,1)S(1)} %get-tuple-element.49.refs_6_.refs_2_, ...), custom_call_target="tpu_custom_call", output_to_operand_aliasing={{}: (9, {})} | custom-call | flops 4294967296 | bytes 20975616 | tf_op jit(solution)/shard_map/experts/pallas_call | solution.py:126
  51.2 2.5 %back.1 = bf16[256,1024]{1,0:T(8,128)(2,1)} custom-call(f32[1,1024]{1,0:T(1,128)S(1)} %get-tuple-element.42.refs_0_, f32[256,1024]{1,0:T(8,128)S(1)} %get-tuple-element.43.refs_5_.refs_1_, f32[256,1024]{1,0:T(8,128)S(1)} %get-tuple-element.44.refs_2_, f32[256,256]{1,0:T(8,128)S(1)} %get-tuple-element.40.refs_3_, f32[128,512]{1,0:T(8,128)S(1)} %get-tuple-element.53.refs_4_, ...), custom_call_target="tpu_custom_call" | custom-call | flops 1000000000 | bytes 3297280 | tf_op jit(solution)/shard_map/back/pallas_call | solution.py:126
  (20 shorter events, 0.1 us)
Async XLA Ops:
  0.6 7.8 %collective-permute-start.1 = (bf16[64,1024]{1,0:T(8,128)(2,1)}, bf16[64,1024]{1,0:T(8,128)(2,1)S(1)}, u32[]{:S(2)}, u32[]{:S(2)}) collective-permute-start(bf16[64,1024]{1,0:T(8,128)(2,1)} %refs_3_.1), channel_id=1, source_target_pairs={{0,8},{4,12},{8,0},{12,4},{16,24},{20,28},{24,16},{28,20},{1,9},{5... | collective-permute-start | bytes 393224 | tf_op jit(solution)/shard_map/ppermute | solution.py:524
  5.0 8.3 %collective-permute-start = (bf16[16,1280]{1,0:T(8,128)(2,1)S(1)}, bf16[16,1280]{1,0:T(8,128)(2,1)S(1)}, u32[]{:S(2)}, u32[]{:S(2)}) collective-permute-start(bf16[16,1280]{1,0:T(8,128)(2,1)S(1)} %get-tuple-element.37), channel_id=1, source_target_pairs={{0,4},{4,8},{8,12},{12,16},{16,20},{20,24},{24,28},{1,5},{5,9},{9,... | collective-permute-start | bytes 122888 | tf_op jit(solution)/shard_map/ppermute | solution.py:667
  8.5 8.7 %collective-permute-start.5 = (bf16[128,1024]{1,0:T(8,128)(2,1)S(1)}, bf16[128,1024]{1,0:T(8,128)(2,1)S(1)}, u32[]{:S(2)}, u32[]{:S(2)}) collective-permute-start(bf16[128,1024]{1,0:T(8,128)(2,1)S(1)} %join.1.refs_8_.refs_2_), channel_id=1, source_target_pairs={{0,4},{4,0},{8,12},{12,8},{16,20},{20,16},{24,28},{28,24},{1,5},{5... | collective-permute-start | bytes 786440 | tf_op jit(solution)/shard_map/ppermute | solution.py:524
  9.2 12.6 %collective-permute-start.4 = (bf16[128,1024]{1,0:T(8,128)(2,1)S(1)}, bf16[128,1024]{1,0:T(8,128)(2,1)S(1)}, u32[]{:S(2)}, u32[]{:S(2)}) collective-permute-start(bf16[128,1024]{1,0:T(8,128)(2,1)S(1)} %join.1.refs_8_.refs_2_), channel_id=1, source_target_pairs={{0,2},{1,3},{2,0},{3,1},{4,6},{5,7},{6,4},{7,5},{8,10},{9,11},{10,... | collective-permute-start | bytes 786440 | tf_op jit(solution)/shard_map/ppermute | solution.py:524
  10.7 13.2 %collective-permute-start.3 = (bf16[128,1024]{1,0:T(8,128)(2,1)S(1)}, bf16[128,1024]{1,0:T(8,128)(2,1)S(1)}, u32[]{:S(2)}, u32[]{:S(2)}) collective-permute-start(bf16[128,1024]{1,0:T(8,128)(2,1)S(1)} %join.1.refs_8_.refs_2_), channel_id=1, source_target_pairs={{0,16},{4,20},{8,24},{12,28},{16,0},{20,4},{24,8},{28,12},{1,17},{... | collective-permute-start | bytes 786440 | tf_op jit(solution)/shard_map/ppermute | solution.py:524
  13.3 23.3 %slice-start.2 = ((s8[8388608]{0:T(1024)(128)(4,1)}), s8[4194304]{0:T(1024)(128)(4,1)S(1)}, s32[]{:S(2)}) async-start(s8[8388608]{0:T(1024)(128)(4,1)} %bitcast.5), calls=%async_computation.2 | async-start | bytes 8388608
  15.7 6.0 %collective-permute-start.2 = (s16[144,512]{1,0:T(8,128)(2,1)S(1)}, s16[144,512]{1,0:T(8,128)(2,1)S(1)}, u32[]{:S(2)}, u32[]{:S(2)}) collective-permute-start(s16[144,512]{1,0:T(8,128)(2,1)S(1)} %get-tuple-element.46), channel_id=1, source_target_pairs={{0,4},{4,0},{8,12},{12,8},{16,20},{20,16},{24,28},{28,24},{1,5},{5... | collective-permute-start | bytes 442376 | tf_op jit(solution)/shard_map/ppermute | solution.py:524
  17.2 6.7 %collective-permute-start.6 = (bf16[128,1024]{1,0:T(8,128)(2,1)S(1)}, bf16[128,1024]{1,0:T(8,128)(2,1)S(1)}, u32[]{:S(2)}, u32[]{:S(2)}) collective-permute-start(bf16[128,1024]{1,0:T(8,128)(2,1)S(1)} %collective-permute-done.5.refs_3_), channel_id=1, source_target_pairs={{0,2},{1,3},{2,0},{3,1},{4,6},{5,7},{6,4},{7,5},{8,10},{9,11},{10,... | collective-permute-start | bytes 786440 | tf_op jit(solution)/shard_map/ppermute | solution.py:524
  17.9 18.7 %slice-start = ((s8[8388608]{0:T(1024)(128)(4,1)}), s8[4194304]{0:T(1024)(128)(4,1)S(1)}, s32[]{:S(2)}) async-start(s8[8388608]{0:T(1024)(128)(4,1)} %bitcast.3), calls=%async_computation | async-start | bytes 8388608
  17.9 18.7 %slice-start.1 = ((s8[8388608]{0:T(1024)(128)(4,1)}), s8[4194304]{0:T(1024)(128)(4,1)S(1)}, s32[]{:S(2)}) async-start(s8[8388608]{0:T(1024)(128)(4,1)} %bitcast.3), calls=%async_computation.1 | async-start | bytes 8388608
  17.9 18.7 %slice-start.3 = ((s8[8388608]{0:T(1024)(128)(4,1)}), s8[4194304]{0:T(1024)(128)(4,1)S(1)}, s32[]{:S(2)}) async-start(s8[8388608]{0:T(1024)(128)(4,1)} %bitcast.5), calls=%async_computation.3 | async-start | bytes 8388608
  24.0 7.7 %collective-permute-start.8 = (bf16[128,1024]{1,0:T(8,128)(2,1)S(1)}, bf16[128,1024]{1,0:T(8,128)(2,1)S(1)}, u32[]{:S(2)}, u32[]{:S(2)}) collective-permute-start(bf16[128,1024]{1,0:T(8,128)(2,1)S(1)} %get-tuple-element.49.refs_6_.refs_2_), channel_id=1, source_target_pairs={{0,4},{4,0},{8,12},{12,8},{16,20},{20,16},{24,28},{28,24},{1,5},{5... | collective-permute-start | bytes 786440 | tf_op jit(solution)/shard_map/ppermute | solution.py:524
  25.7 7.0 %collective-permute-start.9 = (bf16[128,1024]{1,0:T(8,128)(2,1)S(1)}, bf16[128,1024]{1,0:T(8,128)(2,1)S(1)}, u32[]{:S(2)}, u32[]{:S(2)}) collective-permute-start(bf16[128,1024]{1,0:T(8,128)(2,1)S(1)} %get-tuple-element.49.refs_6_.refs_2_), channel_id=1, source_target_pairs={{0,2},{1,3},{2,0},{3,1},{4,6},{5,7},{6,4},{7,5},{8,10},{9,11},{10,... | collective-permute-start | bytes 786440 | tf_op jit(solution)/shard_map/ppermute | solution.py:524
  26.2 5.6 %collective-permute-start.7 = (s16[144,512]{1,0:T(8,128)(2,1)S(1)}, s16[144,512]{1,0:T(8,128)(2,1)S(1)}, u32[]{:S(2)}, u32[]{:S(2)}) collective-permute-start(s16[144,512]{1,0:T(8,128)(2,1)S(1)} %get-tuple-element.48), channel_id=1, source_target_pairs={{0,8},{4,12},{8,0},{12,4},{16,24},{20,28},{24,16},{28,20},{1,9},{5... | collective-permute-start | bytes 442376 | tf_op jit(solution)/shard_map/ppermute | solution.py:524
  33.0 3.6 %collective-permute-start.12 = (bf16[512,1024]{1,0:T(8,128)(2,1)S(1)}, bf16[512,1024]{1,0:T(8,128)(2,1)S(1)}, u32[]{:S(2)}, u32[]{:S(2)}) collective-permute-start(bf16[512,1024]{1,0:T(8,128)(2,1)S(1)} %get-tuple-element.51), channel_id=1, source_target_pairs={{0,1},{1,0},{2,3},{3,2},{4,5},{5,4},{6,7},{7,6},{8,9},{9,8},{10,11... | collective-permute-start | bytes 3145736 | tf_op jit(solution)/shard_map/ppermute | solution.py:524
  33.0 12.0 %collective-permute-start.14 = (bf16[384,1024]{1,0:T(8,128)(2,1)S(1)}, bf16[384,1024]{1,0:T(8,128)(2,1)S(1)}, u32[]{:S(2)}, u32[]{:S(2)}) collective-permute-start(bf16[384,1024]{1,0:T(8,128)(2,1)S(1)} %get-tuple-element.55), channel_id=1, source_target_pairs={{0,1},{1,0},{2,3},{3,2},{4,5},{5,4},{6,7},{7,6},{8,9},{9,8},{10,11... | collective-permute-start | bytes 2359304 | tf_op jit(solution)/shard_map/ppermute | solution.py:524
  33.5 9.9 %collective-permute-start.10 = (s16[144,512]{1,0:T(8,128)(2,1)S(1)}, s16[144,512]{1,0:T(8,128)(2,1)S(1)}, u32[]{:S(2)}, u32[]{:S(2)}) collective-permute-start(s16[144,512]{1,0:T(8,128)(2,1)S(1)} %get-tuple-element.50), channel_id=1, source_target_pairs={{0,16},{4,20},{8,24},{12,28},{16,0},{20,4},{24,8},{28,12},{1,17},{... | collective-permute-start | bytes 442376 | tf_op jit(solution)/shard_map/ppermute | solution.py:524
  34.8 8.7 %collective-permute-start.11 = (bf16[128,1024]{1,0:T(8,128)(2,1)S(1)}, bf16[128,1024]{1,0:T(8,128)(2,1)S(1)}, u32[]{:S(2)}, u32[]{:S(2)}) collective-permute-start(bf16[128,1024]{1,0:T(8,128)(2,1)S(1)} %collective-permute-done.9.refs_8_.refs_4_), channel_id=1, source_target_pairs={{0,4},{4,0},{8,12},{12,8},{16,20},{20,16},{24,28},{28,24},{1,5},{5... | collective-permute-start | bytes 786440 | tf_op jit(solution)/shard_map/ppermute | solution.py:524
  43.8 1.6 %collective-permute-start.15 = (bf16[128,1024]{1,0:T(8,128)(2,1)S(1)}, bf16[128,1024]{1,0:T(8,128)(2,1)S(1)}, u32[]{:S(2)}, u32[]{:S(2)}) collective-permute-start(bf16[128,1024]{1,0:T(8,128)(2,1)S(1)} %get-tuple-element.56), channel_id=1, source_target_pairs={{0,1},{1,0},{2,3},{3,2},{4,5},{5,4},{6,7},{7,6},{8,9},{9,8},{10,11... | collective-permute-start | bytes 786440 | tf_op jit(solution)/shard_map/ppermute | solution.py:524
  43.8 7.4 %collective-permute-start.13 = (s16[144,512]{1,0:T(8,128)(2,1)S(1)}, s16[144,512]{1,0:T(8,128)(2,1)S(1)}, u32[]{:S(2)}, u32[]{:S(2)}) collective-permute-start(s16[144,512]{1,0:T(8,128)(2,1)S(1)} %get-tuple-element.54), channel_id=1, source_target_pairs={{0,4},{4,0},{8,12},{12,8},{16,20},{20,16},{24,28},{28,24},{1,5},{5... | collective-permute-start | bytes 442376 | tf_op jit(solution)/shard_map/ppermute | solution.py:524

commit v21 on v20

--- a/solution.py
+++ b/solution.py
@@ -404,7 +404,7 @@
         [pair_array, sent_array, array(far_rows.shape, BF16)],
         (keep, got, far_rows),
         near=True,
-        after=(*near_pieces[2:], pre),
+        after=(near_pieces[2], pre),
         name="pair",
     )
     far_pieces = spread_rows(rows, 1)

time: 54 us -> 59.1 us (1.094)
  waiting for transfers between devices: 7.63 us -> 13.8 us
  starting transfers between devices: 23 us -> 21.9 us
    ppermute x15, waiting for transfers between devices: 7.63 us -> 13.8 us  [swapped(): lax.ppermute(block, axis, [(i, i ^ bit) for i in range(lax.axis_size(axis...]
    ppermute x15, starting transfers between devices: 19.5 us -> 18.5 us  [swapped(): lax.ppermute(block, axis, [(i, i ^ bit) for i in range(lax.axis_size(axis...]
  transfers between devices with their start and end apart: 16 -> 16, of which waited for: 5 -> 8; matrix products, arithmetic and copies ran while one was open for 0% -> 0% of each run, Pallas kernels for 36% -> 33%
where the time goes in v21:
time: 59.1 us; the launch traced here: 58.9 us
  Pallas kernels  22.2 us (38%)
  starting transfers between devices  21.9 us (37%)
  waiting for transfers between devices  13.8 us (23%)
  between operations  0.95 us (2%)
    pallas_call x10, Pallas kernels, call(): pl.pallas_call(body, out_shape=outs, in_specs=[pl.BlockSpec(memory_space=...  22.2 us
    ppermute x15, starting transfers between devices, swapped(): lax.ppermute(block, axis, [(i, i ^ bit) for i in range(lax.axis_size(axis...  18.5 us
    ppermute x15, waiting for transfers between devices, swapped(): lax.ppermute(block, axis, [(i, i ^ bit) for i in range(lax.axis_size(axis...  13.8 us
    ppermute x1, starting transfers between devices, on_device(): before = lax.ppermute(ends, 'ctx', [(i, i + 1) for i in range(ctx - 1)])  3.4 us
  transfers between devices with their start and end apart: 16, of which 8 were waited for; matrix products, arithmetic and copies ran while one was open for 0% of the time, Pallas kernels for 33%

profile of v21, /device:TPU:0, one launch (start us, length us, event | category | flops | bytes accessed | tf_op | source)
XLA Modules:
  0.0 58.9 jit_solution(9908442558710171454)
XLA Ops:
  0.6 3.1 %collective-permute-start.1 = (bf16[64,1024]{1,0:T(8,128)(2,1)}, bf16[64,1024]{1,0:T(8,128)(2,1)S(1)}, u32[]{:S(2)}, u32[]{:S(2)}) collective-permute-start(bf16[64,1024]{1,0:T(8,128)(2,1)} %refs_3_.1), channel_id=1, source_target_pairs={{0,8},{4,12},{8,0},{12,4},{16,24},{20,28},{24,16},{28,20},{1,9},{5... | collective-permute-start | bytes 393224 | tf_op jit(solution)/shard_map/ppermute | solution.py:524
  3.7 1.3 %ends.1 = (bf16[16,1280]{1,0:T(8,128)(2,1)S(1)}, bf16[256,1024]{1,0:T(8,128)(2,1)S(1)}, bf16[256,128]{1,0:T(8,128)(2,1)S(1)}, bf16[256,128]{1,0:T(8,128)(2,1)S(1...) custom-call(bf16[256,1024]{1,0:T(8,128)(2,1)} %refs_0_.3, ...), custom_call_target="tpu_custom_call" | custom-call | bytes 1688576 | tf_op jit(solution)/shard_map/ends/pallas_call | solution.py:126
  5.0 3.4 %collective-permute-start = (bf16[16,1280]{1,0:T(8,128)(2,1)S(1)}, bf16[16,1280]{1,0:T(8,128)(2,1)S(1)}, u32[]{:S(2)}, u32[]{:S(2)}) collective-permute-start(bf16[16,1280]{1,0:T(8,128)(2,1)S(1)} %get-tuple-element.37), channel_id=1, source_target_pairs={{0,4},{4,8},{8,12},{12,16},{16,20},{20,24},{24,28},{1,5},{5,9},{9,... | collective-permute-start | bytes 122888 | tf_op jit(solution)/shard_map/ppermute | solution.py:667
  8.4 1.6 %collective-permute-start.4 = (bf16[128,1024]{1,0:T(8,128)(2,1)S(1)}, bf16[128,1024]{1,0:T(8,128)(2,1)S(1)}, u32[]{:S(2)}, u32[]{:S(2)}) collective-permute-start(bf16[128,1024]{1,0:T(8,128)(2,1)S(1)} %join.1.refs_8_.refs_2_), channel_id=1, source_target_pairs={{0,2},{1,3},{2,0},{3,1},{4,6},{5,7},{6,4},{7,5},{8,10},{9,11},{10,... | collective-permute-start | bytes 786440 | tf_op jit(solution)/shard_map/ppermute | solution.py:524
  10.0 2.6 %collective-permute-start.3 = (bf16[128,1024]{1,0:T(8,128)(2,1)S(1)}, bf16[128,1024]{1,0:T(8,128)(2,1)S(1)}, u32[]{:S(2)}, u32[]{:S(2)}) collective-permute-start(bf16[128,1024]{1,0:T(8,128)(2,1)S(1)} %join.1.refs_8_.refs_2_), channel_id=1, source_target_pairs={{0,16},{4,20},{8,24},{12,28},{16,0},{20,4},{24,8},{28,12},{1,17},{... | collective-permute-start | bytes 786440 | tf_op jit(solution)/shard_map/ppermute | solution.py:524
  12.6 0.7 %collective-permute-start.6 = (bf16[128,1024]{1,0:T(8,128)(2,1)S(1)}, bf16[128,1024]{1,0:T(8,128)(2,1)S(1)}, u32[]{:S(2)}, u32[]{:S(2)}) collective-permute-start(bf16[128,1024]{1,0:T(8,128)(2,1)S(1)} %join.1.refs_8_.refs_2_), channel_id=1, source_target_pairs={{0,4},{4,0},{8,12},{12,8},{16,20},{20,16},{24,28},{28,24},{1,5},{5... | collective-permute-start | bytes 786440 | tf_op jit(solution)/shard_map/ppermute | solution.py:524
  13.3 2.4 %front.1 = (f32[256,1024]{1,0:T(8,128)S(1)}, f32[256,256]{1,0:T(8,128)S(1)}, f32[2,16,256]{2,1,0:T(8,128)S(1)}, f32[136,512]{1,0:T(8,128)S(1)}, s16[144,512]{1,0:T(8,128)(2,1)S(1)}) custom-call(bf16[256,1024]{1,0:T(8,128)(2,1)S(1)} %get-tuple-element.30.refs_0_, bf16[256,128]{1,0:T(8,128)(2,1)S(1)} %get-tuple-element.31.refs_1_, ...), custom_call_target="tpu_custom_call" | custom-call | flops 5000000000 | bytes 2503168 | tf_op jit(solution)/shard_map/front/pallas_call | solution.py:126
  15.7 1.4 %collective-permute-start.2 = (s16[144,512]{1,0:T(8,128)(2,1)S(1)}, s16[144,512]{1,0:T(8,128)(2,1)S(1)}, u32[]{:S(2)}, u32[]{:S(2)}) collective-permute-start(s16[144,512]{1,0:T(8,128)(2,1)S(1)} %get-tuple-element.46), channel_id=1, source_target_pairs={{0,4},{4,0},{8,12},{12,8},{16,20},{20,16},{24,28},{28,24},{1,5},{5... | collective-permute-start | bytes 442376 | tf_op jit(solution)/shard_map/ppermute | solution.py:524
  17.2 3.9 %inner.1 = (f32[256,1024]{1,0:T(8,128)S(1)}, f32[256,1024]{1,0:T(8,128)S(1)}, f32[1,1024]{1,0:T(1,128)S(1)}) custom-call(f32[1,16]{1,0:T(1,128)} %bitcast.9, f32[1,1024]{1,0:T(1,128)} %bitcast.8, f32[256,1024]{1,0:T(8,128)S(1)} %get-tuple-element.39.refs_2_, f32[256,256]{1,0:T(8,128)S(1)} %get-tuple-element.40.refs_3_, ...), custom_call_target="tpu_custom_call" | custom-call | flops 4000000000 | bytes 3448896 | tf_op jit(solution)/shard_map/inner/pallas_call | solution.py:126
  21.0 1.6 %collective-permute-done.2.refs_1_ = s16[144,512]{1,0:T(8,128)(2,1)S(1)} collective-permute-done((s16[144,512]{1,0:T(8,128)(2,1)S(1)}, s16[144,512]{1,0:T(8,128)(2,1)S(1)}, u32[]{:S(2)}, u32[]{:S(2)}) %collective-permute-start.2) | collective-permute-done | bytes 147488 | tf_op jit(solution)/shard_map/ppermute | solution.py:524
  22.7 0.9 %collective-permute-done.3.refs_2_ = bf16[128,1024]{1,0:T(8,128)(2,1)S(1)} collective-permute-done((bf16[128,1024]{1,0:T(8,128)(2,1)S(1)}, bf16[128,1024]{1,0:T(8,128)(2,1)S(1)}, u32[]{:S(2)}, u32[]{:S(2)}) %collective-permute-start.3) | collective-permute-done | bytes 262176 | tf_op jit(solution)/shard_map/ppermute | solution.py:524
  23.6 0.2 pair.1
  23.8 0.6 %collective-permute-start.8 = (bf16[128,1024]{1,0:T(8,128)(2,1)S(1)}, bf16[128,1024]{1,0:T(8,128)(2,1)S(1)}, u32[]{:S(2)}, u32[]{:S(2)}) collective-permute-start(bf16[128,1024]{1,0:T(8,128)(2,1)S(1)} %get-tuple-element.49.refs_6_.refs_2_), channel_id=1, source_target_pairs={{0,4},{4,0},{8,12},{12,8},{16,20},{20,16},{24,28},{28,24},{1,5},{5... | collective-permute-start | bytes 786440 | tf_op jit(solution)/shard_map/ppermute | solution.py:524
  24.4 0.5 collective-permute-start.9
  24.8 1.6 %collective-permute-start.7 = (bf16[128,1024]{1,0:T(8,128)(2,1)S(1)}, bf16[128,1024]{1,0:T(8,128)(2,1)S(1)}, u32[]{:S(2)}, u32[]{:S(2)}) collective-permute-start(bf16[128,1024]{1,0:T(8,128)(2,1)S(1)} %collective-permute-done.6.refs_3_), channel_id=1, source_target_pairs={{0,2},{1,3},{2,0},{3,1},{4,6},{5,7},{6,4},{7,5},{8,10},{9,11},{10,... | collective-permute-start | bytes 786440 | tf_op jit(solution)/shard_map/ppermute | solution.py:524
  26.4 1.9 %collective-permute-start.5 = (s16[144,512]{1,0:T(8,128)(2,1)S(1)}, s16[144,512]{1,0:T(8,128)(2,1)S(1)}, u32[]{:S(2)}, u32[]{:S(2)}) collective-permute-start(s16[144,512]{1,0:T(8,128)(2,1)S(1)} %get-tuple-element.48), channel_id=1, source_target_pairs={{0,8},{4,12},{8,0},{12,4},{16,24},{20,28},{24,16},{28,20},{1,9},{5... | collective-permute-start | bytes 442376 | tf_op jit(solution)/shard_map/ppermute | solution.py:524
  28.3 3.2 %collective-permute-done.5.refs_1_.refs_3_ = s16[144,512]{1,0:T(8,128)(2,1)S(1)} collective-permute-done((s16[144,512]{1,0:T(8,128)(2,1)S(1)}, s16[144,512]{1,0:T(8,128)(2,1)S(1)}, u32[]{:S(2)}, u32[]{:S(2)}) %collective-permute-start.5) | collective-permute-done | bytes 147488 | tf_op jit(solution)/shard_map/ppermute | solution.py:524
  31.6 0.5 collective-permute-done.8.refs_7_.refs_3_
  32.1 1.5 %collective-permute-done.9.refs_8_.refs_4_ = bf16[128,1024]{1,0:T(8,128)(2,1)S(1)} collective-permute-done((bf16[128,1024]{1,0:T(8,128)(2,1)S(1)}, bf16[128,1024]{1,0:T(8,128)(2,1)S(1)}, u32[]{:S(2)}, u32[]{:S(2)}) %collective-permute-start.9) | collective-permute-done | bytes 262176 | tf_op jit(solution)/shard_map/ppermute | solution.py:524
  33.6 4.2 %collective-permute-done.7.refs_5_ = bf16[128,1024]{1,0:T(8,128)(2,1)S(1)} collective-permute-done((bf16[128,1024]{1,0:T(8,128)(2,1)S(1)}, bf16[128,1024]{1,0:T(8,128)(2,1)S(1)}, u32[]{:S(2)}, u32[]{:S(2)}) %collective-permute-start.7) | collective-permute-done | bytes 262176 | tf_op jit(solution)/shard_map/ppermute | solution.py:524
  37.8 0.3 four.1
  38.0 0.1 collective-permute-start.12
  38.1 0.5 collective-permute-start.14
  38.6 0.8 %collective-permute-start.10 = (s16[144,512]{1,0:T(8,128)(2,1)S(1)}, s16[144,512]{1,0:T(8,128)(2,1)S(1)}, u32[]{:S(2)}, u32[]{:S(2)}) collective-permute-start(s16[144,512]{1,0:T(8,128)(2,1)S(1)} %get-tuple-element.50), channel_id=1, source_target_pairs={{0,16},{4,20},{8,24},{12,28},{16,0},{20,4},{24,8},{28,12},{1,17},{... | collective-permute-start | bytes 442376 | tf_op jit(solution)/shard_map/ppermute | solution.py:524
  39.4 1.8 %collective-permute-start.11 = (bf16[128,1024]{1,0:T(8,128)(2,1)S(1)}, bf16[128,1024]{1,0:T(8,128)(2,1)S(1)}, u32[]{:S(2)}, u32[]{:S(2)}) collective-permute-start(bf16[128,1024]{1,0:T(8,128)(2,1)S(1)} %collective-permute-done.9.refs_8_.refs_4_), channel_id=1, source_target_pairs={{0,4},{4,0},{8,12},{12,8},{16,20},{20,16},{24,28},{28,24},{1,5},{5... | collective-permute-start | bytes 786440 | tf_op jit(solution)/shard_map/ppermute | solution.py:524
  41.2 5.6 %experts.2.refs_6_.refs_9_ = bf16[1,512,1024]{2,1,0:T(8,128)(2,1)} custom-call(bf16[1,4096,1024]{2,1,0:T(8,128)(2,1)S(1)} %bitcast.4, bf16[1,4096,1024]{2,1,0:T(8,128)(2,1)S(1)} %bitcast.6, bf16[128,1024]{1,0:T(8,128)(2,1)S(1)} %join.1.refs_8_.refs_2_, bf16[128,1024]{1,0:T(8,128)(2,1)S(1)} %collective-permute-done.6.refs_3_, ...), custom_call_target="tpu_custom_call" | custom-call | flops 4294967296 | bytes 19927040 | tf_op jit(solution)/shard_map/experts/pallas_call | solution.py:126
  46.8 1.7 %collective-permute-done.10.refs_4_ = s16[144,512]{1,0:T(8,128)(2,1)S(1)} collective-permute-done((s16[144,512]{1,0:T(8,128)(2,1)S(1)}, s16[144,512]{1,0:T(8,128)(2,1)S(1)}, u32[]{:S(2)}, u32[]{:S(2)}) %collective-permute-start.10) | collective-permute-done | bytes 147488 | tf_op jit(solution)/shard_map/ppermute | solution.py:524
  48.5 0.3 turn.1
  48.9 1.4 %collective-permute-start.13 = (s16[144,512]{1,0:T(8,128)(2,1)S(1)}, s16[144,512]{1,0:T(8,128)(2,1)S(1)}, u32[]{:S(2)}, u32[]{:S(2)}) collective-permute-start(s16[144,512]{1,0:T(8,128)(2,1)S(1)} %get-tuple-element.54), channel_id=1, source_target_pairs={{0,4},{4,0},{8,12},{12,8},{16,20},{20,16},{24,28},{28,24},{1,5},{5... | collective-permute-start | bytes 442376 | tf_op jit(solution)/shard_map/ppermute | solution.py:524
  50.4 0.1 collective-permute-done.15.refs_7_
  50.4 5.8 %experts.3.refs_6_ = bf16[1,512,1024]{2,1,0:T(8,128)(2,1)} custom-call(bf16[1,4096,1024]{2,1,0:T(8,128)(2,1)S(1)} %bitcast.4, bf16[1,4096,1024]{2,1,0:T(8,128)(2,1)S(1)} %bitcast.6, bf16[128,1024]{1,0:T(8,128)(2,1)S(1)} %get-tuple-element.49.refs_6_.refs_2_, ...), custom_call_target="tpu_custom_call", output_to_operand_aliasing={{}: (9, {})} | custom-call | flops 4294967296 | bytes 20975616 | tf_op jit(solution)/shard_map/experts/pallas_call | solution.py:126
  56.3 2.5 %back.1 = bf16[256,1024]{1,0:T(8,128)(2,1)} custom-call(f32[1,1024]{1,0:T(1,128)S(1)} %get-tuple-element.42.refs_0_, f32[256,1024]{1,0:T(8,128)S(1)} %get-tuple-element.43.refs_4_.refs_1_, f32[256,1024]{1,0:T(8,128)S(1)} %get-tuple-element.44.refs_2_, f32[256,256]{1,0:T(8,128)S(1)} %get-tuple-element.40.refs_3_, f32[128,512]{1,0:T(8,128)S(1)} %get-tuple-element.53.refs_4_, ...), custom_call_target="tpu_custom_call" | custom-call | flops 1000000000 | bytes 3297280 | tf_op jit(solution)/shard_map/back/pallas_call | solution.py:126
  (20 shorter events, 0.1 us)
Async XLA Ops:
  0.6 7.8 %collective-permute-start.1 = (bf16[64,1024]{1,0:T(8,128)(2,1)}, bf16[64,1024]{1,0:T(8,128)(2,1)S(1)}, u32[]{:S(2)}, u32[]{:S(2)}) collective-permute-start(bf16[64,1024]{1,0:T(8,128)(2,1)} %refs_3_.1), channel_id=1, source_target_pairs={{0,8},{4,12},{8,0},{12,4},{16,24},{20,28},{24,16},{28,20},{1,9},{5... | collective-permute-start | bytes 393224 | tf_op jit(solution)/shard_map/ppermute | solution.py:524
  5.0 8.3 %collective-permute-start = (bf16[16,1280]{1,0:T(8,128)(2,1)S(1)}, bf16[16,1280]{1,0:T(8,128)(2,1)S(1)}, u32[]{:S(2)}, u32[]{:S(2)}) collective-permute-start(bf16[16,1280]{1,0:T(8,128)(2,1)S(1)} %get-tuple-element.37), channel_id=1, source_target_pairs={{0,4},{4,8},{8,12},{12,16},{16,20},{20,24},{24,28},{1,5},{5,9},{9,... | collective-permute-start | bytes 122888 | tf_op jit(solution)/shard_map/ppermute | solution.py:667
  8.4 14.3 %collective-permute-start.4 = (bf16[128,1024]{1,0:T(8,128)(2,1)S(1)}, bf16[128,1024]{1,0:T(8,128)(2,1)S(1)}, u32[]{:S(2)}, u32[]{:S(2)}) collective-permute-start(bf16[128,1024]{1,0:T(8,128)(2,1)S(1)} %join.1.refs_8_.refs_2_), channel_id=1, source_target_pairs={{0,2},{1,3},{2,0},{3,1},{4,6},{5,7},{6,4},{7,5},{8,10},{9,11},{10,... | collective-permute-start | bytes 786440 | tf_op jit(solution)/shard_map/ppermute | solution.py:524
  10.0 13.6 %collective-permute-start.3 = (bf16[128,1024]{1,0:T(8,128)(2,1)S(1)}, bf16[128,1024]{1,0:T(8,128)(2,1)S(1)}, u32[]{:S(2)}, u32[]{:S(2)}) collective-permute-start(bf16[128,1024]{1,0:T(8,128)(2,1)S(1)} %join.1.refs_8_.refs_2_), channel_id=1, source_target_pairs={{0,16},{4,20},{8,24},{12,28},{16,0},{20,4},{24,8},{28,12},{1,17},{... | collective-permute-start | bytes 786440 | tf_op jit(solution)/shard_map/ppermute | solution.py:524
  12.6 12.2 %collective-permute-start.6 = (bf16[128,1024]{1,0:T(8,128)(2,1)S(1)}, bf16[128,1024]{1,0:T(8,128)(2,1)S(1)}, u32[]{:S(2)}, u32[]{:S(2)}) collective-permute-start(bf16[128,1024]{1,0:T(8,128)(2,1)S(1)} %join.1.refs_8_.refs_2_), channel_id=1, source_target_pairs={{0,4},{4,0},{8,12},{12,8},{16,20},{20,16},{24,28},{28,24},{1,5},{5... | collective-permute-start | bytes 786440 | tf_op jit(solution)/shard_map/ppermute | solution.py:524
  13.3 27.9 %slice-start = ((s8[8388608]{0:T(1024)(128)(4,1)}), s8[4194304]{0:T(1024)(128)(4,1)S(1)}, s32[]{:S(2)}) async-start(s8[8388608]{0:T(1024)(128)(4,1)} %bitcast.3), calls=%async_computation | async-start | bytes 8388608
  13.3 27.9 %slice-start.2 = ((s8[8388608]{0:T(1024)(128)(4,1)}), s8[4194304]{0:T(1024)(128)(4,1)S(1)}, s32[]{:S(2)}) async-start(s8[8388608]{0:T(1024)(128)(4,1)} %bitcast.5), calls=%async_computation.2 | async-start | bytes 8388608
  15.7 7.0 %collective-permute-start.2 = (s16[144,512]{1,0:T(8,128)(2,1)S(1)}, s16[144,512]{1,0:T(8,128)(2,1)S(1)}, u32[]{:S(2)}, u32[]{:S(2)}) collective-permute-start(s16[144,512]{1,0:T(8,128)(2,1)S(1)} %get-tuple-element.46), channel_id=1, source_target_pairs={{0,4},{4,0},{8,12},{12,8},{16,20},{20,16},{24,28},{28,24},{1,5},{5... | collective-permute-start | bytes 442376 | tf_op jit(solution)/shard_map/ppermute | solution.py:524
  17.2 24.0 %slice-start.1 = ((s8[8388608]{0:T(1024)(128)(4,1)}), s8[4194304]{0:T(1024)(128)(4,1)S(1)}, s32[]{:S(2)}) async-start(s8[8388608]{0:T(1024)(128)(4,1)} %bitcast.3), calls=%async_computation.1 | async-start | bytes 8388608
  17.2 24.0 %slice-start.3 = ((s8[8388608]{0:T(1024)(128)(4,1)}), s8[4194304]{0:T(1024)(128)(4,1)S(1)}, s32[]{:S(2)}) async-start(s8[8388608]{0:T(1024)(128)(4,1)} %bitcast.5), calls=%async_computation.3 | async-start | bytes 8388608
  23.8 8.3 %collective-permute-start.8 = (bf16[128,1024]{1,0:T(8,128)(2,1)S(1)}, bf16[128,1024]{1,0:T(8,128)(2,1)S(1)}, u32[]{:S(2)}, u32[]{:S(2)}) collective-permute-start(bf16[128,1024]{1,0:T(8,128)(2,1)S(1)} %get-tuple-element.49.refs_6_.refs_2_), channel_id=1, source_target_pairs={{0,4},{4,0},{8,12},{12,8},{16,20},{20,16},{24,28},{28,24},{1,5},{5... | collective-permute-start | bytes 786440 | tf_op jit(solution)/shard_map/ppermute | solution.py:524
  24.4 9.2 %collective-permute-start.9 = (bf16[128,1024]{1,0:T(8,128)(2,1)S(1)}, bf16[128,1024]{1,0:T(8,128)(2,1)S(1)}, u32[]{:S(2)}, u32[]{:S(2)}) collective-permute-start(bf16[128,1024]{1,0:T(8,128)(2,1)S(1)} %get-tuple-element.49.refs_6_.refs_2_), channel_id=1, source_target_pairs={{0,2},{1,3},{2,0},{3,1},{4,6},{5,7},{6,4},{7,5},{8,10},{9,11},{10,... | collective-permute-start | bytes 786440 | tf_op jit(solution)/shard_map/ppermute | solution.py:524
  24.8 12.9 %collective-permute-start.7 = (bf16[128,1024]{1,0:T(8,128)(2,1)S(1)}, bf16[128,1024]{1,0:T(8,128)(2,1)S(1)}, u32[]{:S(2)}, u32[]{:S(2)}) collective-permute-start(bf16[128,1024]{1,0:T(8,128)(2,1)S(1)} %collective-permute-done.6.refs_3_), channel_id=1, source_target_pairs={{0,2},{1,3},{2,0},{3,1},{4,6},{5,7},{6,4},{7,5},{8,10},{9,11},{10,... | collective-permute-start | bytes 786440 | tf_op jit(solution)/shard_map/ppermute | solution.py:524
  26.4 5.1 %collective-permute-start.5 = (s16[144,512]{1,0:T(8,128)(2,1)S(1)}, s16[144,512]{1,0:T(8,128)(2,1)S(1)}, u32[]{:S(2)}, u32[]{:S(2)}) collective-permute-start(s16[144,512]{1,0:T(8,128)(2,1)S(1)} %get-tuple-element.48), channel_id=1, source_target_pairs={{0,8},{4,12},{8,0},{12,4},{16,24},{20,28},{24,16},{28,20},{1,9},{5... | collective-permute-start | bytes 442376 | tf_op jit(solution)/shard_map/ppermute | solution.py:524
  38.0 3.1 %collective-permute-start.12 = (bf16[512,1024]{1,0:T(8,128)(2,1)S(1)}, bf16[512,1024]{1,0:T(8,128)(2,1)S(1)}, u32[]{:S(2)}, u32[]{:S(2)}) collective-permute-start(bf16[512,1024]{1,0:T(8,128)(2,1)S(1)} %get-tuple-element.51), channel_id=1, source_target_pairs={{0,1},{1,0},{2,3},{3,2},{4,5},{5,4},{6,7},{7,6},{8,9},{9,8},{10,11... | collective-permute-start | bytes 3145736 | tf_op jit(solution)/shard_map/ppermute | solution.py:524
  38.1 12.3 %collective-permute-start.14 = (bf16[384,1024]{1,0:T(8,128)(2,1)S(1)}, bf16[384,1024]{1,0:T(8,128)(2,1)S(1)}, u32[]{:S(2)}, u32[]{:S(2)}) collective-permute-start(bf16[384,1024]{1,0:T(8,128)(2,1)S(1)} %get-tuple-element.55), channel_id=1, source_target_pairs={{0,1},{1,0},{2,3},{3,2},{4,5},{5,4},{6,7},{7,6},{8,9},{9,8},{10,11... | collective-permute-start | bytes 2359304 | tf_op jit(solution)/shard_map/ppermute | solution.py:524
  38.6 9.9 %collective-permute-start.10 = (s16[144,512]{1,0:T(8,128)(2,1)S(1)}, s16[144,512]{1,0:T(8,128)(2,1)S(1)}, u32[]{:S(2)}, u32[]{:S(2)}) collective-permute-start(s16[144,512]{1,0:T(8,128)(2,1)S(1)} %get-tuple-element.50), channel_id=1, source_target_pairs={{0,16},{4,20},{8,24},{12,28},{16,0},{20,4},{24,8},{28,12},{1,17},{... | collective-permute-start | bytes 442376 | tf_op jit(solution)/shard_map/ppermute | solution.py:524
  39.4 9.1 %collective-permute-start.11 = (bf16[128,1024]{1,0:T(8,128)(2,1)S(1)}, bf16[128,1024]{1,0:T(8,128)(2,1)S(1)}, u32[]{:S(2)}, u32[]{:S(2)}) collective-permute-start(bf16[128,1024]{1,0:T(8,128)(2,1)S(1)} %collective-permute-done.9.refs_8_.refs_4_), channel_id=1, source_target_pairs={{0,4},{4,0},{8,12},{12,8},{16,20},{20,16},{24,28},{28,24},{1,5},{5... | collective-permute-start | bytes 786440 | tf_op jit(solution)/shard_map/ppermute | solution.py:524
  48.8 1.6 %collective-permute-start.15 = (bf16[128,1024]{1,0:T(8,128)(2,1)S(1)}, bf16[128,1024]{1,0:T(8,128)(2,1)S(1)}, u32[]{:S(2)}, u32[]{:S(2)}) collective-permute-start(bf16[128,1024]{1,0:T(8,128)(2,1)S(1)} %get-tuple-element.56), channel_id=1, source_target_pairs={{0,1},{1,0},{2,3},{3,2},{4,5},{5,4},{6,7},{7,6},{8,9},{9,8},{10,11... | collective-permute-start | bytes 786440 | tf_op jit(solution)/shard_map/ppermute | solution.py:524
  48.9 7.3 %collective-permute-start.13 = (s16[144,512]{1,0:T(8,128)(2,1)S(1)}, s16[144,512]{1,0:T(8,128)(2,1)S(1)}, u32[]{:S(2)}, u32[]{:S(2)}) collective-permute-start(s16[144,512]{1,0:T(8,128)(2,1)S(1)} %get-tuple-element.54), channel_id=1, source_target_pairs={{0,4},{4,0},{8,12},{12,8},{16,20},{20,16},{24,28},{28,24},{1,5},{5... | collective-permute-start | bytes 442376 | tf_op jit(solution)/shard_map/ppermute | solution.py:524
